TPU v7x, 32 devices: a whole 2x2x4 slice. The times are simulated.
32 devices in a mesh: rows: 4 (over x, core), pts: 8 (over z, y).
Axes of the slice: x: 2, y: 2, z: 4, core: 2. Of those that a mesh axis runs over, the one named last changes fastest.
Arguments:
- features: bfloat16 [8192, 128], P('pts'), may hold values from -6 to 6
- targets: bfloat16 [8192, 256], P('pts'), may hold values from -6 to 6
- coefficients: float32 [8192, 256], P('pts'), may hold values from -6 to 6
- momentum: float32 [8192, 256], P('pts'), may hold values from -6 to 6
- block_index: int32 [2, 2048], replicated, may hold values from 0 to 8191, as said below
- pivot_index: int32 [2, 512], replicated, may hold values from 0 to 2047, as said below
- nystrom_core: bfloat16 [2, 512, 512], replicated, may hold values from -0.5 to 3
Outputs:
- new_coefficients: float32 [8192, 256], P('pts')
- new_momentum: float32 [8192, 256], P('pts')
Inputs may be any that keep to these rules, and one draw needn't show every extreme that they name: `block_index`: each row lists 2048 distinct points; a point p belongs to index p // 1024 of pts; in each row one index of pts, drawn from the seed, owns exactly 192 of the points in every aligned group of 512 positions, and no index owns more than 192 points of any such group. `pivot_index`: each row lists 512 distinct positions.
All inputs are finite; a program needn't handle non-finite values.
Results may differ from a plain program's by a relative error of at most 0.0041.
The roundings to bfloat16 on the way count: a program that leaves them out, or rounds other values in their place, can miss the bound.
Values may be sent and summed in bfloat16 or wider, within the bound.
No kernel may reach another device: no remote copies, remote signals or barrier semaphores. Data moves between devices by JAX's collectives and lax.ppermute only.
A program may use at most 64 MiB of HBM per device.

v0:
```python
import jax
import jax.numpy as jnp
from jax import lax
from jax.sharding import PartitionSpec as P

UPDATES = 2


alpha_mix = 0.6
beta_keep = 0.9
step_size = 0.2
momentum_gain = 1.5
ridge_term = 1.0


def kernel_tile(left_rows, right_rows):
    inner_prod = lax.dot_general(
        left_rows, right_rows, (((1,), (1,)), ((), ())), preferred_element_type=jnp.float32
    )
    left_sq = jnp.sum(jnp.square(left_rows.astype(jnp.float32)), axis=1)
    right_sq = jnp.sum(jnp.square(right_rows.astype(jnp.float32)), axis=1)
    squared = left_sq[:, None] + right_sq[None, :] - 2.0 * inner_prod
    return jnp.exp(squared * (-3.5 / left_rows.shape[1])).astype(jnp.bfloat16)


def project_rows(factor, resid):
    return lax.dot_general(
        factor,
        resid.astype(jnp.bfloat16),
        (((0,), (0,)), ((), ())),
        preferred_element_type=jnp.float32,
    )


def finish_step(resid, factor, proj, core_now):
    lifted = jnp.dot(
        core_now, proj.astype(jnp.bfloat16), preferred_element_type=jnp.float32
    ).astype(jnp.bfloat16)
    return (resid - jnp.dot(factor, lifted, preferred_element_type=jnp.float32)).astype(
        jnp.bfloat16
    )


def owned_rows(local_feats, wanted, first_point):
    local_pos = wanted - first_point
    holder = (local_pos >= 0) & (local_pos < local_feats.shape[0])
    safe_pos = jnp.clip(local_pos, 0, local_feats.shape[0] - 1)
    return (holder, safe_pos)


def pack_owned(step_bf, row_points, first_point, local_points, capacity):
    local_pos = row_points - first_point
    owned = (local_pos >= 0) & (local_pos < local_points)
    owned_count = owned.astype(jnp.int32)
    position_rank = jnp.cumsum(owned_count) - owned_count
    slot_range = jnp.arange(capacity, dtype=jnp.int32)
    select = owned[None, :] & (position_rank[None, :] == slot_range[:, None])
    packed = jnp.dot(
        select.astype(jnp.bfloat16), step_bf, preferred_element_type=jnp.float32
    ).astype(jnp.bfloat16)
    filled = jnp.any(select, axis=1)
    slot_ids = jnp.where(
        filled, jnp.sum(jnp.where(select, local_pos[None, :], 0), axis=1), local_points
    )
    return (packed, slot_ids)


def shards(features, targets, coefficients, momentum, block_index, pivot_index, nystrom_core):
    row_count = lax.axis_size("rows")
    pts_count = lax.axis_size("pts")
    row_id = lax.axis_index("rows")
    pts_id = lax.axis_index("pts")
    local_points = features.shape[0]
    per_row = block_index.shape[1] // row_count
    per_device = per_row // pts_count
    first_point = pts_id * local_points
    current = coefficients
    momentum_now = momentum
    for update in range(UPDATES):
        mixed = alpha_mix * momentum_now + (1.0 - alpha_mix) * current
        mixed_bf = mixed.astype(jnp.bfloat16)
        whole_index = block_index[update]
        row_points = lax.dynamic_slice_in_dim(whole_index, row_id * per_row, per_row)
        holder, safe_pos = owned_rows(features, row_points, first_point)
        row_terms = jnp.where(holder[:, None], features[safe_pos], jnp.zeros((), jnp.bfloat16))
        offset = jnp.where(
            holder[:, None],
            ridge_term * mixed[safe_pos] - targets[safe_pos].astype(jnp.float32),
            0.0,
        )
        pivot_points = whole_index[pivot_index[update]]
        pivot_holder, pivot_pos = owned_rows(features, pivot_points, first_point)
        pivot_terms = jnp.where(
            pivot_holder[:, None], features[pivot_pos], jnp.zeros((), jnp.bfloat16)
        )
        got_rows, got_pivots = (
            lax.psum(row_terms, "pts").astype(jnp.float32),
            lax.psum(pivot_terms, "pts").astype(jnp.float32),
        )
        block_feats = got_rows.astype(jnp.bfloat16)
        pivot_feats = got_pivots.astype(jnp.bfloat16)
        partial_value = (
            jnp.dot(
                kernel_tile(block_feats, features), mixed_bf, preferred_element_type=jnp.float32
            )
            + offset
        )
        resid = lax.psum(partial_value, "pts")
        factor = kernel_tile(block_feats, pivot_feats)
        proj = lax.psum(project_rows(factor, resid), "rows")
        step_bf = finish_step(resid, factor, proj, nystrom_core[update])
        packed, slot_ids = pack_owned(
            step_bf, row_points, first_point, local_points, 3 * per_device
        )
        got_steps, got_slots = (
            lax.all_gather(packed, "rows", axis=0, tiled=True),
            lax.all_gather(slot_ids, "rows", axis=0, tiled=True),
        )
        change = got_steps.astype(jnp.float32)
        current = mixed.at[got_slots].add(-step_size * change, mode="drop")
        momentum_now = (
            (beta_keep * momentum_now + (1.0 - beta_keep) * mixed)
            .at[got_slots]
            .add(-step_size * momentum_gain * change, mode="drop")
        )
    return (current, momentum_now)


def solution(mesh):
    in_specs = (P("pts", None), P("pts", None), P("pts", None), P("pts", None), P(), P(), P())
    out_specs = (P("pts", None), P("pts", None))
    return jax.shard_map(shards, mesh=mesh, in_specs=in_specs, out_specs=out_specs, check_vma=False)
```

profile of v0, /device:TPU:0, one launch (start us, length us, event | category | flops | bytes accessed | tf_op | source)
XLA Modules:
  0.0 341.4 jit_solution(3406374783472103803)
XLA Ops:
  7.2 0.8 fusion.66
  8.1 0.8 compare_select_fusion.1
  8.9 3.1 gather_fusion.3
  12.1 3.1 gather_fusion.8
  15.3 1.3 gather_fusion.5
  16.6 1.3 gather_fusion
  18.0 1.3 gather_fusion.9
  19.4 1.3 gather_fusion.4
  20.8 0.8 broadcast_select_fusion.1
  21.6 0.8 broadcast_select_fusion.3
  22.4 0.8 broadcast_select_fusion
  23.2 0.8 broadcast_select_fusion.2
  24.0 0.0 all-reduce.10.cloned.1.call-start
  24.0 0.3 reduce-window.16
  24.3 0.1 slice.33
  24.4 0.1 slice_reduce_fusion.1
  24.5 0.1 broadcast_add_fusion.1
  24.6 0.3 reduce-window.24
  24.9 0.1 slice.38
  25.0 0.1 slice_reduce_fusion
  25.2 0.1 broadcast_add_fusion
  25.2 0.1 fusion.45
  25.4 0.2 select_reduce_fusion
  25.6 2.5 multiply_add_fusion.2
  28.1 0.6 dynamic-slice.2
  29.3 0.1 select_dynamic-update-slice_fusion
  29.4 0.1 fusion.42
  29.6 1.6 gather_fusion.1
  31.2 2.0 gather_fusion.2
  33.1 0.2 select_reduce_fusion.1
  33.3 0.1 select_dynamic-update-slice_fusion.1
  33.4 7.0 %all-reduce.2 = (s32[768]{0:T(1024)S(1)}, s32[768]{0:T(1024)}) all-reduce(s32[768]{0:T(1024)S(1)} %select_dynamic-update-slice_fusion.1, s32[768]{0:T(1024)S(1)} %select_dynamic-update-slice_fusion), channel_id=1, replica_groups=mesh['rows'=4,'pts'=8] {'rows'}, use_global_device_ids=true, to_apply=%add | all-reduce | flops 1536 | bytes 12288
  40.4 0.2 multiply_reduce_fusion
  40.6 59.2 %all-reduce.14.cloned.1.call-done = (bf16[512,128]{1,0:T(8,128)(2,1)}, bf16[512,128]{1,0:T(8,128)(2,1)}, bf16[512,128]{1,0:T(8,128)(2,1)}, bf16[512,128]{1,0:T(8,128)(2,1)}) async-done(((bf16[512,128]{1,0:T(8,128)(2,1)}, bf16[512,128]{1,0:T(8,128)(2,1)}, bf16[512,128]{1,0:T(8,128)(2,1)}, bf16[512,128]{1,0:T(8,128)(2,1)}), (bf16[512,128]{1,0:T(8,128)(2,1)}, bf16[512,128]{1,0:T(8,128)(2,1)}, ...) | async-done | bytes 524304 | tf_op jit(solution)/shard_map/psum | solution.py:97
  99.9 1.0 multiply_reduce_fusion.4
  100.9 2.5 fusion.11
  103.5 0.0 all-reduce.12.cloned.1.call-start
  103.5 0.6 compare_select_fusion.7
  104.1 2.6 gather_fusion.7
  106.7 0.1 multiply_reduce_fusion.3
  106.8 0.7 multiply_reduce_fusion.2
  107.6 0.4 fusion.9
  108.0 67.9 %all-reduce.10.cloned.1.call-done = f32[512,256]{1,0:T(8,128)} async-done(((f32[512,256]{1,0:T(8,128)}), f32[512,256]{1,0:T(8,128)}) %all-reduce.10.cloned.1.call-update) | async-done | bytes 524304 | tf_op jit(solution)/shard_map/psum | solution.py:108
  175.8 1.4 fusion.52
  177.3 16.8 %all-reduce.15 = bf16[512,256]{1,0:T(8,128)(2,1)} all-reduce(f32[512,256]{1,0:T(8,128)S(1)} %fusion.52), channel_id=1, replica_groups=mesh['rows'=4,'pts'=8] {'rows'}, use_global_device_ids=true, to_apply=%region_10.11 | all-reduce | flops 131072 | bytes 786432 | tf_op jit(solution)/shard_map/psum | solution.py:110
  194.1 1.7 fusion.12
  195.9 0.2 convolution_convert_fusion.3
  196.1 6.4 %all_gather.13 = bf16[768,256]{1,0:T(8,128)(2,1)S(1)} all-gather(bf16[192,256]{1,0:T(8,128)(2,1)S(1)} %convolution_convert_fusion.3), channel_id=1, replica_groups=mesh['rows'=4,'pts'=8] {'rows'}, dimensions={0}, use_global_device_ids=true | all-gather | bytes 491520 | tf_op jit(solution)/shard_map/all_gather | solution.py:116
  202.5 6.7 %scatter_custom_fusion.1 = f32[1024,256]{1,0:T(8,128)S(1)} fusion(f32[1024,256]{1,0:T(8,128)S(1)} %get-tuple-element.11, s32[768]{0:T(1024)} %compare_select_fusion.7, bf16[768,256]{1,0:T(8,128)(2,1)S(1)} %all_gather.13, f32[]{:T(128)} %constant.16.clone.1), kind=kCustom, calls=%fused_computation.55 | custom fusion | flops 589824 | bytes 1442304 | tf_op jit(solution)/shard_map/scatter-add | solution.py:120
  209.2 8.0 %scatter_custom_fusion = f32[1024,256]{1,0:T(8,128)} fusion(f32[1024,256]{1,0:T(8,128)} %get-tuple-element.10, s32[768]{0:T(1024)} %compare_select_fusion.7, bf16[768,256]{1,0:T(8,128)(2,1)S(1)} %all_gather.13, f32[]{:T(128)} %constant.15.clone.1), kind=kCustom, calls=%fused_computation.54 | custom fusion | flops 589824 | bytes 1442304 | tf_op jit(solution)/shard_map/scatter-add | solution.py:124
  217.2 2.5 multiply_add_fusion
  219.7 1.6 gather_fusion.6
  221.3 1.6 fusion.10
  223.0 0.1 multiply_reduce_fusion.1
  223.2 0.4 fusion.8
  223.5 70.9 %all-reduce.12.cloned.1.call-done = f32[512,256]{1,0:T(8,128)} async-done(((f32[512,256]{1,0:T(8,128)}), f32[512,256]{1,0:T(8,128)}) %all-reduce.12.cloned.1.call-update) | async-done | bytes 524304 | tf_op jit(solution)/shard_map/psum | solution.py:108
  294.5 1.4 fusion.48
  296.0 16.4 %all-reduce.16 = bf16[512,256]{1,0:T(8,128)(2,1)S(1)} all-reduce(f32[512,256]{1,0:T(8,128)S(1)} %fusion.48), channel_id=1, replica_groups=mesh['rows'=4,'pts'=8] {'rows'}, use_global_device_ids=true, to_apply=%region_22.23 | all-reduce | flops 131072 | bytes 786432 | tf_op jit(solution)/shard_map/psum | solution.py:110
  312.3 1.7 fusion.13
  314.0 0.2 convolution_convert_fusion.2
  314.3 6.5 %all_gather.15 = bf16[768,256]{1,0:T(8,128)(2,1)S(1)} all-gather(bf16[192,256]{1,0:T(8,128)(2,1)S(1)} %convolution_convert_fusion.2), channel_id=1, replica_groups=mesh['rows'=4,'pts'=8] {'rows'}, dimensions={0}, use_global_device_ids=true | all-gather | bytes 491520 | tf_op jit(solution)/shard_map/all_gather | solution.py:116
  320.7 6.6 %scatter_custom_fusion.2 = f32[1024,256]{1,0:T(8,128)S(1)} fusion(f32[1024,256]{1,0:T(8,128)S(1)} %get-tuple-element.9, s32[768]{0:T(1024)S(1)} %compare_select_fusion.6, bf16[768,256]{1,0:T(8,128)(2,1)S(1)} %all_gather.15, f32[]{:T(128)} %constant.16.clone.1), kind=kCustom, calls=%fused_computation.56 | custom fusion | flops 589824 | bytes 1441796 | tf_op jit(solution)/shard_map/scatter-add | solution.py:120
  327.4 6.4 %scatter_custom_fusion.3 = f32[1024,256]{1,0:T(8,128)S(1)} fusion(f32[1024,256]{1,0:T(8,128)S(1)} %copy-done.6, s32[768]{0:T(1024)S(1)} %compare_select_fusion.6, bf16[768,256]{1,0:T(8,128)(2,1)S(1)} %all_gather.15, f32[]{:T(128)} %constant.15.clone.1), kind=kCustom, calls=%fused_computation.57 | custom fusion | flops 589824 | bytes 1441796 | tf_op jit(solution)/shard_map/scatter-add | solution.py:124
  333.9 1.0 copy-done.7
  (63 shorter events, 0.4 us)
Async XLA Ops:
  7.2 24.0 %copy-start = (bf16[1024,256]{1,0:T(8,128)(2,1)S(1)}, bf16[1024,256]{1,0:T(8,128)(2,1)}, u32[]{:S(2)}) copy-start(bf16[1024,256]{1,0:T(8,128)(2,1)} %param.8) | copy-start | bytes 1572868
  7.2 92.7 %all-reduce.14.cloned.1.call-start = ((), (), s32[]{:S(2)}) async-start(), calls=%async_computation.2 | async-start | bytes 1048576 | tf_op jit(solution)/shard_map/psum | solution.py:97
  12.0 3.2 copy-start.1
  20.7 4.8 %copy-start.5 = (f32[1024,256]{1,0:T(8,128)S(1)}, f32[1024,256]{1,0:T(8,128)}, u32[]{:S(2)}) copy-start(f32[1024,256]{1,0:T(8,128)} %param.10) | copy-start | bytes 3145732
  20.8 80.1 %copy-start.13 = (pred[512]{0:T(512)(128)(4,1)}, pred[512]{0:T(512)(128)(4,1)S(1)}, u32[]{:S(2)}) copy-start(pred[512]{0:T(512)(128)(4,1)S(1)} %get-tuple-element.22) | copy-start | bytes 1540
  24.0 151.9 %all-reduce.10.cloned.1.call-start = ((), (), s32[]{:S(2)}) async-start(), calls=%async_computation | async-start | bytes 1048576 | tf_op jit(solution)/shard_map/psum | solution.py:108
  25.6 2.5 copy-start.19
  40.6 62.8 %copy-start.15 = (f32[1024]{0:T(1024)}, f32[1024]{0:T(1024)S(1)}, u32[]{:S(2)}) copy-start(f32[1024]{0:T(1024)S(1)} %multiply_reduce_fusion) | copy-start | bytes 12292
  103.5 191.0 %all-reduce.12.cloned.1.call-start = ((), (), s32[]{:S(2)}) async-start(), calls=%async_computation.1 | async-start | bytes 1048576 | tf_op jit(solution)/shard_map/psum | solution.py:108
  104.1 2.6 copy-start.12
  104.1 2.7 copy-start.9
  104.1 3.5 %copy-start.11 = (bf16[512,128]{1,0:T(8,128)(2,1)S(1)}, bf16[512,128]{1,0:T(8,128)(2,1)}, u32[]{:S(2)}) copy-start(bf16[512,128]{1,0:T(8,128)(2,1)} %get-tuple-element.4) | copy-start | bytes 393220
  175.8 18.3 %copy-start.3 = (f32[512,256]{1,0:T(8,128)S(1)}, f32[512,256]{1,0:T(8,128)}, u32[]{:S(2)}) copy-start(f32[512,256]{1,0:T(8,128)} %all-reduce.10.cloned.1.call-done) | copy-start | bytes 1572868
  194.1 1.7 copy-start.14
  219.7 1.6 copy-start.8
  219.7 1.6 copy-start.16
  219.7 1.6 copy-start.18
  221.3 1.7 copy-start.17
  221.3 1.7 copy-start.10
  294.5 17.8 %copy-start.4 = (f32[512,256]{1,0:T(8,128)S(1)}, f32[512,256]{1,0:T(8,128)}, u32[]{:S(2)}) copy-start(f32[512,256]{1,0:T(8,128)} %all-reduce.12.cloned.1.call-done) | copy-start | bytes 1572868
  314.2 13.2 %copy-start.6 = (f32[1024,256]{1,0:T(8,128)S(1)}, f32[1024,256]{1,0:T(8,128)}, u32[]{:S(2)}) copy-start(f32[1024,256]{1,0:T(8,128)} %get-tuple-element.8) | copy-start | bytes 3145732
  327.4 6.5 %copy-start.2 = (f32[1024,256]{1,0:T(8,128)}, f32[1024,256]{1,0:T(8,128)S(1)}, u32[]{:S(2)}) copy-start(f32[1024,256]{1,0:T(8,128)S(1)} %scatter_custom_fusion.2) | copy-start | bytes 3145732
  333.9 1.0 copy-start.7
Sparse Core Ops, SparseCore 0:
  24.1 75.7 all-reduce.13
  104.2 71.5 all-reduce.9
  223.1 71.3 all-reduce.11
where the time goes:
time: 342 us; the launch traced here: 341 us
  waiting for transfers between devices  198 us (58%)
  blocking collectives  53 us (15%)
  other arithmetic  41.4 us (12%)
  local copies, waits for them, and re-layouts  22.2 us (6%)
  between operations  14.9 us (4%)
  matrix products  11.6 us (3%)
    psum x2, waiting for transfers between devices, shards(): resid = lax.psum(partial_value, 'pts')  139 us
    psum x1, waiting for transfers between devices, shards(): lax.psum(row_terms, 'pts').astype(jnp.float32)  59.2 us
    psum x2, blocking collectives, shards(): proj = lax.psum(project_rows(factor, resid), 'rows')  33.2 us
    scatter-add x2, other arithmetic, shards(): momentum_now = (beta_keep * momentum_now + (1.0 - beta_keep) * mixed).at[...  14.5 us
    scatter-add x2, other arithmetic, shards(): current = mixed.at[got_slots].add(-step_size * change, mode='drop')  13.4 us
    all_gather x2, blocking collectives, shards(): lax.all_gather(packed, 'rows', axis=0, tiled=True)  12.8 us
    unnamed x1, blocking collectives  7 us
  transfers between devices with their start and end apart: 3, of which 3 were waited for; matrix products, arithmetic and copies ran while one was open for 4% of the time, Pallas kernels for 0%

commit v1 on v0

v1 whole, which is shorter than its diff:
```python
import jax
import jax.numpy as jnp
from jax import lax
from jax.sharding import PartitionSpec as P

UPDATES = 2


alpha_mix = 0.6
beta_keep = 0.9
step_size = 0.2
momentum_gain = 1.5
ridge_term = 1.0

f32 = jnp.float32
bf16 = jnp.bfloat16


def mm(a, b, ca, cb):
    return lax.dot_general(a, b, (((ca,), (cb,)), ((), ())), preferred_element_type=f32)


def kernel_tile(left_rows, right_rows):
    inner_prod = mm(left_rows, right_rows, 1, 1)
    left_sq = jnp.sum(jnp.square(left_rows.astype(f32)), axis=1)
    right_sq = jnp.sum(jnp.square(right_rows.astype(f32)), axis=1)
    squared = left_sq[:, None] + right_sq[None, :] - 2.0 * inner_prod
    return jnp.exp(squared * (-3.5 / left_rows.shape[1])).astype(bf16)


def split_two(value):
    high = value.astype(bf16)
    return high, (value - high.astype(f32)).astype(bf16)


def shards(features, targets, coefficients, momentum, block_index, pivot_index, nystrom_core):
    row_count = lax.axis_size("rows")
    pts_count = lax.axis_size("pts")
    row_id = lax.axis_index("rows")
    pts_id = lax.axis_index("pts")
    local_points = features.shape[0]
    block = block_index.shape[1]
    rank = pivot_index.shape[1]
    outputs = coefficients.shape[1]
    per_row = block // row_count
    per_device = per_row // pts_count
    row_cols = outputs // row_count
    own_cols = row_cols // pts_count
    first_point = pts_id * local_points
    points = lax.broadcasted_iota(jnp.int32, (local_points, 1), 0) + first_point

    place = [(points == block_index[u][None, :]).astype(bf16) for u in range(UPDATES)]

    own_rows = []
    for u in range(UPDATES):
        mine = lax.dynamic_slice_in_dim(place[u], row_id * per_row, per_row, axis=1)
        own_rows.append(mm(mine, features, 0, 0).astype(bf16).reshape(pts_count, per_device, -1))
    sent = jnp.concatenate(own_rows, axis=1)
    came = lax.all_to_all(sent, "pts", 0, 0, tiled=False)
    chunk = jnp.sum(came.astype(f32), axis=0).astype(bf16)
    over_pts = lax.all_gather(chunk, "pts", axis=0, tiled=False)
    over_rows = lax.all_gather(over_pts, "rows", axis=0, tiled=False)
    over_rows = over_rows.reshape(row_count, pts_count, UPDATES, per_device, features.shape[1])
    block_feats = [over_rows[:, :, u].reshape(block, features.shape[1]) for u in range(UPDATES)]

    first_col = row_id * row_cols
    current = lax.dynamic_slice_in_dim(coefficients, first_col, row_cols, axis=1).T
    moving = lax.dynamic_slice_in_dim(momentum, first_col, row_cols, axis=1).T
    goal = lax.dynamic_slice_in_dim(targets, first_col, row_cols, axis=1).T.astype(f32)

    all_steps = []
    for u in range(UPDATES):
        mixed = alpha_mix * moving + (1.0 - alpha_mix) * current
        high, low = split_two(ridge_term * mixed - goal)
        tile = kernel_tile(features, block_feats[u])
        partial_value = (
            mm(mixed.astype(bf16), tile, 1, 0) + mm(high, place[u], 1, 0) + mm(low, place[u], 1, 0)
        )
        pieces = partial_value.astype(bf16).reshape(pts_count, own_cols, block)
        summed = lax.all_to_all(pieces, "pts", 0, 0, tiled=False)
        resid = jnp.sum(summed.astype(f32), axis=0)
        at_pivot = (
            lax.broadcasted_iota(jnp.int32, (block, 1), 0) == pivot_index[u][None, :]
        ).astype(bf16)
        pivot_feats = mm(at_pivot, block_feats[u], 0, 0).astype(bf16)
        factor = kernel_tile(block_feats[u], pivot_feats)
        proj = mm(resid.astype(bf16), factor, 1, 0)
        lifted = mm(proj.astype(bf16), nystrom_core[u], 1, 1).astype(bf16)
        step_bf = (resid - mm(lifted, factor, 1, 1)).astype(bf16)
        steps = lax.all_gather(step_bf, "pts", axis=0, tiled=True)
        change = mm(steps, place[u], 1, 1)
        all_steps.append(change.astype(bf16))
        current = mixed - step_size * change
        moving = beta_keep * moving + (1.0 - beta_keep) * mixed - step_size * momentum_gain * change

    gathered = lax.all_gather(jnp.stack(all_steps), "rows", axis=1, tiled=True)
    current = coefficients
    moving = momentum
    for u in range(UPDATES):
        change = gathered[u].T.astype(f32)
        mixed = alpha_mix * moving + (1.0 - alpha_mix) * current
        current = mixed - step_size * change
        moving = beta_keep * moving + (1.0 - beta_keep) * mixed - step_size * momentum_gain * change
    return (current, moving)


def solution(mesh):
    in_specs = (P("pts", None), P("pts", None), P("pts", None), P("pts", None), P(), P(), P())
    out_specs = (P("pts", None), P("pts", None))
    return jax.shard_map(shards, mesh=mesh, in_specs=in_specs, out_specs=out_specs, check_vma=False)
```

time: 342 us -> 222 us (0.65)
  waiting for transfers between devices: 198 us -> 39.3 us
  blocking collectives: 53 us -> 111 us
  other arithmetic: 41.4 us -> 8.36 us
  matrix products: 11.6 us -> 28.8 us
  local copies, waits for them, and re-layouts: 22.2 us -> 10.6 us
  starting transfers between devices: 0.12 us -> 9.06 us
    psum x3 -> x0, waiting for transfers between devices: 198 us -> none  [the longest x2 139 us: shards(): resid = lax.psum(partial_value, 'pts')]
    all_gather x2 -> x3, blocking collectives: 12.8 us -> 95 us  [the longest x2 62.2 us: shards(): steps = lax.all_gather(step_bf, 'pts', axis=0, tiled=True)]
    psum x2 -> x0, blocking collectives: 33.2 us -> none  [shards(): proj = lax.psum(project_rows(factor, resid), 'rows')]
    scatter-add x4 -> x0, other arithmetic: 27.8 us -> none  [the longest x2 14.5 us: shards(): momentum_now = (beta_keep * momentum_now + (1.0 - beta_keep) * mixed).at[...]
    all_gather x0 -> x2, waiting for transfers between devices: none -> 25.8 us  [the longest x1 14.3 us: shards(): gathered = lax.all_gather(jnp.stack(all_steps), 'rows', axis=1, tiled=True)]
    gather x10 -> x0, local copies, waits for them, and re-layouts: 19.3 us -> none  [the longest x2 6.29 us: shards(): pivot_points = whole_index[pivot_index[update]]]
    dot_general x10 -> x18, matrix products: 11.6 us -> 28.8 us  [mm(): lax.dot_general(a, b, (((ca,), (cb,)), ((), ())), preferred_element_type=...]
    all_to_all x0 -> x1, blocking collectives: none -> 16 us  [shards(): came = lax.all_to_all(sent, 'pts', 0, 0, tiled=False)]
  transfers between devices with their start and end apart: 3 -> 4, of which waited for: 3 -> 4; matrix products, arithmetic and copies ran while one was open for 4% -> 4% of each run, Pallas kernels for 0% -> 0%
where the time goes in v1:
time: 222 us; the launch traced here: 221 us
  blocking collectives  111 us (50%)
  waiting for transfers between devices  39.3 us (18%)
  matrix products  28.8 us (13%)
  between operations  14.3 us (6%)
  local copies, waits for them, and re-layouts  10.6 us (5%)
  starting transfers between devices  9.06 us (4%)
  other arithmetic  8.36 us (4%)
    all_gather x2, blocking collectives, shards(): steps = lax.all_gather(step_bf, 'pts', axis=0, tiled=True)  62.2 us
    all_gather x1, blocking collectives, shards(): over_pts = lax.all_gather(chunk, 'pts', axis=0, tiled=False)  32.8 us
    dot_general x18, matrix products, mm(): lax.dot_general(a, b, (((ca,), (cb,)), ((), ())), preferred_element_type=...  28.8 us
    all_to_all x1, blocking collectives, shards(): came = lax.all_to_all(sent, 'pts', 0, 0, tiled=False)  16 us
    all_gather x1, waiting for transfers between devices, shards(): gathered = lax.all_gather(jnp.stack(all_steps), 'rows', axis=1, tiled=True)  14.3 us
    all_to_all x2, waiting for transfers between devices, shards(): summed = lax.all_to_all(pieces, 'pts', 0, 0, tiled=False)  13.5 us
    all_gather x1, waiting for transfers between devices, shards(): over_rows = lax.all_gather(over_pts, 'rows', axis=0, tiled=False)  11.5 us
    all_to_all x2, starting transfers between devices, shards(): summed = lax.all_to_all(pieces, 'pts', 0, 0, tiled=False)  8.99 us
  transfers between devices with their start and end apart: 4, of which 4 were waited for; matrix products, arithmetic and copies ran while one was open for 4% of the time, Pallas kernels for 0%

profile of v1, /device:TPU:0, one launch (start us, length us, event | category | flops | bytes accessed | tf_op | source)
XLA Modules:
  0.0 221.5 jit_solution(7223261956274164094)
XLA Ops:
  7.2 0.0 copy-start
  7.2 0.0 all-gather.7.cloned.1.call-start
  7.2 0.8 fusion.115
  8.1 0.0 copy-start.10
  8.1 2.6 %broadcast_compare_fusion.1 = (pred[1024,2048]{1,0:T(32,128)(4,1)S(1)}, pred[1024,2048]{1,0:T(32,128)(4,1)S(1)}) fusion(s32[2048]{0:T(1024)S(1)} %bitcast.175, s32[1024]{0:T(1024)S(1)} %iota_add_fusion, s32[2048]{0:T(1024)S(1)} %bitcast.171), kind=kLoop, calls=%fused_computation.31 | loop fusion | flops 4194304 | bytes 4214784 | tf_op jit(solution)/shard_map/eq | solution.py:52
  10.7 0.0 copy-start.7
  10.7 0.0 copy-done.10
  10.7 0.8 fusion.69
  11.5 0.8 fusion.66
  12.3 16.0 %all_to_all.15 = bf16[8,128,128]{2,1,0:T(8,128)(2,1)S(1)} all-to-all(bf16[8,128,128]{2,1,0:T(8,128)(2,1)S(1)} %pad_maximum_fusion), channel_id=1, replica_groups=mesh['rows'=4,'pts'=8] {'pts'}, dimensions={0} | all-to-all | bytes 524288 | tf_op jit(solution)/shard_map/all_to_all | solution.py:59
  28.4 32.8 %all-gather = bf16[1024,128]{1,0:T(8,128)(2,1)} all-gather(bf16[128,128]{1,0:T(8,128)(2,1)S(1)} %reduce_sum.88), channel_id=2, replica_groups=mesh['rows'=4,'pts'=8] {'pts'}, dimensions={0}, use_global_device_ids=true | all-gather | bytes 294912 | tf_op jit(solution)/shard_map/all_gather | solution.py:61
  61.2 0.0 all-gather.7.cloned.1.call-update
  61.2 0.0 copy-done.7
  61.2 0.3 copy.17
  61.5 0.0 copy-start.1
  61.5 0.0 copy-start.18
  61.6 1.9 copy.19
  63.5 0.0 copy-start.3
  63.5 0.0 copy-done
  63.5 0.1 constant_dynamic-slice_fusion
  63.7 0.8 copy.25
  64.5 0.8 multiply_add_fusion.1
  65.3 0.2 multiply_reduce_fusion.2
  65.5 0.0 copy-done.18
  65.5 11.5 %all-gather.7.cloned.1.call-done = bf16[32,128,128]{2,1,0:T(8,128)(2,1)} async-done(((bf16[8,128,128]{2,1,0:T(8,128)(2,1)}), bf16[32,128,128]{2,1,0:T(8,128)(2,1)}) %all-gather.7.cloned.1.call-update) | async-done | bytes 1048592 | tf_op jit(solution)/shard_map/all_gather | solution.py:62
  77.0 2.2 %fusion.114 = (bf16[4,8,1,64,128]{4,3,2,1,0:T(8,128)(2,1)}, bf16[4,8,1,64,128]{4,3,2,1,0:T(8,128)(2,1)S(1)}) fusion(bf16[4,8,2,64,128]{4,3,2,1,0:T(8,128)(2,1)} %bitcast.160), kind=kLoop, calls=%fused_computation.125 | loop fusion | bytes 2097152 | tf_op jit(solution)/shard_map/slice | solution.py:64
  79.2 0.0 copy-done.1
  79.2 0.0 copy-done.6
  79.2 0.6 multiply_reduce_fusion.1
  79.9 0.0 copy-done.3
  79.9 0.1 add.129
  79.9 0.1 add.119
  80.0 3.6 %fusion.64 = f32[64,2048]{1,0:T(8,128)S(1)} fusion(bf16[2048,128]{1,0:T(8,128)(2,1)} %bitcast.166, bf16[1024,128]{1,0:T(8,128)(2,1)S(1)} %copy-done.11, f32[2048]{0:T(1024)S(1)} %add.119, f32[1024]{0:T(1024)S(1)} %multiply_reduce_fusion.2, f32[1024,64]{0,1:T(8,128)} %multiply_add_fusion.1), kind=kOutput, calls=%fused_computation.58 | convolution fusion | flops 815792128 | bytes 1585152 | tf_op jit(solution)/shard_map/dot_general | solution.py:20
  83.7 1.6 fusion.32
  85.3 2.3 %fusion.50 = bf16[8,8,2048]{2,1,0:T(8,128)(2,1)} fusion(f32[64,2048]{1,0:T(8,128)S(1)} %fusion.32, s32[2048]{0:T(1024)S(1)} %bitcast.177, s32[1024]{0:T(1024)S(1)} %iota_add_fusion, bf16[1024,64]{0,1:T(8,128)(2,1)S(1)} %copy-done.15, f32[1024,64]{0,1:T(8,128)S(1)} %copy-done.13), kind=kOutput, calls=%fused_computation.46 | convolution fusion | flops 271187968 | bytes 1191936 | tf_op jit(solution)/shard_map/dot_general | solution.py:20
  87.6 5.5 %all-to-all-start.1 = ((bf16[8,8,2048]{2,1,0:T(8,128)(2,1)}), bf16[8,8,2048]{2,1,0:T(8,128)(2,1)S(1)}, u32[]{:S(2)}, u32[]{:S(2)}) async-start(bf16[8,8,2048]{2,1,0:T(8,128)(2,1)} %fusion.50), calls=%async_computation.1 | async-start | bytes 524288 | tf_op jit(solution)/shard_map/all_to_all | solution.py:80
  93.2 0.9 multiply_reduce_fusion.4
  94.1 0.1 copy-done.9
  94.2 1.0 exponential_convert_fusion.1
  95.2 7.2 %all-to-all-done.1 = bf16[8,8,2048]{2,1,0:T(8,128)(2,1)S(1)} async-done(((bf16[8,8,2048]{2,1,0:T(8,128)(2,1)}), bf16[8,8,2048]{2,1,0:T(8,128)(2,1)S(1)}, u32[]{:S(2)}, u32[]{:S(2)}) %all-to-all-start.1) | async-done | bytes 262176 | tf_op jit(solution)/shard_map/all_to_all | solution.py:80
  102.5 1.6 convolution_convert_fusion.3
  104.1 0.7 fusion.56
  104.8 31.0 %all_gather.25 = bf16[64,2048]{1,0:T(8,128)(2,1)S(1)} all-gather(bf16[8,2048]{1,0:T(8,128)(2,1)S(1)} %fusion.56), channel_id=1, replica_groups=mesh['rows'=4,'pts'=8] {'pts'}, dimensions={0}, use_global_device_ids=true | all-gather | bytes 294912 | tf_op jit(solution)/shard_map/all_gather | solution.py:90
  135.8 3.3 %convert_bitcast_fusion = (bf16[1,64,1024]{2,1,0:T(8,128)(2,1)}, f32[64,1024]{1,0:T(8,128)S(1)}) fusion(f32[1024,64]{0,1:T(8,128)S(1)} %copy-done.14, f32[1024,256]{0,1:T(8,128)} %copy-done.1, s32[]{:T(128)S(6)} %select_n.4, bf16[64,2048]{1,0:T(8,128)(2,1)S(1)} %all_gather.25, s32[2048]{0:T(1024)S(1)} %bitcast.178, s32[1024]{0:T(1024)S(1)} %iota_add_fusion), kind=kOutput, calls=%fused_computation.114 | convolution fusion | flops 271253504 | bytes 1191940 | tf_op jit(solution)/shard_map/dot_general | solution.py:20
  139.0 2.5 %fusion.65 = f32[64,2048]{1,0:T(8,128)S(1)} fusion(bf16[2048,128]{1,0:T(8,128)(2,1)S(1)} %bitcast.163, bf16[1024,128]{1,0:T(8,128)(2,1)S(1)} %copy-done.12, f32[2048]{0:T(1024)S(1)} %add.129, f32[1024]{0:T(1024)S(1)} %multiply_reduce_fusion.2, f32[64,1024]{1,0:T(8,128)S(1)} %get-tuple-element.13), kind=kOutput, calls=%fused_computation.59 | convolution fusion | flops 815857664 | bytes 1585152 | tf_op jit(solution)/shard_map/dot_general | solution.py:20
  141.5 1.6 fusion.38
  143.1 2.3 %fusion.53 = bf16[8,8,2048]{2,1,0:T(8,128)(2,1)} fusion(f32[64,2048]{1,0:T(8,128)S(1)} %fusion.38, s32[2048]{0:T(1024)S(1)} %bitcast.173, s32[1024]{0:T(1024)S(1)} %iota_add_fusion, f32[64,1024]{1,0:T(8,128)S(1)} %get-tuple-element.13, bf16[1024,64]{0,1:T(8,128)(2,1)S(1)} %copy-done.16), kind=kOutput, calls=%fused_computation.47 | convolution fusion | flops 271187968 | bytes 1191936 | tf_op jit(solution)/shard_map/dot_general | solution.py:20
  145.5 3.5 %all-to-all-start.2 = ((bf16[8,8,2048]{2,1,0:T(8,128)(2,1)}), bf16[8,8,2048]{2,1,0:T(8,128)(2,1)S(1)}, u32[]{:S(2)}, u32[]{:S(2)}) async-start(bf16[8,8,2048]{2,1,0:T(8,128)(2,1)} %fusion.53), calls=%async_computation.2 | async-start | bytes 524288 | tf_op jit(solution)/shard_map/all_to_all | solution.py:80
  149.0 0.0 all-gather.5.cloned.1.call-start
  149.0 0.9 multiply_reduce_fusion.3
  149.9 1.0 exponential_convert_fusion
  150.9 6.2 %all-to-all-done.2 = bf16[8,8,2048]{2,1,0:T(8,128)(2,1)S(1)} async-done(((bf16[8,8,2048]{2,1,0:T(8,128)(2,1)}), bf16[8,8,2048]{2,1,0:T(8,128)(2,1)S(1)}, u32[]{:S(2)}, u32[]{:S(2)}) %all-to-all-start.2) | async-done | bytes 262176 | tf_op jit(solution)/shard_map/all_to_all | solution.py:80
  157.2 1.6 convolution_convert_fusion.2
  158.8 0.7 fusion.57
  159.5 0.0 copy-start.4
  159.5 31.2 %all_gather.26 = bf16[64,2048]{1,0:T(8,128)(2,1)S(1)} all-gather(bf16[8,2048]{1,0:T(8,128)(2,1)S(1)} %fusion.57), channel_id=1, replica_groups=mesh['rows'=4,'pts'=8] {'pts'}, dimensions={0}, use_global_device_ids=true | all-gather | bytes 294912 | tf_op jit(solution)/shard_map/all_gather | solution.py:90
  190.7 1.6 fusion.77
  192.3 0.7 pad_maximum_fusion.1
  193.1 0.0 all-gather.5.cloned.1.call-update
  193.1 14.3 %all-gather.5.cloned.1.call-done = bf16[2,256,1024]{2,1,0:T(8,128)(2,1)} async-done(((bf16[2,64,1024]{2,1,0:T(8,128)(2,1)}), bf16[2,256,1024]{2,1,0:T(8,128)(2,1)}) %all-gather.5.cloned.1.call-update) | async-done | bytes 1048592 | tf_op jit(solution)/shard_map/all_gather | solution.py:96
  207.4 0.0 copy-done.2
  207.4 3.3 %fusion.89 = (f32[1024,256]{0,1:T(8,128)}, f32[1024,256]{0,1:T(8,128)}) fusion(f32[1024,256]{0,1:T(8,128)S(1)} %copy-done.2, f32[1024,256]{0,1:T(8,128)S(1)} %copy-done.4, bf16[2,256,1024]{2,1,0:T(8,128)(2,1)} %all-gather.5.cloned.1.call-done), kind=kLoop, calls=%fused_computation.83 | loop fusion | flops 5767168 | bytes 5242880 | tf_op jit(solution)/shard_map/sub | solution.py:103
  210.7 2.6 %copy.23 = f32[1024,256]{1,0:T(8,128)} copy(f32[1024,256]{0,1:T(8,128)} %get-tuple-element.9) | data formatting | bytes 2097152
  213.3 1.3 copy.24
  (28 shorter events, 0.2 us)
Async XLA Ops:
  7.2 56.4 %copy-start = (bf16[1024,256]{1,0:T(8,128)(2,1)S(1)}, bf16[1024,256]{1,0:T(8,128)(2,1)}, u32[]{:S(2)}) copy-start(bf16[1024,256]{1,0:T(8,128)(2,1)} %param.8) | copy-start | bytes 1572868
  7.2 69.8 %all-gather.7.cloned.1.call-start = ((), (), s32[]{:S(2)}) async-start(), calls=%async_computation.4 | async-start | bytes 1310720 | tf_op jit(solution)/shard_map/all_gather | solution.py:62
  8.1 2.7 %copy-start.10 = (bf16[1024,128]{1,0:T(8,128)(2,1)S(1)}, bf16[1024,128]{1,0:T(8,128)(2,1)}, u32[]{:S(2)}) copy-start(bf16[1024,128]{1,0:T(8,128)(2,1)} %param.7) | copy-start | bytes 786436
  10.7 50.5 %copy-start.7 = (f32[1024,256]{1,0:T(8,128)S(1)}, f32[1024,256]{1,0:T(8,128)}, u32[]{:S(2)}) copy-start(f32[1024,256]{1,0:T(8,128)} %param.10) | copy-start | bytes 3145732
  61.5 17.7 %copy-start.1 = (f32[1024,256]{0,1:T(8,128)}, f32[1024,256]{0,1:T(8,128)S(1)}, u32[]{:S(2)}) copy-start(f32[1024,256]{0,1:T(8,128)S(1)} %copy.17) | copy-start | bytes 3145732
  61.5 4.0 %copy-start.18 = (s32[2,512]{1,0:T(2,128)S(1)}, s32[2,512]{1,0:T(2,128)}, u32[]{:S(2)}) copy-start(s32[2,512]{1,0:T(2,128)} %param.12) | copy-start | bytes 12292
  63.5 16.4 %copy-start.3 = (f32[1024,256]{0,1:T(8,128)}, f32[1024,256]{0,1:T(8,128)S(1)}, u32[]{:S(2)}) copy-start(f32[1024,256]{0,1:T(8,128)S(1)} %copy.19) | copy-start | bytes 3145732
  64.5 15.5 %copy-start.11 = (bf16[1024,128]{1,0:T(8,128)(2,1)S(1)}, bf16[1024,128]{1,0:T(8,128)(2,1)}, u32[]{:S(2)}) copy-start(bf16[1024,128]{1,0:T(8,128)(2,1)} %param.7) | copy-start | bytes 786436
  77.0 2.2 %copy-start.6 = (bf16[32,128,128]{2,1,0:T(8,128)(2,1)S(1)}, bf16[32,128,128]{2,1,0:T(8,128)(2,1)}, u32[]{:S(2)}) copy-start(bf16[32,128,128]{2,1,0:T(8,128)(2,1)} %all-gather.7.cloned.1.call-done) | copy-start | bytes 3145732
  80.0 3.7 %copy-start.13 = (f32[1024,64]{0,1:T(8,128)S(1)}, f32[1024,64]{0,1:T(8,128)}, u32[]{:S(2)}) copy-start(f32[1024,64]{0,1:T(8,128)} %multiply_add_fusion.1) | copy-start | bytes 786436
  80.0 3.7 %copy-start.15 = (bf16[1024,64]{0,1:T(8,128)(2,1)S(1)}, bf16[1024,64]{0,1:T(8,128)(2,1)}, u32[]{:S(2)}) copy-start(bf16[1024,64]{0,1:T(8,128)(2,1)} %copy.25) | copy-start | bytes 393220
  85.3 7.9 %copy-start.8 = (bf16[4,8,1,64,128]{4,3,2,1,0:T(8,128)(2,1)S(1)}, bf16[4,8,1,64,128]{4,3,2,1,0:T(8,128)(2,1)}, u32[]{:S(2)}) copy-start(bf16[4,8,1,64,128]{4,3,2,1,0:T(8,128)(2,1)} %get-tuple-element.10) | copy-start | bytes 1572868
  87.6 14.8 %all-to-all-start.1 = ((bf16[8,8,2048]{2,1,0:T(8,128)(2,1)}), bf16[8,8,2048]{2,1,0:T(8,128)(2,1)S(1)}, u32[]{:S(2)}, u32[]{:S(2)}) async-start(bf16[8,8,2048]{2,1,0:T(8,128)(2,1)} %fusion.50), calls=%async_computation.1 | async-start | bytes 524288 | tf_op jit(solution)/shard_map/all_to_all | solution.py:80
  93.1 1.0 copy-start.9
  104.1 31.7 %copy-start.14 = (f32[1024,64]{0,1:T(8,128)S(1)}, f32[1024,64]{0,1:T(8,128)}, u32[]{:S(2)}) copy-start(f32[1024,64]{0,1:T(8,128)} %multiply_add_fusion.1) | copy-start | bytes 786436
  104.7 34.3 %copy-start.12 = (bf16[1024,128]{1,0:T(8,128)(2,1)S(1)}, bf16[1024,128]{1,0:T(8,128)(2,1)}, u32[]{:S(2)}) copy-start(bf16[1024,128]{1,0:T(8,128)(2,1)} %param.7) | copy-start | bytes 786436
  139.0 2.5 %copy-start.16 = (bf16[1024,64]{0,1:T(8,128)(2,1)S(1)}, bf16[1024,64]{0,1:T(8,128)(2,1)}, u32[]{:S(2)}) copy-start(bf16[1024,64]{0,1:T(8,128)(2,1)} %copy.25) | copy-start | bytes 393220
  145.5 11.7 %all-to-all-start.2 = ((bf16[8,8,2048]{2,1,0:T(8,128)(2,1)}), bf16[8,8,2048]{2,1,0:T(8,128)(2,1)S(1)}, u32[]{:S(2)}, u32[]{:S(2)}) async-start(bf16[8,8,2048]{2,1,0:T(8,128)(2,1)} %fusion.53), calls=%async_computation.2 | async-start | bytes 524288 | tf_op jit(solution)/shard_map/all_to_all | solution.py:80
  149.0 58.5 %all-gather.5.cloned.1.call-start = ((), (), s32[]{:S(2)}) async-start(), calls=%async_computation.3 | async-start | bytes 1310720 | tf_op jit(solution)/shard_map/all_gather | solution.py:96
  159.5 32.8 %copy-start.17 = (bf16[1,64,1024]{2,1,0:T(8,128)(2,1)S(1)}, bf16[1,64,1024]{2,1,0:T(8,128)(2,1)}, u32[]{:S(2)}) copy-start(bf16[1,64,1024]{2,1,0:T(8,128)(2,1)} %get-tuple-element.12) | copy-start | bytes 393220
  159.5 47.9 %copy-start.2 = (f32[1024,256]{0,1:T(8,128)S(1)}, f32[1024,256]{0,1:T(8,128)}, u32[]{:S(2)}) copy-start(f32[1024,256]{0,1:T(8,128)} %copy-done.1) | copy-start | bytes 3145732
  159.5 47.9 %copy-start.4 = (f32[1024,256]{0,1:T(8,128)S(1)}, f32[1024,256]{0,1:T(8,128)}, u32[]{:S(2)}) copy-start(f32[1024,256]{0,1:T(8,128)} %copy-done.3) | copy-start | bytes 3145732
  210.7 2.6 %copy-start.5 = (f32[1024,256]{0,1:T(8,128)S(1)}, f32[1024,256]{0,1:T(8,128)}, u32[]{:S(2)}) copy-start(f32[1024,256]{0,1:T(8,128)} %get-tuple-element.8) | copy-start | bytes 3145732
Sparse Core Ops, SparseCore 0:
  61.3 15.6 all-gather.6
  193.2 14.1 all-gather.4

commit v2 on v1

--- a/solution.py
+++ b/solution.py
@@ -33,6 +33,16 @@
     return high, (value - high.astype(f32)).astype(bf16)
 
 
+def gather_direct(value, axis):
+    count = lax.axis_size(axis)
+    me = lax.axis_index(axis)
+    held = [value]
+    for away in range(1, count):
+        held.append(lax.ppermute(value, axis, [(i, (i - away) % count) for i in range(count)]))
+    twice = jnp.stack(held + held)
+    return lax.dynamic_slice_in_dim(twice, (count - me) % count, count, axis=0)
+
+
 def shards(features, targets, coefficients, momentum, block_index, pivot_index, nystrom_core):
     row_count = lax.axis_size("rows")
     pts_count = lax.axis_size("pts")
@@ -58,8 +68,8 @@
     sent = jnp.concatenate(own_rows, axis=1)
     came = lax.all_to_all(sent, "pts", 0, 0, tiled=False)
     chunk = jnp.sum(came.astype(f32), axis=0).astype(bf16)
-    over_pts = lax.all_gather(chunk, "pts", axis=0, tiled=False)
-    over_rows = lax.all_gather(over_pts, "rows", axis=0, tiled=False)
+    over_pts = gather_direct(chunk, "pts")
+    over_rows = gather_direct(over_pts, "rows")
     over_rows = over_rows.reshape(row_count, pts_count, UPDATES, per_device, features.shape[1])
     block_feats = [over_rows[:, :, u].reshape(block, features.shape[1]) for u in range(UPDATES)]
 
@@ -87,13 +97,14 @@
         proj = mm(resid.astype(bf16), factor, 1, 0)
         lifted = mm(proj.astype(bf16), nystrom_core[u], 1, 1).astype(bf16)
         step_bf = (resid - mm(lifted, factor, 1, 1)).astype(bf16)
-        steps = lax.all_gather(step_bf, "pts", axis=0, tiled=True)
+        steps = gather_direct(step_bf, "pts").reshape(row_cols, block)
         change = mm(steps, place[u], 1, 1)
         all_steps.append(change.astype(bf16))
         current = mixed - step_size * change
         moving = beta_keep * moving + (1.0 - beta_keep) * mixed - step_size * momentum_gain * change
 
-    gathered = lax.all_gather(jnp.stack(all_steps), "rows", axis=1, tiled=True)
+    gathered = gather_direct(jnp.stack(all_steps), "rows")
+    gathered = gathered.transpose(1, 0, 2, 3).reshape(UPDATES, outputs, local_points)
     current = coefficients
     moving = momentum
     for u in range(UPDATES):

time: 222 us -> 174 us (0.78)
  blocking collectives: 111 us -> 0 us
  starting transfers between devices: 9.06 us -> 44.5 us
  local copies, waits for them, and re-layouts: 10.6 us -> 30.3 us
  waiting for transfers between devices: 39.3 us -> 53.9 us
  between operations: 14.3 us -> 1.33 us
  other arithmetic: 8.36 us -> 12.1 us
    all_gather x3 -> x0, blocking collectives: 95 us -> none  [the longest x2 62.2 us: shards(): steps = lax.all_gather(step_bf, 'pts', axis=0, tiled=True)]
    ppermute x0 -> x27, waiting for transfers between devices: none -> 34.2 us  [gather_direct(): lax.ppermute(value, axis, [(i, (i - away) % count) for i in range(count)])]
    ppermute x0 -> x27, starting transfers between devices: none -> 30 us  [gather_direct(): lax.ppermute(value, axis, [(i, (i - away) % count) for i in range(count)])]
    all_gather x2 -> x0, waiting for transfers between devices: 25.8 us -> none  [the longest x1 14.3 us: shards(): gathered = lax.all_gather(jnp.stack(all_steps), 'rows', axis=1, tiled=True)]
    all_to_all x1 -> x0, blocking collectives: 16 us -> none  [shards(): came = lax.all_to_all(sent, 'pts', 0, 0, tiled=False)]
    unnamed x43 -> x110, local copies, waits for them, and re-layouts: 7.27 us -> 16.9 us
    all_to_all x0 -> x1, waiting for transfers between devices: none -> 8.31 us  [shards(): came = lax.all_to_all(sent, 'pts', 0, 0, tiled=False)]
    mul x0 -> x4, local copies, waits for them, and re-layouts: none -> 7.73 us  [the longest x2 5.09 us: shards(): step_size * momentum_gain * change]
  transfers between devices with their start and end apart: 4 -> 30, of which waited for: 4 -> 18; matrix products, arithmetic and copies ran while one was open for 4% -> 9% of each run, Pallas kernels for 0% -> 0%
where the time goes in v2:
time: 174 us; the launch traced here: 173 us
  waiting for transfers between devices  53.9 us (31%)
  starting transfers between devices  44.5 us (26%)
  matrix products  30.7 us (18%)
  local copies, waits for them, and re-layouts  30.3 us (17%)
  other arithmetic  12.1 us (7%)
    ppermute x27, waiting for transfers between devices, gather_direct(): lax.ppermute(value, axis, [(i, (i - away) % count) for i in range(count)])  34.2 us
    dot_general x18, matrix products, mm(): lax.dot_general(a, b, (((ca,), (cb,)), ((), ())), preferred_element_type=...  30.7 us
    ppermute x27, starting transfers between devices, gather_direct(): lax.ppermute(value, axis, [(i, (i - away) % count) for i in range(count)])  30 us
    unnamed x110, local copies, waits for them, and re-layouts  16.9 us
    all_to_all x2, waiting for transfers between devices, shards(): summed = lax.all_to_all(pieces, 'pts', 0, 0, tiled=False)  11.3 us
    all_to_all x1, waiting for transfers between devices, shards(): came = lax.all_to_all(sent, 'pts', 0, 0, tiled=False)  8.31 us
    all_to_all x1, starting transfers between devices, shards(): came = lax.all_to_all(sent, 'pts', 0, 0, tiled=False)  7.28 us
    all_to_all x2, starting transfers between devices, shards(): summed = lax.all_to_all(pieces, 'pts', 0, 0, tiled=False)  7.23 us
  transfers between devices with their start and end apart: 30, of which 18 were waited for; matrix products, arithmetic and copies ran while one was open for 9% of the time, Pallas kernels for 0%

profile of v2, /device:TPU:0, one launch (start us, length us, event | category | flops | bytes accessed | tf_op | source)
XLA Modules:
  0.0 172.8 jit_solution(6044211261240861315)
XLA Ops:
  0.6 0.8 fusion.112
  1.5 2.6 %broadcast_compare_fusion.1 = (pred[1024,2048]{1,0:T(32,128)(4,1)S(1)}, pred[1024,2048]{1,0:T(32,128)(4,1)S(1)}) fusion(s32[2048]{0:T(1024)S(1)} %bitcast.260, s32[1024]{0:T(1024)S(1)} %iota_add_fusion, s32[2048]{0:T(1024)S(1)} %bitcast.256), kind=kLoop, calls=%fused_computation.31 | loop fusion | flops 4194304 | bytes 4214784 | tf_op jit(solution)/shard_map/eq | solution.py:62
  4.2 0.8 fusion.69
  6.5 7.3 %all-to-all-start = ((bf16[8,128,128]{2,1,0:T(8,128)(2,1)}), bf16[8,128,128]{2,1,0:T(8,128)(2,1)S(1)}, u32[]{:S(2)}, u32[]{:S(2)}) async-start(bf16[8,128,128]{2,1,0:T(8,128)(2,1)} %pad_maximum_fusion), calls=%async_computation | async-start | bytes 524288 | tf_op jit(solution)/shard_map/all_to_all | solution.py:69
  14.4 8.3 %all-to-all-done = bf16[8,128,128]{2,1,0:T(8,128)(2,1)S(1)} async-done(((bf16[8,128,128]{2,1,0:T(8,128)(2,1)}), bf16[8,128,128]{2,1,0:T(8,128)(2,1)S(1)}, u32[]{:S(2)}, u32[]{:S(2)}) %all-to-all-start) | async-done | bytes 262176 | tf_op jit(solution)/shard_map/all_to_all | solution.py:69
  22.8 2.4 %collective-permute-start = (bf16[128,128]{1,0:T(8,128)(2,1)S(1)}, bf16[128,128]{1,0:T(8,128)(2,1)S(1)}, u32[]{:S(2)}, u32[]{:S(2)}) collective-permute-start(bf16[128,128]{1,0:T(8,128)(2,1)S(1)} %reduce_sum.88), channel_id=1, source_target_pairs={{0,7},{1,0},{2,1},{3,2},{4,3},{5,4},{6,5},{7,6},{8,15},{9,8},{10,9... | collective-permute-start | bytes 98312 | tf_op jit(solution)/shard_map/ppermute | solution.py:41
  25.1 1.7 collective-permute-start.2
  26.8 1.5 collective-permute-start.3
  28.3 1.7 %collective-permute-start.4 = (bf16[128,128]{1,0:T(8,128)(2,1)S(1)}, bf16[128,128]{1,0:T(8,128)(2,1)S(1)}, u32[]{:S(2)}, u32[]{:S(2)}) collective-permute-start(bf16[128,128]{1,0:T(8,128)(2,1)S(1)} %reduce_sum.88), channel_id=1, source_target_pairs={{0,3},{1,4},{2,5},{3,6},{4,7},{5,0},{6,1},{7,2},{8,11},{9,12},{10,... | collective-permute-start | bytes 98312 | tf_op jit(solution)/shard_map/ppermute | solution.py:41
  30.1 1.0 collective-permute-start.5
  32.0 2.6 %collective-permute-done.4 = bf16[128,128]{1,0:T(8,128)(2,1)S(1)} collective-permute-done((bf16[128,128]{1,0:T(8,128)(2,1)S(1)}, bf16[128,128]{1,0:T(8,128)(2,1)S(1)}, u32[]{:S(2)}, u32[]{:S(2)}) %collective-permute-start.4) | collective-permute-done | bytes 32800 | tf_op jit(solution)/shard_map/ppermute | solution.py:41
  34.6 1.2 collective-permute-done.5
  35.8 1.9 %collective-permute-done.6 = bf16[128,128]{1,0:T(8,128)(2,1)S(1)} collective-permute-done((bf16[128,128]{1,0:T(8,128)(2,1)S(1)}, bf16[128,128]{1,0:T(8,128)(2,1)S(1)}, u32[]{:S(2)}, u32[]{:S(2)}) %collective-permute-start.6) | collective-permute-done | bytes 32800 | tf_op jit(solution)/shard_map/ppermute | solution.py:41
  37.9 0.9 bitcast_dynamic-update-slice_fusion.14
  38.8 1.8 %multiply_reduce_fusion.2 = f32[1024]{0:T(1024)} fusion(bf16[1024,128]{1,0:T(8,128)(2,1)} %param.7), kind=kLoop, calls=%fused_computation.90 | loop fusion | flops 392192 | bytes 266240 | tf_op jit(solution)/shard_map/reduce_sum | solution.py:25
  40.5 1.1 constant_dynamic-slice_fusion.3
  41.6 1.5 collective-permute-start.8
  43.3 1.2 copy.24
  45.9 5.1 %collective-permute-done.8 = bf16[8,128,128]{2,1,0:T(8,128)(2,1)S(1)} collective-permute-done((bf16[8,128,128]{2,1,0:T(8,128)(2,1)}, bf16[8,128,128]{2,1,0:T(8,128)(2,1)S(1)}, u32[]{:S(2)}, u32[]{:S(2)}) %collective-permute-start.8) | collective-permute-done | bytes 262176 | tf_op jit(solution)/shard_map/ppermute | solution.py:41
  51.7 1.7 collective-permute-done.9
  54.1 1.7 bitcast_dynamic-update-slice_fusion.15
  58.0 1.3 constant_dynamic-slice_fusion.1
  60.2 3.3 %fusion.64 = f32[64,2048]{1,0:T(8,128)} fusion(bf16[2048,128]{1,0:T(8,128)(2,1)S(1)} %bitcast.251, bf16[1024,128]{1,0:T(8,128)(2,1)S(1)} %copy-done.8, f32[2048]{0:T(1024)S(1)} %add.142, f32[1024]{0:T(1024)S(1)} %copy-done.21, f32[1024,64]{0,1:T(8,128)S(1)} %copy.24, f32[1024,64]{0,1:T(8,128)S(1)} %copy.23), kind=kOutput, calls=%fused_computation.58 | convolution fusion | flops 816054272 | bytes 1847296 | tf_op jit(solution)/shard_map/dot_general | solution.py:20
  63.5 2.7 %fusion.32 = f32[64,2048]{1,0:T(8,128)S(1)} fusion(f32[64,2048]{1,0:T(8,128)} %fusion.64, s32[2048]{0:T(1024)S(1)} %bitcast.262, s32[1024]{0:T(1024)S(1)} %copy-done.17, bf16[1024,64]{0,1:T(8,128)(2,1)S(1)} %copy.25, f32[1024,64]{0,1:T(8,128)S(1)} %copy.24, f32[1024,64]{0,1:T(8,128)S(1)} %copy.23), kind=kOutput, calls=%fused_computation.40 | convolution fusion | flops 271056896 | bytes 1716224 | tf_op jit(solution)/shard_map/dot_general | solution.py:20
  66.2 2.3 %fusion.50 = bf16[8,8,2048]{2,1,0:T(8,128)(2,1)} fusion(f32[64,2048]{1,0:T(8,128)S(1)} %fusion.32, s32[2048]{0:T(1024)S(1)} %bitcast.263, s32[1024]{0:T(1024)S(1)} %copy-done.17, bf16[1024,64]{0,1:T(8,128)(2,1)S(1)} %copy.25, f32[1024,64]{0,1:T(8,128)S(1)} %copy.24, f32[1024,64]{0,1:T(8,128)S(1)} %copy.23), kind=kOutput, calls=%fused_computation.46 | convolution fusion | flops 271384576 | bytes 1454080 | tf_op jit(solution)/shard_map/dot_general | solution.py:20
  68.6 3.6 %all-to-all-start.1 = ((bf16[8,8,2048]{2,1,0:T(8,128)(2,1)}), bf16[8,8,2048]{2,1,0:T(8,128)(2,1)S(1)}, u32[]{:S(2)}, u32[]{:S(2)}) async-start(bf16[8,8,2048]{2,1,0:T(8,128)(2,1)} %fusion.50), calls=%async_computation.1 | async-start | bytes 524288 | tf_op jit(solution)/shard_map/all_to_all | solution.py:90
  72.2 0.9 multiply_reduce_fusion.4
  73.1 2.1 %exponential_convert_fusion.1 = bf16[2048,512]{1,0:T(8,128)(2,1)S(1)} fusion(bf16[2048,128]{1,0:T(8,128)(2,1)} %bitcast.253, bf16[512,128]{0,1:T(8,128)(2,1)S(1)} %get-tuple-element.23, f32[512]{0:T(512)S(1)} %get-tuple-element.22, f32[2048]{0:T(1024)S(1)} %add.142), kind=kOutput, calls=%fused_computation.22 | convolution fusion | flops 273678336 | bytes 2762752 | tf_op jit(solution)/shard_map/dot_general | solution.py:20
  75.2 5.4 %all-to-all-done.1 = bf16[8,8,2048]{2,1,0:T(8,128)(2,1)S(1)} async-done(((bf16[8,8,2048]{2,1,0:T(8,128)(2,1)}), bf16[8,8,2048]{2,1,0:T(8,128)(2,1)S(1)}, u32[]{:S(2)}, u32[]{:S(2)}) %all-to-all-start.1) | async-done | bytes 262176 | tf_op jit(solution)/shard_map/all_to_all | solution.py:90
  80.5 1.6 convolution_convert_fusion.3
  82.1 1.3 constant_dynamic-update-slice_fusion.31
  83.4 2.3 %collective-permute-start.10 = (bf16[8,2048]{1,0:T(8,128)(2,1)S(1)}, bf16[8,2048]{1,0:T(8,128)(2,1)S(1)}, u32[]{:S(2)}, u32[]{:S(2)}) collective-permute-start(bf16[8,2048]{1,0:T(8,128)(2,1)S(1)} %get-tuple-element.25), channel_id=1, source_target_pairs={{0,7},{1,0},{2,1},{3,2},{4,3},{5,4},{6,5},{7,6},{8,15},{9,8},{10,9... | collective-permute-start | bytes 98312 | tf_op jit(solution)/shard_map/ppermute | solution.py:41
  85.8 1.7 %collective-permute-start.12 = (bf16[8,2048]{1,0:T(8,128)(2,1)S(1)}, bf16[8,2048]{1,0:T(8,128)(2,1)S(1)}, u32[]{:S(2)}, u32[]{:S(2)}) collective-permute-start(bf16[8,2048]{1,0:T(8,128)(2,1)S(1)} %get-tuple-element.25), channel_id=1, source_target_pairs={{0,5},{1,6},{2,7},{3,0},{4,1},{5,2},{6,3},{7,4},{8,13},{9,14},{10,... | collective-permute-start | bytes 98312 | tf_op jit(solution)/shard_map/ppermute | solution.py:41
  87.5 1.7 collective-permute-start.13
  89.2 1.6 collective-permute-start.14
  90.8 0.9 collective-permute-start.15
  97.1 1.8 %collective-permute-done.16 = bf16[8,2048]{1,0:T(8,128)(2,1)S(1)} collective-permute-done((bf16[8,2048]{1,0:T(8,128)(2,1)S(1)}, bf16[8,2048]{1,0:T(8,128)(2,1)S(1)}, u32[]{:S(2)}, u32[]{:S(2)}) %collective-permute-start.16) | collective-permute-done | bytes 32800 | tf_op jit(solution)/shard_map/ppermute | solution.py:41
  104.5 2.8 %convert_bitcast_fusion = (bf16[1,64,1024]{2,1,0:T(8,128)(2,1)S(1)}, f32[64,1024]{1,0:T(8,128)S(1)}) fusion(f32[1024,64]{0,1:T(8,128)} %copy-done.5, f32[1024,64]{0,1:T(8,128)} %copy-done.6, s32[2048]{0:T(1024)} %bitcast.261, s32[1024]{0:T(1024)} %copy-done.16, bf16[16,8,2048]{2,1,0:T(8,128)(2,1)} %constant_dynamic-update-slice_fusion.16, s32[]{:T(128)S(6)} %select_n.38), kind=kOutput, calls=%fused_computation.179 | convolution fusion | flops 271450112 | bytes 1191940 | tf_op jit(solution)/shard_map/dot_general | solution.py:20
  107.4 2.5 %fusion.65 = f32[64,2048]{1,0:T(8,128)S(1)} fusion(bf16[2048,128]{1,0:T(8,128)(2,1)S(1)} %bitcast.248, bf16[1024,128]{1,0:T(8,128)(2,1)S(1)} %copy-done.9, f32[2048]{0:T(1024)S(1)} %add.152, f32[1024]{0:T(1024)S(1)} %copy-done.22, f32[64,1024]{1,0:T(8,128)S(1)} %get-tuple-element.15), kind=kOutput, calls=%fused_computation.59 | convolution fusion | flops 815857664 | bytes 1585152 | tf_op jit(solution)/shard_map/dot_general | solution.py:20
  109.9 1.6 fusion.38
  111.5 2.3 %fusion.53 = bf16[8,8,2048]{2,1,0:T(8,128)(2,1)} fusion(f32[64,2048]{1,0:T(8,128)S(1)} %fusion.38, s32[2048]{0:T(1024)S(1)} %bitcast.258, s32[1024]{0:T(1024)S(1)} %copy-done.18, f32[64,1024]{1,0:T(8,128)S(1)} %get-tuple-element.15, bf16[1024,64]{0,1:T(8,128)(2,1)S(1)} %copy-done.11), kind=kOutput, calls=%fused_computation.47 | convolution fusion | flops 271187968 | bytes 1191936 | tf_op jit(solution)/shard_map/dot_general | solution.py:20
  113.9 3.6 %all-to-all-start.2 = ((bf16[8,8,2048]{2,1,0:T(8,128)(2,1)}), bf16[8,8,2048]{2,1,0:T(8,128)(2,1)S(1)}, u32[]{:S(2)}, u32[]{:S(2)}) async-start(bf16[8,8,2048]{2,1,0:T(8,128)(2,1)} %fusion.53), calls=%async_computation.2 | async-start | bytes 524288 | tf_op jit(solution)/shard_map/all_to_all | solution.py:90
  117.5 0.9 multiply_reduce_fusion.3
  118.4 1.0 exponential_convert_fusion
  119.5 6.0 %all-to-all-done.2 = bf16[8,8,2048]{2,1,0:T(8,128)(2,1)S(1)} async-done(((bf16[8,8,2048]{2,1,0:T(8,128)(2,1)}), bf16[8,8,2048]{2,1,0:T(8,128)(2,1)S(1)}, u32[]{:S(2)}, u32[]{:S(2)}) %all-to-all-start.2) | async-done | bytes 262176 | tf_op jit(solution)/shard_map/all_to_all | solution.py:90
  125.5 1.6 convolution_convert_fusion.2
  127.7 1.6 collective-permute-start.17
  129.3 1.4 collective-permute-start.19
  130.8 1.9 %collective-permute-start.20 = (bf16[8,2048]{1,0:T(8,128)(2,1)S(1)}, bf16[8,2048]{1,0:T(8,128)(2,1)S(1)}, u32[]{:S(2)}, u32[]{:S(2)}) collective-permute-start(bf16[8,2048]{1,0:T(8,128)(2,1)S(1)} %get-tuple-element.29), channel_id=1, source_target_pairs={{0,4},{1,5},{2,6},{3,7},{4,0},{5,1},{6,2},{7,3},{8,12},{9,13},{10,... | collective-permute-start | bytes 98312 | tf_op jit(solution)/shard_map/ppermute | solution.py:41
  132.7 0.9 collective-permute-start.21
  133.6 2.4 %collective-permute-start.22 = (bf16[8,2048]{1,0:T(8,128)(2,1)S(1)}, bf16[8,2048]{1,0:T(8,128)(2,1)S(1)}, u32[]{:S(2)}, u32[]{:S(2)}) collective-permute-start(bf16[8,2048]{1,0:T(8,128)(2,1)S(1)} %get-tuple-element.29), channel_id=1, source_target_pairs={{0,2},{1,3},{2,4},{3,5},{4,6},{5,7},{6,0},{7,1},{8,10},{9,11},{10,... | collective-permute-start | bytes 98312 | tf_op jit(solution)/shard_map/ppermute | solution.py:41
  136.2 2.2 %collective-permute-done.21 = bf16[8,2048]{1,0:T(8,128)(2,1)S(1)} collective-permute-done((bf16[8,2048]{1,0:T(8,128)(2,1)S(1)}, bf16[8,2048]{1,0:T(8,128)(2,1)S(1)}, u32[]{:S(2)}, u32[]{:S(2)}) %collective-permute-start.21) | collective-permute-done | bytes 32800 | tf_op jit(solution)/shard_map/ppermute | solution.py:41
  138.4 1.4 collective-permute-done.22
  139.8 2.8 %collective-permute-done.23 = bf16[8,2048]{1,0:T(8,128)(2,1)S(1)} collective-permute-done((bf16[8,2048]{1,0:T(8,128)(2,1)S(1)}, bf16[8,2048]{1,0:T(8,128)(2,1)S(1)}, u32[]{:S(2)}, u32[]{:S(2)}) %collective-permute-start.23) | collective-permute-done | bytes 32800 | tf_op jit(solution)/shard_map/ppermute | solution.py:41
  142.7 1.6 fusion.77
  144.4 1.5 collective-permute-start.25
  146.2 3.9 %collective-permute-done.24 = bf16[2,64,1024]{2,1,0:T(8,128)(2,1)S(1)} collective-permute-done((bf16[2,64,1024]{2,1,0:T(8,128)(2,1)S(1)}, bf16[2,64,1024]{2,1,0:T(8,128)(2,1)S(1)}, u32[]{:S(2)}, u32[]{:S(2)}) %collective-permute-start.24) | collective-permute-done | bytes 262176 | tf_op jit(solution)/shard_map/ppermute | solution.py:41
  150.1 8.4 %collective-permute-done.25 = bf16[2,64,1024]{2,1,0:T(8,128)(2,1)S(1)} collective-permute-done((bf16[2,64,1024]{2,1,0:T(8,128)(2,1)S(1)}, bf16[2,64,1024]{2,1,0:T(8,128)(2,1)S(1)}, u32[]{:S(2)}, u32[]{:S(2)}) %collective-permute-start.25) | collective-permute-done | bytes 262176 | tf_op jit(solution)/shard_map/ppermute | solution.py:41
  158.9 1.9 %convert_multiply_fusion = (f32[1,4,64,1024]{3,2,0,1:T(8,128)}, f32[1,4,64,1024]{3,2,0,1:T(8,128)S(1)}, f32[1,4,64,1024]{3,2,0,1:T(8,128)S(1)}, f32[1,4,64,1024]{3,2,0,1:T(8,128)}) fusion(bf16[2,4,64,1024]{3,2,0,1:T(8,128)(2,1)S(1)} %dynamic-slice_bitcast_fusion), kind=kLoop, calls=%fused_computation.60 | loop fusion | flops 1572864 | bytes 5242880 | tf_op jit(solution)/shard_map/mul | solution.py:114
  160.7 2.6 %copy.22 = f32[256,1024]{0,1:T(8,128)} copy(f32[256,1024]{1,0:T(8,128)} %bitcast.247) | data formatting | bytes 2097152 | tf_op jit(solution)/shard_map/mul | solution.py:114
  163.3 2.5 %copy.19 = f32[256,1024]{0,1:T(8,128)} copy(f32[256,1024]{1,0:T(8,128)} %bitcast.246) | data formatting | bytes 2097152 | tf_op jit(solution)/shard_map/mul | solution.py:114
  165.8 1.3 copy.20
  167.1 1.3 copy.21
  168.5 4.4 %bitcast_subtract_fusion.2 = (f32[1024,256]{1,0:T(8,128)}, f32[1024,256]{1,0:T(8,128)}) fusion(f32[256,1024]{0,1:T(8,128)S(1)} %copy-done.1, f32[256,1024]{0,1:T(8,128)} %copy.19, f32[1024,256]{1,0:T(8,128)} %param.9, f32[1024,256]{1,0:T(8,128)} %param.10, f32[256,1024]{0,1:T(8,128)} %copy.20, f32[256,1024]{0,1:T(8,128)} %copy.21), kind=kLoop, calls=%fused_computation.74 | loop fusion | flops 4194304 | bytes 8388608 | tf_op jit(solution)/shard_map/sub | solution.py:114
  (155 shorter events, 22.0 us)
Async XLA Ops:
  0.6 42.5 %copy-start = (bf16[1024,256]{1,0:T(8,128)(2,1)S(1)}, bf16[1024,256]{1,0:T(8,128)(2,1)}, u32[]{:S(2)}) copy-start(bf16[1024,256]{1,0:T(8,128)(2,1)} %param.8) | copy-start | bytes 1572868
  1.5 2.7 %copy-start.12 = (s32[1,2048]{1,0:T(1,128)}, s32[1,2048]{1,0:T(1,128)S(1)}, u32[]{:S(2)}) copy-start(s32[1,2048]{1,0:T(1,128)S(1)} %get-tuple-element.17) | copy-start | bytes 24580
  1.5 2.7 %copy-start.14 = (s32[1,2048]{1,0:T(1,128)}, s32[1,2048]{1,0:T(1,128)S(1)}, u32[]{:S(2)}) copy-start(s32[1,2048]{1,0:T(1,128)S(1)} %get-tuple-element.16) | copy-start | bytes 24580
  1.5 2.7 %copy-start.16 = (s32[1024]{0:T(1024)}, s32[1024]{0:T(1024)S(1)}, u32[]{:S(2)}) copy-start(s32[1024]{0:T(1024)S(1)} %iota_add_fusion) | copy-start | bytes 12292
  1.5 2.7 %copy-start.7 = (bf16[1024,128]{1,0:T(8,128)(2,1)S(1)}, bf16[1024,128]{1,0:T(8,128)(2,1)}, u32[]{:S(2)}) copy-start(bf16[1024,128]{1,0:T(8,128)(2,1)} %param.7) | copy-start | bytes 786436
  4.2 9.6 %copy-start.23 = (s32[2,512]{1,0:T(2,128)S(1)}, s32[2,512]{1,0:T(2,128)}, u32[]{:S(2)}) copy-start(s32[2,512]{1,0:T(2,128)} %param.12) | copy-start | bytes 12292
  5.0 35.5 %copy-start.2 = (f32[1024,256]{1,0:T(8,128)S(1)}, f32[1024,256]{1,0:T(8,128)}, u32[]{:S(2)}) copy-start(f32[1024,256]{1,0:T(8,128)} %param.9) | copy-start | bytes 3145732
  5.0 35.5 %copy-start.3 = (f32[1024,256]{1,0:T(8,128)S(1)}, f32[1024,256]{1,0:T(8,128)}, u32[]{:S(2)}) copy-start(f32[1024,256]{1,0:T(8,128)} %param.10) | copy-start | bytes 3145732
  6.5 16.2 %all-to-all-start = ((bf16[8,128,128]{2,1,0:T(8,128)(2,1)}), bf16[8,128,128]{2,1,0:T(8,128)(2,1)S(1)}, u32[]{:S(2)}, u32[]{:S(2)}) async-start(bf16[8,128,128]{2,1,0:T(8,128)(2,1)} %pad_maximum_fusion), calls=%async_computation | async-start | bytes 524288 | tf_op jit(solution)/shard_map/all_to_all | solution.py:69
  22.8 7.3 %collective-permute-start = (bf16[128,128]{1,0:T(8,128)(2,1)S(1)}, bf16[128,128]{1,0:T(8,128)(2,1)S(1)}, u32[]{:S(2)}, u32[]{:S(2)}) collective-permute-start(bf16[128,128]{1,0:T(8,128)(2,1)S(1)} %reduce_sum.88), channel_id=1, source_target_pairs={{0,7},{1,0},{2,1},{3,2},{4,3},{5,4},{6,5},{7,6},{8,15},{9,8},{10,9... | collective-permute-start | bytes 98312 | tf_op jit(solution)/shard_map/ppermute | solution.py:41
  25.1 5.9 %collective-permute-start.1 = (bf16[128,128]{1,0:T(8,128)(2,1)S(1)}, bf16[128,128]{1,0:T(8,128)(2,1)S(1)}, u32[]{:S(2)}, u32[]{:S(2)}) collective-permute-start(bf16[128,128]{1,0:T(8,128)(2,1)S(1)} %reduce_sum.88), channel_id=1, source_target_pairs={{0,6},{1,7},{2,0},{3,1},{4,2},{5,3},{6,4},{7,5},{8,14},{9,15},{10,... | collective-permute-start | bytes 98312 | tf_op jit(solution)/shard_map/ppermute | solution.py:41
  25.1 6.7 %collective-permute-start.2 = (bf16[128,128]{1,0:T(8,128)(2,1)S(1)}, bf16[128,128]{1,0:T(8,128)(2,1)S(1)}, u32[]{:S(2)}, u32[]{:S(2)}) collective-permute-start(bf16[128,128]{1,0:T(8,128)(2,1)S(1)} %reduce_sum.88), channel_id=1, source_target_pairs={{0,5},{1,6},{2,7},{3,0},{4,1},{5,2},{6,3},{7,4},{8,13},{9,14},{10,... | collective-permute-start | bytes 98312 | tf_op jit(solution)/shard_map/ppermute | solution.py:41
  26.8 5.2 %collective-permute-start.3 = (bf16[128,128]{1,0:T(8,128)(2,1)S(1)}, bf16[128,128]{1,0:T(8,128)(2,1)S(1)}, u32[]{:S(2)}, u32[]{:S(2)}) collective-permute-start(bf16[128,128]{1,0:T(8,128)(2,1)S(1)} %reduce_sum.88), channel_id=1, source_target_pairs={{0,4},{1,5},{2,6},{3,7},{4,0},{5,1},{6,2},{7,3},{8,12},{9,13},{10,... | collective-permute-start | bytes 98312 | tf_op jit(solution)/shard_map/ppermute | solution.py:41
  28.3 6.2 %collective-permute-start.4 = (bf16[128,128]{1,0:T(8,128)(2,1)S(1)}, bf16[128,128]{1,0:T(8,128)(2,1)S(1)}, u32[]{:S(2)}, u32[]{:S(2)}) collective-permute-start(bf16[128,128]{1,0:T(8,128)(2,1)S(1)} %reduce_sum.88), channel_id=1, source_target_pairs={{0,3},{1,4},{2,5},{3,6},{4,7},{5,0},{6,1},{7,2},{8,11},{9,12},{10,... | collective-permute-start | bytes 98312 | tf_op jit(solution)/shard_map/ppermute | solution.py:41
  30.1 5.7 %collective-permute-start.5 = (bf16[128,128]{1,0:T(8,128)(2,1)S(1)}, bf16[128,128]{1,0:T(8,128)(2,1)S(1)}, u32[]{:S(2)}, u32[]{:S(2)}) collective-permute-start(bf16[128,128]{1,0:T(8,128)(2,1)S(1)} %reduce_sum.88), channel_id=1, source_target_pairs={{0,2},{1,3},{2,4},{3,5},{4,6},{5,7},{6,0},{7,1},{8,10},{9,11},{10,... | collective-permute-start | bytes 98312 | tf_op jit(solution)/shard_map/ppermute | solution.py:41
  31.1 6.7 %collective-permute-start.6 = (bf16[128,128]{1,0:T(8,128)(2,1)S(1)}, bf16[128,128]{1,0:T(8,128)(2,1)S(1)}, u32[]{:S(2)}, u32[]{:S(2)}) collective-permute-start(bf16[128,128]{1,0:T(8,128)(2,1)S(1)} %reduce_sum.88), channel_id=1, source_target_pairs={{0,1},{1,2},{2,3},{3,4},{4,5},{5,6},{6,7},{7,0},{8,9},{9,10},{10,1... | collective-permute-start | bytes 98312 | tf_op jit(solution)/shard_map/ppermute | solution.py:41
  38.8 6.4 %collective-permute-start.7 = (bf16[8,128,128]{2,1,0:T(8,128)(2,1)}, bf16[8,128,128]{2,1,0:T(8,128)(2,1)S(1)}, u32[]{:S(2)}, u32[]{:S(2)}) collective-permute-start(bf16[8,128,128]{2,1,0:T(8,128)(2,1)} %get-tuple-element.5), channel_id=1, source_target_pairs={{0,24},{8,0},{16,8},{24,16},{1,25},{9,1},{17,9},{25,17},{2,26},{10... | collective-permute-start | bytes 786440 | tf_op jit(solution)/shard_map/ppermute | solution.py:41
  41.6 9.3 %collective-permute-start.8 = (bf16[8,128,128]{2,1,0:T(8,128)(2,1)}, bf16[8,128,128]{2,1,0:T(8,128)(2,1)S(1)}, u32[]{:S(2)}, u32[]{:S(2)}) collective-permute-start(bf16[8,128,128]{2,1,0:T(8,128)(2,1)} %get-tuple-element.5), channel_id=1, source_target_pairs={{0,16},{8,24},{16,0},{24,8},{1,17},{9,25},{17,1},{25,9},{2,18},{10... | collective-permute-start | bytes 786440 | tf_op jit(solution)/shard_map/ppermute | solution.py:41
  44.5 21.7 %copy-start.5 = (f32[1024,64]{0,1:T(8,128)}, f32[1024,64]{0,1:T(8,128)S(1)}, u32[]{:S(2)}) copy-start(f32[1024,64]{0,1:T(8,128)S(1)} %copy.24) | copy-start | bytes 786436
  44.7 21.5 %copy-start.6 = (f32[1024,64]{0,1:T(8,128)}, f32[1024,64]{0,1:T(8,128)S(1)}, u32[]{:S(2)}) copy-start(f32[1024,64]{0,1:T(8,128)S(1)} %copy.23) | copy-start | bytes 786436
  44.9 21.3 %copy-start.10 = (bf16[1024,64]{0,1:T(8,128)(2,1)}, bf16[1024,64]{0,1:T(8,128)(2,1)S(1)}, u32[]{:S(2)}) copy-start(bf16[1024,64]{0,1:T(8,128)(2,1)S(1)} %copy.25) | copy-start | bytes 393220
  44.9 8.5 %collective-permute-start.9 = (bf16[8,128,128]{2,1,0:T(8,128)(2,1)}, bf16[8,128,128]{2,1,0:T(8,128)(2,1)S(1)}, u32[]{:S(2)}, u32[]{:S(2)}) collective-permute-start(bf16[8,128,128]{2,1,0:T(8,128)(2,1)} %get-tuple-element.5), channel_id=1, source_target_pairs={{0,8},{8,16},{16,24},{24,0},{1,9},{9,17},{17,25},{25,1},{2,10},{10... | collective-permute-start | bytes 786440 | tf_op jit(solution)/shard_map/ppermute | solution.py:41
  59.3 1.0 copy-start.8
  59.3 0.9 copy-start.21
  59.4 12.8 %copy-start.4 = (bf16[4,8,1,64,128]{4,3,2,1,0:T(8,128)(2,1)}, bf16[4,8,1,64,128]{4,3,2,1,0:T(8,128)(2,1)S(1)}, u32[]{:S(2)}) copy-start(bf16[4,8,1,64,128]{4,3,2,1,0:T(8,128)(2,1)S(1)} %get-tuple-element.12) | copy-start | bytes 1572868
  60.2 3.3 %copy-start.15 = (s32[1,2048]{1,0:T(1,128)S(1)}, s32[1,2048]{1,0:T(1,128)}, u32[]{:S(2)}) copy-start(s32[1,2048]{1,0:T(1,128)} %copy-done.14) | copy-start | bytes 24580
  60.2 3.3 %copy-start.17 = (s32[1024]{0:T(1024)S(1)}, s32[1024]{0:T(1024)}, u32[]{:S(2)}) copy-start(s32[1024]{0:T(1024)} %copy-done.16) | copy-start | bytes 12292
  66.2 6.0 %copy-start.25 = (s32[1,512]{1,0:T(1,128)S(1)}, s32[1,512]{1,0:T(1,128)}, u32[]{:S(2)}) copy-start(s32[1,512]{1,0:T(1,128)} %get-tuple-element.19) | copy-start | bytes 6148
  68.6 11.9 %all-to-all-start.1 = ((bf16[8,8,2048]{2,1,0:T(8,128)(2,1)}), bf16[8,8,2048]{2,1,0:T(8,128)(2,1)S(1)}, u32[]{:S(2)}, u32[]{:S(2)}) async-start(bf16[8,8,2048]{2,1,0:T(8,128)(2,1)} %fusion.50), calls=%async_computation.1 | async-start | bytes 524288 | tf_op jit(solution)/shard_map/all_to_all | solution.py:90
  83.4 7.4 %collective-permute-start.10 = (bf16[8,2048]{1,0:T(8,128)(2,1)S(1)}, bf16[8,2048]{1,0:T(8,128)(2,1)S(1)}, u32[]{:S(2)}, u32[]{:S(2)}) collective-permute-start(bf16[8,2048]{1,0:T(8,128)(2,1)S(1)} %get-tuple-element.25), channel_id=1, source_target_pairs={{0,7},{1,0},{2,1},{3,2},{4,3},{5,4},{6,5},{7,6},{8,15},{9,8},{10,9... | collective-permute-start | bytes 98312 | tf_op jit(solution)/shard_map/ppermute | solution.py:41
  85.8 21.6 %copy-start.19 = (f32[2048]{0:T(1024)}, f32[2048]{0:T(1024)S(1)}, u32[]{:S(2)}) copy-start(f32[2048]{0:T(1024)S(1)} %add.152) | copy-start | bytes 24580
  85.8 6.6 %collective-permute-start.11 = (bf16[8,2048]{1,0:T(8,128)(2,1)S(1)}, bf16[8,2048]{1,0:T(8,128)(2,1)S(1)}, u32[]{:S(2)}, u32[]{:S(2)}) collective-permute-start(bf16[8,2048]{1,0:T(8,128)(2,1)S(1)} %get-tuple-element.25), channel_id=1, source_target_pairs={{0,6},{1,7},{2,0},{3,1},{4,2},{5,3},{6,4},{7,5},{8,14},{9,15},{10,... | collective-permute-start | bytes 98312 | tf_op jit(solution)/shard_map/ppermute | solution.py:41
  85.8 7.9 %collective-permute-start.12 = (bf16[8,2048]{1,0:T(8,128)(2,1)S(1)}, bf16[8,2048]{1,0:T(8,128)(2,1)S(1)}, u32[]{:S(2)}, u32[]{:S(2)}) collective-permute-start(bf16[8,2048]{1,0:T(8,128)(2,1)S(1)} %get-tuple-element.25), channel_id=1, source_target_pairs={{0,5},{1,6},{2,7},{3,0},{4,1},{5,2},{6,3},{7,4},{8,13},{9,14},{10,... | collective-permute-start | bytes 98312 | tf_op jit(solution)/shard_map/ppermute | solution.py:41
  87.5 6.7 %collective-permute-start.13 = (bf16[8,2048]{1,0:T(8,128)(2,1)S(1)}, bf16[8,2048]{1,0:T(8,128)(2,1)S(1)}, u32[]{:S(2)}, u32[]{:S(2)}) collective-permute-start(bf16[8,2048]{1,0:T(8,128)(2,1)S(1)} %get-tuple-element.25), channel_id=1, source_target_pairs={{0,4},{1,5},{2,6},{3,7},{4,0},{5,1},{6,2},{7,3},{8,12},{9,13},{10,... | collective-permute-start | bytes 98312 | tf_op jit(solution)/shard_map/ppermute | solution.py:41
  89.2 6.4 %collective-permute-start.14 = (bf16[8,2048]{1,0:T(8,128)(2,1)S(1)}, bf16[8,2048]{1,0:T(8,128)(2,1)S(1)}, u32[]{:S(2)}, u32[]{:S(2)}) collective-permute-start(bf16[8,2048]{1,0:T(8,128)(2,1)S(1)} %get-tuple-element.25), channel_id=1, source_target_pairs={{0,3},{1,4},{2,5},{3,6},{4,7},{5,0},{6,1},{7,2},{8,11},{9,12},{10,... | collective-permute-start | bytes 98312 | tf_op jit(solution)/shard_map/ppermute | solution.py:41
  90.8 5.7 %collective-permute-start.15 = (bf16[8,2048]{1,0:T(8,128)(2,1)S(1)}, bf16[8,2048]{1,0:T(8,128)(2,1)S(1)}, u32[]{:S(2)}, u32[]{:S(2)}) collective-permute-start(bf16[8,2048]{1,0:T(8,128)(2,1)S(1)} %get-tuple-element.25), channel_id=1, source_target_pairs={{0,2},{1,3},{2,4},{3,5},{4,6},{5,7},{6,0},{7,1},{8,10},{9,11},{10,... | collective-permute-start | bytes 98312 | tf_op jit(solution)/shard_map/ppermute | solution.py:41
  92.4 6.6 %collective-permute-start.16 = (bf16[8,2048]{1,0:T(8,128)(2,1)S(1)}, bf16[8,2048]{1,0:T(8,128)(2,1)S(1)}, u32[]{:S(2)}, u32[]{:S(2)}) collective-permute-start(bf16[8,2048]{1,0:T(8,128)(2,1)S(1)} %get-tuple-element.25), channel_id=1, source_target_pairs={{0,1},{1,2},{2,3},{3,4},{4,5},{5,6},{6,7},{7,0},{8,9},{9,10},{10,1... | collective-permute-start | bytes 98312 | tf_op jit(solution)/shard_map/ppermute | solution.py:41
  102.1 5.3 %copy-start.9 = (bf16[1024,128]{1,0:T(8,128)(2,1)S(1)}, bf16[1024,128]{1,0:T(8,128)(2,1)}, u32[]{:S(2)}) copy-start(bf16[1024,128]{1,0:T(8,128)(2,1)} %param.7) | copy-start | bytes 786436
  102.1 5.3 %copy-start.22 = (f32[1024]{0:T(1024)S(1)}, f32[1024]{0:T(1024)}, u32[]{:S(2)}) copy-start(f32[1024]{0:T(1024)} %multiply_reduce_fusion.2) | copy-start | bytes 12292
  107.4 2.5 %copy-start.11 = (bf16[1024,64]{0,1:T(8,128)(2,1)S(1)}, bf16[1024,64]{0,1:T(8,128)(2,1)}, u32[]{:S(2)}) copy-start(bf16[1024,64]{0,1:T(8,128)(2,1)} %copy-done.10) | copy-start | bytes 393220
  107.4 2.5 %copy-start.13 = (s32[1,2048]{1,0:T(1,128)S(1)}, s32[1,2048]{1,0:T(1,128)}, u32[]{:S(2)}) copy-start(s32[1,2048]{1,0:T(1,128)} %copy-done.12) | copy-start | bytes 24580
  107.4 2.5 %copy-start.18 = (s32[1024]{0:T(1024)S(1)}, s32[1024]{0:T(1024)}, u32[]{:S(2)}) copy-start(s32[1024]{0:T(1024)} %copy-done.16) | copy-start | bytes 12292
  111.5 6.0 %copy-start.24 = (s32[1,512]{1,0:T(1,128)S(1)}, s32[1,512]{1,0:T(1,128)}, u32[]{:S(2)}) copy-start(s32[1,512]{1,0:T(1,128)} %get-tuple-element.18) | copy-start | bytes 6148
  113.9 11.6 %all-to-all-start.2 = ((bf16[8,8,2048]{2,1,0:T(8,128)(2,1)}), bf16[8,8,2048]{2,1,0:T(8,128)(2,1)S(1)}, u32[]{:S(2)}, u32[]{:S(2)}) async-start(bf16[8,8,2048]{2,1,0:T(8,128)(2,1)} %fusion.53), calls=%async_computation.2 | async-start | bytes 524288 | tf_op jit(solution)/shard_map/all_to_all | solution.py:90
  117.5 0.9 copy-start.20
  127.7 5.9 %collective-permute-start.17 = (bf16[8,2048]{1,0:T(8,128)(2,1)S(1)}, bf16[8,2048]{1,0:T(8,128)(2,1)S(1)}, u32[]{:S(2)}, u32[]{:S(2)}) collective-permute-start(bf16[8,2048]{1,0:T(8,128)(2,1)S(1)} %get-tuple-element.29), channel_id=1, source_target_pairs={{0,7},{1,0},{2,1},{3,2},{4,3},{5,4},{6,5},{7,6},{8,15},{9,8},{10,9... | collective-permute-start | bytes 98312 | tf_op jit(solution)/shard_map/ppermute | solution.py:41
  129.3 6.7 %collective-permute-start.18 = (bf16[8,2048]{1,0:T(8,128)(2,1)S(1)}, bf16[8,2048]{1,0:T(8,128)(2,1)S(1)}, u32[]{:S(2)}, u32[]{:S(2)}) collective-permute-start(bf16[8,2048]{1,0:T(8,128)(2,1)S(1)} %get-tuple-element.29), channel_id=1, source_target_pairs={{0,6},{1,7},{2,0},{3,1},{4,2},{5,3},{6,4},{7,5},{8,14},{9,15},{10,... | collective-permute-start | bytes 98312 | tf_op jit(solution)/shard_map/ppermute | solution.py:41
  129.3 6.9 %collective-permute-start.19 = (bf16[8,2048]{1,0:T(8,128)(2,1)S(1)}, bf16[8,2048]{1,0:T(8,128)(2,1)S(1)}, u32[]{:S(2)}, u32[]{:S(2)}) collective-permute-start(bf16[8,2048]{1,0:T(8,128)(2,1)S(1)} %get-tuple-element.29), channel_id=1, source_target_pairs={{0,5},{1,6},{2,7},{3,0},{4,1},{5,2},{6,3},{7,4},{8,13},{9,14},{10,... | collective-permute-start | bytes 98312 | tf_op jit(solution)/shard_map/ppermute | solution.py:41
  130.8 5.5 %collective-permute-start.20 = (bf16[8,2048]{1,0:T(8,128)(2,1)S(1)}, bf16[8,2048]{1,0:T(8,128)(2,1)S(1)}, u32[]{:S(2)}, u32[]{:S(2)}) collective-permute-start(bf16[8,2048]{1,0:T(8,128)(2,1)S(1)} %get-tuple-element.29), channel_id=1, source_target_pairs={{0,4},{1,5},{2,6},{3,7},{4,0},{5,1},{6,2},{7,3},{8,12},{9,13},{10,... | collective-permute-start | bytes 98312 | tf_op jit(solution)/shard_map/ppermute | solution.py:41
  132.7 5.7 %collective-permute-start.21 = (bf16[8,2048]{1,0:T(8,128)(2,1)S(1)}, bf16[8,2048]{1,0:T(8,128)(2,1)S(1)}, u32[]{:S(2)}, u32[]{:S(2)}) collective-permute-start(bf16[8,2048]{1,0:T(8,128)(2,1)S(1)} %get-tuple-element.29), channel_id=1, source_target_pairs={{0,3},{1,4},{2,5},{3,6},{4,7},{5,0},{6,1},{7,2},{8,11},{9,12},{10,... | collective-permute-start | bytes 98312 | tf_op jit(solution)/shard_map/ppermute | solution.py:41
  133.6 6.2 %collective-permute-start.22 = (bf16[8,2048]{1,0:T(8,128)(2,1)S(1)}, bf16[8,2048]{1,0:T(8,128)(2,1)S(1)}, u32[]{:S(2)}, u32[]{:S(2)}) collective-permute-start(bf16[8,2048]{1,0:T(8,128)(2,1)S(1)} %get-tuple-element.29), channel_id=1, source_target_pairs={{0,2},{1,3},{2,4},{3,5},{4,6},{5,7},{6,0},{7,1},{8,10},{9,11},{10,... | collective-permute-start | bytes 98312 | tf_op jit(solution)/shard_map/ppermute | solution.py:41
  136.0 6.6 %collective-permute-start.23 = (bf16[8,2048]{1,0:T(8,128)(2,1)S(1)}, bf16[8,2048]{1,0:T(8,128)(2,1)S(1)}, u32[]{:S(2)}, u32[]{:S(2)}) collective-permute-start(bf16[8,2048]{1,0:T(8,128)(2,1)S(1)} %get-tuple-element.29), channel_id=1, source_target_pairs={{0,1},{1,2},{2,3},{3,4},{4,5},{5,6},{6,7},{7,0},{8,9},{9,10},{10,1... | collective-permute-start | bytes 98312 | tf_op jit(solution)/shard_map/ppermute | solution.py:41
  144.3 5.7 %collective-permute-start.24 = (bf16[2,64,1024]{2,1,0:T(8,128)(2,1)S(1)}, bf16[2,64,1024]{2,1,0:T(8,128)(2,1)S(1)}, u32[]{:S(2)}, u32[]{:S(2)}) collective-permute-start(bf16[2,64,1024]{2,1,0:T(8,128)(2,1)S(1)} %pad_maximum_fusion.1), channel_id=1, source_target_pairs={{0,24},{8,0},{16,8},{24,16},{1,25},{9,1},{17,9},{25,17},{2,26},{10... | collective-permute-start | bytes 786440 | tf_op jit(solution)/shard_map/ppermute | solution.py:41
  144.4 14.1 %collective-permute-start.25 = (bf16[2,64,1024]{2,1,0:T(8,128)(2,1)S(1)}, bf16[2,64,1024]{2,1,0:T(8,128)(2,1)S(1)}, u32[]{:S(2)}, u32[]{:S(2)}) collective-permute-start(bf16[2,64,1024]{2,1,0:T(8,128)(2,1)S(1)} %pad_maximum_fusion.1), channel_id=1, source_target_pairs={{0,16},{8,24},{16,0},{24,8},{1,17},{9,25},{17,1},{25,9},{2,18},{10... | collective-permute-start | bytes 786440 | tf_op jit(solution)/shard_map/ppermute | solution.py:41
  146.0 12.7 %collective-permute-start.26 = (bf16[2,64,1024]{2,1,0:T(8,128)(2,1)S(1)}, bf16[2,64,1024]{2,1,0:T(8,128)(2,1)S(1)}, u32[]{:S(2)}, u32[]{:S(2)}) collective-permute-start(bf16[2,64,1024]{2,1,0:T(8,128)(2,1)S(1)} %pad_maximum_fusion.1), channel_id=1, source_target_pairs={{0,8},{8,16},{16,24},{24,0},{1,9},{9,17},{17,25},{25,1},{2,10},{10... | collective-permute-start | bytes 786440 | tf_op jit(solution)/shard_map/ppermute | solution.py:41
  167.1 1.3 copy-start.1

commit v3 on v1

v3 whole, which is shorter than its diff:
```python
import functools
import math

import jax
import jax.numpy as jnp
from jax import lax
from jax.experimental import pallas as pl
from jax.experimental.pallas import tpu as pltpu
from jax.sharding import PartitionSpec as P

UPDATES = 2


alpha_mix = 0.6
beta_keep = 0.9
step_size = 0.2
momentum_gain = 1.5
ridge_term = 1.0

f32 = jnp.float32
bf16 = jnp.bfloat16
i32 = jnp.int32


def mm(a, b, ca, cb):
    return lax.dot_general(a, b, (((ca,), (cb,)), ((), ())), preferred_element_type=f32)


def split_two(value):
    high = value.astype(bf16)
    return high, (value - high.astype(f32)).astype(bf16)


def mixed_of(current, moving):
    return alpha_mix * moving + (1.0 - alpha_mix) * current


def stepped(current, moving, change):
    mixed = mixed_of(current, moving)
    return (
        mixed - step_size * change,
        beta_keep * moving + (1.0 - beta_keep) * mixed - step_size * momentum_gain * change,
    )


def iota(shape, axis):
    return lax.broadcasted_iota(i32, shape, axis)


def before_matrix(n):
    return jnp.where(iota((n, n), 0) < iota((n, n), 1), 1.0, 0.0).astype(bf16)


def slots_of(indices, before, points, owners, cap):
    owner = lax.div(indices, jnp.full_like(indices, points))
    marks = iota((owners, indices.shape[1]), 0) == owner
    counts = jnp.where(marks, 1.0, 0.0)
    earlier = mm(counts.astype(bf16), before, 1, 0)
    rank = jnp.sum(counts * earlier, axis=0, keepdims=True)
    return owner * cap + rank.astype(i32)


def point_rows(indices, slots, me, points, cap):
    held = iota((cap, indices.shape[1]), 0) + me * cap == slots
    local = (indices - me * points + 1).astype(f32)
    point = jnp.sum(jnp.where(held, local, 0.0), axis=1, keepdims=True).astype(i32) - 1
    return jnp.where(iota((cap, points), 1) == point, 1.0, 0.0).astype(bf16)


def pack_kernel(cap, owners, where_ref, blocks_ref, feats_ref, *outs):
    row, me = where_ref[0], where_ref[1]
    points = feats_ref.shape[0]
    before = before_matrix(blocks_ref.shape[3])
    for u, out in enumerate(outs):
        indices = blocks_ref[u, row]
        slots = slots_of(indices, before, points, owners, cap)
        rows = point_rows(indices, slots, me, points, cap)
        packed = mm(rows, feats_ref[...], 1, 0).astype(bf16)
        for o in range(owners):
            out[o] = packed


def index_kernel(cap, owners, points, where_ref, blocks_ref, slots_ref, *rows_refs):
    me = where_ref[1]
    before = before_matrix(blocks_ref.shape[3])
    for u, rows_ref in enumerate(rows_refs):
        for g in range(blocks_ref.shape[1]):
            indices = blocks_ref[u, g]
            slots = slots_of(indices, before, points, owners, cap)
            slots_ref[u, g] = slots
            rows_ref[g * cap : (g + 1) * cap, :] = point_rows(indices, slots, me, points, cap)


def compact_kernel(u, where_ref, slots_ref, got_ref, out_ref):
    owners, cap, width = got_ref.shape
    slots = slots_ref[u, where_ref[0]]
    place = jnp.where(iota((owners * cap, slots.shape[1]), 0) == slots, 1.0, 0.0).astype(bf16)
    out_ref[...] = mm(got_ref[...].reshape(owners * cap, width), place, 0, 0).astype(bf16)


def tile_of(left, left_norm, right_t, right_norm):
    scale = 7.0 / left.shape[1] * math.log2(math.e)
    return jnp.exp2(mm(left, right_t, 1, 0) * scale - left_norm - right_norm).astype(bf16)


def scaled_norm(rows, axis):
    width = rows.shape[axis]
    return jnp.sum(jnp.square(rows.astype(f32)), axis=axis, keepdims=True) * (
        3.5 / width * math.log2(math.e)
    )


def partial_kernel(u, where_ref, blocks_ref, feats_ref, b0, b1, b2, b3, w_ref, z_ref, t_ref, *rest):
    *done, out_ref, part_ref, coef_ref = rest
    row, me = where_ref[0], where_ref[1]
    points = feats_ref.shape[0]
    groups, count = blocks_ref.shape[1], blocks_ref.shape[3]
    current, moving = w_ref[...], z_ref[...]
    if done:
        current, moving = stepped(current, moving, dense_steps(done[0][...], done[1][...]))
    mixed = mixed_of(current, moving)
    high, low = split_two(ridge_term * mixed - t_ref[...])
    cols = mixed.shape[0]
    coef_ref[0:cols] = mixed.astype(bf16)
    coef_ref[cols : 2 * cols] = high
    coef_ref[2 * cols : 3 * cols] = low
    chunk = 256
    for k, b_ref in enumerate((b0, b1, b2, b3)):
        group = lax.bitwise_xor(row, k)
        right = b_ref[...]
        right_norm = scaled_norm(right, 0)
        local = blocks_ref[u, group] - me * points
        total = jnp.zeros((cols, count), f32)
        for c in range(0, points, chunk):
            left = feats_ref[c : c + chunk, :]
            tile = tile_of(left, scaled_norm(left, 1), right, right_norm)
            place = jnp.where(iota((chunk, count), 0) + c == local, 1.0, 0.0).astype(bf16)
            total += mm(coef_ref[0:cols, c : c + chunk], tile, 1, 0)
            offset = mm(coef_ref[cols : 3 * cols, c : c + chunk], place, 1, 0)
            total += offset[:cols] + offset[cols:]
        half = groups // 2
        start = pl.multiple_of(lax.rem(group, half) * count, count)
        part_ref[lax.div(group, half), :, pl.ds(start, count)] = total
    own = cols // out_ref.shape[0]
    for o in range(out_ref.shape[0]):
        both = jnp.concatenate([part_ref[h, o * own : (o + 1) * own, :] for h in range(2)], axis=0)
        out_ref[o] = both.astype(bf16)


def dense_steps(got, rows):
    sources, double, lanes = got.shape
    own = double // 2
    wide = got.astype(f32)
    total = None
    for h in range(2):
        packed = wide[:, h * own : (h + 1) * own, :].reshape(sources * own, lanes).astype(bf16)
        part = mm(packed, rows[h * lanes : (h + 1) * lanes, :], 1, 0)
        total = part if total is None else total + part
    return total


def factor_kernel(where_ref, pivots_ref, b0, b1, b2, b3, out_ref):
    row = where_ref[0]
    count = b0.shape[1]
    pivots = pivots_ref[...]
    feats = jnp.zeros((b0.shape[0], pivots.shape[1]), f32)
    blocks = (b0, b1, b2, b3)
    for k, b_ref in enumerate(blocks):
        first = lax.bitwise_xor(row, k) * count
        chosen = iota((count, pivots.shape[1]), 0) + first == pivots
        feats += mm(b_ref[...], jnp.where(chosen, 1.0, 0.0).astype(bf16), 1, 0)
    left = feats.T
    left_norm = scaled_norm(left, 1)
    left = left.astype(bf16)
    for k, b_ref in enumerate(blocks):
        right = b_ref[...]
        start = pl.multiple_of(lax.bitwise_xor(row, k) * count, count)
        out_ref[:, pl.ds(start, count)] = tile_of(left, left_norm, right, scaled_norm(right, 0))


def chain_kernel(u, cap, got_ref, factor_ref, core_ref, slots_ref, out_ref):
    owners = got_ref.shape[0]
    groups, count = slots_ref.shape[1], slots_ref.shape[3]
    summed = got_ref[0].astype(f32)
    for o in range(1, owners):
        summed += got_ref[o].astype(f32)
    own = summed.shape[0] // 2
    resid = jnp.concatenate([summed[:own], summed[own:]], axis=1)
    factor = factor_ref[...]
    proj = mm(resid.astype(bf16), factor, 1, 1)
    lifted = mm(proj.astype(bf16), core_ref[...], 1, 1).astype(bf16)
    step = (resid - mm(lifted, factor, 1, 0)).astype(bf16)
    packed = []
    for g in range(groups):
        place = iota((owners * cap, count), 0) == slots_ref[u, g]
        packed.append(
            mm(step[:, g * count : (g + 1) * count], jnp.where(place, 1.0, 0.0).astype(bf16), 1, 1)
        )
    half = groups // 2
    for o in range(owners):
        lanes = [x[:, o * cap : (o + 1) * cap] for x in packed]
        both = jnp.concatenate(
            [jnp.concatenate(lanes[h * half : (h + 1) * half], axis=1) for h in range(2)], axis=0
        ).astype(bf16)
        for copy in range(out_ref.shape[0] // owners):
            out_ref[copy * owners + o] = both


def finish_kernel(
    where_ref, w_ref, z_ref, s0, s1, s2, s3, last_ref, rows0_ref, rows1_ref, wo_ref, zo_ref, dense_ref
):
    row = where_ref[0]
    cols = s0.shape[0] * s0.shape[1] // 2
    for k, s_ref in enumerate((s0, s1, s2, s3)):
        start = pl.multiple_of(lax.bitwise_xor(row, k) * cols, cols)
        dense_ref[pl.ds(start, cols), :] = dense_steps(s_ref[...], rows0_ref[...])
    current, moving = stepped(w_ref[...], z_ref[...], dense_ref[...].T)
    current, moving = stepped(current, moving, dense_steps(last_ref[...], rows1_ref[...]).T)
    wo_ref[...] = current
    zo_ref[...] = moving


VMEM = pl.BlockSpec(memory_space=pltpu.VMEM)
SMEM = pl.BlockSpec(memory_space=pltpu.SMEM)


def call(body, outs, *args, scratch=(), flops=0):
    out_bytes = sum(math.prod(o.shape) * o.dtype.itemsize for o in outs)
    in_bytes = sum(math.prod(a.shape) * a.dtype.itemsize for a in args)
    return pl.pallas_call(
        body,
        out_shape=outs,
        in_specs=[SMEM if a.ndim == 1 else VMEM for a in args],
        out_specs=[VMEM] * len(outs),
        scratch_shapes=list(scratch),
        compiler_params=pltpu.CompilerParams(vmem_limit_bytes=40 * 2**20),
        cost_estimate=pl.CostEstimate(
            flops=int(flops), bytes_accessed=in_bytes + out_bytes, transcendentals=0
        ),
    )(*args)


def like(shape, dtype=bf16):
    return jax.ShapeDtypeStruct(shape, dtype)


def swap_rows(value, k):
    count = lax.axis_size("rows")
    return lax.ppermute(value, "rows", [(i, i ^ k) for i in range(count)])


def with_kernels(features, current, moving, goal, coefficients, momentum, block_index, pivot_index, core):
    rows, owners = lax.axis_size("rows"), lax.axis_size("pts")
    points, width = features.shape
    block = block_index.shape[1]
    rank = pivot_index.shape[1]
    outputs = coefficients.shape[1]
    count = block // rows
    cap = 3 * count // owners
    cols = outputs // rows
    own = cols // owners
    where = jnp.stack([lax.axis_index("rows"), lax.axis_index("pts")]).astype(i32)
    blocks = block_index.reshape(UPDATES, rows, 1, count)
    flops = 2.0 * points * block * (width + 3 * cols)

    packed = call(
        functools.partial(pack_kernel, cap, owners),
        [like((owners, cap, width))] * UPDATES,
        where,
        blocks,
        features,
    )
    came = [lax.all_to_all(packed[u], "pts", 0, 0, tiled=True) for u in range(UPDATES)]
    slots, *place = call(
        functools.partial(index_kernel, cap, owners, points),
        [like((UPDATES, rows, 1, count), i32)] + [like((rows * cap, points))] * UPDATES,
        where,
        blocks,
    )
    feats = []
    for u in range(UPDATES):
        (mine,) = call(
            functools.partial(compact_kernel, u), [like((width, count))], where, slots, came[u]
        )
        feats.append([mine] + [swap_rows(mine, k) for k in range(1, rows)])

    half = rows // 2
    done = []
    for u in range(UPDATES):
        (pieces,) = call(
            functools.partial(partial_kernel, u),
            [like((owners, 2 * own, half * count))],
            where,
            blocks,
            features,
            *feats[u],
            current,
            moving,
            goal,
            *done,
            scratch=[pltpu.VMEM((2, cols, half * count), f32), pltpu.VMEM((3 * cols, points), bf16)],
            flops=flops,
        )
        summed = lax.all_to_all(pieces, "pts", 0, 0, tiled=True)
        (factor,) = call(
            factor_kernel,
            [like((rank, block))],
            where,
            pivot_index[u][None, :],
            *feats[u],
            flops=2.0 * rank * block * (2 * width),
        )
        last = u == UPDATES - 1
        copies = owners * (rows if last else 1)
        (steps,) = call(
            functools.partial(chain_kernel, u, cap),
            [like((copies, 2 * own, half * cap))],
            summed,
            factor,
            core[u],
            slots,
        )
        if last:
            final = lax.all_to_all(steps, ("rows", "pts"), 0, 0, tiled=True)
        else:
            got = lax.all_to_all(steps, "pts", 0, 0, tiled=True)
            done = [got, place[u]]
            first = [got] + [swap_rows(got, k) for k in range(1, rows)]

    return call(
        finish_kernel,
        [like(coefficients.shape, f32)] * 2,
        where,
        coefficients,
        momentum,
        *first,
        final,
        *place,
        scratch=[pltpu.VMEM((outputs, points), f32)],
    )


def kernel_tile(left_rows, right_rows):
    inner_prod = mm(left_rows, right_rows, 1, 1)
    left_sq = jnp.sum(jnp.square(left_rows.astype(f32)), axis=1)
    right_sq = jnp.sum(jnp.square(right_rows.astype(f32)), axis=1)
    squared = left_sq[:, None] + right_sq[None, :] - 2.0 * inner_prod
    return jnp.exp(squared * (-3.5 / left_rows.shape[1])).astype(bf16)


def with_operations(features, current, moving, goal, coefficients, momentum, block_index, pivot_index, core):
    row_count, pts_count = lax.axis_size("rows"), lax.axis_size("pts")
    row_id, pts_id = lax.axis_index("rows"), lax.axis_index("pts")
    points = features.shape[0]
    block = block_index.shape[1]
    outputs = coefficients.shape[1]
    per_row = block // row_count
    per_device = per_row // pts_count
    row_cols = outputs // row_count
    own_cols = row_cols // pts_count
    ids = iota((points, 1), 0) + pts_id * points
    place = [(ids == block_index[u][None, :]).astype(bf16) for u in range(UPDATES)]
    own_rows = []
    for u in range(UPDATES):
        mine = lax.dynamic_slice_in_dim(place[u], row_id * per_row, per_row, axis=1)
        own_rows.append(mm(mine, features, 0, 0).astype(bf16).reshape(pts_count, per_device, -1))
    came = lax.all_to_all(jnp.concatenate(own_rows, axis=1), "pts", 0, 0, tiled=False)
    chunk = jnp.sum(came.astype(f32), axis=0).astype(bf16)
    spread = lax.all_gather(lax.all_gather(chunk, "pts", axis=0), "rows", axis=0)
    spread = spread.reshape(row_count, pts_count, UPDATES, per_device, features.shape[1])
    all_steps = []
    for u in range(UPDATES):
        block_feats = spread[:, :, u].reshape(block, features.shape[1])
        mixed = mixed_of(current, moving)
        high, low = split_two(ridge_term * mixed - goal)
        tile = kernel_tile(features, block_feats)
        partial_value = (
            mm(mixed.astype(bf16), tile, 1, 0) + mm(high, place[u], 1, 0) + mm(low, place[u], 1, 0)
        )
        pieces = partial_value.astype(bf16).reshape(pts_count, own_cols, block)
        summed = lax.all_to_all(pieces, "pts", 0, 0, tiled=False)
        resid = jnp.sum(summed.astype(f32), axis=0)
        at_pivot = (iota((block, 1), 0) == pivot_index[u][None, :]).astype(bf16)
        factor = kernel_tile(block_feats, mm(at_pivot, block_feats, 0, 0).astype(bf16))
        proj = mm(resid.astype(bf16), factor, 1, 0)
        lifted = mm(proj.astype(bf16), core[u], 1, 1).astype(bf16)
        step_bf = (resid - mm(lifted, factor, 1, 1)).astype(bf16)
        steps = lax.all_gather(step_bf, "pts", axis=0, tiled=True)
        change = mm(steps, place[u], 1, 1)
        all_steps.append(change.astype(bf16))
        current, moving = stepped(current, moving, change)
    gathered = lax.all_gather(jnp.stack(all_steps), "rows", axis=1, tiled=True)
    current, moving = coefficients, momentum
    for u in range(UPDATES):
        current, moving = stepped(current, moving, gathered[u].T.astype(f32))
    return (current, moving)


def shards(features, targets, coefficients, momentum, block_index, pivot_index, nystrom_core):
    rows, owners = lax.axis_size("rows"), lax.axis_size("pts")
    outputs = coefficients.shape[1]
    cols = outputs // rows
    count = block_index.shape[1] // rows
    first = lax.axis_index("rows") * cols

    def own_columns(value):
        return lax.dynamic_slice_in_dim(value, first, cols, axis=1).T.astype(f32)

    fits = rows == 4 and cols == 8 * owners and count % 128 == 0 and (3 * count // owners) % 64 == 0
    plan = with_kernels if fits else with_operations
    current, moving = plan(
        features,
        own_columns(coefficients),
        own_columns(momentum),
        own_columns(targets),
        coefficients,
        momentum,
        block_index,
        pivot_index,
        nystrom_core,
    )
    return (current, moving)


def solution(mesh):
    in_specs = (P("pts", None), P("pts", None), P("pts", None), P("pts", None), P(), P(), P())
    out_specs = (P("pts", None), P("pts", None))
    return jax.shard_map(shards, mesh=mesh, in_specs=in_specs, out_specs=out_specs, check_vma=False)
```

time: 222 us -> 140 us (0.63)
  blocking collectives: 111 us -> 14.8 us
  Pallas kernels: 0 us -> 34.4 us
  matrix products: 28.8 us -> 0 us
  starting transfers between devices: 9.06 us -> 30.1 us
  local copies, waits for them, and re-layouts: 10.6 us -> 27 us
  between operations: 14.3 us -> 1.02 us
  waiting for transfers between devices: 39.3 us -> 30 us
  other arithmetic: 8.36 us -> 1 us
    all_gather x3 -> x0, blocking collectives: 95 us -> none  [the longest x2 62.2 us: shards(): steps = lax.all_gather(step_bf, 'pts', axis=0, tiled=True)]
    pallas_call x0 -> x11, Pallas kernels: none -> 34.4 us  [call(): pl.pallas_call(body, out_shape=outs, in_specs=[SMEM if a.ndim == 1 else V...]
    dot_general x18 -> x0, matrix products: 28.8 us -> none  [mm(): lax.dot_general(a, b, (((ca,), (cb,)), ((), ())), preferred_element_type=...]
    all_gather x2 -> x0, waiting for transfers between devices: 25.8 us -> none  [the longest x1 14.3 us: shards(): gathered = lax.all_gather(jnp.stack(all_steps), 'rows', axis=1, tiled=True)]
    ppermute x0 -> x9, waiting for transfers between devices: none -> 19.6 us  [swap_rows(): return lax.ppermute(value, 'rows', [(i, i ^ k) for i in range(count)])]
    all_to_all x2 -> x5, starting transfers between devices: 8.99 us -> 24.2 us  [the longest x2 11 us: with_kernels(): lax.all_to_all(packed[u], 'pts', 0, 0, tiled=True)]
    unnamed x43 -> x79, local copies, waits for them, and re-layouts: 7.27 us -> 19.7 us
    ppermute x0 -> x9, starting transfers between devices: none -> 5.87 us  [swap_rows(): return lax.ppermute(value, 'rows', [(i, i ^ k) for i in range(count)])]
  transfers between devices with their start and end apart: 4 -> 14, of which waited for: 4 -> 10; matrix products, arithmetic and copies ran while one was open for 4% -> 8% of each run, Pallas kernels for 0% -> 8%
where the time goes in v3:
time: 140 us; the launch traced here: 138 us
  Pallas kernels  34.4 us (25%)
  starting transfers between devices  30.1 us (22%)
  waiting for transfers between devices  30 us (21%)
  local copies, waits for them, and re-layouts  27 us (19%)
  blocking collectives  14.8 us (11%)
    pallas_call x11, Pallas kernels, call(): pl.pallas_call(body, out_shape=outs, in_specs=[SMEM if a.ndim == 1 else V...  34.4 us
    unnamed x79, local copies, waits for them, and re-layouts  19.7 us
    ppermute x9, waiting for transfers between devices, swap_rows(): return lax.ppermute(value, 'rows', [(i, i ^ k) for i in range(count)])  19.6 us
    all_to_all x1, blocking collectives, with_kernels(): summed = lax.all_to_all(pieces, 'pts', 0, 0, tiled=True)  14.8 us
    all_to_all x2, starting transfers between devices, with_kernels(): lax.all_to_all(packed[u], 'pts', 0, 0, tiled=True)  11 us
    all_to_all x1, starting transfers between devices, with_kernels(): summed = lax.all_to_all(pieces, 'pts', 0, 0, tiled=True)  6.01 us
    ppermute x9, starting transfers between devices, swap_rows(): return lax.ppermute(value, 'rows', [(i, i ^ k) for i in range(count)])  5.87 us
    dynamic_slice x2, local copies, waits for them, and re-layouts, own_columns(): return lax.dynamic_slice_in_dim(value, first, cols, axis=1).T.astype(f32)  3.92 us
  transfers between devices with their start and end apart: 14, of which 10 were waited for; matrix products, arithmetic and copies ran while one was open for 8% of the time, Pallas kernels for 8%

profile of v3, /device:TPU:0, one launch (start us, length us, event | category | flops | bytes accessed | tf_op | source)
XLA Modules:
  0.0 138.4 jit_solution(8800809139256219209)
XLA Ops:
  0.6 0.0 copy-start
  0.7 0.8 reshape.7.blocks_ref
  1.5 0.1 pad_add_fusion.where_ref
  1.5 0.9 copy-done.15
  2.5 2.3 %shard_map.87 = (bf16[8,192,128]{2,1,0:T(8,128)(2,1)}, bf16[8,192,128]{2,1,0:T(8,128)(2,1)}) custom-call(s32[2]{0:T(128)S(1)} %pad_add_fusion.where_ref, s32[2,4,1,512]{3,2,1,0:T(1,128)S(1)} %reshape.7.blocks_ref, bf16[1024,128]{1,0:T(8,128)(2,1)S(1)} %copy-done.15), custom_call_target="tpu_custom_call" | custom-call | bytes 1064968 | tf_op jit(solution)/shard_map/pallas_call | solution.py:230
  4.8 7.3 %all-to-all-start = ((bf16[8,192,128]{2,1,0:T(8,128)(2,1)}), bf16[8,192,128]{2,1,0:T(8,128)(2,1)S(1)}, u32[]{:S(2)}, u32[]{:S(2)}) async-start(bf16[8,192,128]{2,1,0:T(8,128)(2,1)} %get-tuple-element.8), calls=%async_computation | async-start | bytes 786432 | tf_op jit(solution)/shard_map/all_to_all | solution.py:273
  12.1 1.9 %shard_map.86 = (s32[2,4,1,512]{3,2,1,0:T(1,128)S(1)}, bf16[768,1024]{1,0:T(8,128)(2,1)S(1)}, bf16[768,1024]{1,0:T(8,128)(2,1)S(1)}) custom-call(s32[2]{0:T(128)S(1)} %pad_add_fusion.where_ref, s32[2,4,1,512]{3,2,1,0:T(1,128)S(1)} %reshape.7.blocks_ref), custom_call_target="tpu_custom_call" | custom-call | bytes 3178504 | tf_op jit(solution)/shard_map/pallas_call | solution.py:230
  14.0 1.2 copy-done.5
  15.2 3.1 %constant_dynamic-slice_fusion.1 = (f32[1024,64]{1,0:T(8,128)}, f32[1024,64]{1,0:T(8,128)}) fusion(f32[1024,256]{1,0:T(8,128)} %z_ref.1, s32[]{:T(128)S(6)} %select_n.2, f32[1024,256]{1,0:T(8,128)} %w_ref.1), kind=kLoop, calls=%fused_computation.4 | loop fusion | bytes 1048580 | tf_op jit(solution)/shard_map/dynamic_slice | solution.py:407
  18.2 1.3 copy.12
  19.5 0.0 copy-start.9
  19.5 1.3 copy.13
  20.9 0.8 constant_dynamic-slice_fusion
  21.7 1.7 %copy.14 = bf16[1024,64]{0,1:T(8,128)(2,1)} copy(bf16[1024,64]{1,0:T(8,128)(2,1)} %constant_dynamic-slice_fusion) | data formatting | bytes 262144
  23.5 0.4 all-to-all-done.got_ref
  23.8 1.0 shard_map.88.b0
  24.8 0.1 collective-permute-start
  24.9 1.6 %collective-permute-start.1 = (bf16[128,512]{1,0:T(8,128)(2,1)S(1)}, bf16[128,512]{1,0:T(8,128)(2,1)S(1)}, u32[]{:S(2)}, u32[]{:S(2)}) collective-permute-start(bf16[128,512]{1,0:T(8,128)(2,1)S(1)} %shard_map.88.b0), channel_id=1, source_target_pairs={{0,16},{8,24},{16,0},{24,8},{1,17},{9,25},{17,1},{25,9},{2,18},{10... | collective-permute-start | bytes 393224 | tf_op jit(solution)/shard_map/ppermute | solution.py:249
  26.5 0.3 collective-permute-start.2
  26.8 0.9 convert_bitcast_fusion.t_ref
  27.7 0.0 copy-start.13
  27.7 3.5 %collective-permute-done.1.b2 = bf16[128,512]{1,0:T(8,128)(2,1)S(1)} collective-permute-done((bf16[128,512]{1,0:T(8,128)(2,1)S(1)}, bf16[128,512]{1,0:T(8,128)(2,1)S(1)}, u32[]{:S(2)}, u32[]{:S(2)}) %collective-permute-start.1) | collective-permute-done | bytes 131104 | tf_op jit(solution)/shard_map/ppermute | solution.py:249
  31.3 1.9 %collective-permute-done.2.b3 = bf16[128,512]{1,0:T(8,128)(2,1)S(1)} collective-permute-done((bf16[128,512]{1,0:T(8,128)(2,1)S(1)}, bf16[128,512]{1,0:T(8,128)(2,1)S(1)}, u32[]{:S(2)}, u32[]{:S(2)}) %collective-permute-start.2) | collective-permute-done | bytes 131104 | tf_op jit(solution)/shard_map/ppermute | solution.py:249
  33.2 5.7 %shard_map.89 = bf16[8,16,1024]{2,1,0:T(8,128)(2,1)S(1)} custom-call(s32[2]{0:T(128)S(1)} %pad_add_fusion.where_ref, s32[2,4,1,512]{3,2,1,0:T(1,128)S(1)} %reshape.7.blocks_ref, bf16[1024,128]{1,0:T(8,128)(2,1)S(1)} %copy-done.16, bf16[128,512]{1,0:T(8,128)(2,1)S(1)} %shard_map.88.b0, bf16[128,512]{1,0:T(8,128)(2,1)S(1)} %collective-permute-done.b1, ...), custom_call_target="tpu_custom_call" | custom-call | flops 1342177280 | bytes 1851400 | tf_op jit(solution)/shard_map/pallas_call | solution.py:230
  38.9 14.8 %all_to_all.30.got_ref = bf16[8,16,1024]{2,1,0:T(8,128)(2,1)S(1)} all-to-all(bf16[8,16,1024]{2,1,0:T(8,128)(2,1)S(1)} %shard_map.89), channel_id=1, replica_groups=mesh['rows'=4,'pts'=8] {'pts'}, dimensions={0} | all-to-all | bytes 524288 | tf_op jit(solution)/shard_map/all_to_all | solution.py:304
  53.7 3.7 %all-to-all-start.3 = ((bf16[8,192,128]{2,1,0:T(8,128)(2,1)}), bf16[8,192,128]{2,1,0:T(8,128)(2,1)S(1)}, u32[]{:S(2)}, u32[]{:S(2)}) async-start(bf16[8,192,128]{2,1,0:T(8,128)(2,1)} %get-tuple-element.9), calls=%async_computation.3 | async-start | bytes 786432 | tf_op jit(solution)/shard_map/all_to_all | solution.py:273
  57.5 1.3 fusion
  58.8 1.3 slice_bitcast_fusion
  60.1 2.2 %shard_map.90.factor_ref = bf16[512,2048]{1,0:T(8,128)(2,1)S(1)} custom-call(s32[2]{0:T(128)S(1)} %copy-done.33, s32[1,512]{1,0:T(1,128)S(1)} %get-tuple-element.15.pivots_ref, bf16[128,512]{1,0:T(8,128)(2,1)S(1)} %shard_map.88.b0, bf16[128,512]{1,0:T(8,128)(2,1)S(1)} %copy-done.21, bf16[128,512]{1,0:T(8,128)(2,1)S(1)} %copy-done.25, ...), custom_call_target="tpu_custom_call" | custom-call | flops 536870912 | bytes 2623496 | tf_op jit(solution)/shard_map/pallas_call | solution.py:230
  62.4 3.5 %shard_map.91 = bf16[8,16,384]{2,1,0:T(8,128)(2,1)} custom-call(bf16[8,16,1024]{2,1,0:T(8,128)(2,1)S(1)} %all_to_all.30.got_ref, bf16[512,2048]{1,0:T(8,128)(2,1)S(1)} %shard_map.90.factor_ref, bf16[512,512]{1,0:T(8,128)(2,1)S(1)} %get-tuple-element.13.core_ref, s32[2,4,1,512]{3,2,1,0:T(1,128)S(1)} %get-tuple-element.7.slots_ref), custom_call_target="tpu_custom_call" | custom-call | bytes 2998272 | tf_op jit(solution)/shard_map/pallas_call | solution.py:230
  65.9 3.2 %all-to-all-done.3.got_ref = bf16[8,192,128]{2,1,0:T(8,128)(2,1)S(1)} async-done(((bf16[8,192,128]{2,1,0:T(8,128)(2,1)}), bf16[8,192,128]{2,1,0:T(8,128)(2,1)S(1)}, u32[]{:S(2)}, u32[]{:S(2)}) %all-to-all-start.3) | async-done | bytes 393248 | tf_op jit(solution)/shard_map/all_to_all | solution.py:273
  69.1 3.6 %all-to-all-start.2 = ((bf16[8,16,384]{2,1,0:T(8,128)(2,1)}), bf16[8,16,384]{2,1,0:T(8,128)(2,1)S(1)}, u32[]{:S(2)}, u32[]{:S(2)}) async-start(bf16[8,16,384]{2,1,0:T(8,128)(2,1)} %shard_map.91), calls=%async_computation.2 | async-start | bytes 196608 | tf_op jit(solution)/shard_map/all_to_all | solution.py:326
  72.8 1.0 shard_map.92.b0
  73.8 0.1 collective-permute-start.6
  73.9 1.6 %collective-permute-start.7 = (bf16[128,512]{1,0:T(8,128)(2,1)S(1)}, bf16[128,512]{1,0:T(8,128)(2,1)S(1)}, u32[]{:S(2)}, u32[]{:S(2)}) collective-permute-start(bf16[128,512]{1,0:T(8,128)(2,1)S(1)} %shard_map.92.b0), channel_id=1, source_target_pairs={{0,16},{8,24},{16,0},{24,8},{1,17},{9,25},{17,1},{25,9},{2,18},{10... | collective-permute-start | bytes 393224 | tf_op jit(solution)/shard_map/ppermute | solution.py:249
  75.4 0.3 collective-permute-start.8
  75.7 4.5 %collective-permute-done.7.b2 = bf16[128,512]{1,0:T(8,128)(2,1)S(1)} collective-permute-done((bf16[128,512]{1,0:T(8,128)(2,1)S(1)}, bf16[128,512]{1,0:T(8,128)(2,1)S(1)}, u32[]{:S(2)}, u32[]{:S(2)}) %collective-permute-start.7) | collective-permute-done | bytes 131104 | tf_op jit(solution)/shard_map/ppermute | solution.py:249
  80.2 1.9 %collective-permute-done.8.b3 = bf16[128,512]{1,0:T(8,128)(2,1)S(1)} collective-permute-done((bf16[128,512]{1,0:T(8,128)(2,1)S(1)}, bf16[128,512]{1,0:T(8,128)(2,1)S(1)}, u32[]{:S(2)}, u32[]{:S(2)}) %collective-permute-start.8) | collective-permute-done | bytes 131104 | tf_op jit(solution)/shard_map/ppermute | solution.py:249
  82.2 0.0 copy-start.10
  82.2 1.0 copy-done.10
  83.2 0.9 copy-done.12
  84.1 0.9 copy-done.14
  85.1 0.9 copy-done.17
  86.0 6.8 %shard_map.93 = bf16[8,16,1024]{2,1,0:T(8,128)(2,1)} custom-call(s32[2]{0:T(128)S(1)} %copy-done.34, s32[2,4,1,512]{3,2,1,0:T(1,128)S(1)} %copy-done.19, bf16[1024,128]{1,0:T(8,128)(2,1)S(1)} %copy-done.17, bf16[128,512]{1,0:T(8,128)(2,1)S(1)} %shard_map.92.b0, bf16[128,512]{1,0:T(8,128)(2,1)S(1)} %collective-permute-done.6.b1, ...), custom_call_target="tpu_custom_call" | custom-call | flops 1342177280 | bytes 3522568 | tf_op jit(solution)/shard_map/pallas_call | solution.py:230
  92.8 6.0 %all-to-all-start.4 = ((bf16[8,16,1024]{2,1,0:T(8,128)(2,1)}), bf16[8,16,1024]{2,1,0:T(8,128)(2,1)S(1)}, u32[]{:S(2)}, u32[]{:S(2)}) async-start(bf16[8,16,1024]{2,1,0:T(8,128)(2,1)} %shard_map.93), calls=%async_computation.4 | async-start | bytes 524288 | tf_op jit(solution)/shard_map/all_to_all | solution.py:304
  98.9 0.9 copy-done.23
  99.8 0.9 copy-done.27
  100.7 0.9 copy-done.31
  101.6 0.7 copy-done.35
  102.2 0.7 copy-done.37
  102.9 2.2 %shard_map.94.factor_ref = bf16[512,2048]{1,0:T(8,128)(2,1)S(1)} custom-call(s32[2]{0:T(128)S(1)} %copy-done.35, s32[1,512]{1,0:T(1,128)S(1)} %copy-done.37, bf16[128,512]{1,0:T(8,128)(2,1)S(1)} %shard_map.92.b0, bf16[128,512]{1,0:T(8,128)(2,1)S(1)} %copy-done.23, bf16[128,512]{1,0:T(8,128)(2,1)S(1)} %copy-done.27, bf16[128,512]{1,0:T(8,128)(2,1)S(1)} %copy-done.31), custom_call_target="tpu_custom_call" | custom-call | flops 536870912 | bytes 2623496 | tf_op jit(solution)/shard_map/pallas_call | solution.py:230
  105.2 3.1 %all-to-all-done.4.got_ref = bf16[8,16,1024]{2,1,0:T(8,128)(2,1)S(1)} async-done(((bf16[8,16,1024]{2,1,0:T(8,128)(2,1)}), bf16[8,16,1024]{2,1,0:T(8,128)(2,1)S(1)}, u32[]{:S(2)}, u32[]{:S(2)}) %all-to-all-start.4) | async-done | bytes 262176 | tf_op jit(solution)/shard_map/all_to_all | solution.py:304
  108.2 3.6 %shard_map.95 = bf16[32,16,384]{2,1,0:T(8,128)(2,1)} custom-call(bf16[8,16,1024]{2,1,0:T(8,128)(2,1)S(1)} %all-to-all-done.4.got_ref, bf16[512,2048]{1,0:T(8,128)(2,1)S(1)} %shard_map.94.factor_ref, bf16[512,512]{1,0:T(8,128)(2,1)S(1)} %get-tuple-element.12.core_ref, s32[2,4,1,512]{3,2,1,0:T(1,128)S(1)} %get-tuple-element.7.slots_ref), custom_call_target="tpu_custom_call" | custom-call | bytes 3293184 | tf_op jit(solution)/shard_map/pallas_call | solution.py:230
  111.9 3.6 %all-to-all-start.5 = ((bf16[32,16,384]{2,1,0:T(8,128)(2,1)}), bf16[32,16,384]{2,1,0:T(8,128)(2,1)S(1)}, u32[]{:S(2)}, u32[]{:S(2)}) async-start(bf16[32,16,384]{2,1,0:T(8,128)(2,1)} %shard_map.95), calls=%async_computation.5 | async-start | bytes 786432 | tf_op jit(solution)/shard_map/all_to_all | solution.py:324
  115.5 0.3 collective-permute-start.3
  115.8 1.7 %collective-permute-start.4 = (bf16[8,16,384]{2,1,0:T(8,128)(2,1)S(1)}, bf16[8,16,384]{2,1,0:T(8,128)(2,1)S(1)}, u32[]{:S(2)}, u32[]{:S(2)}) collective-permute-start(bf16[8,16,384]{2,1,0:T(8,128)(2,1)S(1)} %copy-done.8), channel_id=1, source_target_pairs={{0,16},{8,24},{16,0},{24,8},{1,17},{9,25},{17,1},{25,9},{2,18},{10... | collective-permute-start | bytes 294920 | tf_op jit(solution)/shard_map/ppermute | solution.py:249
  117.5 6.2 %collective-permute-done.4.s2 = bf16[8,16,384]{2,1,0:T(8,128)(2,1)S(1)} collective-permute-done((bf16[8,16,384]{2,1,0:T(8,128)(2,1)S(1)}, bf16[8,16,384]{2,1,0:T(8,128)(2,1)S(1)}, u32[]{:S(2)}, u32[]{:S(2)}) %collective-permute-start.4) | collective-permute-done | bytes 98336 | tf_op jit(solution)/shard_map/ppermute | solution.py:249
  123.7 1.6 %collective-permute-done.5.s3 = bf16[8,16,384]{2,1,0:T(8,128)(2,1)S(1)} collective-permute-done((bf16[8,16,384]{2,1,0:T(8,128)(2,1)S(1)}, bf16[8,16,384]{2,1,0:T(8,128)(2,1)S(1)}, u32[]{:S(2)}, u32[]{:S(2)}) %collective-permute-start.5) | collective-permute-done | bytes 98336 | tf_op jit(solution)/shard_map/ppermute | solution.py:249
  125.3 3.7 %all-to-all-done.5.last_ref = bf16[32,16,384]{2,1,0:T(8,128)(2,1)S(1)} async-done(((bf16[32,16,384]{2,1,0:T(8,128)(2,1)}), bf16[32,16,384]{2,1,0:T(8,128)(2,1)S(1)}, u32[]{:S(2)}, u32[]{:S(2)}) %all-to-all-start.5) | async-done | bytes 393248 | tf_op jit(solution)/shard_map/all_to_all | solution.py:324
  129.0 1.2 copy-done.1
  130.2 1.2 copy-done.2
  131.5 1.4 %copy-done.4 = bf16[768,1024]{1,0:T(8,128)(2,1)S(1)} copy-done((bf16[768,1024]{1,0:T(8,128)(2,1)S(1)}, bf16[768,1024]{1,0:T(8,128)(2,1)}, u32[]{:S(2)}) %copy-start.4) | copy-done | bytes 1572888
  132.9 1.4 %copy-done.6 = bf16[768,1024]{1,0:T(8,128)(2,1)S(1)} copy-done((bf16[768,1024]{1,0:T(8,128)(2,1)S(1)}, bf16[768,1024]{1,0:T(8,128)(2,1)}, u32[]{:S(2)}) %copy-start.6) | copy-done | bytes 1572888
  134.3 4.1 %shard_map.96 = (f32[1024,256]{1,0:T(8,128)}, f32[1024,256]{1,0:T(8,128)}) custom-call(s32[2]{0:T(128)S(1)} %copy-done.36, f32[1024,256]{1,0:T(8,128)S(1)} %copy-done.1, f32[1024,256]{1,0:T(8,128)S(1)} %copy-done.2, bf16[8,16,384]{2,1,0:T(8,128)(2,1)S(1)} %copy-done.8, bf16[8,16,384]{2,1,0:T(8,128)(2,1)S(1)} %collective-permute-done.3.s1, ...), custom_call_target="tpu_custom_call" | custom-call | bytes 8126472 | tf_op jit(solution)/shard_map/pallas_call | solution.py:230
  (62 shorter events, 0.1 us)
Async XLA Ops:
  0.6 20.2 %copy-start = (bf16[1024,256]{1,0:T(8,128)(2,1)S(1)}, bf16[1024,256]{1,0:T(8,128)(2,1)}, u32[]{:S(2)}) copy-start(bf16[1024,256]{1,0:T(8,128)(2,1)} %param.8) | copy-start | bytes 1572868
  1.5 31.7 %copy-start.18 = (s32[2,4,1,512]{3,2,1,0:T(1,128)}, s32[2,4,1,512]{3,2,1,0:T(1,128)S(1)}, u32[]{:S(2)}) copy-start(s32[2,4,1,512]{3,2,1,0:T(1,128)S(1)} %reshape.7.blocks_ref) | copy-start | bytes 49156
  1.5 1.0 copy-start.15
  2.5 30.7 %copy-start.32 = (s32[2]{0:T(128)}, s32[2]{0:T(128)S(1)}, u32[]{:S(2)}) copy-start(s32[2]{0:T(128)S(1)} %pad_add_fusion.where_ref) | copy-start | bytes 28
  4.8 19.0 %all-to-all-start = ((bf16[8,192,128]{2,1,0:T(8,128)(2,1)}), bf16[8,192,128]{2,1,0:T(8,128)(2,1)S(1)}, u32[]{:S(2)}, u32[]{:S(2)}) async-start(bf16[8,192,128]{2,1,0:T(8,128)(2,1)} %get-tuple-element.8), calls=%async_computation | async-start | bytes 786432 | tf_op jit(solution)/shard_map/all_to_all | solution.py:273
  14.0 1.2 copy-start.5
  15.2 67.0 %copy-start.3 = (bf16[768,1024]{1,0:T(8,128)(2,1)}, bf16[768,1024]{1,0:T(8,128)(2,1)S(1)}, u32[]{:S(2)}) copy-start(bf16[768,1024]{1,0:T(8,128)(2,1)S(1)} %get-tuple-element.10.rest_1_.rows0_ref) | copy-start | bytes 4718596
  18.2 14.9 %copy-start.16 = (bf16[1024,128]{1,0:T(8,128)(2,1)S(1)}, bf16[1024,128]{1,0:T(8,128)(2,1)}, u32[]{:S(2)}) copy-start(bf16[1024,128]{1,0:T(8,128)(2,1)} %feats_ref.5) | copy-start | bytes 786436
  19.5 19.4 %copy-start.9 = (f32[1024,64]{0,1:T(8,128)}, f32[1024,64]{0,1:T(8,128)S(1)}, u32[]{:S(2)}) copy-start(f32[1024,64]{0,1:T(8,128)S(1)} %copy.12) | copy-start | bytes 786436
  20.9 18.0 %copy-start.11 = (f32[1024,64]{0,1:T(8,128)}, f32[1024,64]{0,1:T(8,128)S(1)}, u32[]{:S(2)}) copy-start(f32[1024,64]{0,1:T(8,128)S(1)} %copy.13) | copy-start | bytes 786436
  24.8 2.9 %collective-permute-start = (bf16[128,512]{1,0:T(8,128)(2,1)S(1)}, bf16[128,512]{1,0:T(8,128)(2,1)S(1)}, u32[]{:S(2)}, u32[]{:S(2)}) collective-permute-start(bf16[128,512]{1,0:T(8,128)(2,1)S(1)} %shard_map.88.b0), channel_id=1, source_target_pairs={{0,8},{8,0},{16,24},{24,16},{1,9},{9,1},{17,25},{25,17},{2,10},{10... | collective-permute-start | bytes 393224 | tf_op jit(solution)/shard_map/ppermute | solution.py:249
  24.9 6.4 %collective-permute-start.1 = (bf16[128,512]{1,0:T(8,128)(2,1)S(1)}, bf16[128,512]{1,0:T(8,128)(2,1)S(1)}, u32[]{:S(2)}, u32[]{:S(2)}) collective-permute-start(bf16[128,512]{1,0:T(8,128)(2,1)S(1)} %shard_map.88.b0), channel_id=1, source_target_pairs={{0,16},{8,24},{16,0},{24,8},{1,17},{9,25},{17,1},{25,9},{2,18},{10... | collective-permute-start | bytes 393224 | tf_op jit(solution)/shard_map/ppermute | solution.py:249
  26.5 6.7 %collective-permute-start.2 = (bf16[128,512]{1,0:T(8,128)(2,1)S(1)}, bf16[128,512]{1,0:T(8,128)(2,1)S(1)}, u32[]{:S(2)}, u32[]{:S(2)}) collective-permute-start(bf16[128,512]{1,0:T(8,128)(2,1)S(1)} %shard_map.88.b0), channel_id=1, source_target_pairs={{0,24},{8,16},{16,8},{24,0},{1,25},{9,17},{17,9},{25,1},{2,26},{10... | collective-permute-start | bytes 393224 | tf_op jit(solution)/shard_map/ppermute | solution.py:249
  27.7 11.2 %copy-start.13 = (f32[64,1024]{1,0:T(8,128)}, f32[64,1024]{1,0:T(8,128)S(1)}, u32[]{:S(2)}) copy-start(f32[64,1024]{1,0:T(8,128)S(1)} %convert_bitcast_fusion.t_ref) | copy-start | bytes 786436
  27.7 11.2 %copy-start.20 = (bf16[128,512]{1,0:T(8,128)(2,1)}, bf16[128,512]{1,0:T(8,128)(2,1)S(1)}, u32[]{:S(2)}) copy-start(bf16[128,512]{1,0:T(8,128)(2,1)S(1)} %collective-permute-done.b1) | copy-start | bytes 393220
  31.3 7.6 %copy-start.24 = (bf16[128,512]{1,0:T(8,128)(2,1)}, bf16[128,512]{1,0:T(8,128)(2,1)S(1)}, u32[]{:S(2)}) copy-start(bf16[128,512]{1,0:T(8,128)(2,1)S(1)} %collective-permute-done.1.b2) | copy-start | bytes 393220
  33.2 5.7 %copy-start.28 = (bf16[128,512]{1,0:T(8,128)(2,1)}, bf16[128,512]{1,0:T(8,128)(2,1)S(1)}, u32[]{:S(2)}) copy-start(bf16[128,512]{1,0:T(8,128)(2,1)S(1)} %collective-permute-done.2.b3) | copy-start | bytes 393220
  53.7 6.4 %copy-start.21 = (bf16[128,512]{1,0:T(8,128)(2,1)S(1)}, bf16[128,512]{1,0:T(8,128)(2,1)}, u32[]{:S(2)}) copy-start(bf16[128,512]{1,0:T(8,128)(2,1)} %copy-done.20) | copy-start | bytes 393220
  53.7 15.4 %all-to-all-start.3 = ((bf16[8,192,128]{2,1,0:T(8,128)(2,1)}), bf16[8,192,128]{2,1,0:T(8,128)(2,1)S(1)}, u32[]{:S(2)}, u32[]{:S(2)}) async-start(bf16[8,192,128]{2,1,0:T(8,128)(2,1)} %get-tuple-element.9), calls=%async_computation.3 | async-start | bytes 786432 | tf_op jit(solution)/shard_map/all_to_all | solution.py:273
  57.4 2.6 %copy-start.25 = (bf16[128,512]{1,0:T(8,128)(2,1)S(1)}, bf16[128,512]{1,0:T(8,128)(2,1)}, u32[]{:S(2)}) copy-start(bf16[128,512]{1,0:T(8,128)(2,1)} %copy-done.24) | copy-start | bytes 393220
  57.5 2.6 %copy-start.29 = (bf16[128,512]{1,0:T(8,128)(2,1)S(1)}, bf16[128,512]{1,0:T(8,128)(2,1)}, u32[]{:S(2)}) copy-start(bf16[128,512]{1,0:T(8,128)(2,1)} %copy-done.28) | copy-start | bytes 393220
  57.5 2.6 %copy-start.33 = (s32[2]{0:T(128)S(1)}, s32[2]{0:T(128)}, u32[]{:S(2)}) copy-start(s32[2]{0:T(128)} %copy-done.32) | copy-start | bytes 28
  62.3 10.4 %copy-start.34 = (s32[2]{0:T(128)S(1)}, s32[2]{0:T(128)}, u32[]{:S(2)}) copy-start(s32[2]{0:T(128)} %copy-done.32) | copy-start | bytes 28
  62.4 19.8 %copy-start.19 = (s32[2,4,1,512]{3,2,1,0:T(1,128)S(1)}, s32[2,4,1,512]{3,2,1,0:T(1,128)}, u32[]{:S(2)}) copy-start(s32[2,4,1,512]{3,2,1,0:T(1,128)} %copy-done.18) | copy-start | bytes 49156
  69.1 13.0 %all-to-all-start.2 = ((bf16[8,16,384]{2,1,0:T(8,128)(2,1)}), bf16[8,16,384]{2,1,0:T(8,128)(2,1)S(1)}, u32[]{:S(2)}, u32[]{:S(2)}) async-start(bf16[8,16,384]{2,1,0:T(8,128)(2,1)} %shard_map.91), calls=%async_computation.2 | async-start | bytes 196608 | tf_op jit(solution)/shard_map/all_to_all | solution.py:326
  73.8 1.9 %collective-permute-start.6 = (bf16[128,512]{1,0:T(8,128)(2,1)S(1)}, bf16[128,512]{1,0:T(8,128)(2,1)S(1)}, u32[]{:S(2)}, u32[]{:S(2)}) collective-permute-start(bf16[128,512]{1,0:T(8,128)(2,1)S(1)} %shard_map.92.b0), channel_id=1, source_target_pairs={{0,8},{8,0},{16,24},{24,16},{1,9},{9,1},{17,25},{25,17},{2,10},{10... | collective-permute-start | bytes 393224 | tf_op jit(solution)/shard_map/ppermute | solution.py:249
  73.9 6.4 %collective-permute-start.7 = (bf16[128,512]{1,0:T(8,128)(2,1)S(1)}, bf16[128,512]{1,0:T(8,128)(2,1)S(1)}, u32[]{:S(2)}, u32[]{:S(2)}) collective-permute-start(bf16[128,512]{1,0:T(8,128)(2,1)S(1)} %shard_map.92.b0), channel_id=1, source_target_pairs={{0,16},{8,24},{16,0},{24,8},{1,17},{9,25},{17,1},{25,9},{2,18},{10... | collective-permute-start | bytes 393224 | tf_op jit(solution)/shard_map/ppermute | solution.py:249
  75.4 6.7 %collective-permute-start.8 = (bf16[128,512]{1,0:T(8,128)(2,1)S(1)}, bf16[128,512]{1,0:T(8,128)(2,1)S(1)}, u32[]{:S(2)}, u32[]{:S(2)}) collective-permute-start(bf16[128,512]{1,0:T(8,128)(2,1)S(1)} %shard_map.92.b0), channel_id=1, source_target_pairs={{0,24},{8,16},{16,8},{24,0},{1,25},{9,17},{17,9},{25,1},{2,26},{10... | collective-permute-start | bytes 393224 | tf_op jit(solution)/shard_map/ppermute | solution.py:249
  75.7 17.1 %copy-start.22 = (bf16[128,512]{1,0:T(8,128)(2,1)}, bf16[128,512]{1,0:T(8,128)(2,1)S(1)}, u32[]{:S(2)}) copy-start(bf16[128,512]{1,0:T(8,128)(2,1)S(1)} %collective-permute-done.6.b1) | copy-start | bytes 393220
  80.2 12.6 %copy-start.26 = (bf16[128,512]{1,0:T(8,128)(2,1)}, bf16[128,512]{1,0:T(8,128)(2,1)S(1)}, u32[]{:S(2)}) copy-start(bf16[128,512]{1,0:T(8,128)(2,1)S(1)} %collective-permute-done.7.b2) | copy-start | bytes 393220
  82.1 10.7 %copy-start.30 = (bf16[128,512]{1,0:T(8,128)(2,1)}, bf16[128,512]{1,0:T(8,128)(2,1)S(1)}, u32[]{:S(2)}) copy-start(bf16[128,512]{1,0:T(8,128)(2,1)S(1)} %collective-permute-done.8.b3) | copy-start | bytes 393220
  82.1 10.7 %copy-start.7 = (bf16[8,16,384]{2,1,0:T(8,128)(2,1)}, bf16[8,16,384]{2,1,0:T(8,128)(2,1)S(1)}, u32[]{:S(2)}) copy-start(bf16[8,16,384]{2,1,0:T(8,128)(2,1)S(1)} %all-to-all-done.2.rest_0_.s0) | copy-start | bytes 294916
  82.2 1.0 copy-start.10
  83.2 0.9 copy-start.12
  84.1 0.9 copy-start.14
  85.1 0.9 copy-start.17
  92.8 15.4 %all-to-all-start.4 = ((bf16[8,16,1024]{2,1,0:T(8,128)(2,1)}), bf16[8,16,1024]{2,1,0:T(8,128)(2,1)S(1)}, u32[]{:S(2)}, u32[]{:S(2)}) async-start(bf16[8,16,1024]{2,1,0:T(8,128)(2,1)} %shard_map.93), calls=%async_computation.4 | async-start | bytes 524288 | tf_op jit(solution)/shard_map/all_to_all | solution.py:304
  98.9 0.9 copy-start.23
  99.8 0.9 copy-start.27
  100.7 0.9 copy-start.31
  101.6 0.7 copy-start.35
  102.2 0.7 copy-start.37
  105.1 10.3 %copy-start.8 = (bf16[8,16,384]{2,1,0:T(8,128)(2,1)S(1)}, bf16[8,16,384]{2,1,0:T(8,128)(2,1)}, u32[]{:S(2)}) copy-start(bf16[8,16,384]{2,1,0:T(8,128)(2,1)} %copy-done.7) | copy-start | bytes 294916
  105.1 23.9 %copy-start.36 = (s32[2]{0:T(128)S(1)}, s32[2]{0:T(128)}, u32[]{:S(2)}) copy-start(s32[2]{0:T(128)} %copy-done.32) | copy-start | bytes 28
  111.9 17.2 %all-to-all-start.5 = ((bf16[32,16,384]{2,1,0:T(8,128)(2,1)}), bf16[32,16,384]{2,1,0:T(8,128)(2,1)S(1)}, u32[]{:S(2)}, u32[]{:S(2)}) async-start(bf16[32,16,384]{2,1,0:T(8,128)(2,1)} %shard_map.95), calls=%async_computation.5 | async-start | bytes 786432 | tf_op jit(solution)/shard_map/all_to_all | solution.py:324
  115.5 2.0 %collective-permute-start.3 = (bf16[8,16,384]{2,1,0:T(8,128)(2,1)S(1)}, bf16[8,16,384]{2,1,0:T(8,128)(2,1)S(1)}, u32[]{:S(2)}, u32[]{:S(2)}) collective-permute-start(bf16[8,16,384]{2,1,0:T(8,128)(2,1)S(1)} %copy-done.8), channel_id=1, source_target_pairs={{0,8},{8,0},{16,24},{24,16},{1,9},{9,1},{17,25},{25,17},{2,10},{10... | collective-permute-start | bytes 294920 | tf_op jit(solution)/shard_map/ppermute | solution.py:249
  115.8 7.9 %collective-permute-start.4 = (bf16[8,16,384]{2,1,0:T(8,128)(2,1)S(1)}, bf16[8,16,384]{2,1,0:T(8,128)(2,1)S(1)}, u32[]{:S(2)}, u32[]{:S(2)}) collective-permute-start(bf16[8,16,384]{2,1,0:T(8,128)(2,1)S(1)} %copy-done.8), channel_id=1, source_target_pairs={{0,16},{8,24},{16,0},{24,8},{1,17},{9,25},{17,1},{25,9},{2,18},{10... | collective-permute-start | bytes 294920 | tf_op jit(solution)/shard_map/ppermute | solution.py:249
  117.5 7.8 %collective-permute-start.5 = (bf16[8,16,384]{2,1,0:T(8,128)(2,1)S(1)}, bf16[8,16,384]{2,1,0:T(8,128)(2,1)S(1)}, u32[]{:S(2)}, u32[]{:S(2)}) collective-permute-start(bf16[8,16,384]{2,1,0:T(8,128)(2,1)S(1)} %copy-done.8), channel_id=1, source_target_pairs={{0,24},{8,16},{16,8},{24,0},{1,25},{9,17},{17,9},{25,1},{2,26},{10... | collective-permute-start | bytes 294920 | tf_op jit(solution)/shard_map/ppermute | solution.py:249
  129.0 1.2 copy-start.1
  130.2 1.2 copy-start.2
  131.5 1.4 %copy-start.4 = (bf16[768,1024]{1,0:T(8,128)(2,1)S(1)}, bf16[768,1024]{1,0:T(8,128)(2,1)}, u32[]{:S(2)}) copy-start(bf16[768,1024]{1,0:T(8,128)(2,1)} %copy-done.3) | copy-start | bytes 4718596
  132.9 1.4 %copy-start.6 = (bf16[768,1024]{1,0:T(8,128)(2,1)S(1)}, bf16[768,1024]{1,0:T(8,128)(2,1)}, u32[]{:S(2)}) copy-start(bf16[768,1024]{1,0:T(8,128)(2,1)} %copy-done.5) | copy-start | bytes 4718596

commit v4 on v3

--- a/solution.py
+++ b/solution.py
@@ -35,8 +35,13 @@
     return alpha_mix * moving + (1.0 - alpha_mix) * current
 
 
+mix_per_step = alpha_mix * step_size * momentum_gain + (1.0 - alpha_mix) * step_size
+
+
 def stepped(current, moving, change):
     mixed = mixed_of(current, moving)
+    if change is None:
+        return mixed, beta_keep * moving + (1.0 - beta_keep) * mixed
     return (
         mixed - step_size * change,
         beta_keep * moving + (1.0 - beta_keep) * mixed - step_size * momentum_gain * change,
@@ -91,60 +96,67 @@
             rows_ref[g * cap : (g + 1) * cap, :] = point_rows(indices, slots, me, points, cap)
 
 
-def compact_kernel(u, where_ref, slots_ref, got_ref, out_ref):
+def prepare_kernel(w_ref, z_ref, t_ref, coef_ref, base_ref, goal_ref):
+    current, moving = w_ref[...], z_ref[...]
+    mixed = mixed_of(current, moving)
+    goal = t_ref[...].astype(f32)
+    base_ref[...] = mixed_of(*stepped(current, moving, None)).T
+    goal_ref[...] = goal.T
+    put_coefficients(coef_ref, mixed.T, goal.T)
+
+
+def put_coefficients(coef_ref, mixed, goal):
+    cols = mixed.shape[0]
+    high, low = split_two(ridge_term * mixed - goal)
+    coef_ref[0:cols] = mixed.astype(bf16)
+    coef_ref[cols : 2 * cols] = high
+    coef_ref[2 * cols : 3 * cols] = low
+
+
+def scaled_norm(rows, axis):
+    scale = 3.5 / rows.shape[axis] * math.log2(math.e)
+    return jnp.sum(jnp.square(rows.astype(f32)), axis=axis, keepdims=True) * scale
+
+
+def tile_of(left, left_norm, right_t, right_norm):
+    scale = 7.0 / left.shape[1] * math.log2(math.e)
+    return jnp.exp2(mm(left, right_t, 1, 0) * scale - left_norm - right_norm).astype(bf16)
+
+
+def tile_kernel(u, where_ref, slots_ref, got_ref, feats_ref, block_ref, tile_ref):
     owners, cap, width = got_ref.shape
     slots = slots_ref[u, where_ref[0]]
     place = jnp.where(iota((owners * cap, slots.shape[1]), 0) == slots, 1.0, 0.0).astype(bf16)
-    out_ref[...] = mm(got_ref[...].reshape(owners * cap, width), place, 0, 0).astype(bf16)
-
-
-def tile_of(left, left_norm, right_t, right_norm):
-    scale = 7.0 / left.shape[1] * math.log2(math.e)
-    return jnp.exp2(mm(left, right_t, 1, 0) * scale - left_norm - right_norm).astype(bf16)
-
-
-def scaled_norm(rows, axis):
-    width = rows.shape[axis]
-    return jnp.sum(jnp.square(rows.astype(f32)), axis=axis, keepdims=True) * (
-        3.5 / width * math.log2(math.e)
-    )
-
-
-def partial_kernel(u, where_ref, blocks_ref, feats_ref, b0, b1, b2, b3, w_ref, z_ref, t_ref, *rest):
-    *done, out_ref, part_ref, coef_ref = rest
+    block = mm(got_ref[...].reshape(owners * cap, width), place, 0, 0)
+    block_norm = scaled_norm(block, 0)
+    block = block.astype(bf16)
+    block_ref[...] = block
+    chunk = 256
+    for c in range(0, feats_ref.shape[0], chunk):
+        left = feats_ref[c : c + chunk, :]
+        tile_ref[c : c + chunk, :] = tile_of(left, scaled_norm(left, 1), block, block_norm)
+
+
+def product_kernel(u, where_ref, blocks_ref, tile_ref, *rest):
+    *given, out_ref, coef_ref = rest
     row, me = where_ref[0], where_ref[1]
-    points = feats_ref.shape[0]
-    groups, count = blocks_ref.shape[1], blocks_ref.shape[3]
-    current, moving = w_ref[...], z_ref[...]
-    if done:
-        current, moving = stepped(current, moving, dense_steps(done[0][...], done[1][...]))
-    mixed = mixed_of(current, moving)
-    high, low = split_two(ridge_term * mixed - t_ref[...])
-    cols = mixed.shape[0]
-    coef_ref[0:cols] = mixed.astype(bf16)
-    coef_ref[cols : 2 * cols] = high
-    coef_ref[2 * cols : 3 * cols] = low
-    chunk = 256
-    for k, b_ref in enumerate((b0, b1, b2, b3)):
-        group = lax.bitwise_xor(row, k)
-        right = b_ref[...]
-        right_norm = scaled_norm(right, 0)
-        local = blocks_ref[u, group] - me * points
-        total = jnp.zeros((cols, count), f32)
-        for c in range(0, points, chunk):
-            left = feats_ref[c : c + chunk, :]
-            tile = tile_of(left, scaled_norm(left, 1), right, right_norm)
-            place = jnp.where(iota((chunk, count), 0) + c == local, 1.0, 0.0).astype(bf16)
-            total += mm(coef_ref[0:cols, c : c + chunk], tile, 1, 0)
-            offset = mm(coef_ref[cols : 3 * cols, c : c + chunk], place, 1, 0)
-            total += offset[:cols] + offset[cols:]
-        half = groups // 2
-        start = pl.multiple_of(lax.rem(group, half) * count, count)
-        part_ref[lax.div(group, half), :, pl.ds(start, count)] = total
-    own = cols // out_ref.shape[0]
-    for o in range(out_ref.shape[0]):
-        both = jnp.concatenate([part_ref[h, o * own : (o + 1) * own, :] for h in range(2)], axis=0)
-        out_ref[o] = both.astype(bf16)
+    points, count = tile_ref.shape
+    if len(given) == 1:
+        coef_ref = given[0]
+    else:
+        base_ref, goal_ref, got_ref, rows_ref = given
+        change = dense_steps(got_ref[...], rows_ref[...])
+        put_coefficients(coef_ref, base_ref[...] - mix_per_step * change, goal_ref[...])
+    cols = coef_ref.shape[0] // 3
+    local = blocks_ref[u, row] - me * points
+    place = jnp.where(iota((points, count), 0) == local, 1.0, 0.0).astype(bf16)
+    total = mm(coef_ref[0:cols], tile_ref[...], 1, 0)
+    total += mm(coef_ref[cols : 2 * cols], place, 1, 0) + mm(coef_ref[2 * cols :], place, 1, 0)
+    pieces, double, lanes = out_ref.shape
+    own = double // 2
+    for d in range(pieces):
+        part = total[d * own : (d + 1) * own]
+        out_ref[d] = jnp.concatenate([part[:, :lanes], part[:, lanes:]], axis=0).astype(bf16)
 
 
 def dense_steps(got, rows):
@@ -159,10 +171,10 @@
     return total
 
 
-def factor_kernel(where_ref, pivots_ref, b0, b1, b2, b3, out_ref):
+def factor_kernel(u, where_ref, pivots_ref, b0, b1, b2, b3, out_ref):
     row = where_ref[0]
     count = b0.shape[1]
-    pivots = pivots_ref[...]
+    pivots = pivots_ref[u]
     feats = jnp.zeros((b0.shape[0], pivots.shape[1]), f32)
     blocks = (b0, b1, b2, b3)
     for k, b_ref in enumerate(blocks):
@@ -178,17 +190,19 @@
         out_ref[:, pl.ds(start, count)] = tile_of(left, left_norm, right, scaled_norm(right, 0))
 
 
-def chain_kernel(u, cap, got_ref, factor_ref, core_ref, slots_ref, out_ref):
-    owners = got_ref.shape[0]
+def chain_kernel(u, cap, owners, got_ref, factor_ref, core_ref, slots_ref, out_ref):
     groups, count = slots_ref.shape[1], slots_ref.shape[3]
-    summed = got_ref[0].astype(f32)
-    for o in range(1, owners):
-        summed += got_ref[o].astype(f32)
-    own = summed.shape[0] // 2
-    resid = jnp.concatenate([summed[:own], summed[own:]], axis=1)
+    own = got_ref.shape[1] // 2
+    sums = []
+    for g in range(groups):
+        summed = got_ref[g * owners].astype(f32)
+        for o in range(1, owners):
+            summed += got_ref[g * owners + o].astype(f32)
+        sums += [summed[:own], summed[own:]]
+    resid = jnp.concatenate(sums, axis=1)
     factor = factor_ref[...]
     proj = mm(resid.astype(bf16), factor, 1, 1)
-    lifted = mm(proj.astype(bf16), core_ref[...], 1, 1).astype(bf16)
+    lifted = mm(proj.astype(bf16), core_ref[u], 1, 1).astype(bf16)
     step = (resid - mm(lifted, factor, 1, 0)).astype(bf16)
     packed = []
     for g in range(groups):
@@ -206,18 +220,16 @@
             out_ref[copy * owners + o] = both
 
 
-def finish_kernel(
-    where_ref, w_ref, z_ref, s0, s1, s2, s3, last_ref, rows0_ref, rows1_ref, wo_ref, zo_ref, dense_ref
-):
-    row = where_ref[0]
-    cols = s0.shape[0] * s0.shape[1] // 2
-    for k, s_ref in enumerate((s0, s1, s2, s3)):
-        start = pl.multiple_of(lax.bitwise_xor(row, k) * cols, cols)
-        dense_ref[pl.ds(start, cols), :] = dense_steps(s_ref[...], rows0_ref[...])
-    current, moving = stepped(w_ref[...], z_ref[...], dense_ref[...].T)
-    current, moving = stepped(current, moving, dense_steps(last_ref[...], rows1_ref[...]).T)
-    wo_ref[...] = current
-    zo_ref[...] = moving
+def middle_kernel(w_ref, z_ref, got_ref, rows_ref, mixed_ref, kept_ref):
+    change = dense_steps(got_ref[...], rows_ref[...]).T
+    state = stepped(w_ref[...], z_ref[...], change)
+    mixed_ref[...], kept_ref[...] = stepped(*state, None)
+
+
+def finish_kernel(mixed_ref, kept_ref, got_ref, rows_ref, w_ref, z_ref):
+    change = dense_steps(got_ref[...], rows_ref[...]).T
+    w_ref[...] = mixed_ref[...] - step_size * change
+    z_ref[...] = kept_ref[...] - step_size * momentum_gain * change
 
 
 VMEM = pl.BlockSpec(memory_space=pltpu.VMEM)
@@ -249,7 +261,7 @@
     return lax.ppermute(value, "rows", [(i, i ^ k) for i in range(count)])
 
 
-def with_kernels(features, current, moving, goal, coefficients, momentum, block_index, pivot_index, core):
+def with_kernels(features, targets, coefficients, momentum, block_index, pivot_index, core):
     rows, owners = lax.axis_size("rows"), lax.axis_size("pts")
     points, width = features.shape
     block = block_index.shape[1]
@@ -257,11 +269,11 @@
     outputs = coefficients.shape[1]
     count = block // rows
     cap = 3 * count // owners
-    cols = outputs // rows
-    own = cols // owners
+    own = outputs // rows // owners
+    half = rows // 2
     where = jnp.stack([lax.axis_index("rows"), lax.axis_index("pts")]).astype(i32)
     blocks = block_index.reshape(UPDATES, rows, 1, count)
-    flops = 2.0 * points * block * (width + 3 * cols)
+    pivots = pivot_index.reshape(UPDATES, 1, rank)
 
     packed = call(
         functools.partial(pack_kernel, cap, owners),
@@ -277,66 +289,69 @@
         where,
         blocks,
     )
-    feats = []
+    coef, base, goal = call(
+        prepare_kernel,
+        [like((3 * outputs, points)), like((outputs, points), f32), like((outputs, points), f32)],
+        coefficients,
+        momentum,
+        targets,
+    )
+    tiles, feats = [], []
     for u in range(UPDATES):
-        (mine,) = call(
-            functools.partial(compact_kernel, u), [like((width, count))], where, slots, came[u]
-        )
+        mine, tile = call(
+            functools.partial(tile_kernel, u),
+            [like((width, count)), like((points, count))],
+            where,
+            slots,
+            came[u],
+            features,
+            flops=2.0 * points * count * width,
+        )
+        tiles.append(tile)
         feats.append([mine] + [swap_rows(mine, k) for k in range(1, rows)])
 
-    half = rows // 2
-    done = []
+    given = [coef]
     for u in range(UPDATES):
         (pieces,) = call(
-            functools.partial(partial_kernel, u),
-            [like((owners, 2 * own, half * count))],
+            functools.partial(product_kernel, u),
+            [like((rows * owners, 2 * own, count // 2))],
             where,
             blocks,
-            features,
-            *feats[u],
-            current,
-            moving,
-            goal,
-            *done,
-            scratch=[pltpu.VMEM((2, cols, half * count), f32), pltpu.VMEM((3 * cols, points), bf16)],
-            flops=flops,
-        )
-        summed = lax.all_to_all(pieces, "pts", 0, 0, tiled=True)
+            tiles[u],
+            *given,
+            scratch=[pltpu.VMEM(coef.shape, bf16)],
+            flops=2.0 * points * count * 3 * outputs,
+        )
+        summed = lax.all_to_all(pieces, ("rows", "pts"), 0, 0, tiled=True)
         (factor,) = call(
-            factor_kernel,
+            functools.partial(factor_kernel, u),
             [like((rank, block))],
             where,
-            pivot_index[u][None, :],
+            pivots,
             *feats[u],
             flops=2.0 * rank * block * (2 * width),
         )
-        last = u == UPDATES - 1
-        copies = owners * (rows if last else 1)
         (steps,) = call(
-            functools.partial(chain_kernel, u, cap),
-            [like((copies, 2 * own, half * cap))],
+            functools.partial(chain_kernel, u, cap, owners),
+            [like((rows * owners, 2 * own, half * cap))],
             summed,
             factor,
-            core[u],
+            core,
             slots,
         )
-        if last:
-            final = lax.all_to_all(steps, ("rows", "pts"), 0, 0, tiled=True)
-        else:
-            got = lax.all_to_all(steps, "pts", 0, 0, tiled=True)
-            done = [got, place[u]]
-            first = [got] + [swap_rows(got, k) for k in range(1, rows)]
-
+        got = lax.all_to_all(steps, ("rows", "pts"), 0, 0, tiled=True)
+        if u + 1 < UPDATES:
+            given = [base, goal, got, place[u]]
+            mixed, kept = call(
+                middle_kernel,
+                [like(coefficients.shape, f32)] * 2,
+                coefficients,
+                momentum,
+                got,
+                place[u],
+            )
     return call(
-        finish_kernel,
-        [like(coefficients.shape, f32)] * 2,
-        where,
-        coefficients,
-        momentum,
-        *first,
-        final,
-        *place,
-        scratch=[pltpu.VMEM((outputs, points), f32)],
+        finish_kernel, [like(coefficients.shape, f32)] * 2, mixed, kept, got, place[UPDATES - 1]
     )
 
 
@@ -348,7 +363,7 @@
     return jnp.exp(squared * (-3.5 / left_rows.shape[1])).astype(bf16)
 
 
-def with_operations(features, current, moving, goal, coefficients, momentum, block_index, pivot_index, core):
+def with_operations(features, targets, coefficients, momentum, block_index, pivot_index, core):
     row_count, pts_count = lax.axis_size("rows"), lax.axis_size("pts")
     row_id, pts_id = lax.axis_index("rows"), lax.axis_index("pts")
     points = features.shape[0]
@@ -358,6 +373,11 @@
     per_device = per_row // pts_count
     row_cols = outputs // row_count
     own_cols = row_cols // pts_count
+    first = row_id * row_cols
+    current, moving, goal = (
+        lax.dynamic_slice_in_dim(value, first, row_cols, axis=1).T.astype(f32)
+        for value in (coefficients, momentum, targets)
+    )
     ids = iota((points, 1), 0) + pts_id * points
     place = [(ids == block_index[u][None, :]).astype(bf16) for u in range(UPDATES)]
     own_rows = []
@@ -398,28 +418,13 @@
 
 def shards(features, targets, coefficients, momentum, block_index, pivot_index, nystrom_core):
     rows, owners = lax.axis_size("rows"), lax.axis_size("pts")
-    outputs = coefficients.shape[1]
-    cols = outputs // rows
     count = block_index.shape[1] // rows
-    first = lax.axis_index("rows") * cols
-
-    def own_columns(value):
-        return lax.dynamic_slice_in_dim(value, first, cols, axis=1).T.astype(f32)
-
-    fits = rows == 4 and cols == 8 * owners and count % 128 == 0 and (3 * count // owners) % 64 == 0
+    fits = rows == 4 and coefficients.shape[1] == 8 * rows * owners
+    fits = fits and count % 256 == 0 and (3 * count // owners) % 64 == 0 and UPDATES == 2
     plan = with_kernels if fits else with_operations
-    current, moving = plan(
-        features,
-        own_columns(coefficients),
-        own_columns(momentum),
-        own_columns(targets),
-        coefficients,
-        momentum,
-        block_index,
-        pivot_index,
-        nystrom_core,
-    )
-    return (current, moving)
+    return plan(
+        features, targets, coefficients, momentum, block_index, pivot_index, nystrom_core
+    )
 
 
 def solution(mesh):

time: 140 us -> 140 us (level)
  Pallas kernels: 34.4 us -> 27.2 us
  local copies, waits for them, and re-layouts: 27 us -> 33.9 us
  waiting for transfers between devices: 30 us -> 34.2 us
  starting transfers between devices: 30.1 us -> 27.9 us
    unnamed x79 -> x84, local copies, waits for them, and re-layouts: 19.7 us -> 32.3 us
    all_to_all x3, waiting for transfers between devices: 6.79 us -> 17.1 us  [the longest x2 17.1 us: with_kernels(): got = lax.all_to_all(steps, ('rows', 'pts'), 0, 0, tiled=True)]
    pallas_call x11 -> x13, Pallas kernels: 34.4 us -> 27.2 us  [call(): pl.pallas_call(body, out_shape=outs, in_specs=[SMEM if a.ndim == 1 else V...]
    ppermute x9 -> x6, waiting for transfers between devices: 19.6 us -> 14.8 us  [swap_rows(): return lax.ppermute(value, 'rows', [(i, i ^ k) for i in range(count)])]
    dynamic_slice x2 -> x0, local copies, waits for them, and re-layouts: 3.92 us -> none  [own_columns(): return lax.dynamic_slice_in_dim(value, first, cols, axis=1).T.astype(f32)]
    ppermute x9 -> x6, starting transfers between devices: 5.87 us -> 3.87 us  [swap_rows(): return lax.ppermute(value, 'rows', [(i, i ^ k) for i in range(count)])]
  transfers between devices with their start and end apart: 14 -> 11, of which waited for: 10 -> 7; matrix products, arithmetic and copies ran while one was open for 8% -> 0% of each run, Pallas kernels for 8% -> 9%
where the time goes in v4:
time: 140 us; the launch traced here: 138 us
  waiting for transfers between devices  34.2 us (24%)
  local copies, waits for them, and re-layouts  33.9 us (24%)
  starting transfers between devices  27.9 us (20%)
  Pallas kernels  27.2 us (19%)
  blocking collectives  14.2 us (10%)
    unnamed x84, local copies, waits for them, and re-layouts  32.3 us
    pallas_call x13, Pallas kernels, call(): pl.pallas_call(body, out_shape=outs, in_specs=[SMEM if a.ndim == 1 else V...  27.2 us
    all_to_all x2, waiting for transfers between devices, with_kernels(): got = lax.all_to_all(steps, ('rows', 'pts'), 0, 0, tiled=True)  17.1 us
    ppermute x6, waiting for transfers between devices, swap_rows(): return lax.ppermute(value, 'rows', [(i, i ^ k) for i in range(count)])  14.8 us
    all_to_all x1, blocking collectives, with_kernels(): summed = lax.all_to_all(pieces, ('rows', 'pts'), 0, 0, tiled=True)  14.2 us
    all_to_all x2, starting transfers between devices, with_kernels(): lax.all_to_all(packed[u], 'pts', 0, 0, tiled=True)  10.7 us
    all_to_all x2, starting transfers between devices, with_kernels(): got = lax.all_to_all(steps, ('rows', 'pts'), 0, 0, tiled=True)  9.77 us
    ppermute x6, starting transfers between devices, swap_rows(): return lax.ppermute(value, 'rows', [(i, i ^ k) for i in range(count)])  3.87 us
  transfers between devices with their start and end apart: 11, of which 7 were waited for; matrix products, arithmetic and copies ran while one was open for 0% of the time, Pallas kernels for 9%

profile of v4, /device:TPU:0, one launch (start us, length us, event | category | flops | bytes accessed | tf_op | source)
XLA Modules:
  0.0 138.3 jit_solution(9179407144426500511)
XLA Ops:
  0.6 0.8 reshape.10.blocks_ref
  1.6 0.9 copy-done.7
  2.5 2.1 %shard_map.87 = (bf16[8,192,128]{2,1,0:T(8,128)(2,1)}, bf16[8,192,128]{2,1,0:T(8,128)(2,1)S(1)}) custom-call(s32[2]{0:T(128)S(1)} %pad_add_fusion.where_ref, s32[2,4,1,512]{3,2,1,0:T(1,128)S(1)} %reshape.10.blocks_ref, bf16[1024,128]{1,0:T(8,128)(2,1)S(1)} %copy-done.7), custom_call_target="tpu_custom_call" | custom-call | bytes 1064968 | tf_op jit(solution)/shard_map/pallas_call | solution.py:242
  4.6 0.7 copy-done.26
  5.4 7.3 %all-to-all-start = ((bf16[8,192,128]{2,1,0:T(8,128)(2,1)}), bf16[8,192,128]{2,1,0:T(8,128)(2,1)S(1)}, u32[]{:S(2)}, u32[]{:S(2)}) async-start(bf16[8,192,128]{2,1,0:T(8,128)(2,1)} %get-tuple-element.17), calls=%async_computation | async-start | bytes 786432 | tf_op jit(solution)/shard_map/all_to_all | solution.py:285
  12.7 1.9 %shard_map.86 = (s32[2,4,1,512]{3,2,1,0:T(1,128)S(1)}, bf16[768,1024]{1,0:T(8,128)(2,1)S(1)}, bf16[768,1024]{1,0:T(8,128)(2,1)S(1)}) custom-call(s32[2]{0:T(128)S(1)} %pad_add_fusion.where_ref, s32[2,4,1,512]{3,2,1,0:T(1,128)S(1)} %reshape.10.blocks_ref), custom_call_target="tpu_custom_call" | custom-call | bytes 3178504 | tf_op jit(solution)/shard_map/pallas_call | solution.py:242
  14.6 1.2 copy-done.13
  15.7 1.2 copy-done.3
  17.0 1.0 copy-done.25
  18.0 0.9 shard_map.89
  18.9 1.0 copy-done.15
  19.9 1.0 copy-done.17
  20.9 1.2 copy-done.40
  22.1 2.3 %all-to-all-done.got_ref = bf16[8,192,128]{2,1,0:T(8,128)(2,1)S(1)} async-done(((bf16[8,192,128]{2,1,0:T(8,128)(2,1)}), bf16[8,192,128]{2,1,0:T(8,128)(2,1)S(1)}, u32[]{:S(2)}, u32[]{:S(2)}) %all-to-all-start) | async-done | bytes 393248 | tf_op jit(solution)/shard_map/all_to_all | solution.py:285
  24.4 1.6 %shard_map.88 = (bf16[128,512]{1,0:T(8,128)(2,1)S(1)}, bf16[1024,512]{1,0:T(8,128)(2,1)S(1)}) custom-call(s32[2]{0:T(128)S(1)} %pad_add_fusion.where_ref, s32[2,4,1,512]{3,2,1,0:T(1,128)S(1)} %get-tuple-element.16.slots_ref, bf16[8,192,128]{2,1,0:T(8,128)(2,1)S(1)} %all-to-all-done.got_ref, bf16[1024,128]{1,0:T(8,128)(2,1)S(1)} %copy-done.8), custom_call_target="tpu_custom_call" | custom-call | flops 134217728 | bytes 1851400 | tf_op jit(solution)/shard_map/pallas_call | solution.py:242
  26.0 0.6 copy-done.31
  26.6 1.4 %copy-done.41 = bf16[768,1024]{1,0:T(8,128)(2,1)S(1)} copy-done((bf16[768,1024]{1,0:T(8,128)(2,1)S(1)}, bf16[768,1024]{1,0:T(8,128)(2,1)}, u32[]{:S(2)}) %copy-start.41) | copy-done | bytes 1572888
  28.0 1.6 %shard_map.90 = bf16[32,16,256]{2,1,0:T(8,128)(2,1)S(1)} custom-call(s32[2]{0:T(128)S(1)} %pad_add_fusion.where_ref, s32[2,4,1,512]{3,2,1,0:T(1,128)S(1)} %reshape.10.blocks_ref, bf16[1024,512]{1,0:T(8,128)(2,1)S(1)} %get-tuple-element.18.tile_ref, bf16[768,1024]{1,0:T(8,128)(2,1)S(1)} %copy-done.41), custom_call_target="tpu_custom_call" | custom-call | flops 805306368 | bytes 2899976 | tf_op jit(solution)/shard_map/pallas_call | solution.py:242
  29.7 14.2 %all_to_all.30.got_ref = bf16[32,16,256]{2,1,0:T(8,128)(2,1)S(1)} all-to-all(bf16[32,16,256]{2,1,0:T(8,128)(2,1)S(1)} %shard_map.90), channel_id=1, replica_groups=mesh['rows'=4,'pts'=8] {'rows','pts'}, dimensions={0} | all-to-all | bytes 524288 | tf_op jit(solution)/shard_map/all_to_all | solution.py:325
  43.8 3.5 %all-to-all-start.3 = ((bf16[8,192,128]{2,1,0:T(8,128)(2,1)}), bf16[8,192,128]{2,1,0:T(8,128)(2,1)S(1)}, u32[]{:S(2)}, u32[]{:S(2)}) async-start(bf16[8,192,128]{2,1,0:T(8,128)(2,1)} %copy-done.26), calls=%async_computation.3 | async-start | bytes 786432 | tf_op jit(solution)/shard_map/all_to_all | solution.py:285
  47.4 0.9 collective-permute-start.1
  48.3 0.9 collective-permute-start.2
  49.2 0.7 reshape.11.pivots_ref
  49.9 4.0 %collective-permute-done.1.b2 = bf16[128,512]{1,0:T(8,128)(2,1)S(1)} collective-permute-done((bf16[128,512]{1,0:T(8,128)(2,1)}, bf16[128,512]{1,0:T(8,128)(2,1)S(1)}, u32[]{:S(2)}, u32[]{:S(2)}) %collective-permute-start.1) | collective-permute-done | bytes 131104 | tf_op jit(solution)/shard_map/ppermute | solution.py:261
  53.9 1.9 %collective-permute-done.2.b3 = bf16[128,512]{1,0:T(8,128)(2,1)S(1)} collective-permute-done((bf16[128,512]{1,0:T(8,128)(2,1)}, bf16[128,512]{1,0:T(8,128)(2,1)S(1)}, u32[]{:S(2)}, u32[]{:S(2)}) %collective-permute-start.2) | collective-permute-done | bytes 131104 | tf_op jit(solution)/shard_map/ppermute | solution.py:261
  55.9 0.9 copy-done.32
  56.8 0.7 copy-done.36
  57.4 2.2 %shard_map.91.factor_ref = bf16[512,2048]{1,0:T(8,128)(2,1)S(1)} custom-call(s32[2]{0:T(128)S(1)} %copy-done.36, s32[2,1,512]{2,1,0:T(1,128)S(1)} %reshape.11.pivots_ref, bf16[128,512]{1,0:T(8,128)(2,1)S(1)} %copy-done.32, bf16[128,512]{1,0:T(8,128)(2,1)S(1)} %collective-permute-done.b1, bf16[128,512]{1,0:T(8,128)(2,1)S(1)} %collective-permute-done.1.b2, ...), custom_call_target="tpu_custom_call" | custom-call | flops 536870912 | bytes 2625544 | tf_op jit(solution)/shard_map/pallas_call | solution.py:242
  59.7 2.9 %shard_map.92 = bf16[32,16,384]{2,1,0:T(8,128)(2,1)S(1)} custom-call(bf16[32,16,256]{2,1,0:T(8,128)(2,1)S(1)} %all_to_all.30.got_ref, bf16[512,2048]{1,0:T(8,128)(2,1)S(1)} %shard_map.91.factor_ref, bf16[2,512,512]{2,1,0:T(8,128)(2,1)S(1)} %copy-done.5, s32[2,4,1,512]{3,2,1,0:T(1,128)S(1)} %get-tuple-element.16.slots_ref), custom_call_target="tpu_custom_call" | custom-call | bytes 3817472 | tf_op jit(solution)/shard_map/pallas_call | solution.py:242
  62.6 0.8 copy-done.11
  63.3 0.7 copy-done.9
  64.1 5.1 %all-to-all-start.2 = ((bf16[32,16,384]{2,1,0:T(8,128)(2,1)}), bf16[32,16,384]{2,1,0:T(8,128)(2,1)S(1)}, u32[]{:S(2)}, u32[]{:S(2)}) async-start(bf16[32,16,384]{2,1,0:T(8,128)(2,1)} %copy-done.11), calls=%async_computation.2 | async-start | bytes 786432 | tf_op jit(solution)/shard_map/all_to_all | solution.py:342
  69.2 1.0 copy-done.10
  70.2 0.7 copy-done.37
  70.9 1.6 %shard_map.94 = (bf16[128,512]{1,0:T(8,128)(2,1)S(1)}, bf16[1024,512]{1,0:T(8,128)(2,1)S(1)}) custom-call(s32[2]{0:T(128)S(1)} %copy-done.37, s32[2,4,1,512]{3,2,1,0:T(1,128)S(1)} %get-tuple-element.16.slots_ref, bf16[8,192,128]{2,1,0:T(8,128)(2,1)S(1)} %copy-done.10, bf16[1024,128]{1,0:T(8,128)(2,1)S(1)} %copy-done.8), custom_call_target="tpu_custom_call" | custom-call | flops 134217728 | bytes 1851400 | tf_op jit(solution)/shard_map/pallas_call | solution.py:242
  72.5 1.0 copy-done.23
  73.4 9.3 %all-to-all-done.2.got_ref.rest_2_ = bf16[32,16,384]{2,1,0:T(8,128)(2,1)S(1)} async-done(((bf16[32,16,384]{2,1,0:T(8,128)(2,1)}), bf16[32,16,384]{2,1,0:T(8,128)(2,1)S(1)}, u32[]{:S(2)}, u32[]{:S(2)}) %all-to-all-start.2) | async-done | bytes 393248 | tf_op jit(solution)/shard_map/all_to_all | solution.py:342
  82.8 1.2 copy-done.16
  84.0 1.2 copy-done.18
  85.2 1.2 copy-done.24
  86.4 0.7 copy-done.28
  87.1 0.7 copy-done.38
  87.8 3.0 %shard_map.95 = bf16[32,16,256]{2,1,0:T(8,128)(2,1)} custom-call(s32[2]{0:T(128)S(1)} %copy-done.38, s32[2,4,1,512]{3,2,1,0:T(1,128)S(1)} %copy-done.28, bf16[1024,512]{1,0:T(8,128)(2,1)S(1)} %copy-done.24, f32[256,1024]{1,0:T(8,128)S(1)} %copy-done.16, f32[256,1024]{1,0:T(8,128)S(1)} %copy-done.18, bf16[32,16,384]{2,1,0:T(8,128)(2,1)S(1)} %all-to-all-done.2.got_ref.rest_2_, ...), custom_call_target="tpu_custom_call" | custom-call | flops 805306368 | bytes 5390344 | tf_op jit(solution)/shard_map/pallas_call | solution.py:242
  90.8 3.5 %all-to-all-start.4 = ((bf16[32,16,256]{2,1,0:T(8,128)(2,1)}), bf16[32,16,256]{2,1,0:T(8,128)(2,1)}, u32[]{:S(2)}, u32[]{:S(2)}) async-start(bf16[32,16,256]{2,1,0:T(8,128)(2,1)} %shard_map.95), calls=%async_computation.4 | async-start | bytes 524288 | tf_op jit(solution)/shard_map/all_to_all | solution.py:325
  94.4 1.5 %collective-permute-start.4 = (bf16[128,512]{1,0:T(8,128)(2,1)S(1)}, bf16[128,512]{1,0:T(8,128)(2,1)S(1)}, u32[]{:S(2)}, u32[]{:S(2)}) collective-permute-start(bf16[128,512]{1,0:T(8,128)(2,1)S(1)} %get-tuple-element.28.b0), channel_id=1, source_target_pairs={{0,16},{8,24},{16,0},{24,8},{1,17},{9,25},{17,1},{25,9},{2,18},{10... | collective-permute-start | bytes 393224 | tf_op jit(solution)/shard_map/ppermute | solution.py:261
  96.3 6.0 %collective-permute-done.4.b2 = bf16[128,512]{1,0:T(8,128)(2,1)S(1)} collective-permute-done((bf16[128,512]{1,0:T(8,128)(2,1)S(1)}, bf16[128,512]{1,0:T(8,128)(2,1)S(1)}, u32[]{:S(2)}, u32[]{:S(2)}) %collective-permute-start.4) | collective-permute-done | bytes 131104 | tf_op jit(solution)/shard_map/ppermute | solution.py:261
  102.2 2.9 %collective-permute-done.5.b3 = bf16[128,512]{1,0:T(8,128)(2,1)S(1)} collective-permute-done((bf16[128,512]{1,0:T(8,128)(2,1)S(1)}, bf16[128,512]{1,0:T(8,128)(2,1)S(1)}, u32[]{:S(2)}, u32[]{:S(2)}) %collective-permute-start.5) | collective-permute-done | bytes 131104 | tf_op jit(solution)/shard_map/ppermute | solution.py:261
  105.1 0.9 copy-done.30
  106.0 0.7 copy-done.34
  106.7 0.7 copy-done.39
  107.4 2.2 %shard_map.96.factor_ref = bf16[512,2048]{1,0:T(8,128)(2,1)S(1)} custom-call(s32[2]{0:T(128)S(1)} %copy-done.39, s32[2,1,512]{2,1,0:T(1,128)S(1)} %copy-done.34, bf16[128,512]{1,0:T(8,128)(2,1)S(1)} %copy-done.30, bf16[128,512]{1,0:T(8,128)(2,1)S(1)} %collective-permute-done.3.b1, bf16[128,512]{1,0:T(8,128)(2,1)S(1)} %collective-permute-done.4.b2, ...), custom_call_target="tpu_custom_call" | custom-call | flops 536870912 | bytes 2625544 | tf_op jit(solution)/shard_map/pallas_call | solution.py:242
  109.6 1.2 copy-done.6
  110.9 3.8 %shard_map.97 = bf16[32,16,384]{2,1,0:T(8,128)(2,1)S(1)} custom-call(bf16[32,16,256]{2,1,0:T(8,128)(2,1)} %all-to-all-done.4.got_ref, bf16[512,2048]{1,0:T(8,128)(2,1)S(1)} %shard_map.96.factor_ref, bf16[2,512,512]{2,1,0:T(8,128)(2,1)S(1)} %copy-done.6, s32[2,4,1,512]{3,2,1,0:T(1,128)S(1)} %get-tuple-element.16.slots_ref), custom_call_target="tpu_custom_call" | custom-call | bytes 3817472 | tf_op jit(solution)/shard_map/pallas_call | solution.py:242
  114.7 0.8 copy-done.12
  115.5 4.7 %all-to-all-start.5 = ((bf16[32,16,384]{2,1,0:T(8,128)(2,1)}), bf16[32,16,384]{2,1,0:T(8,128)(2,1)S(1)}, u32[]{:S(2)}, u32[]{:S(2)}) async-start(bf16[32,16,384]{2,1,0:T(8,128)(2,1)} %copy-done.12), calls=%async_computation.5 | async-start | bytes 786432 | tf_op jit(solution)/shard_map/all_to_all | solution.py:342
  120.1 1.4 %copy-done.1 = bf16[768,1024]{1,0:T(8,128)(2,1)S(1)} copy-done((bf16[768,1024]{1,0:T(8,128)(2,1)S(1)}, bf16[768,1024]{1,0:T(8,128)(2,1)}, u32[]{:S(2)}) %copy-start.1) | copy-done | bytes 1572888
  121.5 1.2 copy-done.4
  122.8 1.2 shard_map.93
  123.9 1.0 copy-done.19
  124.9 1.0 copy-done.21
  125.9 7.8 %all-to-all-done.5.got_ref = bf16[32,16,384]{2,1,0:T(8,128)(2,1)S(1)} async-done(((bf16[32,16,384]{2,1,0:T(8,128)(2,1)}), bf16[32,16,384]{2,1,0:T(8,128)(2,1)S(1)}, u32[]{:S(2)}, u32[]{:S(2)}) %all-to-all-start.5) | async-done | bytes 393248 | tf_op jit(solution)/shard_map/all_to_all | solution.py:342
  133.7 1.2 copy-done.20
  134.9 1.2 copy-done.22
  136.1 2.2 %shard_map.98 = (f32[1024,256]{1,0:T(8,128)}, f32[1024,256]{1,0:T(8,128)}) custom-call(f32[1024,256]{1,0:T(8,128)S(1)} %copy-done.20, f32[1024,256]{1,0:T(8,128)S(1)} %copy-done.22, bf16[32,16,384]{2,1,0:T(8,128)(2,1)S(1)} %all-to-all-done.5.got_ref, bf16[768,1024]{1,0:T(8,128)(2,1)S(1)} %copy-done.14), custom_call_target="tpu_custom_call" | custom-call | bytes 6160384 | tf_op jit(solution)/shard_map/pallas_call | solution.py:242
  (59 shorter events, 0.7 us)
Async XLA Ops:
  0.6 15.1 %copy-start.2 = (f32[1024,256]{1,0:T(8,128)S(1)}, f32[1024,256]{1,0:T(8,128)}, u32[]{:S(2)}) copy-start(f32[1024,256]{1,0:T(8,128)} %w_ref.3) | copy-start | bytes 3145732
  1.5 24.5 %copy-start.27 = (s32[2,4,1,512]{3,2,1,0:T(1,128)}, s32[2,4,1,512]{3,2,1,0:T(1,128)S(1)}, u32[]{:S(2)}) copy-start(s32[2,4,1,512]{3,2,1,0:T(1,128)S(1)} %reshape.10.blocks_ref) | copy-start | bytes 49156
  1.6 1.0 copy-start.7
  2.5 23.5 %copy-start.35 = (s32[2]{0:T(128)}, s32[2]{0:T(128)S(1)}, u32[]{:S(2)}) copy-start(s32[2]{0:T(128)S(1)} %pad_add_fusion.where_ref) | copy-start | bytes 28
  4.6 0.8 copy-start.26
  5.4 19.0 %all-to-all-start = ((bf16[8,192,128]{2,1,0:T(8,128)(2,1)}), bf16[8,192,128]{2,1,0:T(8,128)(2,1)S(1)}, u32[]{:S(2)}, u32[]{:S(2)}) async-start(bf16[8,192,128]{2,1,0:T(8,128)(2,1)} %get-tuple-element.17), calls=%async_computation | async-start | bytes 786432 | tf_op jit(solution)/shard_map/all_to_all | solution.py:285
  14.5 1.2 copy-start.13
  15.7 1.2 copy-start.3
  17.0 1.0 copy-start.25
  18.0 64.7 %copy-start = (bf16[768,1024]{1,0:T(8,128)(2,1)}, bf16[768,1024]{1,0:T(8,128)(2,1)S(1)}, u32[]{:S(2)}) copy-start(bf16[768,1024]{1,0:T(8,128)(2,1)S(1)} %get-tuple-element.21.rows_ref.rest_3_) | copy-start | bytes 4718596
  18.0 6.4 %copy-start.8 = (bf16[1024,128]{1,0:T(8,128)(2,1)S(1)}, bf16[1024,128]{1,0:T(8,128)(2,1)}, u32[]{:S(2)}) copy-start(bf16[1024,128]{1,0:T(8,128)(2,1)} %feats_ref.5) | copy-start | bytes 786436
  18.9 1.0 copy-start.15
  19.9 1.0 copy-start.17
  20.9 1.2 copy-start.40
  26.0 0.7 copy-start.31
  26.6 1.4 %copy-start.41 = (bf16[768,1024]{1,0:T(8,128)(2,1)S(1)}, bf16[768,1024]{1,0:T(8,128)(2,1)}, u32[]{:S(2)}) copy-start(bf16[768,1024]{1,0:T(8,128)(2,1)} %copy-done.40) | copy-start | bytes 4718596
  43.8 19.5 %all-to-all-start.3 = ((bf16[8,192,128]{2,1,0:T(8,128)(2,1)}), bf16[8,192,128]{2,1,0:T(8,128)(2,1)S(1)}, u32[]{:S(2)}, u32[]{:S(2)}) async-start(bf16[8,192,128]{2,1,0:T(8,128)(2,1)} %copy-done.26), calls=%async_computation.3 | async-start | bytes 786432 | tf_op jit(solution)/shard_map/all_to_all | solution.py:285
  47.3 12.4 %copy-start.5 = (bf16[2,512,512]{2,1,0:T(8,128)(2,1)S(1)}, bf16[2,512,512]{2,1,0:T(8,128)(2,1)}, u32[]{:S(2)}) copy-start(bf16[2,512,512]{2,1,0:T(8,128)(2,1)} %core_ref.3) | copy-start | bytes 3145732
  47.3 2.6 %collective-permute-start = (bf16[128,512]{1,0:T(8,128)(2,1)}, bf16[128,512]{1,0:T(8,128)(2,1)S(1)}, u32[]{:S(2)}, u32[]{:S(2)}) collective-permute-start(bf16[128,512]{1,0:T(8,128)(2,1)} %copy-done.31), channel_id=1, source_target_pairs={{0,8},{8,0},{16,24},{24,16},{1,9},{9,1},{17,25},{25,17},{2,10},{10... | collective-permute-start | bytes 393224 | tf_op jit(solution)/shard_map/ppermute | solution.py:261
  47.4 6.6 %collective-permute-start.1 = (bf16[128,512]{1,0:T(8,128)(2,1)}, bf16[128,512]{1,0:T(8,128)(2,1)S(1)}, u32[]{:S(2)}, u32[]{:S(2)}) collective-permute-start(bf16[128,512]{1,0:T(8,128)(2,1)} %copy-done.31), channel_id=1, source_target_pairs={{0,16},{8,24},{16,0},{24,8},{1,17},{9,25},{17,1},{25,9},{2,18},{10... | collective-permute-start | bytes 393224 | tf_op jit(solution)/shard_map/ppermute | solution.py:261
  48.3 7.5 %collective-permute-start.2 = (bf16[128,512]{1,0:T(8,128)(2,1)}, bf16[128,512]{1,0:T(8,128)(2,1)S(1)}, u32[]{:S(2)}, u32[]{:S(2)}) collective-permute-start(bf16[128,512]{1,0:T(8,128)(2,1)} %copy-done.31), channel_id=1, source_target_pairs={{0,24},{8,16},{16,8},{24,0},{1,25},{9,17},{17,9},{25,1},{2,26},{10... | collective-permute-start | bytes 393224 | tf_op jit(solution)/shard_map/ppermute | solution.py:261
  49.9 9.7 %copy-start.33 = (s32[2,1,512]{2,1,0:T(1,128)}, s32[2,1,512]{2,1,0:T(1,128)S(1)}, u32[]{:S(2)}) copy-start(s32[2,1,512]{2,1,0:T(1,128)S(1)} %reshape.11.pivots_ref) | copy-start | bytes 12292
  55.9 0.9 copy-start.32
  56.8 0.7 copy-start.36
  62.6 0.8 copy-start.11
  63.3 0.7 copy-start.9
  64.1 18.7 %all-to-all-start.2 = ((bf16[32,16,384]{2,1,0:T(8,128)(2,1)}), bf16[32,16,384]{2,1,0:T(8,128)(2,1)S(1)}, u32[]{:S(2)}, u32[]{:S(2)}) async-start(bf16[32,16,384]{2,1,0:T(8,128)(2,1)} %copy-done.11), calls=%async_computation.2 | async-start | bytes 786432 | tf_op jit(solution)/shard_map/all_to_all | solution.py:342
  69.2 1.0 copy-start.10
  70.2 0.7 copy-start.37
  72.5 1.0 copy-start.23
  73.4 22.5 %copy-start.29 = (bf16[128,512]{1,0:T(8,128)(2,1)}, bf16[128,512]{1,0:T(8,128)(2,1)S(1)}, u32[]{:S(2)}) copy-start(bf16[128,512]{1,0:T(8,128)(2,1)S(1)} %get-tuple-element.28.b0) | copy-start | bytes 393220
  82.7 1.2 copy-start.16
  84.0 1.2 copy-start.18
  85.2 1.2 copy-start.24
  86.4 0.7 copy-start.28
  87.1 0.7 copy-start.38
  90.8 18.8 %all-to-all-start.4 = ((bf16[32,16,256]{2,1,0:T(8,128)(2,1)}), bf16[32,16,256]{2,1,0:T(8,128)(2,1)}, u32[]{:S(2)}, u32[]{:S(2)}) async-start(bf16[32,16,256]{2,1,0:T(8,128)(2,1)} %shard_map.95), calls=%async_computation.4 | async-start | bytes 524288 | tf_op jit(solution)/shard_map/all_to_all | solution.py:325
  94.3 1.9 %collective-permute-start.3 = (bf16[128,512]{1,0:T(8,128)(2,1)S(1)}, bf16[128,512]{1,0:T(8,128)(2,1)S(1)}, u32[]{:S(2)}, u32[]{:S(2)}) collective-permute-start(bf16[128,512]{1,0:T(8,128)(2,1)S(1)} %get-tuple-element.28.b0), channel_id=1, source_target_pairs={{0,8},{8,0},{16,24},{24,16},{1,9},{9,1},{17,25},{25,17},{2,10},{10... | collective-permute-start | bytes 393224 | tf_op jit(solution)/shard_map/ppermute | solution.py:261
  94.4 7.8 %collective-permute-start.4 = (bf16[128,512]{1,0:T(8,128)(2,1)S(1)}, bf16[128,512]{1,0:T(8,128)(2,1)S(1)}, u32[]{:S(2)}, u32[]{:S(2)}) collective-permute-start(bf16[128,512]{1,0:T(8,128)(2,1)S(1)} %get-tuple-element.28.b0), channel_id=1, source_target_pairs={{0,16},{8,24},{16,0},{24,8},{1,17},{9,25},{17,1},{25,9},{2,18},{10... | collective-permute-start | bytes 393224 | tf_op jit(solution)/shard_map/ppermute | solution.py:261
  95.9 9.2 %collective-permute-start.5 = (bf16[128,512]{1,0:T(8,128)(2,1)S(1)}, bf16[128,512]{1,0:T(8,128)(2,1)S(1)}, u32[]{:S(2)}, u32[]{:S(2)}) collective-permute-start(bf16[128,512]{1,0:T(8,128)(2,1)S(1)} %get-tuple-element.28.b0), channel_id=1, source_target_pairs={{0,24},{8,16},{16,8},{24,0},{1,25},{9,17},{17,9},{25,1},{2,26},{10... | collective-permute-start | bytes 393224 | tf_op jit(solution)/shard_map/ppermute | solution.py:261
  105.1 0.9 copy-start.30
  106.0 0.7 copy-start.34
  106.7 0.7 copy-start.39
  109.6 1.2 copy-start.6
  114.7 0.8 copy-start.12
  115.5 18.2 %all-to-all-start.5 = ((bf16[32,16,384]{2,1,0:T(8,128)(2,1)}), bf16[32,16,384]{2,1,0:T(8,128)(2,1)S(1)}, u32[]{:S(2)}, u32[]{:S(2)}) async-start(bf16[32,16,384]{2,1,0:T(8,128)(2,1)} %copy-done.12), calls=%async_computation.5 | async-start | bytes 786432 | tf_op jit(solution)/shard_map/all_to_all | solution.py:342
  120.1 1.4 %copy-start.1 = (bf16[768,1024]{1,0:T(8,128)(2,1)S(1)}, bf16[768,1024]{1,0:T(8,128)(2,1)}, u32[]{:S(2)}) copy-start(bf16[768,1024]{1,0:T(8,128)(2,1)} %copy-done) | copy-start | bytes 4718596
  121.5 1.2 copy-start.4
  122.8 10.9 %copy-start.14 = (bf16[768,1024]{1,0:T(8,128)(2,1)S(1)}, bf16[768,1024]{1,0:T(8,128)(2,1)}, u32[]{:S(2)}) copy-start(bf16[768,1024]{1,0:T(8,128)(2,1)} %copy-done.13) | copy-start | bytes 4718596
  123.9 1.0 copy-start.19
  124.9 1.0 copy-start.21
  133.7 1.2 copy-start.20
  134.9 1.2 copy-start.22

commit v5 on v1

v5 whole, which is shorter than its diff:
```python
import functools
import math

import jax
import jax.numpy as jnp
from jax import lax
from jax.experimental import pallas as pl
from jax.experimental.pallas import tpu as pltpu
from jax.sharding import PartitionSpec as P

UPDATES = 2


alpha_mix = 0.6
beta_keep = 0.9
step_size = 0.2
momentum_gain = 1.5
ridge_term = 1.0

f32 = jnp.float32
bf16 = jnp.bfloat16
i32 = jnp.int32


def mm(a, b, ca, cb):
    return lax.dot_general(a, b, (((ca,), (cb,)), ((), ())), preferred_element_type=f32)


def split_two(value):
    high = value.astype(bf16)
    return high, (value - high.astype(f32)).astype(bf16)


def mixed_of(current, moving):
    return alpha_mix * moving + (1.0 - alpha_mix) * current


mix_per_step = alpha_mix * step_size * momentum_gain + (1.0 - alpha_mix) * step_size


def stepped(current, moving, change):
    mixed = mixed_of(current, moving)
    if change is None:
        return mixed, beta_keep * moving + (1.0 - beta_keep) * mixed
    return (
        mixed - step_size * change,
        beta_keep * moving + (1.0 - beta_keep) * mixed - step_size * momentum_gain * change,
    )


def iota(shape, axis):
    return lax.broadcasted_iota(i32, shape, axis)


def one_hot(chosen):
    return jnp.where(chosen, 1.0, 0.0).astype(bf16)


def before_matrix(n):
    return one_hot(iota((n, n), 0) < iota((n, n), 1))


def slots_of(indices, before, points, owners, cap):
    owner = lax.div(indices, jnp.full_like(indices, points))
    marks = iota((owners, indices.shape[1]), 0) == owner
    counts = jnp.where(marks, 1.0, 0.0)
    earlier = mm(counts.astype(bf16), before, 1, 0)
    rank = jnp.sum(counts * earlier, axis=0, keepdims=True)
    return owner * cap + rank.astype(i32)


def point_rows(indices, slots, me, points, cap):
    held = iota((cap, indices.shape[1]), 0) + me * cap == slots
    local = (indices - me * points + 1).astype(f32)
    point = jnp.sum(jnp.where(held, local, 0.0), axis=1, keepdims=True).astype(i32) - 1
    return one_hot(iota((cap, points), 1) == point)


def start_all(pairs, sems):
    copies = [pltpu.make_async_copy(a, b, sems.at[n]) for n, (a, b) in enumerate(pairs)]
    for copy in copies:
        copy.start()
    return copies


def wait_all(copies):
    for copy in copies:
        copy.wait()


def group_row(blocks, u, group, count):
    return blocks[u : u + 1, pl.ds(pl.multiple_of(group * count, count), count)]


def pack_kernel(count, cap, blocks_hbm, feats_hbm, out_hbm, blocks, feats, packed, sems):
    row, me = lax.axis_index("rows"), lax.axis_index("pts")
    points, owners = feats.shape[0], out_hbm.shape[0]
    reads = start_all([(blocks_hbm, blocks), (feats_hbm, feats)], sems)
    before = before_matrix(count)
    reads[0].wait()
    rows = []
    for u in range(UPDATES):
        indices = group_row(blocks, u, row, count)
        slots = slots_of(indices, before, points, owners, cap)
        rows.append(point_rows(indices, slots, me, points, cap))
    reads[1].wait()
    for u in range(UPDATES):
        packed[u * cap : (u + 1) * cap, :] = mm(rows[u], feats[...], 1, 0).astype(bf16)
    wait_all(start_all([(packed, out_hbm.at[o]) for o in range(owners)], sems))


def coefficients_of(mixed, goal):
    high, low = split_two(ridge_term * mixed - goal)
    return mixed.astype(bf16), high, low


def prepare_kernel(
    count, cap, owners,
    blocks_hbm, w_hbm, z_hbm, t_hbm, coef_hbm, rows_hbm, slots_hbm,
    blocks, w, z, t, coef, rows, slots, sems,
):
    me = lax.axis_index("pts")
    points, outputs = w.shape
    reads = start_all([(blocks_hbm, blocks), (w_hbm, w), (z_hbm, z), (t_hbm, t)], sems)
    before = before_matrix(count)
    reads[0].wait()
    groups = blocks.shape[1] // count
    for u in range(UPDATES):
        for g in range(groups):
            indices = blocks[u : u + 1, g * count : (g + 1) * count]
            held = slots_of(indices, before, points, owners, cap)
            n = u * groups + g
            slots[n : n + 1, :] = held
            rows[u, g * cap : (g + 1) * cap, :] = point_rows(indices, held, me, points, cap)
    wait_all(reads[1:])
    current, moving = w[...], z[...]
    goal = t[...].astype(f32).T
    for u in range(UPDATES):
        mixed = mixed_of(current, moving).T
        for n, part in enumerate(coefficients_of(mixed, goal)):
            coef[u, n * outputs : (n + 1) * outputs, :] = part
        current, moving = stepped(current, moving, None)
    wait_all(start_all([(coef, coef_hbm), (rows, rows_hbm), (slots, slots_hbm)], sems))


def scaled_norm(rows, axis):
    scale = 3.5 / rows.shape[axis] * math.log2(math.e)
    return jnp.sum(jnp.square(rows.astype(f32)), axis=axis, keepdims=True) * scale


def tile_of(left, left_norm, right_t, right_norm):
    scale = 7.0 / left.shape[1] * math.log2(math.e)
    return jnp.exp2(mm(left, right_t, 1, 0) * scale - left_norm - right_norm)


CHUNK = 256


def sums_kernel(
    cap,
    came, blocks_hbm, feats_hbm, coef_hbm, block_hbm, pieces_hbm,
    blocks, feats, coef, block, tile, place, pieces, sems,
):
    row, me = lax.axis_index("rows"), lax.axis_index("pts")
    owners, _, width = came.shape
    points, count = tile.shape
    outputs = coef.shape[1] // 3
    reads = start_all([(blocks_hbm, blocks), (feats_hbm, feats), (coef_hbm, coef)], sems)
    before = before_matrix(count)
    reads[0].wait()
    for u in range(UPDATES):
        indices = group_row(blocks, u, row, count)
        slots = slots_of(indices, before, points, owners, cap)
        chosen = one_hot(iota((owners * cap, count), 0) == slots)
        packed = came[:, u * cap : (u + 1) * cap, :].reshape(owners * cap, width)
        block[u] = mm(packed, chosen, 0, 0).astype(bf16)
    reads[1].wait()
    writes = [pltpu.make_async_copy(block, block_hbm, sems.at[0])]
    writes[0].start()
    for u in range(UPDATES):
        right = block[u]
        right_norm = scaled_norm(right, 0)
        local = group_row(blocks, u, row, count) - me * points
        for c in range(0, points, CHUNK):
            left = feats[c : c + CHUNK, :]
            tile[c : c + CHUNK, :] = tile_of(left, scaled_norm(left, 1), right, right_norm).astype(bf16)
            place[c : c + CHUNK, :] = one_hot(iota((CHUNK, count), 0) + c == local)
        if u == 0:
            reads[2].wait()
        total = mm(coef[u, 0:outputs], tile[...], 1, 0)
        total += mm(coef[u, outputs : 2 * outputs], place[...], 1, 0)
        total += mm(coef[u, 2 * outputs :], place[...], 1, 0)
        devices, _, lanes = pieces.shape
        own = outputs // devices
        for d in range(devices):
            part = total[d * own : (d + 1) * own]
            pieces[d, 2 * own * u : 2 * own * (u + 1), :] = jnp.concatenate(
                [part[:, :lanes], part[:, lanes:]], axis=0
            ).astype(bf16)
    writes.append(pltpu.make_async_copy(pieces, pieces_hbm, sems.at[1]))
    writes[1].start()
    wait_all(writes)


def factors_kernel(
    b0_hbm, b1_hbm, b2_hbm, b3_hbm, blocks_hbm, pivots_hbm, factor_hbm, cross_hbm,
    feats, blocks, pivots, factor, cross, sems,
):
    row = lax.axis_index("rows")
    groups, _, width, count = feats.shape
    pairs = [(b_hbm, feats.at[k]) for k, b_hbm in enumerate((b0_hbm, b1_hbm, b2_hbm, b3_hbm))]
    wait_all(start_all(pairs + [(blocks_hbm, blocks), (pivots_hbm, pivots)], sems))
    places = [lax.bitwise_xor(row, k) for k in range(groups)]
    for u in range(UPDATES):
        chosen_feats = jnp.zeros((width, pivots.shape[1]), f32)
        for k in range(groups):
            chosen = iota((count, pivots.shape[1]), 0) + places[k] * count == pivots[u : u + 1, :]
            chosen_feats += mm(feats[k, u], one_hot(chosen), 1, 0)
        left = chosen_feats.T
        left_norm = scaled_norm(left, 1)
        left = left.astype(bf16)
        for k in range(groups):
            right = feats[k, u]
            start = pl.multiple_of(places[k] * count, count)
            factor[u, :, pl.ds(start, count)] = tile_of(
                left, left_norm, right, scaled_norm(right, 0)
            ).astype(bf16)
    writes = start_all([(factor, factor_hbm)], sems)
    sent = 1
    for k in range(groups):
        left = feats[k, 0].astype(f32).T
        left_norm = scaled_norm(left, 1)
        left = left.astype(bf16)
        left_points = group_row(blocks, 0, places[k], count).astype(f32)
        left_points = jnp.broadcast_to(left_points, (8, count)).T[:, 0:1]
        for m in range(groups):
            right = feats[m, 1]
            right_norm = scaled_norm(right, 0)
            right_points = group_row(blocks, 1, places[m], count).astype(f32)
            for c in range(0, count, CHUNK):
                rows = slice(c, c + CHUNK)
                value = tile_of(left[rows], left_norm[rows], right, right_norm)
                same = jnp.where(left_points[rows] == right_points, ridge_term, 0.0)
                cross[m, k, rows, :] = (value.astype(bf16).astype(f32) + same).astype(bf16)
            start = pl.multiple_of(places[k] * count, count)
            copy = pltpu.make_async_copy(
                cross.at[m, k], cross_hbm.at[places[m], pl.ds(start, count), :], sems.at[sent]
            )
            copy.start()
            writes.append(copy)
            sent += 1
    wait_all(writes)


def chain_kernel(
    cap, owners,
    summed, factor_hbm, core_hbm, cross_hbm, slots_hbm, out_hbm,
    factor, core, cross, slots, packed, sems,
):
    groups, _, count = cross.shape
    own = summed.shape[1] // (2 * UPDATES)
    pairs = []
    for u in range(UPDATES):
        pairs += [(factor_hbm.at[u], factor.at[u]), (core_hbm.at[u], core.at[u])]
        if u == 0:
            pairs += [(slots_hbm, slots)]
            pairs += [(cross_hbm.at[g], cross.at[g]) for g in range(groups)]
    reads = start_all(pairs, sems)
    step = None
    for u in range(UPDATES):
        sums = []
        for g in range(groups):
            part = summed[g * owners, 2 * own * u : 2 * own * (u + 1), :].astype(f32)
            for o in range(1, owners):
                part += summed[g * owners + o, 2 * own * u : 2 * own * (u + 1), :].astype(f32)
            part = jnp.concatenate([part[:own], part[own:]], axis=1)
            if u:
                reads[3 + g].wait()
                part -= mix_per_step * mm(step, cross[g], 1, 0)
            sums.append(part)
        resid = jnp.concatenate(sums, axis=1)
        wait_all(reads[0:3] if u == 0 else reads[3 + groups :])
        proj = mm(resid.astype(bf16), factor[u], 1, 1)
        lifted = mm(proj.astype(bf16), core[u], 1, 1).astype(bf16)
        step = (resid - mm(lifted, factor[u], 1, 0)).astype(bf16)
        parts = []
        for g in range(groups):
            n = u * groups + g
            place = one_hot(iota((owners * cap, count), 0) == slots[n : n + 1, :])
            parts.append(mm(step[:, g * count : (g + 1) * count], place, 1, 1))
        half = groups // 2
        for o in range(owners):
            lanes = [x[:, o * cap : (o + 1) * cap] for x in parts]
            packed[o, 2 * own * u : 2 * own * (u + 1), :] = jnp.concatenate(
                [jnp.concatenate(lanes[h * half : (h + 1) * half], axis=1) for h in range(2)], axis=0
            ).astype(bf16)
    copies = out_hbm.shape[0] // owners
    wait_all(
        start_all([(packed, out_hbm.at[pl.ds(n * owners, owners)]) for n in range(copies)], sems)
    )


def finish_kernel(
    got, w_hbm, z_hbm, rows_hbm, w_out, z_out, w, z, rows, steps, w_new, z_new, sems, out_sems
):
    points = w.shape[0]
    sources, deep, lanes = got.shape
    own = deep // (2 * UPDATES)
    chunks = range(0, points, CHUNK)
    pairs = []
    for c in chunks:
        part = slice(c, c + CHUNK)
        pairs += [(rows_hbm.at[:, :, part], rows.at[:, :, part])]
        pairs += [(w_hbm.at[part], w.at[part]), (z_hbm.at[part], z.at[part])]
    reads = start_all(pairs, sems)
    wide = got[...].astype(f32)
    for u in range(UPDATES):
        for h in range(2):
            first = own * (2 * u + h)
            part = wide[:, first : first + own, :].reshape(sources * own, lanes)
            steps[u, :, h * lanes : (h + 1) * lanes] = part.astype(bf16)
    writes = []
    for n, c in enumerate(chunks):
        part = slice(c, c + CHUNK)
        wait_all(reads[3 * n : 3 * n + 3])
        current, moving = w[part, :], z[part, :]
        for u in range(UPDATES):
            change = mm(steps[u], rows[u, :, part], 1, 0).T
            current, moving = stepped(current, moving, change)
        w_new[part, :] = current
        z_new[part, :] = moving
        for m, (a, b) in enumerate(((w_new, w_out), (z_new, z_out))):
            copy = pltpu.make_async_copy(a.at[part], b.at[part], out_sems.at[2 * n + m])
            copy.start()
            writes.append(copy)
    wait_all(writes)


VMEM = pl.BlockSpec(memory_space=pltpu.VMEM)
HBM = pl.BlockSpec(memory_space=pltpu.HBM)


def like(shape, dtype=bf16):
    return jax.ShapeDtypeStruct(shape, dtype)


def call(body, outs, inside, *args, near=0, sems=(), flops=0):
    moved = sum(math.prod(o.shape) * o.dtype.itemsize for o in [*outs, *args])
    return pl.pallas_call(
        body,
        out_shape=outs,
        in_specs=[VMEM] * near + [HBM] * (len(args) - near),
        out_specs=[HBM] * len(outs),
        scratch_shapes=[pltpu.VMEM(x.shape, x.dtype) for x in inside]
        + [pltpu.SemaphoreType.DMA((n,)) for n in sems],
        compiler_params=pltpu.CompilerParams(vmem_limit_bytes=48 * 2**20),
        cost_estimate=pl.CostEstimate(flops=int(flops), bytes_accessed=moved, transcendentals=0),
    )(*args)


def swap_rows(value, k):
    count = lax.axis_size("rows")
    return lax.ppermute(value, "rows", [(i, i ^ k) for i in range(count)])


def with_kernels(features, targets, coefficients, momentum, block_index, pivot_index, core):
    rows, owners = lax.axis_size("rows"), lax.axis_size("pts")
    points, width = features.shape
    block = block_index.shape[1]
    rank = pivot_index.shape[1]
    outputs = coefficients.shape[1]
    count = block // rows
    cap = 3 * count // owners
    devices = rows * owners
    own = outputs // devices
    deep = 2 * own * UPDATES
    half = rows // 2
    wide = like(coefficients.shape, f32)

    (packed,) = call(
        functools.partial(pack_kernel, count, cap),
        [like((owners, UPDATES * cap, width))],
        [block_index, features, like((UPDATES * cap, width))],
        block_index,
        features,
        sems=(owners,),
    )
    came = lax.all_to_all(packed, "pts", 0, 0, tiled=True)
    kept = [
        like((UPDATES, 3 * outputs, points)),
        like((UPDATES, rows * cap, points)),
        like((UPDATES * rows, count), i32),
    ]
    coef, place, slots = call(
        functools.partial(prepare_kernel, count, cap, owners),
        kept,
        [block_index, coefficients, momentum, targets, *kept],
        block_index,
        coefficients,
        momentum,
        targets,
        sems=(4,),
    )
    feats = like((UPDATES, width, count))
    pieces = like((devices, deep, count // 2))
    tile = like((points, count))
    mine, pieces = call(
        functools.partial(sums_kernel, cap),
        [feats, pieces],
        [block_index, features, coef, feats, tile, tile, pieces],
        came,
        block_index,
        features,
        coef,
        near=1,
        sems=(3,),
        flops=2.0 * UPDATES * points * count * (width + 3 * outputs),
    )
    summed = lax.all_to_all(pieces, ("rows", "pts"), 0, 0, tiled=True)
    beside, across = swap_rows(mine, 1), swap_rows(mine, 2)
    kept = [like((UPDATES, rank, block)), like((rows, block, count))]
    factor, cross = call(
        factors_kernel,
        kept,
        [
            like((rows, *feats.shape)),
            block_index,
            pivot_index,
            kept[0],
            like((rows, rows, count, count)),
        ],
        mine,
        beside,
        across,
        swap_rows(across, 1),
        block_index,
        pivot_index,
        sems=(rows * rows + 1,),
        flops=2.0 * width * block * (UPDATES * rank + block),
    )
    (steps,) = call(
        functools.partial(chain_kernel, cap, owners),
        [like((devices, deep, half * cap))],
        [factor, core, cross, slots, like((owners, deep, half * cap))],
        summed,
        factor,
        core,
        cross,
        slots,
        near=1,
        sems=(2 * UPDATES + 1 + rows,),
    )
    got = lax.all_to_all(steps, ("rows", "pts"), 0, 0, tiled=True)
    parts = points // CHUNK
    return call(
        finish_kernel,
        [wide] * 2,
        [wide, wide, place, like((UPDATES, outputs, rows * cap)), wide, wide],
        got,
        coefficients,
        momentum,
        place,
        near=1,
        sems=(3 * parts, 2 * parts),
    )


def kernel_tile(left_rows, right_rows):
    inner_prod = mm(left_rows, right_rows, 1, 1)
    left_sq = jnp.sum(jnp.square(left_rows.astype(f32)), axis=1)
    right_sq = jnp.sum(jnp.square(right_rows.astype(f32)), axis=1)
    squared = left_sq[:, None] + right_sq[None, :] - 2.0 * inner_prod
    return jnp.exp(squared * (-3.5 / left_rows.shape[1])).astype(bf16)


def with_operations(features, targets, coefficients, momentum, block_index, pivot_index, core):
    row_count, pts_count = lax.axis_size("rows"), lax.axis_size("pts")
    row_id, pts_id = lax.axis_index("rows"), lax.axis_index("pts")
    points = features.shape[0]
    block = block_index.shape[1]
    outputs = coefficients.shape[1]
    per_row = block // row_count
    per_device = per_row // pts_count
    row_cols = outputs // row_count
    own_cols = row_cols // pts_count
    first = row_id * row_cols
    current, moving, goal = (
        lax.dynamic_slice_in_dim(value, first, row_cols, axis=1).T.astype(f32)
        for value in (coefficients, momentum, targets)
    )
    ids = iota((points, 1), 0) + pts_id * points
    place = [(ids == block_index[u][None, :]).astype(bf16) for u in range(UPDATES)]
    own_rows = []
    for u in range(UPDATES):
        mine = lax.dynamic_slice_in_dim(place[u], row_id * per_row, per_row, axis=1)
        own_rows.append(mm(mine, features, 0, 0).astype(bf16).reshape(pts_count, per_device, -1))
    came = lax.all_to_all(jnp.concatenate(own_rows, axis=1), "pts", 0, 0, tiled=False)
    chunk = jnp.sum(came.astype(f32), axis=0).astype(bf16)
    spread = lax.all_gather(lax.all_gather(chunk, "pts", axis=0), "rows", axis=0)
    spread = spread.reshape(row_count, pts_count, UPDATES, per_device, features.shape[1])
    all_steps = []
    for u in range(UPDATES):
        block_feats = spread[:, :, u].reshape(block, features.shape[1])
        mixed = mixed_of(current, moving)
        high, low = split_two(ridge_term * mixed - goal)
        tile = kernel_tile(features, block_feats)
        partial_value = (
            mm(mixed.astype(bf16), tile, 1, 0) + mm(high, place[u], 1, 0) + mm(low, place[u], 1, 0)
        )
        pieces = partial_value.astype(bf16).reshape(pts_count, own_cols, block)
        summed = lax.all_to_all(pieces, "pts", 0, 0, tiled=False)
        resid = jnp.sum(summed.astype(f32), axis=0)
        at_pivot = (iota((block, 1), 0) == pivot_index[u][None, :]).astype(bf16)
        factor = kernel_tile(block_feats, mm(at_pivot, block_feats, 0, 0).astype(bf16))
        proj = mm(resid.astype(bf16), factor, 1, 0)
        lifted = mm(proj.astype(bf16), core[u], 1, 1).astype(bf16)
        step_bf = (resid - mm(lifted, factor, 1, 1)).astype(bf16)
        steps = lax.all_gather(step_bf, "pts", axis=0, tiled=True)
        change = mm(steps, place[u], 1, 1)
        all_steps.append(change.astype(bf16))
        current, moving = stepped(current, moving, change)
    gathered = lax.all_gather(jnp.stack(all_steps), "rows", axis=1, tiled=True)
    current, moving = coefficients, momentum
    for u in range(UPDATES):
        current, moving = stepped(current, moving, gathered[u].T.astype(f32))
    return (current, moving)


def shards(features, targets, coefficients, momentum, block_index, pivot_index, nystrom_core):
    rows, owners = lax.axis_size("rows"), lax.axis_size("pts")
    count = block_index.shape[1] // rows
    fits = rows == 4 and coefficients.shape[1] == 8 * rows * owners
    fits = fits and coefficients.shape[0] % CHUNK == 0 and count % CHUNK == 0 and (3 * count // owners) % 64 == 0
    plan = with_kernels if fits else with_operations
    return plan(
        features, targets, coefficients, momentum, block_index, pivot_index, nystrom_core
    )


def solution(mesh):
    in_specs = (P("pts", None), P("pts", None), P("pts", None), P("pts", None), P(), P(), P())
    out_specs = (P("pts", None), P("pts", None))
    return jax.shard_map(shards, mesh=mesh, in_specs=in_specs, out_specs=out_specs, check_vma=False)
```

time: 222 us -> 114 us (0.51)
  blocking collectives: 111 us -> 27.3 us
  Pallas kernels: 0 us -> 38.2 us
  matrix products: 28.8 us -> 0 us
  waiting for transfers between devices: 39.3 us -> 22.8 us
  between operations: 14.3 us -> 0.93 us
  other arithmetic: 8.36 us -> 0 us
  starting transfers between devices: 9.06 us -> 12.7 us
    all_gather x3 -> x0, blocking collectives: 95 us -> none  [the longest x2 62.2 us: shards(): steps = lax.all_gather(step_bf, 'pts', axis=0, tiled=True)]
    pallas_call x0 -> x6, Pallas kernels: none -> 38.2 us  [call(): pl.pallas_call(body, out_shape=outs, in_specs=[VMEM] * near + [HBM] * (le...]
    dot_general x18 -> x0, matrix products: 28.8 us -> none  [mm(): lax.dot_general(a, b, (((ca,), (cb,)), ((), ())), preferred_element_type=...]
    all_gather x2 -> x0, waiting for transfers between devices: 25.8 us -> none  [the longest x1 14.3 us: shards(): gathered = lax.all_gather(jnp.stack(all_steps), 'rows', axis=1, tiled=True)]
    ppermute x0 -> x3, waiting for transfers between devices: none -> 12.9 us  [swap_rows(): return lax.ppermute(value, 'rows', [(i, i ^ k) for i in range(count)])]
    all_to_all x1, blocking collectives: 16 us -> 27.3 us  [with_kernels(): got = lax.all_to_all(steps, ('rows', 'pts'), 0, 0, tiled=True)]
    unnamed x43 -> x32, local copies, waits for them, and re-layouts: 7.27 us -> 11.4 us
    all_to_all x2, waiting for transfers between devices: 13.5 us -> 9.84 us  [the longest x1 9.84 us: with_kernels(): came = lax.all_to_all(packed, 'pts', 0, 0, tiled=True)]
  transfers between devices with their start and end apart: 4 -> 5, of which waited for: 4 -> 3; matrix products, arithmetic and copies ran while one was open for 4% -> 0% of each run, Pallas kernels for 0% -> 15%
where the time goes in v5:
time: 114 us; the launch traced here: 113 us
  Pallas kernels  38.2 us (34%)
  blocking collectives  27.3 us (24%)
  waiting for transfers between devices  22.8 us (20%)
  starting transfers between devices  12.7 us (11%)
  local copies, waits for them, and re-layouts  11.4 us (10%)
    pallas_call x6, Pallas kernels, call(): pl.pallas_call(body, out_shape=outs, in_specs=[VMEM] * near + [HBM] * (le...  38.2 us
    all_to_all x1, blocking collectives, with_kernels(): got = lax.all_to_all(steps, ('rows', 'pts'), 0, 0, tiled=True)  27.3 us
    ppermute x3, waiting for transfers between devices, swap_rows(): return lax.ppermute(value, 'rows', [(i, i ^ k) for i in range(count)])  12.9 us
    unnamed x32, local copies, waits for them, and re-layouts  11.4 us
    all_to_all x1, waiting for transfers between devices, with_kernels(): came = lax.all_to_all(packed, 'pts', 0, 0, tiled=True)  9.84 us
    all_to_all x1, starting transfers between devices, with_kernels(): came = lax.all_to_all(packed, 'pts', 0, 0, tiled=True)  7.29 us
    all_to_all x1, starting transfers between devices, with_kernels(): summed = lax.all_to_all(pieces, ('rows', 'pts'), 0, 0, tiled=True)  3.76 us
  transfers between devices with their start and end apart: 5, of which 3 were waited for; matrix products, arithmetic and copies ran while one was open for 0% of the time, Pallas kernels for 15%

profile of v5, /device:TPU:0, one launch (start us, length us, event | category | flops | bytes accessed | tf_op | source)
XLA Modules:
  0.0 113.3 jit_solution(6850265993495194580)
XLA Ops:
  0.6 0.0 copy-start.8
  0.6 0.9 copy-done.8
  1.6 0.0 copy-start.10
  1.6 0.7 copy-done.10
  2.3 0.0 copy-start.9
  2.3 0.0 copy-start.12
  2.3 1.9 %shard_map.86 = bf16[8,384,128]{2,1,0:T(8,128)(2,1)} custom-call(s32[2,2048]{1,0:T(2,128)S(1)} %copy-done.10, bf16[1024,128]{1,0:T(8,128)(2,1)S(1)} %copy-done.8), custom_call_target="tpu_custom_call" | custom-call | bytes 1064960 | tf_op jit(solution)/shard_map/pallas_call | solution.py:349
  4.2 7.3 %all-to-all-start = ((bf16[8,384,128]{2,1,0:T(8,128)(2,1)}), bf16[8,384,128]{2,1,0:T(8,128)(2,1)S(1)}, u32[]{:S(2)}, u32[]{:S(2)}) async-start(bf16[8,384,128]{2,1,0:T(8,128)(2,1)} %shard_map.86), calls=%async_computation | async-start | bytes 1572864 | tf_op jit(solution)/shard_map/all_to_all | solution.py:388
  11.5 0.0 copy-start.1
  11.5 1.2 %copy-done.1 = f32[1024,256]{1,0:T(8,128)S(1)} copy-done((f32[1024,256]{1,0:T(8,128)S(1)}, f32[1024,256]{1,0:T(8,128)}, u32[]{:S(2)}) %copy-start.1) | copy-done | bytes 1048600
  12.7 0.0 copy-start.3
  12.7 1.2 %copy-done.3 = f32[1024,256]{1,0:T(8,128)S(1)} copy-done((f32[1024,256]{1,0:T(8,128)S(1)}, f32[1024,256]{1,0:T(8,128)}, u32[]{:S(2)}) %copy-start.3) | copy-done | bytes 1048600
  13.9 0.0 copy-start.7
  14.0 1.0 copy-done.7
  15.0 0.0 copy-start.11
  15.0 0.7 copy-done.11
  15.7 0.0 copy-start.15
  15.7 4.5 %shard_map.87 = (bf16[2,768,1024]{2,1,0:T(8,128)(2,1)S(1)}, bf16[2,768,1024]{2,1,0:T(8,128)(2,1)}, s32[8,512]{1,0:T(8,128)S(1)}) custom-call(s32[2,2048]{1,0:T(2,128)S(1)} %copy-done.11, f32[1024,256]{1,0:T(8,128)S(1)} %copy-done.1, f32[1024,256]{1,0:T(8,128)S(1)} %copy-done.3, bf16[1024,256]{1,0:T(8,128)(2,1)S(1)} %copy-done.7), custom_call_target="tpu_custom_call" | custom-call | bytes 8945664 | tf_op jit(solution)/shard_map/pallas_call | solution.py:349
  20.2 0.0 copy-start.13
  20.2 1.6 %copy-done.13 = bf16[2,768,1024]{2,1,0:T(8,128)(2,1)} copy-done((bf16[2,768,1024]{2,1,0:T(8,128)(2,1)}, bf16[2,768,1024]{2,1,0:T(8,128)(2,1)S(1)}, u32[]{:S(2)}) %copy-start.13) | copy-done | bytes 3145752
  21.8 9.8 %all-to-all-done.came = bf16[8,384,128]{2,1,0:T(8,128)(2,1)S(1)} async-done(((bf16[8,384,128]{2,1,0:T(8,128)(2,1)}), bf16[8,384,128]{2,1,0:T(8,128)(2,1)S(1)}, u32[]{:S(2)}, u32[]{:S(2)}) %all-to-all-start) | async-done | bytes 786464 | tf_op jit(solution)/shard_map/all_to_all | solution.py:388
  31.7 0.0 copy-done.9
  31.7 0.0 copy-done.12
  31.7 0.0 copy-start.14
  31.7 1.9 %copy-done.14 = bf16[2,768,1024]{2,1,0:T(8,128)(2,1)S(1)} copy-done((bf16[2,768,1024]{2,1,0:T(8,128)(2,1)S(1)}, bf16[2,768,1024]{2,1,0:T(8,128)(2,1)}, u32[]{:S(2)}) %copy-start.14) | copy-done | bytes 3145752
  33.6 5.1 %shard_map.88 = (bf16[2,128,512]{2,1,0:T(8,128)(2,1)S(1)}, bf16[32,32,256]{2,1,0:T(8,128)(2,1)}) custom-call(bf16[8,384,128]{2,1,0:T(8,128)(2,1)S(1)} %all-to-all-done.came, s32[2,2048]{1,0:T(2,128)S(1)} %copy-done.12, bf16[1024,128]{1,0:T(8,128)(2,1)S(1)} %copy-done.9, bf16[2,768,1024]{2,1,0:T(8,128)(2,1)S(1)} %copy-done.14), custom_call_target="tpu_custom_call" | custom-call | flops 1879048192 | bytes 4997120 | tf_op jit(solution)/shard_map/pallas_call | solution.py:349
  38.7 0.0 copy-start.6
  38.7 3.8 %all-to-all-start.1 = ((bf16[32,32,256]{2,1,0:T(8,128)(2,1)}), bf16[32,32,256]{2,1,0:T(8,128)(2,1)S(1)}, u32[]{:S(2)}, u32[]{:S(2)}) async-start(bf16[32,32,256]{2,1,0:T(8,128)(2,1)} %get-tuple-element.10), calls=%async_computation.1 | async-start | bytes 1048576 | tf_op jit(solution)/shard_map/all_to_all | solution.py:419
  42.4 1.7 %collective-permute-start.1 = (bf16[2,128,512]{2,1,0:T(8,128)(2,1)S(1)}, bf16[2,128,512]{2,1,0:T(8,128)(2,1)S(1)}, u32[]{:S(2)}, u32[]{:S(2)}) collective-permute-start(bf16[2,128,512]{2,1,0:T(8,128)(2,1)S(1)} %get-tuple-element.11.b0_hbm), channel_id=1, source_target_pairs={{0,16},{8,24},{16,0},{24,8},{1,17},{9,25},{17,1},{25,9},{2,18},{10... | collective-permute-start | bytes 786440 | tf_op jit(solution)/shard_map/ppermute | solution.py:363
  44.1 0.0 collective-permute-start
  44.1 11.4 %collective-permute-done.1.b2_hbm = bf16[2,128,512]{2,1,0:T(8,128)(2,1)S(1)} collective-permute-done((bf16[2,128,512]{2,1,0:T(8,128)(2,1)S(1)}, bf16[2,128,512]{2,1,0:T(8,128)(2,1)S(1)}, u32[]{:S(2)}, u32[]{:S(2)}) %collective-permute-start.1) | collective-permute-done | bytes 262176 | tf_op jit(solution)/shard_map/ppermute | solution.py:363
  55.5 0.0 collective-permute-start.2
  55.5 0.0 collective-permute-done.b1_hbm
  55.5 1.5 %collective-permute-done.2.b3_hbm = bf16[2,128,512]{2,1,0:T(8,128)(2,1)S(1)} collective-permute-done((bf16[2,128,512]{2,1,0:T(8,128)(2,1)S(1)}, bf16[2,128,512]{2,1,0:T(8,128)(2,1)S(1)}, u32[]{:S(2)}, u32[]{:S(2)}) %collective-permute-start.2) | collective-permute-done | bytes 262176 | tf_op jit(solution)/shard_map/ppermute | solution.py:363
  57.0 0.0 copy-done.15
  57.0 12.8 %shard_map.89 = (bf16[2,512,2048]{2,1,0:T(8,128)(2,1)S(1)}, bf16[4,2048,512]{2,1,0:T(8,128)(2,1)}) custom-call(bf16[2,128,512]{2,1,0:T(8,128)(2,1)S(1)} %get-tuple-element.11.b0_hbm, bf16[2,128,512]{2,1,0:T(8,128)(2,1)S(1)} %collective-permute-done.b1_hbm, bf16[2,128,512]{2,1,0:T(8,128)(2,1)S(1)} %collective-permute-done.1.b2_hbm, ...), custom_call_target="tpu_custom_call" | custom-call | flops 1610612736 | bytes 13651968 | tf_op jit(solution)/shard_map/pallas_call | solution.py:349
  69.8 0.0 copy-start
  69.8 2.0 %copy-done = bf16[2,512,2048]{2,1,0:T(8,128)(2,1)} copy-done((bf16[2,512,2048]{2,1,0:T(8,128)(2,1)}, bf16[2,512,2048]{2,1,0:T(8,128)(2,1)S(1)}, u32[]{:S(2)}) %copy-start) | copy-done | bytes 4194328
  71.8 0.0 all-to-all-done.1.summed
  71.8 0.0 copy-done.6
  71.8 0.0 copy-start.2
  71.8 0.0 copy-start.4
  71.8 0.0 copy-start.5
  71.8 10.2 %shard_map.90 = bf16[32,32,384]{2,1,0:T(8,128)(2,1)S(1)} custom-call(bf16[32,32,256]{2,1,0:T(8,128)(2,1)S(1)} %all-to-all-done.1.summed, bf16[2,512,2048]{2,1,0:T(8,128)(2,1)} %copy-done, bf16[2,512,512]{2,1,0:T(8,128)(2,1)S(1)} %copy-done.6, bf16[4,2048,512]{2,1,0:T(8,128)(2,1)} %get-tuple-element.13.cross_hbm, s32[8,512]{1,0:T(8,128)S(1)} %get-tuple-element.14.slots_hbm), custom_call_target="tpu_custom_call" | custom-call | bytes 14958592 | tf_op jit(solution)/shard_map/pallas_call | solution.py:349
  82.0 27.3 %all_to_all.15.got = bf16[32,32,384]{2,1,0:T(8,128)(2,1)S(1)} all-to-all(bf16[32,32,384]{2,1,0:T(8,128)(2,1)S(1)} %shard_map.90), channel_id=1, replica_groups=mesh['rows'=4,'pts'=8] {'rows','pts'}, dimensions={0} | all-to-all | bytes 1572864 | tf_op jit(solution)/shard_map/all_to_all | solution.py:453
  109.3 0.0 copy-done.2
  109.3 0.0 copy-done.4
  109.3 0.0 copy-done.5
  109.3 3.8 %shard_map.91 = (f32[1024,256]{1,0:T(8,128)}, f32[1024,256]{1,0:T(8,128)}) custom-call(bf16[32,32,384]{2,1,0:T(8,128)(2,1)S(1)} %all_to_all.15.got, f32[1024,256]{1,0:T(8,128)S(1)} %copy-done.2, f32[1024,256]{1,0:T(8,128)S(1)} %copy-done.4, bf16[2,768,1024]{2,1,0:T(8,128)(2,1)S(1)} %copy-done.5), custom_call_target="tpu_custom_call" | custom-call | bytes 8126464 | tf_op jit(solution)/shard_map/pallas_call | solution.py:349
Async XLA Ops:
  0.6 1.0 copy-start.8
  1.6 0.7 copy-start.10
  2.3 29.4 %copy-start.9 = (bf16[1024,128]{1,0:T(8,128)(2,1)S(1)}, bf16[1024,128]{1,0:T(8,128)(2,1)}, u32[]{:S(2)}) copy-start(bf16[1024,128]{1,0:T(8,128)(2,1)} %feats_hbm.3) | copy-start | bytes 786436
  2.3 29.4 %copy-start.12 = (s32[2,2048]{1,0:T(2,128)S(1)}, s32[2,2048]{1,0:T(2,128)}, u32[]{:S(2)}) copy-start(s32[2,2048]{1,0:T(2,128)} %blocks_hbm.7) | copy-start | bytes 49156
  4.2 27.5 %all-to-all-start = ((bf16[8,384,128]{2,1,0:T(8,128)(2,1)}), bf16[8,384,128]{2,1,0:T(8,128)(2,1)S(1)}, u32[]{:S(2)}, u32[]{:S(2)}) async-start(bf16[8,384,128]{2,1,0:T(8,128)(2,1)} %shard_map.86), calls=%async_computation | async-start | bytes 1572864 | tf_op jit(solution)/shard_map/all_to_all | solution.py:388
  11.5 1.2 %copy-start.1 = (f32[1024,256]{1,0:T(8,128)S(1)}, f32[1024,256]{1,0:T(8,128)}, u32[]{:S(2)}) copy-start(f32[1024,256]{1,0:T(8,128)} %w_hbm.3) | copy-start | bytes 3145732
  12.7 1.2 %copy-start.3 = (f32[1024,256]{1,0:T(8,128)S(1)}, f32[1024,256]{1,0:T(8,128)}, u32[]{:S(2)}) copy-start(f32[1024,256]{1,0:T(8,128)} %z_hbm.3) | copy-start | bytes 3145732
  13.9 1.0 copy-start.7
  15.0 0.7 copy-start.11
  15.7 41.3 %copy-start.15 = (s32[2,512]{1,0:T(2,128)S(1)}, s32[2,512]{1,0:T(2,128)}, u32[]{:S(2)}) copy-start(s32[2,512]{1,0:T(2,128)} %pivots_hbm.1) | copy-start | bytes 12292
  20.2 1.6 %copy-start.13 = (bf16[2,768,1024]{2,1,0:T(8,128)(2,1)}, bf16[2,768,1024]{2,1,0:T(8,128)(2,1)S(1)}, u32[]{:S(2)}) copy-start(bf16[2,768,1024]{2,1,0:T(8,128)(2,1)S(1)} %get-tuple-element.9.coef_hbm) | copy-start | bytes 9437188
  31.7 1.9 %copy-start.14 = (bf16[2,768,1024]{2,1,0:T(8,128)(2,1)S(1)}, bf16[2,768,1024]{2,1,0:T(8,128)(2,1)}, u32[]{:S(2)}) copy-start(bf16[2,768,1024]{2,1,0:T(8,128)(2,1)} %copy-done.13) | copy-start | bytes 9437188
  38.7 33.2 %copy-start.6 = (bf16[2,512,512]{2,1,0:T(8,128)(2,1)S(1)}, bf16[2,512,512]{2,1,0:T(8,128)(2,1)}, u32[]{:S(2)}) copy-start(bf16[2,512,512]{2,1,0:T(8,128)(2,1)} %core_hbm.1) | copy-start | bytes 3145732
  38.7 33.1 %all-to-all-start.1 = ((bf16[32,32,256]{2,1,0:T(8,128)(2,1)}), bf16[32,32,256]{2,1,0:T(8,128)(2,1)S(1)}, u32[]{:S(2)}, u32[]{:S(2)}) async-start(bf16[32,32,256]{2,1,0:T(8,128)(2,1)} %get-tuple-element.10), calls=%async_computation.1 | async-start | bytes 1048576 | tf_op jit(solution)/shard_map/all_to_all | solution.py:419
  42.4 13.1 %collective-permute-start.1 = (bf16[2,128,512]{2,1,0:T(8,128)(2,1)S(1)}, bf16[2,128,512]{2,1,0:T(8,128)(2,1)S(1)}, u32[]{:S(2)}, u32[]{:S(2)}) collective-permute-start(bf16[2,128,512]{2,1,0:T(8,128)(2,1)S(1)} %get-tuple-element.11.b0_hbm), channel_id=1, source_target_pairs={{0,16},{8,24},{16,0},{24,8},{1,17},{9,25},{17,1},{25,9},{2,18},{10... | collective-permute-start | bytes 786440 | tf_op jit(solution)/shard_map/ppermute | solution.py:363
  44.1 11.4 %collective-permute-start = (bf16[2,128,512]{2,1,0:T(8,128)(2,1)S(1)}, bf16[2,128,512]{2,1,0:T(8,128)(2,1)S(1)}, u32[]{:S(2)}, u32[]{:S(2)}) collective-permute-start(bf16[2,128,512]{2,1,0:T(8,128)(2,1)S(1)} %get-tuple-element.11.b0_hbm), channel_id=1, source_target_pairs={{0,8},{8,0},{16,24},{24,16},{1,9},{9,1},{17,25},{25,17},{2,10},{10... | collective-permute-start | bytes 786440 | tf_op jit(solution)/shard_map/ppermute | solution.py:363
  55.5 1.5 %collective-permute-start.2 = (bf16[2,128,512]{2,1,0:T(8,128)(2,1)S(1)}, bf16[2,128,512]{2,1,0:T(8,128)(2,1)S(1)}, u32[]{:S(2)}, u32[]{:S(2)}) collective-permute-start(bf16[2,128,512]{2,1,0:T(8,128)(2,1)S(1)} %collective-permute-done.1.b2_hbm), channel_id=1, source_target_pairs={{0,8},{8,0},{16,24},{24,16},{1,9},{9,1},{17,25},{25,17},{2,10},{10... | collective-permute-start | bytes 786440 | tf_op jit(solution)/shard_map/ppermute | solution.py:363
  69.8 2.0 %copy-start = (bf16[2,512,2048]{2,1,0:T(8,128)(2,1)}, bf16[2,512,2048]{2,1,0:T(8,128)(2,1)S(1)}, u32[]{:S(2)}) copy-start(bf16[2,512,2048]{2,1,0:T(8,128)(2,1)S(1)} %get-tuple-element.12.factor_hbm) | copy-start | bytes 12582916
  71.8 37.5 %copy-start.2 = (f32[1024,256]{1,0:T(8,128)S(1)}, f32[1024,256]{1,0:T(8,128)}, u32[]{:S(2)}) copy-start(f32[1024,256]{1,0:T(8,128)} %w_hbm.3) | copy-start | bytes 3145732
  71.8 37.5 %copy-start.4 = (f32[1024,256]{1,0:T(8,128)S(1)}, f32[1024,256]{1,0:T(8,128)}, u32[]{:S(2)}) copy-start(f32[1024,256]{1,0:T(8,128)} %z_hbm.3) | copy-start | bytes 3145732
  71.8 37.5 %copy-start.5 = (bf16[2,768,1024]{2,1,0:T(8,128)(2,1)S(1)}, bf16[2,768,1024]{2,1,0:T(8,128)(2,1)}, u32[]{:S(2)}) copy-start(bf16[2,768,1024]{2,1,0:T(8,128)(2,1)} %get-tuple-element.15.rows_hbm) | copy-start | bytes 9437188

commit v6 on v5

--- a/solution.py
+++ b/solution.py
@@ -143,50 +143,60 @@
     wait_all(start_all([(coef, coef_hbm), (rows, rows_hbm), (slots, slots_hbm)], sems))
 
 
-def scaled_norm(rows, axis):
-    scale = 3.5 / rows.shape[axis] * math.log2(math.e)
-    return jnp.sum(jnp.square(rows.astype(f32)), axis=axis, keepdims=True) * scale
-
-
-def tile_of(left, left_norm, right_t, right_norm):
-    scale = 7.0 / left.shape[1] * math.log2(math.e)
-    return jnp.exp2(mm(left, right_t, 1, 0) * scale - left_norm - right_norm)
+def extended(rows, axis, first):
+    rest = -0.5 * jnp.sum(jnp.square(rows.astype(f32)), axis=axis, keepdims=True)
+    parts = []
+    for _ in range(3):
+        parts.append(rest.astype(bf16).astype(f32))
+        rest = rest - parts[-1]
+    parts = parts + [1.0] * 3 if first else [1.0] * 3 + parts
+    at = iota(rows.shape, axis)
+    extra = jnp.zeros(rows.shape, f32)
+    for n, part in enumerate(parts):
+        extra = jnp.where(at == n, part, extra)
+    return jnp.concatenate([rows.astype(bf16), extra.astype(bf16)], axis=axis)
+
+
+def exponent(left, right):
+    return mm(left, right, 1, 0) * (7.0 / (left.shape[1] // 2) * math.log2(math.e))
 
 
 CHUNK = 256
 
 
-def sums_kernel(
-    cap,
-    came, blocks_hbm, feats_hbm, coef_hbm, block_hbm, pieces_hbm,
-    blocks, feats, coef, block, tile, place, pieces, sems,
-):
-    row, me = lax.axis_index("rows"), lax.axis_index("pts")
+def compact_kernel(cap, points, came, blocks_hbm, block_hbm, blocks, block, sems):
+    row = lax.axis_index("rows")
     owners, _, width = came.shape
-    points, count = tile.shape
-    outputs = coef.shape[1] // 3
-    reads = start_all([(blocks_hbm, blocks), (feats_hbm, feats), (coef_hbm, coef)], sems)
+    count = block.shape[2]
+    wait_all(start_all([(blocks_hbm, blocks)], sems))
     before = before_matrix(count)
-    reads[0].wait()
-    for u in range(UPDATES):
-        indices = group_row(blocks, u, row, count)
-        slots = slots_of(indices, before, points, owners, cap)
+    for u in range(UPDATES):
+        slots = slots_of(group_row(blocks, u, row, count), before, points, owners, cap)
         chosen = one_hot(iota((owners * cap, count), 0) == slots)
         packed = came[:, u * cap : (u + 1) * cap, :].reshape(owners * cap, width)
         block[u] = mm(packed, chosen, 0, 0).astype(bf16)
-    reads[1].wait()
-    writes = [pltpu.make_async_copy(block, block_hbm, sems.at[0])]
-    writes[0].start()
-    for u in range(UPDATES):
-        right = block[u]
-        right_norm = scaled_norm(right, 0)
+    wait_all(start_all([(block, block_hbm)], sems))
+
+
+def sums_kernel(
+    blocks_hbm, block_hbm, feats_hbm, coef_hbm, pieces_hbm,
+    blocks, block, feats, coef, tile, place, pieces, sems,
+):
+    row, me = lax.axis_index("rows"), lax.axis_index("pts")
+    points, count = tile.shape
+    outputs = coef.shape[1] // 3
+    pairs = [(blocks_hbm, blocks), (block_hbm, block), (feats_hbm, feats), (coef_hbm, coef)]
+    reads = start_all(pairs, sems)
+    wait_all(reads[:3])
+    left = extended(feats[...], 1, True)
+    for u in range(UPDATES):
+        right = extended(block[u], 0, False)
         local = group_row(blocks, u, row, count) - me * points
         for c in range(0, points, CHUNK):
-            left = feats[c : c + CHUNK, :]
-            tile[c : c + CHUNK, :] = tile_of(left, scaled_norm(left, 1), right, right_norm).astype(bf16)
+            tile[c : c + CHUNK, :] = jnp.exp2(exponent(left[c : c + CHUNK], right)).astype(bf16)
             place[c : c + CHUNK, :] = one_hot(iota((CHUNK, count), 0) + c == local)
         if u == 0:
-            reads[2].wait()
+            reads[3].wait()
         total = mm(coef[u, 0:outputs], tile[...], 1, 0)
         total += mm(coef[u, outputs : 2 * outputs], place[...], 1, 0)
         total += mm(coef[u, 2 * outputs :], place[...], 1, 0)
@@ -197,9 +207,7 @@
             pieces[d, 2 * own * u : 2 * own * (u + 1), :] = jnp.concatenate(
                 [part[:, :lanes], part[:, lanes:]], axis=0
             ).astype(bf16)
-    writes.append(pltpu.make_async_copy(pieces, pieces_hbm, sems.at[1]))
-    writes[1].start()
-    wait_all(writes)
+    wait_all(start_all([(pieces, pieces_hbm)], sems))
 
 
 def factors_kernel(
@@ -211,37 +219,30 @@
     pairs = [(b_hbm, feats.at[k]) for k, b_hbm in enumerate((b0_hbm, b1_hbm, b2_hbm, b3_hbm))]
     wait_all(start_all(pairs + [(blocks_hbm, blocks), (pivots_hbm, pivots)], sems))
     places = [lax.bitwise_xor(row, k) for k in range(groups)]
+    rights = [[extended(feats[k, u], 0, False) for k in range(groups)] for u in range(UPDATES)]
     for u in range(UPDATES):
         chosen_feats = jnp.zeros((width, pivots.shape[1]), f32)
         for k in range(groups):
             chosen = iota((count, pivots.shape[1]), 0) + places[k] * count == pivots[u : u + 1, :]
             chosen_feats += mm(feats[k, u], one_hot(chosen), 1, 0)
-        left = chosen_feats.T
-        left_norm = scaled_norm(left, 1)
-        left = left.astype(bf16)
+        left = extended(chosen_feats.T, 1, True)
         for k in range(groups):
-            right = feats[k, u]
             start = pl.multiple_of(places[k] * count, count)
-            factor[u, :, pl.ds(start, count)] = tile_of(
-                left, left_norm, right, scaled_norm(right, 0)
-            ).astype(bf16)
+            value = jnp.exp2(exponent(left, rights[u][k]))
+            factor[u, :, pl.ds(start, count)] = value.astype(bf16)
     writes = start_all([(factor, factor_hbm)], sems)
     sent = 1
     for k in range(groups):
-        left = feats[k, 0].astype(f32).T
-        left_norm = scaled_norm(left, 1)
-        left = left.astype(bf16)
+        left = extended(feats[k, 0].astype(f32).T, 1, True)
         left_points = group_row(blocks, 0, places[k], count).astype(f32)
         left_points = jnp.broadcast_to(left_points, (8, count)).T[:, 0:1]
         for m in range(groups):
-            right = feats[m, 1]
-            right_norm = scaled_norm(right, 0)
             right_points = group_row(blocks, 1, places[m], count).astype(f32)
             for c in range(0, count, CHUNK):
                 rows = slice(c, c + CHUNK)
-                value = tile_of(left[rows], left_norm[rows], right, right_norm)
-                same = jnp.where(left_points[rows] == right_points, ridge_term, 0.0)
-                cross[m, k, rows, :] = (value.astype(bf16).astype(f32) + same).astype(bf16)
+                power = exponent(left[rows], rights[1][m])
+                power = jnp.where(left_points[rows] == right_points, math.log2(1.0 + ridge_term), power)
+                cross[m, k, rows, :] = jnp.exp2(power).astype(bf16)
             start = pl.multiple_of(places[k] * count, count)
             copy = pltpu.make_async_copy(
                 cross.at[m, k], cross_hbm.at[places[m], pl.ds(start, count), :], sems.at[sent]
@@ -353,7 +354,7 @@
         out_specs=[HBM] * len(outs),
         scratch_shapes=[pltpu.VMEM(x.shape, x.dtype) for x in inside]
         + [pltpu.SemaphoreType.DMA((n,)) for n in sems],
-        compiler_params=pltpu.CompilerParams(vmem_limit_bytes=48 * 2**20),
+        compiler_params=pltpu.CompilerParams(vmem_limit_bytes=62 * 2**20),
         cost_estimate=pl.CostEstimate(flops=int(flops), bytes_accessed=moved, transcendentals=0),
     )(*args)
 
@@ -404,20 +405,28 @@
     feats = like((UPDATES, width, count))
     pieces = like((devices, deep, count // 2))
     tile = like((points, count))
-    mine, pieces = call(
-        functools.partial(sums_kernel, cap),
-        [feats, pieces],
-        [block_index, features, coef, feats, tile, tile, pieces],
+    (mine,) = call(
+        functools.partial(compact_kernel, cap, points),
+        [feats],
+        [block_index, feats],
         came,
         block_index,
+        near=1,
+        sems=(1,),
+    )
+    beside, across = swap_rows(mine, 1), swap_rows(mine, 2)
+    (pieces,) = call(
+        sums_kernel,
+        [pieces],
+        [block_index, feats, features, coef, tile, tile, pieces],
+        block_index,
+        mine,
         features,
         coef,
-        near=1,
-        sems=(3,),
+        sems=(4,),
         flops=2.0 * UPDATES * points * count * (width + 3 * outputs),
     )
     summed = lax.all_to_all(pieces, ("rows", "pts"), 0, 0, tiled=True)
-    beside, across = swap_rows(mine, 1), swap_rows(mine, 2)
     kept = [like((UPDATES, rank, block)), like((rows, block, count))]
     factor, cross = call(
         factors_kernel,

time: 114 us -> 115 us (level)
  local copies, waits for them, and re-layouts: 11.4 us -> 2.4 us
  Pallas kernels: 38.2 us -> 43.4 us
  waiting for transfers between devices: 22.8 us -> 27.3 us
    unnamed x32 -> x12, local copies, waits for them, and re-layouts: 11.4 us -> 2.4 us
    pallas_call x6 -> x7, Pallas kernels: 38.2 us -> 43.4 us  [call(): pl.pallas_call(body, out_shape=outs, in_specs=[VMEM] * near + [HBM] * (le...]
    all_to_all x1, waiting for transfers between devices: 9.84 us -> 14.4 us  [with_kernels(): came = lax.all_to_all(packed, 'pts', 0, 0, tiled=True)]
  transfers between devices with their start and end apart: 5 -> 5, of which waited for: 3 -> 3; matrix products, arithmetic and copies ran while one was open for 0% -> 0% of each run, Pallas kernels for 15% -> 14%
where the time goes in v6:
time: 115 us; the launch traced here: 114 us
  Pallas kernels  43.4 us (38%)
  blocking collectives  27.6 us (24%)
  waiting for transfers between devices  27.3 us (24%)
  starting transfers between devices  12.7 us (11%)
  local copies, waits for them, and re-layouts  2.4 us (2%)
    pallas_call x7, Pallas kernels, call(): pl.pallas_call(body, out_shape=outs, in_specs=[VMEM] * near + [HBM] * (le...  43.4 us
    all_to_all x1, blocking collectives, with_kernels(): got = lax.all_to_all(steps, ('rows', 'pts'), 0, 0, tiled=True)  27.6 us
    all_to_all x1, waiting for transfers between devices, with_kernels(): came = lax.all_to_all(packed, 'pts', 0, 0, tiled=True)  14.4 us
    ppermute x3, waiting for transfers between devices, swap_rows(): return lax.ppermute(value, 'rows', [(i, i ^ k) for i in range(count)])  12.9 us
    all_to_all x1, starting transfers between devices, with_kernels(): came = lax.all_to_all(packed, 'pts', 0, 0, tiled=True)  7.29 us
    all_to_all x1, starting transfers between devices, with_kernels(): summed = lax.all_to_all(pieces, ('rows', 'pts'), 0, 0, tiled=True)  3.76 us
    unnamed x12, local copies, waits for them, and re-layouts  2.4 us
  transfers between devices with their start and end apart: 5, of which 3 were waited for; matrix products, arithmetic and copies ran while one was open for 0% of the time, Pallas kernels for 14%

profile of v6, /device:TPU:0, one launch (start us, length us, event | category | flops | bytes accessed | tf_op | source)
XLA Modules:
  0.0 114.3 jit_solution(17613616320110978433)
XLA Ops:
  0.6 2.6 %shard_map.86 = bf16[8,384,128]{2,1,0:T(8,128)(2,1)} custom-call(s32[2,2048]{1,0:T(2,128)} %blocks_hbm.9, bf16[1024,128]{1,0:T(8,128)(2,1)} %feats_hbm.3), custom_call_target="tpu_custom_call" | custom-call | bytes 1064960 | tf_op jit(solution)/shard_map/pallas_call | solution.py:350
  3.2 7.3 %all-to-all-start = ((bf16[8,384,128]{2,1,0:T(8,128)(2,1)}), bf16[8,384,128]{2,1,0:T(8,128)(2,1)S(1)}, u32[]{:S(2)}, u32[]{:S(2)}) async-start(bf16[8,384,128]{2,1,0:T(8,128)(2,1)} %shard_map.86), calls=%async_computation | async-start | bytes 1572864 | tf_op jit(solution)/shard_map/all_to_all | solution.py:389
  10.5 5.7 %shard_map.88 = (bf16[2,768,1024]{2,1,0:T(8,128)(2,1)}, bf16[2,768,1024]{2,1,0:T(8,128)(2,1)}, s32[8,512]{1,0:T(8,128)}) custom-call(s32[2,2048]{1,0:T(2,128)} %blocks_hbm.9, f32[1024,256]{1,0:T(8,128)} %w_hbm.3, f32[1024,256]{1,0:T(8,128)} %z_hbm.3, bf16[1024,256]{1,0:T(8,128)(2,1)} %t_hbm.1), custom_call_target="tpu_custom_call" | custom-call | bytes 8945664 | tf_op jit(solution)/shard_map/pallas_call | solution.py:350
  16.2 14.4 %all-to-all-done.came = bf16[8,384,128]{2,1,0:T(8,128)(2,1)S(1)} async-done(((bf16[8,384,128]{2,1,0:T(8,128)(2,1)}), bf16[8,384,128]{2,1,0:T(8,128)(2,1)S(1)}, u32[]{:S(2)}, u32[]{:S(2)}) %all-to-all-start) | async-done | bytes 786464 | tf_op jit(solution)/shard_map/all_to_all | solution.py:389
  30.7 0.0 copy-start
  30.7 0.9 copy-done
  31.5 3.6 %shard_map.87.block_hbm.b0_hbm = bf16[2,128,512]{2,1,0:T(8,128)(2,1)} custom-call(bf16[8,384,128]{2,1,0:T(8,128)(2,1)} %copy-done, s32[2,2048]{1,0:T(2,128)} %blocks_hbm.9), custom_call_target="tpu_custom_call" | custom-call | bytes 1064960 | tf_op jit(solution)/shard_map/pallas_call | solution.py:350
  35.2 0.0 copy-start.2
  35.2 5.1 %shard_map.89 = bf16[32,32,256]{2,1,0:T(8,128)(2,1)} custom-call(s32[2,2048]{1,0:T(2,128)} %blocks_hbm.9, bf16[2,128,512]{2,1,0:T(8,128)(2,1)} %shard_map.87.block_hbm.b0_hbm, bf16[1024,128]{1,0:T(8,128)(2,1)} %feats_hbm.3, bf16[2,768,1024]{2,1,0:T(8,128)(2,1)} %get-tuple-element.7.coef_hbm), custom_call_target="tpu_custom_call" | custom-call | flops 1879048192 | bytes 4210688 | tf_op jit(solution)/shard_map/pallas_call | solution.py:350
  40.3 3.8 %all-to-all-start.1 = ((bf16[32,32,256]{2,1,0:T(8,128)(2,1)}), bf16[32,32,256]{2,1,0:T(8,128)(2,1)S(1)}, u32[]{:S(2)}, u32[]{:S(2)}) async-start(bf16[32,32,256]{2,1,0:T(8,128)(2,1)} %shard_map.89), calls=%async_computation.1 | async-start | bytes 1048576 | tf_op jit(solution)/shard_map/all_to_all | solution.py:429
  44.0 0.0 copy-done.2
  44.0 1.7 %collective-permute-start.1 = (bf16[2,128,512]{2,1,0:T(8,128)(2,1)S(1)}, bf16[2,128,512]{2,1,0:T(8,128)(2,1)S(1)}, u32[]{:S(2)}, u32[]{:S(2)}) collective-permute-start(bf16[2,128,512]{2,1,0:T(8,128)(2,1)S(1)} %copy-done.2), channel_id=1, source_target_pairs={{0,16},{8,24},{16,0},{24,8},{1,17},{9,25},{17,1},{25,9},{2,18},{10... | collective-permute-start | bytes 786440 | tf_op jit(solution)/shard_map/ppermute | solution.py:364
  45.7 0.0 collective-permute-start
  45.7 11.4 %collective-permute-done.1.b2_hbm = bf16[2,128,512]{2,1,0:T(8,128)(2,1)S(1)} collective-permute-done((bf16[2,128,512]{2,1,0:T(8,128)(2,1)S(1)}, bf16[2,128,512]{2,1,0:T(8,128)(2,1)S(1)}, u32[]{:S(2)}, u32[]{:S(2)}) %collective-permute-start.1) | collective-permute-done | bytes 262176 | tf_op jit(solution)/shard_map/ppermute | solution.py:364
  57.1 0.0 copy-start.3
  57.1 0.0 collective-permute-start.2
  57.1 0.0 collective-permute-done.b1_hbm
  57.1 0.0 copy-start.4
  57.1 1.5 %collective-permute-done.2.b3_hbm = bf16[2,128,512]{2,1,0:T(8,128)(2,1)S(1)} collective-permute-done((bf16[2,128,512]{2,1,0:T(8,128)(2,1)S(1)}, bf16[2,128,512]{2,1,0:T(8,128)(2,1)S(1)}, u32[]{:S(2)}, u32[]{:S(2)}) %collective-permute-start.2) | collective-permute-done | bytes 262176 | tf_op jit(solution)/shard_map/ppermute | solution.py:364
  58.6 0.0 copy-done.3
  58.6 0.0 copy-done.4
  58.6 0.0 copy-start.5
  58.6 0.7 copy-done.5
  59.4 9.7 %shard_map.90 = (bf16[2,512,2048]{2,1,0:T(8,128)(2,1)}, bf16[4,2048,512]{2,1,0:T(8,128)(2,1)}) custom-call(bf16[2,128,512]{2,1,0:T(8,128)(2,1)} %shard_map.87.block_hbm.b0_hbm, bf16[2,128,512]{2,1,0:T(8,128)(2,1)} %copy-done.4, bf16[2,128,512]{2,1,0:T(8,128)(2,1)} %copy-done.3, bf16[2,128,512]{2,1,0:T(8,128)(2,1)} %copy-done.5, s32[2,2048]{1,0:T(2,128)} %blocks_hbm.9, ...), custom_call_target="tpu_custom_call" | custom-call | flops 1610612736 | bytes 13651968 | tf_op jit(solution)/shard_map/pallas_call | solution.py:350
  69.1 0.0 all-to-all-done.1.summed
  69.1 0.0 copy-start.1
  69.1 0.8 copy-done.1
  69.9 11.0 %shard_map.91 = bf16[32,32,384]{2,1,0:T(8,128)(2,1)} custom-call(bf16[32,32,256]{2,1,0:T(8,128)(2,1)} %copy-done.1, bf16[2,512,2048]{2,1,0:T(8,128)(2,1)} %get-tuple-element.8.factor_hbm, bf16[2,512,512]{2,1,0:T(8,128)(2,1)} %core_hbm.1, bf16[4,2048,512]{2,1,0:T(8,128)(2,1)} %get-tuple-element.9.cross_hbm, s32[8,512]{1,0:T(8,128)} %get-tuple-element.10.slots_hbm), custom_call_target="tpu_custom_call" | custom-call | bytes 14958592 | tf_op jit(solution)/shard_map/pallas_call | solution.py:350
  81.0 27.6 %all_to_all.15.got = bf16[32,32,384]{2,1,0:T(8,128)(2,1)} all-to-all(bf16[32,32,384]{2,1,0:T(8,128)(2,1)} %shard_map.91), channel_id=1, replica_groups=mesh['rows'=4,'pts'=8] {'rows','pts'}, dimensions={0} | all-to-all | bytes 1572864 | tf_op jit(solution)/shard_map/all_to_all | solution.py:462
  108.5 5.6 %shard_map.92 = (f32[1024,256]{1,0:T(8,128)}, f32[1024,256]{1,0:T(8,128)}) custom-call(bf16[32,32,384]{2,1,0:T(8,128)(2,1)} %all_to_all.15.got, f32[1024,256]{1,0:T(8,128)} %w_hbm.3, f32[1024,256]{1,0:T(8,128)} %z_hbm.3, bf16[2,768,1024]{2,1,0:T(8,128)(2,1)} %get-tuple-element.11.rows_hbm), custom_call_target="tpu_custom_call" | custom-call | bytes 8126464 | tf_op jit(solution)/shard_map/pallas_call | solution.py:350
Async XLA Ops:
  3.2 27.5 %all-to-all-start = ((bf16[8,384,128]{2,1,0:T(8,128)(2,1)}), bf16[8,384,128]{2,1,0:T(8,128)(2,1)S(1)}, u32[]{:S(2)}, u32[]{:S(2)}) async-start(bf16[8,384,128]{2,1,0:T(8,128)(2,1)} %shard_map.86), calls=%async_computation | async-start | bytes 1572864 | tf_op jit(solution)/shard_map/all_to_all | solution.py:389
  30.7 0.9 copy-start
  35.2 8.9 %copy-start.2 = (bf16[2,128,512]{2,1,0:T(8,128)(2,1)S(1)}, bf16[2,128,512]{2,1,0:T(8,128)(2,1)}, u32[]{:S(2)}) copy-start(bf16[2,128,512]{2,1,0:T(8,128)(2,1)} %shard_map.87.block_hbm.b0_hbm) | copy-start | bytes 786436
  40.3 28.8 %all-to-all-start.1 = ((bf16[32,32,256]{2,1,0:T(8,128)(2,1)}), bf16[32,32,256]{2,1,0:T(8,128)(2,1)S(1)}, u32[]{:S(2)}, u32[]{:S(2)}) async-start(bf16[32,32,256]{2,1,0:T(8,128)(2,1)} %shard_map.89), calls=%async_computation.1 | async-start | bytes 1048576 | tf_op jit(solution)/shard_map/all_to_all | solution.py:429
  44.0 13.0 %collective-permute-start.1 = (bf16[2,128,512]{2,1,0:T(8,128)(2,1)S(1)}, bf16[2,128,512]{2,1,0:T(8,128)(2,1)S(1)}, u32[]{:S(2)}, u32[]{:S(2)}) collective-permute-start(bf16[2,128,512]{2,1,0:T(8,128)(2,1)S(1)} %copy-done.2), channel_id=1, source_target_pairs={{0,16},{8,24},{16,0},{24,8},{1,17},{9,25},{17,1},{25,9},{2,18},{10... | collective-permute-start | bytes 786440 | tf_op jit(solution)/shard_map/ppermute | solution.py:364
  45.7 11.4 %collective-permute-start = (bf16[2,128,512]{2,1,0:T(8,128)(2,1)S(1)}, bf16[2,128,512]{2,1,0:T(8,128)(2,1)S(1)}, u32[]{:S(2)}, u32[]{:S(2)}) collective-permute-start(bf16[2,128,512]{2,1,0:T(8,128)(2,1)S(1)} %copy-done.2), channel_id=1, source_target_pairs={{0,8},{8,0},{16,24},{24,16},{1,9},{9,1},{17,25},{25,17},{2,10},{10... | collective-permute-start | bytes 786440 | tf_op jit(solution)/shard_map/ppermute | solution.py:364
  57.1 1.5 %copy-start.3 = (bf16[2,128,512]{2,1,0:T(8,128)(2,1)}, bf16[2,128,512]{2,1,0:T(8,128)(2,1)S(1)}, u32[]{:S(2)}) copy-start(bf16[2,128,512]{2,1,0:T(8,128)(2,1)S(1)} %collective-permute-done.1.b2_hbm) | copy-start | bytes 786436
  57.1 1.5 %collective-permute-start.2 = (bf16[2,128,512]{2,1,0:T(8,128)(2,1)S(1)}, bf16[2,128,512]{2,1,0:T(8,128)(2,1)S(1)}, u32[]{:S(2)}, u32[]{:S(2)}) collective-permute-start(bf16[2,128,512]{2,1,0:T(8,128)(2,1)S(1)} %collective-permute-done.1.b2_hbm), channel_id=1, source_target_pairs={{0,8},{8,0},{16,24},{24,16},{1,9},{9,1},{17,25},{25,17},{2,10},{10... | collective-permute-start | bytes 786440 | tf_op jit(solution)/shard_map/ppermute | solution.py:364
  57.1 1.5 %copy-start.4 = (bf16[2,128,512]{2,1,0:T(8,128)(2,1)}, bf16[2,128,512]{2,1,0:T(8,128)(2,1)S(1)}, u32[]{:S(2)}) copy-start(bf16[2,128,512]{2,1,0:T(8,128)(2,1)S(1)} %collective-permute-done.b1_hbm) | copy-start | bytes 786436
  58.6 0.7 copy-start.5
  69.1 0.8 copy-start.1

commit v7 on v6

--- a/solution.py
+++ b/solution.py
@@ -109,38 +109,67 @@
     wait_all(start_all([(packed, out_hbm.at[o]) for o in range(owners)], sems))
 
 
-def coefficients_of(mixed, goal):
-    high, low = split_two(ridge_term * mixed - goal)
-    return mixed.astype(bf16), high, low
+def two_digits(row):
+    high = lax.shift_right_logical(row, jnp.full_like(row, 7))
+    shape = (8, row.shape[1])
+    value = jnp.where(iota(shape, 0) == 0, high, lax.bitwise_and(row, jnp.full_like(row, 127)))
+    return value.astype(f32).astype(bf16)
+
+
+def from_digits(digits):
+    return (digits[0:1] * 128.0 + digits[1:2]).astype(i32)
 
 
 def prepare_kernel(
     count, cap, owners,
-    blocks_hbm, w_hbm, z_hbm, t_hbm, coef_hbm, rows_hbm, slots_hbm,
-    blocks, w, z, t, coef, rows, slots, sems,
+    blocks_hbm, pivots_hbm, w_hbm, z_hbm, t_hbm,
+    coef_hbm, offset_hbm, rows_hbm, ids_hbm, starts_hbm, chosen_hbm,
+    blocks, pivots, w, z, t, coef, offset, rows, ids, starts, chosen, sems,
 ):
-    me = lax.axis_index("pts")
+    row, me = lax.axis_index("rows"), lax.axis_index("pts")
     points, outputs = w.shape
-    reads = start_all([(blocks_hbm, blocks), (w_hbm, w), (z_hbm, z), (t_hbm, t)], sems)
+    pairs = [(blocks_hbm, blocks), (pivots_hbm, pivots), (w_hbm, w), (z_hbm, z), (t_hbm, t)]
+    reads = start_all(pairs, sems)
     before = before_matrix(count)
-    reads[0].wait()
+    wait_all(reads[:2])
     groups = blocks.shape[1] // count
     for u in range(UPDATES):
+        pivot = pivots[u : u + 1, :]
+        found = jnp.zeros((8, pivot.shape[1]), f32)
         for g in range(groups):
+            n = u * groups + g
             indices = blocks[u : u + 1, g * count : (g + 1) * count]
-            held = slots_of(indices, before, points, owners, cap)
-            n = u * groups + g
-            slots[n : n + 1, :] = held
+            owner = lax.div(indices, jnp.full_like(indices, points))
+            owner_ids = iota((owners, count), 0)
+            marks = jnp.where(owner_ids == owner, 1.0, 0.0)
+            earlier = mm(marks.astype(bf16), before, 1, 0)
+            start = jnp.sum(jnp.where(owner < owner_ids, 1.0, 0.0), axis=1, keepdims=True)
+            rank = jnp.sum(marks * earlier, axis=0, keepdims=True)
+            place = (rank + jnp.sum(marks * start, axis=0, keepdims=True)).astype(i32)
+            held = owner * cap + rank.astype(i32)
             rows[u, g * cap : (g + 1) * cap, :] = point_rows(indices, held, me, points, cap)
-    wait_all(reads[1:])
+            ordered = one_hot(iota((count, count), 0) == place)
+            ids[n : n + 1, :] = from_digits(mm(two_digits(indices), ordered, 1, 1))
+            diagonal = iota((owners, 128), 0) == iota((owners, 128), 1)
+            starts[n : n + 1, :] = jnp.sum(
+                jnp.where(diagonal, start, 0.0), axis=0, keepdims=True
+            ).astype(i32)
+            at_pivot = one_hot(iota((count, pivot.shape[1]), 0) + g * count == pivot)
+            found += mm(two_digits(place + g * count), at_pivot, 1, 0)
+        chosen[u : u + 1, :] = from_digits(found)
+    wait_all(reads[2:])
     current, moving = w[...], z[...]
     goal = t[...].astype(f32).T
     for u in range(UPDATES):
         mixed = mixed_of(current, moving).T
-        for n, part in enumerate(coefficients_of(mixed, goal)):
-            coef[u, n * outputs : (n + 1) * outputs, :] = part
+        high, low = split_two(ridge_term * mixed - goal)
+        coef[u] = mixed.astype(bf16)
+        local = ids[pl.ds(u * groups + row, 1), :] - me * points
+        place = one_hot(iota((points, count), 0) == local)
+        offset[u] = mm(high, place, 1, 0) + mm(low, place, 1, 0)
         current, moving = stepped(current, moving, None)
-    wait_all(start_all([(coef, coef_hbm), (rows, rows_hbm), (slots, slots_hbm)], sems))
+    pairs = [(coef, coef_hbm), (offset, offset_hbm), (rows, rows_hbm), (ids, ids_hbm)]
+    wait_all(start_all([*pairs, (starts, starts_hbm), (chosen, chosen_hbm)], sems))
 
 
 def extended(rows, axis, first):
@@ -164,42 +193,38 @@
 CHUNK = 256
 
 
-def compact_kernel(cap, points, came, blocks_hbm, block_hbm, blocks, block, sems):
+def compact_kernel(came, starts_hbm, block_hbm, starts, wide, block, sems):
     row = lax.axis_index("rows")
-    owners, _, width = came.shape
+    owners, deep, _ = came.shape
+    cap = deep // UPDATES
+    groups = starts.shape[0] // UPDATES
     count = block.shape[2]
-    wait_all(start_all([(blocks_hbm, blocks)], sems))
-    before = before_matrix(count)
-    for u in range(UPDATES):
-        slots = slots_of(group_row(blocks, u, row, count), before, points, owners, cap)
-        chosen = one_hot(iota((owners * cap, count), 0) == slots)
-        packed = came[:, u * cap : (u + 1) * cap, :].reshape(owners * cap, width)
-        block[u] = mm(packed, chosen, 0, 0).astype(bf16)
+    wait_all(start_all([(starts_hbm, starts)], sems))
+    for u in range(UPDATES):
+        for o in range(owners):
+            start = starts[u * groups + row, o]
+            wide[u, pl.ds(start, cap), :] = came[o, u * cap : (u + 1) * cap, :].astype(f32)
+        block[u] = wide[u, 0:count, :].T.astype(bf16)
     wait_all(start_all([(block, block_hbm)], sems))
 
 
 def sums_kernel(
-    blocks_hbm, block_hbm, feats_hbm, coef_hbm, pieces_hbm,
-    blocks, block, feats, coef, tile, place, pieces, sems,
+    block_hbm, feats_hbm, coef_hbm, offset_hbm, pieces_hbm,
+    block, feats, coef, offset, tile, pieces, sems,
 ):
-    row, me = lax.axis_index("rows"), lax.axis_index("pts")
     points, count = tile.shape
-    outputs = coef.shape[1] // 3
-    pairs = [(blocks_hbm, blocks), (block_hbm, block), (feats_hbm, feats), (coef_hbm, coef)]
+    outputs = coef.shape[1]
+    pairs = [(block_hbm, block), (feats_hbm, feats), (coef_hbm, coef), (offset_hbm, offset)]
     reads = start_all(pairs, sems)
-    wait_all(reads[:3])
+    wait_all(reads[:2])
     left = extended(feats[...], 1, True)
     for u in range(UPDATES):
         right = extended(block[u], 0, False)
-        local = group_row(blocks, u, row, count) - me * points
         for c in range(0, points, CHUNK):
             tile[c : c + CHUNK, :] = jnp.exp2(exponent(left[c : c + CHUNK], right)).astype(bf16)
-            place[c : c + CHUNK, :] = one_hot(iota((CHUNK, count), 0) + c == local)
         if u == 0:
-            reads[3].wait()
-        total = mm(coef[u, 0:outputs], tile[...], 1, 0)
-        total += mm(coef[u, outputs : 2 * outputs], place[...], 1, 0)
-        total += mm(coef[u, 2 * outputs :], place[...], 1, 0)
+            wait_all(reads[2:])
+        total = offset[u] + mm(coef[u], tile[...], 1, 0)
         devices, _, lanes = pieces.shape
         own = outputs // devices
         for d in range(devices):
@@ -211,13 +236,13 @@
 
 
 def factors_kernel(
-    b0_hbm, b1_hbm, b2_hbm, b3_hbm, blocks_hbm, pivots_hbm, factor_hbm, cross_hbm,
-    feats, blocks, pivots, factor, cross, sems,
+    b0_hbm, b1_hbm, b2_hbm, b3_hbm, ids_hbm, pivots_hbm, factor_hbm, cross_hbm,
+    feats, ids, pivots, factor, cross, sems,
 ):
     row = lax.axis_index("rows")
     groups, _, width, count = feats.shape
     pairs = [(b_hbm, feats.at[k]) for k, b_hbm in enumerate((b0_hbm, b1_hbm, b2_hbm, b3_hbm))]
-    wait_all(start_all(pairs + [(blocks_hbm, blocks), (pivots_hbm, pivots)], sems))
+    wait_all(start_all(pairs + [(ids_hbm, ids), (pivots_hbm, pivots)], sems))
     places = [lax.bitwise_xor(row, k) for k in range(groups)]
     rights = [[extended(feats[k, u], 0, False) for k in range(groups)] for u in range(UPDATES)]
     for u in range(UPDATES):
@@ -234,10 +259,10 @@
     sent = 1
     for k in range(groups):
         left = extended(feats[k, 0].astype(f32).T, 1, True)
-        left_points = group_row(blocks, 0, places[k], count).astype(f32)
+        left_points = ids[pl.ds(places[k], 1), :].astype(f32)
         left_points = jnp.broadcast_to(left_points, (8, count)).T[:, 0:1]
         for m in range(groups):
-            right_points = group_row(blocks, 1, places[m], count).astype(f32)
+            right_points = ids[pl.ds(groups + places[m], 1), :].astype(f32)
             for c in range(0, count, CHUNK):
                 rows = slice(c, c + CHUNK)
                 power = exponent(left[rows], rights[1][m])
@@ -255,8 +280,8 @@
 
 def chain_kernel(
     cap, owners,
-    summed, factor_hbm, core_hbm, cross_hbm, slots_hbm, out_hbm,
-    factor, core, cross, slots, packed, sems,
+    summed, factor_hbm, core_hbm, cross_hbm, starts_hbm, out_hbm,
+    factor, core, cross, starts, packed, sems,
 ):
     groups, _, count = cross.shape
     own = summed.shape[1] // (2 * UPDATES)
@@ -264,7 +289,7 @@
     for u in range(UPDATES):
         pairs += [(factor_hbm.at[u], factor.at[u]), (core_hbm.at[u], core.at[u])]
         if u == 0:
-            pairs += [(slots_hbm, slots)]
+            pairs += [(starts_hbm, starts)]
             pairs += [(cross_hbm.at[g], cross.at[g]) for g in range(groups)]
     reads = start_all(pairs, sems)
     step = None
@@ -284,14 +309,13 @@
         proj = mm(resid.astype(bf16), factor[u], 1, 1)
         lifted = mm(proj.astype(bf16), core[u], 1, 1).astype(bf16)
         step = (resid - mm(lifted, factor[u], 1, 0)).astype(bf16)
-        parts = []
-        for g in range(groups):
-            n = u * groups + g
-            place = one_hot(iota((owners * cap, count), 0) == slots[n : n + 1, :])
-            parts.append(mm(step[:, g * count : (g + 1) * count], place, 1, 1))
         half = groups // 2
         for o in range(owners):
-            lanes = [x[:, o * cap : (o + 1) * cap] for x in parts]
+            lanes = []
+            for g in range(groups):
+                part = step[:, g * count : (g + 1) * count].astype(f32)
+                back = lax.rem(count - starts[u * groups + g, o], count)
+                lanes.append(pltpu.roll(part, back, 1)[:, :cap])
             packed[o, 2 * own * u : 2 * own * (u + 1), :] = jnp.concatenate(
                 [jnp.concatenate(lanes[h * half : (h + 1) * half], axis=1) for h in range(2)], axis=0
             ).astype(bf16)
@@ -339,22 +363,25 @@
 
 VMEM = pl.BlockSpec(memory_space=pltpu.VMEM)
 HBM = pl.BlockSpec(memory_space=pltpu.HBM)
+in_smem = type(pltpu.SMEM((1,), i32))
 
 
 def like(shape, dtype=bf16):
     return jax.ShapeDtypeStruct(shape, dtype)
 
 
-def call(body, outs, inside, *args, near=0, sems=(), flops=0):
+def call(body, outs, inside, *args, near=0, sems=(), flops=0, grant=62):
     moved = sum(math.prod(o.shape) * o.dtype.itemsize for o in [*outs, *args])
     return pl.pallas_call(
         body,
         out_shape=outs,
         in_specs=[VMEM] * near + [HBM] * (len(args) - near),
         out_specs=[HBM] * len(outs),
-        scratch_shapes=[pltpu.VMEM(x.shape, x.dtype) for x in inside]
+        scratch_shapes=[
+            x if isinstance(x, in_smem) else pltpu.VMEM(x.shape, x.dtype) for x in inside
+        ]
         + [pltpu.SemaphoreType.DMA((n,)) for n in sems],
-        compiler_params=pltpu.CompilerParams(vmem_limit_bytes=62 * 2**20),
+        compiler_params=pltpu.CompilerParams(vmem_limit_bytes=grant * 2**20),
         cost_estimate=pl.CostEstimate(flops=int(flops), bytes_accessed=moved, transcendentals=0),
     )(*args)
 
@@ -388,44 +415,46 @@
     )
     came = lax.all_to_all(packed, "pts", 0, 0, tiled=True)
     kept = [
-        like((UPDATES, 3 * outputs, points)),
+        like((UPDATES, outputs, points)),
+        like((UPDATES, outputs, count), f32),
         like((UPDATES, rows * cap, points)),
         like((UPDATES * rows, count), i32),
+        like((UPDATES * rows, 128), i32),
+        like((UPDATES, rank), i32),
     ]
-    coef, place, slots = call(
+    given = [block_index, pivot_index, coefficients, momentum, targets]
+    coef, offset, place, ids, starts, chosen = call(
         functools.partial(prepare_kernel, count, cap, owners),
         kept,
-        [block_index, coefficients, momentum, targets, *kept],
-        block_index,
-        coefficients,
-        momentum,
-        targets,
-        sems=(4,),
+        given + kept,
+        *given,
+        sems=(6,),
     )
     feats = like((UPDATES, width, count))
-    pieces = like((devices, deep, count // 2))
-    tile = like((points, count))
+    inside_starts = pltpu.SMEM(starts.shape, i32)
     (mine,) = call(
-        functools.partial(compact_kernel, cap, points),
+        compact_kernel,
         [feats],
-        [block_index, feats],
+        [inside_starts, like((UPDATES, count + cap, width), f32), feats],
         came,
-        block_index,
+        starts,
         near=1,
         sems=(1,),
     )
     beside, across = swap_rows(mine, 1), swap_rows(mine, 2)
+    pieces = like((devices, deep, count // 2))
     (pieces,) = call(
         sums_kernel,
         [pieces],
-        [block_index, feats, features, coef, tile, tile, pieces],
-        block_index,
+        [feats, features, coef, offset, like((points, count)), pieces],
         mine,
         features,
         coef,
+        offset,
         sems=(4,),
-        flops=2.0 * UPDATES * points * count * (width + 3 * outputs),
-    )
+        flops=2.0 * UPDATES * points * count * (2 * width + outputs),
+    )
+    pieces, across = lax.optimization_barrier((pieces, across))
     summed = lax.all_to_all(pieces, ("rows", "pts"), 0, 0, tiled=True)
     kept = [like((UPDATES, rank, block)), like((rows, block, count))]
     factor, cross = call(
@@ -433,8 +462,8 @@
         kept,
         [
             like((rows, *feats.shape)),
-            block_index,
-            pivot_index,
+            ids,
+            chosen,
             kept[0],
             like((rows, rows, count, count)),
         ],
@@ -442,20 +471,20 @@
         beside,
         across,
         swap_rows(across, 1),
-        block_index,
-        pivot_index,
+        ids,
+        chosen,
         sems=(rows * rows + 1,),
         flops=2.0 * width * block * (UPDATES * rank + block),
     )
     (steps,) = call(
         functools.partial(chain_kernel, cap, owners),
         [like((devices, deep, half * cap))],
-        [factor, core, cross, slots, like((owners, deep, half * cap))],
+        [factor, core, cross, inside_starts, like((owners, deep, half * cap))],
         summed,
         factor,
         core,
         cross,
-        slots,
+        starts,
         near=1,
         sems=(2 * UPDATES + 1 + rows,),
     )
@@ -471,6 +500,7 @@
         place,
         near=1,
         sems=(3 * parts, 2 * parts),
+        grant=40,
     )
 
 

time: 115 us -> 104 us (0.904)
  waiting for transfers between devices: 27.3 us -> 18.2 us
  Pallas kernels: 43.4 us -> 39.7 us
  local copies, waits for them, and re-layouts: 2.4 us -> 5.51 us
  blocking collectives: 27.6 us -> 24.6 us
  starting transfers between devices: 12.7 us -> 14.8 us
    ppermute x3, waiting for transfers between devices: 12.9 us -> 3.2 us  [swap_rows(): return lax.ppermute(value, 'rows', [(i, i ^ k) for i in range(count)])]
    all_to_all x1, waiting for transfers between devices: 0.01 us -> 3.74 us  [with_kernels(): summed = lax.all_to_all(pieces, ('rows', 'pts'), 0, 0, tiled=True)]
    pallas_call x7, Pallas kernels: 43.4 us -> 39.7 us  [call(): pl.pallas_call(body, out_shape=outs, in_specs=[VMEM] * near + [HBM] * (le...]
    all_to_all x1, waiting for transfers between devices: 14.4 us -> 11.2 us  [with_kernels(): came = lax.all_to_all(packed, 'pts', 0, 0, tiled=True)]
    unnamed x12 -> x18, local copies, waits for them, and re-layouts: 2.4 us -> 5.51 us
    all_to_all x1, blocking collectives: 27.6 us -> 24.6 us  [with_kernels(): got = lax.all_to_all(steps, ('rows', 'pts'), 0, 0, tiled=True)]
    all_to_all x1, starting transfers between devices: 3.76 us -> 5.34 us  [with_kernels(): summed = lax.all_to_all(pieces, ('rows', 'pts'), 0, 0, tiled=True)]
  transfers between devices with their start and end apart: 5 -> 5, of which waited for: 3 -> 5; matrix products, arithmetic and copies ran while one was open for 0% -> 0% of each run, Pallas kernels for 14% -> 21%
where the time goes in v7:
time: 104 us
  Pallas kernels  39.7 us (38%)
  blocking collectives  24.6 us (24%)
  waiting for transfers between devices  18.2 us (18%)
  starting transfers between devices  14.8 us (14%)
  local copies, waits for them, and re-layouts  5.51 us (5%)
    pallas_call x7, Pallas kernels, call(): pl.pallas_call(body, out_shape=outs, in_specs=[VMEM] * near + [HBM] * (le...  39.7 us
    all_to_all x1, blocking collectives, with_kernels(): got = lax.all_to_all(steps, ('rows', 'pts'), 0, 0, tiled=True)  24.6 us
    all_to_all x1, waiting for transfers between devices, with_kernels(): came = lax.all_to_all(packed, 'pts', 0, 0, tiled=True)  11.2 us
    all_to_all x1, starting transfers between devices, with_kernels(): came = lax.all_to_all(packed, 'pts', 0, 0, tiled=True)  7.29 us
    unnamed x18, local copies, waits for them, and re-layouts  5.51 us
    all_to_all x1, starting transfers between devices, with_kernels(): summed = lax.all_to_all(pieces, ('rows', 'pts'), 0, 0, tiled=True)  5.34 us
    all_to_all x1, waiting for transfers between devices, with_kernels(): summed = lax.all_to_all(pieces, ('rows', 'pts'), 0, 0, tiled=True)  3.74 us
    ppermute x3, waiting for transfers between devices, swap_rows(): return lax.ppermute(value, 'rows', [(i, i ^ k) for i in range(count)])  3.2 us
  transfers between devices with their start and end apart: 5, of which 5 were waited for; matrix products, arithmetic and copies ran while one was open for 0% of the time, Pallas kernels for 21%

profile of v7, /device:TPU:0, one launch (start us, length us, event | category | flops | bytes accessed | tf_op | source)
XLA Modules:
  0.0 103.7 jit_solution(16126260981717833043)
XLA Ops:
  0.6 2.6 %shard_map.86 = bf16[8,384,128]{2,1,0:T(8,128)(2,1)} custom-call(s32[2,2048]{1,0:T(2,128)} %blocks_hbm.3, bf16[1024,128]{1,0:T(8,128)(2,1)} %feats_hbm.3), custom_call_target="tpu_custom_call" | custom-call | bytes 1064960 | tf_op jit(solution)/shard_map/pallas_call | solution.py:375
  3.2 7.3 %all-to-all-start = ((bf16[8,384,128]{2,1,0:T(8,128)(2,1)}), bf16[8,384,128]{2,1,0:T(8,128)(2,1)S(1)}, u32[]{:S(2)}, u32[]{:S(2)}) async-start(bf16[8,384,128]{2,1,0:T(8,128)(2,1)} %shard_map.86), calls=%async_computation | async-start | bytes 1572864 | tf_op jit(solution)/shard_map/all_to_all | solution.py:416
  10.5 8.9 %shard_map.87 = (bf16[2,256,1024]{2,1,0:T(8,128)(2,1)}, f32[2,256,512]{2,1,0:T(8,128)}, bf16[2,768,1024]{2,1,0:T(8,128)(2,1)}, s32[8,512]{1,0:T(8,128)}, s32[8,128]{1,0:T(8,128)}, /*index=5*/s32[2,512]{1,0:T(2,128)}) custom-call(s32[2,2048]{1,0:T(2,128)} %blocks_hbm.3, s32[2,512]{1,0:T(2,128)} %pivots_hbm.1, f32[1024,256]{1,0:T(8,128)} %w_hbm.3, ...), custom_call_target="tpu_custom_call" | custom-call | bytes 7909376 | tf_op jit(solution)/shard_map/pallas_call | solution.py:375
  19.5 11.2 %all-to-all-done.came = bf16[8,384,128]{2,1,0:T(8,128)(2,1)S(1)} async-done(((bf16[8,384,128]{2,1,0:T(8,128)(2,1)}), bf16[8,384,128]{2,1,0:T(8,128)(2,1)S(1)}, u32[]{:S(2)}, u32[]{:S(2)}) %all-to-all-start) | async-done | bytes 786464 | tf_op jit(solution)/shard_map/all_to_all | solution.py:416
  30.7 0.0 copy-start.3
  30.7 0.9 copy-done.3
  31.6 2.8 %shard_map.88.block_hbm.b0_hbm = bf16[2,128,512]{2,1,0:T(8,128)(2,1)} custom-call(bf16[8,384,128]{2,1,0:T(8,128)(2,1)} %copy-done.3, s32[8,128]{1,0:T(8,128)} %get-tuple-element.12.starts_hbm), custom_call_target="tpu_custom_call" | custom-call | bytes 1052672 | tf_op jit(solution)/shard_map/pallas_call | solution.py:375
  34.4 0.0 copy-start.5
  34.4 1.6 %collective-permute-start = (bf16[2,128,512]{2,1,0:T(8,128)(2,1)}, bf16[2,128,512]{2,1,0:T(8,128)(2,1)S(1)}, u32[]{:S(2)}, u32[]{:S(2)}) collective-permute-start(bf16[2,128,512]{2,1,0:T(8,128)(2,1)} %shard_map.88.block_hbm.b0_hbm), channel_id=1, source_target_pairs={{0,16},{8,24},{16,0},{24,8},{1,17},{9,25},{17,1},{25,9},{2,18},{10... | collective-permute-start | bytes 786440 | tf_op jit(solution)/shard_map/ppermute | solution.py:391
  36.0 3.5 %shard_map.89 = bf16[32,32,256]{2,1,0:T(8,128)(2,1)} custom-call(bf16[2,128,512]{2,1,0:T(8,128)(2,1)} %shard_map.88.block_hbm.b0_hbm, bf16[1024,128]{1,0:T(8,128)(2,1)} %feats_hbm.3, bf16[2,256,1024]{2,1,0:T(8,128)(2,1)} %get-tuple-element.13.coef_hbm, f32[2,256,512]{2,1,0:T(8,128)} %get-tuple-element.14.offset_hbm), custom_call_target="tpu_custom_call" | custom-call | flops 1073741824 | bytes 3145728 | tf_op jit(solution)/shard_map/pallas_call | solution.py:375
  39.5 1.8 %collective-permute-done.b2_hbm = bf16[2,128,512]{2,1,0:T(8,128)(2,1)S(1)} collective-permute-done((bf16[2,128,512]{2,1,0:T(8,128)(2,1)}, bf16[2,128,512]{2,1,0:T(8,128)(2,1)S(1)}, u32[]{:S(2)}, u32[]{:S(2)}) %collective-permute-start) | collective-permute-done | bytes 262176 | tf_op jit(solution)/shard_map/ppermute | solution.py:391
  41.3 0.0 copy-start.6
  41.3 5.3 %all-to-all-start.1 = ((bf16[32,32,256]{2,1,0:T(8,128)(2,1)}), bf16[32,32,256]{2,1,0:T(8,128)(2,1)S(1)}, u32[]{:S(2)}, u32[]{:S(2)}) async-start(bf16[32,32,256]{2,1,0:T(8,128)(2,1)} %shard_map.89), calls=%async_computation.1 | async-start | bytes 1048576 | tf_op jit(solution)/shard_map/all_to_all | solution.py:458
  46.7 0.0 copy-done.5
  46.7 0.1 collective-permute-start.1
  46.8 0.4 collective-permute-start.2
  47.3 1.0 collective-permute-done.1.b1_hbm
  48.3 0.0 copy-start.7
  48.3 0.4 collective-permute-done.2.b3_hbm
  48.7 0.0 copy-start.8
  48.7 0.0 copy-done.6
  48.7 0.3 copy-done.7
  49.0 0.4 copy-done.8
  49.4 9.7 %shard_map.90 = (bf16[2,512,2048]{2,1,0:T(8,128)(2,1)}, bf16[4,2048,512]{2,1,0:T(8,128)(2,1)}) custom-call(bf16[2,128,512]{2,1,0:T(8,128)(2,1)} %shard_map.88.block_hbm.b0_hbm, bf16[2,128,512]{2,1,0:T(8,128)(2,1)} %copy-done.7, bf16[2,128,512]{2,1,0:T(8,128)(2,1)} %copy-done.6, bf16[2,128,512]{2,1,0:T(8,128)(2,1)} %copy-done.8, ...), custom_call_target="tpu_custom_call" | custom-call | flops 1610612736 | bytes 13651968 | tf_op jit(solution)/shard_map/pallas_call | solution.py:375
  59.1 3.7 %all-to-all-done.1.summed = bf16[32,32,256]{2,1,0:T(8,128)(2,1)S(1)} async-done(((bf16[32,32,256]{2,1,0:T(8,128)(2,1)}), bf16[32,32,256]{2,1,0:T(8,128)(2,1)S(1)}, u32[]{:S(2)}, u32[]{:S(2)}) %all-to-all-start.1) | async-done | bytes 524320 | tf_op jit(solution)/shard_map/all_to_all | solution.py:458
  62.9 0.0 copy-start.4
  62.9 0.8 copy-done.4
  63.7 0.0 copy-start
  63.7 8.3 %shard_map.91 = bf16[32,32,384]{2,1,0:T(8,128)(2,1)} custom-call(bf16[32,32,256]{2,1,0:T(8,128)(2,1)} %copy-done.4, bf16[2,512,2048]{2,1,0:T(8,128)(2,1)} %get-tuple-element.19.factor_hbm, bf16[2,512,512]{2,1,0:T(8,128)(2,1)} %core_hbm.1, bf16[4,2048,512]{2,1,0:T(8,128)(2,1)} %get-tuple-element.20.cross_hbm, s32[8,128]{1,0:T(8,128)} %get-tuple-element.12.starts_hbm), custom_call_target="tpu_custom_call" | custom-call | bytes 14946304 | tf_op jit(solution)/shard_map/pallas_call | solution.py:375
  71.9 24.6 %all_to_all.15.got = bf16[32,32,384]{2,1,0:T(8,128)(2,1)S(1)} all-to-all(bf16[32,32,384]{2,1,0:T(8,128)(2,1)} %shard_map.91), channel_id=1, replica_groups=mesh['rows'=4,'pts'=8] {'rows','pts'}, dimensions={0} | all-to-all | bytes 1572864 | tf_op jit(solution)/shard_map/all_to_all | solution.py:491
  96.5 0.0 copy-done
  96.5 0.0 copy-start.1
  96.6 1.2 %copy-done.1 = f32[1024,256]{1,0:T(8,128)S(1)} copy-done((f32[1024,256]{1,0:T(8,128)S(1)}, f32[1024,256]{1,0:T(8,128)}, u32[]{:S(2)}) %copy-start.1) | copy-done | bytes 1048600
  97.8 0.0 copy-start.2
  97.8 1.9 %copy-done.2 = bf16[2,768,1024]{2,1,0:T(8,128)(2,1)S(1)} copy-done((bf16[2,768,1024]{2,1,0:T(8,128)(2,1)S(1)}, bf16[2,768,1024]{2,1,0:T(8,128)(2,1)}, u32[]{:S(2)}) %copy-start.2) | copy-done | bytes 3145752
  99.7 3.8 %shard_map.92 = (f32[1024,256]{1,0:T(8,128)}, f32[1024,256]{1,0:T(8,128)}) custom-call(bf16[32,32,384]{2,1,0:T(8,128)(2,1)S(1)} %all_to_all.15.got, f32[1024,256]{1,0:T(8,128)S(1)} %copy-done, f32[1024,256]{1,0:T(8,128)S(1)} %copy-done.1, bf16[2,768,1024]{2,1,0:T(8,128)(2,1)S(1)} %copy-done.2), custom_call_target="tpu_custom_call" | custom-call | bytes 8126464 | tf_op jit(solution)/shard_map/pallas_call | solution.py:375
Async XLA Ops:
  3.2 27.5 %all-to-all-start = ((bf16[8,384,128]{2,1,0:T(8,128)(2,1)}), bf16[8,384,128]{2,1,0:T(8,128)(2,1)S(1)}, u32[]{:S(2)}, u32[]{:S(2)}) async-start(bf16[8,384,128]{2,1,0:T(8,128)(2,1)} %shard_map.86), calls=%async_computation | async-start | bytes 1572864 | tf_op jit(solution)/shard_map/all_to_all | solution.py:416
  30.7 0.9 copy-start.3
  34.4 12.3 %copy-start.5 = (bf16[2,128,512]{2,1,0:T(8,128)(2,1)S(1)}, bf16[2,128,512]{2,1,0:T(8,128)(2,1)}, u32[]{:S(2)}) copy-start(bf16[2,128,512]{2,1,0:T(8,128)(2,1)} %shard_map.88.block_hbm.b0_hbm) | copy-start | bytes 786436
  34.4 6.9 %collective-permute-start = (bf16[2,128,512]{2,1,0:T(8,128)(2,1)}, bf16[2,128,512]{2,1,0:T(8,128)(2,1)S(1)}, u32[]{:S(2)}, u32[]{:S(2)}) collective-permute-start(bf16[2,128,512]{2,1,0:T(8,128)(2,1)} %shard_map.88.block_hbm.b0_hbm), channel_id=1, source_target_pairs={{0,16},{8,24},{16,0},{24,8},{1,17},{9,25},{17,1},{25,9},{2,18},{10... | collective-permute-start | bytes 786440 | tf_op jit(solution)/shard_map/ppermute | solution.py:391
  41.3 7.3 %copy-start.6 = (bf16[2,128,512]{2,1,0:T(8,128)(2,1)}, bf16[2,128,512]{2,1,0:T(8,128)(2,1)S(1)}, u32[]{:S(2)}) copy-start(bf16[2,128,512]{2,1,0:T(8,128)(2,1)S(1)} %collective-permute-done.b2_hbm) | copy-start | bytes 786436
  41.3 21.5 %all-to-all-start.1 = ((bf16[32,32,256]{2,1,0:T(8,128)(2,1)}), bf16[32,32,256]{2,1,0:T(8,128)(2,1)S(1)}, u32[]{:S(2)}, u32[]{:S(2)}) async-start(bf16[32,32,256]{2,1,0:T(8,128)(2,1)} %shard_map.89), calls=%async_computation.1 | async-start | bytes 1048576 | tf_op jit(solution)/shard_map/all_to_all | solution.py:458
  46.7 1.6 %collective-permute-start.1 = (bf16[2,128,512]{2,1,0:T(8,128)(2,1)S(1)}, bf16[2,128,512]{2,1,0:T(8,128)(2,1)S(1)}, u32[]{:S(2)}, u32[]{:S(2)}) collective-permute-start(bf16[2,128,512]{2,1,0:T(8,128)(2,1)S(1)} %copy-done.5), channel_id=1, source_target_pairs={{0,8},{8,0},{16,24},{24,16},{1,9},{9,1},{17,25},{25,17},{2,10},{10... | collective-permute-start | bytes 786440 | tf_op jit(solution)/shard_map/ppermute | solution.py:391
  46.8 1.8 %collective-permute-start.2 = (bf16[2,128,512]{2,1,0:T(8,128)(2,1)S(1)}, bf16[2,128,512]{2,1,0:T(8,128)(2,1)S(1)}, u32[]{:S(2)}, u32[]{:S(2)}) collective-permute-start(bf16[2,128,512]{2,1,0:T(8,128)(2,1)S(1)} %collective-permute-done.b2_hbm), channel_id=1, source_target_pairs={{0,8},{8,0},{16,24},{24,16},{1,9},{9,1},{17,25},{25,17},{2,10},{10... | collective-permute-start | bytes 786440 | tf_op jit(solution)/shard_map/ppermute | solution.py:391
  48.3 0.7 copy-start.7
  48.7 0.7 copy-start.8
  62.9 0.8 copy-start.4
  63.7 32.9 %copy-start = (f32[1024,256]{1,0:T(8,128)S(1)}, f32[1024,256]{1,0:T(8,128)}, u32[]{:S(2)}) copy-start(f32[1024,256]{1,0:T(8,128)} %w_hbm.3) | copy-start | bytes 3145732
  96.5 1.2 %copy-start.1 = (f32[1024,256]{1,0:T(8,128)S(1)}, f32[1024,256]{1,0:T(8,128)}, u32[]{:S(2)}) copy-start(f32[1024,256]{1,0:T(8,128)} %z_hbm.3) | copy-start | bytes 3145732
  97.8 1.9 %copy-start.2 = (bf16[2,768,1024]{2,1,0:T(8,128)(2,1)S(1)}, bf16[2,768,1024]{2,1,0:T(8,128)(2,1)}, u32[]{:S(2)}) copy-start(bf16[2,768,1024]{2,1,0:T(8,128)(2,1)} %get-tuple-element.21.rows_hbm) | copy-start | bytes 9437188

commit v8 on v7

--- a/solution.py
+++ b/solution.py
@@ -92,9 +92,9 @@
     return blocks[u : u + 1, pl.ds(pl.multiple_of(group * count, count), count)]
 
 
-def pack_kernel(count, cap, blocks_hbm, feats_hbm, out_hbm, blocks, feats, packed, sems):
+def pack_kernel(count, cap, owners, blocks_hbm, feats_hbm, out_hbm, blocks, feats, packed, sems):
     row, me = lax.axis_index("rows"), lax.axis_index("pts")
-    points, owners = feats.shape[0], out_hbm.shape[0]
+    points = feats.shape[0]
     reads = start_all([(blocks_hbm, blocks), (feats_hbm, feats)], sems)
     before = before_matrix(count)
     reads[0].wait()
@@ -106,7 +106,7 @@
     reads[1].wait()
     for u in range(UPDATES):
         packed[u * cap : (u + 1) * cap, :] = mm(rows[u], feats[...], 1, 0).astype(bf16)
-    wait_all(start_all([(packed, out_hbm.at[o]) for o in range(owners)], sems))
+    wait_all(start_all([(packed, out_hbm)], sems))
 
 
 def two_digits(row):
@@ -193,17 +193,20 @@
 CHUNK = 256
 
 
-def compact_kernel(came, starts_hbm, block_hbm, starts, wide, block, sems):
-    row = lax.axis_index("rows")
+def compact_kernel(*refs):
+    *came_hbm, starts_hbm, block_hbm, came, starts, wide, block, sems = refs
+    row, me = lax.axis_index("rows"), lax.axis_index("pts")
     owners, deep, _ = came.shape
     cap = deep // UPDATES
     groups = starts.shape[0] // UPDATES
     count = block.shape[2]
-    wait_all(start_all([(starts_hbm, starts)], sems))
+    pairs = [(a, came.at[k]) for k, a in enumerate(came_hbm)]
+    wait_all(start_all([*pairs, (starts_hbm, starts)], sems))
     for u in range(UPDATES):
         for o in range(owners):
             start = starts[u * groups + row, o]
-            wide[u, pl.ds(start, cap), :] = came[o, u * cap : (u + 1) * cap, :].astype(f32)
+            rows = came[lax.bitwise_xor(me, o), u * cap : (u + 1) * cap, :]
+            wide[u, pl.ds(start, cap), :] = rows.astype(f32)
         block[u] = wide[u, 0:count, :].T.astype(bf16)
     wait_all(start_all([(block, block_hbm)], sems))
 
@@ -386,9 +389,8 @@
     )(*args)
 
 
-def swap_rows(value, k):
-    count = lax.axis_size("rows")
-    return lax.ppermute(value, "rows", [(i, i ^ k) for i in range(count)])
+def swap(value, axis, k):
+    return lax.ppermute(value, axis, [(i, i ^ k) for i in range(lax.axis_size(axis))])
 
 
 def with_kernels(features, targets, coefficients, momentum, block_index, pivot_index, core):
@@ -406,14 +408,14 @@
     wide = like(coefficients.shape, f32)
 
     (packed,) = call(
-        functools.partial(pack_kernel, count, cap),
-        [like((owners, UPDATES * cap, width))],
+        functools.partial(pack_kernel, count, cap, owners),
+        [like((UPDATES * cap, width))],
         [block_index, features, like((UPDATES * cap, width))],
         block_index,
         features,
-        sems=(owners,),
-    )
-    came = lax.all_to_all(packed, "pts", 0, 0, tiled=True)
+        sems=(2,),
+    )
+    came = {k: swap(packed, "pts", k) for k in reversed(range(1, owners))}
     kept = [
         like((UPDATES, outputs, points)),
         like((UPDATES, outputs, count), f32),
@@ -435,13 +437,19 @@
     (mine,) = call(
         compact_kernel,
         [feats],
-        [inside_starts, like((UPDATES, count + cap, width), f32), feats],
-        came,
+        [
+            like((owners, *packed.shape)),
+            inside_starts,
+            like((UPDATES, count + cap, width), f32),
+            feats,
+        ],
+        packed,
+        *[came[k] for k in range(1, owners)],
         starts,
-        near=1,
-        sems=(1,),
-    )
-    beside, across = swap_rows(mine, 1), swap_rows(mine, 2)
+        sems=(owners + 1,),
+        grant=40,
+    )
+    beside, across = swap(mine, "rows", 1), swap(mine, "rows", 2)
     pieces = like((devices, deep, count // 2))
     (pieces,) = call(
         sums_kernel,
@@ -470,7 +478,7 @@
         mine,
         beside,
         across,
-        swap_rows(across, 1),
+        swap(across, "rows", 1),
         ids,
         chosen,
         sems=(rows * rows + 1,),
@@ -500,7 +508,7 @@
         place,
         near=1,
         sems=(3 * parts, 2 * parts),
-        grant=40,
+        grant=48,
     )
 
 
@@ -568,7 +576,7 @@
 def shards(features, targets, coefficients, momentum, block_index, pivot_index, nystrom_core):
     rows, owners = lax.axis_size("rows"), lax.axis_size("pts")
     count = block_index.shape[1] // rows
-    fits = rows == 4 and coefficients.shape[1] == 8 * rows * owners
+    fits = rows == 4 and owners == 8 and coefficients.shape[1] == 8 * rows * owners
     fits = fits and coefficients.shape[0] % CHUNK == 0 and count % CHUNK == 0 and (3 * count // owners) % 64 == 0
     plan = with_kernels if fits else with_operations
     return plan(

time: 104 us -> 104 us (level)
  starting transfers between devices: 14.8 us -> 26.6 us
  waiting for transfers between devices: 18.2 us -> 6.46 us
  Pallas kernels: 39.7 us -> 38.5 us
    ppermute x3 -> x10, starting transfers between devices: 2.13 us -> 21.2 us  [swap(): lax.ppermute(value, axis, [(i, i ^ k) for i in range(lax.axis_size(axis))])]
    all_to_all x1 -> x0, waiting for transfers between devices: 11.2 us -> none  [with_kernels(): came = lax.all_to_all(packed, 'pts', 0, 0, tiled=True)]
    all_to_all x1 -> x0, starting transfers between devices: 7.29 us -> none  [with_kernels(): came = lax.all_to_all(packed, 'pts', 0, 0, tiled=True)]
    pallas_call x7, Pallas kernels: 39.7 us -> 38.5 us  [call(): pl.pallas_call(body, out_shape=outs, in_specs=[VMEM] * near + [HBM] * (le...]
    unnamed x18 -> x20, local copies, waits for them, and re-layouts: 5.51 us -> 6.18 us
    ppermute x3 -> x10, waiting for transfers between devices: 3.2 us -> 2.76 us  [swap(): lax.ppermute(value, axis, [(i, i ^ k) for i in range(lax.axis_size(axis))])]
  transfers between devices with their start and end apart: 5 -> 11, of which waited for: 5 -> 4; matrix products, arithmetic and copies ran while one was open for 0% -> 0% of each run, Pallas kernels for 21% -> 22%
where the time goes in v8:
time: 104 us; the launch traced here: 103 us
  Pallas kernels  38.5 us (37%)
  starting transfers between devices  26.6 us (26%)
  blocking collectives  24.6 us (24%)
  waiting for transfers between devices  6.46 us (6%)
  local copies, waits for them, and re-layouts  6.18 us (6%)
    pallas_call x7, Pallas kernels, call(): pl.pallas_call(body, out_shape=outs, in_specs=[VMEM] * near + [HBM] * (le...  38.5 us
    all_to_all x1, blocking collectives, with_kernels(): got = lax.all_to_all(steps, ('rows', 'pts'), 0, 0, tiled=True)  24.6 us
    ppermute x10, starting transfers between devices, swap(): lax.ppermute(value, axis, [(i, i ^ k) for i in range(lax.axis_size(axis))])  21.2 us
    unnamed x20, local copies, waits for them, and re-layouts  6.18 us
    all_to_all x1, starting transfers between devices, with_kernels(): summed = lax.all_to_all(pieces, ('rows', 'pts'), 0, 0, tiled=True)  5.31 us
    all_to_all x1, waiting for transfers between devices, with_kernels(): summed = lax.all_to_all(pieces, ('rows', 'pts'), 0, 0, tiled=True)  3.7 us
    ppermute x10, waiting for transfers between devices, swap(): lax.ppermute(value, axis, [(i, i ^ k) for i in range(lax.axis_size(axis))])  2.76 us
  transfers between devices with their start and end apart: 11, of which 4 were waited for; matrix products, arithmetic and copies ran while one was open for 0% of the time, Pallas kernels for 22%

profile of v8, /device:TPU:0, one launch (start us, length us, event | category | flops | bytes accessed | tf_op | source)
XLA Modules:
  0.0 103.3 jit_solution(696357404299404006)
XLA Ops:
  0.6 2.3 %shard_map.86.refs_0_ = bf16[384,128]{1,0:T(8,128)(2,1)} custom-call(s32[2,2048]{1,0:T(2,128)} %blocks_hbm.3, bf16[1024,128]{1,0:T(8,128)(2,1)} %feats_hbm.3), custom_call_target="tpu_custom_call" | custom-call | bytes 376832 | tf_op jit(solution)/shard_map/pallas_call | solution.py:378
  2.9 6.1 %collective-permute-start.6 = (bf16[384,128]{1,0:T(8,128)(2,1)}, bf16[384,128]{1,0:T(8,128)(2,1)S(1)}, u32[]{:S(2)}, u32[]{:S(2)}) collective-permute-start(bf16[384,128]{1,0:T(8,128)(2,1)} %shard_map.86.refs_0_), channel_id=1, source_target_pairs={{0,7},{1,6},{2,5},{3,4},{4,3},{5,2},{6,1},{7,0},{8,15},{9,14},{10,... | collective-permute-start | bytes 294920 | tf_op jit(solution)/shard_map/ppermute | solution.py:393
  9.0 0.2 collective-permute-start.5
  9.2 0.7 collective-permute-start.4
  9.9 2.0 %collective-permute-start.3 = (bf16[384,128]{1,0:T(8,128)(2,1)}, bf16[384,128]{1,0:T(8,128)(2,1)S(1)}, u32[]{:S(2)}, u32[]{:S(2)}) collective-permute-start(bf16[384,128]{1,0:T(8,128)(2,1)} %shard_map.86.refs_0_), channel_id=1, source_target_pairs={{0,4},{1,5},{2,6},{3,7},{4,0},{5,1},{6,2},{7,3},{8,12},{9,13},{10,... | collective-permute-start | bytes 294920 | tf_op jit(solution)/shard_map/ppermute | solution.py:393
  12.0 2.3 %collective-permute-start.2 = (bf16[384,128]{1,0:T(8,128)(2,1)}, bf16[384,128]{1,0:T(8,128)(2,1)S(1)}, u32[]{:S(2)}, u32[]{:S(2)}) collective-permute-start(bf16[384,128]{1,0:T(8,128)(2,1)} %shard_map.86.refs_0_), channel_id=1, source_target_pairs={{0,3},{1,2},{2,1},{3,0},{4,7},{5,6},{6,5},{7,4},{8,11},{9,10},{10,... | collective-permute-start | bytes 294920 | tf_op jit(solution)/shard_map/ppermute | solution.py:393
  14.3 0.0 collective-permute-done.6.refs_7_
  14.3 6.8 %collective-permute-start.1 = (bf16[384,128]{1,0:T(8,128)(2,1)}, bf16[384,128]{1,0:T(8,128)(2,1)S(1)}, u32[]{:S(2)}, u32[]{:S(2)}) collective-permute-start(bf16[384,128]{1,0:T(8,128)(2,1)} %shard_map.86.refs_0_), channel_id=1, source_target_pairs={{0,2},{1,3},{2,0},{3,1},{4,6},{5,7},{6,4},{7,5},{8,10},{9,11},{10,... | collective-permute-start | bytes 294920 | tf_op jit(solution)/shard_map/ppermute | solution.py:393
  21.1 0.0 collective-permute-done.5.refs_6_
  21.1 1.0 collective-permute-start
  22.0 8.9 %shard_map.87 = (bf16[2,256,1024]{2,1,0:T(8,128)(2,1)}, f32[2,256,512]{2,1,0:T(8,128)}, bf16[2,768,1024]{2,1,0:T(8,128)(2,1)}, s32[8,512]{1,0:T(8,128)}, s32[8,128]{1,0:T(8,128)}, /*index=5*/s32[2,512]{1,0:T(2,128)}) custom-call(s32[2,2048]{1,0:T(2,128)} %blocks_hbm.3, s32[2,512]{1,0:T(2,128)} %pivots_hbm.1, f32[1024,256]{1,0:T(8,128)} %w_hbm.3, ...), custom_call_target="tpu_custom_call" | custom-call | bytes 7909376 | tf_op jit(solution)/shard_map/pallas_call | solution.py:378
  30.9 0.0 collective-permute-done.4.refs_5_
  30.9 0.0 collective-permute-done.3.refs_4_
  31.0 0.0 collective-permute-done.2.refs_3_
  31.0 0.0 collective-permute-done.1.refs_2_
  31.0 0.0 collective-permute-done.refs_1_
  31.0 0.0 copy-start.3
  31.0 0.9 copy-done.3
  31.9 0.0 copy-start.5
  31.9 0.7 copy-done.5
  32.6 1.9 %shard_map.88.block_hbm.b0_hbm = bf16[2,128,512]{2,1,0:T(8,128)(2,1)S(1)} custom-call(bf16[384,128]{1,0:T(8,128)(2,1)S(1)} %copy-done.3, bf16[384,128]{1,0:T(8,128)(2,1)S(1)} %collective-permute-done.refs_1_, bf16[384,128]{1,0:T(8,128)(2,1)S(1)} %collective-permute-done.1.refs_2_, bf16[384,128]{1,0:T(8,128)(2,1)S(1)} %collective-permute-done.2.refs_3_, ...), custom_call_target="tpu_custom_call" | custom-call | bytes 1052672 | tf_op jit(solution)/shard_map/pallas_call | solution.py:378
  34.5 0.0 copy-start.4
  34.5 1.6 %collective-permute-start.7 = (bf16[2,128,512]{2,1,0:T(8,128)(2,1)S(1)}, bf16[2,128,512]{2,1,0:T(8,128)(2,1)S(1)}, u32[]{:S(2)}, u32[]{:S(2)}) collective-permute-start(bf16[2,128,512]{2,1,0:T(8,128)(2,1)S(1)} %shard_map.88.block_hbm.b0_hbm), channel_id=1, source_target_pairs={{0,16},{8,24},{16,0},{24,8},{1,17},{9,25},{17,1},{25,9},{2,18},{10... | collective-permute-start | bytes 786440 | tf_op jit(solution)/shard_map/ppermute | solution.py:393
  36.1 0.0 copy-done.4
  36.1 3.5 %shard_map.89 = bf16[32,32,256]{2,1,0:T(8,128)(2,1)} custom-call(bf16[2,128,512]{2,1,0:T(8,128)(2,1)} %copy-done.4, bf16[1024,128]{1,0:T(8,128)(2,1)} %feats_hbm.3, bf16[2,256,1024]{2,1,0:T(8,128)(2,1)} %get-tuple-element.13.coef_hbm, f32[2,256,512]{2,1,0:T(8,128)} %get-tuple-element.14.offset_hbm), custom_call_target="tpu_custom_call" | custom-call | flops 1073741824 | bytes 3145728 | tf_op jit(solution)/shard_map/pallas_call | solution.py:378
  39.6 1.3 %collective-permute-done.7.b2_hbm = bf16[2,128,512]{2,1,0:T(8,128)(2,1)S(1)} collective-permute-done((bf16[2,128,512]{2,1,0:T(8,128)(2,1)S(1)}, bf16[2,128,512]{2,1,0:T(8,128)(2,1)S(1)}, u32[]{:S(2)}, u32[]{:S(2)}) %collective-permute-start.7) | collective-permute-done | bytes 262176 | tf_op jit(solution)/shard_map/ppermute | solution.py:393
  41.0 0.0 copy-start.7
  41.0 5.3 %all-to-all-start = ((bf16[32,32,256]{2,1,0:T(8,128)(2,1)}), bf16[32,32,256]{2,1,0:T(8,128)(2,1)S(1)}, u32[]{:S(2)}, u32[]{:S(2)}) async-start(bf16[32,32,256]{2,1,0:T(8,128)(2,1)} %shard_map.89), calls=%async_computation | async-start | bytes 1048576 | tf_op jit(solution)/shard_map/all_to_all | solution.py:466
  46.3 0.1 collective-permute-start.8
  46.4 0.4 collective-permute-start.9
  46.9 1.2 %collective-permute-done.8.b1_hbm = bf16[2,128,512]{2,1,0:T(8,128)(2,1)S(1)} collective-permute-done((bf16[2,128,512]{2,1,0:T(8,128)(2,1)}, bf16[2,128,512]{2,1,0:T(8,128)(2,1)S(1)}, u32[]{:S(2)}, u32[]{:S(2)}) %collective-permute-start.8) | collective-permute-done | bytes 262176 | tf_op jit(solution)/shard_map/ppermute | solution.py:393
  48.1 0.0 copy-start.8
  48.1 0.2 collective-permute-done.9.b3_hbm
  48.3 0.0 copy-start.9
  48.3 0.0 copy-done.7
  48.3 0.5 copy-done.8
  48.8 0.2 copy-done.9
  49.0 9.8 %shard_map.90 = (bf16[2,512,2048]{2,1,0:T(8,128)(2,1)}, bf16[4,2048,512]{2,1,0:T(8,128)(2,1)}) custom-call(bf16[2,128,512]{2,1,0:T(8,128)(2,1)} %copy-done.4, bf16[2,128,512]{2,1,0:T(8,128)(2,1)} %copy-done.8, bf16[2,128,512]{2,1,0:T(8,128)(2,1)} %copy-done.7, bf16[2,128,512]{2,1,0:T(8,128)(2,1)} %copy-done.9, s32[8,512]{1,0:T(8,128)} %get-tuple-element.17.ids_hbm, ...), custom_call_target="tpu_custom_call" | custom-call | flops 1610612736 | bytes 13651968 | tf_op jit(solution)/shard_map/pallas_call | solution.py:378
  58.8 3.7 %all-to-all-done.summed = bf16[32,32,256]{2,1,0:T(8,128)(2,1)S(1)} async-done(((bf16[32,32,256]{2,1,0:T(8,128)(2,1)}), bf16[32,32,256]{2,1,0:T(8,128)(2,1)S(1)}, u32[]{:S(2)}, u32[]{:S(2)}) %all-to-all-start) | async-done | bytes 524320 | tf_op jit(solution)/shard_map/all_to_all | solution.py:466
  62.5 0.0 copy-start.6
  62.5 0.8 copy-done.6
  63.3 0.0 copy-start
  63.3 8.3 %shard_map.91 = bf16[32,32,384]{2,1,0:T(8,128)(2,1)} custom-call(bf16[32,32,256]{2,1,0:T(8,128)(2,1)} %copy-done.6, bf16[2,512,2048]{2,1,0:T(8,128)(2,1)} %get-tuple-element.19.factor_hbm, bf16[2,512,512]{2,1,0:T(8,128)(2,1)} %core_hbm.1, bf16[4,2048,512]{2,1,0:T(8,128)(2,1)} %get-tuple-element.20.cross_hbm, s32[8,128]{1,0:T(8,128)} %get-tuple-element.12.refs_8_.starts_hbm), custom_call_target="tpu_custom_call" | custom-call | bytes 14946304 | tf_op jit(solution)/shard_map/pallas_call | solution.py:378
  71.5 24.6 %all_to_all.10.got = bf16[32,32,384]{2,1,0:T(8,128)(2,1)S(1)} all-to-all(bf16[32,32,384]{2,1,0:T(8,128)(2,1)} %shard_map.91), channel_id=1, replica_groups=mesh['rows'=4,'pts'=8] {'rows','pts'}, dimensions={0} | all-to-all | bytes 1572864 | tf_op jit(solution)/shard_map/all_to_all | solution.py:499
  96.1 0.0 copy-done
  96.2 0.0 copy-start.1
  96.2 1.2 %copy-done.1 = f32[1024,256]{1,0:T(8,128)S(1)} copy-done((f32[1024,256]{1,0:T(8,128)S(1)}, f32[1024,256]{1,0:T(8,128)}, u32[]{:S(2)}) %copy-start.1) | copy-done | bytes 1048600
  97.4 0.0 copy-start.2
  97.4 1.9 %copy-done.2 = bf16[2,768,1024]{2,1,0:T(8,128)(2,1)S(1)} copy-done((bf16[2,768,1024]{2,1,0:T(8,128)(2,1)S(1)}, bf16[2,768,1024]{2,1,0:T(8,128)(2,1)}, u32[]{:S(2)}) %copy-start.2) | copy-done | bytes 3145752
  99.3 3.8 %shard_map.92 = (f32[1024,256]{1,0:T(8,128)}, f32[1024,256]{1,0:T(8,128)}) custom-call(bf16[32,32,384]{2,1,0:T(8,128)(2,1)S(1)} %all_to_all.10.got, f32[1024,256]{1,0:T(8,128)S(1)} %copy-done, f32[1024,256]{1,0:T(8,128)S(1)} %copy-done.1, bf16[2,768,1024]{2,1,0:T(8,128)(2,1)S(1)} %copy-done.2), custom_call_target="tpu_custom_call" | custom-call | bytes 8126464 | tf_op jit(solution)/shard_map/pallas_call | solution.py:378
Async XLA Ops:
  2.9 11.4 %collective-permute-start.6 = (bf16[384,128]{1,0:T(8,128)(2,1)}, bf16[384,128]{1,0:T(8,128)(2,1)S(1)}, u32[]{:S(2)}, u32[]{:S(2)}) collective-permute-start(bf16[384,128]{1,0:T(8,128)(2,1)} %shard_map.86.refs_0_), channel_id=1, source_target_pairs={{0,7},{1,6},{2,5},{3,4},{4,3},{5,2},{6,1},{7,0},{8,15},{9,14},{10,... | collective-permute-start | bytes 294920 | tf_op jit(solution)/shard_map/ppermute | solution.py:393
  9.0 12.1 %collective-permute-start.5 = (bf16[384,128]{1,0:T(8,128)(2,1)}, bf16[384,128]{1,0:T(8,128)(2,1)S(1)}, u32[]{:S(2)}, u32[]{:S(2)}) collective-permute-start(bf16[384,128]{1,0:T(8,128)(2,1)} %shard_map.86.refs_0_), channel_id=1, source_target_pairs={{0,6},{1,7},{2,4},{3,5},{4,2},{5,3},{6,0},{7,1},{8,14},{9,15},{10,... | collective-permute-start | bytes 294920 | tf_op jit(solution)/shard_map/ppermute | solution.py:393
  9.2 21.7 %collective-permute-start.4 = (bf16[384,128]{1,0:T(8,128)(2,1)}, bf16[384,128]{1,0:T(8,128)(2,1)S(1)}, u32[]{:S(2)}, u32[]{:S(2)}) collective-permute-start(bf16[384,128]{1,0:T(8,128)(2,1)} %shard_map.86.refs_0_), channel_id=1, source_target_pairs={{0,5},{1,4},{2,7},{3,6},{4,1},{5,0},{6,3},{7,2},{8,13},{9,12},{10,... | collective-permute-start | bytes 294920 | tf_op jit(solution)/shard_map/ppermute | solution.py:393
  9.9 21.0 %collective-permute-start.3 = (bf16[384,128]{1,0:T(8,128)(2,1)}, bf16[384,128]{1,0:T(8,128)(2,1)S(1)}, u32[]{:S(2)}, u32[]{:S(2)}) collective-permute-start(bf16[384,128]{1,0:T(8,128)(2,1)} %shard_map.86.refs_0_), channel_id=1, source_target_pairs={{0,4},{1,5},{2,6},{3,7},{4,0},{5,1},{6,2},{7,3},{8,12},{9,13},{10,... | collective-permute-start | bytes 294920 | tf_op jit(solution)/shard_map/ppermute | solution.py:393
  12.0 19.0 %collective-permute-start.2 = (bf16[384,128]{1,0:T(8,128)(2,1)}, bf16[384,128]{1,0:T(8,128)(2,1)S(1)}, u32[]{:S(2)}, u32[]{:S(2)}) collective-permute-start(bf16[384,128]{1,0:T(8,128)(2,1)} %shard_map.86.refs_0_), channel_id=1, source_target_pairs={{0,3},{1,2},{2,1},{3,0},{4,7},{5,6},{6,5},{7,4},{8,11},{9,10},{10,... | collective-permute-start | bytes 294920 | tf_op jit(solution)/shard_map/ppermute | solution.py:393
  14.3 16.7 %collective-permute-start.1 = (bf16[384,128]{1,0:T(8,128)(2,1)}, bf16[384,128]{1,0:T(8,128)(2,1)S(1)}, u32[]{:S(2)}, u32[]{:S(2)}) collective-permute-start(bf16[384,128]{1,0:T(8,128)(2,1)} %shard_map.86.refs_0_), channel_id=1, source_target_pairs={{0,2},{1,3},{2,0},{3,1},{4,6},{5,7},{6,4},{7,5},{8,10},{9,11},{10,... | collective-permute-start | bytes 294920 | tf_op jit(solution)/shard_map/ppermute | solution.py:393
  21.1 9.9 %collective-permute-start = (bf16[384,128]{1,0:T(8,128)(2,1)}, bf16[384,128]{1,0:T(8,128)(2,1)S(1)}, u32[]{:S(2)}, u32[]{:S(2)}) collective-permute-start(bf16[384,128]{1,0:T(8,128)(2,1)} %shard_map.86.refs_0_), channel_id=1, source_target_pairs={{0,1},{1,0},{2,3},{3,2},{4,5},{5,4},{6,7},{7,6},{8,9},{9,8},{10,11... | collective-permute-start | bytes 294920 | tf_op jit(solution)/shard_map/ppermute | solution.py:393
  31.0 0.9 copy-start.3
  31.9 0.7 copy-start.5
  34.5 1.6 %copy-start.4 = (bf16[2,128,512]{2,1,0:T(8,128)(2,1)}, bf16[2,128,512]{2,1,0:T(8,128)(2,1)S(1)}, u32[]{:S(2)}) copy-start(bf16[2,128,512]{2,1,0:T(8,128)(2,1)S(1)} %shard_map.88.block_hbm.b0_hbm) | copy-start | bytes 786436
  34.5 6.4 %collective-permute-start.7 = (bf16[2,128,512]{2,1,0:T(8,128)(2,1)S(1)}, bf16[2,128,512]{2,1,0:T(8,128)(2,1)S(1)}, u32[]{:S(2)}, u32[]{:S(2)}) collective-permute-start(bf16[2,128,512]{2,1,0:T(8,128)(2,1)S(1)} %shard_map.88.block_hbm.b0_hbm), channel_id=1, source_target_pairs={{0,16},{8,24},{16,0},{24,8},{1,17},{9,25},{17,1},{25,9},{2,18},{10... | collective-permute-start | bytes 786440 | tf_op jit(solution)/shard_map/ppermute | solution.py:393
  41.0 7.3 %copy-start.7 = (bf16[2,128,512]{2,1,0:T(8,128)(2,1)}, bf16[2,128,512]{2,1,0:T(8,128)(2,1)S(1)}, u32[]{:S(2)}) copy-start(bf16[2,128,512]{2,1,0:T(8,128)(2,1)S(1)} %collective-permute-done.7.b2_hbm) | copy-start | bytes 786436
  41.0 21.5 %all-to-all-start = ((bf16[32,32,256]{2,1,0:T(8,128)(2,1)}), bf16[32,32,256]{2,1,0:T(8,128)(2,1)S(1)}, u32[]{:S(2)}, u32[]{:S(2)}) async-start(bf16[32,32,256]{2,1,0:T(8,128)(2,1)} %shard_map.89), calls=%async_computation | async-start | bytes 1048576 | tf_op jit(solution)/shard_map/all_to_all | solution.py:466
  46.3 1.8 %collective-permute-start.8 = (bf16[2,128,512]{2,1,0:T(8,128)(2,1)}, bf16[2,128,512]{2,1,0:T(8,128)(2,1)S(1)}, u32[]{:S(2)}, u32[]{:S(2)}) collective-permute-start(bf16[2,128,512]{2,1,0:T(8,128)(2,1)} %copy-done.4), channel_id=1, source_target_pairs={{0,8},{8,0},{16,24},{24,16},{1,9},{9,1},{17,25},{25,17},{2,10},{10... | collective-permute-start | bytes 786440 | tf_op jit(solution)/shard_map/ppermute | solution.py:393
  46.4 1.8 %collective-permute-start.9 = (bf16[2,128,512]{2,1,0:T(8,128)(2,1)S(1)}, bf16[2,128,512]{2,1,0:T(8,128)(2,1)S(1)}, u32[]{:S(2)}, u32[]{:S(2)}) collective-permute-start(bf16[2,128,512]{2,1,0:T(8,128)(2,1)S(1)} %collective-permute-done.7.b2_hbm), channel_id=1, source_target_pairs={{0,8},{8,0},{16,24},{24,16},{1,9},{9,1},{17,25},{25,17},{2,10},{10... | collective-permute-start | bytes 786440 | tf_op jit(solution)/shard_map/ppermute | solution.py:393
  48.1 0.7 copy-start.8
  48.3 0.7 copy-start.9
  62.5 0.8 copy-start.6
  63.3 32.9 %copy-start = (f32[1024,256]{1,0:T(8,128)S(1)}, f32[1024,256]{1,0:T(8,128)}, u32[]{:S(2)}) copy-start(f32[1024,256]{1,0:T(8,128)} %w_hbm.3) | copy-start | bytes 3145732
  96.2 1.2 %copy-start.1 = (f32[1024,256]{1,0:T(8,128)S(1)}, f32[1024,256]{1,0:T(8,128)}, u32[]{:S(2)}) copy-start(f32[1024,256]{1,0:T(8,128)} %z_hbm.3) | copy-start | bytes 3145732
  97.4 1.9 %copy-start.2 = (bf16[2,768,1024]{2,1,0:T(8,128)(2,1)S(1)}, bf16[2,768,1024]{2,1,0:T(8,128)(2,1)}, u32[]{:S(2)}) copy-start(bf16[2,768,1024]{2,1,0:T(8,128)(2,1)} %get-tuple-element.21.rows_hbm) | copy-start | bytes 9437188

commit v9 on v8

--- a/solution.py
+++ b/solution.py
@@ -124,7 +124,7 @@
     count, cap, owners,
     blocks_hbm, pivots_hbm, w_hbm, z_hbm, t_hbm,
     coef_hbm, offset_hbm, rows_hbm, ids_hbm, starts_hbm, chosen_hbm,
-    blocks, pivots, w, z, t, coef, offset, rows, ids, starts, chosen, sems,
+    blocks, pivots, w, z, t, coef, offset, rows, ids, starts, chosen, sems, out_sems,
 ):
     row, me = lax.axis_index("rows"), lax.axis_index("pts")
     points, outputs = w.shape
@@ -157,6 +157,8 @@
             at_pivot = one_hot(iota((count, pivot.shape[1]), 0) + g * count == pivot)
             found += mm(two_digits(place + g * count), at_pivot, 1, 0)
         chosen[u : u + 1, :] = from_digits(found)
+    pairs = [(starts, starts_hbm), (ids, ids_hbm), (chosen, chosen_hbm), (rows, rows_hbm)]
+    writes = start_all(pairs, out_sems)
     wait_all(reads[2:])
     current, moving = w[...], z[...]
     goal = t[...].astype(f32).T
@@ -168,8 +170,10 @@
         place = one_hot(iota((points, count), 0) == local)
         offset[u] = mm(high, place, 1, 0) + mm(low, place, 1, 0)
         current, moving = stepped(current, moving, None)
-    pairs = [(coef, coef_hbm), (offset, offset_hbm), (rows, rows_hbm), (ids, ids_hbm)]
-    wait_all(start_all([*pairs, (starts, starts_hbm), (chosen, chosen_hbm)], sems))
+        for a, b in ((coef, coef_hbm), (offset, offset_hbm)):
+            writes.append(pltpu.make_async_copy(a.at[u], b.at[u], out_sems.at[len(writes)]))
+            writes[-1].start()
+    wait_all(writes)
 
 
 def extended(rows, axis, first):
@@ -283,18 +287,20 @@
 
 def chain_kernel(
     cap, owners,
-    summed, factor_hbm, core_hbm, cross_hbm, starts_hbm, out_hbm,
-    factor, core, cross, starts, packed, sems,
+    summed_hbm, factor_hbm, core_hbm, cross_hbm, starts_hbm, out_hbm,
+    summed, factor, core, cross, starts, packed, sems,
 ):
     groups, _, count = cross.shape
     own = summed.shape[1] // (2 * UPDATES)
-    pairs = []
+    pairs = [(summed_hbm, summed)]
     for u in range(UPDATES):
         pairs += [(factor_hbm.at[u], factor.at[u]), (core_hbm.at[u], core.at[u])]
         if u == 0:
             pairs += [(starts_hbm, starts)]
             pairs += [(cross_hbm.at[g], cross.at[g]) for g in range(groups)]
     reads = start_all(pairs, sems)
+    first, *reads = reads
+    first.wait()
     step = None
     for u in range(UPDATES):
         sums = []
@@ -322,25 +328,30 @@
             packed[o, 2 * own * u : 2 * own * (u + 1), :] = jnp.concatenate(
                 [jnp.concatenate(lanes[h * half : (h + 1) * half], axis=1) for h in range(2)], axis=0
             ).astype(bf16)
-    copies = out_hbm.shape[0] // owners
-    wait_all(
-        start_all([(packed, out_hbm.at[pl.ds(n * owners, owners)]) for n in range(copies)], sems)
-    )
+    wait_all(start_all([(packed, out_hbm)], sems))
 
 
 def finish_kernel(
-    got, w_hbm, z_hbm, rows_hbm, w_out, z_out, w, z, rows, steps, w_new, z_new, sems, out_sems
+    g0_hbm, g1_hbm, g2_hbm, g3_hbm, w_hbm, z_hbm, rows_hbm, w_out, z_out,
+    got, w, z, rows, steps, w_new, z_new, sems, out_sems,
 ):
+    row = lax.axis_index("rows")
     points = w.shape[0]
     sources, deep, lanes = got.shape
     own = deep // (2 * UPDATES)
     chunks = range(0, points, CHUNK)
     pairs = []
+    for k, g_hbm in enumerate((g0_hbm, g1_hbm, g2_hbm, g3_hbm)):
+        size = g_hbm.shape[0]
+        first = pl.multiple_of(lax.bitwise_xor(row, k) * size, size)
+        pairs.append((g_hbm, got.at[pl.ds(first, size)]))
     for c in chunks:
         part = slice(c, c + CHUNK)
         pairs += [(rows_hbm.at[:, :, part], rows.at[:, :, part])]
         pairs += [(w_hbm.at[part], w.at[part]), (z_hbm.at[part], z.at[part])]
     reads = start_all(pairs, sems)
+    wait_all(reads[:4])
+    reads = reads[4:]
     wide = got[...].astype(f32)
     for u in range(UPDATES):
         for h in range(2):
@@ -415,7 +426,7 @@
         features,
         sems=(2,),
     )
-    came = {k: swap(packed, "pts", k) for k in reversed(range(1, owners))}
+    came = {k: swap(packed, "pts", k) for k in reversed(range(owners // 2, owners))}
     kept = [
         like((UPDATES, outputs, points)),
         like((UPDATES, outputs, count), f32),
@@ -430,8 +441,10 @@
         kept,
         given + kept,
         *given,
-        sems=(6,),
-    )
+        sems=(5, 4 + 2 * UPDATES),
+    )
+    again, starts = lax.optimization_barrier((packed, starts))
+    came.update({k: swap(again, "pts", k) for k in reversed(range(1, owners // 2))})
     feats = like((UPDATES, width, count))
     inside_starts = pltpu.SMEM(starts.shape, i32)
     (mine,) = call(
@@ -447,7 +460,6 @@
         *[came[k] for k in range(1, owners)],
         starts,
         sems=(owners + 1,),
-        grant=40,
     )
     beside, across = swap(mine, "rows", 1), swap(mine, "rows", 2)
     pieces = like((devices, deep, count // 2))
@@ -484,31 +496,41 @@
         sems=(rows * rows + 1,),
         flops=2.0 * width * block * (UPDATES * rank + block),
     )
+    pieces = like((owners, deep, half * cap))
     (steps,) = call(
         functools.partial(chain_kernel, cap, owners),
-        [like((devices, deep, half * cap))],
-        [factor, core, cross, inside_starts, like((owners, deep, half * cap))],
+        [pieces],
+        [summed, factor, core, cross, inside_starts, pieces],
         summed,
         factor,
         core,
         cross,
         starts,
-        near=1,
-        sems=(2 * UPDATES + 1 + rows,),
-    )
-    got = lax.all_to_all(steps, ("rows", "pts"), 0, 0, tiled=True)
+        sems=(2 * UPDATES + 2 + rows,),
+    )
+    got = lax.all_to_all(steps, "pts", 0, 0, tiled=True)
+    beside, across = swap(got, "rows", 1), swap(got, "rows", 2)
     parts = points // CHUNK
     return call(
         finish_kernel,
         [wide] * 2,
-        [wide, wide, place, like((UPDATES, outputs, rows * cap)), wide, wide],
+        [
+            like((devices, deep, half * cap)),
+            wide,
+            wide,
+            place,
+            like((UPDATES, outputs, rows * cap)),
+            wide,
+            wide,
+        ],
         got,
+        beside,
+        across,
+        swap(across, "rows", 1),
         coefficients,
         momentum,
         place,
-        near=1,
-        sems=(3 * parts, 2 * parts),
-        grant=48,
+        sems=(rows + 3 * parts, 2 * parts),
     )
 
 

time: 104 us -> 95 us (0.913)
  waiting for transfers between devices: 6.46 us -> 21.1 us
  blocking collectives: 24.6 us -> 11.4 us
  starting transfers between devices: 26.6 us -> 19.9 us
  local copies, waits for them, and re-layouts: 6.18 us -> 3.44 us
    ppermute x10 -> x13, waiting for transfers between devices: 2.76 us -> 17.4 us  [swap(): lax.ppermute(value, axis, [(i, i ^ k) for i in range(lax.axis_size(axis))])]
    all_to_all x1, blocking collectives: 24.6 us -> 11.4 us  [with_kernels(): got = lax.all_to_all(steps, 'pts', 0, 0, tiled=True)]
    ppermute x10 -> x13, starting transfers between devices: 21.2 us -> 16 us  [swap(): lax.ppermute(value, axis, [(i, i ^ k) for i in range(lax.axis_size(axis))])]
    unnamed x20 -> x32, local copies, waits for them, and re-layouts: 6.18 us -> 3.44 us
    all_to_all x1, starting transfers between devices: 5.31 us -> 3.99 us  [with_kernels(): summed = lax.all_to_all(pieces, ('rows', 'pts'), 0, 0, tiled=True)]
  transfers between devices with their start and end apart: 11 -> 14, of which waited for: 4 -> 10; matrix products, arithmetic and copies ran while one was open for 0% -> 0% of each run, Pallas kernels for 22% -> 22%
where the time goes in v9:
time: 95 us; the launch traced here: 94.4 us
  Pallas kernels  37.7 us (40%)
  waiting for transfers between devices  21.1 us (22%)
  starting transfers between devices  19.9 us (21%)
  blocking collectives  11.4 us (12%)
  local copies, waits for them, and re-layouts  3.44 us (4%)
    pallas_call x7, Pallas kernels, call(): pl.pallas_call(body, out_shape=outs, in_specs=[VMEM] * near + [HBM] * (le...  37.7 us
    ppermute x13, waiting for transfers between devices, swap(): lax.ppermute(value, axis, [(i, i ^ k) for i in range(lax.axis_size(axis))])  17.4 us
    ppermute x13, starting transfers between devices, swap(): lax.ppermute(value, axis, [(i, i ^ k) for i in range(lax.axis_size(axis))])  16 us
    all_to_all x1, blocking collectives, with_kernels(): got = lax.all_to_all(steps, 'pts', 0, 0, tiled=True)  11.4 us
    all_to_all x1, starting transfers between devices, with_kernels(): summed = lax.all_to_all(pieces, ('rows', 'pts'), 0, 0, tiled=True)  3.99 us
    all_to_all x1, waiting for transfers between devices, with_kernels(): summed = lax.all_to_all(pieces, ('rows', 'pts'), 0, 0, tiled=True)  3.64 us
    unnamed x32, local copies, waits for them, and re-layouts  3.44 us
  transfers between devices with their start and end apart: 14, of which 10 were waited for; matrix products, arithmetic and copies ran while one was open for 0% of the time, Pallas kernels for 22%

profile of v9, /device:TPU:0, one launch (start us, length us, event | category | flops | bytes accessed | tf_op | source)
XLA Modules:
  0.0 94.4 jit_solution(5015351539394227797)
XLA Ops:
  0.6 2.3 %shard_map.86.refs_0_ = bf16[384,128]{1,0:T(8,128)(2,1)} custom-call(s32[2,2048]{1,0:T(2,128)} %blocks_hbm.3, bf16[1024,128]{1,0:T(8,128)(2,1)} %feats_hbm.3), custom_call_target="tpu_custom_call" | custom-call | bytes 376832 | tf_op jit(solution)/shard_map/pallas_call | solution.py:389
  2.9 6.1 %collective-permute-start.6 = (bf16[384,128]{1,0:T(8,128)(2,1)}, bf16[384,128]{1,0:T(8,128)(2,1)S(1)}, u32[]{:S(2)}, u32[]{:S(2)}) collective-permute-start(bf16[384,128]{1,0:T(8,128)(2,1)} %shard_map.86.refs_0_), channel_id=1, source_target_pairs={{0,7},{1,6},{2,5},{3,4},{4,3},{5,2},{6,1},{7,0},{8,15},{9,14},{10,... | collective-permute-start | bytes 294920 | tf_op jit(solution)/shard_map/ppermute | solution.py:404
  9.0 0.2 collective-permute-start.5
  9.2 0.7 collective-permute-start.4
  9.9 2.0 %collective-permute-start.3 = (bf16[384,128]{1,0:T(8,128)(2,1)}, bf16[384,128]{1,0:T(8,128)(2,1)S(1)}, u32[]{:S(2)}, u32[]{:S(2)}) collective-permute-start(bf16[384,128]{1,0:T(8,128)(2,1)} %shard_map.86.refs_0_), channel_id=1, source_target_pairs={{0,4},{1,5},{2,6},{3,7},{4,0},{5,1},{6,2},{7,3},{8,12},{9,13},{10,... | collective-permute-start | bytes 294920 | tf_op jit(solution)/shard_map/ppermute | solution.py:404
  12.0 7.8 %shard_map.87 = (bf16[2,256,1024]{2,1,0:T(8,128)(2,1)}, f32[2,256,512]{2,1,0:T(8,128)}, bf16[2,768,1024]{2,1,0:T(8,128)(2,1)}, s32[8,512]{1,0:T(8,128)}, s32[8,128]{1,0:T(8,128)}, /*index=5*/s32[2,512]{1,0:T(2,128)}) custom-call(s32[2,2048]{1,0:T(2,128)} %blocks_hbm.3, s32[2,512]{1,0:T(2,128)} %pivots_hbm.1, f32[1024,256]{1,0:T(8,128)} %w_hbm.3, ...), custom_call_target="tpu_custom_call" | custom-call | bytes 7909376 | tf_op jit(solution)/shard_map/pallas_call | solution.py:389
  19.8 2.4 %collective-permute-start.2 = (bf16[384,128]{1,0:T(8,128)(2,1)}, bf16[384,128]{1,0:T(8,128)(2,1)S(1)}, u32[]{:S(2)}, u32[]{:S(2)}) collective-permute-start(bf16[384,128]{1,0:T(8,128)(2,1)} %shard_map.86.refs_0_), channel_id=1, source_target_pairs={{0,3},{1,2},{2,1},{3,0},{4,7},{5,6},{6,5},{7,4},{8,11},{9,10},{10,... | collective-permute-start | bytes 294920 | tf_op jit(solution)/shard_map/ppermute | solution.py:404
  22.1 0.0 collective-permute-done.6.refs_7_
  22.1 0.0 copy-start.6
  22.1 0.8 collective-permute-start.1
  22.9 0.0 collective-permute-done.5.refs_6_
  22.9 0.0 copy-start.7
  22.9 0.4 collective-permute-start
  23.4 1.5 %collective-permute-done.4.refs_5_ = bf16[384,128]{1,0:T(8,128)(2,1)S(1)} collective-permute-done((bf16[384,128]{1,0:T(8,128)(2,1)}, bf16[384,128]{1,0:T(8,128)(2,1)S(1)}, u32[]{:S(2)}, u32[]{:S(2)}) %collective-permute-start.4) | collective-permute-done | bytes 98336 | tf_op jit(solution)/shard_map/ppermute | solution.py:404
  24.8 0.0 copy-start.8
  24.8 1.1 %collective-permute-done.3.refs_4_ = bf16[384,128]{1,0:T(8,128)(2,1)S(1)} collective-permute-done((bf16[384,128]{1,0:T(8,128)(2,1)}, bf16[384,128]{1,0:T(8,128)(2,1)S(1)}, u32[]{:S(2)}, u32[]{:S(2)}) %collective-permute-start.3) | collective-permute-done | bytes 98336 | tf_op jit(solution)/shard_map/ppermute | solution.py:404
  26.0 0.0 copy-start.9
  26.0 2.0 %collective-permute-done.2.refs_3_ = bf16[384,128]{1,0:T(8,128)(2,1)S(1)} collective-permute-done((bf16[384,128]{1,0:T(8,128)(2,1)}, bf16[384,128]{1,0:T(8,128)(2,1)S(1)}, u32[]{:S(2)}, u32[]{:S(2)}) %collective-permute-start.2) | collective-permute-done | bytes 98336 | tf_op jit(solution)/shard_map/ppermute | solution.py:404
  28.0 0.0 copy-start.10
  28.0 2.1 %collective-permute-done.1.refs_2_ = bf16[384,128]{1,0:T(8,128)(2,1)S(1)} collective-permute-done((bf16[384,128]{1,0:T(8,128)(2,1)}, bf16[384,128]{1,0:T(8,128)(2,1)S(1)}, u32[]{:S(2)}, u32[]{:S(2)}) %collective-permute-start.1) | collective-permute-done | bytes 98336 | tf_op jit(solution)/shard_map/ppermute | solution.py:404
  30.1 0.0 copy-start.11
  30.1 0.0 collective-permute-done.refs_1_
  30.1 0.0 copy-done.6
  30.1 0.0 copy-done.7
  30.1 0.0 copy-done.8
  30.1 0.0 copy-done.9
  30.1 0.0 copy-done.10
  30.1 0.6 copy-done.11
  30.7 0.0 copy-start.12
  30.7 0.7 copy-done.12
  31.4 2.3 %shard_map.88.block_hbm.b0_hbm = bf16[2,128,512]{2,1,0:T(8,128)(2,1)} custom-call(bf16[384,128]{1,0:T(8,128)(2,1)} %shard_map.86.refs_0_, bf16[384,128]{1,0:T(8,128)(2,1)} %copy-done.12, bf16[384,128]{1,0:T(8,128)(2,1)} %copy-done.11, bf16[384,128]{1,0:T(8,128)(2,1)} %copy-done.10, bf16[384,128]{1,0:T(8,128)(2,1)} %copy-done.9, bf16[384,128]{1,0:T(8,128)(2,1)} %copy-done.8, ...), custom_call_target="tpu_custom_call" | custom-call | bytes 1052672 | tf_op jit(solution)/shard_map/pallas_call | solution.py:389
  33.7 0.0 copy-start.2
  33.7 1.6 %collective-permute-start.7 = (bf16[2,128,512]{2,1,0:T(8,128)(2,1)}, bf16[2,128,512]{2,1,0:T(8,128)(2,1)S(1)}, u32[]{:S(2)}, u32[]{:S(2)}) collective-permute-start(bf16[2,128,512]{2,1,0:T(8,128)(2,1)} %shard_map.88.block_hbm.b0_hbm), channel_id=1, source_target_pairs={{0,16},{8,24},{16,0},{24,8},{1,17},{9,25},{17,1},{25,9},{2,18},{10... | collective-permute-start | bytes 786440 | tf_op jit(solution)/shard_map/ppermute | solution.py:404
  35.2 3.5 %shard_map.89 = bf16[32,32,256]{2,1,0:T(8,128)(2,1)} custom-call(bf16[2,128,512]{2,1,0:T(8,128)(2,1)} %shard_map.88.block_hbm.b0_hbm, bf16[1024,128]{1,0:T(8,128)(2,1)} %feats_hbm.3, bf16[2,256,1024]{2,1,0:T(8,128)(2,1)} %get-tuple-element.17.coef_hbm, f32[2,256,512]{2,1,0:T(8,128)} %get-tuple-element.18.offset_hbm), custom_call_target="tpu_custom_call" | custom-call | flops 1073741824 | bytes 3145728 | tf_op jit(solution)/shard_map/pallas_call | solution.py:389
  38.8 3.4 %collective-permute-done.7.b2_hbm = bf16[2,128,512]{2,1,0:T(8,128)(2,1)S(1)} collective-permute-done((bf16[2,128,512]{2,1,0:T(8,128)(2,1)}, bf16[2,128,512]{2,1,0:T(8,128)(2,1)S(1)}, u32[]{:S(2)}, u32[]{:S(2)}) %collective-permute-start.7) | collective-permute-done | bytes 262176 | tf_op jit(solution)/shard_map/ppermute | solution.py:404
  42.1 0.0 copy-start.13
  42.1 4.0 %all-to-all-start = ((bf16[32,32,256]{2,1,0:T(8,128)(2,1)}), bf16[32,32,256]{2,1,0:T(8,128)(2,1)S(1)}, u32[]{:S(2)}, u32[]{:S(2)}) async-start(bf16[32,32,256]{2,1,0:T(8,128)(2,1)} %shard_map.89), calls=%async_computation | async-start | bytes 1048576 | tf_op jit(solution)/shard_map/all_to_all | solution.py:478
  46.1 0.0 copy-done.2
  46.2 0.1 collective-permute-start.8
  46.3 0.4 collective-permute-start.9
  46.7 1.0 %collective-permute-done.8.b1_hbm = bf16[2,128,512]{2,1,0:T(8,128)(2,1)S(1)} collective-permute-done((bf16[2,128,512]{2,1,0:T(8,128)(2,1)S(1)}, bf16[2,128,512]{2,1,0:T(8,128)(2,1)S(1)}, u32[]{:S(2)}, u32[]{:S(2)}) %collective-permute-start.8) | collective-permute-done | bytes 262176 | tf_op jit(solution)/shard_map/ppermute | solution.py:404
  47.8 0.0 copy-start.14
  47.8 0.4 collective-permute-done.9.b3_hbm
  48.1 0.0 copy-start.15
  48.1 0.0 copy-done.13
  48.1 0.3 copy-done.14
  48.5 0.4 copy-done.15
  48.8 9.8 %shard_map.90 = (bf16[2,512,2048]{2,1,0:T(8,128)(2,1)}, bf16[4,2048,512]{2,1,0:T(8,128)(2,1)}) custom-call(bf16[2,128,512]{2,1,0:T(8,128)(2,1)} %shard_map.88.block_hbm.b0_hbm, bf16[2,128,512]{2,1,0:T(8,128)(2,1)} %copy-done.14, bf16[2,128,512]{2,1,0:T(8,128)(2,1)} %copy-done.13, bf16[2,128,512]{2,1,0:T(8,128)(2,1)} %copy-done.15, ...), custom_call_target="tpu_custom_call" | custom-call | flops 1610612736 | bytes 13651968 | tf_op jit(solution)/shard_map/pallas_call | solution.py:389
  58.7 3.6 %all-to-all-done.summed_hbm = bf16[32,32,256]{2,1,0:T(8,128)(2,1)S(1)} async-done(((bf16[32,32,256]{2,1,0:T(8,128)(2,1)}), bf16[32,32,256]{2,1,0:T(8,128)(2,1)S(1)}, u32[]{:S(2)}, u32[]{:S(2)}) %all-to-all-start) | async-done | bytes 524320 | tf_op jit(solution)/shard_map/all_to_all | solution.py:478
  62.3 0.8 copy-done
  63.1 7.1 %shard_map.91 = bf16[8,32,384]{2,1,0:T(8,128)(2,1)} custom-call(bf16[32,32,256]{2,1,0:T(8,128)(2,1)} %copy-done, bf16[2,512,2048]{2,1,0:T(8,128)(2,1)} %get-tuple-element.23.factor_hbm, bf16[2,512,512]{2,1,0:T(8,128)(2,1)} %core_hbm.1, bf16[4,2048,512]{2,1,0:T(8,128)(2,1)} %get-tuple-element.24.cross_hbm, s32[8,128]{1,0:T(8,128)} %get-tuple-element.16.refs_8_.starts_hbm), custom_call_target="tpu_custom_call" | custom-call | bytes 14356480 | tf_op jit(solution)/shard_map/pallas_call | solution.py:389
  70.2 11.4 %all_to_all.10.g0_hbm = bf16[8,32,384]{2,1,0:T(8,128)(2,1)S(1)} all-to-all(bf16[8,32,384]{2,1,0:T(8,128)(2,1)} %shard_map.91), channel_id=1, replica_groups=mesh['rows'=4,'pts'=8] {'pts'}, dimensions={0} | all-to-all | bytes 393216 | tf_op jit(solution)/shard_map/all_to_all | solution.py:511
  81.6 1.2 %collective-permute-start.11 = (bf16[8,32,384]{2,1,0:T(8,128)(2,1)S(1)}, bf16[8,32,384]{2,1,0:T(8,128)(2,1)S(1)}, u32[]{:S(2)}, u32[]{:S(2)}) collective-permute-start(bf16[8,32,384]{2,1,0:T(8,128)(2,1)S(1)} %all_to_all.10.g0_hbm), channel_id=1, source_target_pairs={{0,16},{8,24},{16,0},{24,8},{1,17},{9,25},{17,1},{25,9},{2,18},{10... | collective-permute-start | bytes 589832 | tf_op jit(solution)/shard_map/ppermute | solution.py:404
  82.8 0.0 collective-permute-start.10
  82.8 4.5 %collective-permute-done.11.g2_hbm = bf16[8,32,384]{2,1,0:T(8,128)(2,1)S(1)} collective-permute-done((bf16[8,32,384]{2,1,0:T(8,128)(2,1)S(1)}, bf16[8,32,384]{2,1,0:T(8,128)(2,1)S(1)}, u32[]{:S(2)}, u32[]{:S(2)}) %collective-permute-start.11) | collective-permute-done | bytes 196640 | tf_op jit(solution)/shard_map/ppermute | solution.py:404
  87.3 0.0 collective-permute-start.12
  87.3 0.0 collective-permute-done.10.g1_hbm
  87.3 0.0 copy-start.4
  87.3 1.4 %collective-permute-done.12.g3_hbm = bf16[8,32,384]{2,1,0:T(8,128)(2,1)S(1)} collective-permute-done((bf16[8,32,384]{2,1,0:T(8,128)(2,1)S(1)}, bf16[8,32,384]{2,1,0:T(8,128)(2,1)S(1)}, u32[]{:S(2)}, u32[]{:S(2)}) %collective-permute-start.12) | collective-permute-done | bytes 196640 | tf_op jit(solution)/shard_map/ppermute | solution.py:404
  88.7 0.0 copy-done.1
  88.7 0.0 copy-done.3
  88.7 0.0 copy-done.4
  88.7 0.7 copy-done.5
  89.4 4.9 %shard_map.92 = (f32[1024,256]{1,0:T(8,128)}, f32[1024,256]{1,0:T(8,128)}) custom-call(bf16[8,32,384]{2,1,0:T(8,128)(2,1)} %copy-done.1, bf16[8,32,384]{2,1,0:T(8,128)(2,1)} %copy-done.4, bf16[8,32,384]{2,1,0:T(8,128)(2,1)} %copy-done.3, bf16[8,32,384]{2,1,0:T(8,128)(2,1)} %copy-done.5, f32[1024,256]{1,0:T(8,128)} %w_hbm.3, f32[1024,256]{1,0:T(8,128)} %z_hbm.3, ...), custom_call_target="tpu_custom_call" | custom-call | bytes 8126464 | tf_op jit(solution)/shard_map/pallas_call | solution.py:389
  (4 shorter events, 0.0 us)
Async XLA Ops:
  2.9 19.2 %collective-permute-start.6 = (bf16[384,128]{1,0:T(8,128)(2,1)}, bf16[384,128]{1,0:T(8,128)(2,1)S(1)}, u32[]{:S(2)}, u32[]{:S(2)}) collective-permute-start(bf16[384,128]{1,0:T(8,128)(2,1)} %shard_map.86.refs_0_), channel_id=1, source_target_pairs={{0,7},{1,6},{2,5},{3,4},{4,3},{5,2},{6,1},{7,0},{8,15},{9,14},{10,... | collective-permute-start | bytes 294920 | tf_op jit(solution)/shard_map/ppermute | solution.py:404
  9.0 14.0 %collective-permute-start.5 = (bf16[384,128]{1,0:T(8,128)(2,1)}, bf16[384,128]{1,0:T(8,128)(2,1)S(1)}, u32[]{:S(2)}, u32[]{:S(2)}) collective-permute-start(bf16[384,128]{1,0:T(8,128)(2,1)} %shard_map.86.refs_0_), channel_id=1, source_target_pairs={{0,6},{1,7},{2,4},{3,5},{4,2},{5,3},{6,0},{7,1},{8,14},{9,15},{10,... | collective-permute-start | bytes 294920 | tf_op jit(solution)/shard_map/ppermute | solution.py:404
  9.2 15.6 %collective-permute-start.4 = (bf16[384,128]{1,0:T(8,128)(2,1)}, bf16[384,128]{1,0:T(8,128)(2,1)S(1)}, u32[]{:S(2)}, u32[]{:S(2)}) collective-permute-start(bf16[384,128]{1,0:T(8,128)(2,1)} %shard_map.86.refs_0_), channel_id=1, source_target_pairs={{0,5},{1,4},{2,7},{3,6},{4,1},{5,0},{6,3},{7,2},{8,13},{9,12},{10,... | collective-permute-start | bytes 294920 | tf_op jit(solution)/shard_map/ppermute | solution.py:404
  9.9 16.0 %collective-permute-start.3 = (bf16[384,128]{1,0:T(8,128)(2,1)}, bf16[384,128]{1,0:T(8,128)(2,1)S(1)}, u32[]{:S(2)}, u32[]{:S(2)}) collective-permute-start(bf16[384,128]{1,0:T(8,128)(2,1)} %shard_map.86.refs_0_), channel_id=1, source_target_pairs={{0,4},{1,5},{2,6},{3,7},{4,0},{5,1},{6,2},{7,3},{8,12},{9,13},{10,... | collective-permute-start | bytes 294920 | tf_op jit(solution)/shard_map/ppermute | solution.py:404
  19.8 8.2 %collective-permute-start.2 = (bf16[384,128]{1,0:T(8,128)(2,1)}, bf16[384,128]{1,0:T(8,128)(2,1)S(1)}, u32[]{:S(2)}, u32[]{:S(2)}) collective-permute-start(bf16[384,128]{1,0:T(8,128)(2,1)} %shard_map.86.refs_0_), channel_id=1, source_target_pairs={{0,3},{1,2},{2,1},{3,0},{4,7},{5,6},{6,5},{7,4},{8,11},{9,10},{10,... | collective-permute-start | bytes 294920 | tf_op jit(solution)/shard_map/ppermute | solution.py:404
  22.1 8.0 %copy-start.6 = (bf16[384,128]{1,0:T(8,128)(2,1)}, bf16[384,128]{1,0:T(8,128)(2,1)S(1)}, u32[]{:S(2)}) copy-start(bf16[384,128]{1,0:T(8,128)(2,1)S(1)} %collective-permute-done.6.refs_7_) | copy-start | bytes 294916
  22.1 7.9 %collective-permute-start.1 = (bf16[384,128]{1,0:T(8,128)(2,1)}, bf16[384,128]{1,0:T(8,128)(2,1)S(1)}, u32[]{:S(2)}, u32[]{:S(2)}) collective-permute-start(bf16[384,128]{1,0:T(8,128)(2,1)} %shard_map.86.refs_0_), channel_id=1, source_target_pairs={{0,2},{1,3},{2,0},{3,1},{4,6},{5,7},{6,4},{7,5},{8,10},{9,11},{10,... | collective-permute-start | bytes 294920 | tf_op jit(solution)/shard_map/ppermute | solution.py:404
  22.9 7.2 %copy-start.7 = (bf16[384,128]{1,0:T(8,128)(2,1)}, bf16[384,128]{1,0:T(8,128)(2,1)S(1)}, u32[]{:S(2)}) copy-start(bf16[384,128]{1,0:T(8,128)(2,1)S(1)} %collective-permute-done.5.refs_6_) | copy-start | bytes 294916
  22.9 7.2 %collective-permute-start = (bf16[384,128]{1,0:T(8,128)(2,1)}, bf16[384,128]{1,0:T(8,128)(2,1)S(1)}, u32[]{:S(2)}, u32[]{:S(2)}) collective-permute-start(bf16[384,128]{1,0:T(8,128)(2,1)} %shard_map.86.refs_0_), channel_id=1, source_target_pairs={{0,1},{1,0},{2,3},{3,2},{4,5},{5,4},{6,7},{7,6},{8,9},{9,8},{10,11... | collective-permute-start | bytes 294920 | tf_op jit(solution)/shard_map/ppermute | solution.py:404
  24.8 5.3 %copy-start.8 = (bf16[384,128]{1,0:T(8,128)(2,1)}, bf16[384,128]{1,0:T(8,128)(2,1)S(1)}, u32[]{:S(2)}) copy-start(bf16[384,128]{1,0:T(8,128)(2,1)S(1)} %collective-permute-done.4.refs_5_) | copy-start | bytes 294916
  26.0 4.1 %copy-start.9 = (bf16[384,128]{1,0:T(8,128)(2,1)}, bf16[384,128]{1,0:T(8,128)(2,1)S(1)}, u32[]{:S(2)}) copy-start(bf16[384,128]{1,0:T(8,128)(2,1)S(1)} %collective-permute-done.3.refs_4_) | copy-start | bytes 294916
  28.0 2.1 %copy-start.10 = (bf16[384,128]{1,0:T(8,128)(2,1)}, bf16[384,128]{1,0:T(8,128)(2,1)S(1)}, u32[]{:S(2)}) copy-start(bf16[384,128]{1,0:T(8,128)(2,1)S(1)} %collective-permute-done.2.refs_3_) | copy-start | bytes 294916
  30.1 0.6 copy-start.11
  30.7 0.7 copy-start.12
  33.7 12.5 %copy-start.2 = (bf16[2,128,512]{2,1,0:T(8,128)(2,1)S(1)}, bf16[2,128,512]{2,1,0:T(8,128)(2,1)}, u32[]{:S(2)}) copy-start(bf16[2,128,512]{2,1,0:T(8,128)(2,1)} %shard_map.88.block_hbm.b0_hbm) | copy-start | bytes 786436
  33.7 8.5 %collective-permute-start.7 = (bf16[2,128,512]{2,1,0:T(8,128)(2,1)}, bf16[2,128,512]{2,1,0:T(8,128)(2,1)S(1)}, u32[]{:S(2)}, u32[]{:S(2)}) collective-permute-start(bf16[2,128,512]{2,1,0:T(8,128)(2,1)} %shard_map.88.block_hbm.b0_hbm), channel_id=1, source_target_pairs={{0,16},{8,24},{16,0},{24,8},{1,17},{9,25},{17,1},{25,9},{2,18},{10... | collective-permute-start | bytes 786440 | tf_op jit(solution)/shard_map/ppermute | solution.py:404
  42.1 6.0 %copy-start.13 = (bf16[2,128,512]{2,1,0:T(8,128)(2,1)}, bf16[2,128,512]{2,1,0:T(8,128)(2,1)S(1)}, u32[]{:S(2)}) copy-start(bf16[2,128,512]{2,1,0:T(8,128)(2,1)S(1)} %collective-permute-done.7.b2_hbm) | copy-start | bytes 786436
  42.1 20.2 %all-to-all-start = ((bf16[32,32,256]{2,1,0:T(8,128)(2,1)}), bf16[32,32,256]{2,1,0:T(8,128)(2,1)S(1)}, u32[]{:S(2)}, u32[]{:S(2)}) async-start(bf16[32,32,256]{2,1,0:T(8,128)(2,1)} %shard_map.89), calls=%async_computation | async-start | bytes 1048576 | tf_op jit(solution)/shard_map/all_to_all | solution.py:478
  46.2 1.6 %collective-permute-start.8 = (bf16[2,128,512]{2,1,0:T(8,128)(2,1)S(1)}, bf16[2,128,512]{2,1,0:T(8,128)(2,1)S(1)}, u32[]{:S(2)}, u32[]{:S(2)}) collective-permute-start(bf16[2,128,512]{2,1,0:T(8,128)(2,1)S(1)} %copy-done.2), channel_id=1, source_target_pairs={{0,8},{8,0},{16,24},{24,16},{1,9},{9,1},{17,25},{25,17},{2,10},{10... | collective-permute-start | bytes 786440 | tf_op jit(solution)/shard_map/ppermute | solution.py:404
  46.3 1.8 %collective-permute-start.9 = (bf16[2,128,512]{2,1,0:T(8,128)(2,1)S(1)}, bf16[2,128,512]{2,1,0:T(8,128)(2,1)S(1)}, u32[]{:S(2)}, u32[]{:S(2)}) collective-permute-start(bf16[2,128,512]{2,1,0:T(8,128)(2,1)S(1)} %collective-permute-done.7.b2_hbm), channel_id=1, source_target_pairs={{0,8},{8,0},{16,24},{24,16},{1,9},{9,1},{17,25},{25,17},{2,10},{10... | collective-permute-start | bytes 786440 | tf_op jit(solution)/shard_map/ppermute | solution.py:404
  47.8 0.7 copy-start.14
  48.1 0.7 copy-start.15
  62.3 0.8 copy-start
  81.6 7.1 %copy-start.1 = (bf16[8,32,384]{2,1,0:T(8,128)(2,1)}, bf16[8,32,384]{2,1,0:T(8,128)(2,1)S(1)}, u32[]{:S(2)}) copy-start(bf16[8,32,384]{2,1,0:T(8,128)(2,1)S(1)} %all_to_all.10.g0_hbm) | copy-start | bytes 589828
  81.6 5.7 %collective-permute-start.11 = (bf16[8,32,384]{2,1,0:T(8,128)(2,1)S(1)}, bf16[8,32,384]{2,1,0:T(8,128)(2,1)S(1)}, u32[]{:S(2)}, u32[]{:S(2)}) collective-permute-start(bf16[8,32,384]{2,1,0:T(8,128)(2,1)S(1)} %all_to_all.10.g0_hbm), channel_id=1, source_target_pairs={{0,16},{8,24},{16,0},{24,8},{1,17},{9,25},{17,1},{25,9},{2,18},{10... | collective-permute-start | bytes 589832 | tf_op jit(solution)/shard_map/ppermute | solution.py:404
  82.8 4.5 %collective-permute-start.10 = (bf16[8,32,384]{2,1,0:T(8,128)(2,1)S(1)}, bf16[8,32,384]{2,1,0:T(8,128)(2,1)S(1)}, u32[]{:S(2)}, u32[]{:S(2)}) collective-permute-start(bf16[8,32,384]{2,1,0:T(8,128)(2,1)S(1)} %all_to_all.10.g0_hbm), channel_id=1, source_target_pairs={{0,8},{8,0},{16,24},{24,16},{1,9},{9,1},{17,25},{25,17},{2,10},{10... | collective-permute-start | bytes 589832 | tf_op jit(solution)/shard_map/ppermute | solution.py:404
  87.3 1.5 %copy-start.3 = (bf16[8,32,384]{2,1,0:T(8,128)(2,1)}, bf16[8,32,384]{2,1,0:T(8,128)(2,1)S(1)}, u32[]{:S(2)}) copy-start(bf16[8,32,384]{2,1,0:T(8,128)(2,1)S(1)} %collective-permute-done.11.g2_hbm) | copy-start | bytes 589828
  87.3 1.4 %collective-permute-start.12 = (bf16[8,32,384]{2,1,0:T(8,128)(2,1)S(1)}, bf16[8,32,384]{2,1,0:T(8,128)(2,1)S(1)}, u32[]{:S(2)}, u32[]{:S(2)}) collective-permute-start(bf16[8,32,384]{2,1,0:T(8,128)(2,1)S(1)} %collective-permute-done.11.g2_hbm), channel_id=1, source_target_pairs={{0,8},{8,0},{16,24},{24,16},{1,9},{9,1},{17,25},{25,17},{2,10},{10... | collective-permute-start | bytes 589832 | tf_op jit(solution)/shard_map/ppermute | solution.py:404
  87.3 1.4 %copy-start.4 = (bf16[8,32,384]{2,1,0:T(8,128)(2,1)}, bf16[8,32,384]{2,1,0:T(8,128)(2,1)S(1)}, u32[]{:S(2)}) copy-start(bf16[8,32,384]{2,1,0:T(8,128)(2,1)S(1)} %collective-permute-done.10.g1_hbm) | copy-start | bytes 589828
  88.7 0.7 copy-start.5

commit v10 on v9

--- a/solution.py
+++ b/solution.py
@@ -60,20 +60,40 @@
     return one_hot(iota((n, n), 0) < iota((n, n), 1))
 
 
-def slots_of(indices, before, points, owners, cap):
+def owners_of(indices, before, points, owners):
     owner = lax.div(indices, jnp.full_like(indices, points))
-    marks = iota((owners, indices.shape[1]), 0) == owner
-    counts = jnp.where(marks, 1.0, 0.0)
-    earlier = mm(counts.astype(bf16), before, 1, 0)
-    rank = jnp.sum(counts * earlier, axis=0, keepdims=True)
-    return owner * cap + rank.astype(i32)
-
-
-def point_rows(indices, slots, me, points, cap):
-    held = iota((cap, indices.shape[1]), 0) + me * cap == slots
-    local = (indices - me * points + 1).astype(f32)
-    point = jnp.sum(jnp.where(held, local, 0.0), axis=1, keepdims=True).astype(i32) - 1
-    return one_hot(iota((cap, points), 1) == point)
+    owner_ids = iota((owners, indices.shape[1]), 0)
+    marks = jnp.where(owner_ids == owner, 1.0, 0.0)
+    earlier = mm(marks.astype(bf16), before, 1, 0)
+    rank = jnp.sum(marks * earlier, axis=0, keepdims=True)
+    start = jnp.sum(jnp.where(owner < owner_ids, 1.0, 0.0), axis=1, keepdims=True)
+    return marks, rank, start
+
+
+def sorted_places(marks, rank, start):
+    return (rank + jnp.sum(marks * start, axis=0, keepdims=True)).astype(i32)
+
+
+def lane_row(column):
+    n = column.shape[0]
+    diagonal = iota((n, 128), 0) == iota((n, 128), 1)
+    return jnp.sum(jnp.where(diagonal, column, 0.0), axis=0, keepdims=True).astype(i32)
+
+
+def sorted_points(indices, place):
+    count = indices.shape[1]
+    return from_digits(mm(two_digits(indices), one_hot(iota((count, count), 0) == place), 1, 1))
+
+
+def two_digits(row):
+    high = lax.shift_right_logical(row, jnp.full_like(row, 7))
+    shape = (8, row.shape[1])
+    value = jnp.where(iota(shape, 0) == 0, high, lax.bitwise_and(row, jnp.full_like(row, 127)))
+    return value.astype(f32).astype(bf16)
+
+
+def from_digits(digits):
+    return (digits[0:1] * 128.0 + digits[1:2]).astype(i32)
 
 
 def start_all(pairs, sems):
@@ -101,79 +121,92 @@
     rows = []
     for u in range(UPDATES):
         indices = group_row(blocks, u, row, count)
-        slots = slots_of(indices, before, points, owners, cap)
-        rows.append(point_rows(indices, slots, me, points, cap))
+        local = indices - me * points
+        mine = jnp.where((local >= 0) & (local < points), 1.0, 0.0)
+        rank = mm(jnp.broadcast_to(mine, (8, count)).astype(bf16), before, 1, 0)[0:1]
+        held = (iota((cap, count), 0) == rank.astype(i32)) & (mine > 0.0)
+        point = jnp.sum(jnp.where(held, (local + 1).astype(f32), 0.0), axis=1, keepdims=True)
+        rows.append(one_hot(iota((cap, points), 1) == point.astype(i32) - 1))
     reads[1].wait()
     for u in range(UPDATES):
         packed[u * cap : (u + 1) * cap, :] = mm(rows[u], feats[...], 1, 0).astype(bf16)
     wait_all(start_all([(packed, out_hbm)], sems))
 
 
-def two_digits(row):
-    high = lax.shift_right_logical(row, jnp.full_like(row, 7))
-    shape = (8, row.shape[1])
-    value = jnp.where(iota(shape, 0) == 0, high, lax.bitwise_and(row, jnp.full_like(row, 127)))
-    return value.astype(f32).astype(bf16)
-
-
-def from_digits(digits):
-    return (digits[0:1] * 128.0 + digits[1:2]).astype(i32)
-
-
 def prepare_kernel(
-    count, cap, owners,
-    blocks_hbm, pivots_hbm, w_hbm, z_hbm, t_hbm,
-    coef_hbm, offset_hbm, rows_hbm, ids_hbm, starts_hbm, chosen_hbm,
-    blocks, pivots, w, z, t, coef, offset, rows, ids, starts, chosen, sems, out_sems,
+    count, owners,
+    blocks_hbm, w_hbm, z_hbm, t_hbm, coef_hbm, offset_hbm, starts_hbm,
+    blocks, w, z, t, coef, offset, starts, sems, out_sems,
 ):
     row, me = lax.axis_index("rows"), lax.axis_index("pts")
     points, outputs = w.shape
-    pairs = [(blocks_hbm, blocks), (pivots_hbm, pivots), (w_hbm, w), (z_hbm, z), (t_hbm, t)]
-    reads = start_all(pairs, sems)
+    reads = start_all([(blocks_hbm, blocks), (w_hbm, w), (z_hbm, z), (t_hbm, t)], sems)
     before = before_matrix(count)
-    wait_all(reads[:2])
-    groups = blocks.shape[1] // count
-    for u in range(UPDATES):
-        pivot = pivots[u : u + 1, :]
-        found = jnp.zeros((8, pivot.shape[1]), f32)
-        for g in range(groups):
-            n = u * groups + g
-            indices = blocks[u : u + 1, g * count : (g + 1) * count]
-            owner = lax.div(indices, jnp.full_like(indices, points))
-            owner_ids = iota((owners, count), 0)
-            marks = jnp.where(owner_ids == owner, 1.0, 0.0)
-            earlier = mm(marks.astype(bf16), before, 1, 0)
-            start = jnp.sum(jnp.where(owner < owner_ids, 1.0, 0.0), axis=1, keepdims=True)
-            rank = jnp.sum(marks * earlier, axis=0, keepdims=True)
-            place = (rank + jnp.sum(marks * start, axis=0, keepdims=True)).astype(i32)
-            held = owner * cap + rank.astype(i32)
-            rows[u, g * cap : (g + 1) * cap, :] = point_rows(indices, held, me, points, cap)
-            ordered = one_hot(iota((count, count), 0) == place)
-            ids[n : n + 1, :] = from_digits(mm(two_digits(indices), ordered, 1, 1))
-            diagonal = iota((owners, 128), 0) == iota((owners, 128), 1)
-            starts[n : n + 1, :] = jnp.sum(
-                jnp.where(diagonal, start, 0.0), axis=0, keepdims=True
-            ).astype(i32)
-            at_pivot = one_hot(iota((count, pivot.shape[1]), 0) + g * count == pivot)
-            found += mm(two_digits(place + g * count), at_pivot, 1, 0)
-        chosen[u : u + 1, :] = from_digits(found)
-    pairs = [(starts, starts_hbm), (ids, ids_hbm), (chosen, chosen_hbm), (rows, rows_hbm)]
-    writes = start_all(pairs, out_sems)
-    wait_all(reads[2:])
+    reads[0].wait()
+    locals_of = []
+    for u in range(UPDATES):
+        indices = group_row(blocks, u, row, count)
+        marks, rank, start = owners_of(indices, before, points, owners)
+        starts[u : u + 1, :] = lane_row(start)
+        locals_of.append(sorted_points(indices, sorted_places(marks, rank, start)) - me * points)
+    writes = start_all([(starts, starts_hbm)], out_sems)
+    wait_all(reads[1:])
     current, moving = w[...], z[...]
     goal = t[...].astype(f32).T
     for u in range(UPDATES):
         mixed = mixed_of(current, moving).T
         high, low = split_two(ridge_term * mixed - goal)
         coef[u] = mixed.astype(bf16)
-        local = ids[pl.ds(u * groups + row, 1), :] - me * points
-        place = one_hot(iota((points, count), 0) == local)
+        place = one_hot(iota((points, count), 0) == locals_of[u])
         offset[u] = mm(high, place, 1, 0) + mm(low, place, 1, 0)
         current, moving = stepped(current, moving, None)
         for a, b in ((coef, coef_hbm), (offset, offset_hbm)):
             writes.append(pltpu.make_async_copy(a.at[u], b.at[u], out_sems.at[len(writes)]))
             writes[-1].start()
     wait_all(writes)
+
+
+def order_kernel(
+    count, points, owners,
+    blocks_hbm, pivots_hbm, ids_hbm, starts_hbm, chosen_hbm,
+    blocks, pivots, ids, starts, chosen, sems,
+):
+    wait_all(start_all([(blocks_hbm, blocks), (pivots_hbm, pivots)], sems))
+    before = before_matrix(count)
+    groups = blocks.shape[1] // count
+    for u in range(UPDATES):
+        pivot = pivots[u : u + 1, :]
+        found = jnp.zeros((8, pivot.shape[1]), f32)
+        for g in range(groups):
+            n = u * groups + g
+            indices = blocks[u : u + 1, g * count : (g + 1) * count]
+            marks, rank, start = owners_of(indices, before, points, owners)
+            place = sorted_places(marks, rank, start)
+            ids[n : n + 1, :] = sorted_points(indices, place)
+            starts[n : n + 1, :] = lane_row(start)
+            at_pivot = one_hot(iota((count, pivot.shape[1]), 0) + g * count == pivot)
+            found += mm(two_digits(place + g * count), at_pivot, 1, 0)
+        chosen[u : u + 1, :] = from_digits(found)
+    wait_all(start_all([(ids, ids_hbm), (starts, starts_hbm), (chosen, chosen_hbm)], sems))
+
+
+def slots_kernel(count, points, cap, blocks_hbm, slots_hbm, blocks, slots, sems):
+    me = lax.axis_index("pts")
+    wait_all(start_all([(blocks_hbm, blocks)], sems))
+    before = before_matrix(count)
+    groups = blocks.shape[1] // count
+    for u in range(UPDATES):
+        found = jnp.zeros((8, groups * cap), f32)
+        for g in range(groups):
+            local = blocks[u : u + 1, g * count : (g + 1) * count] - me * points
+            mine = (local >= 0) & (local < points)
+            counts = jnp.where(mine, 1.0, 0.0)
+            rank = mm(jnp.broadcast_to(counts, (8, count)).astype(bf16), before, 1, 0)[0:1]
+            held = jnp.where(mine, rank.astype(i32) + g * cap, -1)
+            chosen = one_hot(iota((groups * cap, count), 0) == held)
+            found += mm(two_digits(jnp.where(mine, local + 1, 0)), chosen, 1, 1)
+        slots[u : u + 1, :] = from_digits(found) - 1
+    wait_all(start_all([(slots, slots_hbm)], sems))
 
 
 def extended(rows, axis, first):
@@ -199,16 +232,15 @@
 
 def compact_kernel(*refs):
     *came_hbm, starts_hbm, block_hbm, came, starts, wide, block, sems = refs
-    row, me = lax.axis_index("rows"), lax.axis_index("pts")
+    me = lax.axis_index("pts")
     owners, deep, _ = came.shape
     cap = deep // UPDATES
-    groups = starts.shape[0] // UPDATES
     count = block.shape[2]
     pairs = [(a, came.at[k]) for k, a in enumerate(came_hbm)]
     wait_all(start_all([*pairs, (starts_hbm, starts)], sems))
     for u in range(UPDATES):
         for o in range(owners):
-            start = starts[u * groups + row, o]
+            start = starts[u, o]
             rows = came[lax.bitwise_xor(me, o), u * cap : (u + 1) * cap, :]
             wide[u, pl.ds(start, cap), :] = rows.astype(f32)
         block[u] = wide[u, 0:count, :].T.astype(bf16)
@@ -332,39 +364,41 @@
 
 
 def finish_kernel(
-    g0_hbm, g1_hbm, g2_hbm, g3_hbm, w_hbm, z_hbm, rows_hbm, w_out, z_out,
-    got, w, z, rows, steps, w_new, z_new, sems, out_sems,
+    g0_hbm, g1_hbm, g2_hbm, g3_hbm, slots_hbm, w_hbm, z_hbm, w_out, z_out,
+    got, slots, w, z, steps, w_new, z_new, sems, out_sems,
 ):
     row = lax.axis_index("rows")
     points = w.shape[0]
     sources, deep, lanes = got.shape
     own = deep // (2 * UPDATES)
     chunks = range(0, points, CHUNK)
-    pairs = []
+    pairs = [(slots_hbm, slots)]
     for k, g_hbm in enumerate((g0_hbm, g1_hbm, g2_hbm, g3_hbm)):
         size = g_hbm.shape[0]
         first = pl.multiple_of(lax.bitwise_xor(row, k) * size, size)
         pairs.append((g_hbm, got.at[pl.ds(first, size)]))
     for c in chunks:
         part = slice(c, c + CHUNK)
-        pairs += [(rows_hbm.at[:, :, part], rows.at[:, :, part])]
         pairs += [(w_hbm.at[part], w.at[part]), (z_hbm.at[part], z.at[part])]
     reads = start_all(pairs, sems)
-    wait_all(reads[:4])
-    reads = reads[4:]
+    wait_all(reads[:5])
+    reads = reads[5:]
     wide = got[...].astype(f32)
     for u in range(UPDATES):
         for h in range(2):
             first = own * (2 * u + h)
             part = wide[:, first : first + own, :].reshape(sources * own, lanes)
-            steps[u, :, h * lanes : (h + 1) * lanes] = part.astype(bf16)
+            steps[u, h * lanes : (h + 1) * lanes, :] = part.T.astype(bf16)
     writes = []
     for n, c in enumerate(chunks):
         part = slice(c, c + CHUNK)
-        wait_all(reads[3 * n : 3 * n + 3])
+        changes = []
+        for u in range(UPDATES):
+            rows = one_hot(iota((CHUNK, slots.shape[1]), 0) + c == slots[u : u + 1, :])
+            changes.append(mm(rows, steps[u], 1, 0))
+        wait_all(reads[2 * n : 2 * n + 2])
         current, moving = w[part, :], z[part, :]
-        for u in range(UPDATES):
-            change = mm(steps[u], rows[u, :, part], 1, 0).T
+        for change in changes:
             current, moving = stepped(current, moving, change)
         w_new[part, :] = current
         z_new[part, :] = moving
@@ -430,23 +464,20 @@
     kept = [
         like((UPDATES, outputs, points)),
         like((UPDATES, outputs, count), f32),
-        like((UPDATES, rows * cap, points)),
-        like((UPDATES * rows, count), i32),
-        like((UPDATES * rows, 128), i32),
-        like((UPDATES, rank), i32),
+        like((8, 128), i32),
     ]
-    given = [block_index, pivot_index, coefficients, momentum, targets]
-    coef, offset, place, ids, starts, chosen = call(
-        functools.partial(prepare_kernel, count, cap, owners),
+    given = [block_index, coefficients, momentum, targets]
+    coef, offset, row_starts = call(
+        functools.partial(prepare_kernel, count, owners),
         kept,
         given + kept,
         *given,
-        sems=(5, 4 + 2 * UPDATES),
-    )
-    again, starts = lax.optimization_barrier((packed, starts))
+        sems=(4, 1 + 2 * UPDATES),
+    )
+    again, row_starts = lax.optimization_barrier((packed, row_starts))
     came.update({k: swap(again, "pts", k) for k in reversed(range(1, owners // 2))})
     feats = like((UPDATES, width, count))
-    inside_starts = pltpu.SMEM(starts.shape, i32)
+    inside_starts = pltpu.SMEM(row_starts.shape, i32)
     (mine,) = call(
         compact_kernel,
         [feats],
@@ -458,8 +489,9 @@
         ],
         packed,
         *[came[k] for k in range(1, owners)],
-        starts,
+        row_starts,
         sems=(owners + 1,),
+        grant=61,
     )
     beside, across = swap(mine, "rows", 1), swap(mine, "rows", 2)
     pieces = like((devices, deep, count // 2))
@@ -474,7 +506,17 @@
         sems=(4,),
         flops=2.0 * UPDATES * points * count * (2 * width + outputs),
     )
-    pieces, across = lax.optimization_barrier((pieces, across))
+    pieces, later_index = lax.optimization_barrier((pieces, block_index))
+    kept = [like((UPDATES * rows, count), i32), like((8, 128), i32), like((UPDATES, rank), i32)]
+    ids, starts, chosen = call(
+        functools.partial(order_kernel, count, points, owners),
+        kept,
+        [block_index, pivot_index, *kept],
+        later_index,
+        pivot_index,
+        sems=(3,),
+    )
+    pieces, across, ids = lax.optimization_barrier((pieces, across, ids))
     summed = lax.all_to_all(pieces, ("rows", "pts"), 0, 0, tiled=True)
     kept = [like((UPDATES, rank, block)), like((rows, block, count))]
     factor, cross = call(
@@ -493,7 +535,8 @@
         swap(across, "rows", 1),
         ids,
         chosen,
-        sems=(rows * rows + 1,),
+        sems=(rows * rows + 2,),
+        grant=61,
         flops=2.0 * width * block * (UPDATES * rank + block),
     )
     pieces = like((owners, deep, half * cap))
@@ -507,6 +550,15 @@
         cross,
         starts,
         sems=(2 * UPDATES + 2 + rows,),
+        grant=61,
+    )
+    steps, later_index = lax.optimization_barrier((steps, block_index))
+    (slots,) = call(
+        functools.partial(slots_kernel, count, points, cap),
+        [like((UPDATES, rows * cap), i32)],
+        [block_index, like((UPDATES, rows * cap), i32)],
+        later_index,
+        sems=(1,),
     )
     got = lax.all_to_all(steps, "pts", 0, 0, tiled=True)
     beside, across = swap(got, "rows", 1), swap(got, "rows", 2)
@@ -516,10 +568,10 @@
         [wide] * 2,
         [
             like((devices, deep, half * cap)),
+            slots,
             wide,
             wide,
-            place,
-            like((UPDATES, outputs, rows * cap)),
+            like((UPDATES, rows * cap, outputs)),
             wide,
             wide,
         ],
@@ -527,10 +579,11 @@
         beside,
         across,
         swap(across, "rows", 1),
+        slots,
         coefficients,
         momentum,
-        place,
-        sems=(rows + 3 * parts, 2 * parts),
+        sems=(1 + rows + 2 * parts, 2 * parts),
+        grant=61,
     )
 
 
@@ -599,7 +652,7 @@
     rows, owners = lax.axis_size("rows"), lax.axis_size("pts")
     count = block_index.shape[1] // rows
     fits = rows == 4 and owners == 8 and coefficients.shape[1] == 8 * rows * owners
-    fits = fits and coefficients.shape[0] % CHUNK == 0 and count % CHUNK == 0 and (3 * count // owners) % 64 == 0
+    fits = fits and coefficients.shape[0] % CHUNK == 0 and count % CHUNK == 0 and (3 * count // owners) % 64 == 0 and UPDATES * rows == 8
     plan = with_kernels if fits else with_operations
     return plan(
         features, targets, coefficients, momentum, block_index, pivot_index, nystrom_core

time: 95 us -> 97.2 us (1.023)
  waiting for transfers between devices: 21.1 us -> 14.9 us
  Pallas kernels: 37.7 us -> 42.9 us
  starting transfers between devices: 19.9 us -> 22.3 us
    ppermute x13, waiting for transfers between devices: 17.4 us -> 11.2 us  [swap(): lax.ppermute(value, axis, [(i, i ^ k) for i in range(lax.axis_size(axis))])]
    pallas_call x7 -> x9, Pallas kernels: 37.7 us -> 42.9 us  [call(): pl.pallas_call(body, out_shape=outs, in_specs=[VMEM] * near + [HBM] * (le...]
    ppermute x13, starting transfers between devices: 16 us -> 18.3 us  [swap(): lax.ppermute(value, axis, [(i, i ^ k) for i in range(lax.axis_size(axis))])]
    unnamed x32 -> x30, local copies, waits for them, and re-layouts: 3.44 us -> 4.04 us
  transfers between devices with their start and end apart: 14 -> 14, of which waited for: 10 -> 8; matrix products, arithmetic and copies ran while one was open for 0% -> 0% of each run, Pallas kernels for 22% -> 28%
where the time goes in v10:
time: 97.2 us; the launch traced here: 96.5 us
  Pallas kernels  42.9 us (44%)
  starting transfers between devices  22.3 us (23%)
  waiting for transfers between devices  14.9 us (15%)
  blocking collectives  11.4 us (12%)
  local copies, waits for them, and re-layouts  4.04 us (4%)
  between operations  0.99 us (1%)
    pallas_call x9, Pallas kernels, call(): pl.pallas_call(body, out_shape=outs, in_specs=[VMEM] * near + [HBM] * (le...  42.9 us
    ppermute x13, starting transfers between devices, swap(): lax.ppermute(value, axis, [(i, i ^ k) for i in range(lax.axis_size(axis))])  18.3 us
    all_to_all x1, blocking collectives, with_kernels(): got = lax.all_to_all(steps, 'pts', 0, 0, tiled=True)  11.4 us
    ppermute x13, waiting for transfers between devices, swap(): lax.ppermute(value, axis, [(i, i ^ k) for i in range(lax.axis_size(axis))])  11.2 us
    unnamed x30, local copies, waits for them, and re-layouts  4.04 us
    all_to_all x1, starting transfers between devices, with_kernels(): summed = lax.all_to_all(pieces, ('rows', 'pts'), 0, 0, tiled=True)  3.96 us
    all_to_all x1, waiting for transfers between devices, with_kernels(): summed = lax.all_to_all(pieces, ('rows', 'pts'), 0, 0, tiled=True)  3.69 us
  transfers between devices with their start and end apart: 14, of which 8 were waited for; matrix products, arithmetic and copies ran while one was open for 0% of the time, Pallas kernels for 28%

profile of v10, /device:TPU:0, one launch (start us, length us, event | category | flops | bytes accessed | tf_op | source)
XLA Modules:
  0.0 96.5 jit_solution(13162059523879474902)
XLA Ops:
  0.6 2.2 %shard_map.86.refs_0_ = bf16[384,128]{1,0:T(8,128)(2,1)} custom-call(s32[2,2048]{1,0:T(2,128)} %blocks_hbm.5, bf16[1024,128]{1,0:T(8,128)(2,1)} %feats_hbm.3), custom_call_target="tpu_custom_call" | custom-call | bytes 376832 | tf_op jit(solution)/shard_map/pallas_call | solution.py:423
  2.9 6.1 %collective-permute-start.6 = (bf16[384,128]{1,0:T(8,128)(2,1)}, bf16[384,128]{1,0:T(8,128)(2,1)S(1)}, u32[]{:S(2)}, u32[]{:S(2)}) collective-permute-start(bf16[384,128]{1,0:T(8,128)(2,1)} %shard_map.86.refs_0_), channel_id=1, source_target_pairs={{0,7},{1,6},{2,5},{3,4},{4,3},{5,2},{6,1},{7,0},{8,15},{9,14},{10,... | collective-permute-start | bytes 294920 | tf_op jit(solution)/shard_map/ppermute | solution.py:438
  9.0 0.2 collective-permute-start.5
  9.2 0.7 collective-permute-start.4
  9.9 2.0 %collective-permute-start.3 = (bf16[384,128]{1,0:T(8,128)(2,1)}, bf16[384,128]{1,0:T(8,128)(2,1)S(1)}, u32[]{:S(2)}, u32[]{:S(2)}) collective-permute-start(bf16[384,128]{1,0:T(8,128)(2,1)} %shard_map.86.refs_0_), channel_id=1, source_target_pairs={{0,4},{1,5},{2,6},{3,7},{4,0},{5,1},{6,2},{7,3},{8,12},{9,13},{10,... | collective-permute-start | bytes 294920 | tf_op jit(solution)/shard_map/ppermute | solution.py:438
  12.0 4.7 %shard_map.87 = (bf16[2,256,1024]{2,1,0:T(8,128)(2,1)}, f32[2,256,512]{2,1,0:T(8,128)}, s32[8,128]{1,0:T(8,128)}) custom-call(s32[2,2048]{1,0:T(2,128)} %blocks_hbm.5, f32[1024,256]{1,0:T(8,128)} %w_hbm.3, f32[1024,256]{1,0:T(8,128)} %z_hbm.3, bf16[1024,256]{1,0:T(8,128)(2,1)} %t_hbm.1), custom_call_target="tpu_custom_call" | custom-call | bytes 4739072 | tf_op jit(solution)/shard_map/pallas_call | solution.py:423
  16.6 2.4 %collective-permute-start.2 = (bf16[384,128]{1,0:T(8,128)(2,1)}, bf16[384,128]{1,0:T(8,128)(2,1)S(1)}, u32[]{:S(2)}, u32[]{:S(2)}) collective-permute-start(bf16[384,128]{1,0:T(8,128)(2,1)} %shard_map.86.refs_0_), channel_id=1, source_target_pairs={{0,3},{1,2},{2,1},{3,0},{4,7},{5,6},{6,5},{7,4},{8,11},{9,10},{10,... | collective-permute-start | bytes 294920 | tf_op jit(solution)/shard_map/ppermute | solution.py:438
  19.0 0.0 collective-permute-done.6.refs_7_
  19.0 0.0 copy-start.5
  19.0 2.2 %collective-permute-start.1 = (bf16[384,128]{1,0:T(8,128)(2,1)}, bf16[384,128]{1,0:T(8,128)(2,1)S(1)}, u32[]{:S(2)}, u32[]{:S(2)}) collective-permute-start(bf16[384,128]{1,0:T(8,128)(2,1)} %shard_map.86.refs_0_), channel_id=1, source_target_pairs={{0,2},{1,3},{2,0},{3,1},{4,6},{5,7},{6,4},{7,5},{8,10},{9,11},{10,... | collective-permute-start | bytes 294920 | tf_op jit(solution)/shard_map/ppermute | solution.py:438
  21.2 0.0 collective-permute-done.5.refs_6_
  21.2 0.0 copy-start.6
  21.2 1.4 %collective-permute-start = (bf16[384,128]{1,0:T(8,128)(2,1)}, bf16[384,128]{1,0:T(8,128)(2,1)S(1)}, u32[]{:S(2)}, u32[]{:S(2)}) collective-permute-start(bf16[384,128]{1,0:T(8,128)(2,1)} %shard_map.86.refs_0_), channel_id=1, source_target_pairs={{0,1},{1,0},{2,3},{3,2},{4,5},{5,4},{6,7},{7,6},{8,9},{9,8},{10,11... | collective-permute-start | bytes 294920 | tf_op jit(solution)/shard_map/ppermute | solution.py:438
  22.6 2.2 %collective-permute-done.4.refs_5_ = bf16[384,128]{1,0:T(8,128)(2,1)S(1)} collective-permute-done((bf16[384,128]{1,0:T(8,128)(2,1)}, bf16[384,128]{1,0:T(8,128)(2,1)S(1)}, u32[]{:S(2)}, u32[]{:S(2)}) %collective-permute-start.4) | collective-permute-done | bytes 98336 | tf_op jit(solution)/shard_map/ppermute | solution.py:438
  24.8 1.1 %collective-permute-done.3.refs_4_ = bf16[384,128]{1,0:T(8,128)(2,1)S(1)} collective-permute-done((bf16[384,128]{1,0:T(8,128)(2,1)}, bf16[384,128]{1,0:T(8,128)(2,1)S(1)}, u32[]{:S(2)}, u32[]{:S(2)}) %collective-permute-start.3) | collective-permute-done | bytes 98336 | tf_op jit(solution)/shard_map/ppermute | solution.py:438
  26.0 0.0 copy-start.8
  26.0 0.9 collective-permute-done.2.refs_3_
  26.8 0.0 copy-start.9
  26.8 1.1 %collective-permute-done.1.refs_2_ = bf16[384,128]{1,0:T(8,128)(2,1)S(1)} collective-permute-done((bf16[384,128]{1,0:T(8,128)(2,1)}, bf16[384,128]{1,0:T(8,128)(2,1)S(1)}, u32[]{:S(2)}, u32[]{:S(2)}) %collective-permute-start.1) | collective-permute-done | bytes 98336 | tf_op jit(solution)/shard_map/ppermute | solution.py:438
  27.9 0.0 copy-start.10
  27.9 0.0 collective-permute-done.refs_1_
  27.9 0.0 copy-done.5
  27.9 0.0 copy-done.6
  27.9 0.0 copy-done.7
  27.9 0.0 copy-done.8
  27.9 0.0 copy-done.9
  27.9 0.6 copy-done.10
  28.5 0.0 copy-start.11
  28.5 0.6 copy-done.11
  29.2 2.3 %shard_map.88.block_hbm.b0_hbm = bf16[2,128,512]{2,1,0:T(8,128)(2,1)} custom-call(bf16[384,128]{1,0:T(8,128)(2,1)} %shard_map.86.refs_0_, bf16[384,128]{1,0:T(8,128)(2,1)} %copy-done.11, bf16[384,128]{1,0:T(8,128)(2,1)} %copy-done.10, bf16[384,128]{1,0:T(8,128)(2,1)} %copy-done.9, bf16[384,128]{1,0:T(8,128)(2,1)} %copy-done.8, bf16[384,128]{1,0:T(8,128)(2,1)} %copy-done.7, ...), custom_call_target="tpu_custom_call" | custom-call | bytes 1052672 | tf_op jit(solution)/shard_map/pallas_call | solution.py:423
  31.4 1.6 %collective-permute-start.7 = (bf16[2,128,512]{2,1,0:T(8,128)(2,1)}, bf16[2,128,512]{2,1,0:T(8,128)(2,1)S(1)}, u32[]{:S(2)}, u32[]{:S(2)}) collective-permute-start(bf16[2,128,512]{2,1,0:T(8,128)(2,1)} %shard_map.88.block_hbm.b0_hbm), channel_id=1, source_target_pairs={{0,16},{8,24},{16,0},{24,8},{1,17},{9,25},{17,1},{25,9},{2,18},{10... | collective-permute-start | bytes 786440 | tf_op jit(solution)/shard_map/ppermute | solution.py:438
  33.0 3.5 %shard_map.89 = bf16[32,32,256]{2,1,0:T(8,128)(2,1)} custom-call(bf16[2,128,512]{2,1,0:T(8,128)(2,1)} %shard_map.88.block_hbm.b0_hbm, bf16[1024,128]{1,0:T(8,128)(2,1)} %feats_hbm.3, bf16[2,256,1024]{2,1,0:T(8,128)(2,1)} %get-tuple-element.22.coef_hbm, f32[2,256,512]{2,1,0:T(8,128)} %get-tuple-element.23.offset_hbm), custom_call_target="tpu_custom_call" | custom-call | flops 1073741824 | bytes 3145728 | tf_op jit(solution)/shard_map/pallas_call | solution.py:423
  36.5 4.4 %shard_map.90 = (s32[8,512]{1,0:T(8,128)}, s32[8,128]{1,0:T(8,128)}, s32[2,512]{1,0:T(2,128)}) custom-call(s32[2,2048]{1,0:T(2,128)} %blocks_hbm.5, s32[2,512]{1,0:T(2,128)} %pivots_hbm.1), custom_call_target="tpu_custom_call" | custom-call | bytes 45056 | tf_op jit(solution)/shard_map/pallas_call | solution.py:423
  41.0 0.0 collective-permute-done.7.b2_hbm
  41.0 0.0 copy-start.12
  41.0 4.0 %all-to-all-start = ((bf16[32,32,256]{2,1,0:T(8,128)(2,1)}), bf16[32,32,256]{2,1,0:T(8,128)(2,1)S(1)}, u32[]{:S(2)}, u32[]{:S(2)}) async-start(bf16[32,32,256]{2,1,0:T(8,128)(2,1)} %shard_map.89), calls=%async_computation | async-start | bytes 1048576 | tf_op jit(solution)/shard_map/all_to_all | solution.py:520
  45.0 0.1 collective-permute-start.8
  45.1 0.4 collective-permute-start.9
  45.6 1.2 %collective-permute-done.8.b1_hbm = bf16[2,128,512]{2,1,0:T(8,128)(2,1)S(1)} collective-permute-done((bf16[2,128,512]{2,1,0:T(8,128)(2,1)}, bf16[2,128,512]{2,1,0:T(8,128)(2,1)S(1)}, u32[]{:S(2)}, u32[]{:S(2)}) %collective-permute-start.8) | collective-permute-done | bytes 262176 | tf_op jit(solution)/shard_map/ppermute | solution.py:438
  46.8 0.0 copy-start.13
  46.8 0.2 collective-permute-done.9.b3_hbm
  47.0 0.0 copy-start.14
  47.0 0.0 copy-done.12
  47.0 0.5 copy-done.13
  47.5 0.1 copy-done.14
  47.6 9.8 %shard_map.91 = (bf16[2,512,2048]{2,1,0:T(8,128)(2,1)}, bf16[4,2048,512]{2,1,0:T(8,128)(2,1)}) custom-call(bf16[2,128,512]{2,1,0:T(8,128)(2,1)} %shard_map.88.block_hbm.b0_hbm, bf16[2,128,512]{2,1,0:T(8,128)(2,1)} %copy-done.13, bf16[2,128,512]{2,1,0:T(8,128)(2,1)} %copy-done.12, bf16[2,128,512]{2,1,0:T(8,128)(2,1)} %copy-done.14, ...), custom_call_target="tpu_custom_call" | custom-call | flops 1610612736 | bytes 13651968 | tf_op jit(solution)/shard_map/pallas_call | solution.py:423
  57.5 3.7 %all-to-all-done.summed_hbm = bf16[32,32,256]{2,1,0:T(8,128)(2,1)S(1)} async-done(((bf16[32,32,256]{2,1,0:T(8,128)(2,1)}), bf16[32,32,256]{2,1,0:T(8,128)(2,1)S(1)}, u32[]{:S(2)}, u32[]{:S(2)}) %all-to-all-start) | async-done | bytes 524320 | tf_op jit(solution)/shard_map/all_to_all | solution.py:520
  61.2 0.0 copy-start
  61.2 0.8 copy-done
  61.9 7.1 %shard_map.92 = bf16[8,32,384]{2,1,0:T(8,128)(2,1)} custom-call(bf16[32,32,256]{2,1,0:T(8,128)(2,1)} %copy-done, bf16[2,512,2048]{2,1,0:T(8,128)(2,1)} %get-tuple-element.31.factor_hbm, bf16[2,512,512]{2,1,0:T(8,128)(2,1)} %core_hbm.1, bf16[4,2048,512]{2,1,0:T(8,128)(2,1)} %get-tuple-element.32.cross_hbm, s32[8,128]{1,0:T(8,128)} %get-tuple-element.33.starts_hbm), custom_call_target="tpu_custom_call" | custom-call | bytes 14356480 | tf_op jit(solution)/shard_map/pallas_call | solution.py:423
  69.1 11.4 %all_to_all.10.g0_hbm = bf16[8,32,384]{2,1,0:T(8,128)(2,1)S(1)} all-to-all(bf16[8,32,384]{2,1,0:T(8,128)(2,1)} %shard_map.92), channel_id=1, replica_groups=mesh['rows'=4,'pts'=8] {'pts'}, dimensions={0} | all-to-all | bytes 393216 | tf_op jit(solution)/shard_map/all_to_all | solution.py:563
  80.5 1.2 %collective-permute-start.11 = (bf16[8,32,384]{2,1,0:T(8,128)(2,1)S(1)}, bf16[8,32,384]{2,1,0:T(8,128)(2,1)S(1)}, u32[]{:S(2)}, u32[]{:S(2)}) collective-permute-start(bf16[8,32,384]{2,1,0:T(8,128)(2,1)S(1)} %all_to_all.10.g0_hbm), channel_id=1, source_target_pairs={{0,16},{8,24},{16,0},{24,8},{1,17},{9,25},{17,1},{25,9},{2,18},{10... | collective-permute-start | bytes 589832 | tf_op jit(solution)/shard_map/ppermute | solution.py:438
  81.6 0.0 collective-permute-start.10
  81.6 4.5 %collective-permute-done.11.g2_hbm = bf16[8,32,384]{2,1,0:T(8,128)(2,1)S(1)} collective-permute-done((bf16[8,32,384]{2,1,0:T(8,128)(2,1)S(1)}, bf16[8,32,384]{2,1,0:T(8,128)(2,1)S(1)}, u32[]{:S(2)}, u32[]{:S(2)}) %collective-permute-start.11) | collective-permute-done | bytes 196640 | tf_op jit(solution)/shard_map/ppermute | solution.py:438
  86.1 0.0 collective-permute-start.12
  86.1 4.1 %shard_map.93.slots_hbm = s32[2,768]{1,0:T(2,128)} custom-call(s32[2,2048]{1,0:T(2,128)} %blocks_hbm.5), custom_call_target="tpu_custom_call" | custom-call | bytes 22528 | tf_op jit(solution)/shard_map/pallas_call | solution.py:423
  90.2 0.0 collective-permute-done.10.g1_hbm
  90.2 0.0 copy-start.3
  90.2 0.0 collective-permute-done.12.g3_hbm
  90.2 0.0 copy-done.1
  90.2 0.0 copy-done.2
  90.3 0.6 copy-done.3
  90.9 0.7 copy-done.4
  91.6 4.7 %shard_map.94 = (f32[1024,256]{1,0:T(8,128)}, f32[1024,256]{1,0:T(8,128)}) custom-call(bf16[8,32,384]{2,1,0:T(8,128)(2,1)} %copy-done.1, bf16[8,32,384]{2,1,0:T(8,128)(2,1)} %copy-done.3, bf16[8,32,384]{2,1,0:T(8,128)(2,1)} %copy-done.2, bf16[8,32,384]{2,1,0:T(8,128)(2,1)} %copy-done.4, s32[2,768]{1,0:T(2,128)} %shard_map.93.slots_hbm, f32[1024,256]{1,0:T(8,128)} %w_hbm.3, ...), custom_call_target="tpu_custom_call" | custom-call | bytes 4986880 | tf_op jit(solution)/shard_map/pallas_call | solution.py:423
  (4 shorter events, 0.0 us)
Async XLA Ops:
  2.9 16.1 %collective-permute-start.6 = (bf16[384,128]{1,0:T(8,128)(2,1)}, bf16[384,128]{1,0:T(8,128)(2,1)S(1)}, u32[]{:S(2)}, u32[]{:S(2)}) collective-permute-start(bf16[384,128]{1,0:T(8,128)(2,1)} %shard_map.86.refs_0_), channel_id=1, source_target_pairs={{0,7},{1,6},{2,5},{3,4},{4,3},{5,2},{6,1},{7,0},{8,15},{9,14},{10,... | collective-permute-start | bytes 294920 | tf_op jit(solution)/shard_map/ppermute | solution.py:438
  9.0 12.2 %collective-permute-start.5 = (bf16[384,128]{1,0:T(8,128)(2,1)}, bf16[384,128]{1,0:T(8,128)(2,1)S(1)}, u32[]{:S(2)}, u32[]{:S(2)}) collective-permute-start(bf16[384,128]{1,0:T(8,128)(2,1)} %shard_map.86.refs_0_), channel_id=1, source_target_pairs={{0,6},{1,7},{2,4},{3,5},{4,2},{5,3},{6,0},{7,1},{8,14},{9,15},{10,... | collective-permute-start | bytes 294920 | tf_op jit(solution)/shard_map/ppermute | solution.py:438
  9.2 15.6 %collective-permute-start.4 = (bf16[384,128]{1,0:T(8,128)(2,1)}, bf16[384,128]{1,0:T(8,128)(2,1)S(1)}, u32[]{:S(2)}, u32[]{:S(2)}) collective-permute-start(bf16[384,128]{1,0:T(8,128)(2,1)} %shard_map.86.refs_0_), channel_id=1, source_target_pairs={{0,5},{1,4},{2,7},{3,6},{4,1},{5,0},{6,3},{7,2},{8,13},{9,12},{10,... | collective-permute-start | bytes 294920 | tf_op jit(solution)/shard_map/ppermute | solution.py:438
  9.9 16.0 %collective-permute-start.3 = (bf16[384,128]{1,0:T(8,128)(2,1)}, bf16[384,128]{1,0:T(8,128)(2,1)S(1)}, u32[]{:S(2)}, u32[]{:S(2)}) collective-permute-start(bf16[384,128]{1,0:T(8,128)(2,1)} %shard_map.86.refs_0_), channel_id=1, source_target_pairs={{0,4},{1,5},{2,6},{3,7},{4,0},{5,1},{6,2},{7,3},{8,12},{9,13},{10,... | collective-permute-start | bytes 294920 | tf_op jit(solution)/shard_map/ppermute | solution.py:438
  16.6 10.2 %collective-permute-start.2 = (bf16[384,128]{1,0:T(8,128)(2,1)}, bf16[384,128]{1,0:T(8,128)(2,1)S(1)}, u32[]{:S(2)}, u32[]{:S(2)}) collective-permute-start(bf16[384,128]{1,0:T(8,128)(2,1)} %shard_map.86.refs_0_), channel_id=1, source_target_pairs={{0,3},{1,2},{2,1},{3,0},{4,7},{5,6},{6,5},{7,4},{8,11},{9,10},{10,... | collective-permute-start | bytes 294920 | tf_op jit(solution)/shard_map/ppermute | solution.py:438
  19.0 8.9 %copy-start.5 = (bf16[384,128]{1,0:T(8,128)(2,1)}, bf16[384,128]{1,0:T(8,128)(2,1)S(1)}, u32[]{:S(2)}) copy-start(bf16[384,128]{1,0:T(8,128)(2,1)S(1)} %collective-permute-done.6.refs_7_) | copy-start | bytes 294916
  19.0 8.9 %collective-permute-start.1 = (bf16[384,128]{1,0:T(8,128)(2,1)}, bf16[384,128]{1,0:T(8,128)(2,1)S(1)}, u32[]{:S(2)}, u32[]{:S(2)}) collective-permute-start(bf16[384,128]{1,0:T(8,128)(2,1)} %shard_map.86.refs_0_), channel_id=1, source_target_pairs={{0,2},{1,3},{2,0},{3,1},{4,6},{5,7},{6,4},{7,5},{8,10},{9,11},{10,... | collective-permute-start | bytes 294920 | tf_op jit(solution)/shard_map/ppermute | solution.py:438
  21.2 6.7 %copy-start.6 = (bf16[384,128]{1,0:T(8,128)(2,1)}, bf16[384,128]{1,0:T(8,128)(2,1)S(1)}, u32[]{:S(2)}) copy-start(bf16[384,128]{1,0:T(8,128)(2,1)S(1)} %collective-permute-done.5.refs_6_) | copy-start | bytes 294916
  21.2 6.7 %collective-permute-start = (bf16[384,128]{1,0:T(8,128)(2,1)}, bf16[384,128]{1,0:T(8,128)(2,1)S(1)}, u32[]{:S(2)}, u32[]{:S(2)}) collective-permute-start(bf16[384,128]{1,0:T(8,128)(2,1)} %shard_map.86.refs_0_), channel_id=1, source_target_pairs={{0,1},{1,0},{2,3},{3,2},{4,5},{5,4},{6,7},{7,6},{8,9},{9,8},{10,11... | collective-permute-start | bytes 294920 | tf_op jit(solution)/shard_map/ppermute | solution.py:438
  24.8 3.1 %copy-start.7 = (bf16[384,128]{1,0:T(8,128)(2,1)}, bf16[384,128]{1,0:T(8,128)(2,1)S(1)}, u32[]{:S(2)}) copy-start(bf16[384,128]{1,0:T(8,128)(2,1)S(1)} %collective-permute-done.4.refs_5_) | copy-start | bytes 294916
  26.0 2.0 %copy-start.8 = (bf16[384,128]{1,0:T(8,128)(2,1)}, bf16[384,128]{1,0:T(8,128)(2,1)S(1)}, u32[]{:S(2)}) copy-start(bf16[384,128]{1,0:T(8,128)(2,1)S(1)} %collective-permute-done.3.refs_4_) | copy-start | bytes 294916
  26.8 1.1 %copy-start.9 = (bf16[384,128]{1,0:T(8,128)(2,1)}, bf16[384,128]{1,0:T(8,128)(2,1)S(1)}, u32[]{:S(2)}) copy-start(bf16[384,128]{1,0:T(8,128)(2,1)S(1)} %collective-permute-done.2.refs_3_) | copy-start | bytes 294916
  27.9 0.6 copy-start.10
  28.5 0.6 copy-start.11
  31.4 9.6 %collective-permute-start.7 = (bf16[2,128,512]{2,1,0:T(8,128)(2,1)}, bf16[2,128,512]{2,1,0:T(8,128)(2,1)S(1)}, u32[]{:S(2)}, u32[]{:S(2)}) collective-permute-start(bf16[2,128,512]{2,1,0:T(8,128)(2,1)} %shard_map.88.block_hbm.b0_hbm), channel_id=1, source_target_pairs={{0,16},{8,24},{16,0},{24,8},{1,17},{9,25},{17,1},{25,9},{2,18},{10... | collective-permute-start | bytes 786440 | tf_op jit(solution)/shard_map/ppermute | solution.py:438
  41.0 6.0 %copy-start.12 = (bf16[2,128,512]{2,1,0:T(8,128)(2,1)}, bf16[2,128,512]{2,1,0:T(8,128)(2,1)S(1)}, u32[]{:S(2)}) copy-start(bf16[2,128,512]{2,1,0:T(8,128)(2,1)S(1)} %collective-permute-done.7.b2_hbm) | copy-start | bytes 786436
  41.0 20.1 %all-to-all-start = ((bf16[32,32,256]{2,1,0:T(8,128)(2,1)}), bf16[32,32,256]{2,1,0:T(8,128)(2,1)S(1)}, u32[]{:S(2)}, u32[]{:S(2)}) async-start(bf16[32,32,256]{2,1,0:T(8,128)(2,1)} %shard_map.89), calls=%async_computation | async-start | bytes 1048576 | tf_op jit(solution)/shard_map/all_to_all | solution.py:520
  45.0 1.8 %collective-permute-start.8 = (bf16[2,128,512]{2,1,0:T(8,128)(2,1)}, bf16[2,128,512]{2,1,0:T(8,128)(2,1)S(1)}, u32[]{:S(2)}, u32[]{:S(2)}) collective-permute-start(bf16[2,128,512]{2,1,0:T(8,128)(2,1)} %shard_map.88.block_hbm.b0_hbm), channel_id=1, source_target_pairs={{0,8},{8,0},{16,24},{24,16},{1,9},{9,1},{17,25},{25,17},{2,10},{10... | collective-permute-start | bytes 786440 | tf_op jit(solution)/shard_map/ppermute | solution.py:438
  45.1 1.8 %collective-permute-start.9 = (bf16[2,128,512]{2,1,0:T(8,128)(2,1)S(1)}, bf16[2,128,512]{2,1,0:T(8,128)(2,1)S(1)}, u32[]{:S(2)}, u32[]{:S(2)}) collective-permute-start(bf16[2,128,512]{2,1,0:T(8,128)(2,1)S(1)} %collective-permute-done.7.b2_hbm), channel_id=1, source_target_pairs={{0,8},{8,0},{16,24},{24,16},{1,9},{9,1},{17,25},{25,17},{2,10},{10... | collective-permute-start | bytes 786440 | tf_op jit(solution)/shard_map/ppermute | solution.py:438
  46.8 0.7 copy-start.13
  47.0 0.7 copy-start.14
  61.2 0.8 copy-start
  80.5 9.8 %copy-start.1 = (bf16[8,32,384]{2,1,0:T(8,128)(2,1)}, bf16[8,32,384]{2,1,0:T(8,128)(2,1)S(1)}, u32[]{:S(2)}) copy-start(bf16[8,32,384]{2,1,0:T(8,128)(2,1)S(1)} %all_to_all.10.g0_hbm) | copy-start | bytes 589828
  80.5 5.7 %collective-permute-start.11 = (bf16[8,32,384]{2,1,0:T(8,128)(2,1)S(1)}, bf16[8,32,384]{2,1,0:T(8,128)(2,1)S(1)}, u32[]{:S(2)}, u32[]{:S(2)}) collective-permute-start(bf16[8,32,384]{2,1,0:T(8,128)(2,1)S(1)} %all_to_all.10.g0_hbm), channel_id=1, source_target_pairs={{0,16},{8,24},{16,0},{24,8},{1,17},{9,25},{17,1},{25,9},{2,18},{10... | collective-permute-start | bytes 589832 | tf_op jit(solution)/shard_map/ppermute | solution.py:438
  81.6 8.6 %collective-permute-start.10 = (bf16[8,32,384]{2,1,0:T(8,128)(2,1)S(1)}, bf16[8,32,384]{2,1,0:T(8,128)(2,1)S(1)}, u32[]{:S(2)}, u32[]{:S(2)}) collective-permute-start(bf16[8,32,384]{2,1,0:T(8,128)(2,1)S(1)} %all_to_all.10.g0_hbm), channel_id=1, source_target_pairs={{0,8},{8,0},{16,24},{24,16},{1,9},{9,1},{17,25},{25,17},{2,10},{10... | collective-permute-start | bytes 589832 | tf_op jit(solution)/shard_map/ppermute | solution.py:438
  86.1 4.1 %copy-start.2 = (bf16[8,32,384]{2,1,0:T(8,128)(2,1)}, bf16[8,32,384]{2,1,0:T(8,128)(2,1)S(1)}, u32[]{:S(2)}) copy-start(bf16[8,32,384]{2,1,0:T(8,128)(2,1)S(1)} %collective-permute-done.11.g2_hbm) | copy-start | bytes 589828
  86.1 4.1 %collective-permute-start.12 = (bf16[8,32,384]{2,1,0:T(8,128)(2,1)S(1)}, bf16[8,32,384]{2,1,0:T(8,128)(2,1)S(1)}, u32[]{:S(2)}, u32[]{:S(2)}) collective-permute-start(bf16[8,32,384]{2,1,0:T(8,128)(2,1)S(1)} %collective-permute-done.11.g2_hbm), channel_id=1, source_target_pairs={{0,8},{8,0},{16,24},{24,16},{1,9},{9,1},{17,25},{25,17},{2,10},{10... | collective-permute-start | bytes 589832 | tf_op jit(solution)/shard_map/ppermute | solution.py:438
  90.2 0.7 copy-start.3
  90.9 0.7 copy-start.4

commit v11 on v10

--- a/solution.py
+++ b/solution.py
@@ -251,7 +251,6 @@
     block_hbm, feats_hbm, coef_hbm, offset_hbm, pieces_hbm,
     block, feats, coef, offset, tile, pieces, sems,
 ):
-    points, count = tile.shape
     outputs = coef.shape[1]
     pairs = [(block_hbm, block), (feats_hbm, feats), (coef_hbm, coef), (offset_hbm, offset)]
     reads = start_all(pairs, sems)
@@ -259,8 +258,7 @@
     left = extended(feats[...], 1, True)
     for u in range(UPDATES):
         right = extended(block[u], 0, False)
-        for c in range(0, points, CHUNK):
-            tile[c : c + CHUNK, :] = jnp.exp2(exponent(left[c : c + CHUNK], right)).astype(bf16)
+        tile[...] = jnp.exp2(exponent(left, right)).astype(bf16)
         if u == 0:
             wait_all(reads[2:])
         total = offset[u] + mm(coef[u], tile[...], 1, 0)
@@ -295,18 +293,19 @@
             value = jnp.exp2(exponent(left, rights[u][k]))
             factor[u, :, pl.ds(start, count)] = value.astype(bf16)
     writes = start_all([(factor, factor_hbm)], sems)
+    lefts, left_points = [], []
+    for k in range(groups):
+        lefts.append(extended(feats[k, 0].astype(f32).T, 1, True))
+        points = ids[pl.ds(places[k], 1), :].astype(f32)
+        left_points.append(jnp.broadcast_to(points, (8, count)).T[:, 0:1])
+    left, left_points = jnp.concatenate(lefts, axis=0), jnp.concatenate(left_points, axis=0)
     sent = 1
-    for k in range(groups):
-        left = extended(feats[k, 0].astype(f32).T, 1, True)
-        left_points = ids[pl.ds(places[k], 1), :].astype(f32)
-        left_points = jnp.broadcast_to(left_points, (8, count)).T[:, 0:1]
-        for m in range(groups):
-            right_points = ids[pl.ds(groups + places[m], 1), :].astype(f32)
-            for c in range(0, count, CHUNK):
-                rows = slice(c, c + CHUNK)
-                power = exponent(left[rows], rights[1][m])
-                power = jnp.where(left_points[rows] == right_points, math.log2(1.0 + ridge_term), power)
-                cross[m, k, rows, :] = jnp.exp2(power).astype(bf16)
+    for m in range(groups):
+        right_points = ids[pl.ds(groups + places[m], 1), :].astype(f32)
+        power = exponent(left, rights[1][m])
+        power = jnp.where(left_points == right_points, math.log2(1.0 + ridge_term), power)
+        cross[m] = jnp.exp2(power).astype(bf16).reshape(groups, count, count)
+        for k in range(groups):
             start = pl.multiple_of(places[k] * count, count)
             copy = pltpu.make_async_copy(
                 cross.at[m, k], cross_hbm.at[places[m], pl.ds(start, count), :], sems.at[sent]
@@ -389,17 +388,17 @@
             first = own * (2 * u + h)
             part = wide[:, first : first + own, :].reshape(sources * own, lanes)
             steps[u, h * lanes : (h + 1) * lanes, :] = part.T.astype(bf16)
+    changes = []
+    for u in range(UPDATES):
+        rows = one_hot(iota((points, slots.shape[1]), 0) == slots[u : u + 1, :])
+        changes.append(mm(rows, steps[u], 1, 0))
     writes = []
     for n, c in enumerate(chunks):
         part = slice(c, c + CHUNK)
-        changes = []
-        for u in range(UPDATES):
-            rows = one_hot(iota((CHUNK, slots.shape[1]), 0) + c == slots[u : u + 1, :])
-            changes.append(mm(rows, steps[u], 1, 0))
         wait_all(reads[2 * n : 2 * n + 2])
         current, moving = w[part, :], z[part, :]
         for change in changes:
-            current, moving = stepped(current, moving, change)
+            current, moving = stepped(current, moving, change[part])
         w_new[part, :] = current
         z_new[part, :] = moving
         for m, (a, b) in enumerate(((w_new, w_out), (z_new, z_out))):
@@ -460,7 +459,7 @@
         features,
         sems=(2,),
     )
-    came = {k: swap(packed, "pts", k) for k in reversed(range(owners // 2, owners))}
+    came = {k: swap(packed, "pts", k) for k in reversed(range(1, owners))}
     kept = [
         like((UPDATES, outputs, points)),
         like((UPDATES, outputs, count), f32),
@@ -474,8 +473,6 @@
         *given,
         sems=(4, 1 + 2 * UPDATES),
     )
-    again, row_starts = lax.optimization_barrier((packed, row_starts))
-    came.update({k: swap(again, "pts", k) for k in reversed(range(1, owners // 2))})
     feats = like((UPDATES, width, count))
     inside_starts = pltpu.SMEM(row_starts.shape, i32)
     (mine,) = call(
@@ -561,6 +558,7 @@
         sems=(1,),
     )
     got = lax.all_to_all(steps, "pts", 0, 0, tiled=True)
+    got, slots = lax.optimization_barrier((got, slots))
     beside, across = swap(got, "rows", 1), swap(got, "rows", 2)
     parts = points // CHUNK
     return call(

time: 97.2 us -> 92 us (0.947)
  blocking collectives: 11.4 us -> 0 us
  starting transfers between devices: 22.3 us -> 30.4 us
  local copies, waits for them, and re-layouts: 4.04 us -> 2.84 us
    all_to_all x1 -> x0, blocking collectives: 11.4 us -> none  [with_kernels(): got = lax.all_to_all(steps, 'pts', 0, 0, tiled=True)]
    ppermute x13, starting transfers between devices: 18.3 us -> 22.4 us  [swap(): lax.ppermute(value, axis, [(i, i ^ k) for i in range(lax.axis_size(axis))])]
    ppermute x13, waiting for transfers between devices: 11.2 us -> 7.47 us  [swap(): lax.ppermute(value, axis, [(i, i ^ k) for i in range(lax.axis_size(axis))])]
    all_to_all x0 -> x1, waiting for transfers between devices: none -> 3.71 us  [with_kernels(): got = lax.all_to_all(steps, 'pts', 0, 0, tiled=True)]
    all_to_all x0 -> x1, starting transfers between devices: none -> 3.62 us  [with_kernels(): got = lax.all_to_all(steps, 'pts', 0, 0, tiled=True)]
    unnamed x30, local copies, waits for them, and re-layouts: 4.04 us -> 2.84 us
  transfers between devices with their start and end apart: 14 -> 15, of which waited for: 8 -> 7; matrix products, arithmetic and copies ran while one was open for 0% -> 0% of each run, Pallas kernels for 28% -> 29%
where the time goes in v11:
time: 92 us; the launch traced here: 91.3 us
  Pallas kernels  42.6 us (46%)
  starting transfers between devices  30.4 us (33%)
  waiting for transfers between devices  14.5 us (16%)
  local copies, waits for them, and re-layouts  2.84 us (3%)
  between operations  1.01 us (1%)
    pallas_call x9, Pallas kernels, call(): pl.pallas_call(body, out_shape=outs, in_specs=[VMEM] * near + [HBM] * (le...  42.6 us
    ppermute x13, starting transfers between devices, swap(): lax.ppermute(value, axis, [(i, i ^ k) for i in range(lax.axis_size(axis))])  22.4 us
    ppermute x13, waiting for transfers between devices, swap(): lax.ppermute(value, axis, [(i, i ^ k) for i in range(lax.axis_size(axis))])  7.47 us
    all_to_all x1, starting transfers between devices, with_kernels(): summed = lax.all_to_all(pieces, ('rows', 'pts'), 0, 0, tiled=True)  4.3 us
    all_to_all x1, waiting for transfers between devices, with_kernels(): got = lax.all_to_all(steps, 'pts', 0, 0, tiled=True)  3.71 us
    all_to_all x1, starting transfers between devices, with_kernels(): got = lax.all_to_all(steps, 'pts', 0, 0, tiled=True)  3.62 us
    all_to_all x1, waiting for transfers between devices, with_kernels(): summed = lax.all_to_all(pieces, ('rows', 'pts'), 0, 0, tiled=True)  3.34 us
    unnamed x30, local copies, waits for them, and re-layouts  2.84 us
  transfers between devices with their start and end apart: 15, of which 7 were waited for; matrix products, arithmetic and copies ran while one was open for 0% of the time, Pallas kernels for 29%

profile of v11, /device:TPU:0, one launch (start us, length us, event | category | flops | bytes accessed | tf_op | source)
XLA Modules:
  0.0 91.3 jit_solution(8162374311386608029)
XLA Ops:
  0.6 2.2 %shard_map.86.refs_0_ = bf16[384,128]{1,0:T(8,128)(2,1)} custom-call(s32[2,2048]{1,0:T(2,128)} %blocks_hbm.5, bf16[1024,128]{1,0:T(8,128)(2,1)} %feats_hbm.3), custom_call_target="tpu_custom_call" | custom-call | bytes 376832 | tf_op jit(solution)/shard_map/pallas_call | solution.py:422
  2.9 6.1 %collective-permute-start.6 = (bf16[384,128]{1,0:T(8,128)(2,1)}, bf16[384,128]{1,0:T(8,128)(2,1)S(1)}, u32[]{:S(2)}, u32[]{:S(2)}) collective-permute-start(bf16[384,128]{1,0:T(8,128)(2,1)} %shard_map.86.refs_0_), channel_id=1, source_target_pairs={{0,7},{1,6},{2,5},{3,4},{4,3},{5,2},{6,1},{7,0},{8,15},{9,14},{10,... | collective-permute-start | bytes 294920 | tf_op jit(solution)/shard_map/ppermute | solution.py:437
  9.0 0.2 collective-permute-start.5
  9.2 0.7 collective-permute-start.4
  9.9 2.0 %collective-permute-start.3 = (bf16[384,128]{1,0:T(8,128)(2,1)}, bf16[384,128]{1,0:T(8,128)(2,1)S(1)}, u32[]{:S(2)}, u32[]{:S(2)}) collective-permute-start(bf16[384,128]{1,0:T(8,128)(2,1)} %shard_map.86.refs_0_), channel_id=1, source_target_pairs={{0,4},{1,5},{2,6},{3,7},{4,0},{5,1},{6,2},{7,3},{8,12},{9,13},{10,... | collective-permute-start | bytes 294920 | tf_op jit(solution)/shard_map/ppermute | solution.py:437
  12.0 2.3 %collective-permute-start.2 = (bf16[384,128]{1,0:T(8,128)(2,1)}, bf16[384,128]{1,0:T(8,128)(2,1)S(1)}, u32[]{:S(2)}, u32[]{:S(2)}) collective-permute-start(bf16[384,128]{1,0:T(8,128)(2,1)} %shard_map.86.refs_0_), channel_id=1, source_target_pairs={{0,3},{1,2},{2,1},{3,0},{4,7},{5,6},{6,5},{7,4},{8,11},{9,10},{10,... | collective-permute-start | bytes 294920 | tf_op jit(solution)/shard_map/ppermute | solution.py:437
  14.2 0.0 collective-permute-done.6.refs_7_
  14.2 0.0 copy-start.5
  14.3 6.8 %collective-permute-start.1 = (bf16[384,128]{1,0:T(8,128)(2,1)}, bf16[384,128]{1,0:T(8,128)(2,1)S(1)}, u32[]{:S(2)}, u32[]{:S(2)}) collective-permute-start(bf16[384,128]{1,0:T(8,128)(2,1)} %shard_map.86.refs_0_), channel_id=1, source_target_pairs={{0,2},{1,3},{2,0},{3,1},{4,6},{5,7},{6,4},{7,5},{8,10},{9,11},{10,... | collective-permute-start | bytes 294920 | tf_op jit(solution)/shard_map/ppermute | solution.py:437
  21.0 0.0 collective-permute-done.5.refs_6_
  21.0 0.0 copy-start.6
  21.0 1.0 %collective-permute-start = (bf16[384,128]{1,0:T(8,128)(2,1)}, bf16[384,128]{1,0:T(8,128)(2,1)S(1)}, u32[]{:S(2)}, u32[]{:S(2)}) collective-permute-start(bf16[384,128]{1,0:T(8,128)(2,1)} %shard_map.86.refs_0_), channel_id=1, source_target_pairs={{0,1},{1,0},{2,3},{3,2},{4,5},{5,4},{6,7},{7,6},{8,9},{9,8},{10,11... | collective-permute-start | bytes 294920 | tf_op jit(solution)/shard_map/ppermute | solution.py:437
  22.0 4.7 %shard_map.87 = (bf16[2,256,1024]{2,1,0:T(8,128)(2,1)}, f32[2,256,512]{2,1,0:T(8,128)}, s32[8,128]{1,0:T(8,128)}) custom-call(s32[2,2048]{1,0:T(2,128)} %blocks_hbm.5, f32[1024,256]{1,0:T(8,128)} %w_hbm.3, f32[1024,256]{1,0:T(8,128)} %z_hbm.3, bf16[1024,256]{1,0:T(8,128)(2,1)} %t_hbm.1), custom_call_target="tpu_custom_call" | custom-call | bytes 4739072 | tf_op jit(solution)/shard_map/pallas_call | solution.py:422
  26.7 0.0 collective-permute-done.4.refs_5_
  26.7 0.0 copy-start.7
  26.7 0.0 collective-permute-done.3.refs_4_
  26.7 0.0 copy-start.8
  26.7 0.0 collective-permute-done.2.refs_3_
  26.7 0.0 copy-start.9
  26.8 0.2 collective-permute-done.1.refs_2_
  26.9 0.0 copy-start.10
  26.9 0.0 collective-permute-done.refs_1_
  26.9 0.0 copy-start.11
  26.9 0.0 copy-done.5
  26.9 0.0 copy-done.6
  26.9 0.4 copy-done.7
  27.3 0.1 copy-done.8
  27.4 0.0 copy-done.9
  27.4 0.1 copy-done.10
  27.5 0.0 copy-done.11
  27.6 2.3 %shard_map.88.block_hbm.b0_hbm = bf16[2,128,512]{2,1,0:T(8,128)(2,1)} custom-call(bf16[384,128]{1,0:T(8,128)(2,1)} %shard_map.86.refs_0_, bf16[384,128]{1,0:T(8,128)(2,1)} %copy-done.11, bf16[384,128]{1,0:T(8,128)(2,1)} %copy-done.10, bf16[384,128]{1,0:T(8,128)(2,1)} %copy-done.9, bf16[384,128]{1,0:T(8,128)(2,1)} %copy-done.8, bf16[384,128]{1,0:T(8,128)(2,1)} %copy-done.7, ...), custom_call_target="tpu_custom_call" | custom-call | bytes 1052672 | tf_op jit(solution)/shard_map/pallas_call | solution.py:422
  29.9 1.6 %collective-permute-start.7 = (bf16[2,128,512]{2,1,0:T(8,128)(2,1)}, bf16[2,128,512]{2,1,0:T(8,128)(2,1)S(1)}, u32[]{:S(2)}, u32[]{:S(2)}) collective-permute-start(bf16[2,128,512]{2,1,0:T(8,128)(2,1)} %shard_map.88.block_hbm.b0_hbm), channel_id=1, source_target_pairs={{0,16},{8,24},{16,0},{24,8},{1,17},{9,25},{17,1},{25,9},{2,18},{10... | collective-permute-start | bytes 786440 | tf_op jit(solution)/shard_map/ppermute | solution.py:437
  31.4 3.6 %shard_map.89 = bf16[32,32,256]{2,1,0:T(8,128)(2,1)} custom-call(bf16[2,128,512]{2,1,0:T(8,128)(2,1)} %shard_map.88.block_hbm.b0_hbm, bf16[1024,128]{1,0:T(8,128)(2,1)} %feats_hbm.3, bf16[2,256,1024]{2,1,0:T(8,128)(2,1)} %get-tuple-element.20.coef_hbm, f32[2,256,512]{2,1,0:T(8,128)} %get-tuple-element.21.offset_hbm), custom_call_target="tpu_custom_call" | custom-call | flops 1073741824 | bytes 3145728 | tf_op jit(solution)/shard_map/pallas_call | solution.py:422
  35.0 4.4 %shard_map.90 = (s32[8,512]{1,0:T(8,128)}, s32[8,128]{1,0:T(8,128)}, s32[2,512]{1,0:T(2,128)}) custom-call(s32[2,2048]{1,0:T(2,128)} %blocks_hbm.5, s32[2,512]{1,0:T(2,128)} %pivots_hbm.1), custom_call_target="tpu_custom_call" | custom-call | bytes 45056 | tf_op jit(solution)/shard_map/pallas_call | solution.py:422
  39.4 0.0 collective-permute-done.7.b2_hbm
  39.4 0.0 copy-start.12
  39.5 4.3 %all-to-all-start = ((bf16[32,32,256]{2,1,0:T(8,128)(2,1)}), bf16[32,32,256]{2,1,0:T(8,128)(2,1)S(1)}, u32[]{:S(2)}, u32[]{:S(2)}) async-start(bf16[32,32,256]{2,1,0:T(8,128)(2,1)} %shard_map.89), calls=%async_computation | async-start | bytes 1048576 | tf_op jit(solution)/shard_map/all_to_all | solution.py:517
  43.8 0.1 collective-permute-start.8
  43.9 0.4 collective-permute-start.9
  44.3 1.2 %collective-permute-done.8.b1_hbm = bf16[2,128,512]{2,1,0:T(8,128)(2,1)S(1)} collective-permute-done((bf16[2,128,512]{2,1,0:T(8,128)(2,1)}, bf16[2,128,512]{2,1,0:T(8,128)(2,1)S(1)}, u32[]{:S(2)}, u32[]{:S(2)}) %collective-permute-start.8) | collective-permute-done | bytes 262176 | tf_op jit(solution)/shard_map/ppermute | solution.py:437
  45.6 0.2 collective-permute-done.9.b3_hbm
  45.7 0.0 copy-done.12
  45.7 0.5 copy-done.13
  46.3 0.2 copy-done.14
  46.4 10.2 %shard_map.91 = (bf16[2,512,2048]{2,1,0:T(8,128)(2,1)}, bf16[4,2048,512]{2,1,0:T(8,128)(2,1)}) custom-call(bf16[2,128,512]{2,1,0:T(8,128)(2,1)} %shard_map.88.block_hbm.b0_hbm, bf16[2,128,512]{2,1,0:T(8,128)(2,1)} %copy-done.13, bf16[2,128,512]{2,1,0:T(8,128)(2,1)} %copy-done.12, bf16[2,128,512]{2,1,0:T(8,128)(2,1)} %copy-done.14, ...), custom_call_target="tpu_custom_call" | custom-call | flops 1610612736 | bytes 13651968 | tf_op jit(solution)/shard_map/pallas_call | solution.py:422
  56.6 3.3 %all-to-all-done.summed_hbm = bf16[32,32,256]{2,1,0:T(8,128)(2,1)S(1)} async-done(((bf16[32,32,256]{2,1,0:T(8,128)(2,1)}), bf16[32,32,256]{2,1,0:T(8,128)(2,1)S(1)}, u32[]{:S(2)}, u32[]{:S(2)}) %all-to-all-start) | async-done | bytes 524320 | tf_op jit(solution)/shard_map/all_to_all | solution.py:517
  59.9 0.8 copy-done
  60.7 7.1 %shard_map.92 = bf16[8,32,384]{2,1,0:T(8,128)(2,1)} custom-call(bf16[32,32,256]{2,1,0:T(8,128)(2,1)} %copy-done, bf16[2,512,2048]{2,1,0:T(8,128)(2,1)} %get-tuple-element.29.factor_hbm, bf16[2,512,512]{2,1,0:T(8,128)(2,1)} %core_hbm.1, bf16[4,2048,512]{2,1,0:T(8,128)(2,1)} %get-tuple-element.30.cross_hbm, s32[8,128]{1,0:T(8,128)} %get-tuple-element.31.starts_hbm), custom_call_target="tpu_custom_call" | custom-call | bytes 14356480 | tf_op jit(solution)/shard_map/pallas_call | solution.py:422
  67.8 3.6 %all-to-all-start.1 = ((bf16[8,32,384]{2,1,0:T(8,128)(2,1)}), bf16[8,32,384]{2,1,0:T(8,128)(2,1)S(1)}, u32[]{:S(2)}, u32[]{:S(2)}) async-start(bf16[8,32,384]{2,1,0:T(8,128)(2,1)} %shard_map.92), calls=%async_computation.1 | async-start | bytes 393216 | tf_op jit(solution)/shard_map/all_to_all | solution.py:560
  71.5 4.1 %shard_map.93.slots_hbm = s32[2,768]{1,0:T(2,128)} custom-call(s32[2,2048]{1,0:T(2,128)} %blocks_hbm.5), custom_call_target="tpu_custom_call" | custom-call | bytes 22528 | tf_op jit(solution)/shard_map/pallas_call | solution.py:422
  75.6 3.7 %all-to-all-done.1.g0_hbm = bf16[8,32,384]{2,1,0:T(8,128)(2,1)S(1)} async-done(((bf16[8,32,384]{2,1,0:T(8,128)(2,1)}), bf16[8,32,384]{2,1,0:T(8,128)(2,1)S(1)}, u32[]{:S(2)}, u32[]{:S(2)}) %all-to-all-start.1) | async-done | bytes 196640 | tf_op jit(solution)/shard_map/all_to_all | solution.py:560
  79.3 1.2 %collective-permute-start.11 = (bf16[8,32,384]{2,1,0:T(8,128)(2,1)S(1)}, bf16[8,32,384]{2,1,0:T(8,128)(2,1)S(1)}, u32[]{:S(2)}, u32[]{:S(2)}) collective-permute-start(bf16[8,32,384]{2,1,0:T(8,128)(2,1)S(1)} %all-to-all-done.1.g0_hbm), channel_id=1, source_target_pairs={{0,16},{8,24},{16,0},{24,8},{1,17},{9,25},{17,1},{25,9},{2,18},{10... | collective-permute-start | bytes 589832 | tf_op jit(solution)/shard_map/ppermute | solution.py:437
  80.5 0.0 collective-permute-start.10
  80.5 4.5 %collective-permute-done.11.g2_hbm = bf16[8,32,384]{2,1,0:T(8,128)(2,1)S(1)} collective-permute-done((bf16[8,32,384]{2,1,0:T(8,128)(2,1)S(1)}, bf16[8,32,384]{2,1,0:T(8,128)(2,1)S(1)}, u32[]{:S(2)}, u32[]{:S(2)}) %collective-permute-start.11) | collective-permute-done | bytes 196640 | tf_op jit(solution)/shard_map/ppermute | solution.py:437
  84.9 0.0 collective-permute-start.12
  84.9 0.0 collective-permute-done.10.g1_hbm
  84.9 0.0 copy-start.3
  85.0 1.4 %collective-permute-done.12.g3_hbm = bf16[8,32,384]{2,1,0:T(8,128)(2,1)S(1)} collective-permute-done((bf16[8,32,384]{2,1,0:T(8,128)(2,1)S(1)}, bf16[8,32,384]{2,1,0:T(8,128)(2,1)S(1)}, u32[]{:S(2)}, u32[]{:S(2)}) %collective-permute-start.12) | collective-permute-done | bytes 196640 | tf_op jit(solution)/shard_map/ppermute | solution.py:437
  86.4 0.0 copy-done.1
  86.4 0.0 copy-done.2
  86.4 0.0 copy-done.3
  86.4 0.0 copy-start.4
  86.4 0.7 copy-done.4
  87.1 4.1 %shard_map.94 = (f32[1024,256]{1,0:T(8,128)}, f32[1024,256]{1,0:T(8,128)}) custom-call(bf16[8,32,384]{2,1,0:T(8,128)(2,1)} %copy-done.1, bf16[8,32,384]{2,1,0:T(8,128)(2,1)} %copy-done.3, bf16[8,32,384]{2,1,0:T(8,128)(2,1)} %copy-done.2, bf16[8,32,384]{2,1,0:T(8,128)(2,1)} %copy-done.4, s32[2,768]{1,0:T(2,128)} %shard_map.93.slots_hbm, f32[1024,256]{1,0:T(8,128)} %w_hbm.3, ...), custom_call_target="tpu_custom_call" | custom-call | bytes 4986880 | tf_op jit(solution)/shard_map/pallas_call | solution.py:422
  (5 shorter events, 0.0 us)
Async XLA Ops:
  2.9 11.4 %collective-permute-start.6 = (bf16[384,128]{1,0:T(8,128)(2,1)}, bf16[384,128]{1,0:T(8,128)(2,1)S(1)}, u32[]{:S(2)}, u32[]{:S(2)}) collective-permute-start(bf16[384,128]{1,0:T(8,128)(2,1)} %shard_map.86.refs_0_), channel_id=1, source_target_pairs={{0,7},{1,6},{2,5},{3,4},{4,3},{5,2},{6,1},{7,0},{8,15},{9,14},{10,... | collective-permute-start | bytes 294920 | tf_op jit(solution)/shard_map/ppermute | solution.py:437
  9.0 12.1 %collective-permute-start.5 = (bf16[384,128]{1,0:T(8,128)(2,1)}, bf16[384,128]{1,0:T(8,128)(2,1)S(1)}, u32[]{:S(2)}, u32[]{:S(2)}) collective-permute-start(bf16[384,128]{1,0:T(8,128)(2,1)} %shard_map.86.refs_0_), channel_id=1, source_target_pairs={{0,6},{1,7},{2,4},{3,5},{4,2},{5,3},{6,0},{7,1},{8,14},{9,15},{10,... | collective-permute-start | bytes 294920 | tf_op jit(solution)/shard_map/ppermute | solution.py:437
  9.2 17.5 %collective-permute-start.4 = (bf16[384,128]{1,0:T(8,128)(2,1)}, bf16[384,128]{1,0:T(8,128)(2,1)S(1)}, u32[]{:S(2)}, u32[]{:S(2)}) collective-permute-start(bf16[384,128]{1,0:T(8,128)(2,1)} %shard_map.86.refs_0_), channel_id=1, source_target_pairs={{0,5},{1,4},{2,7},{3,6},{4,1},{5,0},{6,3},{7,2},{8,13},{9,12},{10,... | collective-permute-start | bytes 294920 | tf_op jit(solution)/shard_map/ppermute | solution.py:437
  9.9 16.8 %collective-permute-start.3 = (bf16[384,128]{1,0:T(8,128)(2,1)}, bf16[384,128]{1,0:T(8,128)(2,1)S(1)}, u32[]{:S(2)}, u32[]{:S(2)}) collective-permute-start(bf16[384,128]{1,0:T(8,128)(2,1)} %shard_map.86.refs_0_), channel_id=1, source_target_pairs={{0,4},{1,5},{2,6},{3,7},{4,0},{5,1},{6,2},{7,3},{8,12},{9,13},{10,... | collective-permute-start | bytes 294920 | tf_op jit(solution)/shard_map/ppermute | solution.py:437
  12.0 14.8 %collective-permute-start.2 = (bf16[384,128]{1,0:T(8,128)(2,1)}, bf16[384,128]{1,0:T(8,128)(2,1)S(1)}, u32[]{:S(2)}, u32[]{:S(2)}) collective-permute-start(bf16[384,128]{1,0:T(8,128)(2,1)} %shard_map.86.refs_0_), channel_id=1, source_target_pairs={{0,3},{1,2},{2,1},{3,0},{4,7},{5,6},{6,5},{7,4},{8,11},{9,10},{10,... | collective-permute-start | bytes 294920 | tf_op jit(solution)/shard_map/ppermute | solution.py:437
  14.2 12.7 %copy-start.5 = (bf16[384,128]{1,0:T(8,128)(2,1)}, bf16[384,128]{1,0:T(8,128)(2,1)S(1)}, u32[]{:S(2)}) copy-start(bf16[384,128]{1,0:T(8,128)(2,1)S(1)} %collective-permute-done.6.refs_7_) | copy-start | bytes 294916
  14.3 12.7 %collective-permute-start.1 = (bf16[384,128]{1,0:T(8,128)(2,1)}, bf16[384,128]{1,0:T(8,128)(2,1)S(1)}, u32[]{:S(2)}, u32[]{:S(2)}) collective-permute-start(bf16[384,128]{1,0:T(8,128)(2,1)} %shard_map.86.refs_0_), channel_id=1, source_target_pairs={{0,2},{1,3},{2,0},{3,1},{4,6},{5,7},{6,4},{7,5},{8,10},{9,11},{10,... | collective-permute-start | bytes 294920 | tf_op jit(solution)/shard_map/ppermute | solution.py:437
  21.0 5.9 %copy-start.6 = (bf16[384,128]{1,0:T(8,128)(2,1)}, bf16[384,128]{1,0:T(8,128)(2,1)S(1)}, u32[]{:S(2)}) copy-start(bf16[384,128]{1,0:T(8,128)(2,1)S(1)} %collective-permute-done.5.refs_6_) | copy-start | bytes 294916
  21.0 5.9 %collective-permute-start = (bf16[384,128]{1,0:T(8,128)(2,1)}, bf16[384,128]{1,0:T(8,128)(2,1)S(1)}, u32[]{:S(2)}, u32[]{:S(2)}) collective-permute-start(bf16[384,128]{1,0:T(8,128)(2,1)} %shard_map.86.refs_0_), channel_id=1, source_target_pairs={{0,1},{1,0},{2,3},{3,2},{4,5},{5,4},{6,7},{7,6},{8,9},{9,8},{10,11... | collective-permute-start | bytes 294920 | tf_op jit(solution)/shard_map/ppermute | solution.py:437
  26.7 0.6 copy-start.7
  26.7 0.7 copy-start.8
  26.7 0.7 copy-start.9
  26.9 0.6 copy-start.10
  26.9 0.7 copy-start.11
  29.9 9.6 %collective-permute-start.7 = (bf16[2,128,512]{2,1,0:T(8,128)(2,1)}, bf16[2,128,512]{2,1,0:T(8,128)(2,1)S(1)}, u32[]{:S(2)}, u32[]{:S(2)}) collective-permute-start(bf16[2,128,512]{2,1,0:T(8,128)(2,1)} %shard_map.88.block_hbm.b0_hbm), channel_id=1, source_target_pairs={{0,16},{8,24},{16,0},{24,8},{1,17},{9,25},{17,1},{25,9},{2,18},{10... | collective-permute-start | bytes 786440 | tf_op jit(solution)/shard_map/ppermute | solution.py:437
  39.4 6.3 %copy-start.12 = (bf16[2,128,512]{2,1,0:T(8,128)(2,1)}, bf16[2,128,512]{2,1,0:T(8,128)(2,1)S(1)}, u32[]{:S(2)}) copy-start(bf16[2,128,512]{2,1,0:T(8,128)(2,1)S(1)} %collective-permute-done.7.b2_hbm) | copy-start | bytes 786436
  39.5 20.5 %all-to-all-start = ((bf16[32,32,256]{2,1,0:T(8,128)(2,1)}), bf16[32,32,256]{2,1,0:T(8,128)(2,1)S(1)}, u32[]{:S(2)}, u32[]{:S(2)}) async-start(bf16[32,32,256]{2,1,0:T(8,128)(2,1)} %shard_map.89), calls=%async_computation | async-start | bytes 1048576 | tf_op jit(solution)/shard_map/all_to_all | solution.py:517
  43.8 1.8 %collective-permute-start.8 = (bf16[2,128,512]{2,1,0:T(8,128)(2,1)}, bf16[2,128,512]{2,1,0:T(8,128)(2,1)S(1)}, u32[]{:S(2)}, u32[]{:S(2)}) collective-permute-start(bf16[2,128,512]{2,1,0:T(8,128)(2,1)} %shard_map.88.block_hbm.b0_hbm), channel_id=1, source_target_pairs={{0,8},{8,0},{16,24},{24,16},{1,9},{9,1},{17,25},{25,17},{2,10},{10... | collective-permute-start | bytes 786440 | tf_op jit(solution)/shard_map/ppermute | solution.py:437
  43.9 1.8 %collective-permute-start.9 = (bf16[2,128,512]{2,1,0:T(8,128)(2,1)S(1)}, bf16[2,128,512]{2,1,0:T(8,128)(2,1)S(1)}, u32[]{:S(2)}, u32[]{:S(2)}) collective-permute-start(bf16[2,128,512]{2,1,0:T(8,128)(2,1)S(1)} %collective-permute-done.7.b2_hbm), channel_id=1, source_target_pairs={{0,8},{8,0},{16,24},{24,16},{1,9},{9,1},{17,25},{25,17},{2,10},{10... | collective-permute-start | bytes 786440 | tf_op jit(solution)/shard_map/ppermute | solution.py:437
  45.6 0.7 copy-start.13
  45.7 0.7 copy-start.14
  59.9 0.8 copy-start
  67.8 11.4 %all-to-all-start.1 = ((bf16[8,32,384]{2,1,0:T(8,128)(2,1)}), bf16[8,32,384]{2,1,0:T(8,128)(2,1)S(1)}, u32[]{:S(2)}, u32[]{:S(2)}) async-start(bf16[8,32,384]{2,1,0:T(8,128)(2,1)} %shard_map.92), calls=%async_computation.1 | async-start | bytes 393216 | tf_op jit(solution)/shard_map/all_to_all | solution.py:560
  79.3 7.1 %copy-start.1 = (bf16[8,32,384]{2,1,0:T(8,128)(2,1)}, bf16[8,32,384]{2,1,0:T(8,128)(2,1)S(1)}, u32[]{:S(2)}) copy-start(bf16[8,32,384]{2,1,0:T(8,128)(2,1)S(1)} %all-to-all-done.1.g0_hbm) | copy-start | bytes 589828
  79.3 5.7 %collective-permute-start.11 = (bf16[8,32,384]{2,1,0:T(8,128)(2,1)S(1)}, bf16[8,32,384]{2,1,0:T(8,128)(2,1)S(1)}, u32[]{:S(2)}, u32[]{:S(2)}) collective-permute-start(bf16[8,32,384]{2,1,0:T(8,128)(2,1)S(1)} %all-to-all-done.1.g0_hbm), channel_id=1, source_target_pairs={{0,16},{8,24},{16,0},{24,8},{1,17},{9,25},{17,1},{25,9},{2,18},{10... | collective-permute-start | bytes 589832 | tf_op jit(solution)/shard_map/ppermute | solution.py:437
  80.5 4.5 %collective-permute-start.10 = (bf16[8,32,384]{2,1,0:T(8,128)(2,1)S(1)}, bf16[8,32,384]{2,1,0:T(8,128)(2,1)S(1)}, u32[]{:S(2)}, u32[]{:S(2)}) collective-permute-start(bf16[8,32,384]{2,1,0:T(8,128)(2,1)S(1)} %all-to-all-done.1.g0_hbm), channel_id=1, source_target_pairs={{0,8},{8,0},{16,24},{24,16},{1,9},{9,1},{17,25},{25,17},{2,10},{10... | collective-permute-start | bytes 589832 | tf_op jit(solution)/shard_map/ppermute | solution.py:437
  84.9 1.4 %copy-start.2 = (bf16[8,32,384]{2,1,0:T(8,128)(2,1)}, bf16[8,32,384]{2,1,0:T(8,128)(2,1)S(1)}, u32[]{:S(2)}) copy-start(bf16[8,32,384]{2,1,0:T(8,128)(2,1)S(1)} %collective-permute-done.11.g2_hbm) | copy-start | bytes 589828
  84.9 1.4 %collective-permute-start.12 = (bf16[8,32,384]{2,1,0:T(8,128)(2,1)S(1)}, bf16[8,32,384]{2,1,0:T(8,128)(2,1)S(1)}, u32[]{:S(2)}, u32[]{:S(2)}) collective-permute-start(bf16[8,32,384]{2,1,0:T(8,128)(2,1)S(1)} %collective-permute-done.11.g2_hbm), channel_id=1, source_target_pairs={{0,8},{8,0},{16,24},{24,16},{1,9},{9,1},{17,25},{25,17},{2,10},{10... | collective-permute-start | bytes 589832 | tf_op jit(solution)/shard_map/ppermute | solution.py:437
  84.9 1.4 %copy-start.3 = (bf16[8,32,384]{2,1,0:T(8,128)(2,1)}, bf16[8,32,384]{2,1,0:T(8,128)(2,1)S(1)}, u32[]{:S(2)}) copy-start(bf16[8,32,384]{2,1,0:T(8,128)(2,1)S(1)} %collective-permute-done.10.g1_hbm) | copy-start | bytes 589828
  86.4 0.7 copy-start.4

commit v12 on v11

--- a/solution.py
+++ b/solution.py
@@ -135,8 +135,8 @@
 
 def prepare_kernel(
     count, owners,
-    blocks_hbm, w_hbm, z_hbm, t_hbm, coef_hbm, offset_hbm, starts_hbm,
-    blocks, w, z, t, coef, offset, starts, sems, out_sems,
+    blocks_hbm, w_hbm, z_hbm, t_hbm, coef_hbm, offset_hbm,
+    blocks, w, z, t, coef, offset, sems, out_sems,
 ):
     row, me = lax.axis_index("rows"), lax.axis_index("pts")
     points, outputs = w.shape
@@ -147,9 +147,8 @@
     for u in range(UPDATES):
         indices = group_row(blocks, u, row, count)
         marks, rank, start = owners_of(indices, before, points, owners)
-        starts[u : u + 1, :] = lane_row(start)
         locals_of.append(sorted_points(indices, sorted_places(marks, rank, start)) - me * points)
-    writes = start_all([(starts, starts_hbm)], out_sems)
+    writes = []
     wait_all(reads[1:])
     current, moving = w[...], z[...]
     goal = t[...].astype(f32).T
@@ -231,20 +230,22 @@
 
 
 def compact_kernel(*refs):
-    *came_hbm, starts_hbm, block_hbm, came, starts, wide, block, sems = refs
-    me = lax.axis_index("pts")
+    *came_hbm, starts_hbm, block_hbm, first_hbm, second_hbm, came, starts, wide, block, sems = refs
+    row, me = lax.axis_index("rows"), lax.axis_index("pts")
     owners, deep, _ = came.shape
     cap = deep // UPDATES
+    groups = starts.shape[0] // UPDATES
     count = block.shape[2]
     pairs = [(a, came.at[k]) for k, a in enumerate(came_hbm)]
     wait_all(start_all([*pairs, (starts_hbm, starts)], sems))
     for u in range(UPDATES):
         for o in range(owners):
-            start = starts[u, o]
+            start = starts[u * groups + row, o]
             rows = came[lax.bitwise_xor(me, o), u * cap : (u + 1) * cap, :]
             wide[u, pl.ds(start, cap), :] = rows.astype(f32)
         block[u] = wide[u, 0:count, :].T.astype(bf16)
-    wait_all(start_all([(block, block_hbm)], sems))
+    pairs = [(block, block_hbm), (block.at[0], first_hbm), (block.at[1], second_hbm)]
+    wait_all(start_all(pairs, sems))
 
 
 def sums_kernel(
@@ -273,12 +274,14 @@
 
 
 def factors_kernel(
-    b0_hbm, b1_hbm, b2_hbm, b3_hbm, ids_hbm, pivots_hbm, factor_hbm, cross_hbm,
+    mine_hbm, beside_hbm, a0_hbm, a1_hbm, d0_hbm, d1_hbm, ids_hbm, pivots_hbm, factor_hbm, cross_hbm,
     feats, ids, pivots, factor, cross, sems,
 ):
     row = lax.axis_index("rows")
     groups, _, width, count = feats.shape
-    pairs = [(b_hbm, feats.at[k]) for k, b_hbm in enumerate((b0_hbm, b1_hbm, b2_hbm, b3_hbm))]
+    pairs = [(mine_hbm, feats.at[0]), (beside_hbm, feats.at[1])]
+    pairs += [(a0_hbm, feats.at[2, 0]), (a1_hbm, feats.at[2, 1])]
+    pairs += [(d0_hbm, feats.at[3, 0]), (d1_hbm, feats.at[3, 1])]
     wait_all(start_all(pairs + [(ids_hbm, ids), (pivots_hbm, pivots)], sems))
     places = [lax.bitwise_xor(row, k) for k in range(groups)]
     rights = [[extended(feats[k, u], 0, False) for k in range(groups)] for u in range(UPDATES)]
@@ -459,25 +462,33 @@
         features,
         sems=(2,),
     )
-    came = {k: swap(packed, "pts", k) for k in reversed(range(1, owners))}
-    kept = [
-        like((UPDATES, outputs, points)),
-        like((UPDATES, outputs, count), f32),
-        like((8, 128), i32),
-    ]
+    came = {k: swap(packed, "pts", k) for k in reversed(range(3, owners))}
+    kept = [like((UPDATES, outputs, points)), like((UPDATES, outputs, count), f32)]
     given = [block_index, coefficients, momentum, targets]
-    coef, offset, row_starts = call(
+    coef, offset = call(
         functools.partial(prepare_kernel, count, owners),
         kept,
         given + kept,
         *given,
-        sems=(4, 1 + 2 * UPDATES),
+        sems=(4, 2 * UPDATES),
+    )
+    again, coef, later_index = lax.optimization_barrier((packed, coef, block_index))
+    came.update({k: swap(again, "pts", k) for k in (2, 1)})
+    kept = [like((UPDATES * rows, count), i32), like((8, 128), i32), like((UPDATES, rank), i32)]
+    ids, starts, chosen = call(
+        functools.partial(order_kernel, count, points, owners),
+        kept,
+        [block_index, pivot_index, *kept],
+        later_index,
+        pivot_index,
+        sems=(3,),
     )
     feats = like((UPDATES, width, count))
-    inside_starts = pltpu.SMEM(row_starts.shape, i32)
-    (mine,) = call(
+    one = like((width, count))
+    inside_starts = pltpu.SMEM(starts.shape, i32)
+    mine, first, second = call(
         compact_kernel,
-        [feats],
+        [feats, one, one],
         [
             like((owners, *packed.shape)),
             inside_starts,
@@ -486,11 +497,12 @@
         ],
         packed,
         *[came[k] for k in range(1, owners)],
-        row_starts,
+        starts,
         sems=(owners + 1,),
         grant=61,
     )
-    beside, across = swap(mine, "rows", 1), swap(mine, "rows", 2)
+    beside, across = swap(mine, "rows", 1), swap(first, "rows", 2)
+    across_second = swap(second, "rows", 2)
     pieces = like((devices, deep, count // 2))
     (pieces,) = call(
         sums_kernel,
@@ -503,17 +515,7 @@
         sems=(4,),
         flops=2.0 * UPDATES * points * count * (2 * width + outputs),
     )
-    pieces, later_index = lax.optimization_barrier((pieces, block_index))
-    kept = [like((UPDATES * rows, count), i32), like((8, 128), i32), like((UPDATES, rank), i32)]
-    ids, starts, chosen = call(
-        functools.partial(order_kernel, count, points, owners),
-        kept,
-        [block_index, pivot_index, *kept],
-        later_index,
-        pivot_index,
-        sems=(3,),
-    )
-    pieces, across, ids = lax.optimization_barrier((pieces, across, ids))
+    pieces, across = lax.optimization_barrier((pieces, across))
     summed = lax.all_to_all(pieces, ("rows", "pts"), 0, 0, tiled=True)
     kept = [like((UPDATES, rank, block)), like((rows, block, count))]
     factor, cross = call(
@@ -529,7 +531,9 @@
         mine,
         beside,
         across,
+        across_second,
         swap(across, "rows", 1),
+        swap(across_second, "rows", 1),
         ids,
         chosen,
         sems=(rows * rows + 2,),

time: 92 us -> 97.2 us (1.057)
  waiting for transfers between devices: 14.5 us -> 19.9 us
    ppermute x13 -> x15, waiting for transfers between devices: 7.47 us -> 15.7 us  [swap(): lax.ppermute(value, axis, [(i, i ^ k) for i in range(lax.axis_size(axis))])]
    ppermute x13 -> x15, starting transfers between devices: 22.4 us -> 18.4 us  [swap(): lax.ppermute(value, axis, [(i, i ^ k) for i in range(lax.axis_size(axis))])]
    all_to_all x1, waiting for transfers between devices: 3.34 us -> 0.01 us  [with_kernels(): summed = lax.all_to_all(pieces, ('rows', 'pts'), 0, 0, tiled=True)]
    all_to_all x1, starting transfers between devices: 3.62 us -> 6.7 us  [with_kernels(): got = lax.all_to_all(steps, 'pts', 0, 0, tiled=True)]
    unnamed x30 -> x34, local copies, waits for them, and re-layouts: 2.84 us -> 2.77 us
  transfers between devices with their start and end apart: 15 -> 17, of which waited for: 7 -> 7; matrix products, arithmetic and copies ran while one was open for 0% -> 0% of each run, Pallas kernels for 29% -> 28%
where the time goes in v12:
time: 97.2 us; the launch traced here: 96.5 us
  Pallas kernels  42.6 us (44%)
  starting transfers between devices  30.1 us (31%)
  waiting for transfers between devices  19.9 us (20%)
  local copies, waits for them, and re-layouts  2.77 us (3%)
  between operations  1.06 us (1%)
    pallas_call x9, Pallas kernels, call(): pl.pallas_call(body, out_shape=outs, in_specs=[VMEM] * near + [HBM] * (le...  42.6 us
    ppermute x15, starting transfers between devices, swap(): lax.ppermute(value, axis, [(i, i ^ k) for i in range(lax.axis_size(axis))])  18.4 us
    ppermute x15, waiting for transfers between devices, swap(): lax.ppermute(value, axis, [(i, i ^ k) for i in range(lax.axis_size(axis))])  15.7 us
    all_to_all x1, starting transfers between devices, with_kernels(): got = lax.all_to_all(steps, 'pts', 0, 0, tiled=True)  6.7 us
    all_to_all x1, starting transfers between devices, with_kernels(): summed = lax.all_to_all(pieces, ('rows', 'pts'), 0, 0, tiled=True)  4.96 us
    all_to_all x1, waiting for transfers between devices, with_kernels(): got = lax.all_to_all(steps, 'pts', 0, 0, tiled=True)  4.2 us
    unnamed x34, local copies, waits for them, and re-layouts  2.77 us
  transfers between devices with their start and end apart: 17, of which 7 were waited for; matrix products, arithmetic and copies ran while one was open for 0% of the time, Pallas kernels for 28%

profile of v12, /device:TPU:0, one launch (start us, length us, event | category | flops | bytes accessed | tf_op | source)
XLA Modules:
  0.0 96.5 jit_solution(393139707338845675)
XLA Ops:
  0.6 2.3 %shard_map.86.refs_0_ = bf16[384,128]{1,0:T(8,128)(2,1)} custom-call(s32[2,2048]{1,0:T(2,128)} %blocks_hbm.5, bf16[1024,128]{1,0:T(8,128)(2,1)} %feats_hbm.3), custom_call_target="tpu_custom_call" | custom-call | bytes 376832 | tf_op jit(solution)/shard_map/pallas_call | solution.py:425
  2.9 6.1 %collective-permute-start.6 = (bf16[384,128]{1,0:T(8,128)(2,1)}, bf16[384,128]{1,0:T(8,128)(2,1)S(1)}, u32[]{:S(2)}, u32[]{:S(2)}) collective-permute-start(bf16[384,128]{1,0:T(8,128)(2,1)} %shard_map.86.refs_0_), channel_id=1, source_target_pairs={{0,7},{1,6},{2,5},{3,4},{4,3},{5,2},{6,1},{7,0},{8,15},{9,14},{10,... | collective-permute-start | bytes 294920 | tf_op jit(solution)/shard_map/ppermute | solution.py:440
  9.0 0.2 collective-permute-start.5
  9.2 0.7 collective-permute-start.4
  9.9 2.0 %collective-permute-start.3 = (bf16[384,128]{1,0:T(8,128)(2,1)}, bf16[384,128]{1,0:T(8,128)(2,1)S(1)}, u32[]{:S(2)}, u32[]{:S(2)}) collective-permute-start(bf16[384,128]{1,0:T(8,128)(2,1)} %shard_map.86.refs_0_), channel_id=1, source_target_pairs={{0,4},{1,5},{2,6},{3,7},{4,0},{5,1},{6,2},{7,3},{8,12},{9,13},{10,... | collective-permute-start | bytes 294920 | tf_op jit(solution)/shard_map/ppermute | solution.py:440
  12.0 2.3 %collective-permute-start.2 = (bf16[384,128]{1,0:T(8,128)(2,1)}, bf16[384,128]{1,0:T(8,128)(2,1)S(1)}, u32[]{:S(2)}, u32[]{:S(2)}) collective-permute-start(bf16[384,128]{1,0:T(8,128)(2,1)} %shard_map.86.refs_0_), channel_id=1, source_target_pairs={{0,3},{1,2},{2,1},{3,0},{4,7},{5,6},{6,5},{7,4},{8,11},{9,10},{10,... | collective-permute-start | bytes 294920 | tf_op jit(solution)/shard_map/ppermute | solution.py:440
  14.3 4.7 %shard_map.87 = (bf16[2,256,1024]{2,1,0:T(8,128)(2,1)}, f32[2,256,512]{2,1,0:T(8,128)}) custom-call(s32[2,2048]{1,0:T(2,128)} %blocks_hbm.5, f32[1024,256]{1,0:T(8,128)} %w_hbm.3, f32[1024,256]{1,0:T(8,128)} %z_hbm.3, bf16[1024,256]{1,0:T(8,128)(2,1)} %t_hbm.1), custom_call_target="tpu_custom_call" | custom-call | bytes 4734976 | tf_op jit(solution)/shard_map/pallas_call | solution.py:425
  18.9 0.0 collective-permute-done.6.refs_7_
  18.9 0.0 copy-start.5
  18.9 2.1 %collective-permute-start.1 = (bf16[384,128]{1,0:T(8,128)(2,1)}, bf16[384,128]{1,0:T(8,128)(2,1)S(1)}, u32[]{:S(2)}, u32[]{:S(2)}) collective-permute-start(bf16[384,128]{1,0:T(8,128)(2,1)} %shard_map.86.refs_0_), channel_id=1, source_target_pairs={{0,2},{1,3},{2,0},{3,1},{4,6},{5,7},{6,4},{7,5},{8,10},{9,11},{10,... | collective-permute-start | bytes 294920 | tf_op jit(solution)/shard_map/ppermute | solution.py:440
  21.1 0.0 collective-permute-done.5.refs_6_
  21.1 0.9 collective-permute-start
  22.0 4.4 %shard_map.88 = (s32[8,512]{1,0:T(8,128)}, s32[8,128]{1,0:T(8,128)}, s32[2,512]{1,0:T(2,128)}) custom-call(s32[2,2048]{1,0:T(2,128)} %blocks_hbm.5, s32[2,512]{1,0:T(2,128)} %pivots_hbm.1), custom_call_target="tpu_custom_call" | custom-call | bytes 45056 | tf_op jit(solution)/shard_map/pallas_call | solution.py:425
  26.5 0.0 collective-permute-done.4.refs_5_
  26.5 0.0 copy-start.7
  26.5 0.0 collective-permute-done.3.refs_4_
  26.5 0.0 copy-start.8
  26.5 0.0 collective-permute-done.2.refs_3_
  26.5 0.0 copy-start.9
  26.5 0.4 collective-permute-done.1.refs_2_
  26.9 0.0 collective-permute-done.refs_1_
  26.9 0.0 copy-done.5
  26.9 0.0 copy-done.6
  26.9 0.2 copy-done.7
  27.1 0.0 copy-done.8
  27.1 0.0 copy-done.9
  27.2 0.4 copy-done.10
  27.5 0.0 copy-done.11
  27.6 2.4 %shard_map.89 = (bf16[2,128,512]{2,1,0:T(8,128)(2,1)}, bf16[128,512]{1,0:T(8,128)(2,1)}, bf16[128,512]{1,0:T(8,128)(2,1)}) custom-call(bf16[384,128]{1,0:T(8,128)(2,1)} %shard_map.86.refs_0_, bf16[384,128]{1,0:T(8,128)(2,1)} %copy-done.11, bf16[384,128]{1,0:T(8,128)(2,1)} %copy-done.10, bf16[384,128]{1,0:T(8,128)(2,1)} %copy-done.9, ...), custom_call_target="tpu_custom_call" | custom-call | bytes 1314816 | tf_op jit(solution)/shard_map/pallas_call | solution.py:425
  30.0 1.6 %collective-permute-start.7 = (bf16[128,512]{1,0:T(8,128)(2,1)}, bf16[128,512]{1,0:T(8,128)(2,1)S(1)}, u32[]{:S(2)}, u32[]{:S(2)}) collective-permute-start(bf16[128,512]{1,0:T(8,128)(2,1)} %get-tuple-element.28), channel_id=1, source_target_pairs={{0,16},{8,24},{16,0},{24,8},{1,17},{9,25},{17,1},{25,9},{2,18},{10... | collective-permute-start | bytes 393224 | tf_op jit(solution)/shard_map/ppermute | solution.py:440
  31.5 3.5 %shard_map.90 = bf16[32,32,256]{2,1,0:T(8,128)(2,1)} custom-call(bf16[2,128,512]{2,1,0:T(8,128)(2,1)} %get-tuple-element.25.block_hbm.mine_hbm, bf16[1024,128]{1,0:T(8,128)(2,1)} %feats_hbm.3, bf16[2,256,1024]{2,1,0:T(8,128)(2,1)} %get-tuple-element.26.coef_hbm, f32[2,256,512]{2,1,0:T(8,128)} %get-tuple-element.27.offset_hbm), custom_call_target="tpu_custom_call" | custom-call | flops 1073741824 | bytes 3145728 | tf_op jit(solution)/shard_map/pallas_call | solution.py:425
  35.1 0.1 collective-permute-done.7.a0_hbm
  35.2 5.0 %all-to-all-start = ((bf16[32,32,256]{2,1,0:T(8,128)(2,1)}), bf16[32,32,256]{2,1,0:T(8,128)(2,1)S(1)}, u32[]{:S(2)}, u32[]{:S(2)}) async-start(bf16[32,32,256]{2,1,0:T(8,128)(2,1)} %shard_map.90), calls=%async_computation | async-start | bytes 1048576 | tf_op jit(solution)/shard_map/all_to_all | solution.py:519
  40.2 0.1 collective-permute-start.8
  40.3 1.7 %collective-permute-start.9 = (bf16[128,512]{1,0:T(8,128)(2,1)}, bf16[128,512]{1,0:T(8,128)(2,1)S(1)}, u32[]{:S(2)}, u32[]{:S(2)}) collective-permute-start(bf16[128,512]{1,0:T(8,128)(2,1)} %get-tuple-element.31), channel_id=1, source_target_pairs={{0,16},{8,24},{16,0},{24,8},{1,17},{9,25},{17,1},{25,9},{2,18},{10... | collective-permute-start | bytes 393224 | tf_op jit(solution)/shard_map/ppermute | solution.py:440
  42.0 0.1 collective-permute-start.10
  42.1 7.3 %collective-permute-done.9.a1_hbm = bf16[128,512]{1,0:T(8,128)(2,1)S(1)} collective-permute-done((bf16[128,512]{1,0:T(8,128)(2,1)}, bf16[128,512]{1,0:T(8,128)(2,1)S(1)}, u32[]{:S(2)}, u32[]{:S(2)}) %collective-permute-start.9) | collective-permute-done | bytes 131104 | tf_op jit(solution)/shard_map/ppermute | solution.py:440
  49.4 0.0 collective-permute-start.11
  49.4 0.0 collective-permute-done.8.beside_hbm
  49.4 0.0 copy-start.12
  49.4 0.0 collective-permute-done.10.d0_hbm
  49.4 0.0 copy-start.15
  49.4 1.3 %collective-permute-done.11.d1_hbm = bf16[128,512]{1,0:T(8,128)(2,1)S(1)} collective-permute-done((bf16[128,512]{1,0:T(8,128)(2,1)S(1)}, bf16[128,512]{1,0:T(8,128)(2,1)S(1)}, u32[]{:S(2)}, u32[]{:S(2)}) %collective-permute-start.11) | collective-permute-done | bytes 131104 | tf_op jit(solution)/shard_map/ppermute | solution.py:440
  50.7 0.0 copy-done.13
  50.7 0.0 copy-done.14
  50.7 0.0 copy-done.12
  50.7 0.6 copy-done.16
  51.4 10.2 %shard_map.91 = (bf16[2,512,2048]{2,1,0:T(8,128)(2,1)}, bf16[4,2048,512]{2,1,0:T(8,128)(2,1)}) custom-call(bf16[2,128,512]{2,1,0:T(8,128)(2,1)} %get-tuple-element.25.block_hbm.mine_hbm, bf16[2,128,512]{2,1,0:T(8,128)(2,1)} %copy-done.12, bf16[128,512]{1,0:T(8,128)(2,1)} %copy-done.13, bf16[128,512]{1,0:T(8,128)(2,1)} %copy-done.14, ...), custom_call_target="tpu_custom_call" | custom-call | flops 1610612736 | bytes 13651968 | tf_op jit(solution)/shard_map/pallas_call | solution.py:425
  61.5 0.0 all-to-all-done.summed_hbm
  61.5 0.0 copy-start
  61.6 0.8 copy-done
  62.3 7.1 %shard_map.92 = bf16[8,32,384]{2,1,0:T(8,128)(2,1)} custom-call(bf16[32,32,256]{2,1,0:T(8,128)(2,1)} %copy-done, bf16[2,512,2048]{2,1,0:T(8,128)(2,1)} %get-tuple-element.34.factor_hbm, bf16[2,512,512]{2,1,0:T(8,128)(2,1)} %core_hbm.1, bf16[4,2048,512]{2,1,0:T(8,128)(2,1)} %get-tuple-element.35.cross_hbm, s32[8,128]{1,0:T(8,128)} %get-tuple-element.24.refs_8_.starts_hbm), custom_call_target="tpu_custom_call" | custom-call | bytes 14356480 | tf_op jit(solution)/shard_map/pallas_call | solution.py:425
  69.5 6.7 %all-to-all-start.1 = ((bf16[8,32,384]{2,1,0:T(8,128)(2,1)}), bf16[8,32,384]{2,1,0:T(8,128)(2,1)S(1)}, u32[]{:S(2)}, u32[]{:S(2)}) async-start(bf16[8,32,384]{2,1,0:T(8,128)(2,1)} %shard_map.92), calls=%async_computation.1 | async-start | bytes 393216 | tf_op jit(solution)/shard_map/all_to_all | solution.py:564
  76.2 4.1 %shard_map.93.slots_hbm = s32[2,768]{1,0:T(2,128)} custom-call(s32[2,2048]{1,0:T(2,128)} %blocks_hbm.5), custom_call_target="tpu_custom_call" | custom-call | bytes 22528 | tf_op jit(solution)/shard_map/pallas_call | solution.py:425
  80.2 4.2 %all-to-all-done.1.g0_hbm = bf16[8,32,384]{2,1,0:T(8,128)(2,1)S(1)} async-done(((bf16[8,32,384]{2,1,0:T(8,128)(2,1)}), bf16[8,32,384]{2,1,0:T(8,128)(2,1)S(1)}, u32[]{:S(2)}, u32[]{:S(2)}) %all-to-all-start.1) | async-done | bytes 196640 | tf_op jit(solution)/shard_map/all_to_all | solution.py:564
  84.4 0.5 collective-permute-start.13
  84.9 0.0 collective-permute-start.12
  85.0 5.2 %collective-permute-done.13.g2_hbm = bf16[8,32,384]{2,1,0:T(8,128)(2,1)S(1)} collective-permute-done((bf16[8,32,384]{2,1,0:T(8,128)(2,1)S(1)}, bf16[8,32,384]{2,1,0:T(8,128)(2,1)S(1)}, u32[]{:S(2)}, u32[]{:S(2)}) %collective-permute-start.13) | collective-permute-done | bytes 196640 | tf_op jit(solution)/shard_map/ppermute | solution.py:440
  90.1 0.0 collective-permute-start.14
  90.1 0.0 collective-permute-done.12.g1_hbm
  90.1 1.4 %collective-permute-done.14.g3_hbm = bf16[8,32,384]{2,1,0:T(8,128)(2,1)S(1)} collective-permute-done((bf16[8,32,384]{2,1,0:T(8,128)(2,1)S(1)}, bf16[8,32,384]{2,1,0:T(8,128)(2,1)S(1)}, u32[]{:S(2)}, u32[]{:S(2)}) %collective-permute-start.14) | collective-permute-done | bytes 196640 | tf_op jit(solution)/shard_map/ppermute | solution.py:440
  91.6 0.0 copy-start.4
  91.6 0.7 copy-done.4
  92.2 4.1 %shard_map.94 = (f32[1024,256]{1,0:T(8,128)}, f32[1024,256]{1,0:T(8,128)}) custom-call(bf16[8,32,384]{2,1,0:T(8,128)(2,1)} %copy-done.1, bf16[8,32,384]{2,1,0:T(8,128)(2,1)} %copy-done.3, bf16[8,32,384]{2,1,0:T(8,128)(2,1)} %copy-done.2, bf16[8,32,384]{2,1,0:T(8,128)(2,1)} %copy-done.4, s32[2,768]{1,0:T(2,128)} %shard_map.93.slots_hbm, f32[1024,256]{1,0:T(8,128)} %w_hbm.3, ...), custom_call_target="tpu_custom_call" | custom-call | bytes 4986880 | tf_op jit(solution)/shard_map/pallas_call | solution.py:425
  (13 shorter events, 0.0 us)
Async XLA Ops:
  2.9 16.0 %collective-permute-start.6 = (bf16[384,128]{1,0:T(8,128)(2,1)}, bf16[384,128]{1,0:T(8,128)(2,1)S(1)}, u32[]{:S(2)}, u32[]{:S(2)}) collective-permute-start(bf16[384,128]{1,0:T(8,128)(2,1)} %shard_map.86.refs_0_), channel_id=1, source_target_pairs={{0,7},{1,6},{2,5},{3,4},{4,3},{5,2},{6,1},{7,0},{8,15},{9,14},{10,... | collective-permute-start | bytes 294920 | tf_op jit(solution)/shard_map/ppermute | solution.py:440
  9.0 12.1 %collective-permute-start.5 = (bf16[384,128]{1,0:T(8,128)(2,1)}, bf16[384,128]{1,0:T(8,128)(2,1)S(1)}, u32[]{:S(2)}, u32[]{:S(2)}) collective-permute-start(bf16[384,128]{1,0:T(8,128)(2,1)} %shard_map.86.refs_0_), channel_id=1, source_target_pairs={{0,6},{1,7},{2,4},{3,5},{4,2},{5,3},{6,0},{7,1},{8,14},{9,15},{10,... | collective-permute-start | bytes 294920 | tf_op jit(solution)/shard_map/ppermute | solution.py:440
  9.2 17.3 %collective-permute-start.4 = (bf16[384,128]{1,0:T(8,128)(2,1)}, bf16[384,128]{1,0:T(8,128)(2,1)S(1)}, u32[]{:S(2)}, u32[]{:S(2)}) collective-permute-start(bf16[384,128]{1,0:T(8,128)(2,1)} %shard_map.86.refs_0_), channel_id=1, source_target_pairs={{0,5},{1,4},{2,7},{3,6},{4,1},{5,0},{6,3},{7,2},{8,13},{9,12},{10,... | collective-permute-start | bytes 294920 | tf_op jit(solution)/shard_map/ppermute | solution.py:440
  9.9 16.6 %collective-permute-start.3 = (bf16[384,128]{1,0:T(8,128)(2,1)}, bf16[384,128]{1,0:T(8,128)(2,1)S(1)}, u32[]{:S(2)}, u32[]{:S(2)}) collective-permute-start(bf16[384,128]{1,0:T(8,128)(2,1)} %shard_map.86.refs_0_), channel_id=1, source_target_pairs={{0,4},{1,5},{2,6},{3,7},{4,0},{5,1},{6,2},{7,3},{8,12},{9,13},{10,... | collective-permute-start | bytes 294920 | tf_op jit(solution)/shard_map/ppermute | solution.py:440
  12.0 14.5 %collective-permute-start.2 = (bf16[384,128]{1,0:T(8,128)(2,1)}, bf16[384,128]{1,0:T(8,128)(2,1)S(1)}, u32[]{:S(2)}, u32[]{:S(2)}) collective-permute-start(bf16[384,128]{1,0:T(8,128)(2,1)} %shard_map.86.refs_0_), channel_id=1, source_target_pairs={{0,3},{1,2},{2,1},{3,0},{4,7},{5,6},{6,5},{7,4},{8,11},{9,10},{10,... | collective-permute-start | bytes 294920 | tf_op jit(solution)/shard_map/ppermute | solution.py:440
  18.9 8.0 %copy-start.5 = (bf16[384,128]{1,0:T(8,128)(2,1)}, bf16[384,128]{1,0:T(8,128)(2,1)S(1)}, u32[]{:S(2)}) copy-start(bf16[384,128]{1,0:T(8,128)(2,1)S(1)} %collective-permute-done.6.refs_7_) | copy-start | bytes 294916
  18.9 8.0 %collective-permute-start.1 = (bf16[384,128]{1,0:T(8,128)(2,1)}, bf16[384,128]{1,0:T(8,128)(2,1)S(1)}, u32[]{:S(2)}, u32[]{:S(2)}) collective-permute-start(bf16[384,128]{1,0:T(8,128)(2,1)} %shard_map.86.refs_0_), channel_id=1, source_target_pairs={{0,2},{1,3},{2,0},{3,1},{4,6},{5,7},{6,4},{7,5},{8,10},{9,11},{10,... | collective-permute-start | bytes 294920 | tf_op jit(solution)/shard_map/ppermute | solution.py:440
  21.1 5.9 %copy-start.6 = (bf16[384,128]{1,0:T(8,128)(2,1)}, bf16[384,128]{1,0:T(8,128)(2,1)S(1)}, u32[]{:S(2)}) copy-start(bf16[384,128]{1,0:T(8,128)(2,1)S(1)} %collective-permute-done.5.refs_6_) | copy-start | bytes 294916
  21.1 5.8 %collective-permute-start = (bf16[384,128]{1,0:T(8,128)(2,1)}, bf16[384,128]{1,0:T(8,128)(2,1)S(1)}, u32[]{:S(2)}, u32[]{:S(2)}) collective-permute-start(bf16[384,128]{1,0:T(8,128)(2,1)} %shard_map.86.refs_0_), channel_id=1, source_target_pairs={{0,1},{1,0},{2,3},{3,2},{4,5},{5,4},{6,7},{7,6},{8,9},{9,8},{10,11... | collective-permute-start | bytes 294920 | tf_op jit(solution)/shard_map/ppermute | solution.py:440
  26.5 0.6 copy-start.7
  26.5 0.6 copy-start.8
  26.5 0.7 copy-start.9
  26.9 0.6 copy-start.10
  26.9 0.7 copy-start.11
  30.0 5.2 %collective-permute-start.7 = (bf16[128,512]{1,0:T(8,128)(2,1)}, bf16[128,512]{1,0:T(8,128)(2,1)S(1)}, u32[]{:S(2)}, u32[]{:S(2)}) collective-permute-start(bf16[128,512]{1,0:T(8,128)(2,1)} %get-tuple-element.28), channel_id=1, source_target_pairs={{0,16},{8,24},{16,0},{24,8},{1,17},{9,25},{17,1},{25,9},{2,18},{10... | collective-permute-start | bytes 393224 | tf_op jit(solution)/shard_map/ppermute | solution.py:440
  35.2 15.5 %copy-start.13 = (bf16[128,512]{1,0:T(8,128)(2,1)}, bf16[128,512]{1,0:T(8,128)(2,1)S(1)}, u32[]{:S(2)}) copy-start(bf16[128,512]{1,0:T(8,128)(2,1)S(1)} %collective-permute-done.7.a0_hbm) | copy-start | bytes 393220
  35.2 26.3 %all-to-all-start = ((bf16[32,32,256]{2,1,0:T(8,128)(2,1)}), bf16[32,32,256]{2,1,0:T(8,128)(2,1)S(1)}, u32[]{:S(2)}, u32[]{:S(2)}) async-start(bf16[32,32,256]{2,1,0:T(8,128)(2,1)} %shard_map.90), calls=%async_computation | async-start | bytes 1048576 | tf_op jit(solution)/shard_map/all_to_all | solution.py:519
  40.2 9.2 %collective-permute-start.8 = (bf16[2,128,512]{2,1,0:T(8,128)(2,1)}, bf16[2,128,512]{2,1,0:T(8,128)(2,1)S(1)}, u32[]{:S(2)}, u32[]{:S(2)}) collective-permute-start(bf16[2,128,512]{2,1,0:T(8,128)(2,1)} %get-tuple-element.25.block_hbm.mine_hbm), channel_id=1, source_target_pairs={{0,8},{8,0},{16,24},{24,16},{1,9},{9,1},{17,25},{25,17},{2,10},{10... | collective-permute-start | bytes 786440 | tf_op jit(solution)/shard_map/ppermute | solution.py:440
  40.3 9.0 %collective-permute-start.9 = (bf16[128,512]{1,0:T(8,128)(2,1)}, bf16[128,512]{1,0:T(8,128)(2,1)S(1)}, u32[]{:S(2)}, u32[]{:S(2)}) collective-permute-start(bf16[128,512]{1,0:T(8,128)(2,1)} %get-tuple-element.31), channel_id=1, source_target_pairs={{0,16},{8,24},{16,0},{24,8},{1,17},{9,25},{17,1},{25,9},{2,18},{10... | collective-permute-start | bytes 393224 | tf_op jit(solution)/shard_map/ppermute | solution.py:440
  42.0 7.4 %collective-permute-start.10 = (bf16[128,512]{1,0:T(8,128)(2,1)S(1)}, bf16[128,512]{1,0:T(8,128)(2,1)S(1)}, u32[]{:S(2)}, u32[]{:S(2)}) collective-permute-start(bf16[128,512]{1,0:T(8,128)(2,1)S(1)} %collective-permute-done.7.a0_hbm), channel_id=1, source_target_pairs={{0,8},{8,0},{16,24},{24,16},{1,9},{9,1},{17,25},{25,17},{2,10},{10... | collective-permute-start | bytes 393224 | tf_op jit(solution)/shard_map/ppermute | solution.py:440
  49.4 1.4 %copy-start.14 = (bf16[128,512]{1,0:T(8,128)(2,1)}, bf16[128,512]{1,0:T(8,128)(2,1)S(1)}, u32[]{:S(2)}) copy-start(bf16[128,512]{1,0:T(8,128)(2,1)S(1)} %collective-permute-done.9.a1_hbm) | copy-start | bytes 393220
  49.4 1.3 %collective-permute-start.11 = (bf16[128,512]{1,0:T(8,128)(2,1)S(1)}, bf16[128,512]{1,0:T(8,128)(2,1)S(1)}, u32[]{:S(2)}, u32[]{:S(2)}) collective-permute-start(bf16[128,512]{1,0:T(8,128)(2,1)S(1)} %collective-permute-done.9.a1_hbm), channel_id=1, source_target_pairs={{0,8},{8,0},{16,24},{24,16},{1,9},{9,1},{17,25},{25,17},{2,10},{10... | collective-permute-start | bytes 393224 | tf_op jit(solution)/shard_map/ppermute | solution.py:440
  49.4 1.3 %copy-start.12 = (bf16[2,128,512]{2,1,0:T(8,128)(2,1)}, bf16[2,128,512]{2,1,0:T(8,128)(2,1)S(1)}, u32[]{:S(2)}) copy-start(bf16[2,128,512]{2,1,0:T(8,128)(2,1)S(1)} %collective-permute-done.8.beside_hbm) | copy-start | bytes 786436
  49.4 1.3 %copy-start.15 = (bf16[128,512]{1,0:T(8,128)(2,1)}, bf16[128,512]{1,0:T(8,128)(2,1)S(1)}, u32[]{:S(2)}) copy-start(bf16[128,512]{1,0:T(8,128)(2,1)S(1)} %collective-permute-done.10.d0_hbm) | copy-start | bytes 393220
  50.7 0.6 copy-start.16
  61.5 0.8 copy-start
  69.5 15.0 %all-to-all-start.1 = ((bf16[8,32,384]{2,1,0:T(8,128)(2,1)}), bf16[8,32,384]{2,1,0:T(8,128)(2,1)S(1)}, u32[]{:S(2)}, u32[]{:S(2)}) async-start(bf16[8,32,384]{2,1,0:T(8,128)(2,1)} %shard_map.92), calls=%async_computation.1 | async-start | bytes 393216 | tf_op jit(solution)/shard_map/all_to_all | solution.py:564
  84.4 7.1 %copy-start.1 = (bf16[8,32,384]{2,1,0:T(8,128)(2,1)}, bf16[8,32,384]{2,1,0:T(8,128)(2,1)S(1)}, u32[]{:S(2)}) copy-start(bf16[8,32,384]{2,1,0:T(8,128)(2,1)S(1)} %all-to-all-done.1.g0_hbm) | copy-start | bytes 589828
  84.4 5.7 %collective-permute-start.13 = (bf16[8,32,384]{2,1,0:T(8,128)(2,1)S(1)}, bf16[8,32,384]{2,1,0:T(8,128)(2,1)S(1)}, u32[]{:S(2)}, u32[]{:S(2)}) collective-permute-start(bf16[8,32,384]{2,1,0:T(8,128)(2,1)S(1)} %all-to-all-done.1.g0_hbm), channel_id=1, source_target_pairs={{0,16},{8,24},{16,0},{24,8},{1,17},{9,25},{17,1},{25,9},{2,18},{10... | collective-permute-start | bytes 589832 | tf_op jit(solution)/shard_map/ppermute | solution.py:440
  84.9 5.2 %collective-permute-start.12 = (bf16[8,32,384]{2,1,0:T(8,128)(2,1)S(1)}, bf16[8,32,384]{2,1,0:T(8,128)(2,1)S(1)}, u32[]{:S(2)}, u32[]{:S(2)}) collective-permute-start(bf16[8,32,384]{2,1,0:T(8,128)(2,1)S(1)} %all-to-all-done.1.g0_hbm), channel_id=1, source_target_pairs={{0,8},{8,0},{16,24},{24,16},{1,9},{9,1},{17,25},{25,17},{2,10},{10... | collective-permute-start | bytes 589832 | tf_op jit(solution)/shard_map/ppermute | solution.py:440
  90.1 1.4 %copy-start.2 = (bf16[8,32,384]{2,1,0:T(8,128)(2,1)}, bf16[8,32,384]{2,1,0:T(8,128)(2,1)S(1)}, u32[]{:S(2)}) copy-start(bf16[8,32,384]{2,1,0:T(8,128)(2,1)S(1)} %collective-permute-done.13.g2_hbm) | copy-start | bytes 589828
  90.1 1.4 %collective-permute-start.14 = (bf16[8,32,384]{2,1,0:T(8,128)(2,1)S(1)}, bf16[8,32,384]{2,1,0:T(8,128)(2,1)S(1)}, u32[]{:S(2)}, u32[]{:S(2)}) collective-permute-start(bf16[8,32,384]{2,1,0:T(8,128)(2,1)S(1)} %collective-permute-done.13.g2_hbm), channel_id=1, source_target_pairs={{0,8},{8,0},{16,24},{24,16},{1,9},{9,1},{17,25},{25,17},{2,10},{10... | collective-permute-start | bytes 589832 | tf_op jit(solution)/shard_map/ppermute | solution.py:440
  90.1 1.4 %copy-start.3 = (bf16[8,32,384]{2,1,0:T(8,128)(2,1)}, bf16[8,32,384]{2,1,0:T(8,128)(2,1)S(1)}, u32[]{:S(2)}) copy-start(bf16[8,32,384]{2,1,0:T(8,128)(2,1)S(1)} %collective-permute-done.12.g1_hbm) | copy-start | bytes 589828
  91.6 0.7 copy-start.4

commit v13 on v11

--- a/solution.py
+++ b/solution.py
@@ -459,7 +459,7 @@
         features,
         sems=(2,),
     )
-    came = {k: swap(packed, "pts", k) for k in reversed(range(1, owners))}
+    came = {k: swap(packed, "pts", k) for k in reversed(range(3, owners))}
     kept = [
         like((UPDATES, outputs, points)),
         like((UPDATES, outputs, count), f32),
@@ -473,6 +473,8 @@
         *given,
         sems=(4, 1 + 2 * UPDATES),
     )
+    again, row_starts = lax.optimization_barrier((packed, row_starts))
+    came.update({k: swap(again, "pts", k) for k in (2, 1)})
     feats = like((UPDATES, width, count))
     inside_starts = pltpu.SMEM(row_starts.shape, i32)
     (mine,) = call(
@@ -488,7 +490,7 @@
         *[came[k] for k in range(1, owners)],
         row_starts,
         sems=(owners + 1,),
-        grant=61,
+        grant=60,
     )
     beside, across = swap(mine, "rows", 1), swap(mine, "rows", 2)
     pieces = like((devices, deep, count // 2))
@@ -533,7 +535,7 @@
         ids,
         chosen,
         sems=(rows * rows + 2,),
-        grant=61,
+        grant=60,
         flops=2.0 * width * block * (UPDATES * rank + block),
     )
     pieces = like((owners, deep, half * cap))
@@ -547,7 +549,7 @@
         cross,
         starts,
         sems=(2 * UPDATES + 2 + rows,),
-        grant=61,
+        grant=60,
     )
     steps, later_index = lax.optimization_barrier((steps, block_index))
     (slots,) = call(
@@ -581,7 +583,7 @@
         coefficients,
         momentum,
         sems=(1 + rows + 2 * parts, 2 * parts),
-        grant=61,
+        grant=60,
     )
 
 

time: 92 us -> 91.4 us (level)
  starting transfers between devices: 30.4 us -> 24.4 us
  waiting for transfers between devices: 14.5 us -> 19.3 us
    ppermute x13, waiting for transfers between devices: 7.47 us -> 12.2 us  [swap(): lax.ppermute(value, axis, [(i, i ^ k) for i in range(lax.axis_size(axis))])]
    ppermute x13, starting transfers between devices: 22.4 us -> 17.7 us  [swap(): lax.ppermute(value, axis, [(i, i ^ k) for i in range(lax.axis_size(axis))])]
    all_to_all x1, starting transfers between devices: 4.3 us -> 3.03 us  [with_kernels(): summed = lax.all_to_all(pieces, ('rows', 'pts'), 0, 0, tiled=True)]
  transfers between devices with their start and end apart: 15 -> 15, of which waited for: 7 -> 9; matrix products, arithmetic and copies ran while one was open for 0% -> 0% of each run, Pallas kernels for 29% -> 30%
where the time goes in v13:
time: 91.4 us; the launch traced here: 90.6 us
  Pallas kernels  42.6 us (47%)
  starting transfers between devices  24.4 us (27%)
  waiting for transfers between devices  19.3 us (21%)
  local copies, waits for them, and re-layouts  3.42 us (4%)
  between operations  1 us (1%)
    pallas_call x9, Pallas kernels, call(): pl.pallas_call(body, out_shape=outs, in_specs=[VMEM] * near + [HBM] * (le...  42.6 us
    ppermute x13, starting transfers between devices, swap(): lax.ppermute(value, axis, [(i, i ^ k) for i in range(lax.axis_size(axis))])  17.7 us
    ppermute x13, waiting for transfers between devices, swap(): lax.ppermute(value, axis, [(i, i ^ k) for i in range(lax.axis_size(axis))])  12.2 us
    all_to_all x1, waiting for transfers between devices, with_kernels(): got = lax.all_to_all(steps, 'pts', 0, 0, tiled=True)  3.71 us
    all_to_all x1, starting transfers between devices, with_kernels(): got = lax.all_to_all(steps, 'pts', 0, 0, tiled=True)  3.62 us
    unnamed x30, local copies, waits for them, and re-layouts  3.42 us
    all_to_all x1, waiting for transfers between devices, with_kernels(): summed = lax.all_to_all(pieces, ('rows', 'pts'), 0, 0, tiled=True)  3.34 us
    all_to_all x1, starting transfers between devices, with_kernels(): summed = lax.all_to_all(pieces, ('rows', 'pts'), 0, 0, tiled=True)  3.03 us
  transfers between devices with their start and end apart: 15, of which 9 were waited for; matrix products, arithmetic and copies ran while one was open for 0% of the time, Pallas kernels for 30%

profile of v13, /device:TPU:0, one launch (start us, length us, event | category | flops | bytes accessed | tf_op | source)
XLA Modules:
  0.0 90.6 jit_solution(17740192917483750747)
XLA Ops:
  0.6 2.2 %shard_map.86.refs_0_ = bf16[384,128]{1,0:T(8,128)(2,1)} custom-call(s32[2,2048]{1,0:T(2,128)} %blocks_hbm.5, bf16[1024,128]{1,0:T(8,128)(2,1)} %feats_hbm.3), custom_call_target="tpu_custom_call" | custom-call | bytes 376832 | tf_op jit(solution)/shard_map/pallas_call | solution.py:422
  2.9 6.1 %collective-permute-start.6 = (bf16[384,128]{1,0:T(8,128)(2,1)}, bf16[384,128]{1,0:T(8,128)(2,1)S(1)}, u32[]{:S(2)}, u32[]{:S(2)}) collective-permute-start(bf16[384,128]{1,0:T(8,128)(2,1)} %shard_map.86.refs_0_), channel_id=1, source_target_pairs={{0,7},{1,6},{2,5},{3,4},{4,3},{5,2},{6,1},{7,0},{8,15},{9,14},{10,... | collective-permute-start | bytes 294920 | tf_op jit(solution)/shard_map/ppermute | solution.py:437
  9.0 0.2 collective-permute-start.5
  9.2 0.7 collective-permute-start.4
  9.9 2.0 %collective-permute-start.3 = (bf16[384,128]{1,0:T(8,128)(2,1)}, bf16[384,128]{1,0:T(8,128)(2,1)S(1)}, u32[]{:S(2)}, u32[]{:S(2)}) collective-permute-start(bf16[384,128]{1,0:T(8,128)(2,1)} %shard_map.86.refs_0_), channel_id=1, source_target_pairs={{0,4},{1,5},{2,6},{3,7},{4,0},{5,1},{6,2},{7,3},{8,12},{9,13},{10,... | collective-permute-start | bytes 294920 | tf_op jit(solution)/shard_map/ppermute | solution.py:437
  12.0 2.3 %collective-permute-start.2 = (bf16[384,128]{1,0:T(8,128)(2,1)}, bf16[384,128]{1,0:T(8,128)(2,1)S(1)}, u32[]{:S(2)}, u32[]{:S(2)}) collective-permute-start(bf16[384,128]{1,0:T(8,128)(2,1)} %shard_map.86.refs_0_), channel_id=1, source_target_pairs={{0,3},{1,2},{2,1},{3,0},{4,7},{5,6},{6,5},{7,4},{8,11},{9,10},{10,... | collective-permute-start | bytes 294920 | tf_op jit(solution)/shard_map/ppermute | solution.py:437
  14.2 4.7 %shard_map.87 = (bf16[2,256,1024]{2,1,0:T(8,128)(2,1)}, f32[2,256,512]{2,1,0:T(8,128)}, s32[8,128]{1,0:T(8,128)}) custom-call(s32[2,2048]{1,0:T(2,128)} %blocks_hbm.5, f32[1024,256]{1,0:T(8,128)} %w_hbm.3, f32[1024,256]{1,0:T(8,128)} %z_hbm.3, bf16[1024,256]{1,0:T(8,128)(2,1)} %t_hbm.1), custom_call_target="tpu_custom_call" | custom-call | bytes 4739072 | tf_op jit(solution)/shard_map/pallas_call | solution.py:422
  18.9 0.0 collective-permute-done.6.refs_7_
  18.9 0.0 copy-start.5
  19.0 2.1 %collective-permute-start.1 = (bf16[384,128]{1,0:T(8,128)(2,1)}, bf16[384,128]{1,0:T(8,128)(2,1)S(1)}, u32[]{:S(2)}, u32[]{:S(2)}) collective-permute-start(bf16[384,128]{1,0:T(8,128)(2,1)} %shard_map.86.refs_0_), channel_id=1, source_target_pairs={{0,2},{1,3},{2,0},{3,1},{4,6},{5,7},{6,4},{7,5},{8,10},{9,11},{10,... | collective-permute-start | bytes 294920 | tf_op jit(solution)/shard_map/ppermute | solution.py:437
  21.1 0.0 collective-permute-done.5.refs_6_
  21.1 0.9 %collective-permute-start = (bf16[384,128]{1,0:T(8,128)(2,1)}, bf16[384,128]{1,0:T(8,128)(2,1)S(1)}, u32[]{:S(2)}, u32[]{:S(2)}) collective-permute-start(bf16[384,128]{1,0:T(8,128)(2,1)} %shard_map.86.refs_0_), channel_id=1, source_target_pairs={{0,1},{1,0},{2,3},{3,2},{4,5},{5,4},{6,7},{7,6},{8,9},{9,8},{10,11... | collective-permute-start | bytes 294920 | tf_op jit(solution)/shard_map/ppermute | solution.py:437
  22.0 2.8 %collective-permute-done.4.refs_5_ = bf16[384,128]{1,0:T(8,128)(2,1)S(1)} collective-permute-done((bf16[384,128]{1,0:T(8,128)(2,1)}, bf16[384,128]{1,0:T(8,128)(2,1)S(1)}, u32[]{:S(2)}, u32[]{:S(2)}) %collective-permute-start.4) | collective-permute-done | bytes 98336 | tf_op jit(solution)/shard_map/ppermute | solution.py:437
  24.8 0.0 copy-start.7
  24.8 1.1 %collective-permute-done.3.refs_4_ = bf16[384,128]{1,0:T(8,128)(2,1)S(1)} collective-permute-done((bf16[384,128]{1,0:T(8,128)(2,1)}, bf16[384,128]{1,0:T(8,128)(2,1)S(1)}, u32[]{:S(2)}, u32[]{:S(2)}) %collective-permute-start.3) | collective-permute-done | bytes 98336 | tf_op jit(solution)/shard_map/ppermute | solution.py:437
  26.0 0.0 copy-start.8
  26.0 0.0 collective-permute-done.2.refs_3_
  26.0 0.0 copy-start.9
  26.0 0.9 %collective-permute-done.1.refs_2_ = bf16[384,128]{1,0:T(8,128)(2,1)S(1)} collective-permute-done((bf16[384,128]{1,0:T(8,128)(2,1)}, bf16[384,128]{1,0:T(8,128)(2,1)S(1)}, u32[]{:S(2)}, u32[]{:S(2)}) %collective-permute-start.1) | collective-permute-done | bytes 98336 | tf_op jit(solution)/shard_map/ppermute | solution.py:437
  26.9 0.0 copy-start.10
  26.9 0.0 collective-permute-done.refs_1_
  26.9 0.0 copy-done.5
  26.9 0.0 copy-done.6
  26.9 0.0 copy-done.7
  26.9 0.0 copy-done.8
  27.0 0.0 copy-done.9
  27.0 0.6 copy-done.10
  27.5 0.0 copy-start.11
  27.5 0.6 copy-done.11
  28.2 2.3 %shard_map.88.block_hbm.b0_hbm = bf16[2,128,512]{2,1,0:T(8,128)(2,1)} custom-call(bf16[384,128]{1,0:T(8,128)(2,1)} %shard_map.86.refs_0_, bf16[384,128]{1,0:T(8,128)(2,1)} %copy-done.11, bf16[384,128]{1,0:T(8,128)(2,1)} %copy-done.10, bf16[384,128]{1,0:T(8,128)(2,1)} %copy-done.9, bf16[384,128]{1,0:T(8,128)(2,1)} %copy-done.8, bf16[384,128]{1,0:T(8,128)(2,1)} %copy-done.7, ...), custom_call_target="tpu_custom_call" | custom-call | bytes 1052672 | tf_op jit(solution)/shard_map/pallas_call | solution.py:422
  30.5 1.6 %collective-permute-start.7 = (bf16[2,128,512]{2,1,0:T(8,128)(2,1)}, bf16[2,128,512]{2,1,0:T(8,128)(2,1)S(1)}, u32[]{:S(2)}, u32[]{:S(2)}) collective-permute-start(bf16[2,128,512]{2,1,0:T(8,128)(2,1)} %shard_map.88.block_hbm.b0_hbm), channel_id=1, source_target_pairs={{0,16},{8,24},{16,0},{24,8},{1,17},{9,25},{17,1},{25,9},{2,18},{10... | collective-permute-start | bytes 786440 | tf_op jit(solution)/shard_map/ppermute | solution.py:437
  32.0 3.6 %shard_map.89 = bf16[32,32,256]{2,1,0:T(8,128)(2,1)} custom-call(bf16[2,128,512]{2,1,0:T(8,128)(2,1)} %shard_map.88.block_hbm.b0_hbm, bf16[1024,128]{1,0:T(8,128)(2,1)} %feats_hbm.3, bf16[2,256,1024]{2,1,0:T(8,128)(2,1)} %get-tuple-element.24.coef_hbm, f32[2,256,512]{2,1,0:T(8,128)} %get-tuple-element.25.offset_hbm), custom_call_target="tpu_custom_call" | custom-call | flops 1073741824 | bytes 3145728 | tf_op jit(solution)/shard_map/pallas_call | solution.py:422
  35.6 4.4 %shard_map.90 = (s32[8,512]{1,0:T(8,128)}, s32[8,128]{1,0:T(8,128)}, s32[2,512]{1,0:T(2,128)}) custom-call(s32[2,2048]{1,0:T(2,128)} %blocks_hbm.5, s32[2,512]{1,0:T(2,128)} %pivots_hbm.1), custom_call_target="tpu_custom_call" | custom-call | bytes 45056 | tf_op jit(solution)/shard_map/pallas_call | solution.py:422
  40.0 0.0 collective-permute-done.7.b2_hbm
  40.0 0.0 copy-start.12
  40.0 3.0 %all-to-all-start = ((bf16[32,32,256]{2,1,0:T(8,128)(2,1)}), bf16[32,32,256]{2,1,0:T(8,128)(2,1)S(1)}, u32[]{:S(2)}, u32[]{:S(2)}) async-start(bf16[32,32,256]{2,1,0:T(8,128)(2,1)} %shard_map.89), calls=%async_computation | async-start | bytes 1048576 | tf_op jit(solution)/shard_map/all_to_all | solution.py:519
  43.1 0.1 collective-permute-start.8
  43.2 0.4 collective-permute-start.9
  43.7 1.2 %collective-permute-done.8.b1_hbm = bf16[2,128,512]{2,1,0:T(8,128)(2,1)S(1)} collective-permute-done((bf16[2,128,512]{2,1,0:T(8,128)(2,1)}, bf16[2,128,512]{2,1,0:T(8,128)(2,1)S(1)}, u32[]{:S(2)}, u32[]{:S(2)}) %collective-permute-start.8) | collective-permute-done | bytes 262176 | tf_op jit(solution)/shard_map/ppermute | solution.py:437
  44.9 0.0 copy-start.13
  44.9 0.2 collective-permute-done.9.b3_hbm
  45.1 0.0 copy-done.12
  45.1 0.5 copy-done.13
  45.6 0.2 copy-done.14
  45.8 10.1 %shard_map.91 = (bf16[2,512,2048]{2,1,0:T(8,128)(2,1)}, bf16[4,2048,512]{2,1,0:T(8,128)(2,1)}) custom-call(bf16[2,128,512]{2,1,0:T(8,128)(2,1)} %shard_map.88.block_hbm.b0_hbm, bf16[2,128,512]{2,1,0:T(8,128)(2,1)} %copy-done.13, bf16[2,128,512]{2,1,0:T(8,128)(2,1)} %copy-done.12, bf16[2,128,512]{2,1,0:T(8,128)(2,1)} %copy-done.14, ...), custom_call_target="tpu_custom_call" | custom-call | flops 1610612736 | bytes 13651968 | tf_op jit(solution)/shard_map/pallas_call | solution.py:422
  55.9 3.3 %all-to-all-done.summed_hbm = bf16[32,32,256]{2,1,0:T(8,128)(2,1)S(1)} async-done(((bf16[32,32,256]{2,1,0:T(8,128)(2,1)}), bf16[32,32,256]{2,1,0:T(8,128)(2,1)S(1)}, u32[]{:S(2)}, u32[]{:S(2)}) %all-to-all-start) | async-done | bytes 524320 | tf_op jit(solution)/shard_map/all_to_all | solution.py:519
  59.3 0.8 copy-done
  60.1 7.1 %shard_map.92 = bf16[8,32,384]{2,1,0:T(8,128)(2,1)} custom-call(bf16[32,32,256]{2,1,0:T(8,128)(2,1)} %copy-done, bf16[2,512,2048]{2,1,0:T(8,128)(2,1)} %get-tuple-element.33.factor_hbm, bf16[2,512,512]{2,1,0:T(8,128)(2,1)} %core_hbm.1, bf16[4,2048,512]{2,1,0:T(8,128)(2,1)} %get-tuple-element.34.cross_hbm, s32[8,128]{1,0:T(8,128)} %get-tuple-element.35.starts_hbm), custom_call_target="tpu_custom_call" | custom-call | bytes 14356480 | tf_op jit(solution)/shard_map/pallas_call | solution.py:422
  67.2 3.6 %all-to-all-start.1 = ((bf16[8,32,384]{2,1,0:T(8,128)(2,1)}), bf16[8,32,384]{2,1,0:T(8,128)(2,1)S(1)}, u32[]{:S(2)}, u32[]{:S(2)}) async-start(bf16[8,32,384]{2,1,0:T(8,128)(2,1)} %shard_map.92), calls=%async_computation.1 | async-start | bytes 393216 | tf_op jit(solution)/shard_map/all_to_all | solution.py:562
  70.8 4.1 %shard_map.93.slots_hbm = s32[2,768]{1,0:T(2,128)} custom-call(s32[2,2048]{1,0:T(2,128)} %blocks_hbm.5), custom_call_target="tpu_custom_call" | custom-call | bytes 22528 | tf_op jit(solution)/shard_map/pallas_call | solution.py:422
  74.9 3.7 %all-to-all-done.1.g0_hbm = bf16[8,32,384]{2,1,0:T(8,128)(2,1)S(1)} async-done(((bf16[8,32,384]{2,1,0:T(8,128)(2,1)}), bf16[8,32,384]{2,1,0:T(8,128)(2,1)S(1)}, u32[]{:S(2)}, u32[]{:S(2)}) %all-to-all-start.1) | async-done | bytes 196640 | tf_op jit(solution)/shard_map/all_to_all | solution.py:562
  78.6 1.2 %collective-permute-start.11 = (bf16[8,32,384]{2,1,0:T(8,128)(2,1)S(1)}, bf16[8,32,384]{2,1,0:T(8,128)(2,1)S(1)}, u32[]{:S(2)}, u32[]{:S(2)}) collective-permute-start(bf16[8,32,384]{2,1,0:T(8,128)(2,1)S(1)} %all-to-all-done.1.g0_hbm), channel_id=1, source_target_pairs={{0,16},{8,24},{16,0},{24,8},{1,17},{9,25},{17,1},{25,9},{2,18},{10... | collective-permute-start | bytes 589832 | tf_op jit(solution)/shard_map/ppermute | solution.py:437
  79.8 0.0 collective-permute-start.10
  79.8 4.5 %collective-permute-done.11.g2_hbm = bf16[8,32,384]{2,1,0:T(8,128)(2,1)S(1)} collective-permute-done((bf16[8,32,384]{2,1,0:T(8,128)(2,1)S(1)}, bf16[8,32,384]{2,1,0:T(8,128)(2,1)S(1)}, u32[]{:S(2)}, u32[]{:S(2)}) %collective-permute-start.11) | collective-permute-done | bytes 196640 | tf_op jit(solution)/shard_map/ppermute | solution.py:437
  84.3 0.0 collective-permute-start.12
  84.3 0.0 collective-permute-done.10.g1_hbm
  84.3 0.0 copy-start.3
  84.3 1.4 %collective-permute-done.12.g3_hbm = bf16[8,32,384]{2,1,0:T(8,128)(2,1)S(1)} collective-permute-done((bf16[8,32,384]{2,1,0:T(8,128)(2,1)S(1)}, bf16[8,32,384]{2,1,0:T(8,128)(2,1)S(1)}, u32[]{:S(2)}, u32[]{:S(2)}) %collective-permute-start.12) | collective-permute-done | bytes 196640 | tf_op jit(solution)/shard_map/ppermute | solution.py:437
  85.7 0.0 copy-done.1
  85.7 0.0 copy-done.2
  85.7 0.0 copy-done.3
  85.7 0.0 copy-start.4
  85.7 0.7 copy-done.4
  86.4 4.1 %shard_map.94 = (f32[1024,256]{1,0:T(8,128)}, f32[1024,256]{1,0:T(8,128)}) custom-call(bf16[8,32,384]{2,1,0:T(8,128)(2,1)} %copy-done.1, bf16[8,32,384]{2,1,0:T(8,128)(2,1)} %copy-done.3, bf16[8,32,384]{2,1,0:T(8,128)(2,1)} %copy-done.2, bf16[8,32,384]{2,1,0:T(8,128)(2,1)} %copy-done.4, s32[2,768]{1,0:T(2,128)} %shard_map.93.slots_hbm, f32[1024,256]{1,0:T(8,128)} %w_hbm.3, ...), custom_call_target="tpu_custom_call" | custom-call | bytes 4986880 | tf_op jit(solution)/shard_map/pallas_call | solution.py:422
  (5 shorter events, 0.0 us)
Async XLA Ops:
  2.9 16.1 %collective-permute-start.6 = (bf16[384,128]{1,0:T(8,128)(2,1)}, bf16[384,128]{1,0:T(8,128)(2,1)S(1)}, u32[]{:S(2)}, u32[]{:S(2)}) collective-permute-start(bf16[384,128]{1,0:T(8,128)(2,1)} %shard_map.86.refs_0_), channel_id=1, source_target_pairs={{0,7},{1,6},{2,5},{3,4},{4,3},{5,2},{6,1},{7,0},{8,15},{9,14},{10,... | collective-permute-start | bytes 294920 | tf_op jit(solution)/shard_map/ppermute | solution.py:437
  9.0 12.1 %collective-permute-start.5 = (bf16[384,128]{1,0:T(8,128)(2,1)}, bf16[384,128]{1,0:T(8,128)(2,1)S(1)}, u32[]{:S(2)}, u32[]{:S(2)}) collective-permute-start(bf16[384,128]{1,0:T(8,128)(2,1)} %shard_map.86.refs_0_), channel_id=1, source_target_pairs={{0,6},{1,7},{2,4},{3,5},{4,2},{5,3},{6,0},{7,1},{8,14},{9,15},{10,... | collective-permute-start | bytes 294920 | tf_op jit(solution)/shard_map/ppermute | solution.py:437
  9.2 15.6 %collective-permute-start.4 = (bf16[384,128]{1,0:T(8,128)(2,1)}, bf16[384,128]{1,0:T(8,128)(2,1)S(1)}, u32[]{:S(2)}, u32[]{:S(2)}) collective-permute-start(bf16[384,128]{1,0:T(8,128)(2,1)} %shard_map.86.refs_0_), channel_id=1, source_target_pairs={{0,5},{1,4},{2,7},{3,6},{4,1},{5,0},{6,3},{7,2},{8,13},{9,12},{10,... | collective-permute-start | bytes 294920 | tf_op jit(solution)/shard_map/ppermute | solution.py:437
  9.9 16.0 %collective-permute-start.3 = (bf16[384,128]{1,0:T(8,128)(2,1)}, bf16[384,128]{1,0:T(8,128)(2,1)S(1)}, u32[]{:S(2)}, u32[]{:S(2)}) collective-permute-start(bf16[384,128]{1,0:T(8,128)(2,1)} %shard_map.86.refs_0_), channel_id=1, source_target_pairs={{0,4},{1,5},{2,6},{3,7},{4,0},{5,1},{6,2},{7,3},{8,12},{9,13},{10,... | collective-permute-start | bytes 294920 | tf_op jit(solution)/shard_map/ppermute | solution.py:437
  12.0 14.0 %collective-permute-start.2 = (bf16[384,128]{1,0:T(8,128)(2,1)}, bf16[384,128]{1,0:T(8,128)(2,1)S(1)}, u32[]{:S(2)}, u32[]{:S(2)}) collective-permute-start(bf16[384,128]{1,0:T(8,128)(2,1)} %shard_map.86.refs_0_), channel_id=1, source_target_pairs={{0,3},{1,2},{2,1},{3,0},{4,7},{5,6},{6,5},{7,4},{8,11},{9,10},{10,... | collective-permute-start | bytes 294920 | tf_op jit(solution)/shard_map/ppermute | solution.py:437
  18.9 8.0 %copy-start.5 = (bf16[384,128]{1,0:T(8,128)(2,1)}, bf16[384,128]{1,0:T(8,128)(2,1)S(1)}, u32[]{:S(2)}) copy-start(bf16[384,128]{1,0:T(8,128)(2,1)S(1)} %collective-permute-done.6.refs_7_) | copy-start | bytes 294916
  19.0 8.0 %collective-permute-start.1 = (bf16[384,128]{1,0:T(8,128)(2,1)}, bf16[384,128]{1,0:T(8,128)(2,1)S(1)}, u32[]{:S(2)}, u32[]{:S(2)}) collective-permute-start(bf16[384,128]{1,0:T(8,128)(2,1)} %shard_map.86.refs_0_), channel_id=1, source_target_pairs={{0,2},{1,3},{2,0},{3,1},{4,6},{5,7},{6,4},{7,5},{8,10},{9,11},{10,... | collective-permute-start | bytes 294920 | tf_op jit(solution)/shard_map/ppermute | solution.py:437
  21.1 5.9 %copy-start.6 = (bf16[384,128]{1,0:T(8,128)(2,1)}, bf16[384,128]{1,0:T(8,128)(2,1)S(1)}, u32[]{:S(2)}) copy-start(bf16[384,128]{1,0:T(8,128)(2,1)S(1)} %collective-permute-done.5.refs_6_) | copy-start | bytes 294916
  21.1 5.8 %collective-permute-start = (bf16[384,128]{1,0:T(8,128)(2,1)}, bf16[384,128]{1,0:T(8,128)(2,1)S(1)}, u32[]{:S(2)}, u32[]{:S(2)}) collective-permute-start(bf16[384,128]{1,0:T(8,128)(2,1)} %shard_map.86.refs_0_), channel_id=1, source_target_pairs={{0,1},{1,0},{2,3},{3,2},{4,5},{5,4},{6,7},{7,6},{8,9},{9,8},{10,11... | collective-permute-start | bytes 294920 | tf_op jit(solution)/shard_map/ppermute | solution.py:437
  24.8 2.1 %copy-start.7 = (bf16[384,128]{1,0:T(8,128)(2,1)}, bf16[384,128]{1,0:T(8,128)(2,1)S(1)}, u32[]{:S(2)}) copy-start(bf16[384,128]{1,0:T(8,128)(2,1)S(1)} %collective-permute-done.4.refs_5_) | copy-start | bytes 294916
  26.0 1.0 %copy-start.8 = (bf16[384,128]{1,0:T(8,128)(2,1)}, bf16[384,128]{1,0:T(8,128)(2,1)S(1)}, u32[]{:S(2)}) copy-start(bf16[384,128]{1,0:T(8,128)(2,1)S(1)} %collective-permute-done.3.refs_4_) | copy-start | bytes 294916
  26.0 1.0 %copy-start.9 = (bf16[384,128]{1,0:T(8,128)(2,1)}, bf16[384,128]{1,0:T(8,128)(2,1)S(1)}, u32[]{:S(2)}) copy-start(bf16[384,128]{1,0:T(8,128)(2,1)S(1)} %collective-permute-done.2.refs_3_) | copy-start | bytes 294916
  26.9 0.6 copy-start.10
  27.5 0.6 copy-start.11
  30.5 9.6 %collective-permute-start.7 = (bf16[2,128,512]{2,1,0:T(8,128)(2,1)}, bf16[2,128,512]{2,1,0:T(8,128)(2,1)S(1)}, u32[]{:S(2)}, u32[]{:S(2)}) collective-permute-start(bf16[2,128,512]{2,1,0:T(8,128)(2,1)} %shard_map.88.block_hbm.b0_hbm), channel_id=1, source_target_pairs={{0,16},{8,24},{16,0},{24,8},{1,17},{9,25},{17,1},{25,9},{2,18},{10... | collective-permute-start | bytes 786440 | tf_op jit(solution)/shard_map/ppermute | solution.py:437
  40.0 5.0 %copy-start.12 = (bf16[2,128,512]{2,1,0:T(8,128)(2,1)}, bf16[2,128,512]{2,1,0:T(8,128)(2,1)S(1)}, u32[]{:S(2)}) copy-start(bf16[2,128,512]{2,1,0:T(8,128)(2,1)S(1)} %collective-permute-done.7.b2_hbm) | copy-start | bytes 786436
  40.0 19.2 %all-to-all-start = ((bf16[32,32,256]{2,1,0:T(8,128)(2,1)}), bf16[32,32,256]{2,1,0:T(8,128)(2,1)S(1)}, u32[]{:S(2)}, u32[]{:S(2)}) async-start(bf16[32,32,256]{2,1,0:T(8,128)(2,1)} %shard_map.89), calls=%async_computation | async-start | bytes 1048576 | tf_op jit(solution)/shard_map/all_to_all | solution.py:519
  43.1 1.8 %collective-permute-start.8 = (bf16[2,128,512]{2,1,0:T(8,128)(2,1)}, bf16[2,128,512]{2,1,0:T(8,128)(2,1)S(1)}, u32[]{:S(2)}, u32[]{:S(2)}) collective-permute-start(bf16[2,128,512]{2,1,0:T(8,128)(2,1)} %shard_map.88.block_hbm.b0_hbm), channel_id=1, source_target_pairs={{0,8},{8,0},{16,24},{24,16},{1,9},{9,1},{17,25},{25,17},{2,10},{10... | collective-permute-start | bytes 786440 | tf_op jit(solution)/shard_map/ppermute | solution.py:437
  43.2 1.8 %collective-permute-start.9 = (bf16[2,128,512]{2,1,0:T(8,128)(2,1)S(1)}, bf16[2,128,512]{2,1,0:T(8,128)(2,1)S(1)}, u32[]{:S(2)}, u32[]{:S(2)}) collective-permute-start(bf16[2,128,512]{2,1,0:T(8,128)(2,1)S(1)} %collective-permute-done.7.b2_hbm), channel_id=1, source_target_pairs={{0,8},{8,0},{16,24},{24,16},{1,9},{9,1},{17,25},{25,17},{2,10},{10... | collective-permute-start | bytes 786440 | tf_op jit(solution)/shard_map/ppermute | solution.py:437
  44.9 0.7 copy-start.13
  45.1 0.7 copy-start.14
  59.3 0.8 copy-start
  67.2 11.4 %all-to-all-start.1 = ((bf16[8,32,384]{2,1,0:T(8,128)(2,1)}), bf16[8,32,384]{2,1,0:T(8,128)(2,1)S(1)}, u32[]{:S(2)}, u32[]{:S(2)}) async-start(bf16[8,32,384]{2,1,0:T(8,128)(2,1)} %shard_map.92), calls=%async_computation.1 | async-start | bytes 393216 | tf_op jit(solution)/shard_map/all_to_all | solution.py:562
  78.6 7.1 %copy-start.1 = (bf16[8,32,384]{2,1,0:T(8,128)(2,1)}, bf16[8,32,384]{2,1,0:T(8,128)(2,1)S(1)}, u32[]{:S(2)}) copy-start(bf16[8,32,384]{2,1,0:T(8,128)(2,1)S(1)} %all-to-all-done.1.g0_hbm) | copy-start | bytes 589828
  78.6 5.7 %collective-permute-start.11 = (bf16[8,32,384]{2,1,0:T(8,128)(2,1)S(1)}, bf16[8,32,384]{2,1,0:T(8,128)(2,1)S(1)}, u32[]{:S(2)}, u32[]{:S(2)}) collective-permute-start(bf16[8,32,384]{2,1,0:T(8,128)(2,1)S(1)} %all-to-all-done.1.g0_hbm), channel_id=1, source_target_pairs={{0,16},{8,24},{16,0},{24,8},{1,17},{9,25},{17,1},{25,9},{2,18},{10... | collective-permute-start | bytes 589832 | tf_op jit(solution)/shard_map/ppermute | solution.py:437
  79.8 4.5 %collective-permute-start.10 = (bf16[8,32,384]{2,1,0:T(8,128)(2,1)S(1)}, bf16[8,32,384]{2,1,0:T(8,128)(2,1)S(1)}, u32[]{:S(2)}, u32[]{:S(2)}) collective-permute-start(bf16[8,32,384]{2,1,0:T(8,128)(2,1)S(1)} %all-to-all-done.1.g0_hbm), channel_id=1, source_target_pairs={{0,8},{8,0},{16,24},{24,16},{1,9},{9,1},{17,25},{25,17},{2,10},{10... | collective-permute-start | bytes 589832 | tf_op jit(solution)/shard_map/ppermute | solution.py:437
  84.3 1.4 %copy-start.2 = (bf16[8,32,384]{2,1,0:T(8,128)(2,1)}, bf16[8,32,384]{2,1,0:T(8,128)(2,1)S(1)}, u32[]{:S(2)}) copy-start(bf16[8,32,384]{2,1,0:T(8,128)(2,1)S(1)} %collective-permute-done.11.g2_hbm) | copy-start | bytes 589828
  84.3 1.4 %collective-permute-start.12 = (bf16[8,32,384]{2,1,0:T(8,128)(2,1)S(1)}, bf16[8,32,384]{2,1,0:T(8,128)(2,1)S(1)}, u32[]{:S(2)}, u32[]{:S(2)}) collective-permute-start(bf16[8,32,384]{2,1,0:T(8,128)(2,1)S(1)} %collective-permute-done.11.g2_hbm), channel_id=1, source_target_pairs={{0,8},{8,0},{16,24},{24,16},{1,9},{9,1},{17,25},{25,17},{2,10},{10... | collective-permute-start | bytes 589832 | tf_op jit(solution)/shard_map/ppermute | solution.py:437
  84.3 1.4 %copy-start.3 = (bf16[8,32,384]{2,1,0:T(8,128)(2,1)}, bf16[8,32,384]{2,1,0:T(8,128)(2,1)S(1)}, u32[]{:S(2)}) copy-start(bf16[8,32,384]{2,1,0:T(8,128)(2,1)S(1)} %collective-permute-done.10.g1_hbm) | copy-start | bytes 589828
  85.7 0.7 copy-start.4

commit v14 on v13

--- a/solution.py
+++ b/solution.py
@@ -167,26 +167,24 @@
 
 
 def order_kernel(
-    count, points, owners,
+    u, count, points, owners,
     blocks_hbm, pivots_hbm, ids_hbm, starts_hbm, chosen_hbm,
     blocks, pivots, ids, starts, chosen, sems,
 ):
     wait_all(start_all([(blocks_hbm, blocks), (pivots_hbm, pivots)], sems))
     before = before_matrix(count)
     groups = blocks.shape[1] // count
-    for u in range(UPDATES):
-        pivot = pivots[u : u + 1, :]
-        found = jnp.zeros((8, pivot.shape[1]), f32)
-        for g in range(groups):
-            n = u * groups + g
-            indices = blocks[u : u + 1, g * count : (g + 1) * count]
-            marks, rank, start = owners_of(indices, before, points, owners)
-            place = sorted_places(marks, rank, start)
-            ids[n : n + 1, :] = sorted_points(indices, place)
-            starts[n : n + 1, :] = lane_row(start)
-            at_pivot = one_hot(iota((count, pivot.shape[1]), 0) + g * count == pivot)
-            found += mm(two_digits(place + g * count), at_pivot, 1, 0)
-        chosen[u : u + 1, :] = from_digits(found)
+    pivot = pivots[u : u + 1, :]
+    found = jnp.zeros((8, pivot.shape[1]), f32)
+    for g in range(groups):
+        indices = blocks[u : u + 1, g * count : (g + 1) * count]
+        marks, rank, start = owners_of(indices, before, points, owners)
+        place = sorted_places(marks, rank, start)
+        ids[g : g + 1, :] = sorted_points(indices, place)
+        starts[g : g + 1, :] = lane_row(start)
+        at_pivot = one_hot(iota((count, pivot.shape[1]), 0) + g * count == pivot)
+        found += mm(two_digits(place + g * count), at_pivot, 1, 0)
+    chosen[0:1, :] = from_digits(found)
     wait_all(start_all([(ids, ids_hbm), (starts, starts_hbm), (chosen, chosen_hbm)], sems))
 
 
@@ -273,19 +271,21 @@
 
 
 def factors_kernel(
-    b0_hbm, b1_hbm, b2_hbm, b3_hbm, ids_hbm, pivots_hbm, factor_hbm, cross_hbm,
+    b0_hbm, b1_hbm, b2_hbm, b3_hbm, ids0_hbm, ids1_hbm, pivots0_hbm, pivots1_hbm, factor_hbm, cross_hbm,
     feats, ids, pivots, factor, cross, sems,
 ):
     row = lax.axis_index("rows")
     groups, _, width, count = feats.shape
     pairs = [(b_hbm, feats.at[k]) for k, b_hbm in enumerate((b0_hbm, b1_hbm, b2_hbm, b3_hbm))]
-    wait_all(start_all(pairs + [(ids_hbm, ids), (pivots_hbm, pivots)], sems))
+    pairs += [(ids0_hbm, ids.at[0]), (ids1_hbm, ids.at[1])]
+    pairs += [(pivots0_hbm, pivots.at[0]), (pivots1_hbm, pivots.at[1])]
+    wait_all(start_all(pairs, sems))
     places = [lax.bitwise_xor(row, k) for k in range(groups)]
     rights = [[extended(feats[k, u], 0, False) for k in range(groups)] for u in range(UPDATES)]
     for u in range(UPDATES):
-        chosen_feats = jnp.zeros((width, pivots.shape[1]), f32)
+        chosen_feats = jnp.zeros((width, pivots.shape[2]), f32)
         for k in range(groups):
-            chosen = iota((count, pivots.shape[1]), 0) + places[k] * count == pivots[u : u + 1, :]
+            chosen = iota((count, pivots.shape[2]), 0) + places[k] * count == pivots[u, 0:1, :]
             chosen_feats += mm(feats[k, u], one_hot(chosen), 1, 0)
         left = extended(chosen_feats.T, 1, True)
         for k in range(groups):
@@ -296,12 +296,12 @@
     lefts, left_points = [], []
     for k in range(groups):
         lefts.append(extended(feats[k, 0].astype(f32).T, 1, True))
-        points = ids[pl.ds(places[k], 1), :].astype(f32)
+        points = ids[0, pl.ds(places[k], 1), :].astype(f32)
         left_points.append(jnp.broadcast_to(points, (8, count)).T[:, 0:1])
     left, left_points = jnp.concatenate(lefts, axis=0), jnp.concatenate(left_points, axis=0)
     sent = 1
     for m in range(groups):
-        right_points = ids[pl.ds(groups + places[m], 1), :].astype(f32)
+        right_points = ids[1, pl.ds(places[m], 1), :].astype(f32)
         power = exponent(left, rights[1][m])
         power = jnp.where(left_points == right_points, math.log2(1.0 + ridge_term), power)
         cross[m] = jnp.exp2(power).astype(bf16).reshape(groups, count, count)
@@ -318,20 +318,18 @@
 
 def chain_kernel(
     cap, owners,
-    summed_hbm, factor_hbm, core_hbm, cross_hbm, starts_hbm, out_hbm,
-    summed, factor, core, cross, starts, packed, sems,
+    summed, factor_hbm, core_hbm, cross_hbm, starts0_hbm, starts1_hbm, out_hbm,
+    factor, core, cross, starts0, starts1, packed, sems,
 ):
     groups, _, count = cross.shape
     own = summed.shape[1] // (2 * UPDATES)
-    pairs = [(summed_hbm, summed)]
+    pairs, starts = [], (starts0, starts1)
     for u in range(UPDATES):
         pairs += [(factor_hbm.at[u], factor.at[u]), (core_hbm.at[u], core.at[u])]
         if u == 0:
-            pairs += [(starts_hbm, starts)]
+            pairs += [(starts0_hbm, starts0), (starts1_hbm, starts1)]
             pairs += [(cross_hbm.at[g], cross.at[g]) for g in range(groups)]
     reads = start_all(pairs, sems)
-    first, *reads = reads
-    first.wait()
     step = None
     for u in range(UPDATES):
         sums = []
@@ -341,11 +339,11 @@
                 part += summed[g * owners + o, 2 * own * u : 2 * own * (u + 1), :].astype(f32)
             part = jnp.concatenate([part[:own], part[own:]], axis=1)
             if u:
-                reads[3 + g].wait()
+                reads[4 + g].wait()
                 part -= mix_per_step * mm(step, cross[g], 1, 0)
             sums.append(part)
         resid = jnp.concatenate(sums, axis=1)
-        wait_all(reads[0:3] if u == 0 else reads[3 + groups :])
+        wait_all(reads[0:4] if u == 0 else reads[4 + groups :])
         proj = mm(resid.astype(bf16), factor[u], 1, 1)
         lifted = mm(proj.astype(bf16), core[u], 1, 1).astype(bf16)
         step = (resid - mm(lifted, factor[u], 1, 0)).astype(bf16)
@@ -354,7 +352,7 @@
             lanes = []
             for g in range(groups):
                 part = step[:, g * count : (g + 1) * count].astype(f32)
-                back = lax.rem(count - starts[u * groups + g, o], count)
+                back = lax.rem(count - starts[u][g, o], count)
                 lanes.append(pltpu.roll(part, back, 1)[:, :cap])
             packed[o, 2 * own * u : 2 * own * (u + 1), :] = jnp.concatenate(
                 [jnp.concatenate(lanes[h * half : (h + 1) * half], axis=1) for h in range(2)], axis=0
@@ -473,8 +471,22 @@
         *given,
         sems=(4, 1 + 2 * UPDATES),
     )
-    again, row_starts = lax.optimization_barrier((packed, row_starts))
+    again, row_starts, later_index = lax.optimization_barrier((packed, row_starts, block_index))
     came.update({k: swap(again, "pts", k) for k in (2, 1)})
+
+    def ordered(u, indices):
+        kept = [like((rows, count), i32), like((8, 128), i32), like((8, rank), i32)]
+        return call(
+            functools.partial(order_kernel, u, count, points, owners),
+            kept,
+            [block_index, pivot_index, *kept],
+            indices,
+            pivot_index,
+            sems=(3,),
+        )
+
+    ids, starts, chosen = ordered(0, later_index)
+    row_starts, ids = lax.optimization_barrier((row_starts, ids))
     feats = like((UPDATES, width, count))
     inside_starts = pltpu.SMEM(row_starts.shape, i32)
     (mine,) = call(
@@ -490,7 +502,7 @@
         *[came[k] for k in range(1, owners)],
         row_starts,
         sems=(owners + 1,),
-        grant=60,
+        grant=48,
     )
     beside, across = swap(mine, "rows", 1), swap(mine, "rows", 2)
     pieces = like((devices, deep, count // 2))
@@ -506,16 +518,10 @@
         flops=2.0 * UPDATES * points * count * (2 * width + outputs),
     )
     pieces, later_index = lax.optimization_barrier((pieces, block_index))
-    kept = [like((UPDATES * rows, count), i32), like((8, 128), i32), like((UPDATES, rank), i32)]
-    ids, starts, chosen = call(
-        functools.partial(order_kernel, count, points, owners),
-        kept,
-        [block_index, pivot_index, *kept],
-        later_index,
-        pivot_index,
-        sems=(3,),
-    )
-    pieces, across, ids = lax.optimization_barrier((pieces, across, ids))
+    later_ids, later_starts, later_chosen = ordered(1, later_index)
+    pieces, beside, across, later_ids = lax.optimization_barrier(
+        (pieces, beside, across, later_ids)
+    )
     summed = lax.all_to_all(pieces, ("rows", "pts"), 0, 0, tiled=True)
     kept = [like((UPDATES, rank, block)), like((rows, block, count))]
     factor, cross = call(
@@ -523,8 +529,8 @@
         kept,
         [
             like((rows, *feats.shape)),
-            ids,
-            chosen,
+            like((UPDATES, *ids.shape), i32),
+            like((UPDATES, *chosen.shape), i32),
             kept[0],
             like((rows, rows, count, count)),
         ],
@@ -533,23 +539,27 @@
         across,
         swap(across, "rows", 1),
         ids,
+        later_ids,
         chosen,
+        later_chosen,
         sems=(rows * rows + 2,),
-        grant=60,
+        grant=57,
         flops=2.0 * width * block * (UPDATES * rank + block),
     )
     pieces = like((owners, deep, half * cap))
     (steps,) = call(
         functools.partial(chain_kernel, cap, owners),
         [pieces],
-        [summed, factor, core, cross, inside_starts, pieces],
+        [factor, core, cross, inside_starts, inside_starts, pieces],
         summed,
         factor,
         core,
         cross,
         starts,
+        later_starts,
+        near=1,
         sems=(2 * UPDATES + 2 + rows,),
-        grant=60,
+        grant=52,
     )
     steps, later_index = lax.optimization_barrier((steps, block_index))
     (slots,) = call(
@@ -583,7 +593,7 @@
         coefficients,
         momentum,
         sems=(1 + rows + 2 * parts, 2 * parts),
-        grant=60,
+        grant=48,
     )
 
 

time: 91.4 us -> 92.5 us (1.012)
  local copies, waits for them, and re-layouts: 3.42 us -> 6.1 us
  waiting for transfers between devices: 19.3 us -> 16.8 us
    ppermute x13, waiting for transfers between devices: 12.2 us -> 9.34 us  [swap(): lax.ppermute(value, axis, [(i, i ^ k) for i in range(lax.axis_size(axis))])]
    unnamed x30 -> x24, local copies, waits for them, and re-layouts: 3.42 us -> 6.1 us
    pallas_call x9 -> x10, Pallas kernels: 42.6 us -> 43.3 us  [call(): pl.pallas_call(body, out_shape=outs, in_specs=[VMEM] * near + [HBM] * (le...]
  transfers between devices with their start and end apart: 15 -> 15, of which waited for: 9 -> 7; matrix products, arithmetic and copies ran while one was open for 0% -> 0% of each run, Pallas kernels for 30% -> 31%
where the time goes in v14:
time: 92.5 us; the launch traced here: 91.5 us
  Pallas kernels  43.3 us (47%)
  starting transfers between devices  24.4 us (26%)
  waiting for transfers between devices  16.8 us (18%)
  local copies, waits for them, and re-layouts  6.1 us (7%)
  between operations  0.98 us (1%)
    pallas_call x10, Pallas kernels, call(): pl.pallas_call(body, out_shape=outs, in_specs=[VMEM] * near + [HBM] * (le...  43.3 us
    ppermute x13, starting transfers between devices, swap(): lax.ppermute(value, axis, [(i, i ^ k) for i in range(lax.axis_size(axis))])  17.3 us
    ppermute x13, waiting for transfers between devices, swap(): lax.ppermute(value, axis, [(i, i ^ k) for i in range(lax.axis_size(axis))])  9.34 us
    unnamed x24, local copies, waits for them, and re-layouts  6.1 us
    all_to_all x1, waiting for transfers between devices, with_kernels(): summed = lax.all_to_all(pieces, ('rows', 'pts'), 0, 0, tiled=True)  3.72 us
    all_to_all x1, waiting for transfers between devices, with_kernels(): got = lax.all_to_all(steps, 'pts', 0, 0, tiled=True)  3.71 us
    all_to_all x1, starting transfers between devices, with_kernels(): got = lax.all_to_all(steps, 'pts', 0, 0, tiled=True)  3.62 us
    all_to_all x1, starting transfers between devices, with_kernels(): summed = lax.all_to_all(pieces, ('rows', 'pts'), 0, 0, tiled=True)  3.43 us
  transfers between devices with their start and end apart: 15, of which 7 were waited for; matrix products, arithmetic and copies ran while one was open for 0% of the time, Pallas kernels for 31%

profile of v14, /device:TPU:0, one launch (start us, length us, event | category | flops | bytes accessed | tf_op | source)
XLA Modules:
  0.0 91.5 jit_solution(153699318849594392)
XLA Ops:
  0.6 2.2 %shard_map.86.refs_0_ = bf16[384,128]{1,0:T(8,128)(2,1)} custom-call(s32[2,2048]{1,0:T(2,128)} %blocks_hbm.6, bf16[1024,128]{1,0:T(8,128)(2,1)} %feats_hbm.3), custom_call_target="tpu_custom_call" | custom-call | bytes 376832 | tf_op jit(solution)/shard_map/pallas_call | solution.py:420
  2.9 6.1 %collective-permute-start.6 = (bf16[384,128]{1,0:T(8,128)(2,1)}, bf16[384,128]{1,0:T(8,128)(2,1)S(1)}, u32[]{:S(2)}, u32[]{:S(2)}) collective-permute-start(bf16[384,128]{1,0:T(8,128)(2,1)} %shard_map.86.refs_0_), channel_id=1, source_target_pairs={{0,7},{1,6},{2,5},{3,4},{4,3},{5,2},{6,1},{7,0},{8,15},{9,14},{10,... | collective-permute-start | bytes 294920 | tf_op jit(solution)/shard_map/ppermute | solution.py:435
  9.0 0.2 collective-permute-start.5
  9.2 0.7 collective-permute-start.4
  9.9 2.0 %collective-permute-start.3 = (bf16[384,128]{1,0:T(8,128)(2,1)}, bf16[384,128]{1,0:T(8,128)(2,1)S(1)}, u32[]{:S(2)}, u32[]{:S(2)}) collective-permute-start(bf16[384,128]{1,0:T(8,128)(2,1)} %shard_map.86.refs_0_), channel_id=1, source_target_pairs={{0,4},{1,5},{2,6},{3,7},{4,0},{5,1},{6,2},{7,3},{8,12},{9,13},{10,... | collective-permute-start | bytes 294920 | tf_op jit(solution)/shard_map/ppermute | solution.py:435
  12.0 2.3 %collective-permute-start.2 = (bf16[384,128]{1,0:T(8,128)(2,1)}, bf16[384,128]{1,0:T(8,128)(2,1)S(1)}, u32[]{:S(2)}, u32[]{:S(2)}) collective-permute-start(bf16[384,128]{1,0:T(8,128)(2,1)} %shard_map.86.refs_0_), channel_id=1, source_target_pairs={{0,3},{1,2},{2,1},{3,0},{4,7},{5,6},{6,5},{7,4},{8,11},{9,10},{10,... | collective-permute-start | bytes 294920 | tf_op jit(solution)/shard_map/ppermute | solution.py:435
  14.2 4.7 %shard_map.87 = (bf16[2,256,1024]{2,1,0:T(8,128)(2,1)}, f32[2,256,512]{2,1,0:T(8,128)}, s32[8,128]{1,0:T(8,128)}) custom-call(s32[2,2048]{1,0:T(2,128)} %blocks_hbm.6, f32[1024,256]{1,0:T(8,128)} %w_hbm.3, f32[1024,256]{1,0:T(8,128)} %z_hbm.3, bf16[1024,256]{1,0:T(8,128)(2,1)} %t_hbm.1), custom_call_target="tpu_custom_call" | custom-call | bytes 4739072 | tf_op jit(solution)/shard_map/pallas_call | solution.py:420
  18.9 0.0 collective-permute-done.6.refs_7_
  18.9 2.1 %collective-permute-start.1 = (bf16[384,128]{1,0:T(8,128)(2,1)}, bf16[384,128]{1,0:T(8,128)(2,1)S(1)}, u32[]{:S(2)}, u32[]{:S(2)}) collective-permute-start(bf16[384,128]{1,0:T(8,128)(2,1)} %shard_map.86.refs_0_), channel_id=1, source_target_pairs={{0,2},{1,3},{2,0},{3,1},{4,6},{5,7},{6,4},{7,5},{8,10},{9,11},{10,... | collective-permute-start | bytes 294920 | tf_op jit(solution)/shard_map/ppermute | solution.py:435
  21.1 0.0 collective-permute-done.5.refs_6_
  21.1 0.9 %collective-permute-start = (bf16[384,128]{1,0:T(8,128)(2,1)}, bf16[384,128]{1,0:T(8,128)(2,1)S(1)}, u32[]{:S(2)}, u32[]{:S(2)}) collective-permute-start(bf16[384,128]{1,0:T(8,128)(2,1)} %shard_map.86.refs_0_), channel_id=1, source_target_pairs={{0,1},{1,0},{2,3},{3,2},{4,5},{5,4},{6,7},{7,6},{8,9},{9,8},{10,11... | collective-permute-start | bytes 294920 | tf_op jit(solution)/shard_map/ppermute | solution.py:435
  22.0 2.9 %shard_map.88 = (s32[4,512]{1,0:T(4,128)}, s32[8,128]{1,0:T(8,128)}, s32[8,512]{1,0:T(8,128)}) custom-call(s32[2,2048]{1,0:T(2,128)} %blocks_hbm.6, s32[2,512]{1,0:T(2,128)} %pivots_hbm.3), custom_call_target="tpu_custom_call" | custom-call | bytes 49152 | tf_op jit(solution)/shard_map/pallas_call | solution.py:420
  25.0 0.0 collective-permute-done.4.refs_5_
  25.0 1.0 %collective-permute-done.3.refs_4_ = bf16[384,128]{1,0:T(8,128)(2,1)S(1)} collective-permute-done((bf16[384,128]{1,0:T(8,128)(2,1)}, bf16[384,128]{1,0:T(8,128)(2,1)S(1)}, u32[]{:S(2)}, u32[]{:S(2)}) %collective-permute-start.3) | collective-permute-done | bytes 98336 | tf_op jit(solution)/shard_map/ppermute | solution.py:435
  26.0 0.0 collective-permute-done.2.refs_3_
  26.0 0.9 %collective-permute-done.1.refs_2_ = bf16[384,128]{1,0:T(8,128)(2,1)S(1)} collective-permute-done((bf16[384,128]{1,0:T(8,128)(2,1)}, bf16[384,128]{1,0:T(8,128)(2,1)S(1)}, u32[]{:S(2)}, u32[]{:S(2)}) %collective-permute-start.1) | collective-permute-done | bytes 98336 | tf_op jit(solution)/shard_map/ppermute | solution.py:435
  26.9 0.0 collective-permute-done.refs_1_
  26.9 0.0 copy-start.3
  26.9 0.9 copy-done.3
  27.8 0.0 copy-start.7
  27.8 0.7 copy-done.7
  28.5 0.0 copy-start.6
  28.5 2.0 %shard_map.89.block_hbm.b0_hbm = bf16[2,128,512]{2,1,0:T(8,128)(2,1)S(1)} custom-call(bf16[384,128]{1,0:T(8,128)(2,1)S(1)} %copy-done.3, bf16[384,128]{1,0:T(8,128)(2,1)S(1)} %collective-permute-done.refs_1_, bf16[384,128]{1,0:T(8,128)(2,1)S(1)} %collective-permute-done.1.refs_2_, bf16[384,128]{1,0:T(8,128)(2,1)S(1)} %collective-permute-done.2.refs_3_, ...), custom_call_target="tpu_custom_call" | custom-call | bytes 1052672 | tf_op jit(solution)/shard_map/pallas_call | solution.py:420
  30.5 0.0 copy-start.4
  30.5 1.6 %collective-permute-start.8 = (bf16[2,128,512]{2,1,0:T(8,128)(2,1)S(1)}, bf16[2,128,512]{2,1,0:T(8,128)(2,1)S(1)}, u32[]{:S(2)}, u32[]{:S(2)}) collective-permute-start(bf16[2,128,512]{2,1,0:T(8,128)(2,1)S(1)} %shard_map.89.block_hbm.b0_hbm), channel_id=1, source_target_pairs={{0,16},{8,24},{16,0},{24,8},{1,17},{9,25},{17,1},{25,9},{2,18},{10... | collective-permute-start | bytes 786440 | tf_op jit(solution)/shard_map/ppermute | solution.py:435
  32.0 0.0 collective-permute-start.7
  32.0 0.0 copy-done.4
  32.0 3.6 %shard_map.90 = bf16[32,32,256]{2,1,0:T(8,128)(2,1)} custom-call(bf16[2,128,512]{2,1,0:T(8,128)(2,1)} %copy-done.4, bf16[1024,128]{1,0:T(8,128)(2,1)} %feats_hbm.3, bf16[2,256,1024]{2,1,0:T(8,128)(2,1)} %get-tuple-element.34.coef_hbm, f32[2,256,512]{2,1,0:T(8,128)} %get-tuple-element.35.offset_hbm), custom_call_target="tpu_custom_call" | custom-call | flops 1073741824 | bytes 3145728 | tf_op jit(solution)/shard_map/pallas_call | solution.py:420
  35.6 3.0 %shard_map.91 = (s32[4,512]{1,0:T(4,128)}, s32[8,128]{1,0:T(8,128)}, s32[8,512]{1,0:T(8,128)}) custom-call(s32[2,2048]{1,0:T(2,128)} %blocks_hbm.6, s32[2,512]{1,0:T(2,128)} %pivots_hbm.3), custom_call_target="tpu_custom_call" | custom-call | bytes 49152 | tf_op jit(solution)/shard_map/pallas_call | solution.py:420
  38.6 0.0 collective-permute-done.8.b2_hbm
  38.6 0.0 copy-start.9
  38.6 0.0 collective-permute-done.7.b1_hbm
  38.6 0.0 copy-start.10
  38.6 3.4 %all-to-all-start = ((bf16[32,32,256]{2,1,0:T(8,128)(2,1)}), bf16[32,32,256]{2,1,0:T(8,128)(2,1)S(1)}, u32[]{:S(2)}, u32[]{:S(2)}) async-start(bf16[32,32,256]{2,1,0:T(8,128)(2,1)} %shard_map.90), calls=%async_computation | async-start | bytes 1048576 | tf_op jit(solution)/shard_map/all_to_all | solution.py:525
  42.0 0.1 collective-permute-start.9
  42.2 1.5 %collective-permute-done.9.b3_hbm = bf16[2,128,512]{2,1,0:T(8,128)(2,1)S(1)} collective-permute-done((bf16[2,128,512]{2,1,0:T(8,128)(2,1)S(1)}, bf16[2,128,512]{2,1,0:T(8,128)(2,1)S(1)}, u32[]{:S(2)}, u32[]{:S(2)}) %collective-permute-start.9) | collective-permute-done | bytes 262176 | tf_op jit(solution)/shard_map/ppermute | solution.py:435
  43.6 0.0 copy-start.11
  43.6 0.0 copy-done.9
  43.6 0.0 copy-done.10
  43.7 0.7 copy-done.11
  44.3 10.1 %shard_map.92 = (bf16[2,512,2048]{2,1,0:T(8,128)(2,1)}, bf16[4,2048,512]{2,1,0:T(8,128)(2,1)}) custom-call(bf16[2,128,512]{2,1,0:T(8,128)(2,1)} %copy-done.4, bf16[2,128,512]{2,1,0:T(8,128)(2,1)} %copy-done.10, bf16[2,128,512]{2,1,0:T(8,128)(2,1)} %copy-done.9, bf16[2,128,512]{2,1,0:T(8,128)(2,1)} %copy-done.11, s32[4,512]{1,0:T(4,128)} %get-tuple-element.42.ids0_hbm, ...), custom_call_target="tpu_custom_call" | custom-call | flops 1610612736 | bytes 13680640 | tf_op jit(solution)/shard_map/pallas_call | solution.py:420
  54.5 0.0 copy-start
  54.5 3.7 %all-to-all-done.summed = bf16[32,32,256]{2,1,0:T(8,128)(2,1)S(1)} async-done(((bf16[32,32,256]{2,1,0:T(8,128)(2,1)}), bf16[32,32,256]{2,1,0:T(8,128)(2,1)S(1)}, u32[]{:S(2)}, u32[]{:S(2)}) %all-to-all-start) | async-done | bytes 524320 | tf_op jit(solution)/shard_map/all_to_all | solution.py:525
  58.2 0.0 copy-done.6
  58.2 0.0 copy-start.2
  58.2 1.2 %copy-done.2 = bf16[2,512,512]{2,1,0:T(8,128)(2,1)S(1)} copy-done((bf16[2,512,512]{2,1,0:T(8,128)(2,1)S(1)}, bf16[2,512,512]{2,1,0:T(8,128)(2,1)}, u32[]{:S(2)}) %copy-start.2) | copy-done | bytes 1048600
  59.4 0.0 copy-start.8
  59.4 0.7 copy-done.8
  60.1 6.8 %shard_map.93 = bf16[8,32,384]{2,1,0:T(8,128)(2,1)} custom-call(bf16[32,32,256]{2,1,0:T(8,128)(2,1)S(1)} %all-to-all-done.summed, bf16[2,512,2048]{2,1,0:T(8,128)(2,1)} %get-tuple-element.46.factor_hbm, bf16[2,512,512]{2,1,0:T(8,128)(2,1)S(1)} %copy-done.2, bf16[4,2048,512]{2,1,0:T(8,128)(2,1)} %get-tuple-element.47.cross_hbm, s32[8,128]{1,0:T(8,128)S(1)} %copy-done.6, ...), custom_call_target="tpu_custom_call" | custom-call | bytes 14360576 | tf_op jit(solution)/shard_map/pallas_call | solution.py:420
  66.9 3.6 %all-to-all-start.1 = ((bf16[8,32,384]{2,1,0:T(8,128)(2,1)}), bf16[8,32,384]{2,1,0:T(8,128)(2,1)S(1)}, u32[]{:S(2)}, u32[]{:S(2)}) async-start(bf16[8,32,384]{2,1,0:T(8,128)(2,1)} %shard_map.93), calls=%async_computation.1 | async-start | bytes 393216 | tf_op jit(solution)/shard_map/all_to_all | solution.py:572
  70.5 4.1 %shard_map.94.slots_hbm = s32[2,768]{1,0:T(2,128)} custom-call(s32[2,2048]{1,0:T(2,128)} %blocks_hbm.6), custom_call_target="tpu_custom_call" | custom-call | bytes 22528 | tf_op jit(solution)/shard_map/pallas_call | solution.py:420
  74.6 3.7 %all-to-all-done.1.g0_hbm = bf16[8,32,384]{2,1,0:T(8,128)(2,1)S(1)} async-done(((bf16[8,32,384]{2,1,0:T(8,128)(2,1)}), bf16[8,32,384]{2,1,0:T(8,128)(2,1)S(1)}, u32[]{:S(2)}, u32[]{:S(2)}) %all-to-all-start.1) | async-done | bytes 196640 | tf_op jit(solution)/shard_map/all_to_all | solution.py:572
  78.3 1.2 %collective-permute-start.11 = (bf16[8,32,384]{2,1,0:T(8,128)(2,1)S(1)}, bf16[8,32,384]{2,1,0:T(8,128)(2,1)S(1)}, u32[]{:S(2)}, u32[]{:S(2)}) collective-permute-start(bf16[8,32,384]{2,1,0:T(8,128)(2,1)S(1)} %all-to-all-done.1.g0_hbm), channel_id=1, source_target_pairs={{0,16},{8,24},{16,0},{24,8},{1,17},{9,25},{17,1},{25,9},{2,18},{10... | collective-permute-start | bytes 589832 | tf_op jit(solution)/shard_map/ppermute | solution.py:435
  79.5 0.0 collective-permute-start.10
  79.5 4.5 %collective-permute-done.11.g2_hbm = bf16[8,32,384]{2,1,0:T(8,128)(2,1)S(1)} collective-permute-done((bf16[8,32,384]{2,1,0:T(8,128)(2,1)S(1)}, bf16[8,32,384]{2,1,0:T(8,128)(2,1)S(1)}, u32[]{:S(2)}, u32[]{:S(2)}) %collective-permute-start.11) | collective-permute-done | bytes 196640 | tf_op jit(solution)/shard_map/ppermute | solution.py:435
  84.0 0.0 collective-permute-start.12
  84.0 0.0 collective-permute-done.10.g1_hbm
  84.0 1.4 %collective-permute-done.12.g3_hbm = bf16[8,32,384]{2,1,0:T(8,128)(2,1)S(1)} collective-permute-done((bf16[8,32,384]{2,1,0:T(8,128)(2,1)S(1)}, bf16[8,32,384]{2,1,0:T(8,128)(2,1)S(1)}, u32[]{:S(2)}, u32[]{:S(2)}) %collective-permute-start.12) | collective-permute-done | bytes 196640 | tf_op jit(solution)/shard_map/ppermute | solution.py:435
  85.4 0.0 copy-done
  85.5 0.0 copy-start.1
  85.5 1.2 %copy-done.1 = f32[1024,256]{1,0:T(8,128)S(1)} copy-done((f32[1024,256]{1,0:T(8,128)S(1)}, f32[1024,256]{1,0:T(8,128)}, u32[]{:S(2)}) %copy-start.1) | copy-done | bytes 1048600
  86.7 0.0 copy-start.5
  86.7 0.7 copy-done.5
  87.4 4.0 %shard_map.95 = (f32[1024,256]{1,0:T(8,128)}, f32[1024,256]{1,0:T(8,128)}) custom-call(bf16[8,32,384]{2,1,0:T(8,128)(2,1)S(1)} %all-to-all-done.1.g0_hbm, bf16[8,32,384]{2,1,0:T(8,128)(2,1)S(1)} %collective-permute-done.10.g1_hbm, bf16[8,32,384]{2,1,0:T(8,128)(2,1)S(1)} %collective-permute-done.11.g2_hbm, ...), custom_call_target="tpu_custom_call" | custom-call | bytes 4986880 | tf_op jit(solution)/shard_map/pallas_call | solution.py:420
Async XLA Ops:
  2.9 16.1 %collective-permute-start.6 = (bf16[384,128]{1,0:T(8,128)(2,1)}, bf16[384,128]{1,0:T(8,128)(2,1)S(1)}, u32[]{:S(2)}, u32[]{:S(2)}) collective-permute-start(bf16[384,128]{1,0:T(8,128)(2,1)} %shard_map.86.refs_0_), channel_id=1, source_target_pairs={{0,7},{1,6},{2,5},{3,4},{4,3},{5,2},{6,1},{7,0},{8,15},{9,14},{10,... | collective-permute-start | bytes 294920 | tf_op jit(solution)/shard_map/ppermute | solution.py:435
  9.0 12.1 %collective-permute-start.5 = (bf16[384,128]{1,0:T(8,128)(2,1)}, bf16[384,128]{1,0:T(8,128)(2,1)S(1)}, u32[]{:S(2)}, u32[]{:S(2)}) collective-permute-start(bf16[384,128]{1,0:T(8,128)(2,1)} %shard_map.86.refs_0_), channel_id=1, source_target_pairs={{0,6},{1,7},{2,4},{3,5},{4,2},{5,3},{6,0},{7,1},{8,14},{9,15},{10,... | collective-permute-start | bytes 294920 | tf_op jit(solution)/shard_map/ppermute | solution.py:435
  9.2 15.8 %collective-permute-start.4 = (bf16[384,128]{1,0:T(8,128)(2,1)}, bf16[384,128]{1,0:T(8,128)(2,1)S(1)}, u32[]{:S(2)}, u32[]{:S(2)}) collective-permute-start(bf16[384,128]{1,0:T(8,128)(2,1)} %shard_map.86.refs_0_), channel_id=1, source_target_pairs={{0,5},{1,4},{2,7},{3,6},{4,1},{5,0},{6,3},{7,2},{8,13},{9,12},{10,... | collective-permute-start | bytes 294920 | tf_op jit(solution)/shard_map/ppermute | solution.py:435
  9.9 16.0 %collective-permute-start.3 = (bf16[384,128]{1,0:T(8,128)(2,1)}, bf16[384,128]{1,0:T(8,128)(2,1)S(1)}, u32[]{:S(2)}, u32[]{:S(2)}) collective-permute-start(bf16[384,128]{1,0:T(8,128)(2,1)} %shard_map.86.refs_0_), channel_id=1, source_target_pairs={{0,4},{1,5},{2,6},{3,7},{4,0},{5,1},{6,2},{7,3},{8,12},{9,13},{10,... | collective-permute-start | bytes 294920 | tf_op jit(solution)/shard_map/ppermute | solution.py:435
  12.0 14.0 %collective-permute-start.2 = (bf16[384,128]{1,0:T(8,128)(2,1)}, bf16[384,128]{1,0:T(8,128)(2,1)S(1)}, u32[]{:S(2)}, u32[]{:S(2)}) collective-permute-start(bf16[384,128]{1,0:T(8,128)(2,1)} %shard_map.86.refs_0_), channel_id=1, source_target_pairs={{0,3},{1,2},{2,1},{3,0},{4,7},{5,6},{6,5},{7,4},{8,11},{9,10},{10,... | collective-permute-start | bytes 294920 | tf_op jit(solution)/shard_map/ppermute | solution.py:435
  18.9 8.0 %collective-permute-start.1 = (bf16[384,128]{1,0:T(8,128)(2,1)}, bf16[384,128]{1,0:T(8,128)(2,1)S(1)}, u32[]{:S(2)}, u32[]{:S(2)}) collective-permute-start(bf16[384,128]{1,0:T(8,128)(2,1)} %shard_map.86.refs_0_), channel_id=1, source_target_pairs={{0,2},{1,3},{2,0},{3,1},{4,6},{5,7},{6,4},{7,5},{8,10},{9,11},{10,... | collective-permute-start | bytes 294920 | tf_op jit(solution)/shard_map/ppermute | solution.py:435
  21.1 5.8 %collective-permute-start = (bf16[384,128]{1,0:T(8,128)(2,1)}, bf16[384,128]{1,0:T(8,128)(2,1)S(1)}, u32[]{:S(2)}, u32[]{:S(2)}) collective-permute-start(bf16[384,128]{1,0:T(8,128)(2,1)} %shard_map.86.refs_0_), channel_id=1, source_target_pairs={{0,1},{1,0},{2,3},{3,2},{4,5},{5,4},{6,7},{7,6},{8,9},{9,8},{10,11... | collective-permute-start | bytes 294920 | tf_op jit(solution)/shard_map/ppermute | solution.py:435
  26.9 0.9 copy-start.3
  27.8 0.7 copy-start.7
  28.5 29.7 %copy-start.6 = (s32[8,128]{1,0:T(8,128)S(1)}, s32[8,128]{1,0:T(8,128)}, u32[]{:S(2)}) copy-start(s32[8,128]{1,0:T(8,128)} %get-tuple-element.48.starts0_hbm) | copy-start | bytes 12292
  30.5 1.6 %copy-start.4 = (bf16[2,128,512]{2,1,0:T(8,128)(2,1)}, bf16[2,128,512]{2,1,0:T(8,128)(2,1)S(1)}, u32[]{:S(2)}) copy-start(bf16[2,128,512]{2,1,0:T(8,128)(2,1)S(1)} %shard_map.89.block_hbm.b0_hbm) | copy-start | bytes 786436
  30.5 8.1 %collective-permute-start.8 = (bf16[2,128,512]{2,1,0:T(8,128)(2,1)S(1)}, bf16[2,128,512]{2,1,0:T(8,128)(2,1)S(1)}, u32[]{:S(2)}, u32[]{:S(2)}) collective-permute-start(bf16[2,128,512]{2,1,0:T(8,128)(2,1)S(1)} %shard_map.89.block_hbm.b0_hbm), channel_id=1, source_target_pairs={{0,16},{8,24},{16,0},{24,8},{1,17},{9,25},{17,1},{25,9},{2,18},{10... | collective-permute-start | bytes 786440 | tf_op jit(solution)/shard_map/ppermute | solution.py:435
  32.0 6.6 %collective-permute-start.7 = (bf16[2,128,512]{2,1,0:T(8,128)(2,1)S(1)}, bf16[2,128,512]{2,1,0:T(8,128)(2,1)S(1)}, u32[]{:S(2)}, u32[]{:S(2)}) collective-permute-start(bf16[2,128,512]{2,1,0:T(8,128)(2,1)S(1)} %shard_map.89.block_hbm.b0_hbm), channel_id=1, source_target_pairs={{0,8},{8,0},{16,24},{24,16},{1,9},{9,1},{17,25},{25,17},{2,10},{10... | collective-permute-start | bytes 786440 | tf_op jit(solution)/shard_map/ppermute | solution.py:435
  38.6 5.1 %copy-start.9 = (bf16[2,128,512]{2,1,0:T(8,128)(2,1)}, bf16[2,128,512]{2,1,0:T(8,128)(2,1)S(1)}, u32[]{:S(2)}) copy-start(bf16[2,128,512]{2,1,0:T(8,128)(2,1)S(1)} %collective-permute-done.8.b2_hbm) | copy-start | bytes 786436
  38.6 5.1 %copy-start.10 = (bf16[2,128,512]{2,1,0:T(8,128)(2,1)}, bf16[2,128,512]{2,1,0:T(8,128)(2,1)S(1)}, u32[]{:S(2)}) copy-start(bf16[2,128,512]{2,1,0:T(8,128)(2,1)S(1)} %collective-permute-done.7.b1_hbm) | copy-start | bytes 786436
  38.6 19.6 %all-to-all-start = ((bf16[32,32,256]{2,1,0:T(8,128)(2,1)}), bf16[32,32,256]{2,1,0:T(8,128)(2,1)S(1)}, u32[]{:S(2)}, u32[]{:S(2)}) async-start(bf16[32,32,256]{2,1,0:T(8,128)(2,1)} %shard_map.90), calls=%async_computation | async-start | bytes 1048576 | tf_op jit(solution)/shard_map/all_to_all | solution.py:525
  42.0 1.6 %collective-permute-start.9 = (bf16[2,128,512]{2,1,0:T(8,128)(2,1)S(1)}, bf16[2,128,512]{2,1,0:T(8,128)(2,1)S(1)}, u32[]{:S(2)}, u32[]{:S(2)}) collective-permute-start(bf16[2,128,512]{2,1,0:T(8,128)(2,1)S(1)} %collective-permute-done.8.b2_hbm), channel_id=1, source_target_pairs={{0,8},{8,0},{16,24},{24,16},{1,9},{9,1},{17,25},{25,17},{2,10},{10... | collective-permute-start | bytes 786440 | tf_op jit(solution)/shard_map/ppermute | solution.py:435
  43.6 0.7 copy-start.11
  54.5 31.0 %copy-start = (f32[1024,256]{1,0:T(8,128)S(1)}, f32[1024,256]{1,0:T(8,128)}, u32[]{:S(2)}) copy-start(f32[1024,256]{1,0:T(8,128)} %w_hbm.3) | copy-start | bytes 3145732
  58.2 1.2 %copy-start.2 = (bf16[2,512,512]{2,1,0:T(8,128)(2,1)S(1)}, bf16[2,512,512]{2,1,0:T(8,128)(2,1)}, u32[]{:S(2)}) copy-start(bf16[2,512,512]{2,1,0:T(8,128)(2,1)} %core_hbm.1) | copy-start | bytes 3145732
  59.4 0.7 copy-start.8
  66.9 11.4 %all-to-all-start.1 = ((bf16[8,32,384]{2,1,0:T(8,128)(2,1)}), bf16[8,32,384]{2,1,0:T(8,128)(2,1)S(1)}, u32[]{:S(2)}, u32[]{:S(2)}) async-start(bf16[8,32,384]{2,1,0:T(8,128)(2,1)} %shard_map.93), calls=%async_computation.1 | async-start | bytes 393216 | tf_op jit(solution)/shard_map/all_to_all | solution.py:572
  78.3 5.7 %collective-permute-start.11 = (bf16[8,32,384]{2,1,0:T(8,128)(2,1)S(1)}, bf16[8,32,384]{2,1,0:T(8,128)(2,1)S(1)}, u32[]{:S(2)}, u32[]{:S(2)}) collective-permute-start(bf16[8,32,384]{2,1,0:T(8,128)(2,1)S(1)} %all-to-all-done.1.g0_hbm), channel_id=1, source_target_pairs={{0,16},{8,24},{16,0},{24,8},{1,17},{9,25},{17,1},{25,9},{2,18},{10... | collective-permute-start | bytes 589832 | tf_op jit(solution)/shard_map/ppermute | solution.py:435
  79.5 4.5 %collective-permute-start.10 = (bf16[8,32,384]{2,1,0:T(8,128)(2,1)S(1)}, bf16[8,32,384]{2,1,0:T(8,128)(2,1)S(1)}, u32[]{:S(2)}, u32[]{:S(2)}) collective-permute-start(bf16[8,32,384]{2,1,0:T(8,128)(2,1)S(1)} %all-to-all-done.1.g0_hbm), channel_id=1, source_target_pairs={{0,8},{8,0},{16,24},{24,16},{1,9},{9,1},{17,25},{25,17},{2,10},{10... | collective-permute-start | bytes 589832 | tf_op jit(solution)/shard_map/ppermute | solution.py:435
  84.0 1.4 %collective-permute-start.12 = (bf16[8,32,384]{2,1,0:T(8,128)(2,1)S(1)}, bf16[8,32,384]{2,1,0:T(8,128)(2,1)S(1)}, u32[]{:S(2)}, u32[]{:S(2)}) collective-permute-start(bf16[8,32,384]{2,1,0:T(8,128)(2,1)S(1)} %collective-permute-done.11.g2_hbm), channel_id=1, source_target_pairs={{0,8},{8,0},{16,24},{24,16},{1,9},{9,1},{17,25},{25,17},{2,10},{10... | collective-permute-start | bytes 589832 | tf_op jit(solution)/shard_map/ppermute | solution.py:435
  85.5 1.2 %copy-start.1 = (f32[1024,256]{1,0:T(8,128)S(1)}, f32[1024,256]{1,0:T(8,128)}, u32[]{:S(2)}) copy-start(f32[1024,256]{1,0:T(8,128)} %z_hbm.3) | copy-start | bytes 3145732
  86.7 0.7 copy-start.5

commit v15 on v14

--- a/solution.py
+++ b/solution.py
@@ -318,18 +318,20 @@
 
 def chain_kernel(
     cap, owners,
-    summed, factor_hbm, core_hbm, cross_hbm, starts0_hbm, starts1_hbm, out_hbm,
-    factor, core, cross, starts0, starts1, packed, sems,
+    summed_hbm, factor_hbm, core_hbm, cross_hbm, starts0_hbm, starts1_hbm, out_hbm,
+    summed, factor, core, cross, starts0, starts1, packed, sems,
 ):
     groups, _, count = cross.shape
     own = summed.shape[1] // (2 * UPDATES)
-    pairs, starts = [], (starts0, starts1)
+    pairs, starts = [(summed_hbm, summed)], (starts0, starts1)
     for u in range(UPDATES):
         pairs += [(factor_hbm.at[u], factor.at[u]), (core_hbm.at[u], core.at[u])]
         if u == 0:
             pairs += [(starts0_hbm, starts0), (starts1_hbm, starts1)]
             pairs += [(cross_hbm.at[g], cross.at[g]) for g in range(groups)]
     reads = start_all(pairs, sems)
+    first, *reads = reads
+    first.wait()
     step = None
     for u in range(UPDATES):
         sums = []
@@ -457,7 +459,7 @@
         features,
         sems=(2,),
     )
-    came = {k: swap(packed, "pts", k) for k in reversed(range(3, owners))}
+    came = {k: swap(packed, "pts", k) for k in (1, 2, *reversed(range(3, owners)))}
     kept = [
         like((UPDATES, outputs, points)),
         like((UPDATES, outputs, count), f32),
@@ -471,8 +473,7 @@
         *given,
         sems=(4, 1 + 2 * UPDATES),
     )
-    again, row_starts, later_index = lax.optimization_barrier((packed, row_starts, block_index))
-    came.update({k: swap(again, "pts", k) for k in (2, 1)})
+    row_starts, later_index = lax.optimization_barrier((row_starts, block_index))
 
     def ordered(u, indices):
         kept = [like((rows, count), i32), like((8, 128), i32), like((8, rank), i32)]
@@ -502,7 +503,7 @@
         *[came[k] for k in range(1, owners)],
         row_starts,
         sems=(owners + 1,),
-        grant=48,
+        grant=60,
     )
     beside, across = swap(mine, "rows", 1), swap(mine, "rows", 2)
     pieces = like((devices, deep, count // 2))
@@ -543,23 +544,22 @@
         chosen,
         later_chosen,
         sems=(rows * rows + 2,),
-        grant=57,
+        grant=60,
         flops=2.0 * width * block * (UPDATES * rank + block),
     )
     pieces = like((owners, deep, half * cap))
     (steps,) = call(
         functools.partial(chain_kernel, cap, owners),
         [pieces],
-        [factor, core, cross, inside_starts, inside_starts, pieces],
+        [summed, factor, core, cross, inside_starts, inside_starts, pieces],
         summed,
         factor,
         core,
         cross,
         starts,
         later_starts,
-        near=1,
-        sems=(2 * UPDATES + 2 + rows,),
-        grant=52,
+        sems=(2 * UPDATES + 3 + rows,),
+        grant=60,
     )
     steps, later_index = lax.optimization_barrier((steps, block_index))
     (slots,) = call(
@@ -593,7 +593,7 @@
         coefficients,
         momentum,
         sems=(1 + rows + 2 * parts, 2 * parts),
-        grant=48,
+        grant=60,
     )
 
 

time: 92.5 us -> 94.4 us (1.021)
  starting transfers between devices: 24.4 us -> 30.1 us
  local copies, waits for them, and re-layouts: 6.1 us -> 3.46 us
  waiting for transfers between devices: 16.8 us -> 14.9 us
    ppermute x13, starting transfers between devices: 17.3 us -> 22 us  [swap(): lax.ppermute(value, axis, [(i, i ^ k) for i in range(lax.axis_size(axis))])]
    unnamed x24 -> x30, local copies, waits for them, and re-layouts: 6.1 us -> 3.46 us
    ppermute x13, waiting for transfers between devices: 9.34 us -> 7.39 us  [swap(): lax.ppermute(value, axis, [(i, i ^ k) for i in range(lax.axis_size(axis))])]
    all_to_all x1, starting transfers between devices: 3.43 us -> 4.5 us  [with_kernels(): summed = lax.all_to_all(pieces, ('rows', 'pts'), 0, 0, tiled=True)]
  transfers between devices with their start and end apart: 15 -> 15, of which waited for: 7 -> 5; matrix products, arithmetic and copies ran while one was open for 0% -> 0% of each run, Pallas kernels for 31% -> 30%
where the time goes in v15:
time: 94.4 us; the launch traced here: 93.5 us
  Pallas kernels  44 us (47%)
  starting transfers between devices  30.1 us (32%)
  waiting for transfers between devices  14.9 us (16%)
  local copies, waits for them, and re-layouts  3.46 us (4%)
  between operations  1.06 us (1%)
    pallas_call x10, Pallas kernels, call(): pl.pallas_call(body, out_shape=outs, in_specs=[VMEM] * near + [HBM] * (le...  44 us
    ppermute x13, starting transfers between devices, swap(): lax.ppermute(value, axis, [(i, i ^ k) for i in range(lax.axis_size(axis))])  22 us
    ppermute x13, waiting for transfers between devices, swap(): lax.ppermute(value, axis, [(i, i ^ k) for i in range(lax.axis_size(axis))])  7.39 us
    all_to_all x1, starting transfers between devices, with_kernels(): summed = lax.all_to_all(pieces, ('rows', 'pts'), 0, 0, tiled=True)  4.5 us
    all_to_all x1, waiting for transfers between devices, with_kernels(): summed = lax.all_to_all(pieces, ('rows', 'pts'), 0, 0, tiled=True)  3.74 us
    all_to_all x1, waiting for transfers between devices, with_kernels(): got = lax.all_to_all(steps, 'pts', 0, 0, tiled=True)  3.72 us
    all_to_all x1, starting transfers between devices, with_kernels(): got = lax.all_to_all(steps, 'pts', 0, 0, tiled=True)  3.62 us
    unnamed x30, local copies, waits for them, and re-layouts  3.46 us
  transfers between devices with their start and end apart: 15, of which 5 were waited for; matrix products, arithmetic and copies ran while one was open for 0% of the time, Pallas kernels for 30%

profile of v15, /device:TPU:0, one launch (start us, length us, event | category | flops | bytes accessed | tf_op | source)
XLA Modules:
  0.0 93.5 jit_solution(17122501253312659916)
XLA Ops:
  0.6 2.2 %shard_map.86.refs_0_ = bf16[384,128]{1,0:T(8,128)(2,1)} custom-call(s32[2,2048]{1,0:T(2,128)} %blocks_hbm.6, bf16[1024,128]{1,0:T(8,128)(2,1)} %feats_hbm.3), custom_call_target="tpu_custom_call" | custom-call | bytes 376832 | tf_op jit(solution)/shard_map/pallas_call | solution.py:422
  2.9 6.1 %collective-permute-start.6 = (bf16[384,128]{1,0:T(8,128)(2,1)}, bf16[384,128]{1,0:T(8,128)(2,1)S(1)}, u32[]{:S(2)}, u32[]{:S(2)}) collective-permute-start(bf16[384,128]{1,0:T(8,128)(2,1)} %shard_map.86.refs_0_), channel_id=1, source_target_pairs={{0,7},{1,6},{2,5},{3,4},{4,3},{5,2},{6,1},{7,0},{8,15},{9,14},{10,... | collective-permute-start | bytes 294920 | tf_op jit(solution)/shard_map/ppermute | solution.py:437
  9.0 0.2 collective-permute-start.5
  9.2 0.7 collective-permute-start.4
  9.9 2.0 %collective-permute-start.3 = (bf16[384,128]{1,0:T(8,128)(2,1)}, bf16[384,128]{1,0:T(8,128)(2,1)S(1)}, u32[]{:S(2)}, u32[]{:S(2)}) collective-permute-start(bf16[384,128]{1,0:T(8,128)(2,1)} %shard_map.86.refs_0_), channel_id=1, source_target_pairs={{0,4},{1,5},{2,6},{3,7},{4,0},{5,1},{6,2},{7,3},{8,12},{9,13},{10,... | collective-permute-start | bytes 294920 | tf_op jit(solution)/shard_map/ppermute | solution.py:437
  12.0 2.3 %collective-permute-start.2 = (bf16[384,128]{1,0:T(8,128)(2,1)}, bf16[384,128]{1,0:T(8,128)(2,1)S(1)}, u32[]{:S(2)}, u32[]{:S(2)}) collective-permute-start(bf16[384,128]{1,0:T(8,128)(2,1)} %shard_map.86.refs_0_), channel_id=1, source_target_pairs={{0,3},{1,2},{2,1},{3,0},{4,7},{5,6},{6,5},{7,4},{8,11},{9,10},{10,... | collective-permute-start | bytes 294920 | tf_op jit(solution)/shard_map/ppermute | solution.py:437
  14.2 0.0 collective-permute-done.6.refs_7_
  14.2 0.0 copy-start.5
  14.2 6.8 %collective-permute-start.1 = (bf16[384,128]{1,0:T(8,128)(2,1)}, bf16[384,128]{1,0:T(8,128)(2,1)S(1)}, u32[]{:S(2)}, u32[]{:S(2)}) collective-permute-start(bf16[384,128]{1,0:T(8,128)(2,1)} %shard_map.86.refs_0_), channel_id=1, source_target_pairs={{0,2},{1,3},{2,0},{3,1},{4,6},{5,7},{6,4},{7,5},{8,10},{9,11},{10,... | collective-permute-start | bytes 294920 | tf_op jit(solution)/shard_map/ppermute | solution.py:437
  21.0 0.0 collective-permute-done.5.refs_6_
  21.0 1.0 %collective-permute-start = (bf16[384,128]{1,0:T(8,128)(2,1)}, bf16[384,128]{1,0:T(8,128)(2,1)S(1)}, u32[]{:S(2)}, u32[]{:S(2)}) collective-permute-start(bf16[384,128]{1,0:T(8,128)(2,1)} %shard_map.86.refs_0_), channel_id=1, source_target_pairs={{0,1},{1,0},{2,3},{3,2},{4,5},{5,4},{6,7},{7,6},{8,9},{9,8},{10,11... | collective-permute-start | bytes 294920 | tf_op jit(solution)/shard_map/ppermute | solution.py:437
  22.0 4.7 %shard_map.87 = (bf16[2,256,1024]{2,1,0:T(8,128)(2,1)}, f32[2,256,512]{2,1,0:T(8,128)}, s32[8,128]{1,0:T(8,128)}) custom-call(s32[2,2048]{1,0:T(2,128)} %blocks_hbm.6, f32[1024,256]{1,0:T(8,128)} %w_hbm.3, f32[1024,256]{1,0:T(8,128)} %z_hbm.3, bf16[1024,256]{1,0:T(8,128)(2,1)} %t_hbm.1), custom_call_target="tpu_custom_call" | custom-call | bytes 4739072 | tf_op jit(solution)/shard_map/pallas_call | solution.py:422
  26.7 2.9 %shard_map.88 = (s32[4,512]{1,0:T(4,128)}, s32[8,128]{1,0:T(8,128)}, s32[8,512]{1,0:T(8,128)}) custom-call(s32[2,2048]{1,0:T(2,128)} %blocks_hbm.6, s32[2,512]{1,0:T(2,128)} %pivots_hbm.3), custom_call_target="tpu_custom_call" | custom-call | bytes 49152 | tf_op jit(solution)/shard_map/pallas_call | solution.py:422
  29.6 0.0 collective-permute-done.4.refs_5_
  29.7 0.0 copy-start.7
  29.7 0.0 collective-permute-done.3.refs_4_
  29.7 0.0 copy-start.8
  29.7 0.0 collective-permute-done.2.refs_3_
  29.7 0.0 copy-start.9
  29.7 0.0 collective-permute-done.1.refs_2_
  29.7 0.0 copy-start.10
  29.7 0.0 collective-permute-done.refs_1_
  29.7 0.0 copy-done.5
  29.8 0.0 copy-done.6
  29.8 0.5 copy-done.7
  30.3 0.0 copy-done.8
  30.3 0.0 copy-done.9
  30.4 0.0 copy-done.10
  30.4 0.6 copy-done.11
  31.0 2.3 %shard_map.89.block_hbm.b0_hbm = bf16[2,128,512]{2,1,0:T(8,128)(2,1)} custom-call(bf16[384,128]{1,0:T(8,128)(2,1)} %shard_map.86.refs_0_, bf16[384,128]{1,0:T(8,128)(2,1)} %copy-done.11, bf16[384,128]{1,0:T(8,128)(2,1)} %copy-done.10, bf16[384,128]{1,0:T(8,128)(2,1)} %copy-done.9, bf16[384,128]{1,0:T(8,128)(2,1)} %copy-done.8, bf16[384,128]{1,0:T(8,128)(2,1)} %copy-done.7, ...), custom_call_target="tpu_custom_call" | custom-call | bytes 1052672 | tf_op jit(solution)/shard_map/pallas_call | solution.py:422
  33.3 1.6 %collective-permute-start.8 = (bf16[2,128,512]{2,1,0:T(8,128)(2,1)}, bf16[2,128,512]{2,1,0:T(8,128)(2,1)S(1)}, u32[]{:S(2)}, u32[]{:S(2)}) collective-permute-start(bf16[2,128,512]{2,1,0:T(8,128)(2,1)} %shard_map.89.block_hbm.b0_hbm), channel_id=1, source_target_pairs={{0,16},{8,24},{16,0},{24,8},{1,17},{9,25},{17,1},{25,9},{2,18},{10... | collective-permute-start | bytes 786440 | tf_op jit(solution)/shard_map/ppermute | solution.py:437
  34.9 0.0 collective-permute-start.7
  34.9 3.5 %shard_map.90 = bf16[32,32,256]{2,1,0:T(8,128)(2,1)} custom-call(bf16[2,128,512]{2,1,0:T(8,128)(2,1)} %shard_map.89.block_hbm.b0_hbm, bf16[1024,128]{1,0:T(8,128)(2,1)} %feats_hbm.3, bf16[2,256,1024]{2,1,0:T(8,128)(2,1)} %get-tuple-element.32.coef_hbm, f32[2,256,512]{2,1,0:T(8,128)} %get-tuple-element.33.offset_hbm), custom_call_target="tpu_custom_call" | custom-call | flops 1073741824 | bytes 3145728 | tf_op jit(solution)/shard_map/pallas_call | solution.py:422
  38.4 3.0 %shard_map.91 = (s32[4,512]{1,0:T(4,128)}, s32[8,128]{1,0:T(8,128)}, s32[8,512]{1,0:T(8,128)}) custom-call(s32[2,2048]{1,0:T(2,128)} %blocks_hbm.6, s32[2,512]{1,0:T(2,128)} %pivots_hbm.3), custom_call_target="tpu_custom_call" | custom-call | bytes 49152 | tf_op jit(solution)/shard_map/pallas_call | solution.py:422
  41.4 0.0 collective-permute-done.8.b2_hbm
  41.4 0.0 copy-start.12
  41.4 0.0 collective-permute-done.7.b1_hbm
  41.4 0.0 copy-start.13
  41.4 4.5 %all-to-all-start = ((bf16[32,32,256]{2,1,0:T(8,128)(2,1)}), bf16[32,32,256]{2,1,0:T(8,128)(2,1)S(1)}, u32[]{:S(2)}, u32[]{:S(2)}) async-start(bf16[32,32,256]{2,1,0:T(8,128)(2,1)} %shard_map.90), calls=%async_computation | async-start | bytes 1048576 | tf_op jit(solution)/shard_map/all_to_all | solution.py:526
  46.0 0.1 collective-permute-start.9
  46.1 1.5 %collective-permute-done.9.b3_hbm = bf16[2,128,512]{2,1,0:T(8,128)(2,1)S(1)} collective-permute-done((bf16[2,128,512]{2,1,0:T(8,128)(2,1)S(1)}, bf16[2,128,512]{2,1,0:T(8,128)(2,1)S(1)}, u32[]{:S(2)}, u32[]{:S(2)}) %collective-permute-start.9) | collective-permute-done | bytes 262176 | tf_op jit(solution)/shard_map/ppermute | solution.py:437
  47.6 0.0 copy-done.12
  47.6 0.0 copy-done.13
  47.6 0.7 copy-done.14
  48.2 10.1 %shard_map.92 = (bf16[2,512,2048]{2,1,0:T(8,128)(2,1)}, bf16[4,2048,512]{2,1,0:T(8,128)(2,1)}) custom-call(bf16[2,128,512]{2,1,0:T(8,128)(2,1)} %shard_map.89.block_hbm.b0_hbm, bf16[2,128,512]{2,1,0:T(8,128)(2,1)} %copy-done.13, bf16[2,128,512]{2,1,0:T(8,128)(2,1)} %copy-done.12, bf16[2,128,512]{2,1,0:T(8,128)(2,1)} %copy-done.14, ...), custom_call_target="tpu_custom_call" | custom-call | flops 1610612736 | bytes 13680640 | tf_op jit(solution)/shard_map/pallas_call | solution.py:422
  58.4 3.7 %all-to-all-done.summed_hbm = bf16[32,32,256]{2,1,0:T(8,128)(2,1)S(1)} async-done(((bf16[32,32,256]{2,1,0:T(8,128)(2,1)}), bf16[32,32,256]{2,1,0:T(8,128)(2,1)S(1)}, u32[]{:S(2)}, u32[]{:S(2)}) %all-to-all-start) | async-done | bytes 524320 | tf_op jit(solution)/shard_map/all_to_all | solution.py:526
  62.1 0.8 copy-done
  62.9 7.1 %shard_map.93 = bf16[8,32,384]{2,1,0:T(8,128)(2,1)} custom-call(bf16[32,32,256]{2,1,0:T(8,128)(2,1)} %copy-done, bf16[2,512,2048]{2,1,0:T(8,128)(2,1)} %get-tuple-element.44.factor_hbm, bf16[2,512,512]{2,1,0:T(8,128)(2,1)} %core_hbm.1, bf16[4,2048,512]{2,1,0:T(8,128)(2,1)} %get-tuple-element.45.cross_hbm, s32[8,128]{1,0:T(8,128)} %get-tuple-element.46.starts0_hbm, ...), custom_call_target="tpu_custom_call" | custom-call | bytes 14360576 | tf_op jit(solution)/shard_map/pallas_call | solution.py:422
  70.0 3.6 %all-to-all-start.1 = ((bf16[8,32,384]{2,1,0:T(8,128)(2,1)}), bf16[8,32,384]{2,1,0:T(8,128)(2,1)S(1)}, u32[]{:S(2)}, u32[]{:S(2)}) async-start(bf16[8,32,384]{2,1,0:T(8,128)(2,1)} %shard_map.93), calls=%async_computation.1 | async-start | bytes 393216 | tf_op jit(solution)/shard_map/all_to_all | solution.py:572
  73.7 4.1 %shard_map.94.slots_hbm = s32[2,768]{1,0:T(2,128)} custom-call(s32[2,2048]{1,0:T(2,128)} %blocks_hbm.6), custom_call_target="tpu_custom_call" | custom-call | bytes 22528 | tf_op jit(solution)/shard_map/pallas_call | solution.py:422
  77.7 3.7 %all-to-all-done.1.g0_hbm = bf16[8,32,384]{2,1,0:T(8,128)(2,1)S(1)} async-done(((bf16[8,32,384]{2,1,0:T(8,128)(2,1)}), bf16[8,32,384]{2,1,0:T(8,128)(2,1)S(1)}, u32[]{:S(2)}, u32[]{:S(2)}) %all-to-all-start.1) | async-done | bytes 196640 | tf_op jit(solution)/shard_map/all_to_all | solution.py:572
  81.5 1.2 %collective-permute-start.11 = (bf16[8,32,384]{2,1,0:T(8,128)(2,1)S(1)}, bf16[8,32,384]{2,1,0:T(8,128)(2,1)S(1)}, u32[]{:S(2)}, u32[]{:S(2)}) collective-permute-start(bf16[8,32,384]{2,1,0:T(8,128)(2,1)S(1)} %all-to-all-done.1.g0_hbm), channel_id=1, source_target_pairs={{0,16},{8,24},{16,0},{24,8},{1,17},{9,25},{17,1},{25,9},{2,18},{10... | collective-permute-start | bytes 589832 | tf_op jit(solution)/shard_map/ppermute | solution.py:437
  82.7 0.0 collective-permute-start.10
  82.7 4.5 %collective-permute-done.11.g2_hbm = bf16[8,32,384]{2,1,0:T(8,128)(2,1)S(1)} collective-permute-done((bf16[8,32,384]{2,1,0:T(8,128)(2,1)S(1)}, bf16[8,32,384]{2,1,0:T(8,128)(2,1)S(1)}, u32[]{:S(2)}, u32[]{:S(2)}) %collective-permute-start.11) | collective-permute-done | bytes 196640 | tf_op jit(solution)/shard_map/ppermute | solution.py:437
  87.1 0.0 collective-permute-start.12
  87.1 0.0 collective-permute-done.10.g1_hbm
  87.2 0.0 copy-start.3
  87.2 1.4 %collective-permute-done.12.g3_hbm = bf16[8,32,384]{2,1,0:T(8,128)(2,1)S(1)} collective-permute-done((bf16[8,32,384]{2,1,0:T(8,128)(2,1)S(1)}, bf16[8,32,384]{2,1,0:T(8,128)(2,1)S(1)}, u32[]{:S(2)}, u32[]{:S(2)}) %collective-permute-start.12) | collective-permute-done | bytes 196640 | tf_op jit(solution)/shard_map/ppermute | solution.py:437
  88.6 0.0 copy-done.1
  88.6 0.0 copy-done.2
  88.6 0.0 copy-done.3
  88.6 0.0 copy-start.4
  88.6 0.7 copy-done.4
  89.3 4.1 %shard_map.95 = (f32[1024,256]{1,0:T(8,128)}, f32[1024,256]{1,0:T(8,128)}) custom-call(bf16[8,32,384]{2,1,0:T(8,128)(2,1)} %copy-done.1, bf16[8,32,384]{2,1,0:T(8,128)(2,1)} %copy-done.3, bf16[8,32,384]{2,1,0:T(8,128)(2,1)} %copy-done.2, bf16[8,32,384]{2,1,0:T(8,128)(2,1)} %copy-done.4, s32[2,768]{1,0:T(2,128)} %shard_map.94.slots_hbm, f32[1024,256]{1,0:T(8,128)} %w_hbm.3, ...), custom_call_target="tpu_custom_call" | custom-call | bytes 4986880 | tf_op jit(solution)/shard_map/pallas_call | solution.py:422
  (6 shorter events, 0.0 us)
Async XLA Ops:
  2.9 11.4 %collective-permute-start.6 = (bf16[384,128]{1,0:T(8,128)(2,1)}, bf16[384,128]{1,0:T(8,128)(2,1)S(1)}, u32[]{:S(2)}, u32[]{:S(2)}) collective-permute-start(bf16[384,128]{1,0:T(8,128)(2,1)} %shard_map.86.refs_0_), channel_id=1, source_target_pairs={{0,7},{1,6},{2,5},{3,4},{4,3},{5,2},{6,1},{7,0},{8,15},{9,14},{10,... | collective-permute-start | bytes 294920 | tf_op jit(solution)/shard_map/ppermute | solution.py:437
  9.0 12.1 %collective-permute-start.5 = (bf16[384,128]{1,0:T(8,128)(2,1)}, bf16[384,128]{1,0:T(8,128)(2,1)S(1)}, u32[]{:S(2)}, u32[]{:S(2)}) collective-permute-start(bf16[384,128]{1,0:T(8,128)(2,1)} %shard_map.86.refs_0_), channel_id=1, source_target_pairs={{0,6},{1,7},{2,4},{3,5},{4,2},{5,3},{6,0},{7,1},{8,14},{9,15},{10,... | collective-permute-start | bytes 294920 | tf_op jit(solution)/shard_map/ppermute | solution.py:437
  9.2 20.5 %collective-permute-start.4 = (bf16[384,128]{1,0:T(8,128)(2,1)}, bf16[384,128]{1,0:T(8,128)(2,1)S(1)}, u32[]{:S(2)}, u32[]{:S(2)}) collective-permute-start(bf16[384,128]{1,0:T(8,128)(2,1)} %shard_map.86.refs_0_), channel_id=1, source_target_pairs={{0,5},{1,4},{2,7},{3,6},{4,1},{5,0},{6,3},{7,2},{8,13},{9,12},{10,... | collective-permute-start | bytes 294920 | tf_op jit(solution)/shard_map/ppermute | solution.py:437
  9.9 19.8 %collective-permute-start.3 = (bf16[384,128]{1,0:T(8,128)(2,1)}, bf16[384,128]{1,0:T(8,128)(2,1)S(1)}, u32[]{:S(2)}, u32[]{:S(2)}) collective-permute-start(bf16[384,128]{1,0:T(8,128)(2,1)} %shard_map.86.refs_0_), channel_id=1, source_target_pairs={{0,4},{1,5},{2,6},{3,7},{4,0},{5,1},{6,2},{7,3},{8,12},{9,13},{10,... | collective-permute-start | bytes 294920 | tf_op jit(solution)/shard_map/ppermute | solution.py:437
  12.0 17.7 %collective-permute-start.2 = (bf16[384,128]{1,0:T(8,128)(2,1)}, bf16[384,128]{1,0:T(8,128)(2,1)S(1)}, u32[]{:S(2)}, u32[]{:S(2)}) collective-permute-start(bf16[384,128]{1,0:T(8,128)(2,1)} %shard_map.86.refs_0_), channel_id=1, source_target_pairs={{0,3},{1,2},{2,1},{3,0},{4,7},{5,6},{6,5},{7,4},{8,11},{9,10},{10,... | collective-permute-start | bytes 294920 | tf_op jit(solution)/shard_map/ppermute | solution.py:437
  14.2 15.5 %copy-start.5 = (bf16[384,128]{1,0:T(8,128)(2,1)}, bf16[384,128]{1,0:T(8,128)(2,1)S(1)}, u32[]{:S(2)}) copy-start(bf16[384,128]{1,0:T(8,128)(2,1)S(1)} %collective-permute-done.6.refs_7_) | copy-start | bytes 294916
  14.2 15.5 %collective-permute-start.1 = (bf16[384,128]{1,0:T(8,128)(2,1)}, bf16[384,128]{1,0:T(8,128)(2,1)S(1)}, u32[]{:S(2)}, u32[]{:S(2)}) collective-permute-start(bf16[384,128]{1,0:T(8,128)(2,1)} %shard_map.86.refs_0_), channel_id=1, source_target_pairs={{0,2},{1,3},{2,0},{3,1},{4,6},{5,7},{6,4},{7,5},{8,10},{9,11},{10,... | collective-permute-start | bytes 294920 | tf_op jit(solution)/shard_map/ppermute | solution.py:437
  21.0 8.7 %copy-start.6 = (bf16[384,128]{1,0:T(8,128)(2,1)}, bf16[384,128]{1,0:T(8,128)(2,1)S(1)}, u32[]{:S(2)}) copy-start(bf16[384,128]{1,0:T(8,128)(2,1)S(1)} %collective-permute-done.5.refs_6_) | copy-start | bytes 294916
  21.0 8.7 %collective-permute-start = (bf16[384,128]{1,0:T(8,128)(2,1)}, bf16[384,128]{1,0:T(8,128)(2,1)S(1)}, u32[]{:S(2)}, u32[]{:S(2)}) collective-permute-start(bf16[384,128]{1,0:T(8,128)(2,1)} %shard_map.86.refs_0_), channel_id=1, source_target_pairs={{0,1},{1,0},{2,3},{3,2},{4,5},{5,4},{6,7},{7,6},{8,9},{9,8},{10,11... | collective-permute-start | bytes 294920 | tf_op jit(solution)/shard_map/ppermute | solution.py:437
  29.7 0.6 copy-start.7
  29.7 0.7 copy-start.8
  29.7 0.7 copy-start.9
  29.7 0.7 copy-start.10
  30.4 0.6 copy-start.11
  33.3 8.1 %collective-permute-start.8 = (bf16[2,128,512]{2,1,0:T(8,128)(2,1)}, bf16[2,128,512]{2,1,0:T(8,128)(2,1)S(1)}, u32[]{:S(2)}, u32[]{:S(2)}) collective-permute-start(bf16[2,128,512]{2,1,0:T(8,128)(2,1)} %shard_map.89.block_hbm.b0_hbm), channel_id=1, source_target_pairs={{0,16},{8,24},{16,0},{24,8},{1,17},{9,25},{17,1},{25,9},{2,18},{10... | collective-permute-start | bytes 786440 | tf_op jit(solution)/shard_map/ppermute | solution.py:437
  34.9 6.5 %collective-permute-start.7 = (bf16[2,128,512]{2,1,0:T(8,128)(2,1)}, bf16[2,128,512]{2,1,0:T(8,128)(2,1)S(1)}, u32[]{:S(2)}, u32[]{:S(2)}) collective-permute-start(bf16[2,128,512]{2,1,0:T(8,128)(2,1)} %shard_map.89.block_hbm.b0_hbm), channel_id=1, source_target_pairs={{0,8},{8,0},{16,24},{24,16},{1,9},{9,1},{17,25},{25,17},{2,10},{10... | collective-permute-start | bytes 786440 | tf_op jit(solution)/shard_map/ppermute | solution.py:437
  41.4 6.2 %copy-start.12 = (bf16[2,128,512]{2,1,0:T(8,128)(2,1)}, bf16[2,128,512]{2,1,0:T(8,128)(2,1)S(1)}, u32[]{:S(2)}) copy-start(bf16[2,128,512]{2,1,0:T(8,128)(2,1)S(1)} %collective-permute-done.8.b2_hbm) | copy-start | bytes 786436
  41.4 6.1 %copy-start.13 = (bf16[2,128,512]{2,1,0:T(8,128)(2,1)}, bf16[2,128,512]{2,1,0:T(8,128)(2,1)S(1)}, u32[]{:S(2)}) copy-start(bf16[2,128,512]{2,1,0:T(8,128)(2,1)S(1)} %collective-permute-done.7.b1_hbm) | copy-start | bytes 786436
  41.4 20.7 %all-to-all-start = ((bf16[32,32,256]{2,1,0:T(8,128)(2,1)}), bf16[32,32,256]{2,1,0:T(8,128)(2,1)S(1)}, u32[]{:S(2)}, u32[]{:S(2)}) async-start(bf16[32,32,256]{2,1,0:T(8,128)(2,1)} %shard_map.90), calls=%async_computation | async-start | bytes 1048576 | tf_op jit(solution)/shard_map/all_to_all | solution.py:526
  46.0 1.6 %collective-permute-start.9 = (bf16[2,128,512]{2,1,0:T(8,128)(2,1)S(1)}, bf16[2,128,512]{2,1,0:T(8,128)(2,1)S(1)}, u32[]{:S(2)}, u32[]{:S(2)}) collective-permute-start(bf16[2,128,512]{2,1,0:T(8,128)(2,1)S(1)} %collective-permute-done.8.b2_hbm), channel_id=1, source_target_pairs={{0,8},{8,0},{16,24},{24,16},{1,9},{9,1},{17,25},{25,17},{2,10},{10... | collective-permute-start | bytes 786440 | tf_op jit(solution)/shard_map/ppermute | solution.py:437
  47.6 0.7 copy-start.14
  62.1 0.8 copy-start
  70.0 11.4 %all-to-all-start.1 = ((bf16[8,32,384]{2,1,0:T(8,128)(2,1)}), bf16[8,32,384]{2,1,0:T(8,128)(2,1)S(1)}, u32[]{:S(2)}, u32[]{:S(2)}) async-start(bf16[8,32,384]{2,1,0:T(8,128)(2,1)} %shard_map.93), calls=%async_computation.1 | async-start | bytes 393216 | tf_op jit(solution)/shard_map/all_to_all | solution.py:572
  81.5 7.1 %copy-start.1 = (bf16[8,32,384]{2,1,0:T(8,128)(2,1)}, bf16[8,32,384]{2,1,0:T(8,128)(2,1)S(1)}, u32[]{:S(2)}) copy-start(bf16[8,32,384]{2,1,0:T(8,128)(2,1)S(1)} %all-to-all-done.1.g0_hbm) | copy-start | bytes 589828
  81.5 5.7 %collective-permute-start.11 = (bf16[8,32,384]{2,1,0:T(8,128)(2,1)S(1)}, bf16[8,32,384]{2,1,0:T(8,128)(2,1)S(1)}, u32[]{:S(2)}, u32[]{:S(2)}) collective-permute-start(bf16[8,32,384]{2,1,0:T(8,128)(2,1)S(1)} %all-to-all-done.1.g0_hbm), channel_id=1, source_target_pairs={{0,16},{8,24},{16,0},{24,8},{1,17},{9,25},{17,1},{25,9},{2,18},{10... | collective-permute-start | bytes 589832 | tf_op jit(solution)/shard_map/ppermute | solution.py:437
  82.7 4.5 %collective-permute-start.10 = (bf16[8,32,384]{2,1,0:T(8,128)(2,1)S(1)}, bf16[8,32,384]{2,1,0:T(8,128)(2,1)S(1)}, u32[]{:S(2)}, u32[]{:S(2)}) collective-permute-start(bf16[8,32,384]{2,1,0:T(8,128)(2,1)S(1)} %all-to-all-done.1.g0_hbm), channel_id=1, source_target_pairs={{0,8},{8,0},{16,24},{24,16},{1,9},{9,1},{17,25},{25,17},{2,10},{10... | collective-permute-start | bytes 589832 | tf_op jit(solution)/shard_map/ppermute | solution.py:437
  87.1 1.4 %copy-start.2 = (bf16[8,32,384]{2,1,0:T(8,128)(2,1)}, bf16[8,32,384]{2,1,0:T(8,128)(2,1)S(1)}, u32[]{:S(2)}) copy-start(bf16[8,32,384]{2,1,0:T(8,128)(2,1)S(1)} %collective-permute-done.11.g2_hbm) | copy-start | bytes 589828
  87.1 1.4 %collective-permute-start.12 = (bf16[8,32,384]{2,1,0:T(8,128)(2,1)S(1)}, bf16[8,32,384]{2,1,0:T(8,128)(2,1)S(1)}, u32[]{:S(2)}, u32[]{:S(2)}) collective-permute-start(bf16[8,32,384]{2,1,0:T(8,128)(2,1)S(1)} %collective-permute-done.11.g2_hbm), channel_id=1, source_target_pairs={{0,8},{8,0},{16,24},{24,16},{1,9},{9,1},{17,25},{25,17},{2,10},{10... | collective-permute-start | bytes 589832 | tf_op jit(solution)/shard_map/ppermute | solution.py:437
  87.2 1.4 %copy-start.3 = (bf16[8,32,384]{2,1,0:T(8,128)(2,1)}, bf16[8,32,384]{2,1,0:T(8,128)(2,1)S(1)}, u32[]{:S(2)}) copy-start(bf16[8,32,384]{2,1,0:T(8,128)(2,1)S(1)} %collective-permute-done.10.g1_hbm) | copy-start | bytes 589828
  88.6 0.7 copy-start.4

commit v16 on v15

--- a/solution.py
+++ b/solution.py
@@ -380,7 +380,11 @@
         part = slice(c, c + CHUNK)
         pairs += [(w_hbm.at[part], w.at[part]), (z_hbm.at[part], z.at[part])]
     reads = start_all(pairs, sems)
-    wait_all(reads[:5])
+    reads[0].wait()
+    places = []
+    for u in range(UPDATES):
+        places.append(one_hot(iota((points, slots.shape[1]), 0) == slots[u : u + 1, :]))
+    wait_all(reads[1:5])
     reads = reads[5:]
     wide = got[...].astype(f32)
     for u in range(UPDATES):
@@ -388,10 +392,7 @@
             first = own * (2 * u + h)
             part = wide[:, first : first + own, :].reshape(sources * own, lanes)
             steps[u, h * lanes : (h + 1) * lanes, :] = part.T.astype(bf16)
-    changes = []
-    for u in range(UPDATES):
-        rows = one_hot(iota((points, slots.shape[1]), 0) == slots[u : u + 1, :])
-        changes.append(mm(rows, steps[u], 1, 0))
+    changes = [mm(places[u], steps[u], 1, 0) for u in range(UPDATES)]
     writes = []
     for n, c in enumerate(chunks):
         part = slice(c, c + CHUNK)
@@ -459,7 +460,9 @@
         features,
         sems=(2,),
     )
-    came = {k: swap(packed, "pts", k) for k in (1, 2, *reversed(range(3, owners)))}
+    came = {k: swap(packed, "pts", k) for k in reversed(range(2, owners, 2))}
+    came[1] = swap(packed, "pts", 1)
+    came[3] = swap(came[2], "pts", 1)
     kept = [
         like((UPDATES, outputs, points)),
         like((UPDATES, outputs, count), f32),
@@ -473,7 +476,10 @@
         *given,
         sems=(4, 1 + 2 * UPDATES),
     )
-    row_starts, later_index = lax.optimization_barrier((row_starts, block_index))
+    came[4], came[6], row_starts, later_index = lax.optimization_barrier(
+        (came[4], came[6], row_starts, block_index)
+    )
+    came[5], came[7] = swap(came[4], "pts", 1), swap(came[6], "pts", 1)
 
     def ordered(u, indices):
         kept = [like((rows, count), i32), like((8, 128), i32), like((8, rank), i32)]

time: 94.4 us -> 88.1 us (0.933)
  starting transfers between devices: 30.1 us -> 21 us
  waiting for transfers between devices: 14.9 us -> 18 us
    ppermute x13, starting transfers between devices: 22 us -> 13.8 us  [swap(): lax.ppermute(value, axis, [(i, i ^ k) for i in range(lax.axis_size(axis))])]
    ppermute x13, waiting for transfers between devices: 7.39 us -> 10.6 us  [swap(): lax.ppermute(value, axis, [(i, i ^ k) for i in range(lax.axis_size(axis))])]
    all_to_all x1, starting transfers between devices: 4.5 us -> 3.52 us  [with_kernels(): summed = lax.all_to_all(pieces, ('rows', 'pts'), 0, 0, tiled=True)]
  transfers between devices with their start and end apart: 15 -> 15, of which waited for: 5 -> 8; matrix products, arithmetic and copies ran while one was open for 0% -> 0% of each run, Pallas kernels for 30% -> 32%
where the time goes in v16:
time: 88.1 us; the launch traced here: 87.2 us
  Pallas kernels  44.3 us (50%)
  starting transfers between devices  21 us (24%)
  waiting for transfers between devices  18 us (20%)
  local copies, waits for them, and re-layouts  2.81 us (3%)
  between operations  1.04 us (1%)
    pallas_call x10, Pallas kernels, call(): pl.pallas_call(body, out_shape=outs, in_specs=[VMEM] * near + [HBM] * (le...  44.3 us
    ppermute x13, starting transfers between devices, swap(): lax.ppermute(value, axis, [(i, i ^ k) for i in range(lax.axis_size(axis))])  13.8 us
    ppermute x13, waiting for transfers between devices, swap(): lax.ppermute(value, axis, [(i, i ^ k) for i in range(lax.axis_size(axis))])  10.6 us
    all_to_all x1, waiting for transfers between devices, with_kernels(): summed = lax.all_to_all(pieces, ('rows', 'pts'), 0, 0, tiled=True)  3.73 us
    all_to_all x1, waiting for transfers between devices, with_kernels(): got = lax.all_to_all(steps, 'pts', 0, 0, tiled=True)  3.72 us
    all_to_all x1, starting transfers between devices, with_kernels(): got = lax.all_to_all(steps, 'pts', 0, 0, tiled=True)  3.62 us
    all_to_all x1, starting transfers between devices, with_kernels(): summed = lax.all_to_all(pieces, ('rows', 'pts'), 0, 0, tiled=True)  3.52 us
    unnamed x30, local copies, waits for them, and re-layouts  2.81 us
  transfers between devices with their start and end apart: 15, of which 8 were waited for; matrix products, arithmetic and copies ran while one was open for 0% of the time, Pallas kernels for 32%

profile of v16, /device:TPU:0, one launch (start us, length us, event | category | flops | bytes accessed | tf_op | source)
XLA Modules:
  0.0 87.2 jit_solution(4740744689292440399)
XLA Ops:
  0.6 2.2 %shard_map.86.refs_0_ = bf16[384,128]{1,0:T(8,128)(2,1)} custom-call(s32[2,2048]{1,0:T(2,128)} %blocks_hbm.6, bf16[1024,128]{1,0:T(8,128)(2,1)} %feats_hbm.3), custom_call_target="tpu_custom_call" | custom-call | bytes 376832 | tf_op jit(solution)/shard_map/pallas_call | solution.py:423
  2.9 5.1 %collective-permute-start.4 = (bf16[384,128]{1,0:T(8,128)(2,1)}, bf16[384,128]{1,0:T(8,128)(2,1)S(1)}, u32[]{:S(2)}, u32[]{:S(2)}) collective-permute-start(bf16[384,128]{1,0:T(8,128)(2,1)} %shard_map.86.refs_0_), channel_id=1, source_target_pairs={{0,6},{1,7},{2,4},{3,5},{4,2},{5,3},{6,0},{7,1},{8,14},{9,15},{10,... | collective-permute-start | bytes 294920 | tf_op jit(solution)/shard_map/ppermute | solution.py:438
  8.0 0.0 collective-permute-start.3
  8.0 0.6 collective-permute-start.1
  8.6 1.7 %collective-permute-start = (bf16[384,128]{1,0:T(8,128)(2,1)}, bf16[384,128]{1,0:T(8,128)(2,1)S(1)}, u32[]{:S(2)}, u32[]{:S(2)}) collective-permute-start(bf16[384,128]{1,0:T(8,128)(2,1)} %shard_map.86.refs_0_), channel_id=1, source_target_pairs={{0,1},{1,0},{2,3},{3,2},{4,5},{5,4},{6,7},{7,6},{8,9},{9,8},{10,11... | collective-permute-start | bytes 294920 | tf_op jit(solution)/shard_map/ppermute | solution.py:438
  10.3 4.7 %shard_map.87 = (bf16[2,256,1024]{2,1,0:T(8,128)(2,1)}, f32[2,256,512]{2,1,0:T(8,128)}, s32[8,128]{1,0:T(8,128)}) custom-call(s32[2,2048]{1,0:T(2,128)} %blocks_hbm.6, f32[1024,256]{1,0:T(8,128)} %w_hbm.3, f32[1024,256]{1,0:T(8,128)} %z_hbm.3, bf16[1024,256]{1,0:T(8,128)(2,1)} %t_hbm.1), custom_call_target="tpu_custom_call" | custom-call | bytes 4739072 | tf_op jit(solution)/shard_map/pallas_call | solution.py:423
  15.0 0.0 collective-permute-done.4.refs_6_
  15.0 0.0 copy-start.5
  15.0 1.5 %collective-permute-done.3.refs_4_ = bf16[384,128]{1,0:T(8,128)(2,1)S(1)} collective-permute-done((bf16[384,128]{1,0:T(8,128)(2,1)}, bf16[384,128]{1,0:T(8,128)(2,1)S(1)}, u32[]{:S(2)}, u32[]{:S(2)}) %collective-permute-start.3) | collective-permute-done | bytes 98336 | tf_op jit(solution)/shard_map/ppermute | solution.py:438
  16.5 0.0 copy-start.6
  16.5 1.5 %collective-permute-start.5 = (bf16[384,128]{1,0:T(8,128)(2,1)S(1)}, bf16[384,128]{1,0:T(8,128)(2,1)S(1)}, u32[]{:S(2)}, u32[]{:S(2)}) collective-permute-start(bf16[384,128]{1,0:T(8,128)(2,1)S(1)} %collective-permute-done.3.refs_4_), channel_id=1, source_target_pairs={{0,1},{1,0},{2,3},{3,2},{4,5},{5,4},{6,7},{7,6},{8,9},{9,8},{10,11... | collective-permute-start | bytes 294920 | tf_op jit(solution)/shard_map/ppermute | solution.py:438
  18.0 0.0 collective-permute-done.1.refs_2_
  18.0 0.0 copy-start.7
  18.0 0.5 collective-permute-start.2
  18.5 1.5 %collective-permute-start.6 = (bf16[384,128]{1,0:T(8,128)(2,1)S(1)}, bf16[384,128]{1,0:T(8,128)(2,1)S(1)}, u32[]{:S(2)}, u32[]{:S(2)}) collective-permute-start(bf16[384,128]{1,0:T(8,128)(2,1)S(1)} %collective-permute-done.4.refs_6_), channel_id=1, source_target_pairs={{0,1},{1,0},{2,3},{3,2},{4,5},{5,4},{6,7},{7,6},{8,9},{9,8},{10,11... | collective-permute-start | bytes 294920 | tf_op jit(solution)/shard_map/ppermute | solution.py:438
  20.0 2.9 %shard_map.88 = (s32[4,512]{1,0:T(4,128)}, s32[8,128]{1,0:T(8,128)}, s32[8,512]{1,0:T(8,128)}) custom-call(s32[2,2048]{1,0:T(2,128)} %blocks_hbm.6, s32[2,512]{1,0:T(2,128)} %pivots_hbm.3), custom_call_target="tpu_custom_call" | custom-call | bytes 49152 | tf_op jit(solution)/shard_map/pallas_call | solution.py:423
  23.0 0.0 collective-permute-done.refs_1_
  23.0 0.0 copy-start.8
  23.0 0.7 collective-permute-done.2.refs_3_
  23.7 0.0 collective-permute-done.5.refs_5_
  23.7 1.0 %collective-permute-done.6.refs_7_ = bf16[384,128]{1,0:T(8,128)(2,1)S(1)} collective-permute-done((bf16[384,128]{1,0:T(8,128)(2,1)S(1)}, bf16[384,128]{1,0:T(8,128)(2,1)S(1)}, u32[]{:S(2)}, u32[]{:S(2)}) %collective-permute-start.6) | collective-permute-done | bytes 98336 | tf_op jit(solution)/shard_map/ppermute | solution.py:438
  24.8 0.0 copy-done.5
  24.8 0.0 copy-done.6
  24.8 0.0 copy-done.7
  24.8 0.0 copy-done.8
  24.8 0.0 copy-done.10
  24.8 0.0 copy-done.9
  24.8 0.0 copy-start.11
  24.8 0.6 copy-done.11
  25.4 2.3 %shard_map.89.block_hbm.b0_hbm = bf16[2,128,512]{2,1,0:T(8,128)(2,1)} custom-call(bf16[384,128]{1,0:T(8,128)(2,1)} %shard_map.86.refs_0_, bf16[384,128]{1,0:T(8,128)(2,1)} %copy-done.8, bf16[384,128]{1,0:T(8,128)(2,1)} %copy-done.7, bf16[384,128]{1,0:T(8,128)(2,1)} %copy-done.10, bf16[384,128]{1,0:T(8,128)(2,1)} %copy-done.6, bf16[384,128]{1,0:T(8,128)(2,1)} %copy-done.9, ...), custom_call_target="tpu_custom_call" | custom-call | bytes 1052672 | tf_op jit(solution)/shard_map/pallas_call | solution.py:423
  27.7 1.5 %collective-permute-start.8 = (bf16[2,128,512]{2,1,0:T(8,128)(2,1)}, bf16[2,128,512]{2,1,0:T(8,128)(2,1)S(1)}, u32[]{:S(2)}, u32[]{:S(2)}) collective-permute-start(bf16[2,128,512]{2,1,0:T(8,128)(2,1)} %shard_map.89.block_hbm.b0_hbm), channel_id=1, source_target_pairs={{0,16},{8,24},{16,0},{24,8},{1,17},{9,25},{17,1},{25,9},{2,18},{10... | collective-permute-start | bytes 786440 | tf_op jit(solution)/shard_map/ppermute | solution.py:438
  29.2 0.0 collective-permute-start.7
  29.2 3.5 %shard_map.90 = bf16[32,32,256]{2,1,0:T(8,128)(2,1)} custom-call(bf16[2,128,512]{2,1,0:T(8,128)(2,1)} %shard_map.89.block_hbm.b0_hbm, bf16[1024,128]{1,0:T(8,128)(2,1)} %feats_hbm.3, bf16[2,256,1024]{2,1,0:T(8,128)(2,1)} %get-tuple-element.36.coef_hbm, f32[2,256,512]{2,1,0:T(8,128)} %get-tuple-element.37.offset_hbm), custom_call_target="tpu_custom_call" | custom-call | flops 1073741824 | bytes 3145728 | tf_op jit(solution)/shard_map/pallas_call | solution.py:423
  32.8 3.0 %shard_map.91 = (s32[4,512]{1,0:T(4,128)}, s32[8,128]{1,0:T(8,128)}, s32[8,512]{1,0:T(8,128)}) custom-call(s32[2,2048]{1,0:T(2,128)} %blocks_hbm.6, s32[2,512]{1,0:T(2,128)} %pivots_hbm.3), custom_call_target="tpu_custom_call" | custom-call | bytes 49152 | tf_op jit(solution)/shard_map/pallas_call | solution.py:423
  35.8 0.0 collective-permute-done.8.b2_hbm
  35.8 0.0 copy-start.12
  35.8 0.0 collective-permute-done.7.b1_hbm
  35.8 0.0 copy-start.13
  35.8 3.5 %all-to-all-start = ((bf16[32,32,256]{2,1,0:T(8,128)(2,1)}), bf16[32,32,256]{2,1,0:T(8,128)(2,1)S(1)}, u32[]{:S(2)}, u32[]{:S(2)}) async-start(bf16[32,32,256]{2,1,0:T(8,128)(2,1)} %shard_map.90), calls=%async_computation | async-start | bytes 1048576 | tf_op jit(solution)/shard_map/all_to_all | solution.py:532
  39.3 0.1 collective-permute-start.9
  39.5 1.5 %collective-permute-done.9.b3_hbm = bf16[2,128,512]{2,1,0:T(8,128)(2,1)S(1)} collective-permute-done((bf16[2,128,512]{2,1,0:T(8,128)(2,1)S(1)}, bf16[2,128,512]{2,1,0:T(8,128)(2,1)S(1)}, u32[]{:S(2)}, u32[]{:S(2)}) %collective-permute-start.9) | collective-permute-done | bytes 262176 | tf_op jit(solution)/shard_map/ppermute | solution.py:438
  40.9 0.0 copy-done.12
  40.9 0.0 copy-done.13
  40.9 0.7 copy-done.14
  41.6 10.1 %shard_map.92 = (bf16[2,512,2048]{2,1,0:T(8,128)(2,1)}, bf16[4,2048,512]{2,1,0:T(8,128)(2,1)}) custom-call(bf16[2,128,512]{2,1,0:T(8,128)(2,1)} %shard_map.89.block_hbm.b0_hbm, bf16[2,128,512]{2,1,0:T(8,128)(2,1)} %copy-done.13, bf16[2,128,512]{2,1,0:T(8,128)(2,1)} %copy-done.12, bf16[2,128,512]{2,1,0:T(8,128)(2,1)} %copy-done.14, ...), custom_call_target="tpu_custom_call" | custom-call | flops 1610612736 | bytes 13680640 | tf_op jit(solution)/shard_map/pallas_call | solution.py:423
  51.8 3.7 %all-to-all-done.summed_hbm = bf16[32,32,256]{2,1,0:T(8,128)(2,1)S(1)} async-done(((bf16[32,32,256]{2,1,0:T(8,128)(2,1)}), bf16[32,32,256]{2,1,0:T(8,128)(2,1)S(1)}, u32[]{:S(2)}, u32[]{:S(2)}) %all-to-all-start) | async-done | bytes 524320 | tf_op jit(solution)/shard_map/all_to_all | solution.py:532
  55.5 0.8 copy-done
  56.3 7.1 %shard_map.93 = bf16[8,32,384]{2,1,0:T(8,128)(2,1)} custom-call(bf16[32,32,256]{2,1,0:T(8,128)(2,1)} %copy-done, bf16[2,512,2048]{2,1,0:T(8,128)(2,1)} %get-tuple-element.48.factor_hbm, bf16[2,512,512]{2,1,0:T(8,128)(2,1)} %core_hbm.1, bf16[4,2048,512]{2,1,0:T(8,128)(2,1)} %get-tuple-element.49.cross_hbm, s32[8,128]{1,0:T(8,128)} %get-tuple-element.50.starts0_hbm, ...), custom_call_target="tpu_custom_call" | custom-call | bytes 14360576 | tf_op jit(solution)/shard_map/pallas_call | solution.py:423
  63.4 3.6 %all-to-all-start.1 = ((bf16[8,32,384]{2,1,0:T(8,128)(2,1)}), bf16[8,32,384]{2,1,0:T(8,128)(2,1)S(1)}, u32[]{:S(2)}, u32[]{:S(2)}) async-start(bf16[8,32,384]{2,1,0:T(8,128)(2,1)} %shard_map.93), calls=%async_computation.1 | async-start | bytes 393216 | tf_op jit(solution)/shard_map/all_to_all | solution.py:578
  67.1 4.1 %shard_map.94.slots_hbm = s32[2,768]{1,0:T(2,128)} custom-call(s32[2,2048]{1,0:T(2,128)} %blocks_hbm.6), custom_call_target="tpu_custom_call" | custom-call | bytes 22528 | tf_op jit(solution)/shard_map/pallas_call | solution.py:423
  71.1 3.7 %all-to-all-done.1.g0_hbm = bf16[8,32,384]{2,1,0:T(8,128)(2,1)S(1)} async-done(((bf16[8,32,384]{2,1,0:T(8,128)(2,1)}), bf16[8,32,384]{2,1,0:T(8,128)(2,1)S(1)}, u32[]{:S(2)}, u32[]{:S(2)}) %all-to-all-start.1) | async-done | bytes 196640 | tf_op jit(solution)/shard_map/all_to_all | solution.py:578
  74.8 1.2 %collective-permute-start.11 = (bf16[8,32,384]{2,1,0:T(8,128)(2,1)S(1)}, bf16[8,32,384]{2,1,0:T(8,128)(2,1)S(1)}, u32[]{:S(2)}, u32[]{:S(2)}) collective-permute-start(bf16[8,32,384]{2,1,0:T(8,128)(2,1)S(1)} %all-to-all-done.1.g0_hbm), channel_id=1, source_target_pairs={{0,16},{8,24},{16,0},{24,8},{1,17},{9,25},{17,1},{25,9},{2,18},{10... | collective-permute-start | bytes 589832 | tf_op jit(solution)/shard_map/ppermute | solution.py:438
  76.0 0.0 collective-permute-start.10
  76.0 4.5 %collective-permute-done.11.g2_hbm = bf16[8,32,384]{2,1,0:T(8,128)(2,1)S(1)} collective-permute-done((bf16[8,32,384]{2,1,0:T(8,128)(2,1)S(1)}, bf16[8,32,384]{2,1,0:T(8,128)(2,1)S(1)}, u32[]{:S(2)}, u32[]{:S(2)}) %collective-permute-start.11) | collective-permute-done | bytes 196640 | tf_op jit(solution)/shard_map/ppermute | solution.py:438
  80.5 0.0 collective-permute-start.12
  80.5 0.0 collective-permute-done.10.g1_hbm
  80.5 0.0 copy-start.3
  80.5 1.4 %collective-permute-done.12.g3_hbm = bf16[8,32,384]{2,1,0:T(8,128)(2,1)S(1)} collective-permute-done((bf16[8,32,384]{2,1,0:T(8,128)(2,1)S(1)}, bf16[8,32,384]{2,1,0:T(8,128)(2,1)S(1)}, u32[]{:S(2)}, u32[]{:S(2)}) %collective-permute-start.12) | collective-permute-done | bytes 196640 | tf_op jit(solution)/shard_map/ppermute | solution.py:438
  82.0 0.0 copy-done.1
  82.0 0.0 copy-done.2
  82.0 0.0 copy-done.3
  82.0 0.0 copy-start.4
  82.0 0.7 copy-done.4
  82.6 4.4 %shard_map.95 = (f32[1024,256]{1,0:T(8,128)}, f32[1024,256]{1,0:T(8,128)}) custom-call(bf16[8,32,384]{2,1,0:T(8,128)(2,1)} %copy-done.1, bf16[8,32,384]{2,1,0:T(8,128)(2,1)} %copy-done.3, bf16[8,32,384]{2,1,0:T(8,128)(2,1)} %copy-done.2, bf16[8,32,384]{2,1,0:T(8,128)(2,1)} %copy-done.4, s32[2,768]{1,0:T(2,128)} %shard_map.94.slots_hbm, f32[1024,256]{1,0:T(8,128)} %w_hbm.3, ...), custom_call_target="tpu_custom_call" | custom-call | bytes 4986880 | tf_op jit(solution)/shard_map/pallas_call | solution.py:423
  (6 shorter events, 0.0 us)
Async XLA Ops:
  2.9 12.1 %collective-permute-start.4 = (bf16[384,128]{1,0:T(8,128)(2,1)}, bf16[384,128]{1,0:T(8,128)(2,1)S(1)}, u32[]{:S(2)}, u32[]{:S(2)}) collective-permute-start(bf16[384,128]{1,0:T(8,128)(2,1)} %shard_map.86.refs_0_), channel_id=1, source_target_pairs={{0,6},{1,7},{2,4},{3,5},{4,2},{5,3},{6,0},{7,1},{8,14},{9,15},{10,... | collective-permute-start | bytes 294920 | tf_op jit(solution)/shard_map/ppermute | solution.py:438
  8.0 8.5 %collective-permute-start.3 = (bf16[384,128]{1,0:T(8,128)(2,1)}, bf16[384,128]{1,0:T(8,128)(2,1)S(1)}, u32[]{:S(2)}, u32[]{:S(2)}) collective-permute-start(bf16[384,128]{1,0:T(8,128)(2,1)} %shard_map.86.refs_0_), channel_id=1, source_target_pairs={{0,4},{1,5},{2,6},{3,7},{4,0},{5,1},{6,2},{7,3},{8,12},{9,13},{10,... | collective-permute-start | bytes 294920 | tf_op jit(solution)/shard_map/ppermute | solution.py:438
  8.0 10.0 %collective-permute-start.1 = (bf16[384,128]{1,0:T(8,128)(2,1)}, bf16[384,128]{1,0:T(8,128)(2,1)S(1)}, u32[]{:S(2)}, u32[]{:S(2)}) collective-permute-start(bf16[384,128]{1,0:T(8,128)(2,1)} %shard_map.86.refs_0_), channel_id=1, source_target_pairs={{0,2},{1,3},{2,0},{3,1},{4,6},{5,7},{6,4},{7,5},{8,10},{9,11},{10,... | collective-permute-start | bytes 294920 | tf_op jit(solution)/shard_map/ppermute | solution.py:438
  8.6 14.3 %collective-permute-start = (bf16[384,128]{1,0:T(8,128)(2,1)}, bf16[384,128]{1,0:T(8,128)(2,1)S(1)}, u32[]{:S(2)}, u32[]{:S(2)}) collective-permute-start(bf16[384,128]{1,0:T(8,128)(2,1)} %shard_map.86.refs_0_), channel_id=1, source_target_pairs={{0,1},{1,0},{2,3},{3,2},{4,5},{5,4},{6,7},{7,6},{8,9},{9,8},{10,11... | collective-permute-start | bytes 294920 | tf_op jit(solution)/shard_map/ppermute | solution.py:438
  15.0 9.8 %copy-start.5 = (bf16[384,128]{1,0:T(8,128)(2,1)}, bf16[384,128]{1,0:T(8,128)(2,1)S(1)}, u32[]{:S(2)}) copy-start(bf16[384,128]{1,0:T(8,128)(2,1)S(1)} %collective-permute-done.4.refs_6_) | copy-start | bytes 294916
  16.5 8.3 %copy-start.6 = (bf16[384,128]{1,0:T(8,128)(2,1)}, bf16[384,128]{1,0:T(8,128)(2,1)S(1)}, u32[]{:S(2)}) copy-start(bf16[384,128]{1,0:T(8,128)(2,1)S(1)} %collective-permute-done.3.refs_4_) | copy-start | bytes 294916
  16.5 7.2 %collective-permute-start.5 = (bf16[384,128]{1,0:T(8,128)(2,1)S(1)}, bf16[384,128]{1,0:T(8,128)(2,1)S(1)}, u32[]{:S(2)}, u32[]{:S(2)}) collective-permute-start(bf16[384,128]{1,0:T(8,128)(2,1)S(1)} %collective-permute-done.3.refs_4_), channel_id=1, source_target_pairs={{0,1},{1,0},{2,3},{3,2},{4,5},{5,4},{6,7},{7,6},{8,9},{9,8},{10,11... | collective-permute-start | bytes 294920 | tf_op jit(solution)/shard_map/ppermute | solution.py:438
  18.0 6.8 %copy-start.7 = (bf16[384,128]{1,0:T(8,128)(2,1)}, bf16[384,128]{1,0:T(8,128)(2,1)S(1)}, u32[]{:S(2)}) copy-start(bf16[384,128]{1,0:T(8,128)(2,1)S(1)} %collective-permute-done.1.refs_2_) | copy-start | bytes 294916
  18.0 5.7 %collective-permute-start.2 = (bf16[384,128]{1,0:T(8,128)(2,1)S(1)}, bf16[384,128]{1,0:T(8,128)(2,1)S(1)}, u32[]{:S(2)}, u32[]{:S(2)}) collective-permute-start(bf16[384,128]{1,0:T(8,128)(2,1)S(1)} %collective-permute-done.1.refs_2_), channel_id=1, source_target_pairs={{0,1},{1,0},{2,3},{3,2},{4,5},{5,4},{6,7},{7,6},{8,9},{9,8},{10,11... | collective-permute-start | bytes 294920 | tf_op jit(solution)/shard_map/ppermute | solution.py:438
  18.5 6.3 %collective-permute-start.6 = (bf16[384,128]{1,0:T(8,128)(2,1)S(1)}, bf16[384,128]{1,0:T(8,128)(2,1)S(1)}, u32[]{:S(2)}, u32[]{:S(2)}) collective-permute-start(bf16[384,128]{1,0:T(8,128)(2,1)S(1)} %collective-permute-done.4.refs_6_), channel_id=1, source_target_pairs={{0,1},{1,0},{2,3},{3,2},{4,5},{5,4},{6,7},{7,6},{8,9},{9,8},{10,11... | collective-permute-start | bytes 294920 | tf_op jit(solution)/shard_map/ppermute | solution.py:438
  23.0 1.8 %copy-start.8 = (bf16[384,128]{1,0:T(8,128)(2,1)}, bf16[384,128]{1,0:T(8,128)(2,1)S(1)}, u32[]{:S(2)}) copy-start(bf16[384,128]{1,0:T(8,128)(2,1)S(1)} %collective-permute-done.refs_1_) | copy-start | bytes 294916
  23.7 1.1 %copy-start.10 = (bf16[384,128]{1,0:T(8,128)(2,1)}, bf16[384,128]{1,0:T(8,128)(2,1)S(1)}, u32[]{:S(2)}) copy-start(bf16[384,128]{1,0:T(8,128)(2,1)S(1)} %collective-permute-done.2.refs_3_) | copy-start | bytes 294916
  23.7 1.1 %copy-start.9 = (bf16[384,128]{1,0:T(8,128)(2,1)}, bf16[384,128]{1,0:T(8,128)(2,1)S(1)}, u32[]{:S(2)}) copy-start(bf16[384,128]{1,0:T(8,128)(2,1)S(1)} %collective-permute-done.5.refs_5_) | copy-start | bytes 294916
  24.8 0.6 copy-start.11
  27.7 8.0 %collective-permute-start.8 = (bf16[2,128,512]{2,1,0:T(8,128)(2,1)}, bf16[2,128,512]{2,1,0:T(8,128)(2,1)S(1)}, u32[]{:S(2)}, u32[]{:S(2)}) collective-permute-start(bf16[2,128,512]{2,1,0:T(8,128)(2,1)} %shard_map.89.block_hbm.b0_hbm), channel_id=1, source_target_pairs={{0,16},{8,24},{16,0},{24,8},{1,17},{9,25},{17,1},{25,9},{2,18},{10... | collective-permute-start | bytes 786440 | tf_op jit(solution)/shard_map/ppermute | solution.py:438
  29.2 6.5 %collective-permute-start.7 = (bf16[2,128,512]{2,1,0:T(8,128)(2,1)}, bf16[2,128,512]{2,1,0:T(8,128)(2,1)S(1)}, u32[]{:S(2)}, u32[]{:S(2)}) collective-permute-start(bf16[2,128,512]{2,1,0:T(8,128)(2,1)} %shard_map.89.block_hbm.b0_hbm), channel_id=1, source_target_pairs={{0,8},{8,0},{16,24},{24,16},{1,9},{9,1},{17,25},{25,17},{2,10},{10... | collective-permute-start | bytes 786440 | tf_op jit(solution)/shard_map/ppermute | solution.py:438
  35.8 5.2 %copy-start.12 = (bf16[2,128,512]{2,1,0:T(8,128)(2,1)}, bf16[2,128,512]{2,1,0:T(8,128)(2,1)S(1)}, u32[]{:S(2)}) copy-start(bf16[2,128,512]{2,1,0:T(8,128)(2,1)S(1)} %collective-permute-done.8.b2_hbm) | copy-start | bytes 786436
  35.8 5.1 %copy-start.13 = (bf16[2,128,512]{2,1,0:T(8,128)(2,1)}, bf16[2,128,512]{2,1,0:T(8,128)(2,1)S(1)}, u32[]{:S(2)}) copy-start(bf16[2,128,512]{2,1,0:T(8,128)(2,1)S(1)} %collective-permute-done.7.b1_hbm) | copy-start | bytes 786436
  35.8 19.7 %all-to-all-start = ((bf16[32,32,256]{2,1,0:T(8,128)(2,1)}), bf16[32,32,256]{2,1,0:T(8,128)(2,1)S(1)}, u32[]{:S(2)}, u32[]{:S(2)}) async-start(bf16[32,32,256]{2,1,0:T(8,128)(2,1)} %shard_map.90), calls=%async_computation | async-start | bytes 1048576 | tf_op jit(solution)/shard_map/all_to_all | solution.py:532
  39.3 1.6 %collective-permute-start.9 = (bf16[2,128,512]{2,1,0:T(8,128)(2,1)S(1)}, bf16[2,128,512]{2,1,0:T(8,128)(2,1)S(1)}, u32[]{:S(2)}, u32[]{:S(2)}) collective-permute-start(bf16[2,128,512]{2,1,0:T(8,128)(2,1)S(1)} %collective-permute-done.8.b2_hbm), channel_id=1, source_target_pairs={{0,8},{8,0},{16,24},{24,16},{1,9},{9,1},{17,25},{25,17},{2,10},{10... | collective-permute-start | bytes 786440 | tf_op jit(solution)/shard_map/ppermute | solution.py:438
  40.9 0.7 copy-start.14
  55.5 0.8 copy-start
  63.4 11.4 %all-to-all-start.1 = ((bf16[8,32,384]{2,1,0:T(8,128)(2,1)}), bf16[8,32,384]{2,1,0:T(8,128)(2,1)S(1)}, u32[]{:S(2)}, u32[]{:S(2)}) async-start(bf16[8,32,384]{2,1,0:T(8,128)(2,1)} %shard_map.93), calls=%async_computation.1 | async-start | bytes 393216 | tf_op jit(solution)/shard_map/all_to_all | solution.py:578
  74.8 7.1 %copy-start.1 = (bf16[8,32,384]{2,1,0:T(8,128)(2,1)}, bf16[8,32,384]{2,1,0:T(8,128)(2,1)S(1)}, u32[]{:S(2)}) copy-start(bf16[8,32,384]{2,1,0:T(8,128)(2,1)S(1)} %all-to-all-done.1.g0_hbm) | copy-start | bytes 589828
  74.8 5.7 %collective-permute-start.11 = (bf16[8,32,384]{2,1,0:T(8,128)(2,1)S(1)}, bf16[8,32,384]{2,1,0:T(8,128)(2,1)S(1)}, u32[]{:S(2)}, u32[]{:S(2)}) collective-permute-start(bf16[8,32,384]{2,1,0:T(8,128)(2,1)S(1)} %all-to-all-done.1.g0_hbm), channel_id=1, source_target_pairs={{0,16},{8,24},{16,0},{24,8},{1,17},{9,25},{17,1},{25,9},{2,18},{10... | collective-permute-start | bytes 589832 | tf_op jit(solution)/shard_map/ppermute | solution.py:438
  76.0 4.5 %collective-permute-start.10 = (bf16[8,32,384]{2,1,0:T(8,128)(2,1)S(1)}, bf16[8,32,384]{2,1,0:T(8,128)(2,1)S(1)}, u32[]{:S(2)}, u32[]{:S(2)}) collective-permute-start(bf16[8,32,384]{2,1,0:T(8,128)(2,1)S(1)} %all-to-all-done.1.g0_hbm), channel_id=1, source_target_pairs={{0,8},{8,0},{16,24},{24,16},{1,9},{9,1},{17,25},{25,17},{2,10},{10... | collective-permute-start | bytes 589832 | tf_op jit(solution)/shard_map/ppermute | solution.py:438
  80.5 1.4 %copy-start.2 = (bf16[8,32,384]{2,1,0:T(8,128)(2,1)}, bf16[8,32,384]{2,1,0:T(8,128)(2,1)S(1)}, u32[]{:S(2)}) copy-start(bf16[8,32,384]{2,1,0:T(8,128)(2,1)S(1)} %collective-permute-done.11.g2_hbm) | copy-start | bytes 589828
  80.5 1.4 %collective-permute-start.12 = (bf16[8,32,384]{2,1,0:T(8,128)(2,1)S(1)}, bf16[8,32,384]{2,1,0:T(8,128)(2,1)S(1)}, u32[]{:S(2)}, u32[]{:S(2)}) collective-permute-start(bf16[8,32,384]{2,1,0:T(8,128)(2,1)S(1)} %collective-permute-done.11.g2_hbm), channel_id=1, source_target_pairs={{0,8},{8,0},{16,24},{24,16},{1,9},{9,1},{17,25},{25,17},{2,10},{10... | collective-permute-start | bytes 589832 | tf_op jit(solution)/shard_map/ppermute | solution.py:438
  80.5 1.4 %copy-start.3 = (bf16[8,32,384]{2,1,0:T(8,128)(2,1)}, bf16[8,32,384]{2,1,0:T(8,128)(2,1)S(1)}, u32[]{:S(2)}) copy-start(bf16[8,32,384]{2,1,0:T(8,128)(2,1)S(1)} %collective-permute-done.10.g1_hbm) | copy-start | bytes 589828
  82.0 0.7 copy-start.4

commit v17 on v13

--- a/solution.py
+++ b/solution.py
@@ -60,14 +60,18 @@
     return one_hot(iota((n, n), 0) < iota((n, n), 1))
 
 
-def owners_of(indices, before, points, owners):
-    owner = lax.div(indices, jnp.full_like(indices, points))
-    owner_ids = iota((owners, indices.shape[1]), 0)
-    marks = jnp.where(owner_ids == owner, 1.0, 0.0)
-    earlier = mm(marks.astype(bf16), before, 1, 0)
-    rank = jnp.sum(marks * earlier, axis=0, keepdims=True)
-    start = jnp.sum(jnp.where(owner < owner_ids, 1.0, 0.0), axis=1, keepdims=True)
-    return marks, rank, start
+def owners_of(groups, points, owners):
+    owner_ids = iota((owners, groups[0].shape[1]), 0)
+    owner = [lax.div(x, jnp.full_like(x, points)) for x in groups]
+    marks = [jnp.where(owner_ids == x, 1.0, 0.0) for x in owner]
+    every = jnp.concatenate(marks, axis=0).astype(bf16)
+    earlier = mm(every, before_matrix(every.shape[1]), 1, 0)
+    out = []
+    for n, x in enumerate(owner):
+        rank = jnp.sum(marks[n] * earlier[n * owners : (n + 1) * owners], axis=0, keepdims=True)
+        start = jnp.sum(jnp.where(x < owner_ids, 1.0, 0.0), axis=1, keepdims=True)
+        out.append((marks[n], rank, start))
+    return out
 
 
 def sorted_places(marks, rank, start):
@@ -80,15 +84,14 @@
     return jnp.sum(jnp.where(diagonal, column, 0.0), axis=0, keepdims=True).astype(i32)
 
 
-def sorted_points(indices, place):
-    count = indices.shape[1]
-    return from_digits(mm(two_digits(indices), one_hot(iota((count, count), 0) == place), 1, 1))
-
-
-def two_digits(row):
-    high = lax.shift_right_logical(row, jnp.full_like(row, 7))
-    shape = (8, row.shape[1])
-    value = jnp.where(iota(shape, 0) == 0, high, lax.bitwise_and(row, jnp.full_like(row, 127)))
+def two_digits(*rows):
+    shape = (8, rows[0].shape[1])
+    value = jnp.zeros(shape, i32)
+    for n, row in enumerate(rows):
+        high = lax.shift_right_logical(row, jnp.full_like(row, 7))
+        low = lax.bitwise_and(row, jnp.full_like(row, 127))
+        value = jnp.where(iota(shape, 0) == 2 * n, high, value)
+        value = jnp.where(iota(shape, 0) == 2 * n + 1, low, value)
     return value.astype(f32).astype(bf16)
 
 
@@ -141,14 +144,19 @@
     row, me = lax.axis_index("rows"), lax.axis_index("pts")
     points, outputs = w.shape
     reads = start_all([(blocks_hbm, blocks), (w_hbm, w), (z_hbm, z), (t_hbm, t)], sems)
-    before = before_matrix(count)
     reads[0].wait()
-    locals_of = []
-    for u in range(UPDATES):
-        indices = group_row(blocks, u, row, count)
-        marks, rank, start = owners_of(indices, before, points, owners)
+    groups = [group_row(blocks, u, row, count) for u in range(UPDATES)]
+    found, shift = [], []
+    for u, (_, rank, start) in enumerate(owners_of(groups, points, owners)):
         starts[u : u + 1, :] = lane_row(start)
-        locals_of.append(sorted_points(indices, sorted_places(marks, rank, start)) - me * points)
+        local = groups[u] - me * points
+        mine = (local >= 0) & (local < points)
+        held = jnp.where(mine, rank.astype(i32), -1)
+        chosen = one_hot(iota((count // 2, count), 0) == held)
+        digits = two_digits(jnp.where(mine, local + 1, 0))
+        found.append(from_digits(mm(digits, chosen, 1, 1)) - 1)
+        earlier = jnp.sum(jnp.where(groups[u] < me * points, 1.0, 0.0))
+        shift.append(lax.rem(earlier.astype(i32), count))
     writes = start_all([(starts, starts_hbm)], out_sems)
     wait_all(reads[1:])
     current, moving = w[...], z[...]
@@ -157,8 +165,11 @@
         mixed = mixed_of(current, moving).T
         high, low = split_two(ridge_term * mixed - goal)
         coef[u] = mixed.astype(bf16)
-        place = one_hot(iota((points, count), 0) == locals_of[u])
-        offset[u] = mm(high, place, 1, 0) + mm(low, place, 1, 0)
+        place = one_hot(iota((points, count // 2), 0) == found[u])
+        both = mm(jnp.concatenate([high, low], axis=0), place, 1, 0)
+        held = both[:outputs] + both[outputs:]
+        held = jnp.concatenate([held, jnp.zeros_like(held)], axis=1)
+        offset[u] = pltpu.roll(held, shift[u], 1)
         current, moving = stepped(current, moving, None)
         for a, b in ((coef, coef_hbm), (offset, offset_hbm)):
             writes.append(pltpu.make_async_copy(a.at[u], b.at[u], out_sems.at[len(writes)]))
@@ -168,26 +179,25 @@
 
 def order_kernel(
     count, points, owners,
-    blocks_hbm, pivots_hbm, ids_hbm, starts_hbm, chosen_hbm,
-    blocks, pivots, ids, starts, chosen, sems,
+    blocks_hbm, ids_hbm, from_hbm, starts_hbm,
+    blocks, ids, came_from, starts, sems,
 ):
-    wait_all(start_all([(blocks_hbm, blocks), (pivots_hbm, pivots)], sems))
-    before = before_matrix(count)
-    groups = blocks.shape[1] // count
-    for u in range(UPDATES):
-        pivot = pivots[u : u + 1, :]
-        found = jnp.zeros((8, pivot.shape[1]), f32)
-        for g in range(groups):
-            n = u * groups + g
-            indices = blocks[u : u + 1, g * count : (g + 1) * count]
-            marks, rank, start = owners_of(indices, before, points, owners)
-            place = sorted_places(marks, rank, start)
-            ids[n : n + 1, :] = sorted_points(indices, place)
-            starts[n : n + 1, :] = lane_row(start)
-            at_pivot = one_hot(iota((count, pivot.shape[1]), 0) + g * count == pivot)
-            found += mm(two_digits(place + g * count), at_pivot, 1, 0)
-        chosen[u : u + 1, :] = from_digits(found)
-    wait_all(start_all([(ids, ids_hbm), (starts, starts_hbm), (chosen, chosen_hbm)], sems))
+    wait_all(start_all([(blocks_hbm, blocks)], sems))
+    count_of = blocks.shape[1] // count
+    groups = [
+        blocks[u : u + 1, g * count : (g + 1) * count]
+        for u in range(UPDATES)
+        for g in range(count_of)
+    ]
+    for n, (marks, rank, start) in enumerate(owners_of(groups, points, owners)):
+        place = sorted_places(marks, rank, start)
+        given = iota((1, count), 1) + (n % count_of) * count
+        digits = two_digits(groups[n], given)
+        moved = mm(digits, one_hot(iota((count, count), 0) == place), 1, 1)
+        ids[n : n + 1, :] = from_digits(moved[0:2])
+        came_from[n : n + 1, :] = from_digits(moved[2:4])
+        starts[n : n + 1, :] = lane_row(start)
+    wait_all(start_all([(ids, ids_hbm), (came_from, from_hbm), (starts, starts_hbm)], sems))
 
 
 def slots_kernel(count, points, cap, blocks_hbm, slots_hbm, blocks, slots, sems):
@@ -273,21 +283,25 @@
 
 
 def factors_kernel(
-    b0_hbm, b1_hbm, b2_hbm, b3_hbm, ids_hbm, pivots_hbm, factor_hbm, cross_hbm,
-    feats, ids, pivots, factor, cross, sems,
+    b0_hbm, b1_hbm, b2_hbm, b3_hbm, ids_hbm, from_hbm, pivots_hbm, factor_hbm, cross_hbm,
+    feats, ids, came_from, pivots, factor, cross, sems,
 ):
     row = lax.axis_index("rows")
     groups, _, width, count = feats.shape
     pairs = [(b_hbm, feats.at[k]) for k, b_hbm in enumerate((b0_hbm, b1_hbm, b2_hbm, b3_hbm))]
-    wait_all(start_all(pairs + [(ids_hbm, ids), (pivots_hbm, pivots)], sems))
+    pairs += [(ids_hbm, ids), (from_hbm, came_from), (pivots_hbm, pivots)]
+    wait_all(start_all(pairs, sems))
     places = [lax.bitwise_xor(row, k) for k in range(groups)]
     rights = [[extended(feats[k, u], 0, False) for k in range(groups)] for u in range(UPDATES)]
-    for u in range(UPDATES):
-        chosen_feats = jnp.zeros((width, pivots.shape[1]), f32)
+    given = [[feats[k, u].astype(f32).T for k in range(groups)] for u in range(UPDATES)]
+    for u in range(UPDATES):
+        wanted = pivots[u : u + 1, :].astype(f32)
+        wanted = jnp.broadcast_to(wanted, (8, wanted.shape[1])).T[:, 0:1]
+        chosen_feats = jnp.zeros((pivots.shape[1], width), f32)
         for k in range(groups):
-            chosen = iota((count, pivots.shape[1]), 0) + places[k] * count == pivots[u : u + 1, :]
-            chosen_feats += mm(feats[k, u], one_hot(chosen), 1, 0)
-        left = extended(chosen_feats.T, 1, True)
+            here = came_from[pl.ds(u * groups + places[k], 1), :].astype(f32)
+            chosen_feats += mm(one_hot(wanted == here), given[u][k].astype(bf16), 1, 0)
+        left = extended(chosen_feats, 1, True)
         for k in range(groups):
             start = pl.multiple_of(places[k] * count, count)
             value = jnp.exp2(exponent(left, rights[u][k]))
@@ -295,7 +309,7 @@
     writes = start_all([(factor, factor_hbm)], sems)
     lefts, left_points = [], []
     for k in range(groups):
-        lefts.append(extended(feats[k, 0].astype(f32).T, 1, True))
+        lefts.append(extended(given[0][k], 1, True))
         points = ids[pl.ds(places[k], 1), :].astype(f32)
         left_points.append(jnp.broadcast_to(points, (8, count)).T[:, 0:1])
     left, left_points = jnp.concatenate(lefts, axis=0), jnp.concatenate(left_points, axis=0)
@@ -459,7 +473,9 @@
         features,
         sems=(2,),
     )
-    came = {k: swap(packed, "pts", k) for k in reversed(range(3, owners))}
+    came = {k: swap(packed, "pts", k) for k in reversed(range(2, owners, 2))}
+    came[1] = swap(packed, "pts", 1)
+    came[3] = swap(came[2], "pts", 1)
     kept = [
         like((UPDATES, outputs, points)),
         like((UPDATES, outputs, count), f32),
@@ -473,8 +489,20 @@
         *given,
         sems=(4, 1 + 2 * UPDATES),
     )
-    again, row_starts = lax.optimization_barrier((packed, row_starts))
-    came.update({k: swap(again, "pts", k) for k in (2, 1)})
+    came[4], came[6], row_starts, later_index = lax.optimization_barrier(
+        (came[4], came[6], row_starts, block_index)
+    )
+    came[5], came[7] = swap(came[4], "pts", 1), swap(came[6], "pts", 1)
+
+    kept = [like((UPDATES * rows, count), i32)] * 2 + [like((8, 128), i32)]
+    ids, came_from, starts = call(
+        functools.partial(order_kernel, count, points, owners),
+        kept,
+        [block_index, *kept],
+        later_index,
+        sems=(3,),
+    )
+    row_starts, ids = lax.optimization_barrier((row_starts, ids))
     feats = like((UPDATES, width, count))
     inside_starts = pltpu.SMEM(row_starts.shape, i32)
     (mine,) = call(
@@ -505,17 +533,7 @@
         sems=(4,),
         flops=2.0 * UPDATES * points * count * (2 * width + outputs),
     )
-    pieces, later_index = lax.optimization_barrier((pieces, block_index))
-    kept = [like((UPDATES * rows, count), i32), like((8, 128), i32), like((UPDATES, rank), i32)]
-    ids, starts, chosen = call(
-        functools.partial(order_kernel, count, points, owners),
-        kept,
-        [block_index, pivot_index, *kept],
-        later_index,
-        pivot_index,
-        sems=(3,),
-    )
-    pieces, across, ids = lax.optimization_barrier((pieces, across, ids))
+    pieces, beside, across = lax.optimization_barrier((pieces, beside, across))
     summed = lax.all_to_all(pieces, ("rows", "pts"), 0, 0, tiled=True)
     kept = [like((UPDATES, rank, block)), like((rows, block, count))]
     factor, cross = call(
@@ -524,7 +542,8 @@
         [
             like((rows, *feats.shape)),
             ids,
-            chosen,
+            came_from,
+            pivot_index,
             kept[0],
             like((rows, rows, count, count)),
         ],
@@ -533,7 +552,8 @@
         across,
         swap(across, "rows", 1),
         ids,
-        chosen,
+        came_from,
+        pivot_index,
         sems=(rows * rows + 2,),
         grant=60,
         flops=2.0 * width * block * (UPDATES * rank + block),
@@ -548,7 +568,7 @@
         core,
         cross,
         starts,
-        sems=(2 * UPDATES + 2 + rows,),
+        sems=(2 * UPDATES + 3 + rows,),
         grant=60,
     )
     steps, later_index = lax.optimization_barrier((steps, block_index))
@@ -652,7 +672,7 @@
     rows, owners = lax.axis_size("rows"), lax.axis_size("pts")
     count = block_index.shape[1] // rows
     fits = rows == 4 and owners == 8 and coefficients.shape[1] == 8 * rows * owners
-    fits = fits and coefficients.shape[0] % CHUNK == 0 and count % CHUNK == 0 and (3 * count // owners) % 64 == 0 and UPDATES * rows == 8
+    fits = fits and 6 * count <= count * owners and coefficients.shape[0] % CHUNK == 0 and count % CHUNK == 0 and (3 * count // owners) % 64 == 0 and UPDATES * rows == 8
     plan = with_kernels if fits else with_operations
     return plan(
         features, targets, coefficients, momentum, block_index, pivot_index, nystrom_core

time: 91.4 us -> 87.1 us (0.953)
  starting transfers between devices: 24.4 us -> 21.6 us
    ppermute x13, starting transfers between devices: 17.7 us -> 14.1 us  [swap(): lax.ppermute(value, axis, [(i, i ^ k) for i in range(lax.axis_size(axis))])]
    all_to_all x1, waiting for transfers between devices: 3.34 us -> 2.37 us  [with_kernels(): summed = lax.all_to_all(pieces, ('rows', 'pts'), 0, 0, tiled=True)]
where the time goes in v17:
time: 87.1 us; the launch traced here: 86.4 us
  Pallas kernels  41.8 us (48%)
  starting transfers between devices  21.6 us (25%)
  waiting for transfers between devices  19.1 us (22%)
  local copies, waits for them, and re-layouts  2.82 us (3%)
  between operations  1 us (1%)
    pallas_call x9, Pallas kernels, call(): pl.pallas_call(body, out_shape=outs, in_specs=[VMEM] * near + [HBM] * (le...  41.8 us
    ppermute x13, starting transfers between devices, swap(): lax.ppermute(value, axis, [(i, i ^ k) for i in range(lax.axis_size(axis))])  14.1 us
    ppermute x13, waiting for transfers between devices, swap(): lax.ppermute(value, axis, [(i, i ^ k) for i in range(lax.axis_size(axis))])  12.9 us
    all_to_all x1, starting transfers between devices, with_kernels(): summed = lax.all_to_all(pieces, ('rows', 'pts'), 0, 0, tiled=True)  3.86 us
    all_to_all x1, waiting for transfers between devices, with_kernels(): got = lax.all_to_all(steps, 'pts', 0, 0, tiled=True)  3.85 us
    all_to_all x1, starting transfers between devices, with_kernels(): got = lax.all_to_all(steps, 'pts', 0, 0, tiled=True)  3.62 us
    unnamed x30, local copies, waits for them, and re-layouts  2.82 us
    all_to_all x1, waiting for transfers between devices, with_kernels(): summed = lax.all_to_all(pieces, ('rows', 'pts'), 0, 0, tiled=True)  2.37 us
  transfers between devices with their start and end apart: 15, of which 9 were waited for; matrix products, arithmetic and copies ran while one was open for 0% of the time, Pallas kernels for 30%

profile of v17, /device:TPU:0, one launch (start us, length us, event | category | flops | bytes accessed | tf_op | source)
XLA Modules:
  0.0 86.4 jit_solution(16459671053509846509)
XLA Ops:
  0.6 2.2 %shard_map.86.refs_0_ = bf16[384,128]{1,0:T(8,128)(2,1)} custom-call(s32[2,2048]{1,0:T(2,128)} %blocks_hbm.5, bf16[1024,128]{1,0:T(8,128)(2,1)} %feats_hbm.3), custom_call_target="tpu_custom_call" | custom-call | bytes 376832 | tf_op jit(solution)/shard_map/pallas_call | solution.py:436
  2.9 5.1 %collective-permute-start.4 = (bf16[384,128]{1,0:T(8,128)(2,1)}, bf16[384,128]{1,0:T(8,128)(2,1)S(1)}, u32[]{:S(2)}, u32[]{:S(2)}) collective-permute-start(bf16[384,128]{1,0:T(8,128)(2,1)} %shard_map.86.refs_0_), channel_id=1, source_target_pairs={{0,6},{1,7},{2,4},{3,5},{4,2},{5,3},{6,0},{7,1},{8,14},{9,15},{10,... | collective-permute-start | bytes 294920 | tf_op jit(solution)/shard_map/ppermute | solution.py:451
  8.0 0.0 collective-permute-start.3
  8.0 0.6 collective-permute-start.1
  8.6 1.7 %collective-permute-start = (bf16[384,128]{1,0:T(8,128)(2,1)}, bf16[384,128]{1,0:T(8,128)(2,1)S(1)}, u32[]{:S(2)}, u32[]{:S(2)}) collective-permute-start(bf16[384,128]{1,0:T(8,128)(2,1)} %shard_map.86.refs_0_), channel_id=1, source_target_pairs={{0,1},{1,0},{2,3},{3,2},{4,5},{5,4},{6,7},{7,6},{8,9},{9,8},{10,11... | collective-permute-start | bytes 294920 | tf_op jit(solution)/shard_map/ppermute | solution.py:451
  10.3 4.3 %shard_map.87 = (bf16[2,256,1024]{2,1,0:T(8,128)(2,1)}, f32[2,256,512]{2,1,0:T(8,128)}, s32[8,128]{1,0:T(8,128)}) custom-call(s32[2,2048]{1,0:T(2,128)} %blocks_hbm.5, f32[1024,256]{1,0:T(8,128)} %w_hbm.3, f32[1024,256]{1,0:T(8,128)} %z_hbm.3, bf16[1024,256]{1,0:T(8,128)(2,1)} %t_hbm.1), custom_call_target="tpu_custom_call" | custom-call | bytes 4739072 | tf_op jit(solution)/shard_map/pallas_call | solution.py:436
  14.6 0.0 collective-permute-done.4.refs_6_
  14.6 0.0 copy-start.5
  14.6 1.9 %collective-permute-done.3.refs_4_ = bf16[384,128]{1,0:T(8,128)(2,1)S(1)} collective-permute-done((bf16[384,128]{1,0:T(8,128)(2,1)}, bf16[384,128]{1,0:T(8,128)(2,1)S(1)}, u32[]{:S(2)}, u32[]{:S(2)}) %collective-permute-start.3) | collective-permute-done | bytes 98336 | tf_op jit(solution)/shard_map/ppermute | solution.py:451
  16.5 0.0 copy-start.6
  16.5 1.5 %collective-permute-start.5 = (bf16[384,128]{1,0:T(8,128)(2,1)S(1)}, bf16[384,128]{1,0:T(8,128)(2,1)S(1)}, u32[]{:S(2)}, u32[]{:S(2)}) collective-permute-start(bf16[384,128]{1,0:T(8,128)(2,1)S(1)} %collective-permute-done.3.refs_4_), channel_id=1, source_target_pairs={{0,1},{1,0},{2,3},{3,2},{4,5},{5,4},{6,7},{7,6},{8,9},{9,8},{10,11... | collective-permute-start | bytes 294920 | tf_op jit(solution)/shard_map/ppermute | solution.py:451
  18.0 0.0 collective-permute-done.1.refs_2_
  18.0 0.0 copy-start.7
  18.0 0.5 collective-permute-start.2
  18.5 1.5 %collective-permute-start.6 = (bf16[384,128]{1,0:T(8,128)(2,1)S(1)}, bf16[384,128]{1,0:T(8,128)(2,1)S(1)}, u32[]{:S(2)}, u32[]{:S(2)}) collective-permute-start(bf16[384,128]{1,0:T(8,128)(2,1)S(1)} %collective-permute-done.4.refs_6_), channel_id=1, source_target_pairs={{0,1},{1,0},{2,3},{3,2},{4,5},{5,4},{6,7},{7,6},{8,9},{9,8},{10,11... | collective-permute-start | bytes 294920 | tf_op jit(solution)/shard_map/ppermute | solution.py:451
  20.0 2.8 %shard_map.88 = (s32[8,512]{1,0:T(8,128)}, s32[8,512]{1,0:T(8,128)}, s32[8,128]{1,0:T(8,128)}) custom-call(s32[2,2048]{1,0:T(2,128)} %blocks_hbm.5), custom_call_target="tpu_custom_call" | custom-call | bytes 53248 | tf_op jit(solution)/shard_map/pallas_call | solution.py:436
  22.8 0.0 collective-permute-done.refs_1_
  22.8 0.0 copy-start.8
  22.8 0.9 %collective-permute-done.2.refs_3_ = bf16[384,128]{1,0:T(8,128)(2,1)S(1)} collective-permute-done((bf16[384,128]{1,0:T(8,128)(2,1)S(1)}, bf16[384,128]{1,0:T(8,128)(2,1)S(1)}, u32[]{:S(2)}, u32[]{:S(2)}) %collective-permute-start.2) | collective-permute-done | bytes 98336 | tf_op jit(solution)/shard_map/ppermute | solution.py:451
  23.7 0.0 copy-start.10
  23.7 0.0 collective-permute-done.5.refs_5_
  23.7 0.0 copy-start.9
  23.7 1.0 %collective-permute-done.6.refs_7_ = bf16[384,128]{1,0:T(8,128)(2,1)S(1)} collective-permute-done((bf16[384,128]{1,0:T(8,128)(2,1)S(1)}, bf16[384,128]{1,0:T(8,128)(2,1)S(1)}, u32[]{:S(2)}, u32[]{:S(2)}) %collective-permute-start.6) | collective-permute-done | bytes 98336 | tf_op jit(solution)/shard_map/ppermute | solution.py:451
  24.8 0.0 copy-done.5
  24.8 0.0 copy-done.6
  24.8 0.0 copy-done.7
  24.8 0.0 copy-done.8
  24.8 0.0 copy-done.10
  24.8 0.0 copy-done.9
  24.8 0.0 copy-start.11
  24.8 0.6 copy-done.11
  25.4 2.3 %shard_map.89.block_hbm.b0_hbm = bf16[2,128,512]{2,1,0:T(8,128)(2,1)} custom-call(bf16[384,128]{1,0:T(8,128)(2,1)} %shard_map.86.refs_0_, bf16[384,128]{1,0:T(8,128)(2,1)} %copy-done.8, bf16[384,128]{1,0:T(8,128)(2,1)} %copy-done.7, bf16[384,128]{1,0:T(8,128)(2,1)} %copy-done.10, bf16[384,128]{1,0:T(8,128)(2,1)} %copy-done.6, bf16[384,128]{1,0:T(8,128)(2,1)} %copy-done.9, ...), custom_call_target="tpu_custom_call" | custom-call | bytes 1052672 | tf_op jit(solution)/shard_map/pallas_call | solution.py:436
  27.7 1.5 %collective-permute-start.8 = (bf16[2,128,512]{2,1,0:T(8,128)(2,1)}, bf16[2,128,512]{2,1,0:T(8,128)(2,1)S(1)}, u32[]{:S(2)}, u32[]{:S(2)}) collective-permute-start(bf16[2,128,512]{2,1,0:T(8,128)(2,1)} %shard_map.89.block_hbm.b0_hbm), channel_id=1, source_target_pairs={{0,16},{8,24},{16,0},{24,8},{1,17},{9,25},{17,1},{25,9},{2,18},{10... | collective-permute-start | bytes 786440 | tf_op jit(solution)/shard_map/ppermute | solution.py:451
  29.2 0.0 collective-permute-start.7
  29.2 3.6 %shard_map.90 = bf16[32,32,256]{2,1,0:T(8,128)(2,1)} custom-call(bf16[2,128,512]{2,1,0:T(8,128)(2,1)} %shard_map.89.block_hbm.b0_hbm, bf16[1024,128]{1,0:T(8,128)(2,1)} %feats_hbm.3, bf16[2,256,1024]{2,1,0:T(8,128)(2,1)} %get-tuple-element.30.coef_hbm, f32[2,256,512]{2,1,0:T(8,128)} %get-tuple-element.31.offset_hbm), custom_call_target="tpu_custom_call" | custom-call | flops 1073741824 | bytes 3145728 | tf_op jit(solution)/shard_map/pallas_call | solution.py:436
  32.8 2.0 %collective-permute-done.8.b2_hbm = bf16[2,128,512]{2,1,0:T(8,128)(2,1)S(1)} collective-permute-done((bf16[2,128,512]{2,1,0:T(8,128)(2,1)}, bf16[2,128,512]{2,1,0:T(8,128)(2,1)S(1)}, u32[]{:S(2)}, u32[]{:S(2)}) %collective-permute-start.8) | collective-permute-done | bytes 262176 | tf_op jit(solution)/shard_map/ppermute | solution.py:451
  34.8 0.0 copy-start.12
  34.8 0.0 collective-permute-done.7.b1_hbm
  34.8 3.9 %all-to-all-start = ((bf16[32,32,256]{2,1,0:T(8,128)(2,1)}), bf16[32,32,256]{2,1,0:T(8,128)(2,1)S(1)}, u32[]{:S(2)}, u32[]{:S(2)}) async-start(bf16[32,32,256]{2,1,0:T(8,128)(2,1)} %shard_map.90), calls=%async_computation | async-start | bytes 1048576 | tf_op jit(solution)/shard_map/all_to_all | solution.py:537
  38.7 0.1 collective-permute-start.9
  38.8 1.5 %collective-permute-done.9.b3_hbm = bf16[2,128,512]{2,1,0:T(8,128)(2,1)S(1)} collective-permute-done((bf16[2,128,512]{2,1,0:T(8,128)(2,1)S(1)}, bf16[2,128,512]{2,1,0:T(8,128)(2,1)S(1)}, u32[]{:S(2)}, u32[]{:S(2)}) %collective-permute-start.9) | collective-permute-done | bytes 262176 | tf_op jit(solution)/shard_map/ppermute | solution.py:451
  40.3 0.0 copy-done.12
  40.3 0.0 copy-done.13
  40.3 0.7 copy-done.14
  41.0 11.5 %shard_map.91 = (bf16[2,512,2048]{2,1,0:T(8,128)(2,1)}, bf16[4,2048,512]{2,1,0:T(8,128)(2,1)}) custom-call(bf16[2,128,512]{2,1,0:T(8,128)(2,1)} %shard_map.89.block_hbm.b0_hbm, bf16[2,128,512]{2,1,0:T(8,128)(2,1)} %copy-done.13, bf16[2,128,512]{2,1,0:T(8,128)(2,1)} %copy-done.12, bf16[2,128,512]{2,1,0:T(8,128)(2,1)} %copy-done.14, ...), custom_call_target="tpu_custom_call" | custom-call | flops 1610612736 | bytes 13668352 | tf_op jit(solution)/shard_map/pallas_call | solution.py:436
  52.5 2.4 %all-to-all-done.summed_hbm = bf16[32,32,256]{2,1,0:T(8,128)(2,1)S(1)} async-done(((bf16[32,32,256]{2,1,0:T(8,128)(2,1)}), bf16[32,32,256]{2,1,0:T(8,128)(2,1)S(1)}, u32[]{:S(2)}, u32[]{:S(2)}) %all-to-all-start) | async-done | bytes 524320 | tf_op jit(solution)/shard_map/all_to_all | solution.py:537
  54.8 0.8 copy-done
  55.6 7.1 %shard_map.92 = bf16[8,32,384]{2,1,0:T(8,128)(2,1)} custom-call(bf16[32,32,256]{2,1,0:T(8,128)(2,1)} %copy-done, bf16[2,512,2048]{2,1,0:T(8,128)(2,1)} %get-tuple-element.37.factor_hbm, bf16[2,512,512]{2,1,0:T(8,128)(2,1)} %core_hbm.1, bf16[4,2048,512]{2,1,0:T(8,128)(2,1)} %get-tuple-element.38.cross_hbm, s32[8,128]{1,0:T(8,128)} %get-tuple-element.39.starts_hbm), custom_call_target="tpu_custom_call" | custom-call | bytes 14356480 | tf_op jit(solution)/shard_map/pallas_call | solution.py:436
  62.8 3.6 %all-to-all-start.1 = ((bf16[8,32,384]{2,1,0:T(8,128)(2,1)}), bf16[8,32,384]{2,1,0:T(8,128)(2,1)S(1)}, u32[]{:S(2)}, u32[]{:S(2)}) async-start(bf16[8,32,384]{2,1,0:T(8,128)(2,1)} %shard_map.92), calls=%async_computation.1 | async-start | bytes 393216 | tf_op jit(solution)/shard_map/all_to_all | solution.py:582
  66.4 4.1 %shard_map.93.slots_hbm = s32[2,768]{1,0:T(2,128)} custom-call(s32[2,2048]{1,0:T(2,128)} %blocks_hbm.5), custom_call_target="tpu_custom_call" | custom-call | bytes 22528 | tf_op jit(solution)/shard_map/pallas_call | solution.py:436
  70.5 3.9 %all-to-all-done.1.g0_hbm = bf16[8,32,384]{2,1,0:T(8,128)(2,1)S(1)} async-done(((bf16[8,32,384]{2,1,0:T(8,128)(2,1)}), bf16[8,32,384]{2,1,0:T(8,128)(2,1)S(1)}, u32[]{:S(2)}, u32[]{:S(2)}) %all-to-all-start.1) | async-done | bytes 196640 | tf_op jit(solution)/shard_map/all_to_all | solution.py:582
  74.3 1.4 %collective-permute-start.11 = (bf16[8,32,384]{2,1,0:T(8,128)(2,1)S(1)}, bf16[8,32,384]{2,1,0:T(8,128)(2,1)S(1)}, u32[]{:S(2)}, u32[]{:S(2)}) collective-permute-start(bf16[8,32,384]{2,1,0:T(8,128)(2,1)S(1)} %all-to-all-done.1.g0_hbm), channel_id=1, source_target_pairs={{0,16},{8,24},{16,0},{24,8},{1,17},{9,25},{17,1},{25,9},{2,18},{10... | collective-permute-start | bytes 589832 | tf_op jit(solution)/shard_map/ppermute | solution.py:451
  75.8 0.0 collective-permute-start.10
  75.8 4.2 %collective-permute-done.11.g2_hbm = bf16[8,32,384]{2,1,0:T(8,128)(2,1)S(1)} collective-permute-done((bf16[8,32,384]{2,1,0:T(8,128)(2,1)S(1)}, bf16[8,32,384]{2,1,0:T(8,128)(2,1)S(1)}, u32[]{:S(2)}, u32[]{:S(2)}) %collective-permute-start.11) | collective-permute-done | bytes 196640 | tf_op jit(solution)/shard_map/ppermute | solution.py:451
  80.0 0.0 collective-permute-start.12
  80.0 0.0 collective-permute-done.10.g1_hbm
  80.0 0.0 copy-start.3
  80.0 1.4 %collective-permute-done.12.g3_hbm = bf16[8,32,384]{2,1,0:T(8,128)(2,1)S(1)} collective-permute-done((bf16[8,32,384]{2,1,0:T(8,128)(2,1)S(1)}, bf16[8,32,384]{2,1,0:T(8,128)(2,1)S(1)}, u32[]{:S(2)}, u32[]{:S(2)}) %collective-permute-start.12) | collective-permute-done | bytes 196640 | tf_op jit(solution)/shard_map/ppermute | solution.py:451
  81.4 0.0 copy-done.1
  81.4 0.0 copy-done.2
  81.4 0.0 copy-done.3
  81.5 0.0 copy-start.4
  81.5 0.7 copy-done.4
  82.1 4.1 %shard_map.94 = (f32[1024,256]{1,0:T(8,128)}, f32[1024,256]{1,0:T(8,128)}) custom-call(bf16[8,32,384]{2,1,0:T(8,128)(2,1)} %copy-done.1, bf16[8,32,384]{2,1,0:T(8,128)(2,1)} %copy-done.3, bf16[8,32,384]{2,1,0:T(8,128)(2,1)} %copy-done.2, bf16[8,32,384]{2,1,0:T(8,128)(2,1)} %copy-done.4, s32[2,768]{1,0:T(2,128)} %shard_map.93.slots_hbm, f32[1024,256]{1,0:T(8,128)} %w_hbm.3, ...), custom_call_target="tpu_custom_call" | custom-call | bytes 4986880 | tf_op jit(solution)/shard_map/pallas_call | solution.py:436
  (5 shorter events, 0.0 us)
Async XLA Ops:
  2.9 11.7 %collective-permute-start.4 = (bf16[384,128]{1,0:T(8,128)(2,1)}, bf16[384,128]{1,0:T(8,128)(2,1)S(1)}, u32[]{:S(2)}, u32[]{:S(2)}) collective-permute-start(bf16[384,128]{1,0:T(8,128)(2,1)} %shard_map.86.refs_0_), channel_id=1, source_target_pairs={{0,6},{1,7},{2,4},{3,5},{4,2},{5,3},{6,0},{7,1},{8,14},{9,15},{10,... | collective-permute-start | bytes 294920 | tf_op jit(solution)/shard_map/ppermute | solution.py:451
  8.0 8.5 %collective-permute-start.3 = (bf16[384,128]{1,0:T(8,128)(2,1)}, bf16[384,128]{1,0:T(8,128)(2,1)S(1)}, u32[]{:S(2)}, u32[]{:S(2)}) collective-permute-start(bf16[384,128]{1,0:T(8,128)(2,1)} %shard_map.86.refs_0_), channel_id=1, source_target_pairs={{0,4},{1,5},{2,6},{3,7},{4,0},{5,1},{6,2},{7,3},{8,12},{9,13},{10,... | collective-permute-start | bytes 294920 | tf_op jit(solution)/shard_map/ppermute | solution.py:451
  8.0 10.0 %collective-permute-start.1 = (bf16[384,128]{1,0:T(8,128)(2,1)}, bf16[384,128]{1,0:T(8,128)(2,1)S(1)}, u32[]{:S(2)}, u32[]{:S(2)}) collective-permute-start(bf16[384,128]{1,0:T(8,128)(2,1)} %shard_map.86.refs_0_), channel_id=1, source_target_pairs={{0,2},{1,3},{2,0},{3,1},{4,6},{5,7},{6,4},{7,5},{8,10},{9,11},{10,... | collective-permute-start | bytes 294920 | tf_op jit(solution)/shard_map/ppermute | solution.py:451
  8.6 14.2 %collective-permute-start = (bf16[384,128]{1,0:T(8,128)(2,1)}, bf16[384,128]{1,0:T(8,128)(2,1)S(1)}, u32[]{:S(2)}, u32[]{:S(2)}) collective-permute-start(bf16[384,128]{1,0:T(8,128)(2,1)} %shard_map.86.refs_0_), channel_id=1, source_target_pairs={{0,1},{1,0},{2,3},{3,2},{4,5},{5,4},{6,7},{7,6},{8,9},{9,8},{10,11... | collective-permute-start | bytes 294920 | tf_op jit(solution)/shard_map/ppermute | solution.py:451
  14.6 10.2 %copy-start.5 = (bf16[384,128]{1,0:T(8,128)(2,1)}, bf16[384,128]{1,0:T(8,128)(2,1)S(1)}, u32[]{:S(2)}) copy-start(bf16[384,128]{1,0:T(8,128)(2,1)S(1)} %collective-permute-done.4.refs_6_) | copy-start | bytes 294916
  16.5 8.3 %copy-start.6 = (bf16[384,128]{1,0:T(8,128)(2,1)}, bf16[384,128]{1,0:T(8,128)(2,1)S(1)}, u32[]{:S(2)}) copy-start(bf16[384,128]{1,0:T(8,128)(2,1)S(1)} %collective-permute-done.3.refs_4_) | copy-start | bytes 294916
  16.5 7.2 %collective-permute-start.5 = (bf16[384,128]{1,0:T(8,128)(2,1)S(1)}, bf16[384,128]{1,0:T(8,128)(2,1)S(1)}, u32[]{:S(2)}, u32[]{:S(2)}) collective-permute-start(bf16[384,128]{1,0:T(8,128)(2,1)S(1)} %collective-permute-done.3.refs_4_), channel_id=1, source_target_pairs={{0,1},{1,0},{2,3},{3,2},{4,5},{5,4},{6,7},{7,6},{8,9},{9,8},{10,11... | collective-permute-start | bytes 294920 | tf_op jit(solution)/shard_map/ppermute | solution.py:451
  18.0 6.8 %copy-start.7 = (bf16[384,128]{1,0:T(8,128)(2,1)}, bf16[384,128]{1,0:T(8,128)(2,1)S(1)}, u32[]{:S(2)}) copy-start(bf16[384,128]{1,0:T(8,128)(2,1)S(1)} %collective-permute-done.1.refs_2_) | copy-start | bytes 294916
  18.0 5.7 %collective-permute-start.2 = (bf16[384,128]{1,0:T(8,128)(2,1)S(1)}, bf16[384,128]{1,0:T(8,128)(2,1)S(1)}, u32[]{:S(2)}, u32[]{:S(2)}) collective-permute-start(bf16[384,128]{1,0:T(8,128)(2,1)S(1)} %collective-permute-done.1.refs_2_), channel_id=1, source_target_pairs={{0,1},{1,0},{2,3},{3,2},{4,5},{5,4},{6,7},{7,6},{8,9},{9,8},{10,11... | collective-permute-start | bytes 294920 | tf_op jit(solution)/shard_map/ppermute | solution.py:451
  18.5 6.3 %collective-permute-start.6 = (bf16[384,128]{1,0:T(8,128)(2,1)S(1)}, bf16[384,128]{1,0:T(8,128)(2,1)S(1)}, u32[]{:S(2)}, u32[]{:S(2)}) collective-permute-start(bf16[384,128]{1,0:T(8,128)(2,1)S(1)} %collective-permute-done.4.refs_6_), channel_id=1, source_target_pairs={{0,1},{1,0},{2,3},{3,2},{4,5},{5,4},{6,7},{7,6},{8,9},{9,8},{10,11... | collective-permute-start | bytes 294920 | tf_op jit(solution)/shard_map/ppermute | solution.py:451
  22.8 2.0 %copy-start.8 = (bf16[384,128]{1,0:T(8,128)(2,1)}, bf16[384,128]{1,0:T(8,128)(2,1)S(1)}, u32[]{:S(2)}) copy-start(bf16[384,128]{1,0:T(8,128)(2,1)S(1)} %collective-permute-done.refs_1_) | copy-start | bytes 294916
  23.7 1.1 %copy-start.10 = (bf16[384,128]{1,0:T(8,128)(2,1)}, bf16[384,128]{1,0:T(8,128)(2,1)S(1)}, u32[]{:S(2)}) copy-start(bf16[384,128]{1,0:T(8,128)(2,1)S(1)} %collective-permute-done.2.refs_3_) | copy-start | bytes 294916
  23.7 1.1 %copy-start.9 = (bf16[384,128]{1,0:T(8,128)(2,1)}, bf16[384,128]{1,0:T(8,128)(2,1)S(1)}, u32[]{:S(2)}) copy-start(bf16[384,128]{1,0:T(8,128)(2,1)S(1)} %collective-permute-done.5.refs_5_) | copy-start | bytes 294916
  24.8 0.6 copy-start.11
  27.7 7.1 %collective-permute-start.8 = (bf16[2,128,512]{2,1,0:T(8,128)(2,1)}, bf16[2,128,512]{2,1,0:T(8,128)(2,1)S(1)}, u32[]{:S(2)}, u32[]{:S(2)}) collective-permute-start(bf16[2,128,512]{2,1,0:T(8,128)(2,1)} %shard_map.89.block_hbm.b0_hbm), channel_id=1, source_target_pairs={{0,16},{8,24},{16,0},{24,8},{1,17},{9,25},{17,1},{25,9},{2,18},{10... | collective-permute-start | bytes 786440 | tf_op jit(solution)/shard_map/ppermute | solution.py:451
  29.2 5.6 %collective-permute-start.7 = (bf16[2,128,512]{2,1,0:T(8,128)(2,1)}, bf16[2,128,512]{2,1,0:T(8,128)(2,1)S(1)}, u32[]{:S(2)}, u32[]{:S(2)}) collective-permute-start(bf16[2,128,512]{2,1,0:T(8,128)(2,1)} %shard_map.89.block_hbm.b0_hbm), channel_id=1, source_target_pairs={{0,8},{8,0},{16,24},{24,16},{1,9},{9,1},{17,25},{25,17},{2,10},{10... | collective-permute-start | bytes 786440 | tf_op jit(solution)/shard_map/ppermute | solution.py:451
  34.8 5.5 %copy-start.12 = (bf16[2,128,512]{2,1,0:T(8,128)(2,1)}, bf16[2,128,512]{2,1,0:T(8,128)(2,1)S(1)}, u32[]{:S(2)}) copy-start(bf16[2,128,512]{2,1,0:T(8,128)(2,1)S(1)} %collective-permute-done.8.b2_hbm) | copy-start | bytes 786436
  34.8 5.5 %copy-start.13 = (bf16[2,128,512]{2,1,0:T(8,128)(2,1)}, bf16[2,128,512]{2,1,0:T(8,128)(2,1)S(1)}, u32[]{:S(2)}) copy-start(bf16[2,128,512]{2,1,0:T(8,128)(2,1)S(1)} %collective-permute-done.7.b1_hbm) | copy-start | bytes 786436
  34.8 20.0 %all-to-all-start = ((bf16[32,32,256]{2,1,0:T(8,128)(2,1)}), bf16[32,32,256]{2,1,0:T(8,128)(2,1)S(1)}, u32[]{:S(2)}, u32[]{:S(2)}) async-start(bf16[32,32,256]{2,1,0:T(8,128)(2,1)} %shard_map.90), calls=%async_computation | async-start | bytes 1048576 | tf_op jit(solution)/shard_map/all_to_all | solution.py:537
  38.7 1.6 %collective-permute-start.9 = (bf16[2,128,512]{2,1,0:T(8,128)(2,1)S(1)}, bf16[2,128,512]{2,1,0:T(8,128)(2,1)S(1)}, u32[]{:S(2)}, u32[]{:S(2)}) collective-permute-start(bf16[2,128,512]{2,1,0:T(8,128)(2,1)S(1)} %collective-permute-done.8.b2_hbm), channel_id=1, source_target_pairs={{0,8},{8,0},{16,24},{24,16},{1,9},{9,1},{17,25},{25,17},{2,10},{10... | collective-permute-start | bytes 786440 | tf_op jit(solution)/shard_map/ppermute | solution.py:451
  40.3 0.7 copy-start.14
  54.8 0.8 copy-start
  62.8 11.6 %all-to-all-start.1 = ((bf16[8,32,384]{2,1,0:T(8,128)(2,1)}), bf16[8,32,384]{2,1,0:T(8,128)(2,1)S(1)}, u32[]{:S(2)}, u32[]{:S(2)}) async-start(bf16[8,32,384]{2,1,0:T(8,128)(2,1)} %shard_map.92), calls=%async_computation.1 | async-start | bytes 393216 | tf_op jit(solution)/shard_map/all_to_all | solution.py:582
  74.3 7.1 %copy-start.1 = (bf16[8,32,384]{2,1,0:T(8,128)(2,1)}, bf16[8,32,384]{2,1,0:T(8,128)(2,1)S(1)}, u32[]{:S(2)}) copy-start(bf16[8,32,384]{2,1,0:T(8,128)(2,1)S(1)} %all-to-all-done.1.g0_hbm) | copy-start | bytes 589828
  74.3 5.7 %collective-permute-start.11 = (bf16[8,32,384]{2,1,0:T(8,128)(2,1)S(1)}, bf16[8,32,384]{2,1,0:T(8,128)(2,1)S(1)}, u32[]{:S(2)}, u32[]{:S(2)}) collective-permute-start(bf16[8,32,384]{2,1,0:T(8,128)(2,1)S(1)} %all-to-all-done.1.g0_hbm), channel_id=1, source_target_pairs={{0,16},{8,24},{16,0},{24,8},{1,17},{9,25},{17,1},{25,9},{2,18},{10... | collective-permute-start | bytes 589832 | tf_op jit(solution)/shard_map/ppermute | solution.py:451
  75.8 4.2 %collective-permute-start.10 = (bf16[8,32,384]{2,1,0:T(8,128)(2,1)S(1)}, bf16[8,32,384]{2,1,0:T(8,128)(2,1)S(1)}, u32[]{:S(2)}, u32[]{:S(2)}) collective-permute-start(bf16[8,32,384]{2,1,0:T(8,128)(2,1)S(1)} %all-to-all-done.1.g0_hbm), channel_id=1, source_target_pairs={{0,8},{8,0},{16,24},{24,16},{1,9},{9,1},{17,25},{25,17},{2,10},{10... | collective-permute-start | bytes 589832 | tf_op jit(solution)/shard_map/ppermute | solution.py:451
  80.0 1.4 %copy-start.2 = (bf16[8,32,384]{2,1,0:T(8,128)(2,1)}, bf16[8,32,384]{2,1,0:T(8,128)(2,1)S(1)}, u32[]{:S(2)}) copy-start(bf16[8,32,384]{2,1,0:T(8,128)(2,1)S(1)} %collective-permute-done.11.g2_hbm) | copy-start | bytes 589828
  80.0 1.4 %collective-permute-start.12 = (bf16[8,32,384]{2,1,0:T(8,128)(2,1)S(1)}, bf16[8,32,384]{2,1,0:T(8,128)(2,1)S(1)}, u32[]{:S(2)}, u32[]{:S(2)}) collective-permute-start(bf16[8,32,384]{2,1,0:T(8,128)(2,1)S(1)} %collective-permute-done.11.g2_hbm), channel_id=1, source_target_pairs={{0,8},{8,0},{16,24},{24,16},{1,9},{9,1},{17,25},{25,17},{2,10},{10... | collective-permute-start | bytes 589832 | tf_op jit(solution)/shard_map/ppermute | solution.py:451
  80.0 1.4 %copy-start.3 = (bf16[8,32,384]{2,1,0:T(8,128)(2,1)}, bf16[8,32,384]{2,1,0:T(8,128)(2,1)S(1)}, u32[]{:S(2)}) copy-start(bf16[8,32,384]{2,1,0:T(8,128)(2,1)S(1)} %collective-permute-done.10.g1_hbm) | copy-start | bytes 589828
  81.5 0.7 copy-start.4

commit v18 on v17

--- a/solution.py
+++ b/solution.py
@@ -234,7 +234,7 @@
 
 
 def exponent(left, right):
-    return mm(left, right, 1, 0) * (7.0 / (left.shape[1] // 2) * math.log2(math.e))
+    return mm(left, right, 1, 0) * (7.0 / (left.shape[1] // 2))
 
 
 CHUNK = 256
@@ -268,7 +268,7 @@
     left = extended(feats[...], 1, True)
     for u in range(UPDATES):
         right = extended(block[u], 0, False)
-        tile[...] = jnp.exp2(exponent(left, right)).astype(bf16)
+        tile[...] = jnp.exp(exponent(left, right)).astype(bf16)
         if u == 0:
             wait_all(reads[2:])
         total = offset[u] + mm(coef[u], tile[...], 1, 0)
@@ -304,7 +304,7 @@
         left = extended(chosen_feats, 1, True)
         for k in range(groups):
             start = pl.multiple_of(places[k] * count, count)
-            value = jnp.exp2(exponent(left, rights[u][k]))
+            value = jnp.exp(exponent(left, rights[u][k]))
             factor[u, :, pl.ds(start, count)] = value.astype(bf16)
     writes = start_all([(factor, factor_hbm)], sems)
     lefts, left_points = [], []
@@ -317,8 +317,8 @@
     for m in range(groups):
         right_points = ids[pl.ds(groups + places[m], 1), :].astype(f32)
         power = exponent(left, rights[1][m])
-        power = jnp.where(left_points == right_points, math.log2(1.0 + ridge_term), power)
-        cross[m] = jnp.exp2(power).astype(bf16).reshape(groups, count, count)
+        power = jnp.where(left_points == right_points, math.log(1.0 + ridge_term), power)
+        cross[m] = jnp.exp(power).astype(bf16).reshape(groups, count, count)
         for k in range(groups):
             start = pl.multiple_of(places[k] * count, count)
             copy = pltpu.make_async_copy(
@@ -475,13 +475,14 @@
     )
     came = {k: swap(packed, "pts", k) for k in reversed(range(2, owners, 2))}
     came[1] = swap(packed, "pts", 1)
+    came[2], first_index = lax.optimization_barrier((came[2], block_index))
     came[3] = swap(came[2], "pts", 1)
     kept = [
         like((UPDATES, outputs, points)),
         like((UPDATES, outputs, count), f32),
         like((8, 128), i32),
     ]
-    given = [block_index, coefficients, momentum, targets]
+    given = [first_index, coefficients, momentum, targets]
     coef, offset, row_starts = call(
         functools.partial(prepare_kernel, count, owners),
         kept,

time: 87.1 us -> 87 us (level)
  starting transfers between devices: 21.6 us -> 20.5 us
    ppermute x13, starting transfers between devices: 14.1 us -> 13 us  [swap(): lax.ppermute(value, axis, [(i, i ^ k) for i in range(lax.axis_size(axis))])]
  transfers between devices with their start and end apart: 15 -> 15, of which waited for: 9 -> 9; matrix products, arithmetic and copies ran while one was open for 0% -> 0% of each run, Pallas kernels for 30% -> 31%
where the time goes in v18:
time: 87 us; the launch traced here: 86.3 us
  Pallas kernels  42.1 us (48%)
  starting transfers between devices  20.5 us (24%)
  waiting for transfers between devices  19.9 us (23%)
  local copies, waits for them, and re-layouts  2.82 us (3%)
  between operations  1.02 us (1%)
    pallas_call x9, Pallas kernels, call(): pl.pallas_call(body, out_shape=outs, in_specs=[VMEM] * near + [HBM] * (le...  42.1 us
    ppermute x13, waiting for transfers between devices, swap(): lax.ppermute(value, axis, [(i, i ^ k) for i in range(lax.axis_size(axis))])  13.7 us
    ppermute x13, starting transfers between devices, swap(): lax.ppermute(value, axis, [(i, i ^ k) for i in range(lax.axis_size(axis))])  13 us
    all_to_all x1, waiting for transfers between devices, with_kernels(): got = lax.all_to_all(steps, 'pts', 0, 0, tiled=True)  4.08 us
    all_to_all x1, starting transfers between devices, with_kernels(): summed = lax.all_to_all(pieces, ('rows', 'pts'), 0, 0, tiled=True)  3.84 us
    all_to_all x1, starting transfers between devices, with_kernels(): got = lax.all_to_all(steps, 'pts', 0, 0, tiled=True)  3.62 us
    unnamed x30, local copies, waits for them, and re-layouts  2.82 us
    all_to_all x1, waiting for transfers between devices, with_kernels(): summed = lax.all_to_all(pieces, ('rows', 'pts'), 0, 0, tiled=True)  2.15 us
  transfers between devices with their start and end apart: 15, of which 9 were waited for; matrix products, arithmetic and copies ran while one was open for 0% of the time, Pallas kernels for 31%

profile of v18, /device:TPU:0, one launch (start us, length us, event | category | flops | bytes accessed | tf_op | source)
XLA Modules:
  0.0 86.3 jit_solution(7754639703835305467)
XLA Ops:
  0.6 2.2 %shard_map.86.refs_0_ = bf16[384,128]{1,0:T(8,128)(2,1)} custom-call(s32[2,2048]{1,0:T(2,128)} %blocks_hbm.4, bf16[1024,128]{1,0:T(8,128)(2,1)} %feats_hbm.3), custom_call_target="tpu_custom_call" | custom-call | bytes 376832 | tf_op jit(solution)/shard_map/pallas_call | solution.py:436
  2.9 3.1 %collective-permute-start.1 = (bf16[384,128]{1,0:T(8,128)(2,1)}, bf16[384,128]{1,0:T(8,128)(2,1)S(1)}, u32[]{:S(2)}, u32[]{:S(2)}) collective-permute-start(bf16[384,128]{1,0:T(8,128)(2,1)} %shard_map.86.refs_0_), channel_id=1, source_target_pairs={{0,2},{1,3},{2,0},{3,1},{4,6},{5,7},{6,4},{7,5},{8,10},{9,11},{10,... | collective-permute-start | bytes 294920 | tf_op jit(solution)/shard_map/ppermute | solution.py:451
  6.0 2.5 %collective-permute-start.4 = (bf16[384,128]{1,0:T(8,128)(2,1)}, bf16[384,128]{1,0:T(8,128)(2,1)S(1)}, u32[]{:S(2)}, u32[]{:S(2)}) collective-permute-start(bf16[384,128]{1,0:T(8,128)(2,1)} %shard_map.86.refs_0_), channel_id=1, source_target_pairs={{0,6},{1,7},{2,4},{3,5},{4,2},{5,3},{6,0},{7,1},{8,14},{9,15},{10,... | collective-permute-start | bytes 294920 | tf_op jit(solution)/shard_map/ppermute | solution.py:451
  8.4 0.1 collective-permute-start.3
  8.6 1.5 %collective-permute-start = (bf16[384,128]{1,0:T(8,128)(2,1)}, bf16[384,128]{1,0:T(8,128)(2,1)S(1)}, u32[]{:S(2)}, u32[]{:S(2)}) collective-permute-start(bf16[384,128]{1,0:T(8,128)(2,1)} %shard_map.86.refs_0_), channel_id=1, source_target_pairs={{0,1},{1,0},{2,3},{3,2},{4,5},{5,4},{6,7},{7,6},{8,9},{9,8},{10,11... | collective-permute-start | bytes 294920 | tf_op jit(solution)/shard_map/ppermute | solution.py:451
  10.1 0.0 collective-permute-done.1.refs_2_
  10.1 0.0 copy-start.5
  10.1 0.7 collective-permute-start.2
  10.7 4.3 %shard_map.87 = (bf16[2,256,1024]{2,1,0:T(8,128)(2,1)}, f32[2,256,512]{2,1,0:T(8,128)}, s32[8,128]{1,0:T(8,128)}) custom-call(s32[2,2048]{1,0:T(2,128)} %blocks_hbm.4, f32[1024,256]{1,0:T(8,128)} %w_hbm.3, f32[1024,256]{1,0:T(8,128)} %z_hbm.3, bf16[1024,256]{1,0:T(8,128)(2,1)} %t_hbm.1), custom_call_target="tpu_custom_call" | custom-call | bytes 4739072 | tf_op jit(solution)/shard_map/pallas_call | solution.py:436
  15.0 0.0 collective-permute-done.4.refs_6_
  15.0 0.0 copy-start.6
  15.0 2.6 %collective-permute-done.3.refs_4_ = bf16[384,128]{1,0:T(8,128)(2,1)S(1)} collective-permute-done((bf16[384,128]{1,0:T(8,128)(2,1)}, bf16[384,128]{1,0:T(8,128)(2,1)S(1)}, u32[]{:S(2)}, u32[]{:S(2)}) %collective-permute-start.3) | collective-permute-done | bytes 98336 | tf_op jit(solution)/shard_map/ppermute | solution.py:451
  17.6 0.0 copy-start.7
  17.6 1.5 %collective-permute-start.5 = (bf16[384,128]{1,0:T(8,128)(2,1)S(1)}, bf16[384,128]{1,0:T(8,128)(2,1)S(1)}, u32[]{:S(2)}, u32[]{:S(2)}) collective-permute-start(bf16[384,128]{1,0:T(8,128)(2,1)S(1)} %collective-permute-done.3.refs_4_), channel_id=1, source_target_pairs={{0,1},{1,0},{2,3},{3,2},{4,5},{5,4},{6,7},{7,6},{8,9},{9,8},{10,11... | collective-permute-start | bytes 294920 | tf_op jit(solution)/shard_map/ppermute | solution.py:451
  19.2 0.5 collective-permute-start.6
  19.7 2.8 %shard_map.88 = (s32[8,512]{1,0:T(8,128)}, s32[8,512]{1,0:T(8,128)}, s32[8,128]{1,0:T(8,128)}) custom-call(s32[2,2048]{1,0:T(2,128)} %blocks_hbm.4), custom_call_target="tpu_custom_call" | custom-call | bytes 53248 | tf_op jit(solution)/shard_map/pallas_call | solution.py:436
  22.4 0.0 collective-permute-done.refs_1_
  22.5 0.0 copy-start.8
  22.5 0.0 collective-permute-done.2.refs_3_
  22.5 0.0 copy-start.9
  22.5 0.6 collective-permute-done.5.refs_5_
  23.1 0.0 copy-start.10
  23.1 1.1 %collective-permute-done.6.refs_7_ = bf16[384,128]{1,0:T(8,128)(2,1)S(1)} collective-permute-done((bf16[384,128]{1,0:T(8,128)(2,1)S(1)}, bf16[384,128]{1,0:T(8,128)(2,1)S(1)}, u32[]{:S(2)}, u32[]{:S(2)}) %collective-permute-start.6) | collective-permute-done | bytes 98336 | tf_op jit(solution)/shard_map/ppermute | solution.py:451
  24.2 0.0 copy-done.5
  24.2 0.0 copy-done.6
  24.2 0.0 copy-done.7
  24.2 0.0 copy-done.8
  24.2 0.0 copy-done.9
  24.2 0.0 copy-done.10
  24.2 0.0 copy-start.11
  24.2 0.6 copy-done.11
  24.9 2.3 %shard_map.89.block_hbm.b0_hbm = bf16[2,128,512]{2,1,0:T(8,128)(2,1)} custom-call(bf16[384,128]{1,0:T(8,128)(2,1)} %shard_map.86.refs_0_, bf16[384,128]{1,0:T(8,128)(2,1)} %copy-done.8, bf16[384,128]{1,0:T(8,128)(2,1)} %copy-done.5, bf16[384,128]{1,0:T(8,128)(2,1)} %copy-done.9, bf16[384,128]{1,0:T(8,128)(2,1)} %copy-done.7, bf16[384,128]{1,0:T(8,128)(2,1)} %copy-done.10, ...), custom_call_target="tpu_custom_call" | custom-call | bytes 1052672 | tf_op jit(solution)/shard_map/pallas_call | solution.py:436
  27.1 1.6 %collective-permute-start.8 = (bf16[2,128,512]{2,1,0:T(8,128)(2,1)}, bf16[2,128,512]{2,1,0:T(8,128)(2,1)S(1)}, u32[]{:S(2)}, u32[]{:S(2)}) collective-permute-start(bf16[2,128,512]{2,1,0:T(8,128)(2,1)} %shard_map.89.block_hbm.b0_hbm), channel_id=1, source_target_pairs={{0,16},{8,24},{16,0},{24,8},{1,17},{9,25},{17,1},{25,9},{2,18},{10... | collective-permute-start | bytes 786440 | tf_op jit(solution)/shard_map/ppermute | solution.py:451
  28.7 0.0 collective-permute-start.7
  28.7 3.6 %shard_map.90 = bf16[32,32,256]{2,1,0:T(8,128)(2,1)} custom-call(bf16[2,128,512]{2,1,0:T(8,128)(2,1)} %shard_map.89.block_hbm.b0_hbm, bf16[1024,128]{1,0:T(8,128)(2,1)} %feats_hbm.3, bf16[2,256,1024]{2,1,0:T(8,128)(2,1)} %get-tuple-element.34.coef_hbm, f32[2,256,512]{2,1,0:T(8,128)} %get-tuple-element.35.offset_hbm), custom_call_target="tpu_custom_call" | custom-call | flops 1073741824 | bytes 3145728 | tf_op jit(solution)/shard_map/pallas_call | solution.py:436
  32.3 2.2 %collective-permute-done.8.b2_hbm = bf16[2,128,512]{2,1,0:T(8,128)(2,1)S(1)} collective-permute-done((bf16[2,128,512]{2,1,0:T(8,128)(2,1)}, bf16[2,128,512]{2,1,0:T(8,128)(2,1)S(1)}, u32[]{:S(2)}, u32[]{:S(2)}) %collective-permute-start.8) | collective-permute-done | bytes 262176 | tf_op jit(solution)/shard_map/ppermute | solution.py:451
  34.5 0.0 copy-start.12
  34.5 0.0 collective-permute-done.7.b1_hbm
  34.5 3.8 %all-to-all-start = ((bf16[32,32,256]{2,1,0:T(8,128)(2,1)}), bf16[32,32,256]{2,1,0:T(8,128)(2,1)S(1)}, u32[]{:S(2)}, u32[]{:S(2)}) async-start(bf16[32,32,256]{2,1,0:T(8,128)(2,1)} %shard_map.90), calls=%async_computation | async-start | bytes 1048576 | tf_op jit(solution)/shard_map/all_to_all | solution.py:538
  38.4 0.1 collective-permute-start.9
  38.5 1.5 %collective-permute-done.9.b3_hbm = bf16[2,128,512]{2,1,0:T(8,128)(2,1)S(1)} collective-permute-done((bf16[2,128,512]{2,1,0:T(8,128)(2,1)S(1)}, bf16[2,128,512]{2,1,0:T(8,128)(2,1)S(1)}, u32[]{:S(2)}, u32[]{:S(2)}) %collective-permute-start.9) | collective-permute-done | bytes 262176 | tf_op jit(solution)/shard_map/ppermute | solution.py:451
  40.0 0.0 copy-done.12
  40.0 0.0 copy-done.13
  40.0 0.7 copy-done.14
  40.7 11.7 %shard_map.91 = (bf16[2,512,2048]{2,1,0:T(8,128)(2,1)}, bf16[4,2048,512]{2,1,0:T(8,128)(2,1)}) custom-call(bf16[2,128,512]{2,1,0:T(8,128)(2,1)} %shard_map.89.block_hbm.b0_hbm, bf16[2,128,512]{2,1,0:T(8,128)(2,1)} %copy-done.13, bf16[2,128,512]{2,1,0:T(8,128)(2,1)} %copy-done.12, bf16[2,128,512]{2,1,0:T(8,128)(2,1)} %copy-done.14, ...), custom_call_target="tpu_custom_call" | custom-call | flops 1610612736 | bytes 13668352 | tf_op jit(solution)/shard_map/pallas_call | solution.py:436
  52.4 2.1 %all-to-all-done.summed_hbm = bf16[32,32,256]{2,1,0:T(8,128)(2,1)S(1)} async-done(((bf16[32,32,256]{2,1,0:T(8,128)(2,1)}), bf16[32,32,256]{2,1,0:T(8,128)(2,1)S(1)}, u32[]{:S(2)}, u32[]{:S(2)}) %all-to-all-start) | async-done | bytes 524320 | tf_op jit(solution)/shard_map/all_to_all | solution.py:538
  54.5 0.8 copy-done
  55.3 7.1 %shard_map.92 = bf16[8,32,384]{2,1,0:T(8,128)(2,1)} custom-call(bf16[32,32,256]{2,1,0:T(8,128)(2,1)} %copy-done, bf16[2,512,2048]{2,1,0:T(8,128)(2,1)} %get-tuple-element.41.factor_hbm, bf16[2,512,512]{2,1,0:T(8,128)(2,1)} %core_hbm.1, bf16[4,2048,512]{2,1,0:T(8,128)(2,1)} %get-tuple-element.42.cross_hbm, s32[8,128]{1,0:T(8,128)} %get-tuple-element.43.starts_hbm), custom_call_target="tpu_custom_call" | custom-call | bytes 14356480 | tf_op jit(solution)/shard_map/pallas_call | solution.py:436
  62.5 3.6 %all-to-all-start.1 = ((bf16[8,32,384]{2,1,0:T(8,128)(2,1)}), bf16[8,32,384]{2,1,0:T(8,128)(2,1)S(1)}, u32[]{:S(2)}, u32[]{:S(2)}) async-start(bf16[8,32,384]{2,1,0:T(8,128)(2,1)} %shard_map.92), calls=%async_computation.1 | async-start | bytes 393216 | tf_op jit(solution)/shard_map/all_to_all | solution.py:583
  66.1 4.1 %shard_map.93.slots_hbm = s32[2,768]{1,0:T(2,128)} custom-call(s32[2,2048]{1,0:T(2,128)} %blocks_hbm.4), custom_call_target="tpu_custom_call" | custom-call | bytes 22528 | tf_op jit(solution)/shard_map/pallas_call | solution.py:436
  70.2 4.1 %all-to-all-done.1.g0_hbm = bf16[8,32,384]{2,1,0:T(8,128)(2,1)S(1)} async-done(((bf16[8,32,384]{2,1,0:T(8,128)(2,1)}), bf16[8,32,384]{2,1,0:T(8,128)(2,1)S(1)}, u32[]{:S(2)}, u32[]{:S(2)}) %all-to-all-start.1) | async-done | bytes 196640 | tf_op jit(solution)/shard_map/all_to_all | solution.py:583
  74.2 1.4 %collective-permute-start.11 = (bf16[8,32,384]{2,1,0:T(8,128)(2,1)S(1)}, bf16[8,32,384]{2,1,0:T(8,128)(2,1)S(1)}, u32[]{:S(2)}, u32[]{:S(2)}) collective-permute-start(bf16[8,32,384]{2,1,0:T(8,128)(2,1)S(1)} %all-to-all-done.1.g0_hbm), channel_id=1, source_target_pairs={{0,16},{8,24},{16,0},{24,8},{1,17},{9,25},{17,1},{25,9},{2,18},{10... | collective-permute-start | bytes 589832 | tf_op jit(solution)/shard_map/ppermute | solution.py:451
  75.7 0.0 collective-permute-start.10
  75.7 4.2 %collective-permute-done.11.g2_hbm = bf16[8,32,384]{2,1,0:T(8,128)(2,1)S(1)} collective-permute-done((bf16[8,32,384]{2,1,0:T(8,128)(2,1)S(1)}, bf16[8,32,384]{2,1,0:T(8,128)(2,1)S(1)}, u32[]{:S(2)}, u32[]{:S(2)}) %collective-permute-start.11) | collective-permute-done | bytes 196640 | tf_op jit(solution)/shard_map/ppermute | solution.py:451
  79.9 0.0 collective-permute-start.12
  79.9 0.0 collective-permute-done.10.g1_hbm
  79.9 0.0 copy-start.3
  79.9 1.4 %collective-permute-done.12.g3_hbm = bf16[8,32,384]{2,1,0:T(8,128)(2,1)S(1)} collective-permute-done((bf16[8,32,384]{2,1,0:T(8,128)(2,1)S(1)}, bf16[8,32,384]{2,1,0:T(8,128)(2,1)S(1)}, u32[]{:S(2)}, u32[]{:S(2)}) %collective-permute-start.12) | collective-permute-done | bytes 196640 | tf_op jit(solution)/shard_map/ppermute | solution.py:451
  81.4 0.0 copy-done.1
  81.4 0.0 copy-done.2
  81.4 0.0 copy-done.3
  81.4 0.0 copy-start.4
  81.4 0.7 copy-done.4
  82.0 4.1 %shard_map.94 = (f32[1024,256]{1,0:T(8,128)}, f32[1024,256]{1,0:T(8,128)}) custom-call(bf16[8,32,384]{2,1,0:T(8,128)(2,1)} %copy-done.1, bf16[8,32,384]{2,1,0:T(8,128)(2,1)} %copy-done.3, bf16[8,32,384]{2,1,0:T(8,128)(2,1)} %copy-done.2, bf16[8,32,384]{2,1,0:T(8,128)(2,1)} %copy-done.4, s32[2,768]{1,0:T(2,128)} %shard_map.93.slots_hbm, f32[1024,256]{1,0:T(8,128)} %w_hbm.3, ...), custom_call_target="tpu_custom_call" | custom-call | bytes 4986880 | tf_op jit(solution)/shard_map/pallas_call | solution.py:436
  (5 shorter events, 0.0 us)
Async XLA Ops:
  2.9 7.2 %collective-permute-start.1 = (bf16[384,128]{1,0:T(8,128)(2,1)}, bf16[384,128]{1,0:T(8,128)(2,1)S(1)}, u32[]{:S(2)}, u32[]{:S(2)}) collective-permute-start(bf16[384,128]{1,0:T(8,128)(2,1)} %shard_map.86.refs_0_), channel_id=1, source_target_pairs={{0,2},{1,3},{2,0},{3,1},{4,6},{5,7},{6,4},{7,5},{8,10},{9,11},{10,... | collective-permute-start | bytes 294920 | tf_op jit(solution)/shard_map/ppermute | solution.py:451
  6.0 9.0 %collective-permute-start.4 = (bf16[384,128]{1,0:T(8,128)(2,1)}, bf16[384,128]{1,0:T(8,128)(2,1)S(1)}, u32[]{:S(2)}, u32[]{:S(2)}) collective-permute-start(bf16[384,128]{1,0:T(8,128)(2,1)} %shard_map.86.refs_0_), channel_id=1, source_target_pairs={{0,6},{1,7},{2,4},{3,5},{4,2},{5,3},{6,0},{7,1},{8,14},{9,15},{10,... | collective-permute-start | bytes 294920 | tf_op jit(solution)/shard_map/ppermute | solution.py:451
  8.4 9.2 %collective-permute-start.3 = (bf16[384,128]{1,0:T(8,128)(2,1)}, bf16[384,128]{1,0:T(8,128)(2,1)S(1)}, u32[]{:S(2)}, u32[]{:S(2)}) collective-permute-start(bf16[384,128]{1,0:T(8,128)(2,1)} %shard_map.86.refs_0_), channel_id=1, source_target_pairs={{0,4},{1,5},{2,6},{3,7},{4,0},{5,1},{6,2},{7,3},{8,12},{9,13},{10,... | collective-permute-start | bytes 294920 | tf_op jit(solution)/shard_map/ppermute | solution.py:451
  8.6 13.9 %collective-permute-start = (bf16[384,128]{1,0:T(8,128)(2,1)}, bf16[384,128]{1,0:T(8,128)(2,1)S(1)}, u32[]{:S(2)}, u32[]{:S(2)}) collective-permute-start(bf16[384,128]{1,0:T(8,128)(2,1)} %shard_map.86.refs_0_), channel_id=1, source_target_pairs={{0,1},{1,0},{2,3},{3,2},{4,5},{5,4},{6,7},{7,6},{8,9},{9,8},{10,11... | collective-permute-start | bytes 294920 | tf_op jit(solution)/shard_map/ppermute | solution.py:451
  10.1 14.1 %copy-start.5 = (bf16[384,128]{1,0:T(8,128)(2,1)}, bf16[384,128]{1,0:T(8,128)(2,1)S(1)}, u32[]{:S(2)}) copy-start(bf16[384,128]{1,0:T(8,128)(2,1)S(1)} %collective-permute-done.1.refs_2_) | copy-start | bytes 294916
  10.1 12.4 %collective-permute-start.2 = (bf16[384,128]{1,0:T(8,128)(2,1)S(1)}, bf16[384,128]{1,0:T(8,128)(2,1)S(1)}, u32[]{:S(2)}, u32[]{:S(2)}) collective-permute-start(bf16[384,128]{1,0:T(8,128)(2,1)S(1)} %collective-permute-done.1.refs_2_), channel_id=1, source_target_pairs={{0,1},{1,0},{2,3},{3,2},{4,5},{5,4},{6,7},{7,6},{8,9},{9,8},{10,11... | collective-permute-start | bytes 294920 | tf_op jit(solution)/shard_map/ppermute | solution.py:451
  15.0 9.2 %copy-start.6 = (bf16[384,128]{1,0:T(8,128)(2,1)}, bf16[384,128]{1,0:T(8,128)(2,1)S(1)}, u32[]{:S(2)}) copy-start(bf16[384,128]{1,0:T(8,128)(2,1)S(1)} %collective-permute-done.4.refs_6_) | copy-start | bytes 294916
  17.6 6.6 %copy-start.7 = (bf16[384,128]{1,0:T(8,128)(2,1)}, bf16[384,128]{1,0:T(8,128)(2,1)S(1)}, u32[]{:S(2)}) copy-start(bf16[384,128]{1,0:T(8,128)(2,1)S(1)} %collective-permute-done.3.refs_4_) | copy-start | bytes 294916
  17.6 5.5 %collective-permute-start.5 = (bf16[384,128]{1,0:T(8,128)(2,1)S(1)}, bf16[384,128]{1,0:T(8,128)(2,1)S(1)}, u32[]{:S(2)}, u32[]{:S(2)}) collective-permute-start(bf16[384,128]{1,0:T(8,128)(2,1)S(1)} %collective-permute-done.3.refs_4_), channel_id=1, source_target_pairs={{0,1},{1,0},{2,3},{3,2},{4,5},{5,4},{6,7},{7,6},{8,9},{9,8},{10,11... | collective-permute-start | bytes 294920 | tf_op jit(solution)/shard_map/ppermute | solution.py:451
  19.2 5.0 %collective-permute-start.6 = (bf16[384,128]{1,0:T(8,128)(2,1)S(1)}, bf16[384,128]{1,0:T(8,128)(2,1)S(1)}, u32[]{:S(2)}, u32[]{:S(2)}) collective-permute-start(bf16[384,128]{1,0:T(8,128)(2,1)S(1)} %collective-permute-done.4.refs_6_), channel_id=1, source_target_pairs={{0,1},{1,0},{2,3},{3,2},{4,5},{5,4},{6,7},{7,6},{8,9},{9,8},{10,11... | collective-permute-start | bytes 294920 | tf_op jit(solution)/shard_map/ppermute | solution.py:451
  22.5 1.7 %copy-start.8 = (bf16[384,128]{1,0:T(8,128)(2,1)}, bf16[384,128]{1,0:T(8,128)(2,1)S(1)}, u32[]{:S(2)}) copy-start(bf16[384,128]{1,0:T(8,128)(2,1)S(1)} %collective-permute-done.refs_1_) | copy-start | bytes 294916
  22.5 1.7 %copy-start.9 = (bf16[384,128]{1,0:T(8,128)(2,1)}, bf16[384,128]{1,0:T(8,128)(2,1)S(1)}, u32[]{:S(2)}) copy-start(bf16[384,128]{1,0:T(8,128)(2,1)S(1)} %collective-permute-done.2.refs_3_) | copy-start | bytes 294916
  23.1 1.1 %copy-start.10 = (bf16[384,128]{1,0:T(8,128)(2,1)}, bf16[384,128]{1,0:T(8,128)(2,1)S(1)}, u32[]{:S(2)}) copy-start(bf16[384,128]{1,0:T(8,128)(2,1)S(1)} %collective-permute-done.5.refs_5_) | copy-start | bytes 294916
  24.2 0.6 copy-start.11
  27.1 7.4 %collective-permute-start.8 = (bf16[2,128,512]{2,1,0:T(8,128)(2,1)}, bf16[2,128,512]{2,1,0:T(8,128)(2,1)S(1)}, u32[]{:S(2)}, u32[]{:S(2)}) collective-permute-start(bf16[2,128,512]{2,1,0:T(8,128)(2,1)} %shard_map.89.block_hbm.b0_hbm), channel_id=1, source_target_pairs={{0,16},{8,24},{16,0},{24,8},{1,17},{9,25},{17,1},{25,9},{2,18},{10... | collective-permute-start | bytes 786440 | tf_op jit(solution)/shard_map/ppermute | solution.py:451
  28.7 5.8 %collective-permute-start.7 = (bf16[2,128,512]{2,1,0:T(8,128)(2,1)}, bf16[2,128,512]{2,1,0:T(8,128)(2,1)S(1)}, u32[]{:S(2)}, u32[]{:S(2)}) collective-permute-start(bf16[2,128,512]{2,1,0:T(8,128)(2,1)} %shard_map.89.block_hbm.b0_hbm), channel_id=1, source_target_pairs={{0,8},{8,0},{16,24},{24,16},{1,9},{9,1},{17,25},{25,17},{2,10},{10... | collective-permute-start | bytes 786440 | tf_op jit(solution)/shard_map/ppermute | solution.py:451
  34.5 5.5 %copy-start.12 = (bf16[2,128,512]{2,1,0:T(8,128)(2,1)}, bf16[2,128,512]{2,1,0:T(8,128)(2,1)S(1)}, u32[]{:S(2)}) copy-start(bf16[2,128,512]{2,1,0:T(8,128)(2,1)S(1)} %collective-permute-done.8.b2_hbm) | copy-start | bytes 786436
  34.5 5.5 %copy-start.13 = (bf16[2,128,512]{2,1,0:T(8,128)(2,1)}, bf16[2,128,512]{2,1,0:T(8,128)(2,1)S(1)}, u32[]{:S(2)}) copy-start(bf16[2,128,512]{2,1,0:T(8,128)(2,1)S(1)} %collective-permute-done.7.b1_hbm) | copy-start | bytes 786436
  34.5 20.0 %all-to-all-start = ((bf16[32,32,256]{2,1,0:T(8,128)(2,1)}), bf16[32,32,256]{2,1,0:T(8,128)(2,1)S(1)}, u32[]{:S(2)}, u32[]{:S(2)}) async-start(bf16[32,32,256]{2,1,0:T(8,128)(2,1)} %shard_map.90), calls=%async_computation | async-start | bytes 1048576 | tf_op jit(solution)/shard_map/all_to_all | solution.py:538
  38.4 1.6 %collective-permute-start.9 = (bf16[2,128,512]{2,1,0:T(8,128)(2,1)S(1)}, bf16[2,128,512]{2,1,0:T(8,128)(2,1)S(1)}, u32[]{:S(2)}, u32[]{:S(2)}) collective-permute-start(bf16[2,128,512]{2,1,0:T(8,128)(2,1)S(1)} %collective-permute-done.8.b2_hbm), channel_id=1, source_target_pairs={{0,8},{8,0},{16,24},{24,16},{1,9},{9,1},{17,25},{25,17},{2,10},{10... | collective-permute-start | bytes 786440 | tf_op jit(solution)/shard_map/ppermute | solution.py:451
  40.0 0.7 copy-start.14
  54.5 0.8 copy-start
  62.5 11.8 %all-to-all-start.1 = ((bf16[8,32,384]{2,1,0:T(8,128)(2,1)}), bf16[8,32,384]{2,1,0:T(8,128)(2,1)S(1)}, u32[]{:S(2)}, u32[]{:S(2)}) async-start(bf16[8,32,384]{2,1,0:T(8,128)(2,1)} %shard_map.92), calls=%async_computation.1 | async-start | bytes 393216 | tf_op jit(solution)/shard_map/all_to_all | solution.py:583
  74.2 7.1 %copy-start.1 = (bf16[8,32,384]{2,1,0:T(8,128)(2,1)}, bf16[8,32,384]{2,1,0:T(8,128)(2,1)S(1)}, u32[]{:S(2)}) copy-start(bf16[8,32,384]{2,1,0:T(8,128)(2,1)S(1)} %all-to-all-done.1.g0_hbm) | copy-start | bytes 589828
  74.2 5.7 %collective-permute-start.11 = (bf16[8,32,384]{2,1,0:T(8,128)(2,1)S(1)}, bf16[8,32,384]{2,1,0:T(8,128)(2,1)S(1)}, u32[]{:S(2)}, u32[]{:S(2)}) collective-permute-start(bf16[8,32,384]{2,1,0:T(8,128)(2,1)S(1)} %all-to-all-done.1.g0_hbm), channel_id=1, source_target_pairs={{0,16},{8,24},{16,0},{24,8},{1,17},{9,25},{17,1},{25,9},{2,18},{10... | collective-permute-start | bytes 589832 | tf_op jit(solution)/shard_map/ppermute | solution.py:451
  75.7 4.2 %collective-permute-start.10 = (bf16[8,32,384]{2,1,0:T(8,128)(2,1)S(1)}, bf16[8,32,384]{2,1,0:T(8,128)(2,1)S(1)}, u32[]{:S(2)}, u32[]{:S(2)}) collective-permute-start(bf16[8,32,384]{2,1,0:T(8,128)(2,1)S(1)} %all-to-all-done.1.g0_hbm), channel_id=1, source_target_pairs={{0,8},{8,0},{16,24},{24,16},{1,9},{9,1},{17,25},{25,17},{2,10},{10... | collective-permute-start | bytes 589832 | tf_op jit(solution)/shard_map/ppermute | solution.py:451
  79.9 1.4 %copy-start.2 = (bf16[8,32,384]{2,1,0:T(8,128)(2,1)}, bf16[8,32,384]{2,1,0:T(8,128)(2,1)S(1)}, u32[]{:S(2)}) copy-start(bf16[8,32,384]{2,1,0:T(8,128)(2,1)S(1)} %collective-permute-done.11.g2_hbm) | copy-start | bytes 589828
  79.9 1.4 %collective-permute-start.12 = (bf16[8,32,384]{2,1,0:T(8,128)(2,1)S(1)}, bf16[8,32,384]{2,1,0:T(8,128)(2,1)S(1)}, u32[]{:S(2)}, u32[]{:S(2)}) collective-permute-start(bf16[8,32,384]{2,1,0:T(8,128)(2,1)S(1)} %collective-permute-done.11.g2_hbm), channel_id=1, source_target_pairs={{0,8},{8,0},{16,24},{24,16},{1,9},{9,1},{17,25},{25,17},{2,10},{10... | collective-permute-start | bytes 589832 | tf_op jit(solution)/shard_map/ppermute | solution.py:451
  79.9 1.4 %copy-start.3 = (bf16[8,32,384]{2,1,0:T(8,128)(2,1)}, bf16[8,32,384]{2,1,0:T(8,128)(2,1)S(1)}, u32[]{:S(2)}) copy-start(bf16[8,32,384]{2,1,0:T(8,128)(2,1)S(1)} %collective-permute-done.10.g1_hbm) | copy-start | bytes 589828
  81.4 0.7 copy-start.4

commit v19 on v17

--- a/solution.py
+++ b/solution.py
@@ -219,6 +219,10 @@
     wait_all(start_all([(slots, slots_hbm)], sems))
 
 
+def column_of(row):
+    return jnp.broadcast_to(row.astype(f32), (8, row.shape[1])).T[:, 0:1]
+
+
 def extended(rows, axis, first):
     rest = -0.5 * jnp.sum(jnp.square(rows.astype(f32)), axis=axis, keepdims=True)
     parts = []
@@ -293,15 +297,13 @@
     wait_all(start_all(pairs, sems))
     places = [lax.bitwise_xor(row, k) for k in range(groups)]
     rights = [[extended(feats[k, u], 0, False) for k in range(groups)] for u in range(UPDATES)]
-    given = [[feats[k, u].astype(f32).T for k in range(groups)] for u in range(UPDATES)]
     for u in range(UPDATES):
         wanted = pivots[u : u + 1, :].astype(f32)
-        wanted = jnp.broadcast_to(wanted, (8, wanted.shape[1])).T[:, 0:1]
-        chosen_feats = jnp.zeros((pivots.shape[1], width), f32)
+        chosen_feats = jnp.zeros((width, wanted.shape[1]), f32)
         for k in range(groups):
-            here = came_from[pl.ds(u * groups + places[k], 1), :].astype(f32)
-            chosen_feats += mm(one_hot(wanted == here), given[u][k].astype(bf16), 1, 0)
-        left = extended(chosen_feats, 1, True)
+            here = column_of(came_from[pl.ds(u * groups + places[k], 1), :])
+            chosen_feats += mm(feats[k, u], one_hot(here == wanted), 1, 0)
+        left = extended(chosen_feats.T, 1, True)
         for k in range(groups):
             start = pl.multiple_of(places[k] * count, count)
             value = jnp.exp2(exponent(left, rights[u][k]))
@@ -309,9 +311,8 @@
     writes = start_all([(factor, factor_hbm)], sems)
     lefts, left_points = [], []
     for k in range(groups):
-        lefts.append(extended(given[0][k], 1, True))
-        points = ids[pl.ds(places[k], 1), :].astype(f32)
-        left_points.append(jnp.broadcast_to(points, (8, count)).T[:, 0:1])
+        lefts.append(extended(feats[k, 0].astype(f32).T, 1, True))
+        left_points.append(column_of(ids[pl.ds(places[k], 1), :]))
     left, left_points = jnp.concatenate(lefts, axis=0), jnp.concatenate(left_points, axis=0)
     sent = 1
     for m in range(groups):
@@ -431,7 +432,7 @@
     return jax.ShapeDtypeStruct(shape, dtype)
 
 
-def call(body, outs, inside, *args, near=0, sems=(), flops=0, grant=62):
+def call(body, outs, inside, *args, near=0, sems=(), flops=0, grant=63.9):
     moved = sum(math.prod(o.shape) * o.dtype.itemsize for o in [*outs, *args])
     return pl.pallas_call(
         body,
@@ -442,7 +443,7 @@
             x if isinstance(x, in_smem) else pltpu.VMEM(x.shape, x.dtype) for x in inside
         ]
         + [pltpu.SemaphoreType.DMA((n,)) for n in sems],
-        compiler_params=pltpu.CompilerParams(vmem_limit_bytes=grant * 2**20),
+        compiler_params=pltpu.CompilerParams(vmem_limit_bytes=int(grant * 2**20)),
         cost_estimate=pl.CostEstimate(flops=int(flops), bytes_accessed=moved, transcendentals=0),
     )(*args)
 
@@ -518,7 +519,6 @@
         *[came[k] for k in range(1, owners)],
         row_starts,
         sems=(owners + 1,),
-        grant=60,
     )
     beside, across = swap(mine, "rows", 1), swap(mine, "rows", 2)
     pieces = like((devices, deep, count // 2))
@@ -555,7 +555,6 @@
         came_from,
         pivot_index,
         sems=(rows * rows + 2,),
-        grant=60,
         flops=2.0 * width * block * (UPDATES * rank + block),
     )
     pieces = like((owners, deep, half * cap))
@@ -569,7 +568,6 @@
         cross,
         starts,
         sems=(2 * UPDATES + 3 + rows,),
-        grant=60,
     )
     steps, later_index = lax.optimization_barrier((steps, block_index))
     (slots,) = call(
@@ -603,7 +601,6 @@
         coefficients,
         momentum,
         sems=(1 + rows + 2 * parts, 2 * parts),
-        grant=60,
     )
 
 

time: 87.1 us -> 87.2 us (level)
  waiting for transfers between devices: 19.1 us -> 21.9 us
  local copies, waits for them, and re-layouts: 2.82 us -> 0.68 us
  Pallas kernels: 41.8 us -> 40.7 us
    unnamed x30 -> x2, local copies, waits for them, and re-layouts: 2.82 us -> 0.68 us
    all_to_all x1, waiting for transfers between devices: 2.37 us -> 3.8 us  [with_kernels(): summed = lax.all_to_all(pieces, ('rows', 'pts'), 0, 0, tiled=True)]
    ppermute x13, waiting for transfers between devices: 12.9 us -> 14.3 us  [swap(): lax.ppermute(value, axis, [(i, i ^ k) for i in range(lax.axis_size(axis))])]
    pallas_call x9, Pallas kernels: 41.8 us -> 40.7 us  [call(): pl.pallas_call(body, out_shape=outs, in_specs=[VMEM] * near + [HBM] * (le...]
  transfers between devices with their start and end apart: 15 -> 15, of which waited for: 9 -> 9; matrix products, arithmetic and copies ran while one was open for 0% -> 0% of each run, Pallas kernels for 30% -> 29%
where the time goes in v19:
time: 87.2 us; the launch traced here: 86.4 us
  Pallas kernels  40.7 us (47%)
  starting transfers between devices  22.2 us (25%)
  waiting for transfers between devices  21.9 us (25%)
  between operations  0.92 us (1%)
    pallas_call x9, Pallas kernels, call(): pl.pallas_call(body, out_shape=outs, in_specs=[VMEM] * near + [HBM] * (le...  40.7 us
    ppermute x13, waiting for transfers between devices, swap(): lax.ppermute(value, axis, [(i, i ^ k) for i in range(lax.axis_size(axis))])  14.3 us
    ppermute x13, starting transfers between devices, swap(): lax.ppermute(value, axis, [(i, i ^ k) for i in range(lax.axis_size(axis))])  13.8 us
    all_to_all x1, starting transfers between devices, with_kernels(): got = lax.all_to_all(steps, 'pts', 0, 0, tiled=True)  4.26 us
    all_to_all x1, starting transfers between devices, with_kernels(): summed = lax.all_to_all(pieces, ('rows', 'pts'), 0, 0, tiled=True)  4.11 us
    all_to_all x1, waiting for transfers between devices, with_kernels(): summed = lax.all_to_all(pieces, ('rows', 'pts'), 0, 0, tiled=True)  3.8 us
    all_to_all x1, waiting for transfers between devices, with_kernels(): got = lax.all_to_all(steps, 'pts', 0, 0, tiled=True)  3.79 us
  transfers between devices with their start and end apart: 15, of which 9 were waited for; matrix products, arithmetic and copies ran while one was open for 0% of the time, Pallas kernels for 29%

profile of v19, /device:TPU:0, one launch (start us, length us, event | category | flops | bytes accessed | tf_op | source)
XLA Modules:
  0.0 86.4 jit_solution(10423434770936278865)
XLA Ops:
  0.6 2.3 %shard_map.86.refs_0_ = bf16[384,128]{1,0:T(8,128)(2,1)} custom-call(s32[2,2048]{1,0:T(2,128)} %blocks_hbm.5, bf16[1024,128]{1,0:T(8,128)(2,1)} %feats_hbm.3), custom_call_target="tpu_custom_call" | custom-call | bytes 376832 | tf_op jit(solution)/shard_map/pallas_call | solution.py:437
  2.9 5.1 %collective-permute-start.4 = (bf16[384,128]{1,0:T(8,128)(2,1)}, bf16[384,128]{1,0:T(8,128)(2,1)}, u32[]{:S(2)}, u32[]{:S(2)}) collective-permute-start(bf16[384,128]{1,0:T(8,128)(2,1)} %shard_map.86.refs_0_), channel_id=1, source_target_pairs={{0,6},{1,7},{2,4},{3,5},{4,2},{5,3},{6,0},{7,1},{8,14},{9,15},{10,... | collective-permute-start | bytes 294920 | tf_op jit(solution)/shard_map/ppermute | solution.py:452
  8.0 0.0 collective-permute-start.3
  8.0 0.6 collective-permute-start.1
  8.6 1.7 %collective-permute-start = (bf16[384,128]{1,0:T(8,128)(2,1)}, bf16[384,128]{1,0:T(8,128)(2,1)}, u32[]{:S(2)}, u32[]{:S(2)}) collective-permute-start(bf16[384,128]{1,0:T(8,128)(2,1)} %shard_map.86.refs_0_), channel_id=1, source_target_pairs={{0,1},{1,0},{2,3},{3,2},{4,5},{5,4},{6,7},{7,6},{8,9},{9,8},{10,11... | collective-permute-start | bytes 294920 | tf_op jit(solution)/shard_map/ppermute | solution.py:452
  10.3 4.3 %shard_map.87 = (bf16[2,256,1024]{2,1,0:T(8,128)(2,1)}, f32[2,256,512]{2,1,0:T(8,128)}, s32[8,128]{1,0:T(8,128)}) custom-call(s32[2,2048]{1,0:T(2,128)} %blocks_hbm.5, f32[1024,256]{1,0:T(8,128)} %w_hbm.3, f32[1024,256]{1,0:T(8,128)} %z_hbm.3, bf16[1024,256]{1,0:T(8,128)(2,1)} %t_hbm.1), custom_call_target="tpu_custom_call" | custom-call | bytes 4739072 | tf_op jit(solution)/shard_map/pallas_call | solution.py:437
  14.6 0.0 collective-permute-done.4.refs_6_
  14.6 2.0 %collective-permute-done.3.refs_4_ = bf16[384,128]{1,0:T(8,128)(2,1)} collective-permute-done((bf16[384,128]{1,0:T(8,128)(2,1)}, bf16[384,128]{1,0:T(8,128)(2,1)}, u32[]{:S(2)}, u32[]{:S(2)}) %collective-permute-start.3) | collective-permute-done | bytes 98336 | tf_op jit(solution)/shard_map/ppermute | solution.py:452
  16.6 1.5 %collective-permute-start.5 = (bf16[384,128]{1,0:T(8,128)(2,1)}, bf16[384,128]{1,0:T(8,128)(2,1)}, u32[]{:S(2)}, u32[]{:S(2)}) collective-permute-start(bf16[384,128]{1,0:T(8,128)(2,1)} %collective-permute-done.3.refs_4_), channel_id=1, source_target_pairs={{0,1},{1,0},{2,3},{3,2},{4,5},{5,4},{6,7},{7,6},{8,9},{9,8},{10,11... | collective-permute-start | bytes 294920 | tf_op jit(solution)/shard_map/ppermute | solution.py:452
  18.1 0.0 collective-permute-done.1.refs_2_
  18.1 0.5 collective-permute-start.2
  18.6 1.5 %collective-permute-start.6 = (bf16[384,128]{1,0:T(8,128)(2,1)}, bf16[384,128]{1,0:T(8,128)(2,1)}, u32[]{:S(2)}, u32[]{:S(2)}) collective-permute-start(bf16[384,128]{1,0:T(8,128)(2,1)} %collective-permute-done.4.refs_6_), channel_id=1, source_target_pairs={{0,1},{1,0},{2,3},{3,2},{4,5},{5,4},{6,7},{7,6},{8,9},{9,8},{10,11... | collective-permute-start | bytes 294920 | tf_op jit(solution)/shard_map/ppermute | solution.py:452
  20.1 2.8 %shard_map.88 = (s32[8,512]{1,0:T(8,128)}, s32[8,512]{1,0:T(8,128)}, s32[8,128]{1,0:T(8,128)}) custom-call(s32[2,2048]{1,0:T(2,128)} %blocks_hbm.5), custom_call_target="tpu_custom_call" | custom-call | bytes 53248 | tf_op jit(solution)/shard_map/pallas_call | solution.py:437
  22.9 0.0 collective-permute-done.refs_1_
  22.9 1.2 %collective-permute-done.2.refs_3_ = bf16[384,128]{1,0:T(8,128)(2,1)} collective-permute-done((bf16[384,128]{1,0:T(8,128)(2,1)}, bf16[384,128]{1,0:T(8,128)(2,1)}, u32[]{:S(2)}, u32[]{:S(2)}) %collective-permute-start.2) | collective-permute-done | bytes 98336 | tf_op jit(solution)/shard_map/ppermute | solution.py:452
  24.1 0.0 collective-permute-done.5.refs_5_
  24.1 1.0 %collective-permute-done.6.refs_7_ = bf16[384,128]{1,0:T(8,128)(2,1)} collective-permute-done((bf16[384,128]{1,0:T(8,128)(2,1)}, bf16[384,128]{1,0:T(8,128)(2,1)}, u32[]{:S(2)}, u32[]{:S(2)}) %collective-permute-start.6) | collective-permute-done | bytes 98336 | tf_op jit(solution)/shard_map/ppermute | solution.py:452
  25.1 2.3 %shard_map.89.block_hbm.b0_hbm = bf16[2,128,512]{2,1,0:T(8,128)(2,1)} custom-call(bf16[384,128]{1,0:T(8,128)(2,1)} %shard_map.86.refs_0_, bf16[384,128]{1,0:T(8,128)(2,1)} %collective-permute-done.refs_1_, bf16[384,128]{1,0:T(8,128)(2,1)} %collective-permute-done.1.refs_2_, bf16[384,128]{1,0:T(8,128)(2,1)} %collective-permute-done.2.refs_3_, ...), custom_call_target="tpu_custom_call" | custom-call | bytes 1052672 | tf_op jit(solution)/shard_map/pallas_call | solution.py:437
  27.4 1.6 %collective-permute-start.8 = (bf16[2,128,512]{2,1,0:T(8,128)(2,1)}, bf16[2,128,512]{2,1,0:T(8,128)(2,1)}, u32[]{:S(2)}, u32[]{:S(2)}) collective-permute-start(bf16[2,128,512]{2,1,0:T(8,128)(2,1)} %shard_map.89.block_hbm.b0_hbm), channel_id=1, source_target_pairs={{0,16},{8,24},{16,0},{24,8},{1,17},{9,25},{17,1},{25,9},{2,18},{10... | collective-permute-start | bytes 786440 | tf_op jit(solution)/shard_map/ppermute | solution.py:452
  29.0 0.0 collective-permute-start.7
  29.0 3.5 %shard_map.90 = bf16[32,32,256]{2,1,0:T(8,128)(2,1)} custom-call(bf16[2,128,512]{2,1,0:T(8,128)(2,1)} %shard_map.89.block_hbm.b0_hbm, bf16[1024,128]{1,0:T(8,128)(2,1)} %feats_hbm.3, bf16[2,256,1024]{2,1,0:T(8,128)(2,1)} %get-tuple-element.30.coef_hbm, f32[2,256,512]{2,1,0:T(8,128)} %get-tuple-element.31.offset_hbm), custom_call_target="tpu_custom_call" | custom-call | flops 1073741824 | bytes 3145728 | tf_op jit(solution)/shard_map/pallas_call | solution.py:437
  32.5 2.0 %collective-permute-done.8.b2_hbm = bf16[2,128,512]{2,1,0:T(8,128)(2,1)} collective-permute-done((bf16[2,128,512]{2,1,0:T(8,128)(2,1)}, bf16[2,128,512]{2,1,0:T(8,128)(2,1)}, u32[]{:S(2)}, u32[]{:S(2)}) %collective-permute-start.8) | collective-permute-done | bytes 262176 | tf_op jit(solution)/shard_map/ppermute | solution.py:452
  34.5 0.0 collective-permute-done.7.b1_hbm
  34.5 4.1 %all-to-all-start = ((bf16[32,32,256]{2,1,0:T(8,128)(2,1)}), bf16[32,32,256]{2,1,0:T(8,128)(2,1)}, u32[]{:S(2)}, u32[]{:S(2)}) async-start(bf16[32,32,256]{2,1,0:T(8,128)(2,1)} %shard_map.90), calls=%async_computation | async-start | bytes 1048576 | tf_op jit(solution)/shard_map/all_to_all | solution.py:537
  38.7 0.1 collective-permute-start.9
  38.7 1.9 %collective-permute-done.9.b3_hbm = bf16[2,128,512]{2,1,0:T(8,128)(2,1)} collective-permute-done((bf16[2,128,512]{2,1,0:T(8,128)(2,1)}, bf16[2,128,512]{2,1,0:T(8,128)(2,1)}, u32[]{:S(2)}, u32[]{:S(2)}) %collective-permute-start.9) | collective-permute-done | bytes 262176 | tf_op jit(solution)/shard_map/ppermute | solution.py:452
  40.6 10.4 %shard_map.91 = (bf16[2,512,2048]{2,1,0:T(8,128)(2,1)}, bf16[4,2048,512]{2,1,0:T(8,128)(2,1)}) custom-call(bf16[2,128,512]{2,1,0:T(8,128)(2,1)} %shard_map.89.block_hbm.b0_hbm, bf16[2,128,512]{2,1,0:T(8,128)(2,1)} %collective-permute-done.7.b1_hbm, bf16[2,128,512]{2,1,0:T(8,128)(2,1)} %collective-permute-done.8.b2_hbm, ...), custom_call_target="tpu_custom_call" | custom-call | flops 1610612736 | bytes 13668352 | tf_op jit(solution)/shard_map/pallas_call | solution.py:437
  51.0 3.8 %all-to-all-done.summed_hbm = bf16[32,32,256]{2,1,0:T(8,128)(2,1)} async-done(((bf16[32,32,256]{2,1,0:T(8,128)(2,1)}), bf16[32,32,256]{2,1,0:T(8,128)(2,1)}, u32[]{:S(2)}, u32[]{:S(2)}) %all-to-all-start) | async-done | bytes 524320 | tf_op jit(solution)/shard_map/all_to_all | solution.py:537
  54.8 7.1 %shard_map.92 = bf16[8,32,384]{2,1,0:T(8,128)(2,1)} custom-call(bf16[32,32,256]{2,1,0:T(8,128)(2,1)} %all-to-all-done.summed_hbm, bf16[2,512,2048]{2,1,0:T(8,128)(2,1)} %get-tuple-element.37.factor_hbm, bf16[2,512,512]{2,1,0:T(8,128)(2,1)} %core_hbm.1, bf16[4,2048,512]{2,1,0:T(8,128)(2,1)} %get-tuple-element.38.cross_hbm, s32[8,128]{1,0:T(8,128)} %get-tuple-element.39.starts_hbm), custom_call_target="tpu_custom_call" | custom-call | bytes 14356480 | tf_op jit(solution)/shard_map/pallas_call | solution.py:437
  61.9 4.3 %all-to-all-start.1 = ((bf16[8,32,384]{2,1,0:T(8,128)(2,1)}), bf16[8,32,384]{2,1,0:T(8,128)(2,1)}, u32[]{:S(2)}, u32[]{:S(2)}) async-start(bf16[8,32,384]{2,1,0:T(8,128)(2,1)} %shard_map.92), calls=%async_computation.1 | async-start | bytes 393216 | tf_op jit(solution)/shard_map/all_to_all | solution.py:580
  66.2 4.1 %shard_map.93.slots_hbm = s32[2,768]{1,0:T(2,128)} custom-call(s32[2,2048]{1,0:T(2,128)} %blocks_hbm.5), custom_call_target="tpu_custom_call" | custom-call | bytes 22528 | tf_op jit(solution)/shard_map/pallas_call | solution.py:437
  70.3 3.8 %all-to-all-done.1.g0_hbm = bf16[8,32,384]{2,1,0:T(8,128)(2,1)} async-done(((bf16[8,32,384]{2,1,0:T(8,128)(2,1)}), bf16[8,32,384]{2,1,0:T(8,128)(2,1)}, u32[]{:S(2)}, u32[]{:S(2)}) %all-to-all-start.1) | async-done | bytes 196640 | tf_op jit(solution)/shard_map/all_to_all | solution.py:580
  74.1 1.2 %collective-permute-start.11 = (bf16[8,32,384]{2,1,0:T(8,128)(2,1)}, bf16[8,32,384]{2,1,0:T(8,128)(2,1)S(1)}, u32[]{:S(2)}, u32[]{:S(2)}) collective-permute-start(bf16[8,32,384]{2,1,0:T(8,128)(2,1)} %all-to-all-done.1.g0_hbm), channel_id=1, source_target_pairs={{0,16},{8,24},{16,0},{24,8},{1,17},{9,25},{17,1},{25,9},{2,18},{10... | collective-permute-start | bytes 589832 | tf_op jit(solution)/shard_map/ppermute | solution.py:452
  75.2 0.0 collective-permute-start.10
  75.3 4.7 %collective-permute-done.11.g2_hbm = bf16[8,32,384]{2,1,0:T(8,128)(2,1)S(1)} collective-permute-done((bf16[8,32,384]{2,1,0:T(8,128)(2,1)}, bf16[8,32,384]{2,1,0:T(8,128)(2,1)S(1)}, u32[]{:S(2)}, u32[]{:S(2)}) %collective-permute-start.11) | collective-permute-done | bytes 196640 | tf_op jit(solution)/shard_map/ppermute | solution.py:452
  79.9 0.0 copy-start
  79.9 0.7 copy-done
  80.6 0.0 collective-permute-start.12
  80.6 0.0 collective-permute-done.10.g1_hbm
  80.6 1.6 %collective-permute-done.12.g3_hbm = bf16[8,32,384]{2,1,0:T(8,128)(2,1)} collective-permute-done((bf16[8,32,384]{2,1,0:T(8,128)(2,1)S(1)}, bf16[8,32,384]{2,1,0:T(8,128)(2,1)}, u32[]{:S(2)}, u32[]{:S(2)}) %collective-permute-start.12) | collective-permute-done | bytes 196640 | tf_op jit(solution)/shard_map/ppermute | solution.py:452
  82.2 4.1 %shard_map.94 = (f32[1024,256]{1,0:T(8,128)}, f32[1024,256]{1,0:T(8,128)}) custom-call(bf16[8,32,384]{2,1,0:T(8,128)(2,1)} %all-to-all-done.1.g0_hbm, bf16[8,32,384]{2,1,0:T(8,128)(2,1)} %collective-permute-done.10.g1_hbm, bf16[8,32,384]{2,1,0:T(8,128)(2,1)} %copy-done, bf16[8,32,384]{2,1,0:T(8,128)(2,1)} %collective-permute-done.12.g3_hbm, ...), custom_call_target="tpu_custom_call" | custom-call | bytes 4986880 | tf_op jit(solution)/shard_map/pallas_call | solution.py:437
Async XLA Ops:
  2.9 11.7 %collective-permute-start.4 = (bf16[384,128]{1,0:T(8,128)(2,1)}, bf16[384,128]{1,0:T(8,128)(2,1)}, u32[]{:S(2)}, u32[]{:S(2)}) collective-permute-start(bf16[384,128]{1,0:T(8,128)(2,1)} %shard_map.86.refs_0_), channel_id=1, source_target_pairs={{0,6},{1,7},{2,4},{3,5},{4,2},{5,3},{6,0},{7,1},{8,14},{9,15},{10,... | collective-permute-start | bytes 294920 | tf_op jit(solution)/shard_map/ppermute | solution.py:452
  8.0 8.6 %collective-permute-start.3 = (bf16[384,128]{1,0:T(8,128)(2,1)}, bf16[384,128]{1,0:T(8,128)(2,1)}, u32[]{:S(2)}, u32[]{:S(2)}) collective-permute-start(bf16[384,128]{1,0:T(8,128)(2,1)} %shard_map.86.refs_0_), channel_id=1, source_target_pairs={{0,4},{1,5},{2,6},{3,7},{4,0},{5,1},{6,2},{7,3},{8,12},{9,13},{10,... | collective-permute-start | bytes 294920 | tf_op jit(solution)/shard_map/ppermute | solution.py:452
  8.0 10.1 %collective-permute-start.1 = (bf16[384,128]{1,0:T(8,128)(2,1)}, bf16[384,128]{1,0:T(8,128)(2,1)}, u32[]{:S(2)}, u32[]{:S(2)}) collective-permute-start(bf16[384,128]{1,0:T(8,128)(2,1)} %shard_map.86.refs_0_), channel_id=1, source_target_pairs={{0,2},{1,3},{2,0},{3,1},{4,6},{5,7},{6,4},{7,5},{8,10},{9,11},{10,... | collective-permute-start | bytes 294920 | tf_op jit(solution)/shard_map/ppermute | solution.py:452
  8.6 14.3 %collective-permute-start = (bf16[384,128]{1,0:T(8,128)(2,1)}, bf16[384,128]{1,0:T(8,128)(2,1)}, u32[]{:S(2)}, u32[]{:S(2)}) collective-permute-start(bf16[384,128]{1,0:T(8,128)(2,1)} %shard_map.86.refs_0_), channel_id=1, source_target_pairs={{0,1},{1,0},{2,3},{3,2},{4,5},{5,4},{6,7},{7,6},{8,9},{9,8},{10,11... | collective-permute-start | bytes 294920 | tf_op jit(solution)/shard_map/ppermute | solution.py:452
  16.6 7.5 %collective-permute-start.5 = (bf16[384,128]{1,0:T(8,128)(2,1)}, bf16[384,128]{1,0:T(8,128)(2,1)}, u32[]{:S(2)}, u32[]{:S(2)}) collective-permute-start(bf16[384,128]{1,0:T(8,128)(2,1)} %collective-permute-done.3.refs_4_), channel_id=1, source_target_pairs={{0,1},{1,0},{2,3},{3,2},{4,5},{5,4},{6,7},{7,6},{8,9},{9,8},{10,11... | collective-permute-start | bytes 294920 | tf_op jit(solution)/shard_map/ppermute | solution.py:452
  18.1 6.0 %collective-permute-start.2 = (bf16[384,128]{1,0:T(8,128)(2,1)}, bf16[384,128]{1,0:T(8,128)(2,1)}, u32[]{:S(2)}, u32[]{:S(2)}) collective-permute-start(bf16[384,128]{1,0:T(8,128)(2,1)} %collective-permute-done.1.refs_2_), channel_id=1, source_target_pairs={{0,1},{1,0},{2,3},{3,2},{4,5},{5,4},{6,7},{7,6},{8,9},{9,8},{10,11... | collective-permute-start | bytes 294920 | tf_op jit(solution)/shard_map/ppermute | solution.py:452
  18.6 6.5 %collective-permute-start.6 = (bf16[384,128]{1,0:T(8,128)(2,1)}, bf16[384,128]{1,0:T(8,128)(2,1)}, u32[]{:S(2)}, u32[]{:S(2)}) collective-permute-start(bf16[384,128]{1,0:T(8,128)(2,1)} %collective-permute-done.4.refs_6_), channel_id=1, source_target_pairs={{0,1},{1,0},{2,3},{3,2},{4,5},{5,4},{6,7},{7,6},{8,9},{9,8},{10,11... | collective-permute-start | bytes 294920 | tf_op jit(solution)/shard_map/ppermute | solution.py:452
  27.4 7.1 %collective-permute-start.8 = (bf16[2,128,512]{2,1,0:T(8,128)(2,1)}, bf16[2,128,512]{2,1,0:T(8,128)(2,1)}, u32[]{:S(2)}, u32[]{:S(2)}) collective-permute-start(bf16[2,128,512]{2,1,0:T(8,128)(2,1)} %shard_map.89.block_hbm.b0_hbm), channel_id=1, source_target_pairs={{0,16},{8,24},{16,0},{24,8},{1,17},{9,25},{17,1},{25,9},{2,18},{10... | collective-permute-start | bytes 786440 | tf_op jit(solution)/shard_map/ppermute | solution.py:452
  29.0 5.5 %collective-permute-start.7 = (bf16[2,128,512]{2,1,0:T(8,128)(2,1)}, bf16[2,128,512]{2,1,0:T(8,128)(2,1)}, u32[]{:S(2)}, u32[]{:S(2)}) collective-permute-start(bf16[2,128,512]{2,1,0:T(8,128)(2,1)} %shard_map.89.block_hbm.b0_hbm), channel_id=1, source_target_pairs={{0,8},{8,0},{16,24},{24,16},{1,9},{9,1},{17,25},{25,17},{2,10},{10... | collective-permute-start | bytes 786440 | tf_op jit(solution)/shard_map/ppermute | solution.py:452
  34.5 20.3 %all-to-all-start = ((bf16[32,32,256]{2,1,0:T(8,128)(2,1)}), bf16[32,32,256]{2,1,0:T(8,128)(2,1)}, u32[]{:S(2)}, u32[]{:S(2)}) async-start(bf16[32,32,256]{2,1,0:T(8,128)(2,1)} %shard_map.90), calls=%async_computation | async-start | bytes 1048576 | tf_op jit(solution)/shard_map/all_to_all | solution.py:537
  38.7 1.9 %collective-permute-start.9 = (bf16[2,128,512]{2,1,0:T(8,128)(2,1)}, bf16[2,128,512]{2,1,0:T(8,128)(2,1)}, u32[]{:S(2)}, u32[]{:S(2)}) collective-permute-start(bf16[2,128,512]{2,1,0:T(8,128)(2,1)} %collective-permute-done.8.b2_hbm), channel_id=1, source_target_pairs={{0,8},{8,0},{16,24},{24,16},{1,9},{9,1},{17,25},{25,17},{2,10},{10... | collective-permute-start | bytes 786440 | tf_op jit(solution)/shard_map/ppermute | solution.py:452
  61.9 12.1 %all-to-all-start.1 = ((bf16[8,32,384]{2,1,0:T(8,128)(2,1)}), bf16[8,32,384]{2,1,0:T(8,128)(2,1)}, u32[]{:S(2)}, u32[]{:S(2)}) async-start(bf16[8,32,384]{2,1,0:T(8,128)(2,1)} %shard_map.92), calls=%async_computation.1 | async-start | bytes 393216 | tf_op jit(solution)/shard_map/all_to_all | solution.py:580
  74.1 5.9 %collective-permute-start.11 = (bf16[8,32,384]{2,1,0:T(8,128)(2,1)}, bf16[8,32,384]{2,1,0:T(8,128)(2,1)S(1)}, u32[]{:S(2)}, u32[]{:S(2)}) collective-permute-start(bf16[8,32,384]{2,1,0:T(8,128)(2,1)} %all-to-all-done.1.g0_hbm), channel_id=1, source_target_pairs={{0,16},{8,24},{16,0},{24,8},{1,17},{9,25},{17,1},{25,9},{2,18},{10... | collective-permute-start | bytes 589832 | tf_op jit(solution)/shard_map/ppermute | solution.py:452
  75.2 5.4 %collective-permute-start.10 = (bf16[8,32,384]{2,1,0:T(8,128)(2,1)}, bf16[8,32,384]{2,1,0:T(8,128)(2,1)}, u32[]{:S(2)}, u32[]{:S(2)}) collective-permute-start(bf16[8,32,384]{2,1,0:T(8,128)(2,1)} %all-to-all-done.1.g0_hbm), channel_id=1, source_target_pairs={{0,8},{8,0},{16,24},{24,16},{1,9},{9,1},{17,25},{25,17},{2,10},{10... | collective-permute-start | bytes 589832 | tf_op jit(solution)/shard_map/ppermute | solution.py:452
  79.9 0.7 copy-start
  80.6 1.6 %collective-permute-start.12 = (bf16[8,32,384]{2,1,0:T(8,128)(2,1)S(1)}, bf16[8,32,384]{2,1,0:T(8,128)(2,1)}, u32[]{:S(2)}, u32[]{:S(2)}) collective-permute-start(bf16[8,32,384]{2,1,0:T(8,128)(2,1)S(1)} %collective-permute-done.11.g2_hbm), channel_id=1, source_target_pairs={{0,8},{8,0},{16,24},{24,16},{1,9},{9,1},{17,25},{25,17},{2,10},{10... | collective-permute-start | bytes 589832 | tf_op jit(solution)/shard_map/ppermute | solution.py:452

commit v20 on v19

--- a/solution.py
+++ b/solution.py
@@ -474,9 +474,7 @@
         features,
         sems=(2,),
     )
-    came = {k: swap(packed, "pts", k) for k in reversed(range(2, owners, 2))}
-    came[1] = swap(packed, "pts", 1)
-    came[3] = swap(came[2], "pts", 1)
+    came = {k: swap(packed, "pts", k) for k in (6, 5, 4, 2, 1)}
     kept = [
         like((UPDATES, outputs, points)),
         like((UPDATES, outputs, count), f32),
@@ -490,20 +488,8 @@
         *given,
         sems=(4, 1 + 2 * UPDATES),
     )
-    came[4], came[6], row_starts, later_index = lax.optimization_barrier(
-        (came[4], came[6], row_starts, block_index)
-    )
-    came[5], came[7] = swap(came[4], "pts", 1), swap(came[6], "pts", 1)
-
-    kept = [like((UPDATES * rows, count), i32)] * 2 + [like((8, 128), i32)]
-    ids, came_from, starts = call(
-        functools.partial(order_kernel, count, points, owners),
-        kept,
-        [block_index, *kept],
-        later_index,
-        sems=(3,),
-    )
-    row_starts, ids = lax.optimization_barrier((row_starts, ids))
+    came[2], came[6], row_starts = lax.optimization_barrier((came[2], came[6], row_starts))
+    came[3], came[7] = swap(came[2], "pts", 1), swap(came[6], "pts", 1)
     feats = like((UPDATES, width, count))
     inside_starts = pltpu.SMEM(row_starts.shape, i32)
     (mine,) = call(
@@ -533,7 +519,16 @@
         sems=(4,),
         flops=2.0 * UPDATES * points * count * (2 * width + outputs),
     )
-    pieces, beside, across = lax.optimization_barrier((pieces, beside, across))
+    pieces, later_index = lax.optimization_barrier((pieces, block_index))
+    kept = [like((UPDATES * rows, count), i32)] * 2 + [like((8, 128), i32)]
+    ids, came_from, starts = call(
+        functools.partial(order_kernel, count, points, owners),
+        kept,
+        [block_index, *kept],
+        later_index,
+        sems=(3,),
+    )
+    pieces, beside, across, ids = lax.optimization_barrier((pieces, beside, across, ids))
     summed = lax.all_to_all(pieces, ("rows", "pts"), 0, 0, tiled=True)
     kept = [like((UPDATES, rank, block)), like((rows, block, count))]
     factor, cross = call(
@@ -569,7 +564,9 @@
         starts,
         sems=(2 * UPDATES + 3 + rows,),
     )
-    steps, later_index = lax.optimization_barrier((steps, block_index))
+    got = lax.all_to_all(steps, "pts", 0, 0, tiled=True)
+    got, later_index = lax.optimization_barrier((got, block_index))
+    beside, across = swap(got, "rows", 1), swap(got, "rows", 2)
     (slots,) = call(
         functools.partial(slots_kernel, count, points, cap),
         [like((UPDATES, rows * cap), i32)],
@@ -577,9 +574,7 @@
         later_index,
         sems=(1,),
     )
-    got = lax.all_to_all(steps, "pts", 0, 0, tiled=True)
-    got, slots = lax.optimization_barrier((got, slots))
-    beside, across = swap(got, "rows", 1), swap(got, "rows", 2)
+    across, slots = lax.optimization_barrier((across, slots))
     parts = points // CHUNK
     return call(
         finish_kernel,

time: 87.2 us -> 85.6 us (0.982)
  blocking collectives: 0 us -> 12.1 us
  waiting for transfers between devices: 21.9 us -> 13 us
  starting transfers between devices: 22.2 us -> 18.2 us
    all_to_all x0 -> x1, blocking collectives: none -> 12.1 us  [with_kernels(): got = lax.all_to_all(steps, 'pts', 0, 0, tiled=True)]
    ppermute x13, waiting for transfers between devices: 14.3 us -> 9.16 us  [swap(): lax.ppermute(value, axis, [(i, i ^ k) for i in range(lax.axis_size(axis))])]
    all_to_all x1 -> x0, starting transfers between devices: 4.26 us -> none  [with_kernels(): got = lax.all_to_all(steps, 'pts', 0, 0, tiled=True)]
    all_to_all x1 -> x0, waiting for transfers between devices: 3.79 us -> none  [with_kernels(): got = lax.all_to_all(steps, 'pts', 0, 0, tiled=True)]
  transfers between devices with their start and end apart: 15 -> 14, of which waited for: 9 -> 8; matrix products, arithmetic and copies ran while one was open for 0% -> 0% of each run, Pallas kernels for 29% -> 29%
where the time goes in v20:
time: 85.6 us; the launch traced here: 84.9 us
  Pallas kernels  40.7 us (48%)
  starting transfers between devices  18.2 us (21%)
  waiting for transfers between devices  13 us (15%)
  blocking collectives  12.1 us (14%)
  between operations  0.92 us (1%)
    pallas_call x9, Pallas kernels, call(): pl.pallas_call(body, out_shape=outs, in_specs=[VMEM] * near + [HBM] * (le...  40.7 us
    ppermute x13, starting transfers between devices, swap(): lax.ppermute(value, axis, [(i, i ^ k) for i in range(lax.axis_size(axis))])  14.7 us
    all_to_all x1, blocking collectives, with_kernels(): got = lax.all_to_all(steps, 'pts', 0, 0, tiled=True)  12.1 us
    ppermute x13, waiting for transfers between devices, swap(): lax.ppermute(value, axis, [(i, i ^ k) for i in range(lax.axis_size(axis))])  9.16 us
    all_to_all x1, waiting for transfers between devices, with_kernels(): summed = lax.all_to_all(pieces, ('rows', 'pts'), 0, 0, tiled=True)  3.8 us
    all_to_all x1, starting transfers between devices, with_kernels(): summed = lax.all_to_all(pieces, ('rows', 'pts'), 0, 0, tiled=True)  3.53 us
  transfers between devices with their start and end apart: 14, of which 8 were waited for; matrix products, arithmetic and copies ran while one was open for 0% of the time, Pallas kernels for 29%

profile of v20, /device:TPU:0, one launch (start us, length us, event | category | flops | bytes accessed | tf_op | source)
XLA Modules:
  0.0 84.9 jit_solution(8052593710498034377)
XLA Ops:
  0.6 2.3 %shard_map.86.refs_0_ = bf16[384,128]{1,0:T(8,128)(2,1)} custom-call(s32[2,2048]{1,0:T(2,128)} %blocks_hbm.5, bf16[1024,128]{1,0:T(8,128)(2,1)} %feats_hbm.3), custom_call_target="tpu_custom_call" | custom-call | bytes 376832 | tf_op jit(solution)/shard_map/pallas_call | solution.py:437
  2.9 5.1 %collective-permute-start.2 = (bf16[384,128]{1,0:T(8,128)(2,1)}, bf16[384,128]{1,0:T(8,128)(2,1)}, u32[]{:S(2)}, u32[]{:S(2)}) collective-permute-start(bf16[384,128]{1,0:T(8,128)(2,1)} %shard_map.86.refs_0_), channel_id=1, source_target_pairs={{0,6},{1,7},{2,4},{3,5},{4,2},{5,3},{6,0},{7,1},{8,14},{9,15},{10,... | collective-permute-start | bytes 294920 | tf_op jit(solution)/shard_map/ppermute | solution.py:452
  8.0 0.0 collective-permute-start.1
  8.0 1.7 %collective-permute-start.5 = (bf16[384,128]{1,0:T(8,128)(2,1)}, bf16[384,128]{1,0:T(8,128)(2,1)}, u32[]{:S(2)}, u32[]{:S(2)}) collective-permute-start(bf16[384,128]{1,0:T(8,128)(2,1)} %shard_map.86.refs_0_), channel_id=1, source_target_pairs={{0,5},{1,4},{2,7},{3,6},{4,1},{5,0},{6,3},{7,2},{8,13},{9,12},{10,... | collective-permute-start | bytes 294920 | tf_op jit(solution)/shard_map/ppermute | solution.py:452
  9.8 2.1 %collective-permute-start.4 = (bf16[384,128]{1,0:T(8,128)(2,1)}, bf16[384,128]{1,0:T(8,128)(2,1)}, u32[]{:S(2)}, u32[]{:S(2)}) collective-permute-start(bf16[384,128]{1,0:T(8,128)(2,1)} %shard_map.86.refs_0_), channel_id=1, source_target_pairs={{0,4},{1,5},{2,6},{3,7},{4,0},{5,1},{6,2},{7,3},{8,12},{9,13},{10,... | collective-permute-start | bytes 294920 | tf_op jit(solution)/shard_map/ppermute | solution.py:452
  11.9 0.5 collective-permute-start
  12.4 4.3 %shard_map.87 = (bf16[2,256,1024]{2,1,0:T(8,128)(2,1)}, f32[2,256,512]{2,1,0:T(8,128)}, s32[8,128]{1,0:T(8,128)}) custom-call(s32[2,2048]{1,0:T(2,128)} %blocks_hbm.5, f32[1024,256]{1,0:T(8,128)} %w_hbm.3, f32[1024,256]{1,0:T(8,128)} %z_hbm.3, bf16[1024,256]{1,0:T(8,128)(2,1)} %t_hbm.1), custom_call_target="tpu_custom_call" | custom-call | bytes 4739072 | tf_op jit(solution)/shard_map/pallas_call | solution.py:437
  16.7 0.0 collective-permute-done.2.refs_6_
  16.7 0.0 collective-permute-done.1.refs_2_
  16.7 1.6 %collective-permute-start.3 = (bf16[384,128]{1,0:T(8,128)(2,1)}, bf16[384,128]{1,0:T(8,128)(2,1)}, u32[]{:S(2)}, u32[]{:S(2)}) collective-permute-start(bf16[384,128]{1,0:T(8,128)(2,1)} %collective-permute-done.1.refs_2_), channel_id=1, source_target_pairs={{0,1},{1,0},{2,3},{3,2},{4,5},{5,4},{6,7},{7,6},{8,9},{9,8},{10,11... | collective-permute-start | bytes 294920 | tf_op jit(solution)/shard_map/ppermute | solution.py:452
  18.3 0.5 collective-permute-start.6
  18.8 1.4 %collective-permute-done.5.refs_5_ = bf16[384,128]{1,0:T(8,128)(2,1)} collective-permute-done((bf16[384,128]{1,0:T(8,128)(2,1)}, bf16[384,128]{1,0:T(8,128)(2,1)}, u32[]{:S(2)}, u32[]{:S(2)}) %collective-permute-start.5) | collective-permute-done | bytes 98336 | tf_op jit(solution)/shard_map/ppermute | solution.py:452
  20.2 0.6 collective-permute-done.4.refs_4_
  20.8 0.0 collective-permute-done.refs_1_
  20.9 1.9 %collective-permute-done.3.refs_3_ = bf16[384,128]{1,0:T(8,128)(2,1)} collective-permute-done((bf16[384,128]{1,0:T(8,128)(2,1)}, bf16[384,128]{1,0:T(8,128)(2,1)}, u32[]{:S(2)}, u32[]{:S(2)}) %collective-permute-start.3) | collective-permute-done | bytes 98336 | tf_op jit(solution)/shard_map/ppermute | solution.py:452
  22.7 1.1 %collective-permute-done.6.refs_7_ = bf16[384,128]{1,0:T(8,128)(2,1)} collective-permute-done((bf16[384,128]{1,0:T(8,128)(2,1)}, bf16[384,128]{1,0:T(8,128)(2,1)}, u32[]{:S(2)}, u32[]{:S(2)}) %collective-permute-start.6) | collective-permute-done | bytes 98336 | tf_op jit(solution)/shard_map/ppermute | solution.py:452
  23.8 2.3 %shard_map.88.block_hbm.b0_hbm = bf16[2,128,512]{2,1,0:T(8,128)(2,1)} custom-call(bf16[384,128]{1,0:T(8,128)(2,1)} %shard_map.86.refs_0_, bf16[384,128]{1,0:T(8,128)(2,1)} %collective-permute-done.refs_1_, bf16[384,128]{1,0:T(8,128)(2,1)} %collective-permute-done.1.refs_2_, bf16[384,128]{1,0:T(8,128)(2,1)} %collective-permute-done.3.refs_3_, ...), custom_call_target="tpu_custom_call" | custom-call | bytes 1052672 | tf_op jit(solution)/shard_map/pallas_call | solution.py:437
  26.1 1.6 %collective-permute-start.8 = (bf16[2,128,512]{2,1,0:T(8,128)(2,1)}, bf16[2,128,512]{2,1,0:T(8,128)(2,1)}, u32[]{:S(2)}, u32[]{:S(2)}) collective-permute-start(bf16[2,128,512]{2,1,0:T(8,128)(2,1)} %shard_map.88.block_hbm.b0_hbm), channel_id=1, source_target_pairs={{0,16},{8,24},{16,0},{24,8},{1,17},{9,25},{17,1},{25,9},{2,18},{10... | collective-permute-start | bytes 786440 | tf_op jit(solution)/shard_map/ppermute | solution.py:452
  27.6 0.0 collective-permute-start.7
  27.6 3.5 %shard_map.89 = bf16[32,32,256]{2,1,0:T(8,128)(2,1)} custom-call(bf16[2,128,512]{2,1,0:T(8,128)(2,1)} %shard_map.88.block_hbm.b0_hbm, bf16[1024,128]{1,0:T(8,128)(2,1)} %feats_hbm.3, bf16[2,256,1024]{2,1,0:T(8,128)(2,1)} %get-tuple-element.27.coef_hbm, f32[2,256,512]{2,1,0:T(8,128)} %get-tuple-element.28.offset_hbm), custom_call_target="tpu_custom_call" | custom-call | flops 1073741824 | bytes 3145728 | tf_op jit(solution)/shard_map/pallas_call | solution.py:437
  31.2 2.8 %shard_map.90 = (s32[8,512]{1,0:T(8,128)}, s32[8,512]{1,0:T(8,128)}, s32[8,128]{1,0:T(8,128)}) custom-call(s32[2,2048]{1,0:T(2,128)} %blocks_hbm.5), custom_call_target="tpu_custom_call" | custom-call | bytes 53248 | tf_op jit(solution)/shard_map/pallas_call | solution.py:437
  33.9 0.0 collective-permute-done.8.b2_hbm
  33.9 0.0 collective-permute-done.7.b1_hbm
  34.0 3.5 %all-to-all-start = ((bf16[32,32,256]{2,1,0:T(8,128)(2,1)}), bf16[32,32,256]{2,1,0:T(8,128)(2,1)}, u32[]{:S(2)}, u32[]{:S(2)}) async-start(bf16[32,32,256]{2,1,0:T(8,128)(2,1)} %shard_map.89), calls=%async_computation | async-start | bytes 1048576 | tf_op jit(solution)/shard_map/all_to_all | solution.py:532
  37.5 0.3 collective-permute-start.9
  37.8 1.6 %collective-permute-done.9.b3_hbm = bf16[2,128,512]{2,1,0:T(8,128)(2,1)} collective-permute-done((bf16[2,128,512]{2,1,0:T(8,128)(2,1)}, bf16[2,128,512]{2,1,0:T(8,128)(2,1)}, u32[]{:S(2)}, u32[]{:S(2)}) %collective-permute-start.9) | collective-permute-done | bytes 262176 | tf_op jit(solution)/shard_map/ppermute | solution.py:452
  39.4 10.4 %shard_map.91 = (bf16[2,512,2048]{2,1,0:T(8,128)(2,1)}, bf16[4,2048,512]{2,1,0:T(8,128)(2,1)}) custom-call(bf16[2,128,512]{2,1,0:T(8,128)(2,1)} %shard_map.88.block_hbm.b0_hbm, bf16[2,128,512]{2,1,0:T(8,128)(2,1)} %collective-permute-done.7.b1_hbm, bf16[2,128,512]{2,1,0:T(8,128)(2,1)} %collective-permute-done.8.b2_hbm, ...), custom_call_target="tpu_custom_call" | custom-call | flops 1610612736 | bytes 13668352 | tf_op jit(solution)/shard_map/pallas_call | solution.py:437
  49.8 3.8 %all-to-all-done.summed_hbm = bf16[32,32,256]{2,1,0:T(8,128)(2,1)} async-done(((bf16[32,32,256]{2,1,0:T(8,128)(2,1)}), bf16[32,32,256]{2,1,0:T(8,128)(2,1)}, u32[]{:S(2)}, u32[]{:S(2)}) %all-to-all-start) | async-done | bytes 524320 | tf_op jit(solution)/shard_map/all_to_all | solution.py:532
  53.6 7.1 %shard_map.92 = bf16[8,32,384]{2,1,0:T(8,128)(2,1)} custom-call(bf16[32,32,256]{2,1,0:T(8,128)(2,1)} %all-to-all-done.summed_hbm, bf16[2,512,2048]{2,1,0:T(8,128)(2,1)} %get-tuple-element.37.factor_hbm, bf16[2,512,512]{2,1,0:T(8,128)(2,1)} %core_hbm.1, bf16[4,2048,512]{2,1,0:T(8,128)(2,1)} %get-tuple-element.38.cross_hbm, s32[8,128]{1,0:T(8,128)} %get-tuple-element.39.starts_hbm), custom_call_target="tpu_custom_call" | custom-call | bytes 14356480 | tf_op jit(solution)/shard_map/pallas_call | solution.py:437
  60.8 12.1 %all_to_all.10.g0_hbm = bf16[8,32,384]{2,1,0:T(8,128)(2,1)} all-to-all(bf16[8,32,384]{2,1,0:T(8,128)(2,1)} %shard_map.92), channel_id=1, replica_groups=mesh['rows'=4,'pts'=8] {'pts'}, dimensions={0} | all-to-all | bytes 393216 | tf_op jit(solution)/shard_map/all_to_all | solution.py:567
  72.9 1.2 %collective-permute-start.11 = (bf16[8,32,384]{2,1,0:T(8,128)(2,1)}, bf16[8,32,384]{2,1,0:T(8,128)(2,1)}, u32[]{:S(2)}, u32[]{:S(2)}) collective-permute-start(bf16[8,32,384]{2,1,0:T(8,128)(2,1)} %all_to_all.10.g0_hbm), channel_id=1, source_target_pairs={{0,16},{8,24},{16,0},{24,8},{1,17},{9,25},{17,1},{25,9},{2,18},{10... | collective-permute-start | bytes 589832 | tf_op jit(solution)/shard_map/ppermute | solution.py:452
  74.0 0.0 collective-permute-start.10
  74.1 4.1 %shard_map.93.slots_hbm = s32[2,768]{1,0:T(2,128)} custom-call(s32[2,2048]{1,0:T(2,128)} %blocks_hbm.5), custom_call_target="tpu_custom_call" | custom-call | bytes 22528 | tf_op jit(solution)/shard_map/pallas_call | solution.py:437
  78.1 0.7 collective-permute-done.11.g2_hbm
  78.8 0.0 collective-permute-start.12
  78.9 0.0 collective-permute-done.10.g1_hbm
  78.9 1.8 %collective-permute-done.12.g3_hbm = bf16[8,32,384]{2,1,0:T(8,128)(2,1)} collective-permute-done((bf16[8,32,384]{2,1,0:T(8,128)(2,1)}, bf16[8,32,384]{2,1,0:T(8,128)(2,1)}, u32[]{:S(2)}, u32[]{:S(2)}) %collective-permute-start.12) | collective-permute-done | bytes 196640 | tf_op jit(solution)/shard_map/ppermute | solution.py:452
  80.6 4.1 %shard_map.94 = (f32[1024,256]{1,0:T(8,128)}, f32[1024,256]{1,0:T(8,128)}) custom-call(bf16[8,32,384]{2,1,0:T(8,128)(2,1)} %all_to_all.10.g0_hbm, bf16[8,32,384]{2,1,0:T(8,128)(2,1)} %collective-permute-done.10.g1_hbm, bf16[8,32,384]{2,1,0:T(8,128)(2,1)} %collective-permute-done.11.g2_hbm, bf16[8,32,384]{2,1,0:T(8,128)(2,1)} %collective-permute-done.12.g3_hbm, ...), custom_call_target="tpu_custom_call" | custom-call | bytes 4986880 | tf_op jit(solution)/shard_map/pallas_call | solution.py:437
Async XLA Ops:
  2.9 13.8 %collective-permute-start.2 = (bf16[384,128]{1,0:T(8,128)(2,1)}, bf16[384,128]{1,0:T(8,128)(2,1)}, u32[]{:S(2)}, u32[]{:S(2)}) collective-permute-start(bf16[384,128]{1,0:T(8,128)(2,1)} %shard_map.86.refs_0_), channel_id=1, source_target_pairs={{0,6},{1,7},{2,4},{3,5},{4,2},{5,3},{6,0},{7,1},{8,14},{9,15},{10,... | collective-permute-start | bytes 294920 | tf_op jit(solution)/shard_map/ppermute | solution.py:452
  8.0 8.7 %collective-permute-start.1 = (bf16[384,128]{1,0:T(8,128)(2,1)}, bf16[384,128]{1,0:T(8,128)(2,1)}, u32[]{:S(2)}, u32[]{:S(2)}) collective-permute-start(bf16[384,128]{1,0:T(8,128)(2,1)} %shard_map.86.refs_0_), channel_id=1, source_target_pairs={{0,2},{1,3},{2,0},{3,1},{4,6},{5,7},{6,4},{7,5},{8,10},{9,11},{10,... | collective-permute-start | bytes 294920 | tf_op jit(solution)/shard_map/ppermute | solution.py:452
  8.0 12.2 %collective-permute-start.5 = (bf16[384,128]{1,0:T(8,128)(2,1)}, bf16[384,128]{1,0:T(8,128)(2,1)}, u32[]{:S(2)}, u32[]{:S(2)}) collective-permute-start(bf16[384,128]{1,0:T(8,128)(2,1)} %shard_map.86.refs_0_), channel_id=1, source_target_pairs={{0,5},{1,4},{2,7},{3,6},{4,1},{5,0},{6,3},{7,2},{8,13},{9,12},{10,... | collective-permute-start | bytes 294920 | tf_op jit(solution)/shard_map/ppermute | solution.py:452
  9.8 11.1 %collective-permute-start.4 = (bf16[384,128]{1,0:T(8,128)(2,1)}, bf16[384,128]{1,0:T(8,128)(2,1)}, u32[]{:S(2)}, u32[]{:S(2)}) collective-permute-start(bf16[384,128]{1,0:T(8,128)(2,1)} %shard_map.86.refs_0_), channel_id=1, source_target_pairs={{0,4},{1,5},{2,6},{3,7},{4,0},{5,1},{6,2},{7,3},{8,12},{9,13},{10,... | collective-permute-start | bytes 294920 | tf_op jit(solution)/shard_map/ppermute | solution.py:452
  11.9 9.0 %collective-permute-start = (bf16[384,128]{1,0:T(8,128)(2,1)}, bf16[384,128]{1,0:T(8,128)(2,1)}, u32[]{:S(2)}, u32[]{:S(2)}) collective-permute-start(bf16[384,128]{1,0:T(8,128)(2,1)} %shard_map.86.refs_0_), channel_id=1, source_target_pairs={{0,1},{1,0},{2,3},{3,2},{4,5},{5,4},{6,7},{7,6},{8,9},{9,8},{10,11... | collective-permute-start | bytes 294920 | tf_op jit(solution)/shard_map/ppermute | solution.py:452
  16.7 6.1 %collective-permute-start.3 = (bf16[384,128]{1,0:T(8,128)(2,1)}, bf16[384,128]{1,0:T(8,128)(2,1)}, u32[]{:S(2)}, u32[]{:S(2)}) collective-permute-start(bf16[384,128]{1,0:T(8,128)(2,1)} %collective-permute-done.1.refs_2_), channel_id=1, source_target_pairs={{0,1},{1,0},{2,3},{3,2},{4,5},{5,4},{6,7},{7,6},{8,9},{9,8},{10,11... | collective-permute-start | bytes 294920 | tf_op jit(solution)/shard_map/ppermute | solution.py:452
  18.3 5.5 %collective-permute-start.6 = (bf16[384,128]{1,0:T(8,128)(2,1)}, bf16[384,128]{1,0:T(8,128)(2,1)}, u32[]{:S(2)}, u32[]{:S(2)}) collective-permute-start(bf16[384,128]{1,0:T(8,128)(2,1)} %collective-permute-done.2.refs_6_), channel_id=1, source_target_pairs={{0,1},{1,0},{2,3},{3,2},{4,5},{5,4},{6,7},{7,6},{8,9},{9,8},{10,11... | collective-permute-start | bytes 294920 | tf_op jit(solution)/shard_map/ppermute | solution.py:452
  26.1 7.9 %collective-permute-start.8 = (bf16[2,128,512]{2,1,0:T(8,128)(2,1)}, bf16[2,128,512]{2,1,0:T(8,128)(2,1)}, u32[]{:S(2)}, u32[]{:S(2)}) collective-permute-start(bf16[2,128,512]{2,1,0:T(8,128)(2,1)} %shard_map.88.block_hbm.b0_hbm), channel_id=1, source_target_pairs={{0,16},{8,24},{16,0},{24,8},{1,17},{9,25},{17,1},{25,9},{2,18},{10... | collective-permute-start | bytes 786440 | tf_op jit(solution)/shard_map/ppermute | solution.py:452
  27.6 6.3 %collective-permute-start.7 = (bf16[2,128,512]{2,1,0:T(8,128)(2,1)}, bf16[2,128,512]{2,1,0:T(8,128)(2,1)}, u32[]{:S(2)}, u32[]{:S(2)}) collective-permute-start(bf16[2,128,512]{2,1,0:T(8,128)(2,1)} %shard_map.88.block_hbm.b0_hbm), channel_id=1, source_target_pairs={{0,8},{8,0},{16,24},{24,16},{1,9},{9,1},{17,25},{25,17},{2,10},{10... | collective-permute-start | bytes 786440 | tf_op jit(solution)/shard_map/ppermute | solution.py:452
  34.0 19.7 %all-to-all-start = ((bf16[32,32,256]{2,1,0:T(8,128)(2,1)}), bf16[32,32,256]{2,1,0:T(8,128)(2,1)}, u32[]{:S(2)}, u32[]{:S(2)}) async-start(bf16[32,32,256]{2,1,0:T(8,128)(2,1)} %shard_map.89), calls=%async_computation | async-start | bytes 1048576 | tf_op jit(solution)/shard_map/all_to_all | solution.py:532
  37.5 1.9 %collective-permute-start.9 = (bf16[2,128,512]{2,1,0:T(8,128)(2,1)}, bf16[2,128,512]{2,1,0:T(8,128)(2,1)}, u32[]{:S(2)}, u32[]{:S(2)}) collective-permute-start(bf16[2,128,512]{2,1,0:T(8,128)(2,1)} %collective-permute-done.8.b2_hbm), channel_id=1, source_target_pairs={{0,8},{8,0},{16,24},{24,16},{1,9},{9,1},{17,25},{25,17},{2,10},{10... | collective-permute-start | bytes 786440 | tf_op jit(solution)/shard_map/ppermute | solution.py:452
  72.9 6.0 %collective-permute-start.11 = (bf16[8,32,384]{2,1,0:T(8,128)(2,1)}, bf16[8,32,384]{2,1,0:T(8,128)(2,1)}, u32[]{:S(2)}, u32[]{:S(2)}) collective-permute-start(bf16[8,32,384]{2,1,0:T(8,128)(2,1)} %all_to_all.10.g0_hbm), channel_id=1, source_target_pairs={{0,16},{8,24},{16,0},{24,8},{1,17},{9,25},{17,1},{25,9},{2,18},{10... | collective-permute-start | bytes 589832 | tf_op jit(solution)/shard_map/ppermute | solution.py:452
  74.0 4.8 %collective-permute-start.10 = (bf16[8,32,384]{2,1,0:T(8,128)(2,1)}, bf16[8,32,384]{2,1,0:T(8,128)(2,1)}, u32[]{:S(2)}, u32[]{:S(2)}) collective-permute-start(bf16[8,32,384]{2,1,0:T(8,128)(2,1)} %all_to_all.10.g0_hbm), channel_id=1, source_target_pairs={{0,8},{8,0},{16,24},{24,16},{1,9},{9,1},{17,25},{25,17},{2,10},{10... | collective-permute-start | bytes 589832 | tf_op jit(solution)/shard_map/ppermute | solution.py:452
  78.8 1.8 %collective-permute-start.12 = (bf16[8,32,384]{2,1,0:T(8,128)(2,1)}, bf16[8,32,384]{2,1,0:T(8,128)(2,1)}, u32[]{:S(2)}, u32[]{:S(2)}) collective-permute-start(bf16[8,32,384]{2,1,0:T(8,128)(2,1)} %collective-permute-done.11.g2_hbm), channel_id=1, source_target_pairs={{0,8},{8,0},{16,24},{24,16},{1,9},{9,1},{17,25},{25,17},{2,10},{10... | collective-permute-start | bytes 589832 | tf_op jit(solution)/shard_map/ppermute | solution.py:452

commit v21 on v20

--- a/solution.py
+++ b/solution.py
@@ -475,12 +475,14 @@
         sems=(2,),
     )
     came = {k: swap(packed, "pts", k) for k in (6, 5, 4, 2, 1)}
+    came[2], came[6], first_index = lax.optimization_barrier((came[2], came[6], block_index))
+    came[3], came[7] = swap(came[2], "pts", 1), swap(came[6], "pts", 1)
     kept = [
         like((UPDATES, outputs, points)),
         like((UPDATES, outputs, count), f32),
         like((8, 128), i32),
     ]
-    given = [block_index, coefficients, momentum, targets]
+    given = [first_index, coefficients, momentum, targets]
     coef, offset, row_starts = call(
         functools.partial(prepare_kernel, count, owners),
         kept,
@@ -488,8 +490,6 @@
         *given,
         sems=(4, 1 + 2 * UPDATES),
     )
-    came[2], came[6], row_starts = lax.optimization_barrier((came[2], came[6], row_starts))
-    came[3], came[7] = swap(came[2], "pts", 1), swap(came[6], "pts", 1)
     feats = like((UPDATES, width, count))
     inside_starts = pltpu.SMEM(row_starts.shape, i32)
     (mine,) = call(

time: 85.6 us -> 84.8 us (level)
  waiting for transfers between devices: 13 us -> 11.7 us
    ppermute x13, waiting for transfers between devices: 9.16 us -> 7.91 us  [swap(): lax.ppermute(value, axis, [(i, i ^ k) for i in range(lax.axis_size(axis))])]
  transfers between devices with their start and end apart: 14 -> 14, of which waited for: 8 -> 7; matrix products, arithmetic and copies ran while one was open for 0% -> 0% of each run, Pallas kernels for 29% -> 30%
where the time goes in v21:
time: 84.8 us; the launch traced here: 84.1 us
  Pallas kernels  40.7 us (48%)
  starting transfers between devices  18.7 us (22%)
  blocking collectives  12.1 us (14%)
  waiting for transfers between devices  11.7 us (14%)
  between operations  0.93 us (1%)
    pallas_call x9, Pallas kernels, call(): pl.pallas_call(body, out_shape=outs, in_specs=[VMEM] * near + [HBM] * (le...  40.7 us
    ppermute x13, starting transfers between devices, swap(): lax.ppermute(value, axis, [(i, i ^ k) for i in range(lax.axis_size(axis))])  14.4 us
    all_to_all x1, blocking collectives, with_kernels(): got = lax.all_to_all(steps, 'pts', 0, 0, tiled=True)  12.1 us
    ppermute x13, waiting for transfers between devices, swap(): lax.ppermute(value, axis, [(i, i ^ k) for i in range(lax.axis_size(axis))])  7.91 us
    all_to_all x1, starting transfers between devices, with_kernels(): summed = lax.all_to_all(pieces, ('rows', 'pts'), 0, 0, tiled=True)  4.28 us
    all_to_all x1, waiting for transfers between devices, with_kernels(): summed = lax.all_to_all(pieces, ('rows', 'pts'), 0, 0, tiled=True)  3.81 us
  transfers between devices with their start and end apart: 14, of which 7 were waited for; matrix products, arithmetic and copies ran while one was open for 0% of the time, Pallas kernels for 30%

profile of v21, /device:TPU:0, one launch (start us, length us, event | category | flops | bytes accessed | tf_op | source)
XLA Modules:
  0.0 84.1 jit_solution(292057561755544601)
XLA Ops:
  0.6 2.3 %shard_map.86.refs_0_ = bf16[384,128]{1,0:T(8,128)(2,1)} custom-call(s32[2,2048]{1,0:T(2,128)} %blocks_hbm.4, bf16[1024,128]{1,0:T(8,128)(2,1)} %feats_hbm.3), custom_call_target="tpu_custom_call" | custom-call | bytes 376832 | tf_op jit(solution)/shard_map/pallas_call | solution.py:437
  2.9 5.1 %collective-permute-start.2 = (bf16[384,128]{1,0:T(8,128)(2,1)}, bf16[384,128]{1,0:T(8,128)(2,1)}, u32[]{:S(2)}, u32[]{:S(2)}) collective-permute-start(bf16[384,128]{1,0:T(8,128)(2,1)} %shard_map.86.refs_0_), channel_id=1, source_target_pairs={{0,6},{1,7},{2,4},{3,5},{4,2},{5,3},{6,0},{7,1},{8,14},{9,15},{10,... | collective-permute-start | bytes 294920 | tf_op jit(solution)/shard_map/ppermute | solution.py:452
  8.0 0.0 collective-permute-start.1
  8.0 1.7 %collective-permute-start.5 = (bf16[384,128]{1,0:T(8,128)(2,1)}, bf16[384,128]{1,0:T(8,128)(2,1)}, u32[]{:S(2)}, u32[]{:S(2)}) collective-permute-start(bf16[384,128]{1,0:T(8,128)(2,1)} %shard_map.86.refs_0_), channel_id=1, source_target_pairs={{0,5},{1,4},{2,7},{3,6},{4,1},{5,0},{6,3},{7,2},{8,13},{9,12},{10,... | collective-permute-start | bytes 294920 | tf_op jit(solution)/shard_map/ppermute | solution.py:452
  9.8 2.1 %collective-permute-start.4 = (bf16[384,128]{1,0:T(8,128)(2,1)}, bf16[384,128]{1,0:T(8,128)(2,1)}, u32[]{:S(2)}, u32[]{:S(2)}) collective-permute-start(bf16[384,128]{1,0:T(8,128)(2,1)} %shard_map.86.refs_0_), channel_id=1, source_target_pairs={{0,4},{1,5},{2,6},{3,7},{4,0},{5,1},{6,2},{7,3},{8,12},{9,13},{10,... | collective-permute-start | bytes 294920 | tf_op jit(solution)/shard_map/ppermute | solution.py:452
  11.9 0.5 collective-permute-start
  12.4 0.0 collective-permute-done.2.refs_6_
  12.4 2.1 %collective-permute-done.1.refs_2_ = bf16[384,128]{1,0:T(8,128)(2,1)} collective-permute-done((bf16[384,128]{1,0:T(8,128)(2,1)}, bf16[384,128]{1,0:T(8,128)(2,1)}, u32[]{:S(2)}, u32[]{:S(2)}) %collective-permute-start.1) | collective-permute-done | bytes 98336 | tf_op jit(solution)/shard_map/ppermute | solution.py:452
  14.5 1.3 %collective-permute-start.3 = (bf16[384,128]{1,0:T(8,128)(2,1)}, bf16[384,128]{1,0:T(8,128)(2,1)}, u32[]{:S(2)}, u32[]{:S(2)}) collective-permute-start(bf16[384,128]{1,0:T(8,128)(2,1)} %collective-permute-done.1.refs_2_), channel_id=1, source_target_pairs={{0,1},{1,0},{2,3},{3,2},{4,5},{5,4},{6,7},{7,6},{8,9},{9,8},{10,11... | collective-permute-start | bytes 294920 | tf_op jit(solution)/shard_map/ppermute | solution.py:452
  15.9 0.7 collective-permute-start.6
  16.6 4.3 %shard_map.87 = (bf16[2,256,1024]{2,1,0:T(8,128)(2,1)}, f32[2,256,512]{2,1,0:T(8,128)}, s32[8,128]{1,0:T(8,128)}) custom-call(s32[2,2048]{1,0:T(2,128)} %blocks_hbm.4, f32[1024,256]{1,0:T(8,128)} %w_hbm.3, f32[1024,256]{1,0:T(8,128)} %z_hbm.3, bf16[1024,256]{1,0:T(8,128)(2,1)} %t_hbm.1), custom_call_target="tpu_custom_call" | custom-call | bytes 4739072 | tf_op jit(solution)/shard_map/pallas_call | solution.py:437
  20.8 0.0 collective-permute-done.5.refs_5_
  20.8 0.0 collective-permute-done.4.refs_4_
  20.8 0.0 collective-permute-done.refs_1_
  20.9 0.3 collective-permute-done.3.refs_3_
  21.2 1.1 %collective-permute-done.6.refs_7_ = bf16[384,128]{1,0:T(8,128)(2,1)} collective-permute-done((bf16[384,128]{1,0:T(8,128)(2,1)}, bf16[384,128]{1,0:T(8,128)(2,1)}, u32[]{:S(2)}, u32[]{:S(2)}) %collective-permute-start.6) | collective-permute-done | bytes 98336 | tf_op jit(solution)/shard_map/ppermute | solution.py:452
  22.2 2.3 %shard_map.88.block_hbm.b0_hbm = bf16[2,128,512]{2,1,0:T(8,128)(2,1)} custom-call(bf16[384,128]{1,0:T(8,128)(2,1)} %shard_map.86.refs_0_, bf16[384,128]{1,0:T(8,128)(2,1)} %collective-permute-done.refs_1_, bf16[384,128]{1,0:T(8,128)(2,1)} %collective-permute-done.1.refs_2_, bf16[384,128]{1,0:T(8,128)(2,1)} %collective-permute-done.3.refs_3_, ...), custom_call_target="tpu_custom_call" | custom-call | bytes 1052672 | tf_op jit(solution)/shard_map/pallas_call | solution.py:437
  24.5 1.6 %collective-permute-start.8 = (bf16[2,128,512]{2,1,0:T(8,128)(2,1)}, bf16[2,128,512]{2,1,0:T(8,128)(2,1)}, u32[]{:S(2)}, u32[]{:S(2)}) collective-permute-start(bf16[2,128,512]{2,1,0:T(8,128)(2,1)} %shard_map.88.block_hbm.b0_hbm), channel_id=1, source_target_pairs={{0,16},{8,24},{16,0},{24,8},{1,17},{9,25},{17,1},{25,9},{2,18},{10... | collective-permute-start | bytes 786440 | tf_op jit(solution)/shard_map/ppermute | solution.py:452
  26.1 0.0 collective-permute-start.7
  26.2 3.5 %shard_map.89 = bf16[32,32,256]{2,1,0:T(8,128)(2,1)} custom-call(bf16[2,128,512]{2,1,0:T(8,128)(2,1)} %shard_map.88.block_hbm.b0_hbm, bf16[1024,128]{1,0:T(8,128)(2,1)} %feats_hbm.3, bf16[2,256,1024]{2,1,0:T(8,128)(2,1)} %get-tuple-element.27.coef_hbm, f32[2,256,512]{2,1,0:T(8,128)} %get-tuple-element.28.offset_hbm), custom_call_target="tpu_custom_call" | custom-call | flops 1073741824 | bytes 3145728 | tf_op jit(solution)/shard_map/pallas_call | solution.py:437
  29.7 2.8 %shard_map.90 = (s32[8,512]{1,0:T(8,128)}, s32[8,512]{1,0:T(8,128)}, s32[8,128]{1,0:T(8,128)}) custom-call(s32[2,2048]{1,0:T(2,128)} %blocks_hbm.4), custom_call_target="tpu_custom_call" | custom-call | bytes 53248 | tf_op jit(solution)/shard_map/pallas_call | solution.py:437
  32.4 0.0 collective-permute-done.8.b2_hbm
  32.5 0.0 collective-permute-done.7.b1_hbm
  32.5 4.3 %all-to-all-start = ((bf16[32,32,256]{2,1,0:T(8,128)(2,1)}), bf16[32,32,256]{2,1,0:T(8,128)(2,1)}, u32[]{:S(2)}, u32[]{:S(2)}) async-start(bf16[32,32,256]{2,1,0:T(8,128)(2,1)} %shard_map.89), calls=%async_computation | async-start | bytes 1048576 | tf_op jit(solution)/shard_map/all_to_all | solution.py:532
  36.8 0.1 collective-permute-start.9
  36.8 1.9 %collective-permute-done.9.b3_hbm = bf16[2,128,512]{2,1,0:T(8,128)(2,1)} collective-permute-done((bf16[2,128,512]{2,1,0:T(8,128)(2,1)}, bf16[2,128,512]{2,1,0:T(8,128)(2,1)}, u32[]{:S(2)}, u32[]{:S(2)}) %collective-permute-start.9) | collective-permute-done | bytes 262176 | tf_op jit(solution)/shard_map/ppermute | solution.py:452
  38.7 10.4 %shard_map.91 = (bf16[2,512,2048]{2,1,0:T(8,128)(2,1)}, bf16[4,2048,512]{2,1,0:T(8,128)(2,1)}) custom-call(bf16[2,128,512]{2,1,0:T(8,128)(2,1)} %shard_map.88.block_hbm.b0_hbm, bf16[2,128,512]{2,1,0:T(8,128)(2,1)} %collective-permute-done.7.b1_hbm, bf16[2,128,512]{2,1,0:T(8,128)(2,1)} %collective-permute-done.8.b2_hbm, ...), custom_call_target="tpu_custom_call" | custom-call | flops 1610612736 | bytes 13668352 | tf_op jit(solution)/shard_map/pallas_call | solution.py:437
  49.1 3.8 %all-to-all-done.summed_hbm = bf16[32,32,256]{2,1,0:T(8,128)(2,1)} async-done(((bf16[32,32,256]{2,1,0:T(8,128)(2,1)}), bf16[32,32,256]{2,1,0:T(8,128)(2,1)}, u32[]{:S(2)}, u32[]{:S(2)}) %all-to-all-start) | async-done | bytes 524320 | tf_op jit(solution)/shard_map/all_to_all | solution.py:532
  52.9 7.1 %shard_map.92 = bf16[8,32,384]{2,1,0:T(8,128)(2,1)} custom-call(bf16[32,32,256]{2,1,0:T(8,128)(2,1)} %all-to-all-done.summed_hbm, bf16[2,512,2048]{2,1,0:T(8,128)(2,1)} %get-tuple-element.37.factor_hbm, bf16[2,512,512]{2,1,0:T(8,128)(2,1)} %core_hbm.1, bf16[4,2048,512]{2,1,0:T(8,128)(2,1)} %get-tuple-element.38.cross_hbm, s32[8,128]{1,0:T(8,128)} %get-tuple-element.39.starts_hbm), custom_call_target="tpu_custom_call" | custom-call | bytes 14356480 | tf_op jit(solution)/shard_map/pallas_call | solution.py:437
  60.0 12.1 %all_to_all.10.g0_hbm = bf16[8,32,384]{2,1,0:T(8,128)(2,1)} all-to-all(bf16[8,32,384]{2,1,0:T(8,128)(2,1)} %shard_map.92), channel_id=1, replica_groups=mesh['rows'=4,'pts'=8] {'pts'}, dimensions={0} | all-to-all | bytes 393216 | tf_op jit(solution)/shard_map/all_to_all | solution.py:567
  72.1 1.2 %collective-permute-start.11 = (bf16[8,32,384]{2,1,0:T(8,128)(2,1)}, bf16[8,32,384]{2,1,0:T(8,128)(2,1)}, u32[]{:S(2)}, u32[]{:S(2)}) collective-permute-start(bf16[8,32,384]{2,1,0:T(8,128)(2,1)} %all_to_all.10.g0_hbm), channel_id=1, source_target_pairs={{0,16},{8,24},{16,0},{24,8},{1,17},{9,25},{17,1},{25,9},{2,18},{10... | collective-permute-start | bytes 589832 | tf_op jit(solution)/shard_map/ppermute | solution.py:452
  73.3 0.0 collective-permute-start.10
  73.3 4.1 %shard_map.93.slots_hbm = s32[2,768]{1,0:T(2,128)} custom-call(s32[2,2048]{1,0:T(2,128)} %blocks_hbm.4), custom_call_target="tpu_custom_call" | custom-call | bytes 22528 | tf_op jit(solution)/shard_map/pallas_call | solution.py:437
  77.4 0.7 collective-permute-done.11.g2_hbm
  78.1 0.0 collective-permute-start.12
  78.1 0.0 collective-permute-done.10.g1_hbm
  78.1 1.8 %collective-permute-done.12.g3_hbm = bf16[8,32,384]{2,1,0:T(8,128)(2,1)} collective-permute-done((bf16[8,32,384]{2,1,0:T(8,128)(2,1)}, bf16[8,32,384]{2,1,0:T(8,128)(2,1)}, u32[]{:S(2)}, u32[]{:S(2)}) %collective-permute-start.12) | collective-permute-done | bytes 196640 | tf_op jit(solution)/shard_map/ppermute | solution.py:452
  79.9 4.1 %shard_map.94 = (f32[1024,256]{1,0:T(8,128)}, f32[1024,256]{1,0:T(8,128)}) custom-call(bf16[8,32,384]{2,1,0:T(8,128)(2,1)} %all_to_all.10.g0_hbm, bf16[8,32,384]{2,1,0:T(8,128)(2,1)} %collective-permute-done.10.g1_hbm, bf16[8,32,384]{2,1,0:T(8,128)(2,1)} %collective-permute-done.11.g2_hbm, bf16[8,32,384]{2,1,0:T(8,128)(2,1)} %collective-permute-done.12.g3_hbm, ...), custom_call_target="tpu_custom_call" | custom-call | bytes 4986880 | tf_op jit(solution)/shard_map/pallas_call | solution.py:437
Async XLA Ops:
  2.9 9.5 %collective-permute-start.2 = (bf16[384,128]{1,0:T(8,128)(2,1)}, bf16[384,128]{1,0:T(8,128)(2,1)}, u32[]{:S(2)}, u32[]{:S(2)}) collective-permute-start(bf16[384,128]{1,0:T(8,128)(2,1)} %shard_map.86.refs_0_), channel_id=1, source_target_pairs={{0,6},{1,7},{2,4},{3,5},{4,2},{5,3},{6,0},{7,1},{8,14},{9,15},{10,... | collective-permute-start | bytes 294920 | tf_op jit(solution)/shard_map/ppermute | solution.py:452
  8.0 6.5 %collective-permute-start.1 = (bf16[384,128]{1,0:T(8,128)(2,1)}, bf16[384,128]{1,0:T(8,128)(2,1)}, u32[]{:S(2)}, u32[]{:S(2)}) collective-permute-start(bf16[384,128]{1,0:T(8,128)(2,1)} %shard_map.86.refs_0_), channel_id=1, source_target_pairs={{0,2},{1,3},{2,0},{3,1},{4,6},{5,7},{6,4},{7,5},{8,10},{9,11},{10,... | collective-permute-start | bytes 294920 | tf_op jit(solution)/shard_map/ppermute | solution.py:452
  8.0 12.8 %collective-permute-start.5 = (bf16[384,128]{1,0:T(8,128)(2,1)}, bf16[384,128]{1,0:T(8,128)(2,1)}, u32[]{:S(2)}, u32[]{:S(2)}) collective-permute-start(bf16[384,128]{1,0:T(8,128)(2,1)} %shard_map.86.refs_0_), channel_id=1, source_target_pairs={{0,5},{1,4},{2,7},{3,6},{4,1},{5,0},{6,3},{7,2},{8,13},{9,12},{10,... | collective-permute-start | bytes 294920 | tf_op jit(solution)/shard_map/ppermute | solution.py:452
  9.8 11.1 %collective-permute-start.4 = (bf16[384,128]{1,0:T(8,128)(2,1)}, bf16[384,128]{1,0:T(8,128)(2,1)}, u32[]{:S(2)}, u32[]{:S(2)}) collective-permute-start(bf16[384,128]{1,0:T(8,128)(2,1)} %shard_map.86.refs_0_), channel_id=1, source_target_pairs={{0,4},{1,5},{2,6},{3,7},{4,0},{5,1},{6,2},{7,3},{8,12},{9,13},{10,... | collective-permute-start | bytes 294920 | tf_op jit(solution)/shard_map/ppermute | solution.py:452
  11.9 9.0 %collective-permute-start = (bf16[384,128]{1,0:T(8,128)(2,1)}, bf16[384,128]{1,0:T(8,128)(2,1)}, u32[]{:S(2)}, u32[]{:S(2)}) collective-permute-start(bf16[384,128]{1,0:T(8,128)(2,1)} %shard_map.86.refs_0_), channel_id=1, source_target_pairs={{0,1},{1,0},{2,3},{3,2},{4,5},{5,4},{6,7},{7,6},{8,9},{9,8},{10,11... | collective-permute-start | bytes 294920 | tf_op jit(solution)/shard_map/ppermute | solution.py:452
  14.5 6.7 %collective-permute-start.3 = (bf16[384,128]{1,0:T(8,128)(2,1)}, bf16[384,128]{1,0:T(8,128)(2,1)}, u32[]{:S(2)}, u32[]{:S(2)}) collective-permute-start(bf16[384,128]{1,0:T(8,128)(2,1)} %collective-permute-done.1.refs_2_), channel_id=1, source_target_pairs={{0,1},{1,0},{2,3},{3,2},{4,5},{5,4},{6,7},{7,6},{8,9},{9,8},{10,11... | collective-permute-start | bytes 294920 | tf_op jit(solution)/shard_map/ppermute | solution.py:452
  15.9 6.4 %collective-permute-start.6 = (bf16[384,128]{1,0:T(8,128)(2,1)}, bf16[384,128]{1,0:T(8,128)(2,1)}, u32[]{:S(2)}, u32[]{:S(2)}) collective-permute-start(bf16[384,128]{1,0:T(8,128)(2,1)} %collective-permute-done.2.refs_6_), channel_id=1, source_target_pairs={{0,1},{1,0},{2,3},{3,2},{4,5},{5,4},{6,7},{7,6},{8,9},{9,8},{10,11... | collective-permute-start | bytes 294920 | tf_op jit(solution)/shard_map/ppermute | solution.py:452
  24.5 7.9 %collective-permute-start.8 = (bf16[2,128,512]{2,1,0:T(8,128)(2,1)}, bf16[2,128,512]{2,1,0:T(8,128)(2,1)}, u32[]{:S(2)}, u32[]{:S(2)}) collective-permute-start(bf16[2,128,512]{2,1,0:T(8,128)(2,1)} %shard_map.88.block_hbm.b0_hbm), channel_id=1, source_target_pairs={{0,16},{8,24},{16,0},{24,8},{1,17},{9,25},{17,1},{25,9},{2,18},{10... | collective-permute-start | bytes 786440 | tf_op jit(solution)/shard_map/ppermute | solution.py:452
  26.1 6.3 %collective-permute-start.7 = (bf16[2,128,512]{2,1,0:T(8,128)(2,1)}, bf16[2,128,512]{2,1,0:T(8,128)(2,1)}, u32[]{:S(2)}, u32[]{:S(2)}) collective-permute-start(bf16[2,128,512]{2,1,0:T(8,128)(2,1)} %shard_map.88.block_hbm.b0_hbm), channel_id=1, source_target_pairs={{0,8},{8,0},{16,24},{24,16},{1,9},{9,1},{17,25},{25,17},{2,10},{10... | collective-permute-start | bytes 786440 | tf_op jit(solution)/shard_map/ppermute | solution.py:452
  32.5 20.4 %all-to-all-start = ((bf16[32,32,256]{2,1,0:T(8,128)(2,1)}), bf16[32,32,256]{2,1,0:T(8,128)(2,1)}, u32[]{:S(2)}, u32[]{:S(2)}) async-start(bf16[32,32,256]{2,1,0:T(8,128)(2,1)} %shard_map.89), calls=%async_computation | async-start | bytes 1048576 | tf_op jit(solution)/shard_map/all_to_all | solution.py:532
  36.8 1.9 %collective-permute-start.9 = (bf16[2,128,512]{2,1,0:T(8,128)(2,1)}, bf16[2,128,512]{2,1,0:T(8,128)(2,1)}, u32[]{:S(2)}, u32[]{:S(2)}) collective-permute-start(bf16[2,128,512]{2,1,0:T(8,128)(2,1)} %collective-permute-done.8.b2_hbm), channel_id=1, source_target_pairs={{0,8},{8,0},{16,24},{24,16},{1,9},{9,1},{17,25},{25,17},{2,10},{10... | collective-permute-start | bytes 786440 | tf_op jit(solution)/shard_map/ppermute | solution.py:452
  72.1 6.0 %collective-permute-start.11 = (bf16[8,32,384]{2,1,0:T(8,128)(2,1)}, bf16[8,32,384]{2,1,0:T(8,128)(2,1)}, u32[]{:S(2)}, u32[]{:S(2)}) collective-permute-start(bf16[8,32,384]{2,1,0:T(8,128)(2,1)} %all_to_all.10.g0_hbm), channel_id=1, source_target_pairs={{0,16},{8,24},{16,0},{24,8},{1,17},{9,25},{17,1},{25,9},{2,18},{10... | collective-permute-start | bytes 589832 | tf_op jit(solution)/shard_map/ppermute | solution.py:452
  73.3 4.8 %collective-permute-start.10 = (bf16[8,32,384]{2,1,0:T(8,128)(2,1)}, bf16[8,32,384]{2,1,0:T(8,128)(2,1)}, u32[]{:S(2)}, u32[]{:S(2)}) collective-permute-start(bf16[8,32,384]{2,1,0:T(8,128)(2,1)} %all_to_all.10.g0_hbm), channel_id=1, source_target_pairs={{0,8},{8,0},{16,24},{24,16},{1,9},{9,1},{17,25},{25,17},{2,10},{10... | collective-permute-start | bytes 589832 | tf_op jit(solution)/shard_map/ppermute | solution.py:452
  78.1 1.8 %collective-permute-start.12 = (bf16[8,32,384]{2,1,0:T(8,128)(2,1)}, bf16[8,32,384]{2,1,0:T(8,128)(2,1)}, u32[]{:S(2)}, u32[]{:S(2)}) collective-permute-start(bf16[8,32,384]{2,1,0:T(8,128)(2,1)} %collective-permute-done.11.g2_hbm), channel_id=1, source_target_pairs={{0,8},{8,0},{16,24},{24,16},{1,9},{9,1},{17,25},{25,17},{2,10},{10... | collective-permute-start | bytes 589832 | tf_op jit(solution)/shard_map/ppermute | solution.py:452

commit v22 on v21

--- a/solution.py
+++ b/solution.py
@@ -177,12 +177,7 @@
     wait_all(writes)
 
 
-def order_kernel(
-    count, points, owners,
-    blocks_hbm, ids_hbm, from_hbm, starts_hbm,
-    blocks, ids, came_from, starts, sems,
-):
-    wait_all(start_all([(blocks_hbm, blocks)], sems))
+def put_in_order(count, points, owners, blocks, ids, came_from, starts):
     count_of = blocks.shape[1] // count
     groups = [
         blocks[u : u + 1, g * count : (g + 1) * count]
@@ -197,7 +192,6 @@
         ids[n : n + 1, :] = from_digits(moved[0:2])
         came_from[n : n + 1, :] = from_digits(moved[2:4])
         starts[n : n + 1, :] = lane_row(start)
-    wait_all(start_all([(ids, ids_hbm), (came_from, from_hbm), (starts, starts_hbm)], sems))
 
 
 def slots_kernel(count, points, cap, blocks_hbm, slots_hbm, blocks, slots, sems):
@@ -262,19 +256,24 @@
 
 
 def sums_kernel(
-    block_hbm, feats_hbm, coef_hbm, offset_hbm, pieces_hbm,
-    block, feats, coef, offset, tile, pieces, sems,
+    owners,
+    block_hbm, feats_hbm, blocks_hbm, coef_hbm, offset_hbm,
+    pieces_hbm, ids_hbm, from_hbm, starts_hbm,
+    block, feats, blocks, coef, offset, tile, pieces, ids, came_from, starts, sems, out_sems,
 ):
     outputs = coef.shape[1]
-    pairs = [(block_hbm, block), (feats_hbm, feats), (coef_hbm, coef), (offset_hbm, offset)]
-    reads = start_all(pairs, sems)
-    wait_all(reads[:2])
+    pairs = [(block_hbm, block), (feats_hbm, feats), (blocks_hbm, blocks)]
+    reads = start_all([*pairs, (coef_hbm, coef), (offset_hbm, offset)], sems)
+    wait_all(reads[:3])
+    put_in_order(block.shape[2], feats.shape[0], owners, blocks, ids, came_from, starts)
+    pairs = [(ids, ids_hbm), (came_from, from_hbm), (starts, starts_hbm)]
+    writes = start_all(pairs, out_sems)
     left = extended(feats[...], 1, True)
     for u in range(UPDATES):
         right = extended(block[u], 0, False)
         tile[...] = jnp.exp2(exponent(left, right)).astype(bf16)
         if u == 0:
-            wait_all(reads[2:])
+            wait_all(reads[3:])
         total = offset[u] + mm(coef[u], tile[...], 1, 0)
         devices, _, lanes = pieces.shape
         own = outputs // devices
@@ -283,7 +282,7 @@
             pieces[d, 2 * own * u : 2 * own * (u + 1), :] = jnp.concatenate(
                 [part[:, :lanes], part[:, lanes:]], axis=0
             ).astype(bf16)
-    wait_all(start_all([(pieces, pieces_hbm)], sems))
+    wait_all(writes + start_all([(pieces, pieces_hbm)], sems))
 
 
 def factors_kernel(
@@ -507,28 +506,22 @@
         sems=(owners + 1,),
     )
     beside, across = swap(mine, "rows", 1), swap(mine, "rows", 2)
-    pieces = like((devices, deep, count // 2))
-    (pieces,) = call(
-        sums_kernel,
-        [pieces],
-        [feats, features, coef, offset, like((points, count)), pieces],
-        mine,
-        features,
-        coef,
-        offset,
-        sems=(4,),
+    kept = [
+        like((devices, deep, count // 2)),
+        like((UPDATES * rows, count), i32),
+        like((UPDATES * rows, count), i32),
+        like((8, 128), i32),
+    ]
+    given = [mine, features, block_index, coef, offset]
+    pieces, ids, came_from, starts = call(
+        functools.partial(sums_kernel, owners),
+        kept,
+        [*given, like((points, count)), *kept],
+        *given,
+        sems=(5, 3),
         flops=2.0 * UPDATES * points * count * (2 * width + outputs),
     )
-    pieces, later_index = lax.optimization_barrier((pieces, block_index))
-    kept = [like((UPDATES * rows, count), i32)] * 2 + [like((8, 128), i32)]
-    ids, came_from, starts = call(
-        functools.partial(order_kernel, count, points, owners),
-        kept,
-        [block_index, *kept],
-        later_index,
-        sems=(3,),
-    )
-    pieces, beside, across, ids = lax.optimization_barrier((pieces, beside, across, ids))
+    pieces, beside, across = lax.optimization_barrier((pieces, beside, across))
     summed = lax.all_to_all(pieces, ("rows", "pts"), 0, 0, tiled=True)
     kept = [like((UPDATES, rank, block)), like((rows, block, count))]
     factor, cross = call(

time: 84.8 us -> 84.8 us (level)
  Pallas kernels: 40.7 us -> 39.2 us
  starting transfers between devices: 18.7 us -> 19.6 us
    pallas_call x9 -> x8, Pallas kernels: 40.7 us -> 39.2 us  [call(): pl.pallas_call(body, out_shape=outs, in_specs=[VMEM] * near + [HBM] * (le...]
    all_to_all x1, starting transfers between devices: 4.28 us -> 5.18 us  [with_kernels(): summed = lax.all_to_all(pieces, ('rows', 'pts'), 0, 0, tiled=True)]
  transfers between devices with their start and end apart: 14 -> 14, of which waited for: 7 -> 8; matrix products, arithmetic and copies ran while one was open for 0% -> 0% of each run, Pallas kernels for 30% -> 28%
where the time goes in v22:
time: 84.8 us; the launch traced here: 84.1 us
  Pallas kernels  39.2 us (46%)
  starting transfers between devices  19.6 us (23%)
  waiting for transfers between devices  12.4 us (15%)
  blocking collectives  12.1 us (14%)
  between operations  0.91 us (1%)
    pallas_call x8, Pallas kernels, call(): pl.pallas_call(body, out_shape=outs, in_specs=[VMEM] * near + [HBM] * (le...  39.2 us
    ppermute x13, starting transfers between devices, swap(): lax.ppermute(value, axis, [(i, i ^ k) for i in range(lax.axis_size(axis))])  14.4 us
    all_to_all x1, blocking collectives, with_kernels(): got = lax.all_to_all(steps, 'pts', 0, 0, tiled=True)  12.1 us
    ppermute x13, waiting for transfers between devices, swap(): lax.ppermute(value, axis, [(i, i ^ k) for i in range(lax.axis_size(axis))])  8.56 us
    all_to_all x1, starting transfers between devices, with_kernels(): summed = lax.all_to_all(pieces, ('rows', 'pts'), 0, 0, tiled=True)  5.18 us
    all_to_all x1, waiting for transfers between devices, with_kernels(): summed = lax.all_to_all(pieces, ('rows', 'pts'), 0, 0, tiled=True)  3.81 us
  transfers between devices with their start and end apart: 14, of which 8 were waited for; matrix products, arithmetic and copies ran while one was open for 0% of the time, Pallas kernels for 28%

profile of v22, /device:TPU:0, one launch (start us, length us, event | category | flops | bytes accessed | tf_op | source)
XLA Modules:
  0.0 84.1 jit_solution(6139655931707116151)
XLA Ops:
  0.6 2.3 %shard_map.86.refs_0_ = bf16[384,128]{1,0:T(8,128)(2,1)} custom-call(s32[2,2048]{1,0:T(2,128)} %blocks_hbm.5, bf16[1024,128]{1,0:T(8,128)(2,1)} %feats_hbm.3), custom_call_target="tpu_custom_call" | custom-call | bytes 376832 | tf_op jit(solution)/shard_map/pallas_call | solution.py:436
  2.9 5.1 %collective-permute-start.2 = (bf16[384,128]{1,0:T(8,128)(2,1)}, bf16[384,128]{1,0:T(8,128)(2,1)}, u32[]{:S(2)}, u32[]{:S(2)}) collective-permute-start(bf16[384,128]{1,0:T(8,128)(2,1)} %shard_map.86.refs_0_), channel_id=1, source_target_pairs={{0,6},{1,7},{2,4},{3,5},{4,2},{5,3},{6,0},{7,1},{8,14},{9,15},{10,... | collective-permute-start | bytes 294920 | tf_op jit(solution)/shard_map/ppermute | solution.py:451
  8.0 0.0 collective-permute-start.1
  8.0 1.7 %collective-permute-start.5 = (bf16[384,128]{1,0:T(8,128)(2,1)}, bf16[384,128]{1,0:T(8,128)(2,1)}, u32[]{:S(2)}, u32[]{:S(2)}) collective-permute-start(bf16[384,128]{1,0:T(8,128)(2,1)} %shard_map.86.refs_0_), channel_id=1, source_target_pairs={{0,5},{1,4},{2,7},{3,6},{4,1},{5,0},{6,3},{7,2},{8,13},{9,12},{10,... | collective-permute-start | bytes 294920 | tf_op jit(solution)/shard_map/ppermute | solution.py:451
  9.8 2.1 %collective-permute-start.4 = (bf16[384,128]{1,0:T(8,128)(2,1)}, bf16[384,128]{1,0:T(8,128)(2,1)}, u32[]{:S(2)}, u32[]{:S(2)}) collective-permute-start(bf16[384,128]{1,0:T(8,128)(2,1)} %shard_map.86.refs_0_), channel_id=1, source_target_pairs={{0,4},{1,5},{2,6},{3,7},{4,0},{5,1},{6,2},{7,3},{8,12},{9,13},{10,... | collective-permute-start | bytes 294920 | tf_op jit(solution)/shard_map/ppermute | solution.py:451
  11.9 0.5 collective-permute-start
  12.4 0.0 collective-permute-done.2.refs_6_
  12.4 2.1 %collective-permute-done.1.refs_2_ = bf16[384,128]{1,0:T(8,128)(2,1)} collective-permute-done((bf16[384,128]{1,0:T(8,128)(2,1)}, bf16[384,128]{1,0:T(8,128)(2,1)}, u32[]{:S(2)}, u32[]{:S(2)}) %collective-permute-start.1) | collective-permute-done | bytes 98336 | tf_op jit(solution)/shard_map/ppermute | solution.py:451
  14.5 1.3 %collective-permute-start.3 = (bf16[384,128]{1,0:T(8,128)(2,1)}, bf16[384,128]{1,0:T(8,128)(2,1)}, u32[]{:S(2)}, u32[]{:S(2)}) collective-permute-start(bf16[384,128]{1,0:T(8,128)(2,1)} %collective-permute-done.1.refs_2_), channel_id=1, source_target_pairs={{0,1},{1,0},{2,3},{3,2},{4,5},{5,4},{6,7},{7,6},{8,9},{9,8},{10,11... | collective-permute-start | bytes 294920 | tf_op jit(solution)/shard_map/ppermute | solution.py:451
  15.9 0.7 collective-permute-start.6
  16.6 4.3 %shard_map.87 = (bf16[2,256,1024]{2,1,0:T(8,128)(2,1)}, f32[2,256,512]{2,1,0:T(8,128)}, s32[8,128]{1,0:T(8,128)}) custom-call(s32[2,2048]{1,0:T(2,128)} %blocks_hbm.5, f32[1024,256]{1,0:T(8,128)} %w_hbm.3, f32[1024,256]{1,0:T(8,128)} %z_hbm.3, bf16[1024,256]{1,0:T(8,128)(2,1)} %t_hbm.1), custom_call_target="tpu_custom_call" | custom-call | bytes 4739072 | tf_op jit(solution)/shard_map/pallas_call | solution.py:436
  20.8 0.0 collective-permute-done.5.refs_5_
  20.8 0.0 collective-permute-done.4.refs_4_
  20.8 0.0 collective-permute-done.refs_1_
  20.9 0.3 collective-permute-done.3.refs_3_
  21.2 1.1 %collective-permute-done.6.refs_7_ = bf16[384,128]{1,0:T(8,128)(2,1)} collective-permute-done((bf16[384,128]{1,0:T(8,128)(2,1)}, bf16[384,128]{1,0:T(8,128)(2,1)}, u32[]{:S(2)}, u32[]{:S(2)}) %collective-permute-start.6) | collective-permute-done | bytes 98336 | tf_op jit(solution)/shard_map/ppermute | solution.py:451
  22.2 2.3 %shard_map.88.block_hbm.b0_hbm = bf16[2,128,512]{2,1,0:T(8,128)(2,1)} custom-call(bf16[384,128]{1,0:T(8,128)(2,1)} %shard_map.86.refs_0_, bf16[384,128]{1,0:T(8,128)(2,1)} %collective-permute-done.refs_1_, bf16[384,128]{1,0:T(8,128)(2,1)} %collective-permute-done.1.refs_2_, bf16[384,128]{1,0:T(8,128)(2,1)} %collective-permute-done.3.refs_3_, ...), custom_call_target="tpu_custom_call" | custom-call | bytes 1052672 | tf_op jit(solution)/shard_map/pallas_call | solution.py:436
  24.5 1.6 %collective-permute-start.8 = (bf16[2,128,512]{2,1,0:T(8,128)(2,1)}, bf16[2,128,512]{2,1,0:T(8,128)(2,1)}, u32[]{:S(2)}, u32[]{:S(2)}) collective-permute-start(bf16[2,128,512]{2,1,0:T(8,128)(2,1)} %shard_map.88.block_hbm.b0_hbm), channel_id=1, source_target_pairs={{0,16},{8,24},{16,0},{24,8},{1,17},{9,25},{17,1},{25,9},{2,18},{10... | collective-permute-start | bytes 786440 | tf_op jit(solution)/shard_map/ppermute | solution.py:451
  26.1 0.0 collective-permute-start.7
  26.2 4.8 %shard_map.89 = (bf16[32,32,256]{2,1,0:T(8,128)(2,1)}, s32[8,512]{1,0:T(8,128)}, s32[8,512]{1,0:T(8,128)}, s32[8,128]{1,0:T(8,128)}) custom-call(bf16[2,128,512]{2,1,0:T(8,128)(2,1)} %shard_map.88.block_hbm.b0_hbm, bf16[1024,128]{1,0:T(8,128)(2,1)} %feats_hbm.3, s32[2,2048]{1,0:T(2,128)} %blocks_hbm.5, bf16[2,256,1024]{2,1,0:T(8,128)(2,1)} %get-tuple-element.25.coef_hbm, ...), custom_call_target="tpu_custom_call" | custom-call | flops 1073741824 | bytes 3198976 | tf_op jit(solution)/shard_map/pallas_call | solution.py:436
  30.9 0.6 collective-permute-done.8.b2_hbm
  31.6 0.0 collective-permute-done.7.b1_hbm
  31.6 5.2 %all-to-all-start = ((bf16[32,32,256]{2,1,0:T(8,128)(2,1)}), bf16[32,32,256]{2,1,0:T(8,128)(2,1)}, u32[]{:S(2)}, u32[]{:S(2)}) async-start(bf16[32,32,256]{2,1,0:T(8,128)(2,1)} %get-tuple-element.28), calls=%async_computation | async-start | bytes 1048576 | tf_op jit(solution)/shard_map/all_to_all | solution.py:525
  36.8 0.1 collective-permute-start.9
  36.8 1.9 %collective-permute-done.9.b3_hbm = bf16[2,128,512]{2,1,0:T(8,128)(2,1)} collective-permute-done((bf16[2,128,512]{2,1,0:T(8,128)(2,1)}, bf16[2,128,512]{2,1,0:T(8,128)(2,1)}, u32[]{:S(2)}, u32[]{:S(2)}) %collective-permute-start.9) | collective-permute-done | bytes 262176 | tf_op jit(solution)/shard_map/ppermute | solution.py:451
  38.7 10.4 %shard_map.90 = (bf16[2,512,2048]{2,1,0:T(8,128)(2,1)}, bf16[4,2048,512]{2,1,0:T(8,128)(2,1)}) custom-call(bf16[2,128,512]{2,1,0:T(8,128)(2,1)} %shard_map.88.block_hbm.b0_hbm, bf16[2,128,512]{2,1,0:T(8,128)(2,1)} %collective-permute-done.7.b1_hbm, bf16[2,128,512]{2,1,0:T(8,128)(2,1)} %collective-permute-done.8.b2_hbm, ...), custom_call_target="tpu_custom_call" | custom-call | flops 1610612736 | bytes 13668352 | tf_op jit(solution)/shard_map/pallas_call | solution.py:436
  49.1 3.8 %all-to-all-done.summed_hbm = bf16[32,32,256]{2,1,0:T(8,128)(2,1)} async-done(((bf16[32,32,256]{2,1,0:T(8,128)(2,1)}), bf16[32,32,256]{2,1,0:T(8,128)(2,1)}, u32[]{:S(2)}, u32[]{:S(2)}) %all-to-all-start) | async-done | bytes 524320 | tf_op jit(solution)/shard_map/all_to_all | solution.py:525
  52.9 7.1 %shard_map.91 = bf16[8,32,384]{2,1,0:T(8,128)(2,1)} custom-call(bf16[32,32,256]{2,1,0:T(8,128)(2,1)} %all-to-all-done.summed_hbm, bf16[2,512,2048]{2,1,0:T(8,128)(2,1)} %get-tuple-element.33.factor_hbm, bf16[2,512,512]{2,1,0:T(8,128)(2,1)} %core_hbm.1, bf16[4,2048,512]{2,1,0:T(8,128)(2,1)} %get-tuple-element.34.cross_hbm, s32[8,128]{1,0:T(8,128)} %get-tuple-element.35.starts_hbm), custom_call_target="tpu_custom_call" | custom-call | bytes 14356480 | tf_op jit(solution)/shard_map/pallas_call | solution.py:436
  60.0 12.1 %all_to_all.10.g0_hbm = bf16[8,32,384]{2,1,0:T(8,128)(2,1)} all-to-all(bf16[8,32,384]{2,1,0:T(8,128)(2,1)} %shard_map.91), channel_id=1, replica_groups=mesh['rows'=4,'pts'=8] {'pts'}, dimensions={0} | all-to-all | bytes 393216 | tf_op jit(solution)/shard_map/all_to_all | solution.py:560
  72.1 1.2 %collective-permute-start.11 = (bf16[8,32,384]{2,1,0:T(8,128)(2,1)}, bf16[8,32,384]{2,1,0:T(8,128)(2,1)}, u32[]{:S(2)}, u32[]{:S(2)}) collective-permute-start(bf16[8,32,384]{2,1,0:T(8,128)(2,1)} %all_to_all.10.g0_hbm), channel_id=1, source_target_pairs={{0,16},{8,24},{16,0},{24,8},{1,17},{9,25},{17,1},{25,9},{2,18},{10... | collective-permute-start | bytes 589832 | tf_op jit(solution)/shard_map/ppermute | solution.py:451
  73.3 0.0 collective-permute-start.10
  73.3 4.1 %shard_map.92.slots_hbm = s32[2,768]{1,0:T(2,128)} custom-call(s32[2,2048]{1,0:T(2,128)} %blocks_hbm.5), custom_call_target="tpu_custom_call" | custom-call | bytes 22528 | tf_op jit(solution)/shard_map/pallas_call | solution.py:436
  77.4 0.7 collective-permute-done.11.g2_hbm
  78.1 0.0 collective-permute-start.12
  78.1 0.0 collective-permute-done.10.g1_hbm
  78.1 1.8 %collective-permute-done.12.g3_hbm = bf16[8,32,384]{2,1,0:T(8,128)(2,1)} collective-permute-done((bf16[8,32,384]{2,1,0:T(8,128)(2,1)}, bf16[8,32,384]{2,1,0:T(8,128)(2,1)}, u32[]{:S(2)}, u32[]{:S(2)}) %collective-permute-start.12) | collective-permute-done | bytes 196640 | tf_op jit(solution)/shard_map/ppermute | solution.py:451
  79.9 4.1 %shard_map.93 = (f32[1024,256]{1,0:T(8,128)}, f32[1024,256]{1,0:T(8,128)}) custom-call(bf16[8,32,384]{2,1,0:T(8,128)(2,1)} %all_to_all.10.g0_hbm, bf16[8,32,384]{2,1,0:T(8,128)(2,1)} %collective-permute-done.10.g1_hbm, bf16[8,32,384]{2,1,0:T(8,128)(2,1)} %collective-permute-done.11.g2_hbm, bf16[8,32,384]{2,1,0:T(8,128)(2,1)} %collective-permute-done.12.g3_hbm, ...), custom_call_target="tpu_custom_call" | custom-call | bytes 4986880 | tf_op jit(solution)/shard_map/pallas_call | solution.py:436
Async XLA Ops:
  2.9 9.5 %collective-permute-start.2 = (bf16[384,128]{1,0:T(8,128)(2,1)}, bf16[384,128]{1,0:T(8,128)(2,1)}, u32[]{:S(2)}, u32[]{:S(2)}) collective-permute-start(bf16[384,128]{1,0:T(8,128)(2,1)} %shard_map.86.refs_0_), channel_id=1, source_target_pairs={{0,6},{1,7},{2,4},{3,5},{4,2},{5,3},{6,0},{7,1},{8,14},{9,15},{10,... | collective-permute-start | bytes 294920 | tf_op jit(solution)/shard_map/ppermute | solution.py:451
  8.0 6.5 %collective-permute-start.1 = (bf16[384,128]{1,0:T(8,128)(2,1)}, bf16[384,128]{1,0:T(8,128)(2,1)}, u32[]{:S(2)}, u32[]{:S(2)}) collective-permute-start(bf16[384,128]{1,0:T(8,128)(2,1)} %shard_map.86.refs_0_), channel_id=1, source_target_pairs={{0,2},{1,3},{2,0},{3,1},{4,6},{5,7},{6,4},{7,5},{8,10},{9,11},{10,... | collective-permute-start | bytes 294920 | tf_op jit(solution)/shard_map/ppermute | solution.py:451
  8.0 12.8 %collective-permute-start.5 = (bf16[384,128]{1,0:T(8,128)(2,1)}, bf16[384,128]{1,0:T(8,128)(2,1)}, u32[]{:S(2)}, u32[]{:S(2)}) collective-permute-start(bf16[384,128]{1,0:T(8,128)(2,1)} %shard_map.86.refs_0_), channel_id=1, source_target_pairs={{0,5},{1,4},{2,7},{3,6},{4,1},{5,0},{6,3},{7,2},{8,13},{9,12},{10,... | collective-permute-start | bytes 294920 | tf_op jit(solution)/shard_map/ppermute | solution.py:451
  9.8 11.1 %collective-permute-start.4 = (bf16[384,128]{1,0:T(8,128)(2,1)}, bf16[384,128]{1,0:T(8,128)(2,1)}, u32[]{:S(2)}, u32[]{:S(2)}) collective-permute-start(bf16[384,128]{1,0:T(8,128)(2,1)} %shard_map.86.refs_0_), channel_id=1, source_target_pairs={{0,4},{1,5},{2,6},{3,7},{4,0},{5,1},{6,2},{7,3},{8,12},{9,13},{10,... | collective-permute-start | bytes 294920 | tf_op jit(solution)/shard_map/ppermute | solution.py:451
  11.9 9.0 %collective-permute-start = (bf16[384,128]{1,0:T(8,128)(2,1)}, bf16[384,128]{1,0:T(8,128)(2,1)}, u32[]{:S(2)}, u32[]{:S(2)}) collective-permute-start(bf16[384,128]{1,0:T(8,128)(2,1)} %shard_map.86.refs_0_), channel_id=1, source_target_pairs={{0,1},{1,0},{2,3},{3,2},{4,5},{5,4},{6,7},{7,6},{8,9},{9,8},{10,11... | collective-permute-start | bytes 294920 | tf_op jit(solution)/shard_map/ppermute | solution.py:451
  14.5 6.7 %collective-permute-start.3 = (bf16[384,128]{1,0:T(8,128)(2,1)}, bf16[384,128]{1,0:T(8,128)(2,1)}, u32[]{:S(2)}, u32[]{:S(2)}) collective-permute-start(bf16[384,128]{1,0:T(8,128)(2,1)} %collective-permute-done.1.refs_2_), channel_id=1, source_target_pairs={{0,1},{1,0},{2,3},{3,2},{4,5},{5,4},{6,7},{7,6},{8,9},{9,8},{10,11... | collective-permute-start | bytes 294920 | tf_op jit(solution)/shard_map/ppermute | solution.py:451
  15.9 6.4 %collective-permute-start.6 = (bf16[384,128]{1,0:T(8,128)(2,1)}, bf16[384,128]{1,0:T(8,128)(2,1)}, u32[]{:S(2)}, u32[]{:S(2)}) collective-permute-start(bf16[384,128]{1,0:T(8,128)(2,1)} %collective-permute-done.2.refs_6_), channel_id=1, source_target_pairs={{0,1},{1,0},{2,3},{3,2},{4,5},{5,4},{6,7},{7,6},{8,9},{9,8},{10,11... | collective-permute-start | bytes 294920 | tf_op jit(solution)/shard_map/ppermute | solution.py:451
  24.5 7.1 %collective-permute-start.8 = (bf16[2,128,512]{2,1,0:T(8,128)(2,1)}, bf16[2,128,512]{2,1,0:T(8,128)(2,1)}, u32[]{:S(2)}, u32[]{:S(2)}) collective-permute-start(bf16[2,128,512]{2,1,0:T(8,128)(2,1)} %shard_map.88.block_hbm.b0_hbm), channel_id=1, source_target_pairs={{0,16},{8,24},{16,0},{24,8},{1,17},{9,25},{17,1},{25,9},{2,18},{10... | collective-permute-start | bytes 786440 | tf_op jit(solution)/shard_map/ppermute | solution.py:451
  26.1 5.4 %collective-permute-start.7 = (bf16[2,128,512]{2,1,0:T(8,128)(2,1)}, bf16[2,128,512]{2,1,0:T(8,128)(2,1)}, u32[]{:S(2)}, u32[]{:S(2)}) collective-permute-start(bf16[2,128,512]{2,1,0:T(8,128)(2,1)} %shard_map.88.block_hbm.b0_hbm), channel_id=1, source_target_pairs={{0,8},{8,0},{16,24},{24,16},{1,9},{9,1},{17,25},{25,17},{2,10},{10... | collective-permute-start | bytes 786440 | tf_op jit(solution)/shard_map/ppermute | solution.py:451
  31.6 21.3 %all-to-all-start = ((bf16[32,32,256]{2,1,0:T(8,128)(2,1)}), bf16[32,32,256]{2,1,0:T(8,128)(2,1)}, u32[]{:S(2)}, u32[]{:S(2)}) async-start(bf16[32,32,256]{2,1,0:T(8,128)(2,1)} %get-tuple-element.28), calls=%async_computation | async-start | bytes 1048576 | tf_op jit(solution)/shard_map/all_to_all | solution.py:525
  36.8 1.9 %collective-permute-start.9 = (bf16[2,128,512]{2,1,0:T(8,128)(2,1)}, bf16[2,128,512]{2,1,0:T(8,128)(2,1)}, u32[]{:S(2)}, u32[]{:S(2)}) collective-permute-start(bf16[2,128,512]{2,1,0:T(8,128)(2,1)} %collective-permute-done.8.b2_hbm), channel_id=1, source_target_pairs={{0,8},{8,0},{16,24},{24,16},{1,9},{9,1},{17,25},{25,17},{2,10},{10... | collective-permute-start | bytes 786440 | tf_op jit(solution)/shard_map/ppermute | solution.py:451
  72.1 6.0 %collective-permute-start.11 = (bf16[8,32,384]{2,1,0:T(8,128)(2,1)}, bf16[8,32,384]{2,1,0:T(8,128)(2,1)}, u32[]{:S(2)}, u32[]{:S(2)}) collective-permute-start(bf16[8,32,384]{2,1,0:T(8,128)(2,1)} %all_to_all.10.g0_hbm), channel_id=1, source_target_pairs={{0,16},{8,24},{16,0},{24,8},{1,17},{9,25},{17,1},{25,9},{2,18},{10... | collective-permute-start | bytes 589832 | tf_op jit(solution)/shard_map/ppermute | solution.py:451
  73.3 4.8 %collective-permute-start.10 = (bf16[8,32,384]{2,1,0:T(8,128)(2,1)}, bf16[8,32,384]{2,1,0:T(8,128)(2,1)}, u32[]{:S(2)}, u32[]{:S(2)}) collective-permute-start(bf16[8,32,384]{2,1,0:T(8,128)(2,1)} %all_to_all.10.g0_hbm), channel_id=1, source_target_pairs={{0,8},{8,0},{16,24},{24,16},{1,9},{9,1},{17,25},{25,17},{2,10},{10... | collective-permute-start | bytes 589832 | tf_op jit(solution)/shard_map/ppermute | solution.py:451
  78.1 1.8 %collective-permute-start.12 = (bf16[8,32,384]{2,1,0:T(8,128)(2,1)}, bf16[8,32,384]{2,1,0:T(8,128)(2,1)}, u32[]{:S(2)}, u32[]{:S(2)}) collective-permute-start(bf16[8,32,384]{2,1,0:T(8,128)(2,1)} %collective-permute-done.11.g2_hbm), channel_id=1, source_target_pairs={{0,8},{8,0},{16,24},{24,16},{1,9},{9,1},{17,25},{25,17},{2,10},{10... | collective-permute-start | bytes 589832 | tf_op jit(solution)/shard_map/ppermute | solution.py:451

commit v23 on v22

--- a/solution.py
+++ b/solution.py
@@ -239,20 +239,22 @@
 
 
 def compact_kernel(*refs):
-    *came_hbm, starts_hbm, block_hbm, came, starts, wide, block, sems = refs
+    *came_hbm, starts_hbm, block_hbm, came, starts, wide, block, sems, out_sems = refs
     me = lax.axis_index("pts")
     owners, deep, _ = came.shape
     cap = deep // UPDATES
     count = block.shape[2]
     pairs = [(a, came.at[k]) for k, a in enumerate(came_hbm)]
     wait_all(start_all([*pairs, (starts_hbm, starts)], sems))
+    writes = []
     for u in range(UPDATES):
         for o in range(owners):
             start = starts[u, o]
             rows = came[lax.bitwise_xor(me, o), u * cap : (u + 1) * cap, :]
             wide[u, pl.ds(start, cap), :] = rows.astype(f32)
         block[u] = wide[u, 0:count, :].T.astype(bf16)
-    wait_all(start_all([(block, block_hbm)], sems))
+        writes += start_all([(block.at[u], block_hbm.at[u])], out_sems.at[u : u + 1])
+    wait_all(writes)
 
 
 def sums_kernel(
@@ -401,11 +403,11 @@
         for h in range(2):
             first = own * (2 * u + h)
             part = wide[:, first : first + own, :].reshape(sources * own, lanes)
-            steps[u, h * lanes : (h + 1) * lanes, :] = part.T.astype(bf16)
+            steps[u, :, h * lanes : (h + 1) * lanes] = part.astype(bf16)
     changes = []
     for u in range(UPDATES):
         rows = one_hot(iota((points, slots.shape[1]), 0) == slots[u : u + 1, :])
-        changes.append(mm(rows, steps[u], 1, 0))
+        changes.append(mm(rows, steps[u], 1, 1))
     writes = []
     for n, c in enumerate(chunks):
         part = slice(c, c + CHUNK)
@@ -503,7 +505,7 @@
         packed,
         *[came[k] for k in range(1, owners)],
         row_starts,
-        sems=(owners + 1,),
+        sems=(owners + 1, UPDATES),
     )
     beside, across = swap(mine, "rows", 1), swap(mine, "rows", 2)
     kept = [
@@ -577,7 +579,7 @@
             slots,
             wide,
             wide,
-            like((UPDATES, rows * cap, outputs)),
+            like((UPDATES, outputs, rows * cap)),
             wide,
             wide,
         ],

time: 84.8 us -> 84.7 us (level)
  no operation moved by 1% of the time
where the time goes in v23:
time: 84.7 us; the launch traced here: 84.1 us
  Pallas kernels  39.1 us (46%)
  starting transfers between devices  19.6 us (23%)
  waiting for transfers between devices  12.4 us (15%)
  blocking collectives  12.1 us (14%)
  between operations  0.91 us (1%)
    pallas_call x8, Pallas kernels, call(): pl.pallas_call(body, out_shape=outs, in_specs=[VMEM] * near + [HBM] * (le...  39.1 us
    ppermute x13, starting transfers between devices, swap(): lax.ppermute(value, axis, [(i, i ^ k) for i in range(lax.axis_size(axis))])  14.4 us
    all_to_all x1, blocking collectives, with_kernels(): got = lax.all_to_all(steps, 'pts', 0, 0, tiled=True)  12.1 us
    ppermute x13, waiting for transfers between devices, swap(): lax.ppermute(value, axis, [(i, i ^ k) for i in range(lax.axis_size(axis))])  8.56 us
    all_to_all x1, starting transfers between devices, with_kernels(): summed = lax.all_to_all(pieces, ('rows', 'pts'), 0, 0, tiled=True)  5.18 us
    all_to_all x1, waiting for transfers between devices, with_kernels(): summed = lax.all_to_all(pieces, ('rows', 'pts'), 0, 0, tiled=True)  3.81 us
  transfers between devices with their start and end apart: 14, of which 8 were waited for; matrix products, arithmetic and copies ran while one was open for 0% of the time, Pallas kernels for 28%

profile of v23, /device:TPU:0, one launch (start us, length us, event | category | flops | bytes accessed | tf_op | source)
XLA Modules:
  0.0 84.1 jit_solution(4552888667185398662)
XLA Ops:
  0.6 2.3 %shard_map.86.refs_0_ = bf16[384,128]{1,0:T(8,128)(2,1)} custom-call(s32[2,2048]{1,0:T(2,128)} %blocks_hbm.5, bf16[1024,128]{1,0:T(8,128)(2,1)} %feats_hbm.3), custom_call_target="tpu_custom_call" | custom-call | bytes 376832 | tf_op jit(solution)/shard_map/pallas_call | solution.py:438
  2.9 5.1 %collective-permute-start.2 = (bf16[384,128]{1,0:T(8,128)(2,1)}, bf16[384,128]{1,0:T(8,128)(2,1)}, u32[]{:S(2)}, u32[]{:S(2)}) collective-permute-start(bf16[384,128]{1,0:T(8,128)(2,1)} %shard_map.86.refs_0_), channel_id=1, source_target_pairs={{0,6},{1,7},{2,4},{3,5},{4,2},{5,3},{6,0},{7,1},{8,14},{9,15},{10,... | collective-permute-start | bytes 294920 | tf_op jit(solution)/shard_map/ppermute | solution.py:453
  8.0 0.0 collective-permute-start.1
  8.0 1.7 %collective-permute-start.5 = (bf16[384,128]{1,0:T(8,128)(2,1)}, bf16[384,128]{1,0:T(8,128)(2,1)}, u32[]{:S(2)}, u32[]{:S(2)}) collective-permute-start(bf16[384,128]{1,0:T(8,128)(2,1)} %shard_map.86.refs_0_), channel_id=1, source_target_pairs={{0,5},{1,4},{2,7},{3,6},{4,1},{5,0},{6,3},{7,2},{8,13},{9,12},{10,... | collective-permute-start | bytes 294920 | tf_op jit(solution)/shard_map/ppermute | solution.py:453
  9.8 2.1 %collective-permute-start.4 = (bf16[384,128]{1,0:T(8,128)(2,1)}, bf16[384,128]{1,0:T(8,128)(2,1)}, u32[]{:S(2)}, u32[]{:S(2)}) collective-permute-start(bf16[384,128]{1,0:T(8,128)(2,1)} %shard_map.86.refs_0_), channel_id=1, source_target_pairs={{0,4},{1,5},{2,6},{3,7},{4,0},{5,1},{6,2},{7,3},{8,12},{9,13},{10,... | collective-permute-start | bytes 294920 | tf_op jit(solution)/shard_map/ppermute | solution.py:453
  11.9 0.5 collective-permute-start
  12.4 0.0 collective-permute-done.2.refs_6_
  12.4 2.1 %collective-permute-done.1.refs_2_ = bf16[384,128]{1,0:T(8,128)(2,1)} collective-permute-done((bf16[384,128]{1,0:T(8,128)(2,1)}, bf16[384,128]{1,0:T(8,128)(2,1)}, u32[]{:S(2)}, u32[]{:S(2)}) %collective-permute-start.1) | collective-permute-done | bytes 98336 | tf_op jit(solution)/shard_map/ppermute | solution.py:453
  14.5 1.3 %collective-permute-start.3 = (bf16[384,128]{1,0:T(8,128)(2,1)}, bf16[384,128]{1,0:T(8,128)(2,1)}, u32[]{:S(2)}, u32[]{:S(2)}) collective-permute-start(bf16[384,128]{1,0:T(8,128)(2,1)} %collective-permute-done.1.refs_2_), channel_id=1, source_target_pairs={{0,1},{1,0},{2,3},{3,2},{4,5},{5,4},{6,7},{7,6},{8,9},{9,8},{10,11... | collective-permute-start | bytes 294920 | tf_op jit(solution)/shard_map/ppermute | solution.py:453
  15.9 0.7 collective-permute-start.6
  16.6 4.3 %shard_map.87 = (bf16[2,256,1024]{2,1,0:T(8,128)(2,1)}, f32[2,256,512]{2,1,0:T(8,128)}, s32[8,128]{1,0:T(8,128)}) custom-call(s32[2,2048]{1,0:T(2,128)} %blocks_hbm.5, f32[1024,256]{1,0:T(8,128)} %w_hbm.3, f32[1024,256]{1,0:T(8,128)} %z_hbm.3, bf16[1024,256]{1,0:T(8,128)(2,1)} %t_hbm.1), custom_call_target="tpu_custom_call" | custom-call | bytes 4739072 | tf_op jit(solution)/shard_map/pallas_call | solution.py:438
  20.8 0.0 collective-permute-done.5.refs_5_
  20.8 0.0 collective-permute-done.4.refs_4_
  20.8 0.0 collective-permute-done.refs_1_
  20.9 0.3 collective-permute-done.3.refs_3_
  21.2 1.1 %collective-permute-done.6.refs_7_ = bf16[384,128]{1,0:T(8,128)(2,1)} collective-permute-done((bf16[384,128]{1,0:T(8,128)(2,1)}, bf16[384,128]{1,0:T(8,128)(2,1)}, u32[]{:S(2)}, u32[]{:S(2)}) %collective-permute-start.6) | collective-permute-done | bytes 98336 | tf_op jit(solution)/shard_map/ppermute | solution.py:453
  22.2 2.2 %shard_map.88.block_hbm.b0_hbm = bf16[2,128,512]{2,1,0:T(8,128)(2,1)} custom-call(bf16[384,128]{1,0:T(8,128)(2,1)} %shard_map.86.refs_0_, bf16[384,128]{1,0:T(8,128)(2,1)} %collective-permute-done.refs_1_, bf16[384,128]{1,0:T(8,128)(2,1)} %collective-permute-done.1.refs_2_, bf16[384,128]{1,0:T(8,128)(2,1)} %collective-permute-done.3.refs_3_, ...), custom_call_target="tpu_custom_call" | custom-call | bytes 1052672 | tf_op jit(solution)/shard_map/pallas_call | solution.py:438
  24.5 1.6 %collective-permute-start.8 = (bf16[2,128,512]{2,1,0:T(8,128)(2,1)}, bf16[2,128,512]{2,1,0:T(8,128)(2,1)}, u32[]{:S(2)}, u32[]{:S(2)}) collective-permute-start(bf16[2,128,512]{2,1,0:T(8,128)(2,1)} %shard_map.88.block_hbm.b0_hbm), channel_id=1, source_target_pairs={{0,16},{8,24},{16,0},{24,8},{1,17},{9,25},{17,1},{25,9},{2,18},{10... | collective-permute-start | bytes 786440 | tf_op jit(solution)/shard_map/ppermute | solution.py:453
  26.1 0.0 collective-permute-start.7
  26.1 4.8 %shard_map.89 = (bf16[32,32,256]{2,1,0:T(8,128)(2,1)}, s32[8,512]{1,0:T(8,128)}, s32[8,512]{1,0:T(8,128)}, s32[8,128]{1,0:T(8,128)}) custom-call(bf16[2,128,512]{2,1,0:T(8,128)(2,1)} %shard_map.88.block_hbm.b0_hbm, bf16[1024,128]{1,0:T(8,128)(2,1)} %feats_hbm.3, s32[2,2048]{1,0:T(2,128)} %blocks_hbm.5, bf16[2,256,1024]{2,1,0:T(8,128)(2,1)} %get-tuple-element.25.coef_hbm, ...), custom_call_target="tpu_custom_call" | custom-call | flops 1073741824 | bytes 3198976 | tf_op jit(solution)/shard_map/pallas_call | solution.py:438
  30.9 0.6 collective-permute-done.8.b2_hbm
  31.6 0.0 collective-permute-done.7.b1_hbm
  31.6 5.2 %all-to-all-start = ((bf16[32,32,256]{2,1,0:T(8,128)(2,1)}), bf16[32,32,256]{2,1,0:T(8,128)(2,1)}, u32[]{:S(2)}, u32[]{:S(2)}) async-start(bf16[32,32,256]{2,1,0:T(8,128)(2,1)} %get-tuple-element.28), calls=%async_computation | async-start | bytes 1048576 | tf_op jit(solution)/shard_map/all_to_all | solution.py:527
  36.7 0.1 collective-permute-start.9
  36.8 1.9 %collective-permute-done.9.b3_hbm = bf16[2,128,512]{2,1,0:T(8,128)(2,1)} collective-permute-done((bf16[2,128,512]{2,1,0:T(8,128)(2,1)}, bf16[2,128,512]{2,1,0:T(8,128)(2,1)}, u32[]{:S(2)}, u32[]{:S(2)}) %collective-permute-start.9) | collective-permute-done | bytes 262176 | tf_op jit(solution)/shard_map/ppermute | solution.py:453
  38.7 10.4 %shard_map.90 = (bf16[2,512,2048]{2,1,0:T(8,128)(2,1)}, bf16[4,2048,512]{2,1,0:T(8,128)(2,1)}) custom-call(bf16[2,128,512]{2,1,0:T(8,128)(2,1)} %shard_map.88.block_hbm.b0_hbm, bf16[2,128,512]{2,1,0:T(8,128)(2,1)} %collective-permute-done.7.b1_hbm, bf16[2,128,512]{2,1,0:T(8,128)(2,1)} %collective-permute-done.8.b2_hbm, ...), custom_call_target="tpu_custom_call" | custom-call | flops 1610612736 | bytes 13668352 | tf_op jit(solution)/shard_map/pallas_call | solution.py:438
  49.1 3.8 %all-to-all-done.summed_hbm = bf16[32,32,256]{2,1,0:T(8,128)(2,1)} async-done(((bf16[32,32,256]{2,1,0:T(8,128)(2,1)}), bf16[32,32,256]{2,1,0:T(8,128)(2,1)}, u32[]{:S(2)}, u32[]{:S(2)}) %all-to-all-start) | async-done | bytes 524320 | tf_op jit(solution)/shard_map/all_to_all | solution.py:527
  52.9 7.1 %shard_map.91 = bf16[8,32,384]{2,1,0:T(8,128)(2,1)} custom-call(bf16[32,32,256]{2,1,0:T(8,128)(2,1)} %all-to-all-done.summed_hbm, bf16[2,512,2048]{2,1,0:T(8,128)(2,1)} %get-tuple-element.33.factor_hbm, bf16[2,512,512]{2,1,0:T(8,128)(2,1)} %core_hbm.1, bf16[4,2048,512]{2,1,0:T(8,128)(2,1)} %get-tuple-element.34.cross_hbm, s32[8,128]{1,0:T(8,128)} %get-tuple-element.35.starts_hbm), custom_call_target="tpu_custom_call" | custom-call | bytes 14356480 | tf_op jit(solution)/shard_map/pallas_call | solution.py:438
  60.0 12.1 %all_to_all.10.g0_hbm = bf16[8,32,384]{2,1,0:T(8,128)(2,1)} all-to-all(bf16[8,32,384]{2,1,0:T(8,128)(2,1)} %shard_map.91), channel_id=1, replica_groups=mesh['rows'=4,'pts'=8] {'pts'}, dimensions={0} | all-to-all | bytes 393216 | tf_op jit(solution)/shard_map/all_to_all | solution.py:562
  72.1 1.2 %collective-permute-start.11 = (bf16[8,32,384]{2,1,0:T(8,128)(2,1)}, bf16[8,32,384]{2,1,0:T(8,128)(2,1)}, u32[]{:S(2)}, u32[]{:S(2)}) collective-permute-start(bf16[8,32,384]{2,1,0:T(8,128)(2,1)} %all_to_all.10.g0_hbm), channel_id=1, source_target_pairs={{0,16},{8,24},{16,0},{24,8},{1,17},{9,25},{17,1},{25,9},{2,18},{10... | collective-permute-start | bytes 589832 | tf_op jit(solution)/shard_map/ppermute | solution.py:453
  73.3 0.0 collective-permute-start.10
  73.3 4.1 %shard_map.92.slots_hbm = s32[2,768]{1,0:T(2,128)} custom-call(s32[2,2048]{1,0:T(2,128)} %blocks_hbm.5), custom_call_target="tpu_custom_call" | custom-call | bytes 22528 | tf_op jit(solution)/shard_map/pallas_call | solution.py:438
  77.4 0.7 collective-permute-done.11.g2_hbm
  78.1 0.0 collective-permute-start.12
  78.1 0.0 collective-permute-done.10.g1_hbm
  78.1 1.8 %collective-permute-done.12.g3_hbm = bf16[8,32,384]{2,1,0:T(8,128)(2,1)} collective-permute-done((bf16[8,32,384]{2,1,0:T(8,128)(2,1)}, bf16[8,32,384]{2,1,0:T(8,128)(2,1)}, u32[]{:S(2)}, u32[]{:S(2)}) %collective-permute-start.12) | collective-permute-done | bytes 196640 | tf_op jit(solution)/shard_map/ppermute | solution.py:453
  79.9 4.0 %shard_map.93 = (f32[1024,256]{1,0:T(8,128)}, f32[1024,256]{1,0:T(8,128)}) custom-call(bf16[8,32,384]{2,1,0:T(8,128)(2,1)} %all_to_all.10.g0_hbm, bf16[8,32,384]{2,1,0:T(8,128)(2,1)} %collective-permute-done.10.g1_hbm, bf16[8,32,384]{2,1,0:T(8,128)(2,1)} %collective-permute-done.11.g2_hbm, bf16[8,32,384]{2,1,0:T(8,128)(2,1)} %collective-permute-done.12.g3_hbm, ...), custom_call_target="tpu_custom_call" | custom-call | bytes 4986880 | tf_op jit(solution)/shard_map/pallas_call | solution.py:438
Async XLA Ops:
  2.9 9.5 %collective-permute-start.2 = (bf16[384,128]{1,0:T(8,128)(2,1)}, bf16[384,128]{1,0:T(8,128)(2,1)}, u32[]{:S(2)}, u32[]{:S(2)}) collective-permute-start(bf16[384,128]{1,0:T(8,128)(2,1)} %shard_map.86.refs_0_), channel_id=1, source_target_pairs={{0,6},{1,7},{2,4},{3,5},{4,2},{5,3},{6,0},{7,1},{8,14},{9,15},{10,... | collective-permute-start | bytes 294920 | tf_op jit(solution)/shard_map/ppermute | solution.py:453
  8.0 6.5 %collective-permute-start.1 = (bf16[384,128]{1,0:T(8,128)(2,1)}, bf16[384,128]{1,0:T(8,128)(2,1)}, u32[]{:S(2)}, u32[]{:S(2)}) collective-permute-start(bf16[384,128]{1,0:T(8,128)(2,1)} %shard_map.86.refs_0_), channel_id=1, source_target_pairs={{0,2},{1,3},{2,0},{3,1},{4,6},{5,7},{6,4},{7,5},{8,10},{9,11},{10,... | collective-permute-start | bytes 294920 | tf_op jit(solution)/shard_map/ppermute | solution.py:453
  8.0 12.8 %collective-permute-start.5 = (bf16[384,128]{1,0:T(8,128)(2,1)}, bf16[384,128]{1,0:T(8,128)(2,1)}, u32[]{:S(2)}, u32[]{:S(2)}) collective-permute-start(bf16[384,128]{1,0:T(8,128)(2,1)} %shard_map.86.refs_0_), channel_id=1, source_target_pairs={{0,5},{1,4},{2,7},{3,6},{4,1},{5,0},{6,3},{7,2},{8,13},{9,12},{10,... | collective-permute-start | bytes 294920 | tf_op jit(solution)/shard_map/ppermute | solution.py:453
  9.8 11.1 %collective-permute-start.4 = (bf16[384,128]{1,0:T(8,128)(2,1)}, bf16[384,128]{1,0:T(8,128)(2,1)}, u32[]{:S(2)}, u32[]{:S(2)}) collective-permute-start(bf16[384,128]{1,0:T(8,128)(2,1)} %shard_map.86.refs_0_), channel_id=1, source_target_pairs={{0,4},{1,5},{2,6},{3,7},{4,0},{5,1},{6,2},{7,3},{8,12},{9,13},{10,... | collective-permute-start | bytes 294920 | tf_op jit(solution)/shard_map/ppermute | solution.py:453
  11.9 9.0 %collective-permute-start = (bf16[384,128]{1,0:T(8,128)(2,1)}, bf16[384,128]{1,0:T(8,128)(2,1)}, u32[]{:S(2)}, u32[]{:S(2)}) collective-permute-start(bf16[384,128]{1,0:T(8,128)(2,1)} %shard_map.86.refs_0_), channel_id=1, source_target_pairs={{0,1},{1,0},{2,3},{3,2},{4,5},{5,4},{6,7},{7,6},{8,9},{9,8},{10,11... | collective-permute-start | bytes 294920 | tf_op jit(solution)/shard_map/ppermute | solution.py:453
  14.5 6.7 %collective-permute-start.3 = (bf16[384,128]{1,0:T(8,128)(2,1)}, bf16[384,128]{1,0:T(8,128)(2,1)}, u32[]{:S(2)}, u32[]{:S(2)}) collective-permute-start(bf16[384,128]{1,0:T(8,128)(2,1)} %collective-permute-done.1.refs_2_), channel_id=1, source_target_pairs={{0,1},{1,0},{2,3},{3,2},{4,5},{5,4},{6,7},{7,6},{8,9},{9,8},{10,11... | collective-permute-start | bytes 294920 | tf_op jit(solution)/shard_map/ppermute | solution.py:453
  15.9 6.4 %collective-permute-start.6 = (bf16[384,128]{1,0:T(8,128)(2,1)}, bf16[384,128]{1,0:T(8,128)(2,1)}, u32[]{:S(2)}, u32[]{:S(2)}) collective-permute-start(bf16[384,128]{1,0:T(8,128)(2,1)} %collective-permute-done.2.refs_6_), channel_id=1, source_target_pairs={{0,1},{1,0},{2,3},{3,2},{4,5},{5,4},{6,7},{7,6},{8,9},{9,8},{10,11... | collective-permute-start | bytes 294920 | tf_op jit(solution)/shard_map/ppermute | solution.py:453
  24.5 7.1 %collective-permute-start.8 = (bf16[2,128,512]{2,1,0:T(8,128)(2,1)}, bf16[2,128,512]{2,1,0:T(8,128)(2,1)}, u32[]{:S(2)}, u32[]{:S(2)}) collective-permute-start(bf16[2,128,512]{2,1,0:T(8,128)(2,1)} %shard_map.88.block_hbm.b0_hbm), channel_id=1, source_target_pairs={{0,16},{8,24},{16,0},{24,8},{1,17},{9,25},{17,1},{25,9},{2,18},{10... | collective-permute-start | bytes 786440 | tf_op jit(solution)/shard_map/ppermute | solution.py:453
  26.1 5.4 %collective-permute-start.7 = (bf16[2,128,512]{2,1,0:T(8,128)(2,1)}, bf16[2,128,512]{2,1,0:T(8,128)(2,1)}, u32[]{:S(2)}, u32[]{:S(2)}) collective-permute-start(bf16[2,128,512]{2,1,0:T(8,128)(2,1)} %shard_map.88.block_hbm.b0_hbm), channel_id=1, source_target_pairs={{0,8},{8,0},{16,24},{24,16},{1,9},{9,1},{17,25},{25,17},{2,10},{10... | collective-permute-start | bytes 786440 | tf_op jit(solution)/shard_map/ppermute | solution.py:453
  31.6 21.3 %all-to-all-start = ((bf16[32,32,256]{2,1,0:T(8,128)(2,1)}), bf16[32,32,256]{2,1,0:T(8,128)(2,1)}, u32[]{:S(2)}, u32[]{:S(2)}) async-start(bf16[32,32,256]{2,1,0:T(8,128)(2,1)} %get-tuple-element.28), calls=%async_computation | async-start | bytes 1048576 | tf_op jit(solution)/shard_map/all_to_all | solution.py:527
  36.7 1.9 %collective-permute-start.9 = (bf16[2,128,512]{2,1,0:T(8,128)(2,1)}, bf16[2,128,512]{2,1,0:T(8,128)(2,1)}, u32[]{:S(2)}, u32[]{:S(2)}) collective-permute-start(bf16[2,128,512]{2,1,0:T(8,128)(2,1)} %collective-permute-done.8.b2_hbm), channel_id=1, source_target_pairs={{0,8},{8,0},{16,24},{24,16},{1,9},{9,1},{17,25},{25,17},{2,10},{10... | collective-permute-start | bytes 786440 | tf_op jit(solution)/shard_map/ppermute | solution.py:453
  72.1 6.0 %collective-permute-start.11 = (bf16[8,32,384]{2,1,0:T(8,128)(2,1)}, bf16[8,32,384]{2,1,0:T(8,128)(2,1)}, u32[]{:S(2)}, u32[]{:S(2)}) collective-permute-start(bf16[8,32,384]{2,1,0:T(8,128)(2,1)} %all_to_all.10.g0_hbm), channel_id=1, source_target_pairs={{0,16},{8,24},{16,0},{24,8},{1,17},{9,25},{17,1},{25,9},{2,18},{10... | collective-permute-start | bytes 589832 | tf_op jit(solution)/shard_map/ppermute | solution.py:453
  73.3 4.8 %collective-permute-start.10 = (bf16[8,32,384]{2,1,0:T(8,128)(2,1)}, bf16[8,32,384]{2,1,0:T(8,128)(2,1)}, u32[]{:S(2)}, u32[]{:S(2)}) collective-permute-start(bf16[8,32,384]{2,1,0:T(8,128)(2,1)} %all_to_all.10.g0_hbm), channel_id=1, source_target_pairs={{0,8},{8,0},{16,24},{24,16},{1,9},{9,1},{17,25},{25,17},{2,10},{10... | collective-permute-start | bytes 589832 | tf_op jit(solution)/shard_map/ppermute | solution.py:453
  78.1 1.8 %collective-permute-start.12 = (bf16[8,32,384]{2,1,0:T(8,128)(2,1)}, bf16[8,32,384]{2,1,0:T(8,128)(2,1)}, u32[]{:S(2)}, u32[]{:S(2)}) collective-permute-start(bf16[8,32,384]{2,1,0:T(8,128)(2,1)} %collective-permute-done.11.g2_hbm), channel_id=1, source_target_pairs={{0,8},{8,0},{16,24},{24,16},{1,9},{9,1},{17,25},{25,17},{2,10},{10... | collective-permute-start | bytes 589832 | tf_op jit(solution)/shard_map/ppermute | solution.py:453

commit v24 on v22

--- a/solution.py
+++ b/solution.py
@@ -279,7 +279,8 @@
         own = outputs // devices
         for d in range(devices):
             part = total[d * own : (d + 1) * own]
-            pieces[d, 2 * own * u : 2 * own * (u + 1), :] = jnp.concatenate(
+            place = d % owners * (devices // owners) + d // owners
+            pieces[place, 2 * own * u : 2 * own * (u + 1), :] = jnp.concatenate(
                 [part[:, :lanes], part[:, lanes:]], axis=0
             ).astype(bf16)
     wait_all(writes + start_all([(pieces, pieces_hbm)], sems))
@@ -350,9 +351,9 @@
     for u in range(UPDATES):
         sums = []
         for g in range(groups):
-            part = summed[g * owners, 2 * own * u : 2 * own * (u + 1), :].astype(f32)
+            part = summed[g, 2 * own * u : 2 * own * (u + 1), :].astype(f32)
             for o in range(1, owners):
-                part += summed[g * owners + o, 2 * own * u : 2 * own * (u + 1), :].astype(f32)
+                part += summed[o * groups + g, 2 * own * u : 2 * own * (u + 1), :].astype(f32)
             part = jnp.concatenate([part[:own], part[own:]], axis=1)
             if u:
                 reads[3 + g].wait()
@@ -522,7 +523,7 @@
         flops=2.0 * UPDATES * points * count * (2 * width + outputs),
     )
     pieces, beside, across = lax.optimization_barrier((pieces, beside, across))
-    summed = lax.all_to_all(pieces, ("rows", "pts"), 0, 0, tiled=True)
+    summed = lax.all_to_all(pieces, ("pts", "rows"), 0, 0, tiled=True)
     kept = [like((UPDATES, rank, block)), like((rows, block, count))]
     factor, cross = call(
         factors_kernel,

time: 84.8 us -> 84.2 us (level)
  waiting for transfers between devices: 12.4 us -> 11.2 us
where the time goes in v24:
time: 84.2 us; the launch traced here: 83.6 us
  Pallas kernels  39.2 us (47%)
  starting transfers between devices  20 us (24%)
  blocking collectives  12.3 us (15%)
  waiting for transfers between devices  11.2 us (13%)
  between operations  0.91 us (1%)
    pallas_call x8, Pallas kernels, call(): pl.pallas_call(body, out_shape=outs, in_specs=[VMEM] * near + [HBM] * (le...  39.2 us
    ppermute x13, starting transfers between devices, swap(): lax.ppermute(value, axis, [(i, i ^ k) for i in range(lax.axis_size(axis))])  14.8 us
    all_to_all x1, blocking collectives, with_kernels(): got = lax.all_to_all(steps, 'pts', 0, 0, tiled=True)  12.3 us
    ppermute x13, waiting for transfers between devices, swap(): lax.ppermute(value, axis, [(i, i ^ k) for i in range(lax.axis_size(axis))])  8.18 us
    all_to_all x1, starting transfers between devices, with_kernels(): summed = lax.all_to_all(pieces, ('pts', 'rows'), 0, 0, tiled=True)  5.18 us
    all_to_all x1, waiting for transfers between devices, with_kernels(): summed = lax.all_to_all(pieces, ('pts', 'rows'), 0, 0, tiled=True)  3 us
  transfers between devices with their start and end apart: 14, of which 8 were waited for; matrix products, arithmetic and copies ran while one was open for 0% of the time, Pallas kernels for 28%

profile of v24, /device:TPU:0, one launch (start us, length us, event | category | flops | bytes accessed | tf_op | source)
XLA Modules:
  0.0 83.6 jit_solution(11928460695995116118)
XLA Ops:
  0.6 2.3 %shard_map.86.refs_0_ = bf16[384,128]{1,0:T(8,128)(2,1)} custom-call(s32[2,2048]{1,0:T(2,128)} %blocks_hbm.5, bf16[1024,128]{1,0:T(8,128)(2,1)} %feats_hbm.3), custom_call_target="tpu_custom_call" | custom-call | bytes 376832 | tf_op jit(solution)/shard_map/pallas_call | solution.py:437
  2.9 5.1 %collective-permute-start.2 = (bf16[384,128]{1,0:T(8,128)(2,1)}, bf16[384,128]{1,0:T(8,128)(2,1)}, u32[]{:S(2)}, u32[]{:S(2)}) collective-permute-start(bf16[384,128]{1,0:T(8,128)(2,1)} %shard_map.86.refs_0_), channel_id=1, source_target_pairs={{0,6},{1,7},{2,4},{3,5},{4,2},{5,3},{6,0},{7,1},{8,14},{9,15},{10,... | collective-permute-start | bytes 294920 | tf_op jit(solution)/shard_map/ppermute | solution.py:452
  8.0 0.0 collective-permute-start.1
  8.0 1.7 %collective-permute-start.5 = (bf16[384,128]{1,0:T(8,128)(2,1)}, bf16[384,128]{1,0:T(8,128)(2,1)}, u32[]{:S(2)}, u32[]{:S(2)}) collective-permute-start(bf16[384,128]{1,0:T(8,128)(2,1)} %shard_map.86.refs_0_), channel_id=1, source_target_pairs={{0,5},{1,4},{2,7},{3,6},{4,1},{5,0},{6,3},{7,2},{8,13},{9,12},{10,... | collective-permute-start | bytes 294920 | tf_op jit(solution)/shard_map/ppermute | solution.py:452
  9.8 2.1 %collective-permute-start.4 = (bf16[384,128]{1,0:T(8,128)(2,1)}, bf16[384,128]{1,0:T(8,128)(2,1)}, u32[]{:S(2)}, u32[]{:S(2)}) collective-permute-start(bf16[384,128]{1,0:T(8,128)(2,1)} %shard_map.86.refs_0_), channel_id=1, source_target_pairs={{0,4},{1,5},{2,6},{3,7},{4,0},{5,1},{6,2},{7,3},{8,12},{9,13},{10,... | collective-permute-start | bytes 294920 | tf_op jit(solution)/shard_map/ppermute | solution.py:452
  11.9 0.5 collective-permute-start
  12.4 0.0 collective-permute-done.2.refs_6_
  12.4 2.1 %collective-permute-done.1.refs_2_ = bf16[384,128]{1,0:T(8,128)(2,1)} collective-permute-done((bf16[384,128]{1,0:T(8,128)(2,1)}, bf16[384,128]{1,0:T(8,128)(2,1)}, u32[]{:S(2)}, u32[]{:S(2)}) %collective-permute-start.1) | collective-permute-done | bytes 98336 | tf_op jit(solution)/shard_map/ppermute | solution.py:452
  14.5 1.3 %collective-permute-start.3 = (bf16[384,128]{1,0:T(8,128)(2,1)}, bf16[384,128]{1,0:T(8,128)(2,1)}, u32[]{:S(2)}, u32[]{:S(2)}) collective-permute-start(bf16[384,128]{1,0:T(8,128)(2,1)} %collective-permute-done.1.refs_2_), channel_id=1, source_target_pairs={{0,1},{1,0},{2,3},{3,2},{4,5},{5,4},{6,7},{7,6},{8,9},{9,8},{10,11... | collective-permute-start | bytes 294920 | tf_op jit(solution)/shard_map/ppermute | solution.py:452
  15.9 0.7 collective-permute-start.6
  16.6 4.3 %shard_map.87 = (bf16[2,256,1024]{2,1,0:T(8,128)(2,1)}, f32[2,256,512]{2,1,0:T(8,128)}, s32[8,128]{1,0:T(8,128)}) custom-call(s32[2,2048]{1,0:T(2,128)} %blocks_hbm.5, f32[1024,256]{1,0:T(8,128)} %w_hbm.3, f32[1024,256]{1,0:T(8,128)} %z_hbm.3, bf16[1024,256]{1,0:T(8,128)(2,1)} %t_hbm.1), custom_call_target="tpu_custom_call" | custom-call | bytes 4739072 | tf_op jit(solution)/shard_map/pallas_call | solution.py:437
  20.8 0.0 collective-permute-done.5.refs_5_
  20.8 0.0 collective-permute-done.4.refs_4_
  20.8 0.0 collective-permute-done.refs_1_
  20.9 0.3 collective-permute-done.3.refs_3_
  21.2 1.1 %collective-permute-done.6.refs_7_ = bf16[384,128]{1,0:T(8,128)(2,1)} collective-permute-done((bf16[384,128]{1,0:T(8,128)(2,1)}, bf16[384,128]{1,0:T(8,128)(2,1)}, u32[]{:S(2)}, u32[]{:S(2)}) %collective-permute-start.6) | collective-permute-done | bytes 98336 | tf_op jit(solution)/shard_map/ppermute | solution.py:452
  22.2 2.3 %shard_map.88.block_hbm.b0_hbm = bf16[2,128,512]{2,1,0:T(8,128)(2,1)} custom-call(bf16[384,128]{1,0:T(8,128)(2,1)} %shard_map.86.refs_0_, bf16[384,128]{1,0:T(8,128)(2,1)} %collective-permute-done.refs_1_, bf16[384,128]{1,0:T(8,128)(2,1)} %collective-permute-done.1.refs_2_, bf16[384,128]{1,0:T(8,128)(2,1)} %collective-permute-done.3.refs_3_, ...), custom_call_target="tpu_custom_call" | custom-call | bytes 1052672 | tf_op jit(solution)/shard_map/pallas_call | solution.py:437
  24.5 1.6 %collective-permute-start.8 = (bf16[2,128,512]{2,1,0:T(8,128)(2,1)}, bf16[2,128,512]{2,1,0:T(8,128)(2,1)}, u32[]{:S(2)}, u32[]{:S(2)}) collective-permute-start(bf16[2,128,512]{2,1,0:T(8,128)(2,1)} %shard_map.88.block_hbm.b0_hbm), channel_id=1, source_target_pairs={{0,16},{8,24},{16,0},{24,8},{1,17},{9,25},{17,1},{25,9},{2,18},{10... | collective-permute-start | bytes 786440 | tf_op jit(solution)/shard_map/ppermute | solution.py:452
  26.1 0.0 collective-permute-start.7
  26.2 4.8 %shard_map.89 = (bf16[32,32,256]{2,1,0:T(8,128)(2,1)}, s32[8,512]{1,0:T(8,128)}, s32[8,512]{1,0:T(8,128)}, s32[8,128]{1,0:T(8,128)}) custom-call(bf16[2,128,512]{2,1,0:T(8,128)(2,1)} %shard_map.88.block_hbm.b0_hbm, bf16[1024,128]{1,0:T(8,128)(2,1)} %feats_hbm.3, s32[2,2048]{1,0:T(2,128)} %blocks_hbm.5, bf16[2,256,1024]{2,1,0:T(8,128)(2,1)} %get-tuple-element.25.coef_hbm, ...), custom_call_target="tpu_custom_call" | custom-call | flops 1073741824 | bytes 3198976 | tf_op jit(solution)/shard_map/pallas_call | solution.py:437
  30.9 0.6 collective-permute-done.8.b2_hbm
  31.6 0.0 collective-permute-done.7.b1_hbm
  31.6 5.2 %all-to-all-start = ((bf16[32,32,256]{2,1,0:T(8,128)(2,1)}), bf16[32,32,256]{2,1,0:T(8,128)(2,1)}, u32[]{:S(2)}, u32[]{:S(2)}) async-start(bf16[32,32,256]{2,1,0:T(8,128)(2,1)} %get-tuple-element.28), calls=%async_computation | async-start | bytes 1048576 | tf_op jit(solution)/shard_map/all_to_all | solution.py:526
  36.8 0.1 collective-permute-start.9
  36.8 1.9 %collective-permute-done.9.b3_hbm = bf16[2,128,512]{2,1,0:T(8,128)(2,1)} collective-permute-done((bf16[2,128,512]{2,1,0:T(8,128)(2,1)}, bf16[2,128,512]{2,1,0:T(8,128)(2,1)}, u32[]{:S(2)}, u32[]{:S(2)}) %collective-permute-start.9) | collective-permute-done | bytes 262176 | tf_op jit(solution)/shard_map/ppermute | solution.py:452
  38.7 10.4 %shard_map.90 = (bf16[2,512,2048]{2,1,0:T(8,128)(2,1)}, bf16[4,2048,512]{2,1,0:T(8,128)(2,1)}) custom-call(bf16[2,128,512]{2,1,0:T(8,128)(2,1)} %shard_map.88.block_hbm.b0_hbm, bf16[2,128,512]{2,1,0:T(8,128)(2,1)} %collective-permute-done.7.b1_hbm, bf16[2,128,512]{2,1,0:T(8,128)(2,1)} %collective-permute-done.8.b2_hbm, ...), custom_call_target="tpu_custom_call" | custom-call | flops 1610612736 | bytes 13668352 | tf_op jit(solution)/shard_map/pallas_call | solution.py:437
  49.1 3.0 %all-to-all-done.summed_hbm = bf16[32,32,256]{2,1,0:T(8,128)(2,1)} async-done(((bf16[32,32,256]{2,1,0:T(8,128)(2,1)}), bf16[32,32,256]{2,1,0:T(8,128)(2,1)}, u32[]{:S(2)}, u32[]{:S(2)}) %all-to-all-start) | async-done | bytes 524320 | tf_op jit(solution)/shard_map/all_to_all | solution.py:526
  52.1 7.1 %shard_map.91 = bf16[8,32,384]{2,1,0:T(8,128)(2,1)} custom-call(bf16[32,32,256]{2,1,0:T(8,128)(2,1)} %all-to-all-done.summed_hbm, bf16[2,512,2048]{2,1,0:T(8,128)(2,1)} %get-tuple-element.33.factor_hbm, bf16[2,512,512]{2,1,0:T(8,128)(2,1)} %core_hbm.1, bf16[4,2048,512]{2,1,0:T(8,128)(2,1)} %get-tuple-element.34.cross_hbm, s32[8,128]{1,0:T(8,128)} %get-tuple-element.35.starts_hbm), custom_call_target="tpu_custom_call" | custom-call | bytes 14356480 | tf_op jit(solution)/shard_map/pallas_call | solution.py:437
  59.2 12.3 %all_to_all.10.g0_hbm = bf16[8,32,384]{2,1,0:T(8,128)(2,1)} all-to-all(bf16[8,32,384]{2,1,0:T(8,128)(2,1)} %shard_map.91), channel_id=1, replica_groups=mesh['rows'=4,'pts'=8] {'pts'}, dimensions={0} | all-to-all | bytes 393216 | tf_op jit(solution)/shard_map/all_to_all | solution.py:561
  71.5 1.4 %collective-permute-start.11 = (bf16[8,32,384]{2,1,0:T(8,128)(2,1)}, bf16[8,32,384]{2,1,0:T(8,128)(2,1)}, u32[]{:S(2)}, u32[]{:S(2)}) collective-permute-start(bf16[8,32,384]{2,1,0:T(8,128)(2,1)} %all_to_all.10.g0_hbm), channel_id=1, source_target_pairs={{0,16},{8,24},{16,0},{24,8},{1,17},{9,25},{17,1},{25,9},{2,18},{10... | collective-permute-start | bytes 589832 | tf_op jit(solution)/shard_map/ppermute | solution.py:452
  73.0 0.0 collective-permute-start.10
  73.0 4.1 %shard_map.92.slots_hbm = s32[2,768]{1,0:T(2,128)} custom-call(s32[2,2048]{1,0:T(2,128)} %blocks_hbm.5), custom_call_target="tpu_custom_call" | custom-call | bytes 22528 | tf_op jit(solution)/shard_map/pallas_call | solution.py:437
  77.1 0.5 collective-permute-done.11.g2_hbm
  77.5 0.1 collective-permute-start.12
  77.6 0.0 collective-permute-done.10.g1_hbm
  77.7 1.7 %collective-permute-done.12.g3_hbm = bf16[8,32,384]{2,1,0:T(8,128)(2,1)} collective-permute-done((bf16[8,32,384]{2,1,0:T(8,128)(2,1)}, bf16[8,32,384]{2,1,0:T(8,128)(2,1)}, u32[]{:S(2)}, u32[]{:S(2)}) %collective-permute-start.12) | collective-permute-done | bytes 196640 | tf_op jit(solution)/shard_map/ppermute | solution.py:452
  79.3 4.1 %shard_map.93 = (f32[1024,256]{1,0:T(8,128)}, f32[1024,256]{1,0:T(8,128)}) custom-call(bf16[8,32,384]{2,1,0:T(8,128)(2,1)} %all_to_all.10.g0_hbm, bf16[8,32,384]{2,1,0:T(8,128)(2,1)} %collective-permute-done.10.g1_hbm, bf16[8,32,384]{2,1,0:T(8,128)(2,1)} %collective-permute-done.11.g2_hbm, bf16[8,32,384]{2,1,0:T(8,128)(2,1)} %collective-permute-done.12.g3_hbm, ...), custom_call_target="tpu_custom_call" | custom-call | bytes 4986880 | tf_op jit(solution)/shard_map/pallas_call | solution.py:437
Async XLA Ops:
  2.9 9.5 %collective-permute-start.2 = (bf16[384,128]{1,0:T(8,128)(2,1)}, bf16[384,128]{1,0:T(8,128)(2,1)}, u32[]{:S(2)}, u32[]{:S(2)}) collective-permute-start(bf16[384,128]{1,0:T(8,128)(2,1)} %shard_map.86.refs_0_), channel_id=1, source_target_pairs={{0,6},{1,7},{2,4},{3,5},{4,2},{5,3},{6,0},{7,1},{8,14},{9,15},{10,... | collective-permute-start | bytes 294920 | tf_op jit(solution)/shard_map/ppermute | solution.py:452
  8.0 6.5 %collective-permute-start.1 = (bf16[384,128]{1,0:T(8,128)(2,1)}, bf16[384,128]{1,0:T(8,128)(2,1)}, u32[]{:S(2)}, u32[]{:S(2)}) collective-permute-start(bf16[384,128]{1,0:T(8,128)(2,1)} %shard_map.86.refs_0_), channel_id=1, source_target_pairs={{0,2},{1,3},{2,0},{3,1},{4,6},{5,7},{6,4},{7,5},{8,10},{9,11},{10,... | collective-permute-start | bytes 294920 | tf_op jit(solution)/shard_map/ppermute | solution.py:452
  8.0 12.8 %collective-permute-start.5 = (bf16[384,128]{1,0:T(8,128)(2,1)}, bf16[384,128]{1,0:T(8,128)(2,1)}, u32[]{:S(2)}, u32[]{:S(2)}) collective-permute-start(bf16[384,128]{1,0:T(8,128)(2,1)} %shard_map.86.refs_0_), channel_id=1, source_target_pairs={{0,5},{1,4},{2,7},{3,6},{4,1},{5,0},{6,3},{7,2},{8,13},{9,12},{10,... | collective-permute-start | bytes 294920 | tf_op jit(solution)/shard_map/ppermute | solution.py:452
  9.8 11.1 %collective-permute-start.4 = (bf16[384,128]{1,0:T(8,128)(2,1)}, bf16[384,128]{1,0:T(8,128)(2,1)}, u32[]{:S(2)}, u32[]{:S(2)}) collective-permute-start(bf16[384,128]{1,0:T(8,128)(2,1)} %shard_map.86.refs_0_), channel_id=1, source_target_pairs={{0,4},{1,5},{2,6},{3,7},{4,0},{5,1},{6,2},{7,3},{8,12},{9,13},{10,... | collective-permute-start | bytes 294920 | tf_op jit(solution)/shard_map/ppermute | solution.py:452
  11.9 9.0 %collective-permute-start = (bf16[384,128]{1,0:T(8,128)(2,1)}, bf16[384,128]{1,0:T(8,128)(2,1)}, u32[]{:S(2)}, u32[]{:S(2)}) collective-permute-start(bf16[384,128]{1,0:T(8,128)(2,1)} %shard_map.86.refs_0_), channel_id=1, source_target_pairs={{0,1},{1,0},{2,3},{3,2},{4,5},{5,4},{6,7},{7,6},{8,9},{9,8},{10,11... | collective-permute-start | bytes 294920 | tf_op jit(solution)/shard_map/ppermute | solution.py:452
  14.5 6.7 %collective-permute-start.3 = (bf16[384,128]{1,0:T(8,128)(2,1)}, bf16[384,128]{1,0:T(8,128)(2,1)}, u32[]{:S(2)}, u32[]{:S(2)}) collective-permute-start(bf16[384,128]{1,0:T(8,128)(2,1)} %collective-permute-done.1.refs_2_), channel_id=1, source_target_pairs={{0,1},{1,0},{2,3},{3,2},{4,5},{5,4},{6,7},{7,6},{8,9},{9,8},{10,11... | collective-permute-start | bytes 294920 | tf_op jit(solution)/shard_map/ppermute | solution.py:452
  15.9 6.4 %collective-permute-start.6 = (bf16[384,128]{1,0:T(8,128)(2,1)}, bf16[384,128]{1,0:T(8,128)(2,1)}, u32[]{:S(2)}, u32[]{:S(2)}) collective-permute-start(bf16[384,128]{1,0:T(8,128)(2,1)} %collective-permute-done.2.refs_6_), channel_id=1, source_target_pairs={{0,1},{1,0},{2,3},{3,2},{4,5},{5,4},{6,7},{7,6},{8,9},{9,8},{10,11... | collective-permute-start | bytes 294920 | tf_op jit(solution)/shard_map/ppermute | solution.py:452
  24.5 7.1 %collective-permute-start.8 = (bf16[2,128,512]{2,1,0:T(8,128)(2,1)}, bf16[2,128,512]{2,1,0:T(8,128)(2,1)}, u32[]{:S(2)}, u32[]{:S(2)}) collective-permute-start(bf16[2,128,512]{2,1,0:T(8,128)(2,1)} %shard_map.88.block_hbm.b0_hbm), channel_id=1, source_target_pairs={{0,16},{8,24},{16,0},{24,8},{1,17},{9,25},{17,1},{25,9},{2,18},{10... | collective-permute-start | bytes 786440 | tf_op jit(solution)/shard_map/ppermute | solution.py:452
  26.1 5.4 %collective-permute-start.7 = (bf16[2,128,512]{2,1,0:T(8,128)(2,1)}, bf16[2,128,512]{2,1,0:T(8,128)(2,1)}, u32[]{:S(2)}, u32[]{:S(2)}) collective-permute-start(bf16[2,128,512]{2,1,0:T(8,128)(2,1)} %shard_map.88.block_hbm.b0_hbm), channel_id=1, source_target_pairs={{0,8},{8,0},{16,24},{24,16},{1,9},{9,1},{17,25},{25,17},{2,10},{10... | collective-permute-start | bytes 786440 | tf_op jit(solution)/shard_map/ppermute | solution.py:452
  31.6 20.5 %all-to-all-start = ((bf16[32,32,256]{2,1,0:T(8,128)(2,1)}), bf16[32,32,256]{2,1,0:T(8,128)(2,1)}, u32[]{:S(2)}, u32[]{:S(2)}) async-start(bf16[32,32,256]{2,1,0:T(8,128)(2,1)} %get-tuple-element.28), calls=%async_computation | async-start | bytes 1048576 | tf_op jit(solution)/shard_map/all_to_all | solution.py:526
  36.8 1.9 %collective-permute-start.9 = (bf16[2,128,512]{2,1,0:T(8,128)(2,1)}, bf16[2,128,512]{2,1,0:T(8,128)(2,1)}, u32[]{:S(2)}, u32[]{:S(2)}) collective-permute-start(bf16[2,128,512]{2,1,0:T(8,128)(2,1)} %collective-permute-done.8.b2_hbm), channel_id=1, source_target_pairs={{0,8},{8,0},{16,24},{24,16},{1,9},{9,1},{17,25},{25,17},{2,10},{10... | collective-permute-start | bytes 786440 | tf_op jit(solution)/shard_map/ppermute | solution.py:452
  71.5 6.0 %collective-permute-start.11 = (bf16[8,32,384]{2,1,0:T(8,128)(2,1)}, bf16[8,32,384]{2,1,0:T(8,128)(2,1)}, u32[]{:S(2)}, u32[]{:S(2)}) collective-permute-start(bf16[8,32,384]{2,1,0:T(8,128)(2,1)} %all_to_all.10.g0_hbm), channel_id=1, source_target_pairs={{0,16},{8,24},{16,0},{24,8},{1,17},{9,25},{17,1},{25,9},{2,18},{10... | collective-permute-start | bytes 589832 | tf_op jit(solution)/shard_map/ppermute | solution.py:452
  73.0 4.7 %collective-permute-start.10 = (bf16[8,32,384]{2,1,0:T(8,128)(2,1)}, bf16[8,32,384]{2,1,0:T(8,128)(2,1)}, u32[]{:S(2)}, u32[]{:S(2)}) collective-permute-start(bf16[8,32,384]{2,1,0:T(8,128)(2,1)} %all_to_all.10.g0_hbm), channel_id=1, source_target_pairs={{0,8},{8,0},{16,24},{24,16},{1,9},{9,1},{17,25},{25,17},{2,10},{10... | collective-permute-start | bytes 589832 | tf_op jit(solution)/shard_map/ppermute | solution.py:452
  77.5 1.8 %collective-permute-start.12 = (bf16[8,32,384]{2,1,0:T(8,128)(2,1)}, bf16[8,32,384]{2,1,0:T(8,128)(2,1)}, u32[]{:S(2)}, u32[]{:S(2)}) collective-permute-start(bf16[8,32,384]{2,1,0:T(8,128)(2,1)} %collective-permute-done.11.g2_hbm), channel_id=1, source_target_pairs={{0,8},{8,0},{16,24},{24,16},{1,9},{9,1},{17,25},{25,17},{2,10},{10... | collective-permute-start | bytes 589832 | tf_op jit(solution)/shard_map/ppermute | solution.py:452
